TPU v7x, 32 devices: a whole 2x2x4 slice. The times are simulated.
32 devices in a mesh: dp: 4 (over z), own: 8 (over y, x, core).
Axes of the slice: x: 2, y: 2, z: 4, core: 2. Of those that a mesh axis runs over, the one named last changes fastest.
Arguments:
- signals: bfloat16 [8192, 384], P(('dp', 'own')), may hold values from -6 to 6
- cotangent: bfloat16 [8192, 384], P(('dp', 'own')), may hold values from -6 to 6
- row_insertion: int32 [8192], P(('dp', 'own')), may hold values from 0 to 15, as said below
- touched: int32 [32, 4], replicated, may hold values from 0 to 15, as said below
- slot_map: int32 [16], replicated, may hold values from 0 to 15, each once
- weights: bfloat16 [16, 2, 384, 1024], P(None, None, 'own'), may hold values from -0.3125 to 0.3125
- moment1: float32 [16, 2, 384, 1024], P(None, None, 'own', 'dp'), may hold values from -18.101934 to 18.101934
- moment2: float32 [16, 2, 384, 1024], P(None, None, 'own', 'dp'), may hold values from 0.1024 to 3.072
Outputs:
- predicted: bfloat16 [8192, 384], P(('dp', 'own'))
- new_weights: bfloat16 [16, 2, 384, 1024], P(None, None, 'own')
- new_moment1: float32 [16, 2, 384, 1024], P(None, None, 'own', 'dp')
- new_moment2: float32 [16, 2, 384, 1024], P(None, None, 'own', 'dp')
Inputs may be any that keep to these rules, and one draw needn't show every extreme that they name: `row_insertion`: device d (dp index times the size of own plus own index) holds rows d * 256 to (d + 1) * 256 - 1; their insertions are all in row d of touched; at most 128 rows of one device name the same insertion, and on every device one insertion is named by exactly 128 rows. `touched`: each row lists 4 different insertions.
All inputs are finite; a program needn't handle non-finite values.
Results may differ from a plain program's by a relative error of at most 0.0049.
Values may be sent and summed in bfloat16 or wider, within the bound.
No kernel may reach another device: no remote copies, remote signals or barrier semaphores. Data moves between devices by JAX's collectives and lax.ppermute only.
A program may use at most 128 MiB of HBM per device.

v0:
```python
import math

import jax
import jax.numpy as jnp
from jax import lax
from jax.sharding import PartitionSpec as P

SITES = 384
WIDTH = 1024
TOUCH = 4
CAP = 128


gelu_coef = math.sqrt(2.0 / math.pi)
cubic_coef = 0.044715
learn_rate = 0.01
highest = lax.Precision.HIGHEST


def gelu_parts(preact):
    tanh_input = gelu_coef * (preact + cubic_coef * preact * preact * preact)
    tangent = jnp.tanh(tanh_input)
    gelu_val = 0.5 * preact * (1.0 + tangent)
    slopes = 0.5 * (1.0 + tangent) + 0.5 * preact * (1.0 - tangent * tangent) * gelu_coef * (
        1.0 + 3.0 * cubic_coef * preact * preact
    )
    return (gelu_val, slopes)


def dispatch(row_ids, listed):
    match_table = (row_ids[:, None] == listed[None, :]).astype(jnp.int32)
    running = jnp.cumsum(match_table, axis=0) - 1
    slot_of = jnp.sum(match_table * jnp.arange(listed.shape[0], dtype=jnp.int32)[None, :], axis=1)
    within = jnp.sum(match_table * running, axis=1)
    return slot_of * CAP + within


def adam_step(params, moment_one, moment_two, gradient):
    moment_one = 0.9 * moment_one + 0.1 * gradient
    moment_two = 0.999 * moment_two + 0.001 * gradient * gradient
    correct_one = 1.0 - 0.9**10
    correct_two = 1.0 - 0.999**10
    updated = params - learn_rate * (moment_one / correct_one) / (
        jnp.sqrt(moment_two / correct_two) + 1e-08
    )
    return (updated.astype(jnp.bfloat16), moment_one, moment_two)


def sum_by_insertion(item_rows, arrived_grad, number):
    one_hot = (jnp.arange(number, dtype=jnp.int32)[:, None] == item_rows[None, :]).astype(
        jnp.float32
    )
    flat_grad = arrived_grad.reshape(item_rows.shape[0], -1)
    return jnp.dot(one_hot, flat_grad, precision=highest, preferred_element_type=jnp.float32)


def shards(signals, cotangent, row_insertion, touched, slot_map, weights, moment1, moment2):
    n_own = lax.axis_size("own")
    n_dp = lax.axis_size("dp")
    dp_at = lax.axis_index("dp")
    own_at = lax.axis_index("own")
    number = weights.shape[0]
    piece_rows = weights.shape[2]
    width_part = moment1.shape[3]
    stored = jnp.sum(
        jnp.where(
            touched[:, :, None] == jnp.arange(number, dtype=jnp.int32)[None, None, :],
            slot_map[None, None, :],
            0,
        ),
        axis=2,
    )
    stored_all = stored.reshape(n_dp, n_own, TOUCH)
    group_rows = lax.dynamic_index_in_dim(stored_all, dp_at, 0, keepdims=False)
    flat_rows = group_rows.reshape(-1)
    my_list = lax.dynamic_index_in_dim(touched, dp_at * n_own + own_at, 0, keepdims=False)
    places = dispatch(row_insertion, my_list)
    stacked = (
        jnp.zeros((TOUCH * CAP, 2 * SITES), signals.dtype)
        .at[places]
        .set(jnp.concatenate([signals, cotangent], axis=1))
    )
    stacked = stacked.reshape(TOUCH, CAP, 2 * SITES)
    sig_slots = stacked[:, :, :SITES]
    cot_slots = stacked[:, :, SITES:]
    read_out = None
    outgoing = jnp.take(weights, flat_rows, axis=0).reshape(n_own, TOUCH, 2, piece_rows, WIDTH)
    arrived = lax.all_to_all(outgoing, "own", split_axis=0, concat_axis=3, tiled=True)
    read_in = arrived[0, :, 0]
    read_out = arrived[0, :, 1]
    preact = jnp.einsum("kcs,ksw->kcw", sig_slots, read_in, preferred_element_type=jnp.float32)
    gelu_val, slopes = gelu_parts(preact)
    hidden = gelu_val.astype(jnp.bfloat16)
    pred_slots = jnp.einsum(
        "kcw,ksw->kcs", hidden, read_out, preferred_element_type=jnp.float32
    ).astype(jnp.bfloat16)
    back_hidden = jnp.einsum(
        "kcs,ksw->kcw", cot_slots, read_out, preferred_element_type=jnp.float32
    )
    back_pre = (back_hidden * slopes).astype(jnp.bfloat16)
    grad_in = jnp.einsum("kcs,kcw->ksw", sig_slots, back_pre, preferred_element_type=jnp.float32)
    grad_out = jnp.einsum("kcs,kcw->ksw", cot_slots, hidden, preferred_element_type=jnp.float32)
    grads = jnp.stack([grad_in, grad_out], axis=1)
    arrived_grad = lax.all_to_all(
        lax.all_to_all(grads[None, None], "dp", split_axis=5, concat_axis=0, tiled=True),
        "own",
        split_axis=4,
        concat_axis=1,
        tiled=True,
    )
    table = sum_by_insertion(stored.reshape(-1), arrived_grad, number).reshape(
        number, 2, piece_rows, width_part
    )
    own_params = lax.dynamic_slice_in_dim(weights, dp_at * width_part, width_part, 3).astype(
        jnp.float32
    )
    fresh_part, new_moment1, new_moment2 = adam_step(own_params, moment1, moment2, table)
    new_weights = lax.all_gather(fresh_part, "dp", axis=3, tiled=True)
    predicted = pred_slots.reshape(TOUCH * CAP, SITES)[places]
    return (predicted, new_weights, new_moment1, new_moment2)


def solution(mesh):
    in_specs = (
        P(("dp", "own"), None),
        P(("dp", "own"), None),
        P(("dp", "own")),
        P(),
        P(),
        P(None, None, "own", None),
        P(None, None, "own", "dp"),
        P(None, None, "own", "dp"),
    )
    out_specs = (
        P(("dp", "own"), None),
        P(None, None, "own", None),
        P(None, None, "own", "dp"),
        P(None, None, "own", "dp"),
    )
    return jax.shard_map(shards, mesh=mesh, in_specs=in_specs, out_specs=out_specs, check_vma=False)
```

profile of v0, /device:TPU:2, one launch (start us, length us, event | category | flops | bytes accessed | tf_op | source)
XLA Modules:
  0.0 725.2 jit_solution(13267865411884514006)
XLA Ops:
  7.2 0.9 select_reduce_fusion
  8.1 0.1 reshape.118
  8.2 0.1 copy.103
  8.3 0.1 copy.102
  8.4 0.1 reshape.120
  8.5 0.6 copy-done
  9.1 3.6 gather_fusion
  12.7 3.4 broadcast_select_fusion
  16.2 3.4 copy.104
  19.5 4.8 all-to-all-start
  24.4 0.2 dynamic-slice_reduce_fusion
  24.6 0.8 compare_convert_fusion
  25.3 1.2 reduce-window.6
  26.5 0.1 slice.28
  26.6 0.7 copy.100
  27.3 0.7 reduce-window.9
  28.0 0.6 slice.19
  28.5 0.8 copy.101
  29.3 0.1 add_bitcast_fusion
  29.4 0.8 fusion.26
  30.2 2.6 scatter_custom_fusion
  32.8 61.5 %all-to-all-done = bf16[8,4,2,48,1024]{4,3,1,2,0:T(8,128)(2,1)} async-done(((bf16[8,4,2,48,1024]{4,3,1,2,0:T(8,128)(2,1)}), bf16[8,4,2,48,1024]{4,3,1,2,0:T(8,128)(2,1)}, u32[]{:S(2)}, u32[]{:S(2)}) %all-to-all-start) | async-done | bytes 6291488 | tf_op jit(solution)/shard_map/all_to_all | solution.py:88
  94.2 3.6 copy.105
  97.8 2.7 copy-done.1
  100.5 2.0 fusion
  102.5 7.9 %convolution_bitcast_fusion.1 = f32[4,1,384,1024]{3,2,0,1:T(8,128)} fusion(f32[4,128,1024]{2,1,0:T(8,128)} %fusion, bf16[1,4,2,384,1024]{4,3,1,2,0:T(8,128)(2,1)} %bitcast.74, bf16[4,128,768]{2,1,0:T(8,128)(2,1)} %bitcast.77), kind=kOutput, calls=%fused_computation.13 | convolution fusion | flops 815267840 | bytes 12320768 | tf_op jit(solution)/shard_map/kcs,kcw->ksw/dot_general | solution.py:101
  110.4 5.4 convolution_bitcast_fusion
  115.8 11.9 %maximum_bitcast_fusion = f32[1,1,4,2,384,1024]{5,4,2,3,1,0:T(8,128)} fusion(f32[4,1,384,1024]{3,2,0,1:T(8,128)} %convolution_bitcast_fusion, f32[4,1,384,1024]{3,2,0,1:T(8,128)} %convolution_bitcast_fusion.1), kind=kLoop, calls=%fused_computation.3 | loop fusion | flops 3145728 | bytes 25165824 | tf_op jit(solution)/shard_map/broadcast_in_dim | solution.py:105
  127.7 14.8 %copy.111 = f32[1,1,4,2,384,1024]{4,2,3,1,0,5:T(4,128)} copy(f32[1,1,4,2,384,1024]{5,4,2,3,1,0:T(8,128)} %maximum_bitcast_fusion) | data formatting | bytes 25165824 | tf_op jit(solution)/shard_map/broadcast_in_dim | solution.py:105
  142.6 283.5 %all_to_all.51 = f32[1,1,4,2,384,1024]{4,2,3,1,0,5:T(4,128)} all-to-all(f32[1,1,4,2,384,1024]{4,2,3,1,0,5:T(4,128)} %copy.111), channel_id=1, replica_groups=mesh['dp'=4,'own'=8] {'dp'}, dimensions={5} | all-to-all | bytes 25165824 | tf_op jit(solution)/shard_map/all_to_all | solution.py:105
  426.1 19.2 %copy.112 = f32[1,1,4,2,384,4,256]{6,3,2,5,4,1,0:T(2,128)} copy(f32[1,1,4,2,384,4,256]{4,2,3,6,5,1,0:T(4,128)} %bitcast.69) | data formatting | bytes 25165824 | tf_op jit(solution)/shard_map/all_to_all | solution.py:105
  445.3 5.3 all-to-all-start.2
  450.6 0.2 all-gather.2.cloned.1.call-start
  450.8 0.1 copy.108
  450.9 0.1 eq.65
  451.0 1.0 constant_dynamic-slice_fusion.1
  452.0 134.4 %all-to-all-done.2 = f32[4,1,4,2,384,256]{5,3,2,0,1,4:T(2,128)} async-done(((f32[4,1,4,2,384,256]{5,3,2,0,1,4:T(2,128)}), f32[4,1,4,2,384,256]{5,3,2,0,1,4:T(2,128)}, u32[]{:S(2)}, u32[]{:S(2)}) %all-to-all-start.2) | async-done | bytes 12582944 | tf_op jit(solution)/shard_map/all_to_all | solution.py:104
  586.5 16.3 %copy.113 = f32[4,1,4,2,384,256]{5,4,3,2,0,1:T(8,128)} copy(f32[4,1,4,2,384,256]{5,3,2,0,1,4:T(2,128)} %all-to-all-done.2) | data formatting | bytes 25165824 | tf_op jit(solution)/shard_map/all_to_all | solution.py:104
  602.8 11.0 %copy.114 = f32[4,8,1,4,2,48,256]{6,5,4,3,1,0,2:T(8,128)} copy(f32[4,8,1,4,2,48,256]{6,5,1,4,3,0,2:T(8,128)} %bitcast.70) | data formatting | bytes 25165824 | tf_op jit(solution)/shard_map/all_to_all | solution.py:104
  613.8 12.0 %reshape.122 = f32[128,24576]{1,0:T(8,128)} reshape(f32[4,8,1,4,2,48,256]{6,5,4,3,1,0,2:T(8,128)} %copy.114) | data formatting | bytes 25165824 | tf_op jit(solution)/shard_map/reshape | solution.py:53
  625.8 12.5 %copy.115 = f32[24576,128]{1,0:T(8,128)} copy(f32[24576,128]{0,1:T(8,128)} %bitcast.71) | data formatting | bytes 25165824 | tf_op jit(solution)/shard_map/dot_general | solution.py:54
  638.3 12.2 %subtract_convert_fusion = (bf16[16,2,48,256]{3,0,2,1:T(8,128)(2,1)}, f32[16,2,48,256]{3,0,2,1:T(8,128)}, f32[16,2,48,256]{3,0,2,1:T(8,128)}) fusion(bf16[16,2,48,256]{3,2,1,0:T(8,128)(2,1)} %constant_dynamic-slice_fusion.1, f32[16,2,48,256]{3,2,1,0:T(8,128)} %param.14, f32[16,2,48,256]{3,2,1,0:T(8,128)} %param.15, f32[2,48,256,128]{3,2,1,0:T(8,128)} %bitcast.68, ...), kind=kOutput, calls=%fused_computation.27 | convolution fusion | flops 609486848 | bytes 20447744 | tf_op jit(solution)/shard_map/dot_general | solution.py:54
  650.6 3.7 fusion.12
  654.2 1.8 gather_fusion.1
  656.1 3.7 copy.118
  659.8 2.1 copy.119
  661.8 51.3 %all-gather.2.cloned.1.call-done = bf16[16,2,48,1024]{3,0,2,1:T(8,128)(2,1)} async-done(((bf16[16,2,48,256]{3,0,2,1:T(8,128)(2,1)}), bf16[16,2,48,1024]{3,0,2,1:T(8,128)(2,1)}) %all-gather.2.cloned.1.call-update) | async-done | bytes 3145744 | tf_op jit(solution)/shard_map/all_gather | solution.py:118
  713.1 5.3 copy.117
  (20 shorter events, 0.1 us)
Async XLA Ops:
  7.2 1.9 copy-start
  19.5 4.9 copy-start.6
  19.5 10.6 %copy-start.4 = (bf16[256,384]{1,0:T(8,128)(2,1)S(1)}, bf16[256,384]{1,0:T(8,128)(2,1)}, u32[]{:S(2)}) copy-start(bf16[256,384]{1,0:T(8,128)(2,1)} %param.9) | copy-start | bytes 589828
  19.5 10.6 %copy-start.5 = (bf16[256,384]{1,0:T(8,128)(2,1)S(1)}, bf16[256,384]{1,0:T(8,128)(2,1)}, u32[]{:S(2)}) copy-start(bf16[256,384]{1,0:T(8,128)(2,1)} %param.8) | copy-start | bytes 589828
  19.5 74.7 %all-to-all-start = ((bf16[8,4,2,48,1024]{4,3,1,2,0:T(8,128)(2,1)}), bf16[8,4,2,48,1024]{4,3,1,2,0:T(8,128)(2,1)}, u32[]{:S(2)}, u32[]{:S(2)}) async-start(bf16[8,4,2,48,1024]{4,3,1,2,0:T(8,128)(2,1)} %copy.104), calls=%async_computation | async-start | bytes 12582912 | tf_op jit(solution)/shard_map/all_to_all | solution.py:88
  94.2 6.3 copy-start.3
  97.8 2.7 copy-start.1
  445.3 141.2 %all-to-all-start.2 = ((f32[4,1,4,2,384,256]{5,3,2,0,1,4:T(2,128)}), f32[4,1,4,2,384,256]{5,3,2,0,1,4:T(2,128)}, u32[]{:S(2)}, u32[]{:S(2)}) async-start(f32[4,1,4,2,384,256]{5,3,2,0,1,4:T(2,128)} %bitcast.67), calls=%async_computation.2 | async-start | bytes 25165824 | tf_op jit(solution)/shard_map/all_to_all | solution.py:104
  450.6 262.5 %all-gather.2.cloned.1.call-start = ((), (), s32[]{:S(2)}) async-start(), calls=%async_computation.3 | async-start | bytes 3932160 | tf_op jit(solution)/shard_map/all_gather | solution.py:118
  656.1 3.7 copy-start.2
Sparse Core Ops, SparseCore 0:
  650.7 62.3 all-gather.1
where the time goes:
time: 728 us; the launch traced here: 725 us
  blocking collectives  284 us (39%)
  waiting for transfers between devices  247 us (34%)
  local copies, waits for them, and re-layouts  116 us (16%)
  matrix products  31.2 us (4%)
  other arithmetic  22.4 us (3%)
  between operations  14.1 us (2%)
  starting transfers between devices  10.3 us (1%)
    all_to_all x1, blocking collectives, shards(): lax.all_to_all(grads[None, None], 'dp', split_axis=5, concat_axis=0, tile...  284 us
    all_to_all x1, waiting for transfers between devices, shards(): lax.all_to_all(lax.all_to_all(grads[None, None], 'dp', split_axis=5, conc...  134 us
    all_to_all x1, waiting for transfers between devices, shards(): lax.all_to_all(outgoing, 'own', split_axis=0, concat_axis=3, tiled=True)  61.5 us
    all_gather x1, waiting for transfers between devices, shards(): new_weights = lax.all_gather(fresh_part, 'dp', axis=3, tiled=True)  51.3 us
    all_to_all x2, local copies, waits for them, and re-layouts, shards(): lax.all_to_all(lax.all_to_all(grads[None, None], 'dp', split_axis=5, conc...  27.3 us
    all_to_all x1, local copies, waits for them, and re-layouts, shards(): lax.all_to_all(grads[None, None], 'dp', split_axis=5, concat_axis=0, tile...  19.2 us
    broadcast_in_dim x1, local copies, waits for them, and re-layouts, shards(): grads[None, None]  14.8 us
  transfers between devices with their start and end apart: 3, of which 3 were waited for; matrix products, arithmetic and copies ran while one was open for 3% of the time, Pallas kernels for 0%

commit v1 on v0

v1 whole, which is shorter than its diff:
```python
import math

import jax
import jax.numpy as jnp
from jax import lax
from jax.experimental import pallas as pl
from jax.experimental.pallas import tpu as pltpu
from jax.sharding import PartitionSpec as P

SITES = 384
CAP = 128
CHUNKS = 1
ID_ROWS = 16
VMEM_BYTES = 56 * 2**20

gelu_coef = math.sqrt(2.0 / math.pi)
cubic_coef = 0.044715
learn_rate = 0.01


def gelu_parts(preact):
    tanh_input = gelu_coef * (preact + cubic_coef * preact * preact * preact)
    tangent = jnp.tanh(tanh_input)
    gelu_val = 0.5 * preact * (1.0 + tangent)
    slopes = 0.5 * (1.0 + tangent) + 0.5 * preact * (1.0 - tangent * tangent) * gelu_coef * (
        1.0 + 3.0 * cubic_coef * preact * preact
    )
    return (gelu_val, slopes)


def params():
    return pltpu.CompilerParams(vmem_limit_bytes=VMEM_BYTES)


def vmem():
    return pl.BlockSpec(memory_space=pltpu.VMEM)


def smem():
    return pl.BlockSpec(memory_space=pltpu.SMEM)


def pack_rows(ids, signals, cotangent):
    rows = signals.shape[0]

    def body(ids_ref, sig_ref, cot_ref, out_ref, perm_ref):
        ids_row = ids_ref[...].astype(jnp.float32)
        lane_ids = jnp.broadcast_to(ids_row, (rows, rows))
        same = lane_ids == lane_ids.T
        count = jnp.sum(same.astype(jnp.float32), axis=0, keepdims=True)
        full = jnp.max(jnp.where(count == CAP, ids_row, -1.0), axis=1, keepdims=True)
        chosen = ids_row == full
        from_row = lax.broadcasted_iota(jnp.int32, (rows, rows), 0)
        to_lane = lax.broadcasted_iota(jnp.int32, (rows, rows), 1)
        upto = (from_row <= to_lane).astype(jnp.bfloat16)
        ahead = jnp.dot(
            jnp.broadcast_to(chosen.astype(jnp.float32), (8, rows)).astype(jnp.bfloat16),
            upto,
            preferred_element_type=jnp.float32,
        )[:1].astype(jnp.int32)
        place = jnp.where(chosen, ahead - 1, CAP + to_lane[:1] - ahead)
        perm = (from_row == place).astype(jnp.float32).astype(jnp.bfloat16)
        perm_ref[...] = perm
        out_ref[:rows] = jnp.dot(perm, sig_ref[...], preferred_element_type=jnp.float32).astype(
            jnp.bfloat16
        )
        out_ref[rows : 2 * rows] = jnp.dot(
            perm, cot_ref[...], preferred_element_type=jnp.float32
        ).astype(jnp.bfloat16)
        sorted_ids = lax.dot_general(
            jnp.broadcast_to(ids_row, (ID_ROWS, rows)).astype(jnp.bfloat16),
            perm,
            (((1,), (1,)), ((), ())),
            preferred_element_type=jnp.float32,
        ).astype(jnp.bfloat16)
        out_ref[2 * rows :, :rows] = sorted_ids
        out_ref[2 * rows :, rows:] = jnp.zeros((ID_ROWS, SITES - rows), jnp.bfloat16)

    return pl.pallas_call(
        body,
        out_shape=(
            jax.ShapeDtypeStruct((2 * rows + ID_ROWS, SITES), jnp.bfloat16),
            jax.ShapeDtypeStruct((rows, rows), jnp.bfloat16),
        ),
        in_specs=[vmem(), vmem(), vmem()],
        out_specs=(vmem(), vmem()),
        compiler_params=params(),
        name="pack_rows",
    )(ids, signals, cotangent)


def local_grads(pos, touched, slot_map, mine, other, blocks, n_own, half, piece, width):
    planes = mine.shape[0]
    rows = (mine.shape[1] - ID_ROWS) // 2
    touch = touched.shape[1]
    aligned = piece % 16 == 0
    part = half // CHUNKS

    def body(pos_ref, touched_ref, slot_ref, mine_ref, other_ref, blocks_ref, *rest):
        pred_mine, pred_other = rest[:2]
        grad_refs = rest[2 : 2 + CHUNKS]
        rest = rest[2 + CHUNKS :]
        if aligned:
            acc, id_cols, held, sems = rest
            copies = [
                pltpu.make_async_copy(
                    blocks_ref.at[s], held.at[:, :, pl.ds(s * piece, piece), :], sems.at[s]
                )
                for s in range(n_own)
            ]
            for copy in copies:
                copy.start()
        else:
            acc, id_cols = rest
            held = blocks_ref

        def clear(e, _):
            acc[e] = jnp.zeros(acc.shape[1:], jnp.float32)
            return 0

        lax.fori_loop(0, half, clear, 0)
        pred_mine[...] = jnp.zeros_like(pred_mine)
        pred_other[...] = jnp.zeros_like(pred_other)
        own_at = pos_ref[1]
        core = lax.rem(own_at, 2)
        partner = own_at + 1 - 2 * core
        for which, ref in enumerate((mine_ref, other_ref)):
            for p in range(planes):
                ids_row = ref[p, 2 * rows :, :rows][:1].astype(jnp.float32)
                id_cols[which, p] = jnp.broadcast_to(ids_row, (128, rows)).T
        if aligned:
            for copy in copies:
                copy.wait()
        for which, (ref, pred) in enumerate(((mine_ref, pred_mine), (other_ref, pred_other))):
            source = own_at if which == 0 else partner

            def plane(p, _, which=which, ref=ref, pred=pred, source=source):
                full = jnp.max(id_cols[which, p, :8, :]).astype(jnp.int32)

                def task(j, _):
                    insertion = jnp.where(
                        j == 0, full, touched_ref[p * n_own + source, jnp.maximum(j - 1, 0)]
                    )
                    stored = slot_ref[insertion]
                    here = stored // half == core
                    here = here & ((j == 0) | (insertion != full))
                    first = pl.multiple_of(jnp.where(j == 0, 0, CAP), CAP)

                    @pl.when(here)
                    def _():
                        e = lax.rem(stored, half)
                        keep = (
                            (id_cols[which, p, pl.ds(first, CAP), :] == insertion.astype(jnp.float32))
                            .astype(jnp.float32)
                            .astype(jnp.bfloat16)
                        )
                        keep = jnp.concatenate([keep] * (SITES // 128), axis=1)
                        sig = ref[p, pl.ds(first, CAP), :] * keep
                        cot = ref[p, pl.ds(rows + first, CAP), :] * keep
                        read_in = held[e, 0]
                        read_out = held[e, 1]
                        preact = jnp.dot(sig, read_in, preferred_element_type=jnp.float32)
                        back_hidden = jnp.dot(cot, read_out, preferred_element_type=jnp.float32)
                        gelu_val, slopes = gelu_parts(preact)
                        hidden = gelu_val.astype(jnp.bfloat16)
                        back_pre = (back_hidden * slopes).astype(jnp.bfloat16)
                        pred[p, pl.ds(first, CAP), :] += lax.dot_general(
                            hidden,
                            read_out,
                            (((1,), (1,)), ((), ())),
                            preferred_element_type=jnp.float32,
                        ).astype(jnp.bfloat16)
                        acc[e, 0] += lax.dot_general(
                            sig,
                            back_pre,
                            (((0,), (0,)), ((), ())),
                            preferred_element_type=jnp.float32,
                        )
                        acc[e, 1] += lax.dot_general(
                            cot,
                            hidden,
                            (((0,), (0,)), ((), ())),
                            preferred_element_type=jnp.float32,
                        )

                    return 0

                return lax.fori_loop(0, touch + 1, task, 0)

            lax.fori_loop(0, planes, plane, 0)

        for chunk, grad_ref in enumerate(grad_refs):

            def write(e, _, chunk=chunk, grad_ref=grad_ref):
                if aligned:
                    for s in range(n_own):
                        grad_ref[s, e] = acc[
                            chunk * part + e, :, s * piece : (s + 1) * piece, :
                        ].astype(jnp.bfloat16)
                else:
                    grad_ref[e] = acc[chunk * part + e].astype(jnp.bfloat16)
                return 0

            lax.fori_loop(0, part, write, 0)

    grad_shape = (n_own, part, 2, piece, width) if aligned else (part, 2, SITES, width)
    pred_shape = jax.ShapeDtypeStruct((planes, rows, SITES), jnp.bfloat16)
    scratch = [
        pltpu.VMEM((half, 2, SITES, width), jnp.float32),
        pltpu.VMEM((2, planes, rows, 128), jnp.float32),
    ]
    if aligned:
        scratch += [
            pltpu.VMEM((half, 2, SITES, width), jnp.bfloat16),
            pltpu.SemaphoreType.DMA((n_own,)),
        ]
    else:
        blocks = blocks.transpose(1, 2, 0, 3, 4).reshape(half, 2, SITES, width)
    found = pl.pallas_call(
        body,
        out_shape=(pred_shape, pred_shape)
        + (jax.ShapeDtypeStruct(grad_shape, jnp.bfloat16),) * CHUNKS,
        in_specs=[smem(), smem(), smem(), vmem(), vmem()]
        + [pl.BlockSpec(memory_space=pl.ANY) if aligned else vmem()],
        out_specs=(vmem(),) * (2 + CHUNKS),
        scratch_shapes=scratch,
        compiler_params=params(),
        name="local_grads",
    )(pos, touched, slot_map, mine, other, blocks)
    grads = found[2:]
    if not aligned:
        grads = [
            g.reshape(part, 2, n_own, piece, width).transpose(2, 0, 1, 3, 4) for g in grads
        ]
    return found[0], found[1], grads


def adam(pos, arrived, weights, moment1, moment2, half):
    n_own, part, _, piece, width = arrived.shape
    chips = n_own // 2
    blocks = arrived.reshape(chips, 2, part, 2, piece, width)
    correct_one = 1.0 - 0.9**10
    correct_two = 1.0 - 0.999**10

    def body(pos_ref, arrived_ref, w_ref, m1_ref, m2_ref, new_w, new_m1, new_m2):
        gradient = arrived_ref[0, 0].astype(jnp.float32)
        for s in range(1, chips):
            gradient = gradient + arrived_ref[s, 0].astype(jnp.float32)
        one = 0.9 * m1_ref[...] + 0.1 * gradient
        two = 0.999 * m2_ref[...] + 0.001 * gradient * gradient
        new_m1[...] = one
        new_m2[...] = two
        updated = w_ref[...].astype(jnp.float32) - learn_rate * (one / correct_one) / (
            jnp.sqrt(two / correct_two) + 1e-08
        )
        new_w[...] = updated.astype(jnp.bfloat16)

    def plain(c, i, pos_ref):
        return (c * half + i, 0, 0, 0)

    small = pl.BlockSpec((1, 2, piece, width), plain)
    grid_spec = pltpu.PrefetchScalarGridSpec(
        num_scalar_prefetch=1,
        grid=(2, part),
        in_specs=[
            pl.BlockSpec((chips, 1, 1, 2, piece, width), lambda c, i, pos_ref: (0, c, i, 0, 0, 0)),
            pl.BlockSpec(
                (1, 2, piece, width), lambda c, i, pos_ref: (c * half + i, 0, 0, pos_ref[0])
            ),
            small,
            small,
        ],
        out_specs=(small, small, small),
    )

    def wrapped(pos_ref, arrived_ref, *refs):
        body(pos_ref, arrived_ref.at[:, :, 0], *[r.at[0] for r in refs])

    return pl.pallas_call(
        wrapped,
        out_shape=(
            jax.ShapeDtypeStruct(moment1.shape, jnp.bfloat16),
            jax.ShapeDtypeStruct(moment1.shape, jnp.float32),
            jax.ShapeDtypeStruct(moment1.shape, jnp.float32),
        ),
        grid_spec=grid_spec,
        compiler_params=params(),
        name="adam_step",
    )(pos, blocks, weights, moment1, moment2)


def finish_predicted(perm, parts):
    def body(perm_ref, *refs):
        total = refs[0][...].astype(jnp.float32)
        for ref in refs[1:-1]:
            total = total + ref[...].astype(jnp.float32)
        refs[-1][...] = lax.dot_general(
            perm_ref[...],
            total.astype(jnp.bfloat16),
            (((0,), (0,)), ((), ())),
            preferred_element_type=jnp.float32,
        ).astype(jnp.bfloat16)

    return pl.pallas_call(
        body,
        out_shape=jax.ShapeDtypeStruct(parts[0].shape, jnp.bfloat16),
        in_specs=[vmem()] * (1 + len(parts)),
        out_specs=vmem(),
        compiler_params=params(),
        name="finish_predicted",
    )(perm, *parts)


def shards(signals, cotangent, row_insertion, touched, slot_map, weights, moment1, moment2):
    n_own = lax.axis_size("own")
    n_dp = lax.axis_size("dp")
    dp_at = lax.axis_index("dp")
    own_at = lax.axis_index("own")
    number, _, piece, _ = weights.shape
    width = moment1.shape[3]
    half = number // 2
    rows = signals.shape[0]
    pos = jnp.stack([dp_at, own_at]).astype(jnp.int32)
    swap = [(o, o ^ 1) for o in range(n_own)]

    column = lax.dynamic_slice_in_dim(weights, dp_at * width, width, 3)
    outgoing = jnp.broadcast_to(
        column.reshape(1, 2, half, 2, piece, width), (n_own // 2, 2, half, 2, piece, width)
    ).reshape(n_own, half, 2, piece, width)
    blocks = lax.all_to_all(outgoing, "own", split_axis=0, concat_axis=0, tiled=True)

    packed, perm = pack_rows(row_insertion.reshape(1, rows), signals, cotangent)
    mine = lax.all_gather(packed, "dp", axis=0)
    other = lax.ppermute(mine, "own", swap)

    pred_mine, pred_other, grads = local_grads(
        pos, touched, slot_map, mine, other, blocks, n_own, half, piece, width
    )
    arrived = lax.all_to_all(grads[0], "own", split_axis=0, concat_axis=0, tiled=True)
    fresh, new_moment1, new_moment2 = adam(pos, arrived, weights, moment1, moment2, half)
    new_weights = lax.all_gather(fresh, "dp", axis=3, tiled=True)

    pred_part = pred_mine + lax.ppermute(pred_other, "own", swap)
    parts = [lax.dynamic_index_in_dim(pred_part, dp_at, 0, keepdims=False)]
    for shift in range(1, n_dp):
        block = lax.dynamic_index_in_dim(pred_part, lax.rem(dp_at + shift, n_dp), 0, keepdims=False)
        parts.append(lax.ppermute(block, "dp", [(d, (d + shift) % n_dp) for d in range(n_dp)]))
    predicted = finish_predicted(perm, parts)
    return (predicted, new_weights, new_moment1, new_moment2)


def solution(mesh):
    in_specs = (
        P(("dp", "own"), None),
        P(("dp", "own"), None),
        P(("dp", "own")),
        P(),
        P(),
        P(None, None, "own", None),
        P(None, None, "own", "dp"),
        P(None, None, "own", "dp"),
    )
    out_specs = (
        P(("dp", "own"), None),
        P(None, None, "own", None),
        P(None, None, "own", "dp"),
        P(None, None, "own", "dp"),
    )
    return jax.shard_map(shards, mesh=mesh, in_specs=in_specs, out_specs=out_specs, check_vma=False)
```

time: 728 us -> 220 us (0.30)
  blocking collectives: 284 us -> 42.8 us
  waiting for transfers between devices: 247 us -> 104 us
  local copies, waits for them, and re-layouts: 116 us -> 11.1 us
  Pallas kernels: 0 us -> 33.4 us
  matrix products: 31.2 us -> 0 us
  other arithmetic: 22.4 us -> 0.8 us
    all_to_all x1, blocking collectives: 284 us -> 42.8 us  [shards(): lax.all_to_all(grads[0], 'own', split_axis=0, concat_axis=0, tiled=True)]
    all_to_all x2 -> x1, waiting for transfers between devices: 196 us -> 3.04 us  [shards(): lax.all_to_all(outgoing, 'own', split_axis=0, concat_axis=0, tiled=True)]
    all_to_all x4 -> x0, local copies, waits for them, and re-layouts: 50.1 us -> none  [the longest x2 27.3 us: shards(): lax.all_to_all(lax.all_to_all(grads[None, None], 'dp', split_axis=5, conc...]
    pallas_call x0 -> x4, Pallas kernels: none -> 33.4 us  [the longest x1 16.9 us: local_grads(): pl.pallas_call(body, out_shape=(pred_shape, pred_shape) + (jax.ShapeDtype...]
    dot_general x5 -> x0, matrix products: 31.2 us -> none  [the longest x1 12.2 us: sum_by_insertion(): jnp.dot(one_hot, flat_grad, precision=highest, preferred_element_type=jnp...]
    ppermute x0 -> x5, waiting for transfers between devices: none -> 26.7 us  [the longest x3 24.5 us: shards(): lax.ppermute(block, 'dp', [(d, (d + shift) % n_dp) for d in range(n_dp)])]
    all_gather x1 -> x2, waiting for transfers between devices: 51.3 us -> 74.3 us  [the longest x1 42.3 us: shards(): new_weights = lax.all_gather(fresh, 'dp', axis=3, tiled=True)]
    broadcast_in_dim x1, local copies, waits for them, and re-layouts: 14.8 us -> 2.05 us  [shards(): jnp.broadcast_to(column.reshape(1, 2, half, 2, piece, width), (n_own // 2...]
  transfers between devices with their start and end apart: 3 -> 8, of which waited for: 3 -> 6; matrix products, arithmetic and copies ran while one was open for 3% -> 3% of each run, Pallas kernels for 0% -> 1%
where the time goes in v1:
time: 220 us; the launch traced here: 216 us
  waiting for transfers between devices  104 us (47%)
  blocking collectives  42.8 us (19%)
  Pallas kernels  33.4 us (15%)
  between operations  14.1 us (6%)
  local copies, waits for them, and re-layouts  11.1 us (5%)
  starting transfers between devices  10 us (5%)
    all_to_all x1, blocking collectives, shards(): lax.all_to_all(grads[0], 'own', split_axis=0, concat_axis=0, tiled=True)  42.8 us
    all_gather x1, waiting for transfers between devices, shards(): new_weights = lax.all_gather(fresh, 'dp', axis=3, tiled=True)  42.3 us
    all_gather x1, waiting for transfers between devices, shards(): mine = lax.all_gather(packed, 'dp', axis=0)  32 us
    ppermute x3, waiting for transfers between devices, shards(): lax.ppermute(block, 'dp', [(d, (d + shift) % n_dp) for d in range(n_dp)])  24.5 us
    pallas_call x1, Pallas kernels, local_grads(): pl.pallas_call(body, out_shape=(pred_shape, pred_shape) + (jax.ShapeDtype...  16.9 us
    pallas_call x1, Pallas kernels, adam(): pl.pallas_call(wrapped, out_shape=(jax.ShapeDtypeStruct(moment1.shape, jn...  11.9 us
    unnamed x16, local copies, waits for them, and re-layouts  7.14 us
    ppermute x3, starting transfers between devices, shards(): lax.ppermute(block, 'dp', [(d, (d + shift) % n_dp) for d in range(n_dp)])  5.52 us
  transfers between devices with their start and end apart: 8, of which 6 were waited for; matrix products, arithmetic and copies ran while one was open for 3% of the time, Pallas kernels for 1%

profile of v1, /device:TPU:2, one launch (start us, length us, event | category | flops | bytes accessed | tf_op | source)
XLA Modules:
  0.0 216.4 jit_solution(5011089153706903651)
XLA Ops:
  7.2 0.0 all-gather.6.cloned.1.call-start
  7.2 2.4 %pack_rows.1 = (bf16[528,384]{1,0:T(8,128)(2,1)}, bf16[256,256]{1,0:T(8,128)(2,1)}) custom-call(s32[1,256]{1,0:T(1,128)} %bitcast.20, bf16[256,384]{1,0:T(8,128)(2,1)} %sig_ref.1, bf16[256,384]{1,0:T(8,128)(2,1)} %cot_ref.1), custom_call_target="tpu_custom_call" | custom-call | tf_op jit(solution)/shard_map/pack_rows/pallas_call | solution.py:79
  9.6 0.0 all-gather.6.cloned.1.call-update
  9.6 1.2 constant_dynamic-slice_fusion
  10.8 2.0 broadcast_in_dim.8
  12.9 0.0 copy-start.5
  12.9 4.4 %all-to-all-start = ((bf16[8,8,2,48,256]{4,3,2,1,0:T(8,128)(2,1)}), bf16[8,8,2,48,256]{4,3,2,1,0:T(8,128)(2,1)S(1)}, u32[]{:S(2)}, u32[]{:S(2)}) async-start(bf16[8,8,2,48,256]{4,3,2,1,0:T(8,128)(2,1)} %bitcast.15), calls=%async_computation | async-start | bytes 6291456 | tf_op jit(solution)/shard_map/all_to_all | solution.py:330
  17.3 0.0 all-gather.4.cloned.1.call-start
  17.3 32.0 %all-gather.6.cloned.1.call-done = bf16[2112,384]{1,0:T(8,128)(2,1)} async-done(((bf16[528,384]{1,0:T(8,128)(2,1)}), bf16[2112,384]{1,0:T(8,128)(2,1)}) %all-gather.6.cloned.1.call-update) | async-done | bytes 1622032 | tf_op jit(solution)/shard_map/all_gather | solution.py:333
  49.3 0.0 collective-permute-start
  49.3 0.0 copy-done.5
  49.3 0.7 copy.12.touched_ref
  50.0 0.6 pad_add_fusion.pos_ref
  50.6 3.0 %all-to-all-done.blocks_ref = bf16[8,8,2,48,256]{4,3,2,1,0:T(8,128)(2,1)S(1)} async-done(((bf16[8,8,2,48,256]{4,3,2,1,0:T(8,128)(2,1)}), bf16[8,8,2,48,256]{4,3,2,1,0:T(8,128)(2,1)S(1)}, u32[]{:S(2)}, u32[]{:S(2)}) %all-to-all-start) | async-done | bytes 3145760 | tf_op jit(solution)/shard_map/all_to_all | solution.py:330
  53.6 0.0 copy-start
  53.6 0.0 collective-permute-done.other_ref
  53.7 1.7 copy-done
  55.3 16.9 %local_grads.1 = (bf16[4,256,384]{2,1,0:T(8,128)(2,1)}, bf16[4,256,384]{2,1,0:T(8,128)(2,1)}, bf16[8,8,2,48,256]{4,3,2,1,0:T(8,128)(2,1)}) custom-call(s32[2]{0:T(128)} %pad_add_fusion.pos_ref, s32[32,4]{1,0:T(8,128)} %copy.12.touched_ref, s32[16]{0:T(128)} %slot_ref.1, bf16[4,528,384]{2,1,0:T(8,128)(2,1)} %bitcast.19, ...), custom_call_target="tpu_custom_call" | custom-call | tf_op jit(solution)/shard_map/local_grads/pallas_call | solution.py:219
  72.2 42.8 %all_to_all.10 = bf16[8,8,2,48,256]{4,3,2,1,0:T(8,128)(2,1)} all-to-all(bf16[8,8,2,48,256]{4,3,2,1,0:T(8,128)(2,1)} %get-tuple-element.16), channel_id=1, replica_groups=mesh['dp'=4,'own'=8] {'own'}, dimensions={0} | all-to-all | bytes 6291456 | tf_op jit(solution)/shard_map/all_to_all | solution.py:339
  115.0 0.0 copy-start.6
  115.0 0.0 copy-start.1
  115.0 11.9 %adam_step.1 = (bf16[16,2,48,256]{3,2,1,0:T(8,128)(2,1)}, f32[16,2,48,256]{3,2,1,0:T(8,128)}, f32[16,2,48,256]{3,2,1,0:T(8,128)}) custom-call(s32[2]{0:T(128)} %pad_add_fusion.pos_ref, bf16[4,2,8,2,48,256]{5,4,3,2,1,0:T(8,128)(2,1)} %bitcast.16, bf16[16,2,48,1024]{3,2,1,0:T(8,128)(2,1)} %refs_0_.1, f32[16,2,48,256]{3,2,1,0:T(8,128)} %refs_1_.1, ...), custom_call_target="tpu_custom_call" | custom-call | tf_op jit(solution)/shard_map/adam_step/pallas_call | solution.py:279
  126.9 0.0 all-gather.4.cloned.1.call-update
  127.0 0.0 copy-done.6
  127.0 0.1 collective-permute-start.1
  127.1 2.3 %collective-permute-done.1 = bf16[4,256,384]{2,1,0:T(8,128)(2,1)S(1)} collective-permute-done((bf16[4,256,384]{2,1,0:T(8,128)(2,1)S(1)}, bf16[4,256,384]{2,1,0:T(8,128)(2,1)S(1)}, u32[]{:S(2)}, u32[]{:S(2)}) %collective-permute-start.1) | collective-permute-done | bytes 786464 | tf_op jit(solution)/shard_map/ppermute | solution.py:343
  129.3 0.0 copy-done.1
  129.3 0.2 add.29
  129.5 0.8 dynamic-slice_bitcast_fusion
  130.3 1.6 collective-permute-start.2
  131.9 2.6 %collective-permute-start.3 = (bf16[256,384]{1,0:T(8,128)(2,1)S(1)}, bf16[256,384]{1,0:T(8,128)(2,1)S(1)}, u32[]{:S(2)}, u32[]{:S(2)}) collective-permute-start(bf16[256,384]{1,0:T(8,128)(2,1)S(1)} %get-tuple-element.21), channel_id=1, source_target_pairs={{0,16},{8,24},{16,0},{24,8},{1,17},{9,25},{17,1},{25,9},{2,18},{10... | collective-permute-start | bytes 589832 | tf_op jit(solution)/shard_map/ppermute | solution.py:347
  134.5 1.3 collective-permute-start.4
  135.8 4.2 %collective-permute-done.2.refs_1_ = bf16[256,384]{1,0:T(8,128)(2,1)S(1)} collective-permute-done((bf16[256,384]{1,0:T(8,128)(2,1)S(1)}, bf16[256,384]{1,0:T(8,128)(2,1)S(1)}, u32[]{:S(2)}, u32[]{:S(2)}) %collective-permute-start.2) | collective-permute-done | bytes 196640 | tf_op jit(solution)/shard_map/ppermute | solution.py:347
  140.0 0.0 copy-start.2
  140.0 20.3 %collective-permute-done.3.refs_2_ = bf16[256,384]{1,0:T(8,128)(2,1)S(1)} collective-permute-done((bf16[256,384]{1,0:T(8,128)(2,1)S(1)}, bf16[256,384]{1,0:T(8,128)(2,1)S(1)}, u32[]{:S(2)}, u32[]{:S(2)}) %collective-permute-start.3) | collective-permute-done | bytes 196640 | tf_op jit(solution)/shard_map/ppermute | solution.py:347
  160.3 0.0 copy-start.3
  160.3 0.0 collective-permute-done.4.refs_3_
  160.3 0.0 copy-start.4
  160.3 0.0 copy-done.2
  160.3 0.7 copy-done.3
  161.0 0.1 copy-done.4
  161.0 2.2 %finish_predicted.1 = bf16[256,384]{1,0:T(8,128)(2,1)} custom-call(bf16[256,256]{1,0:T(8,128)(2,1)} %get-tuple-element.12.perm_ref, bf16[256,384]{1,0:T(8,128)(2,1)} %get-tuple-element.23.refs_0_, bf16[256,384]{1,0:T(8,128)(2,1)} %copy-done.2, bf16[256,384]{1,0:T(8,128)(2,1)} %copy-done.3, bf16[256,384]{1,0:T(8,128)(2,1)} %copy-done.4), custom_call_target="tpu_custom_call" | custom-call | tf_op jit(solution)/shard_map/finish_predicted/pallas_call | solution.py:304
  163.2 42.3 %all-gather.4.cloned.1.call-done = bf16[16,2,48,1024]{3,2,1,0:T(8,128)(2,1)} async-done(((bf16[16,2,48,256]{3,2,1,0:T(8,128)(2,1)}), bf16[16,2,48,1024]{3,2,1,0:T(8,128)(2,1)}) %all-gather.4.cloned.1.call-update) | async-done | bytes 3145744 | tf_op jit(solution)/shard_map/all_gather | solution.py:341
  205.5 4.0 %copy.14 = bf16[16,2,48,1024]{3,2,1,0:T(8,128)(2,1)} copy(bf16[16,2,48,1024]{3,2,1,0:T(8,128)(2,1)} %all-gather.4.cloned.1.call-done) | data formatting | bytes 6291456
Async XLA Ops:
  7.2 42.1 %all-gather.6.cloned.1.call-start = ((), (), s32[]{:S(2)}) async-start(), calls=%async_computation.3 | async-start | bytes 2027520 | tf_op jit(solution)/shard_map/all_gather | solution.py:333
  12.9 36.4 %copy-start.5 = (s32[32,4]{0,1:T(4,128)S(1)}, s32[32,4]{0,1:T(4,128)}, u32[]{:S(2)}) copy-start(s32[32,4]{0,1:T(4,128)} %param.11) | copy-start | bytes 1540
  12.9 40.8 %all-to-all-start = ((bf16[8,8,2,48,256]{4,3,2,1,0:T(8,128)(2,1)}), bf16[8,8,2,48,256]{4,3,2,1,0:T(8,128)(2,1)S(1)}, u32[]{:S(2)}, u32[]{:S(2)}) async-start(bf16[8,8,2,48,256]{4,3,2,1,0:T(8,128)(2,1)} %bitcast.15), calls=%async_computation | async-start | bytes 6291456 | tf_op jit(solution)/shard_map/all_to_all | solution.py:330
  17.3 188.3 %all-gather.4.cloned.1.call-start = ((), (), s32[]{:S(2)}) async-start(), calls=%async_computation.2 | async-start | bytes 3932160 | tf_op jit(solution)/shard_map/all_gather | solution.py:341
  49.3 4.3 %collective-permute-start = (bf16[4,528,384]{2,1,0:T(8,128)(2,1)}, bf16[4,528,384]{2,1,0:T(8,128)(2,1)}, u32[]{:S(2)}, u32[]{:S(2)}) collective-permute-start(bf16[4,528,384]{2,1,0:T(8,128)(2,1)} %bitcast.18), channel_id=1, source_target_pairs={{0,1},{1,0},{2,3},{3,2},{4,5},{5,4},{6,7},{7,6},{8,9},{9,8},{10,11... | collective-permute-start | bytes 4866056 | tf_op jit(solution)/shard_map/ppermute | solution.py:334
  53.6 1.7 copy-start
  115.0 11.9 %copy-start.6 = (bf16[4,256,384]{2,1,0:T(8,128)(2,1)S(1)}, bf16[4,256,384]{2,1,0:T(8,128)(2,1)}, u32[]{:S(2)}) copy-start(bf16[4,256,384]{2,1,0:T(8,128)(2,1)} %get-tuple-element.15) | copy-start | bytes 2359300
  115.0 14.3 %copy-start.1 = (bf16[4,256,384]{2,1,0:T(8,128)(2,1)S(1)}, bf16[4,256,384]{2,1,0:T(8,128)(2,1)}, u32[]{:S(2)}) copy-start(bf16[4,256,384]{2,1,0:T(8,128)(2,1)} %get-tuple-element.14) | copy-start | bytes 2359300
  127.0 2.4 %collective-permute-start.1 = (bf16[4,256,384]{2,1,0:T(8,128)(2,1)S(1)}, bf16[4,256,384]{2,1,0:T(8,128)(2,1)S(1)}, u32[]{:S(2)}, u32[]{:S(2)}) collective-permute-start(bf16[4,256,384]{2,1,0:T(8,128)(2,1)S(1)} %copy-done.6), channel_id=1, source_target_pairs={{0,1},{1,0},{2,3},{3,2},{4,5},{5,4},{6,7},{7,6},{8,9},{9,8},{10,11... | collective-permute-start | bytes 2359304 | tf_op jit(solution)/shard_map/ppermute | solution.py:343
  130.3 9.7 %collective-permute-start.2 = (bf16[256,384]{1,0:T(8,128)(2,1)S(1)}, bf16[256,384]{1,0:T(8,128)(2,1)S(1)}, u32[]{:S(2)}, u32[]{:S(2)}) collective-permute-start(bf16[256,384]{1,0:T(8,128)(2,1)S(1)} %get-tuple-element.22), channel_id=1, source_target_pairs={{0,8},{8,16},{16,24},{24,0},{1,9},{9,17},{17,25},{25,1},{2,10},{10... | collective-permute-start | bytes 589832 | tf_op jit(solution)/shard_map/ppermute | solution.py:347
  131.9 28.4 %collective-permute-start.3 = (bf16[256,384]{1,0:T(8,128)(2,1)S(1)}, bf16[256,384]{1,0:T(8,128)(2,1)S(1)}, u32[]{:S(2)}, u32[]{:S(2)}) collective-permute-start(bf16[256,384]{1,0:T(8,128)(2,1)S(1)} %get-tuple-element.21), channel_id=1, source_target_pairs={{0,16},{8,24},{16,0},{24,8},{1,17},{9,25},{17,1},{25,9},{2,18},{10... | collective-permute-start | bytes 589832 | tf_op jit(solution)/shard_map/ppermute | solution.py:347
  134.5 25.8 %collective-permute-start.4 = (bf16[256,384]{1,0:T(8,128)(2,1)S(1)}, bf16[256,384]{1,0:T(8,128)(2,1)S(1)}, u32[]{:S(2)}, u32[]{:S(2)}) collective-permute-start(bf16[256,384]{1,0:T(8,128)(2,1)S(1)} %get-tuple-element.20), channel_id=1, source_target_pairs={{0,24},{8,0},{16,8},{24,16},{1,25},{9,1},{17,9},{25,17},{2,26},{10... | collective-permute-start | bytes 589832 | tf_op jit(solution)/shard_map/ppermute | solution.py:347
  140.0 20.3 %copy-start.2 = (bf16[256,384]{1,0:T(8,128)(2,1)}, bf16[256,384]{1,0:T(8,128)(2,1)S(1)}, u32[]{:S(2)}) copy-start(bf16[256,384]{1,0:T(8,128)(2,1)S(1)} %collective-permute-done.2.refs_1_) | copy-start | bytes 589828
  160.3 0.7 copy-start.3
  160.3 0.7 copy-start.4
Sparse Core Ops, SparseCore 0:
  10.1 39.1 all-gather.5
  127.1 78.3 all-gather.3

commit v2 on v1

v2 whole, which is shorter than its diff:
```python
import math

import jax
import jax.numpy as jnp
from jax import lax
from jax.experimental import pallas as pl
from jax.experimental.pallas import tpu as pltpu
from jax.sharding import PartitionSpec as P

SITES = 384
CAP = 128
CHUNK_PARTS = (2, 2, 2, 2)
ID_ROWS = 16
VMEM_BYTES = 56 * 2**20

gelu_coef = math.sqrt(2.0 / math.pi)
cubic_coef = 0.044715
learn_rate = 0.01


def gelu_parts(preact):
    tanh_input = gelu_coef * (preact + cubic_coef * preact * preact * preact)
    tangent = jnp.tanh(tanh_input)
    gelu_val = 0.5 * preact * (1.0 + tangent)
    slopes = 0.5 * (1.0 + tangent) + 0.5 * preact * (1.0 - tangent * tangent) * gelu_coef * (
        1.0 + 3.0 * cubic_coef * preact * preact
    )
    return (gelu_val, slopes)


def params():
    return pltpu.CompilerParams(vmem_limit_bytes=VMEM_BYTES)


def vmem():
    return pl.BlockSpec(memory_space=pltpu.VMEM)


def smem():
    return pl.BlockSpec(memory_space=pltpu.SMEM)


def pack_rows(ids, signals, cotangent):
    rows = signals.shape[0]

    def body(ids_ref, sig_ref, cot_ref, out_ref, perm_ref):
        ids_row = ids_ref[...].astype(jnp.float32)
        lane_ids = jnp.broadcast_to(ids_row, (rows, rows))
        same = lane_ids == lane_ids.T
        count = jnp.sum(same.astype(jnp.float32), axis=0, keepdims=True)
        full = jnp.max(jnp.where(count == CAP, ids_row, -1.0), axis=1, keepdims=True)
        chosen = ids_row == full
        from_row = lax.broadcasted_iota(jnp.int32, (rows, rows), 0)
        to_lane = lax.broadcasted_iota(jnp.int32, (rows, rows), 1)
        upto = (from_row <= to_lane).astype(jnp.bfloat16)
        ahead = jnp.dot(
            jnp.broadcast_to(chosen.astype(jnp.float32), (8, rows)).astype(jnp.bfloat16),
            upto,
            preferred_element_type=jnp.float32,
        )[:1].astype(jnp.int32)
        place = jnp.where(chosen, ahead - 1, CAP + to_lane[:1] - ahead)
        perm = (from_row == place).astype(jnp.float32).astype(jnp.bfloat16)
        perm_ref[...] = perm
        out_ref[:rows] = jnp.dot(perm, sig_ref[...], preferred_element_type=jnp.float32).astype(
            jnp.bfloat16
        )
        out_ref[rows : 2 * rows] = jnp.dot(
            perm, cot_ref[...], preferred_element_type=jnp.float32
        ).astype(jnp.bfloat16)
        sorted_ids = lax.dot_general(
            jnp.broadcast_to(ids_row, (ID_ROWS, rows)).astype(jnp.bfloat16),
            perm,
            (((1,), (1,)), ((), ())),
            preferred_element_type=jnp.float32,
        ).astype(jnp.bfloat16)
        out_ref[2 * rows :, :rows] = sorted_ids
        out_ref[2 * rows :, rows:] = jnp.zeros((ID_ROWS, SITES - rows), jnp.bfloat16)

    return pl.pallas_call(
        body,
        out_shape=(
            jax.ShapeDtypeStruct((2 * rows + ID_ROWS, SITES), jnp.bfloat16),
            jax.ShapeDtypeStruct((rows, rows), jnp.bfloat16),
        ),
        in_specs=[vmem(), vmem(), vmem()],
        out_specs=(vmem(), vmem()),
        compiler_params=params(),
        name="pack_rows",
    )(ids, signals, cotangent)


def local_grads(pos, touched, slot_map, mine, other, blocks, sizes, piece, width):
    planes = mine.shape[0]
    rows = (mine.shape[1] - ID_ROWS) // 2
    touch = touched.shape[1]
    n_own = len(blocks)
    half = sum(sizes)
    aligned = piece % 16 == 0
    starts = [sum(sizes[:i]) for i in range(len(sizes))]
    n_blocks = n_own if aligned else 1
    n_grads = len(sizes) * n_blocks

    def body(pos_ref, touched_ref, slot_ref, mine_ref, other_ref, *rest):
        block_refs = rest[:n_blocks]
        pred_refs = rest[n_blocks : n_blocks + 2]
        grad_refs = rest[n_blocks + 2 : n_blocks + 2 + n_grads]
        acc, id_cols, held, sorted_rows, pred, full_of, tasks, sems = rest[n_blocks + 2 + n_grads :]
        own_at = pos_ref[1]
        core = lax.rem(own_at, 2)
        partner = own_at + 1 - 2 * core
        row_copies = [
            pltpu.make_async_copy(
                ref, sorted_rows.at[pl.ds(which * planes, planes)], sems.at[which]
            )
            for which, ref in enumerate((mine_ref, other_ref))
        ]
        if aligned:
            block_copies = [
                pltpu.make_async_copy(
                    ref,
                    held.at[
                        :, :, pl.ds(pl.multiple_of((own_at ^ j) * piece, 16), piece), :
                    ],
                    sems.at[2 + j],
                )
                for j, ref in enumerate(block_refs)
            ]
        else:
            block_copies = [pltpu.make_async_copy(block_refs[0], held, sems.at[2])]
        for copy in row_copies + block_copies:
            copy.start()

        def clear(e, _):
            acc[e] = jnp.zeros(acc.shape[1:], jnp.float32)
            return 0

        lax.fori_loop(0, half, clear, 0)
        pred[...] = jnp.zeros_like(pred)
        for copy in row_copies:
            copy.wait()
        for source in range(2 * planes):
            ids_row = sorted_rows[source, 2 * rows :, :rows][:1].astype(jnp.float32)
            id_cols[source] = jnp.broadcast_to(ids_row, (128, rows)).T
            full_of[source] = jnp.max(ids_row[:, :128]).astype(jnp.int32)

        def listing(t, count):
            source = t // (touch + 1)
            j = t - source * (touch + 1)
            which = source // planes
            device = (source - which * planes) * n_own + jnp.where(which == 0, own_at, partner)
            full = full_of[source]
            insertion = jnp.where(j == 0, full, touched_ref[device, jnp.maximum(j - 1, 0)])
            stored = slot_ref[insertion]
            here = (stored // half == core) & ((j == 0) | (insertion != full))
            tasks[0, count] = source
            tasks[1, count] = jnp.where(j == 0, 0, CAP)
            tasks[2, count] = insertion
            tasks[3, count] = stored - core * half
            return count + here.astype(jnp.int32)

        count = lax.fori_loop(0, 2 * planes * (touch + 1), listing, 0)
        tasks[0, count] = 0
        tasks[1, count] = 0
        tasks[2, count] = -1
        tasks[3, count] = 0
        for copy in block_copies:
            copy.wait()

        def pair(i, _):
            loaded = []
            for u in range(2):
                source, insertion, e = tasks[0, 2 * i + u], tasks[2, 2 * i + u], tasks[3, 2 * i + u]
                first = pl.multiple_of(tasks[1, 2 * i + u], CAP)
                keep = (
                    (id_cols[source, pl.ds(first, CAP), :] == insertion.astype(jnp.float32))
                    .astype(jnp.float32)
                    .astype(jnp.bfloat16)
                )
                keep = jnp.concatenate([keep] * (SITES // 128), axis=1)
                sig = sorted_rows[source, pl.ds(first, CAP), :] * keep
                cot = sorted_rows[source, pl.ds(rows + first, CAP), :] * keep
                loaded.append((source, first, e, sig, cot))
            found = []
            for source, first, e, sig, cot in loaded:
                read_out = held[e, 1]
                preact = jnp.dot(sig, held[e, 0], preferred_element_type=jnp.float32)
                back_hidden = jnp.dot(cot, read_out, preferred_element_type=jnp.float32)
                gelu_val, slopes = gelu_parts(preact)
                hidden = gelu_val.astype(jnp.bfloat16)
                back_pre = (back_hidden * slopes).astype(jnp.bfloat16)
                part = lax.dot_general(
                    hidden, read_out, (((1,), (1,)), ((), ())), preferred_element_type=jnp.float32
                ).astype(jnp.bfloat16)
                grad_in = lax.dot_general(
                    sig, back_pre, (((0,), (0,)), ((), ())), preferred_element_type=jnp.float32
                )
                grad_out = lax.dot_general(
                    cot, hidden, (((0,), (0,)), ((), ())), preferred_element_type=jnp.float32
                )
                found.append((part, grad_in, grad_out))
            for (source, first, e, _, _), (part, grad_in, grad_out) in zip(loaded, found):
                pred[source, pl.ds(first, CAP), :] += part
                acc[e, 0] += grad_in
                acc[e, 1] += grad_out
            return 0

        lax.fori_loop(0, (count + 1) // 2, pair, 0)
        for which, ref in enumerate(pred_refs):
            ref[...] = pred[which * planes : (which + 1) * planes]
        for chunk, (start, size) in enumerate(zip(starts, sizes)):
            for j in range(n_blocks):
                ref = grad_refs[chunk * n_blocks + j]

                def write(e, _, start=start, ref=ref, j=j):
                    if aligned:
                        ref[e] = acc[
                            start + e,
                            :,
                            pl.ds(pl.multiple_of((own_at ^ j) * piece, 16), piece),
                            :,
                        ].astype(jnp.bfloat16)
                    else:
                        ref[e] = acc[start + e].astype(jnp.bfloat16)
                    return 0

                lax.fori_loop(0, size, write, 0)

    pred_shape = jax.ShapeDtypeStruct((planes, rows, SITES), jnp.bfloat16)
    grad_rows = piece if aligned else SITES
    grad_shapes = [
        jax.ShapeDtypeStruct((size, 2, grad_rows, width), jnp.bfloat16)
        for size in sizes
        for _ in range(n_blocks)
    ]
    most = 2 * planes * (touch + 1)
    scratch = [
        pltpu.VMEM((half, 2, SITES, width), jnp.float32),
        pltpu.VMEM((2 * planes, rows, 128), jnp.float32),
        pltpu.VMEM((half, 2, SITES, width), jnp.bfloat16),
        pltpu.VMEM((2 * planes,) + mine.shape[1:], jnp.bfloat16),
        pltpu.VMEM((2 * planes, rows, SITES), jnp.bfloat16),
        pltpu.SMEM((2 * planes,), jnp.int32),
        pltpu.SMEM((4, most + 1), jnp.int32),
        pltpu.SemaphoreType.DMA((2 + n_blocks,)),
    ]
    own_at = pos[1]
    if not aligned:
        order = own_at ^ jnp.arange(n_own, dtype=jnp.int32)
        stacked = jnp.take(jnp.stack(blocks), order, axis=0)
        blocks = [stacked.transpose(1, 2, 0, 3, 4).reshape(half, 2, SITES, width)]
    anywhere = pl.BlockSpec(memory_space=pl.ANY)
    found = pl.pallas_call(
        body,
        out_shape=[pred_shape, pred_shape] + grad_shapes,
        in_specs=[smem(), smem(), smem()] + [anywhere] * (2 + n_blocks),
        out_specs=[vmem()] * (2 + n_grads),
        scratch_shapes=scratch,
        compiler_params=params(),
        name="local_grads",
    )(pos, touched, slot_map, mine, other, *blocks)
    grads = []
    for chunk in range(len(sizes)):
        outs = found[2 + chunk * n_blocks : 2 + (chunk + 1) * n_blocks]
        if not aligned:
            outs = [
                lax.dynamic_slice_in_dim(outs[0], (own_at ^ j) * piece, piece, 2)
                for j in range(n_own)
            ]
        grads.append(list(outs))
    return found[0], found[1], grads


def adam(pos, arrived, weights, moment1, moment2, start, before):
    n_own = len(arrived)
    size, _, piece, width = arrived[0].shape
    number = weights.shape[0]
    half = number // 2
    correct_one = 1.0 - 0.9**10
    correct_two = 1.0 - 0.999**10

    def body(pos_ref, *refs):
        grad_refs = refs[:n_own]
        w_ref, m1_ref, m2_ref = refs[n_own : n_own + 3]
        new_w, new_m1, new_m2 = refs[-3:]

        def step(chosen):
            gradient = chosen[0][...].astype(jnp.float32)
            for ref in chosen[1:]:
                gradient = gradient + ref[...].astype(jnp.float32)
            one = 0.9 * m1_ref[...] + 0.1 * gradient
            two = 0.999 * m2_ref[...] + 0.001 * gradient * gradient
            new_m1[...] = one
            new_m2[...] = two
            updated = w_ref[...].astype(jnp.float32) - learn_rate * (one / correct_one) / (
                jnp.sqrt(two / correct_two) + 1e-08
            )
            new_w[0] = updated.astype(jnp.bfloat16)

        pl.when(pl.program_id(0) == 0)(lambda: step(grad_refs[0::2]))
        pl.when(pl.program_id(0) == 1)(lambda: step(grad_refs[1::2]))

    def which(g, pos_ref):
        return lax.rem(pos_ref[1] + g, 2)

    per = math.gcd(size, start) if start else size
    per = math.gcd(per, half)

    def place(g, i, pos_ref):
        return (which(g, pos_ref) * (half // per) + start // per + i, 0, 0, 0)

    small = pl.BlockSpec((per, 2, piece, width), place)
    grad = pl.BlockSpec((per, 2, piece, width), lambda g, i, pos_ref: (i, 0, 0, 0))
    anywhere = pl.BlockSpec(memory_space=pl.ANY)
    grid_spec = pltpu.PrefetchScalarGridSpec(
        num_scalar_prefetch=1,
        grid=(2, size // per),
        in_specs=[grad] * n_own
        + [
            pl.BlockSpec(
                (per, 2, piece, width),
                lambda g, i, pos_ref: place(g, i, pos_ref)[:3] + (pos_ref[0],),
            ),
            small,
            small,
        ]
        + [anywhere] * len(before),
        out_specs=[
            pl.BlockSpec(
                (1, per, 2, piece, width),
                lambda g, i, pos_ref: (which(g, pos_ref), i, 0, 0, 0),
            ),
            small,
            small,
        ],
    )
    return pl.pallas_call(
        body,
        out_shape=[
            jax.ShapeDtypeStruct((2, size, 2, piece, width), jnp.bfloat16),
            jax.ShapeDtypeStruct(moment1.shape, jnp.float32),
            jax.ShapeDtypeStruct(moment1.shape, jnp.float32),
        ],
        grid_spec=grid_spec,
        input_output_aliases={1 + n_own + 3 + i: 1 + i for i in range(len(before))},
        compiler_params=params(),
        name="adam_step",
    )(pos, *arrived, weights, moment1, moment2, *before)


def place_weights(chunk, start, half, before):
    _, size, _, piece, full = chunk.shape

    def body(chunk_ref, *refs):
        out_ref, sems = refs[-2:]
        copies = [
            pltpu.make_async_copy(
                chunk_ref.at[h], out_ref.at[pl.ds(h * half + start, size)], sems.at[h]
            )
            for h in range(2)
        ]
        for copy in copies:
            copy.start()
        for copy in copies:
            copy.wait()

    anywhere = pl.BlockSpec(memory_space=pl.ANY)
    return pl.pallas_call(
        body,
        out_shape=jax.ShapeDtypeStruct((2 * half, 2, piece, full), jnp.bfloat16),
        in_specs=[anywhere] * (1 + len(before)),
        out_specs=anywhere,
        scratch_shapes=[pltpu.SemaphoreType.DMA((2,))],
        input_output_aliases={1: 0} if before else {},
        compiler_params=params(),
        name="place_weights",
    )(chunk, *before)


def finish_predicted(perm, parts):
    def body(perm_ref, *refs):
        total = refs[0][...].astype(jnp.float32)
        for ref in refs[1:-1]:
            total = total + ref[...].astype(jnp.float32)
        refs[-1][...] = lax.dot_general(
            perm_ref[...],
            total.astype(jnp.bfloat16),
            (((0,), (0,)), ((), ())),
            preferred_element_type=jnp.float32,
        ).astype(jnp.bfloat16)

    return pl.pallas_call(
        body,
        out_shape=jax.ShapeDtypeStruct(parts[0].shape, jnp.bfloat16),
        in_specs=[vmem()] * (1 + len(parts)),
        out_specs=vmem(),
        compiler_params=params(),
        name="finish_predicted",
    )(perm, *parts)


def shards(signals, cotangent, row_insertion, touched, slot_map, weights, moment1, moment2):
    n_own = lax.axis_size("own")
    n_dp = lax.axis_size("dp")
    dp_at = lax.axis_index("dp")
    own_at = lax.axis_index("own")
    number, _, piece, _ = weights.shape
    width = moment1.shape[3]
    half = number // 2
    rows = signals.shape[0]
    pos = jnp.stack([dp_at, own_at]).astype(jnp.int32)
    core = lax.rem(own_at, 2)
    parts_of_half = sum(CHUNK_PARTS)
    sizes = [half * part // parts_of_half for part in CHUNK_PARTS]

    def across(value, j):
        return lax.ppermute(value, "own", [(o, o ^ j) for o in range(n_own)])

    packed, perm = pack_rows(row_insertion.reshape(1, rows), signals, cotangent)
    mine = lax.all_gather(packed, "dp", axis=0)

    def column(which):
        return lax.dynamic_slice(
            weights, (which * half, 0, 0, dp_at * width), (half, 2, piece, width)
        )

    outgoing = (column(core), column(1 - core))
    blocks = [outgoing[0]] + [across(outgoing[j % 2], j) for j in range(1, n_own)]
    other = across(mine, 1)

    pred_mine, pred_other, grads = local_grads(
        pos, touched, slot_map, mine, other, blocks, sizes, piece, width
    )
    moments = []
    new_weights = []
    start = 0
    for size, chunk in zip(sizes, grads):
        arrived = [chunk[0]] + [across(chunk[j], j) for j in range(1, n_own)]
        fresh, *moments = adam(pos, arrived, weights, moment1, moment2, start, moments)
        whole = lax.all_gather(fresh, "dp", axis=4, tiled=True)
        new_weights = [place_weights(whole, start, half, new_weights)]
        start += size
    new_weights = new_weights[0]
    new_moment1, new_moment2 = moments

    pred_part = pred_mine + across(pred_other, 1)
    parts = [lax.dynamic_index_in_dim(pred_part, dp_at, 0, keepdims=False)]
    for shift in range(1, n_dp):
        block = lax.dynamic_index_in_dim(pred_part, lax.rem(dp_at + shift, n_dp), 0, keepdims=False)
        parts.append(lax.ppermute(block, "dp", [(d, (d + shift) % n_dp) for d in range(n_dp)]))
    predicted = finish_predicted(perm, parts)
    return (predicted, new_weights, new_moment1, new_moment2)


def solution(mesh):
    in_specs = (
        P(("dp", "own"), None),
        P(("dp", "own"), None),
        P(("dp", "own")),
        P(),
        P(),
        P(None, None, "own", None),
        P(None, None, "own", "dp"),
        P(None, None, "own", "dp"),
    )
    out_specs = (
        P(("dp", "own"), None),
        P(None, None, "own", None),
        P(None, None, "own", "dp"),
        P(None, None, "own", "dp"),
    )
    return jax.shard_map(shards, mesh=mesh, in_specs=in_specs, out_specs=out_specs, check_vma=False)
```

time: 220 us -> 361 us (1.64)
  Pallas kernels: 33.4 us -> 135 us
  blocking collectives: 42.8 us -> 84.6 us
  starting transfers between devices: 10 us -> 40 us
  waiting for transfers between devices: 104 us -> 76.8 us
  local copies, waits for them, and re-layouts: 11.1 us -> 6.24 us
    pallas_call x2 -> x9, Pallas kernels: 28.8 us -> 130 us  [the longest x4 99.8 us: place_weights(): pl.pallas_call(body, out_shape=jax.ShapeDtypeStruct((2 * half, 2, piece,...]
    all_gather x0 -> x4, blocking collectives: none -> 84.6 us  [shards(): whole = lax.all_gather(fresh, 'dp', axis=4, tiled=True)]
    all_to_all x1 -> x0, blocking collectives: 42.8 us -> none  [shards(): lax.all_to_all(grads[0], 'own', split_axis=0, concat_axis=0, tiled=True)]
    all_gather x1 -> x0, waiting for transfers between devices: 42.3 us -> none  [shards(): new_weights = lax.all_gather(fresh, 'dp', axis=3, tiled=True)]
    ppermute x2 -> x37, starting transfers between devices: 0.07 us -> 37.1 us  [across(): return lax.ppermute(value, 'own', [(o, o ^ j) for o in range(n_own)])]
    ppermute x2 -> x37, waiting for transfers between devices: 2.25 us -> 37.1 us  [across(): return lax.ppermute(value, 'own', [(o, o ^ j) for o in range(n_own)])]
    ppermute x3, waiting for transfers between devices: 24.5 us -> 0.01 us  [shards(): lax.ppermute(block, 'dp', [(d, (d + shift) % n_dp) for d in range(n_dp)])]
    all_gather x1, waiting for transfers between devices: 32 us -> 39.7 us  [shards(): mine = lax.all_gather(packed, 'dp', axis=0)]
  transfers between devices with their start and end apart: 8 -> 41, of which waited for: 6 -> 11; matrix products, arithmetic and copies ran while one was open for 3% -> 1% of each run, Pallas kernels for 1% -> 32%
where the time goes in v2:
time: 361 us; the launch traced here: 358 us
  Pallas kernels  135 us (37%)
  blocking collectives  84.6 us (23%)
  waiting for transfers between devices  76.8 us (21%)
  starting transfers between devices  40 us (11%)
  between operations  14.6 us (4%)
  local copies, waits for them, and re-layouts  6.24 us (2%)
    pallas_call x4, Pallas kernels, place_weights(): pl.pallas_call(body, out_shape=jax.ShapeDtypeStruct((2 * half, 2, piece,...  99.8 us
    all_gather x4, blocking collectives, shards(): whole = lax.all_gather(fresh, 'dp', axis=4, tiled=True)  84.6 us
    all_gather x1, waiting for transfers between devices, shards(): mine = lax.all_gather(packed, 'dp', axis=0)  39.7 us
    ppermute x37, starting transfers between devices, across(): return lax.ppermute(value, 'own', [(o, o ^ j) for o in range(n_own)])  37.1 us
    ppermute x37, waiting for transfers between devices, across(): return lax.ppermute(value, 'own', [(o, o ^ j) for o in range(n_own)])  37.1 us
    pallas_call x1, Pallas kernels, local_grads(): pl.pallas_call(body, out_shape=[pred_shape, pred_shape] + grad_shapes, in...  16 us
    pallas_call x4, Pallas kernels, adam(): pl.pallas_call(body, out_shape=[jax.ShapeDtypeStruct((2, size, 2, piece,...  14.5 us
  transfers between devices with their start and end apart: 41, of which 11 were waited for; matrix products, arithmetic and copies ran while one was open for 1% of the time, Pallas kernels for 32%

profile of v2, /device:TPU:2, one launch (start us, length us, event | category | flops | bytes accessed | tf_op | source)
XLA Modules:
  0.0 358.0 jit_solution(10403854735233886700)
XLA Ops:
  7.2 2.4 pack_rows.1
  9.7 39.7 %all-gather.3.cloned.1.call-done = bf16[2112,384]{1,0:T(8,128)(2,1)} async-done(((bf16[528,384]{1,0:T(8,128)(2,1)}), bf16[2112,384]{1,0:T(8,128)(2,1)}) %all-gather.3.cloned.1.call-update) | async-done | bytes 1622032 | tf_op jit(solution)/shard_map/all_gather | solution.py:419
  49.3 1.2 constant_dynamic-slice_fusion
  50.5 1.6 collective-permute-start.7
  52.3 1.6 collective-permute-start.3
  53.9 8.4 %collective-permute-done.7.rest_7_ = bf16[8,2,48,256]{3,2,1,0:T(8,128)(2,1)S(1)} collective-permute-done((bf16[8,2,48,256]{3,2,1,0:T(8,128)(2,1)S(1)}, bf16[8,2,48,256]{3,2,1,0:T(8,128)(2,1)S(1)}, u32[]{:S(2)}, u32[]{:S(2)}) %collective-permute-start.7) | collective-permute-done | bytes 393248 | tf_op jit(solution)/shard_map/ppermute | solution.py:416
  62.3 1.5 collective-permute-start.6
  63.8 8.1 %collective-permute-done.5.rest_5_ = bf16[8,2,48,256]{3,2,1,0:T(8,128)(2,1)S(1)} collective-permute-done((bf16[8,2,48,256]{3,2,1,0:T(8,128)(2,1)S(1)}, bf16[8,2,48,256]{3,2,1,0:T(8,128)(2,1)S(1)}, u32[]{:S(2)}, u32[]{:S(2)}) %collective-permute-start.5) | collective-permute-done | bytes 393248 | tf_op jit(solution)/shard_map/ppermute | solution.py:416
  73.3 1.4 collective-permute-start.2
  76.0 4.6 %collective-permute-done.6.rest_6_ = bf16[8,2,48,256]{3,2,1,0:T(8,128)(2,1)} collective-permute-done((bf16[8,2,48,256]{3,2,1,0:T(8,128)(2,1)S(1)}, bf16[8,2,48,256]{3,2,1,0:T(8,128)(2,1)}, u32[]{:S(2)}, u32[]{:S(2)}) %collective-permute-start.6) | collective-permute-done | bytes 393248 | tf_op jit(solution)/shard_map/ppermute | solution.py:416
  80.6 7.7 %collective-permute-done.4.rest_4_ = bf16[8,2,48,256]{3,2,1,0:T(8,128)(2,1)} collective-permute-done((bf16[8,2,48,256]{3,2,1,0:T(8,128)(2,1)S(1)}, bf16[8,2,48,256]{3,2,1,0:T(8,128)(2,1)}, u32[]{:S(2)}, u32[]{:S(2)}) %collective-permute-start.4) | collective-permute-done | bytes 393248 | tf_op jit(solution)/shard_map/ppermute | solution.py:416
  88.4 1.1 copy-done
  89.6 16.0 %local_grads.1 = (bf16[4,256,384]{2,1,0:T(8,128)(2,1)}, bf16[4,256,384]{2,1,0:T(8,128)(2,1)}, bf16[2,2,48,256]{3,2,1,0:T(8,128)(2,1)}, bf16[2,2,48,256]{3,2,1,0:...) custom-call(s32[2]{0:T(128)} %pad_add_fusion.pos_ref, ...), custom_call_target="tpu_custom_call" | custom-call | tf_op jit(solution)/shard_map/local_grads/pallas_call | solution.py:252
  106.4 1.5 collective-permute-start.27
  108.1 2.3 collective-permute-start.29
  110.4 1.1 collective-permute-done.20.refs_2_
  111.5 2.4 collective-permute-start.31
  114.8 1.3 collective-permute-start.33
  116.1 0.8 collective-permute-start.34
  116.9 2.1 collective-permute-done.30.refs_5_
  119.0 2.2 collective-permute-start.35
  121.6 1.1 collective-permute-start.37
  122.7 1.8 collective-permute-start.38
  124.5 1.1 collective-permute-start.39
  126.2 0.8 collective-permute-done.36.refs_4_
  127.7 3.9 %collective-permute-done.37.refs_5_ = bf16[2,2,48,256]{3,2,1,0:T(8,128)(2,1)S(1)} collective-permute-done((bf16[2,2,48,256]{3,2,1,0:T(8,128)(2,1)}, bf16[2,2,48,256]{3,2,1,0:T(8,128)(2,1)S(1)}, u32[]{:S(2)}, u32[]{:S(2)}) %collective-permute-start.37) | collective-permute-done | bytes 98336 | tf_op jit(solution)/shard_map/ppermute | solution.py:416
  131.6 1.6 collective-permute-start.23
  133.2 1.3 collective-permute-start.24
  134.4 2.1 collective-permute-start.25
  136.6 3.5 adam_step.4
  140.2 3.7 %adam_step.5 = (bf16[2,2,2,48,256]{4,3,2,1,0:T(8,128)(2,1)}, f32[16,2,48,256]{3,2,1,0:T(8,128)}, f32[16,2,48,256]{3,2,1,0:T(8,128)}) custom-call(s32[2]{0:T(128)} %pad_add_fusion.pos_ref, bf16[2,2,48,256]{3,2,1,0:T(8,128)(2,1)} %get-tuple-element.72.refs_0_, bf16[2,2,48,256]{3,2,1,0:T(8,128)(2,1)} %copy-done.14, ...), custom_call_target="tpu_custom_call", output_to_operand_aliasing={{1}: (12, {}), {2}: (13, {})} | custom-call | tf_op jit(solution)/shard_map/adam_step/pallas_call | solution.py:336
  144.0 1.6 collective-permute-start.13
  146.0 0.9 collective-permute-start.15
  147.6 3.7 %adam_step.6 = (bf16[2,2,2,48,256]{4,3,2,1,0:T(8,128)(2,1)}, f32[16,2,48,256]{3,2,1,0:T(8,128)}, f32[16,2,48,256]{3,2,1,0:T(8,128)}) custom-call(s32[2]{0:T(128)} %pad_add_fusion.pos_ref, bf16[2,2,48,256]{3,2,1,0:T(8,128)(2,1)} %get-tuple-element.64.refs_0_, bf16[2,2,48,256]{3,2,1,0:T(8,128)(2,1)} %copy-done.12, ...), custom_call_target="tpu_custom_call", output_to_operand_aliasing={{1}: (12, {}), {2}: (13, {})} | custom-call | tf_op jit(solution)/shard_map/adam_step/pallas_call | solution.py:336
  151.3 19.0 %all_gather.21.chunk_ref = bf16[2,2,2,48,1024]{4,3,2,1,0:T(8,128)(2,1)} all-gather(bf16[2,2,2,48,256]{4,3,2,1,0:T(8,128)(2,1)} %get-tuple-element.95), channel_id=1, replica_groups=mesh['dp'=4,'own'=8] {'dp'}, dimensions={4}, use_global_device_ids=true | all-gather | bytes 983040 | tf_op jit(solution)/shard_map/all_gather | solution.py:439
  170.3 18.2 %all_gather.22.chunk_ref = bf16[2,2,2,48,1024]{4,3,2,1,0:T(8,128)(2,1)} all-gather(bf16[2,2,2,48,256]{4,3,2,1,0:T(8,128)(2,1)S(1)} %copy-done.7), channel_id=1, replica_groups=mesh['dp'=4,'own'=8] {'dp'}, dimensions={4}, use_global_device_ids=true | all-gather | bytes 983040 | tf_op jit(solution)/shard_map/all_gather | solution.py:439
  188.6 1.8 collective-permute-start.17
  190.4 2.1 collective-permute-start.18
  192.6 18.5 %all_gather.23.chunk_ref = bf16[2,2,2,48,1024]{4,3,2,1,0:T(8,128)(2,1)} all-gather(bf16[2,2,2,48,256]{4,3,2,1,0:T(8,128)(2,1)S(1)} %copy-done.6), channel_id=1, replica_groups=mesh['dp'=4,'own'=8] {'dp'}, dimensions={4}, use_global_device_ids=true | all-gather | bytes 983040 | tf_op jit(solution)/shard_map/all_gather | solution.py:439
  211.1 24.9 %place_weights.4.refs_0_ = bf16[16,2,48,1024]{3,2,1,0:T(8,128)(2,1)} custom-call(bf16[2,2,2,48,1024]{4,3,2,1,0:T(8,128)(2,1)} %all_gather.23.chunk_ref), custom_call_target="tpu_custom_call" | custom-call | tf_op jit(solution)/shard_map/place_weights/pallas_call | solution.py:367
  236.0 24.9 %place_weights.5.refs_0_ = bf16[16,2,48,1024]{3,2,1,0:T(8,128)(2,1)} custom-call(bf16[2,2,2,48,1024]{4,3,2,1,0:T(8,128)(2,1)} %all_gather.22.chunk_ref, bf16[16,2,48,1024]{3,2,1,0:T(8,128)(2,1)} %place_weights.4.refs_0_), custom_call_target="tpu_custom_call", output_to_operand_aliasing={{}: (1, {})} | custom-call | tf_op jit(solution)/shard_map/place_weights/pallas_call | solution.py:367
  261.0 24.9 %place_weights.6.refs_0_ = bf16[16,2,48,1024]{3,2,1,0:T(8,128)(2,1)} custom-call(bf16[2,2,2,48,1024]{4,3,2,1,0:T(8,128)(2,1)} %all_gather.21.chunk_ref, bf16[16,2,48,1024]{3,2,1,0:T(8,128)(2,1)} %place_weights.5.refs_0_), custom_call_target="tpu_custom_call", output_to_operand_aliasing={{}: (1, {})} | custom-call | tf_op jit(solution)/shard_map/place_weights/pallas_call | solution.py:367
  286.7 3.7 %adam_step.7 = (bf16[2,2,2,48,256]{4,3,2,1,0:T(8,128)(2,1)}, f32[16,2,48,256]{3,2,1,0:T(8,128)}, f32[16,2,48,256]{3,2,1,0:T(8,128)}) custom-call(s32[2]{0:T(128)} %pad_add_fusion.pos_ref, bf16[2,2,48,256]{3,2,1,0:T(8,128)(2,1)} %get-tuple-element.56.refs_0_, bf16[2,2,48,256]{3,2,1,0:T(8,128)(2,1)} %copy-done.33, ...), custom_call_target="tpu_custom_call", output_to_operand_aliasing={{1}: (12, {}), {2}: (13, {})} | custom-call | tf_op jit(solution)/shard_map/adam_step/pallas_call | solution.py:336
  290.6 0.8 dynamic-slice_bitcast_fusion
  291.4 2.1 collective-permute-start.11
  294.2 28.9 %all_gather.20.chunk_ref = bf16[2,2,2,48,1024]{4,3,2,1,0:T(8,128)(2,1)} all-gather(bf16[2,2,2,48,256]{4,3,2,1,0:T(8,128)(2,1)S(1)} %copy-done.8), channel_id=1, replica_groups=mesh['dp'=4,'own'=8] {'dp'}, dimensions={4}, use_global_device_ids=true | all-gather | bytes 983040 | tf_op jit(solution)/shard_map/all_gather | solution.py:439
  323.1 24.9 %place_weights.7 = bf16[16,2,48,1024]{3,2,1,0:T(8,128)(2,1)} custom-call(bf16[2,2,2,48,1024]{4,3,2,1,0:T(8,128)(2,1)} %all_gather.20.chunk_ref, bf16[16,2,48,1024]{3,2,1,0:T(8,128)(2,1)} %place_weights.6.refs_0_), custom_call_target="tpu_custom_call", output_to_operand_aliasing={{}: (1, {})} | custom-call | tf_op jit(solution)/shard_map/place_weights/pallas_call | solution.py:367
  348.9 2.2 finish_predicted.1
  (153 shorter events, 10.3 us)
Async XLA Ops:
  7.2 67.5 %copy-start.40 = (s32[32,4]{0,1:T(4,128)S(1)}, s32[32,4]{0,1:T(4,128)}, u32[]{:S(2)}) copy-start(s32[32,4]{0,1:T(4,128)} %param.11) | copy-start | bytes 1540
  7.2 42.1 %all-gather.3.cloned.1.call-start = ((), (), s32[]{:S(2)}) async-start(), calls=%async_computation | async-start | bytes 2027520 | tf_op jit(solution)/shard_map/all_gather | solution.py:419
  49.3 39.1 %collective-permute-start = (bf16[4,528,384]{2,1,0:T(8,128)(2,1)}, bf16[4,528,384]{2,1,0:T(8,128)(2,1)S(1)}, u32[]{:S(2)}, u32[]{:S(2)}) collective-permute-start(bf16[4,528,384]{2,1,0:T(8,128)(2,1)} %bitcast.12), channel_id=1, source_target_pairs={{0,1},{1,0},{2,3},{3,2},{4,5},{5,4},{6,7},{7,6},{8,9},{9,8},{10,11... | collective-permute-start | bytes 4866056 | tf_op jit(solution)/shard_map/ppermute | solution.py:416
  50.5 37.9 %copy-start.1 = (bf16[8,2,48,256]{3,2,1,0:T(8,128)(2,1)}, bf16[8,2,48,256]{3,2,1,0:T(8,128)(2,1)S(1)}, u32[]{:S(2)}) copy-start(bf16[8,2,48,256]{3,2,1,0:T(8,128)(2,1)S(1)} %get-tuple-element.101.rest_0_) | copy-start | bytes 1179652
  50.5 11.8 %collective-permute-start.7 = (bf16[8,2,48,256]{3,2,1,0:T(8,128)(2,1)S(1)}, bf16[8,2,48,256]{3,2,1,0:T(8,128)(2,1)S(1)}, u32[]{:S(2)}, u32[]{:S(2)}) collective-permute-start(bf16[8,2,48,256]{3,2,1,0:T(8,128)(2,1)S(1)} %get-tuple-element.100), channel_id=1, source_target_pairs={{0,7},{1,6},{2,5},{3,4},{4,3},{5,2},{6,1},{7,0},{8,15},{9,14},{10,... | collective-permute-start | bytes 1179656 | tf_op jit(solution)/shard_map/ppermute | solution.py:416
  52.2 19.7 %collective-permute-start.5 = (bf16[8,2,48,256]{3,2,1,0:T(8,128)(2,1)S(1)}, bf16[8,2,48,256]{3,2,1,0:T(8,128)(2,1)S(1)}, u32[]{:S(2)}, u32[]{:S(2)}) collective-permute-start(bf16[8,2,48,256]{3,2,1,0:T(8,128)(2,1)S(1)} %get-tuple-element.100), channel_id=1, source_target_pairs={{0,5},{1,4},{2,7},{3,6},{4,1},{5,0},{6,3},{7,2},{8,13},{9,12},{10,... | collective-permute-start | bytes 1179656 | tf_op jit(solution)/shard_map/ppermute | solution.py:416
  52.3 20.2 %collective-permute-start.3 = (bf16[8,2,48,256]{3,2,1,0:T(8,128)(2,1)S(1)}, bf16[8,2,48,256]{3,2,1,0:T(8,128)(2,1)S(1)}, u32[]{:S(2)}, u32[]{:S(2)}) collective-permute-start(bf16[8,2,48,256]{3,2,1,0:T(8,128)(2,1)S(1)} %get-tuple-element.100), channel_id=1, source_target_pairs={{0,3},{1,2},{2,1},{3,0},{4,7},{5,6},{6,5},{7,4},{8,11},{9,10},{10,... | collective-permute-start | bytes 1179656 | tf_op jit(solution)/shard_map/ppermute | solution.py:416
  53.9 22.1 %collective-permute-start.1 = (bf16[8,2,48,256]{3,2,1,0:T(8,128)(2,1)S(1)}, bf16[8,2,48,256]{3,2,1,0:T(8,128)(2,1)}, u32[]{:S(2)}, u32[]{:S(2)}) collective-permute-start(bf16[8,2,48,256]{3,2,1,0:T(8,128)(2,1)S(1)} %get-tuple-element.100), channel_id=1, source_target_pairs={{0,1},{1,0},{2,3},{3,2},{4,5},{5,4},{6,7},{7,6},{8,9},{9,8},{10,11... | collective-permute-start | bytes 1179656 | tf_op jit(solution)/shard_map/ppermute | solution.py:416
  62.3 18.2 %collective-permute-start.6 = (bf16[8,2,48,256]{3,2,1,0:T(8,128)(2,1)S(1)}, bf16[8,2,48,256]{3,2,1,0:T(8,128)(2,1)}, u32[]{:S(2)}, u32[]{:S(2)}) collective-permute-start(bf16[8,2,48,256]{3,2,1,0:T(8,128)(2,1)S(1)} %get-tuple-element.101.rest_0_), channel_id=1, source_target_pairs={{0,6},{1,7},{2,4},{3,5},{4,2},{5,3},{6,0},{7,1},{8,14},{9,15},{10,... | collective-permute-start | bytes 1179656 | tf_op jit(solution)/shard_map/ppermute | solution.py:416
  71.9 16.4 %collective-permute-start.4 = (bf16[8,2,48,256]{3,2,1,0:T(8,128)(2,1)S(1)}, bf16[8,2,48,256]{3,2,1,0:T(8,128)(2,1)}, u32[]{:S(2)}, u32[]{:S(2)}) collective-permute-start(bf16[8,2,48,256]{3,2,1,0:T(8,128)(2,1)S(1)} %get-tuple-element.101.rest_0_), channel_id=1, source_target_pairs={{0,4},{1,5},{2,6},{3,7},{4,0},{5,1},{6,2},{7,3},{8,12},{9,13},{10,... | collective-permute-start | bytes 1179656 | tf_op jit(solution)/shard_map/ppermute | solution.py:416
  73.3 15.1 %collective-permute-start.2 = (bf16[8,2,48,256]{3,2,1,0:T(8,128)(2,1)S(1)}, bf16[8,2,48,256]{3,2,1,0:T(8,128)(2,1)}, u32[]{:S(2)}, u32[]{:S(2)}) collective-permute-start(bf16[8,2,48,256]{3,2,1,0:T(8,128)(2,1)S(1)} %get-tuple-element.101.rest_0_), channel_id=1, source_target_pairs={{0,2},{1,3},{2,0},{3,1},{4,6},{5,7},{6,4},{7,5},{8,10},{9,11},{10,... | collective-permute-start | bytes 1179656 | tf_op jit(solution)/shard_map/ppermute | solution.py:416
  105.5 2.6 collective-permute-start.19
  105.6 5.9 %collective-permute-start.20 = (bf16[2,2,48,256]{3,2,1,0:T(8,128)(2,1)}, bf16[2,2,48,256]{3,2,1,0:T(8,128)(2,1)S(1)}, u32[]{:S(2)}, u32[]{:S(2)}) collective-permute-start(bf16[2,2,48,256]{3,2,1,0:T(8,128)(2,1)} %get-tuple-element.66), channel_id=1, source_target_pairs={{0,2},{1,3},{2,0},{3,1},{4,6},{5,7},{6,4},{7,5},{8,10},{9,11},{10,... | collective-permute-start | bytes 294920 | tf_op jit(solution)/shard_map/ppermute | solution.py:416
  106.2 5.3 %collective-permute-start.26 = (bf16[2,2,48,256]{3,2,1,0:T(8,128)(2,1)}, bf16[2,2,48,256]{3,2,1,0:T(8,128)(2,1)S(1)}, u32[]{:S(2)}, u32[]{:S(2)}) collective-permute-start(bf16[2,2,48,256]{3,2,1,0:T(8,128)(2,1)} %get-tuple-element.73), channel_id=1, source_target_pairs={{0,1},{1,0},{2,3},{3,2},{4,5},{5,4},{6,7},{7,6},{8,9},{9,8},{10,11... | collective-permute-start | bytes 294920 | tf_op jit(solution)/shard_map/ppermute | solution.py:416
  106.4 7.5 %collective-permute-start.27 = (bf16[2,2,48,256]{3,2,1,0:T(8,128)(2,1)}, bf16[2,2,48,256]{3,2,1,0:T(8,128)(2,1)S(1)}, u32[]{:S(2)}, u32[]{:S(2)}) collective-permute-start(bf16[2,2,48,256]{3,2,1,0:T(8,128)(2,1)} %get-tuple-element.74), channel_id=1, source_target_pairs={{0,2},{1,3},{2,0},{3,1},{4,6},{5,7},{6,4},{7,5},{8,10},{9,11},{10,... | collective-permute-start | bytes 294920 | tf_op jit(solution)/shard_map/ppermute | solution.py:416
  107.9 6.9 %collective-permute-start.28 = (bf16[2,2,48,256]{3,2,1,0:T(8,128)(2,1)}, bf16[2,2,48,256]{3,2,1,0:T(8,128)(2,1)S(1)}, u32[]{:S(2)}, u32[]{:S(2)}) collective-permute-start(bf16[2,2,48,256]{3,2,1,0:T(8,128)(2,1)} %get-tuple-element.75), channel_id=1, source_target_pairs={{0,3},{1,2},{2,1},{3,0},{4,7},{5,6},{6,5},{7,4},{8,11},{9,10},{10,... | collective-permute-start | bytes 294920 | tf_op jit(solution)/shard_map/ppermute | solution.py:416
  108.1 8.0 %collective-permute-start.29 = (bf16[2,2,48,256]{3,2,1,0:T(8,128)(2,1)}, bf16[2,2,48,256]{3,2,1,0:T(8,128)(2,1)S(1)}, u32[]{:S(2)}, u32[]{:S(2)}) collective-permute-start(bf16[2,2,48,256]{3,2,1,0:T(8,128)(2,1)} %get-tuple-element.76), channel_id=1, source_target_pairs={{0,4},{1,5},{2,6},{3,7},{4,0},{5,1},{6,2},{7,3},{8,12},{9,13},{10,... | collective-permute-start | bytes 294920 | tf_op jit(solution)/shard_map/ppermute | solution.py:416
  111.5 7.5 %collective-permute-start.30 = (bf16[2,2,48,256]{3,2,1,0:T(8,128)(2,1)}, bf16[2,2,48,256]{3,2,1,0:T(8,128)(2,1)S(1)}, u32[]{:S(2)}, u32[]{:S(2)}) collective-permute-start(bf16[2,2,48,256]{3,2,1,0:T(8,128)(2,1)} %get-tuple-element.77), channel_id=1, source_target_pairs={{0,5},{1,4},{2,7},{3,6},{4,1},{5,0},{6,3},{7,2},{8,13},{9,12},{10,... | collective-permute-start | bytes 294920 | tf_op jit(solution)/shard_map/ppermute | solution.py:416
  111.5 9.7 %collective-permute-start.31 = (bf16[2,2,48,256]{3,2,1,0:T(8,128)(2,1)}, bf16[2,2,48,256]{3,2,1,0:T(8,128)(2,1)S(1)}, u32[]{:S(2)}, u32[]{:S(2)}) collective-permute-start(bf16[2,2,48,256]{3,2,1,0:T(8,128)(2,1)} %get-tuple-element.78), channel_id=1, source_target_pairs={{0,6},{1,7},{2,4},{3,5},{4,2},{5,3},{6,0},{7,1},{8,14},{9,15},{10,... | collective-permute-start | bytes 294920 | tf_op jit(solution)/shard_map/ppermute | solution.py:416
  113.9 7.7 %collective-permute-start.32 = (bf16[2,2,48,256]{3,2,1,0:T(8,128)(2,1)}, bf16[2,2,48,256]{3,2,1,0:T(8,128)(2,1)S(1)}, u32[]{:S(2)}, u32[]{:S(2)}) collective-permute-start(bf16[2,2,48,256]{3,2,1,0:T(8,128)(2,1)} %get-tuple-element.79), channel_id=1, source_target_pairs={{0,7},{1,6},{2,5},{3,4},{4,3},{5,2},{6,1},{7,0},{8,15},{9,14},{10,... | collective-permute-start | bytes 294920 | tf_op jit(solution)/shard_map/ppermute | solution.py:416
  114.8 7.9 %collective-permute-start.33 = (bf16[2,2,48,256]{3,2,1,0:T(8,128)(2,1)}, bf16[2,2,48,256]{3,2,1,0:T(8,128)(2,1)S(1)}, u32[]{:S(2)}, u32[]{:S(2)}) collective-permute-start(bf16[2,2,48,256]{3,2,1,0:T(8,128)(2,1)} %get-tuple-element.81), channel_id=1, source_target_pairs={{0,1},{1,0},{2,3},{3,2},{4,5},{5,4},{6,7},{7,6},{8,9},{9,8},{10,11... | collective-permute-start | bytes 294920 | tf_op jit(solution)/shard_map/ppermute | solution.py:416
  116.1 8.4 %collective-permute-start.34 = (bf16[2,2,48,256]{3,2,1,0:T(8,128)(2,1)}, bf16[2,2,48,256]{3,2,1,0:T(8,128)(2,1)S(1)}, u32[]{:S(2)}, u32[]{:S(2)}) collective-permute-start(bf16[2,2,48,256]{3,2,1,0:T(8,128)(2,1)} %get-tuple-element.82), channel_id=1, source_target_pairs={{0,2},{1,3},{2,0},{3,1},{4,6},{5,7},{6,4},{7,5},{8,10},{9,11},{10,... | collective-permute-start | bytes 294920 | tf_op jit(solution)/shard_map/ppermute | solution.py:416
  119.0 6.6 %collective-permute-start.35 = (bf16[2,2,48,256]{3,2,1,0:T(8,128)(2,1)}, bf16[2,2,48,256]{3,2,1,0:T(8,128)(2,1)S(1)}, u32[]{:S(2)}, u32[]{:S(2)}) collective-permute-start(bf16[2,2,48,256]{3,2,1,0:T(8,128)(2,1)} %get-tuple-element.83), channel_id=1, source_target_pairs={{0,3},{1,2},{2,1},{3,0},{4,7},{5,6},{6,5},{7,4},{8,11},{9,10},{10,... | collective-permute-start | bytes 294920 | tf_op jit(solution)/shard_map/ppermute | solution.py:416
  121.2 5.9 %collective-permute-start.36 = (bf16[2,2,48,256]{3,2,1,0:T(8,128)(2,1)}, bf16[2,2,48,256]{3,2,1,0:T(8,128)(2,1)S(1)}, u32[]{:S(2)}, u32[]{:S(2)}) collective-permute-start(bf16[2,2,48,256]{3,2,1,0:T(8,128)(2,1)} %get-tuple-element.84), channel_id=1, source_target_pairs={{0,4},{1,5},{2,6},{3,7},{4,0},{5,1},{6,2},{7,3},{8,12},{9,13},{10,... | collective-permute-start | bytes 294920 | tf_op jit(solution)/shard_map/ppermute | solution.py:416
  121.6 10.0 %collective-permute-start.37 = (bf16[2,2,48,256]{3,2,1,0:T(8,128)(2,1)}, bf16[2,2,48,256]{3,2,1,0:T(8,128)(2,1)S(1)}, u32[]{:S(2)}, u32[]{:S(2)}) collective-permute-start(bf16[2,2,48,256]{3,2,1,0:T(8,128)(2,1)} %get-tuple-element.85), channel_id=1, source_target_pairs={{0,5},{1,4},{2,7},{3,6},{4,1},{5,0},{6,3},{7,2},{8,13},{9,12},{10,... | collective-permute-start | bytes 294920 | tf_op jit(solution)/shard_map/ppermute | solution.py:416
  122.7 10.5 %collective-permute-start.38 = (bf16[2,2,48,256]{3,2,1,0:T(8,128)(2,1)}, bf16[2,2,48,256]{3,2,1,0:T(8,128)(2,1)S(1)}, u32[]{:S(2)}, u32[]{:S(2)}) collective-permute-start(bf16[2,2,48,256]{3,2,1,0:T(8,128)(2,1)} %get-tuple-element.86), channel_id=1, source_target_pairs={{0,6},{1,7},{2,4},{3,5},{4,2},{5,3},{6,0},{7,1},{8,14},{9,15},{10,... | collective-permute-start | bytes 294920 | tf_op jit(solution)/shard_map/ppermute | solution.py:416
  124.5 10.0 %collective-permute-start.39 = (bf16[2,2,48,256]{3,2,1,0:T(8,128)(2,1)}, bf16[2,2,48,256]{3,2,1,0:T(8,128)(2,1)S(1)}, u32[]{:S(2)}, u32[]{:S(2)}) collective-permute-start(bf16[2,2,48,256]{3,2,1,0:T(8,128)(2,1)} %get-tuple-element.87), channel_id=1, source_target_pairs={{0,7},{1,6},{2,5},{3,4},{4,3},{5,2},{6,1},{7,0},{8,15},{9,14},{10,... | collective-permute-start | bytes 294920 | tf_op jit(solution)/shard_map/ppermute | solution.py:416
  125.6 18.3 %collective-permute-start.21 = (bf16[2,2,48,256]{3,2,1,0:T(8,128)(2,1)}, bf16[2,2,48,256]{3,2,1,0:T(8,128)(2,1)S(1)}, u32[]{:S(2)}, u32[]{:S(2)}) collective-permute-start(bf16[2,2,48,256]{3,2,1,0:T(8,128)(2,1)} %get-tuple-element.67), channel_id=1, source_target_pairs={{0,3},{1,2},{2,1},{3,0},{4,7},{5,6},{6,5},{7,4},{8,11},{9,10},{10,... | collective-permute-start | bytes 294920 | tf_op jit(solution)/shard_map/ppermute | solution.py:416
  127.1 17.0 %collective-permute-start.22 = (bf16[2,2,48,256]{3,2,1,0:T(8,128)(2,1)}, bf16[2,2,48,256]{3,2,1,0:T(8,128)(2,1)S(1)}, u32[]{:S(2)}, u32[]{:S(2)}) collective-permute-start(bf16[2,2,48,256]{3,2,1,0:T(8,128)(2,1)} %get-tuple-element.68), channel_id=1, source_target_pairs={{0,4},{1,5},{2,6},{3,7},{4,0},{5,1},{6,2},{7,3},{8,12},{9,13},{10,... | collective-permute-start | bytes 294920 | tf_op jit(solution)/shard_map/ppermute | solution.py:416
  131.6 14.1 %collective-permute-start.23 = (bf16[2,2,48,256]{3,2,1,0:T(8,128)(2,1)}, bf16[2,2,48,256]{3,2,1,0:T(8,128)(2,1)S(1)}, u32[]{:S(2)}, u32[]{:S(2)}) collective-permute-start(bf16[2,2,48,256]{3,2,1,0:T(8,128)(2,1)} %get-tuple-element.69), channel_id=1, source_target_pairs={{0,5},{1,4},{2,7},{3,6},{4,1},{5,0},{6,3},{7,2},{8,13},{9,12},{10,... | collective-permute-start | bytes 294920 | tf_op jit(solution)/shard_map/ppermute | solution.py:416
  133.2 12.8 %collective-permute-start.24 = (bf16[2,2,48,256]{3,2,1,0:T(8,128)(2,1)}, bf16[2,2,48,256]{3,2,1,0:T(8,128)(2,1)S(1)}, u32[]{:S(2)}, u32[]{:S(2)}) collective-permute-start(bf16[2,2,48,256]{3,2,1,0:T(8,128)(2,1)} %get-tuple-element.70), channel_id=1, source_target_pairs={{0,6},{1,7},{2,4},{3,5},{4,2},{5,3},{6,0},{7,1},{8,14},{9,15},{10,... | collective-permute-start | bytes 294920 | tf_op jit(solution)/shard_map/ppermute | solution.py:416
  134.4 12.5 %collective-permute-start.25 = (bf16[2,2,48,256]{3,2,1,0:T(8,128)(2,1)}, bf16[2,2,48,256]{3,2,1,0:T(8,128)(2,1)S(1)}, u32[]{:S(2)}, u32[]{:S(2)}) collective-permute-start(bf16[2,2,48,256]{3,2,1,0:T(8,128)(2,1)} %get-tuple-element.71), channel_id=1, source_target_pairs={{0,7},{1,6},{2,5},{3,4},{4,3},{5,2},{6,1},{7,0},{8,15},{9,14},{10,... | collective-permute-start | bytes 294920 | tf_op jit(solution)/shard_map/ppermute | solution.py:416
  143.9 44.6 %collective-permute-start.12 = (bf16[2,2,48,256]{3,2,1,0:T(8,128)(2,1)S(1)}, bf16[2,2,48,256]{3,2,1,0:T(8,128)(2,1)S(1)}, u32[]{:S(2)}, u32[]{:S(2)}) collective-permute-start(bf16[2,2,48,256]{3,2,1,0:T(8,128)(2,1)S(1)} %copy-done.48), channel_id=1, source_target_pairs={{0,1},{1,0},{2,3},{3,2},{4,5},{5,4},{6,7},{7,6},{8,9},{9,8},{10,11... | collective-permute-start | bytes 294920 | tf_op jit(solution)/shard_map/ppermute | solution.py:416
  144.0 44.6 %collective-permute-start.13 = (bf16[2,2,48,256]{3,2,1,0:T(8,128)(2,1)S(1)}, bf16[2,2,48,256]{3,2,1,0:T(8,128)(2,1)S(1)}, u32[]{:S(2)}, u32[]{:S(2)}) collective-permute-start(bf16[2,2,48,256]{3,2,1,0:T(8,128)(2,1)S(1)} %copy-done.47), channel_id=1, source_target_pairs={{0,2},{1,3},{2,0},{3,1},{4,6},{5,7},{6,4},{7,5},{8,10},{9,11},{10,... | collective-permute-start | bytes 294920 | tf_op jit(solution)/shard_map/ppermute | solution.py:416
  145.7 44.8 %collective-permute-start.14 = (bf16[2,2,48,256]{3,2,1,0:T(8,128)(2,1)S(1)}, bf16[2,2,48,256]{3,2,1,0:T(8,128)(2,1)S(1)}, u32[]{:S(2)}, u32[]{:S(2)}) collective-permute-start(bf16[2,2,48,256]{3,2,1,0:T(8,128)(2,1)S(1)} %copy-done.46), channel_id=1, source_target_pairs={{0,3},{1,2},{2,1},{3,0},{4,7},{5,6},{6,5},{7,4},{8,11},{9,10},{10,... | collective-permute-start | bytes 294920 | tf_op jit(solution)/shard_map/ppermute | solution.py:416
  146.0 139.9 %collective-permute-start.15 = (bf16[2,2,48,256]{3,2,1,0:T(8,128)(2,1)S(1)}, bf16[2,2,48,256]{3,2,1,0:T(8,128)(2,1)S(1)}, u32[]{:S(2)}, u32[]{:S(2)}) collective-permute-start(bf16[2,2,48,256]{3,2,1,0:T(8,128)(2,1)S(1)} %copy-done.45), channel_id=1, source_target_pairs={{0,4},{1,5},{2,6},{3,7},{4,0},{5,1},{6,2},{7,3},{8,12},{9,13},{10,... | collective-permute-start | bytes 294920 | tf_op jit(solution)/shard_map/ppermute | solution.py:416
  147.0 143.4 %collective-permute-start.8 = (bf16[4,256,384]{2,1,0:T(8,128)(2,1)S(1)}, bf16[4,256,384]{2,1,0:T(8,128)(2,1)S(1)}, u32[]{:S(2)}, u32[]{:S(2)}) collective-permute-start(bf16[4,256,384]{2,1,0:T(8,128)(2,1)S(1)} %copy-done.41), channel_id=1, source_target_pairs={{0,1},{1,0},{2,3},{3,2},{4,5},{5,4},{6,7},{7,6},{8,9},{9,8},{10,11... | collective-permute-start | bytes 2359304 | tf_op jit(solution)/shard_map/ppermute | solution.py:416
  151.3 39.2 %copy-start.42 = (bf16[2,2,48,256]{3,2,1,0:T(8,128)(2,1)S(1)}, bf16[2,2,48,256]{3,2,1,0:T(8,128)(2,1)}, u32[]{:S(2)}) copy-start(bf16[2,2,48,256]{3,2,1,0:T(8,128)(2,1)} %get-tuple-element.63) | copy-start | bytes 294916
  151.3 41.3 %copy-start.6 = (bf16[2,2,2,48,256]{4,3,2,1,0:T(8,128)(2,1)S(1)}, bf16[2,2,2,48,256]{4,3,2,1,0:T(8,128)(2,1)}, u32[]{:S(2)}) copy-start(bf16[2,2,2,48,256]{4,3,2,1,0:T(8,128)(2,1)} %get-tuple-element.97) | copy-start | bytes 589828
  188.5 47.5 %copy-start.33 = (bf16[2,2,48,256]{3,2,1,0:T(8,128)(2,1)}, bf16[2,2,48,256]{3,2,1,0:T(8,128)(2,1)S(1)}, u32[]{:S(2)}) copy-start(bf16[2,2,48,256]{3,2,1,0:T(8,128)(2,1)S(1)} %collective-permute-done.12.refs_1_) | copy-start | bytes 294916
  188.5 97.4 %collective-permute-start.16 = (bf16[2,2,48,256]{3,2,1,0:T(8,128)(2,1)S(1)}, bf16[2,2,48,256]{3,2,1,0:T(8,128)(2,1)S(1)}, u32[]{:S(2)}, u32[]{:S(2)}) collective-permute-start(bf16[2,2,48,256]{3,2,1,0:T(8,128)(2,1)S(1)} %copy-done.44), channel_id=1, source_target_pairs={{0,5},{1,4},{2,7},{3,6},{4,1},{5,0},{6,3},{7,2},{8,13},{9,12},{10,... | collective-permute-start | bytes 294920 | tf_op jit(solution)/shard_map/ppermute | solution.py:416
  188.6 47.4 %copy-start.34 = (bf16[2,2,48,256]{3,2,1,0:T(8,128)(2,1)}, bf16[2,2,48,256]{3,2,1,0:T(8,128)(2,1)S(1)}, u32[]{:S(2)}) copy-start(bf16[2,2,48,256]{3,2,1,0:T(8,128)(2,1)S(1)} %collective-permute-done.13.refs_2_) | copy-start | bytes 294916
  188.6 97.3 %collective-permute-start.17 = (bf16[2,2,48,256]{3,2,1,0:T(8,128)(2,1)S(1)}, bf16[2,2,48,256]{3,2,1,0:T(8,128)(2,1)S(1)}, u32[]{:S(2)}, u32[]{:S(2)}) collective-permute-start(bf16[2,2,48,256]{3,2,1,0:T(8,128)(2,1)S(1)} %copy-done.43), channel_id=1, source_target_pairs={{0,6},{1,7},{2,4},{3,5},{4,2},{5,3},{6,0},{7,1},{8,14},{9,15},{10,... | collective-permute-start | bytes 294920 | tf_op jit(solution)/shard_map/ppermute | solution.py:416
  190.4 45.6 %copy-start.35 = (bf16[2,2,48,256]{3,2,1,0:T(8,128)(2,1)}, bf16[2,2,48,256]{3,2,1,0:T(8,128)(2,1)S(1)}, u32[]{:S(2)}) copy-start(bf16[2,2,48,256]{3,2,1,0:T(8,128)(2,1)S(1)} %collective-permute-done.14.refs_3_) | copy-start | bytes 294916
  190.4 95.6 %collective-permute-start.18 = (bf16[2,2,48,256]{3,2,1,0:T(8,128)(2,1)S(1)}, bf16[2,2,48,256]{3,2,1,0:T(8,128)(2,1)S(1)}, u32[]{:S(2)}, u32[]{:S(2)}) collective-permute-start(bf16[2,2,48,256]{3,2,1,0:T(8,128)(2,1)S(1)} %copy-done.42), channel_id=1, source_target_pairs={{0,7},{1,6},{2,5},{3,4},{4,3},{5,2},{6,1},{7,0},{8,15},{9,14},{10,... | collective-permute-start | bytes 294920 | tf_op jit(solution)/shard_map/ppermute | solution.py:416
  291.4 56.7 %collective-permute-start.11 = (bf16[256,384]{1,0:T(8,128)(2,1)S(1)}, bf16[256,384]{1,0:T(8,128)(2,1)S(1)}, u32[]{:S(2)}, u32[]{:S(2)}) collective-permute-start(bf16[256,384]{1,0:T(8,128)(2,1)S(1)} %get-tuple-element.102), channel_id=1, source_target_pairs={{0,24},{8,0},{16,8},{24,16},{1,25},{9,1},{17,9},{25,17},{2,26},{10... | collective-permute-start | bytes 589832 | tf_op jit(solution)/shard_map/ppermute | solution.py:449
  293.5 54.7 %collective-permute-start.10 = (bf16[256,384]{1,0:T(8,128)(2,1)S(1)}, bf16[256,384]{1,0:T(8,128)(2,1)S(1)}, u32[]{:S(2)}, u32[]{:S(2)}) collective-permute-start(bf16[256,384]{1,0:T(8,128)(2,1)S(1)} %get-tuple-element.103), channel_id=1, source_target_pairs={{0,16},{8,24},{16,0},{24,8},{1,17},{9,25},{17,1},{25,9},{2,18},{10... | collective-permute-start | bytes 589832 | tf_op jit(solution)/shard_map/ppermute | solution.py:449
  293.5 54.7 %collective-permute-start.9 = (bf16[256,384]{1,0:T(8,128)(2,1)S(1)}, bf16[256,384]{1,0:T(8,128)(2,1)S(1)}, u32[]{:S(2)}, u32[]{:S(2)}) collective-permute-start(bf16[256,384]{1,0:T(8,128)(2,1)S(1)} %get-tuple-element.104), channel_id=1, source_target_pairs={{0,8},{8,16},{16,24},{24,0},{1,9},{9,17},{17,25},{25,1},{2,10},{10... | collective-permute-start | bytes 589832 | tf_op jit(solution)/shard_map/ppermute | solution.py:449
  (42 other events, 471.1 us)
Sparse Core Ops, SparseCore 0:
  10.2 39.1 all-gather.2

commit v3 on v2

--- a/solution.py
+++ b/solution.py
@@ -93,7 +93,7 @@
     planes = mine.shape[0]
     rows = (mine.shape[1] - ID_ROWS) // 2
     touch = touched.shape[1]
-    n_own = len(blocks)
+    n_own = blocks.shape[0]
     half = sum(sizes)
     aligned = piece % 16 == 0
     starts = [sum(sizes[:i]) for i in range(len(sizes))]
@@ -101,10 +101,10 @@
     n_grads = len(sizes) * n_blocks
 
     def body(pos_ref, touched_ref, slot_ref, mine_ref, other_ref, *rest):
-        block_refs = rest[:n_blocks]
-        pred_refs = rest[n_blocks : n_blocks + 2]
-        grad_refs = rest[n_blocks + 2 : n_blocks + 2 + n_grads]
-        acc, id_cols, held, sorted_rows, pred, full_of, tasks, sems = rest[n_blocks + 2 + n_grads :]
+        blocks_ref = rest[0]
+        pred_refs = rest[1:3]
+        grad_refs = rest[3 : 3 + n_grads]
+        acc, id_cols, held, sorted_rows, pred, full_of, tasks, sems = rest[3 + n_grads :]
         own_at = pos_ref[1]
         core = lax.rem(own_at, 2)
         partner = own_at + 1 - 2 * core
@@ -117,16 +117,12 @@
         if aligned:
             block_copies = [
                 pltpu.make_async_copy(
-                    ref,
-                    held.at[
-                        :, :, pl.ds(pl.multiple_of((own_at ^ j) * piece, 16), piece), :
-                    ],
-                    sems.at[2 + j],
+                    blocks_ref.at[s], held.at[:, :, pl.ds(s * piece, piece), :], sems.at[2 + s]
                 )
-                for j, ref in enumerate(block_refs)
+                for s in range(n_own)
             ]
         else:
-            block_copies = [pltpu.make_async_copy(block_refs[0], held, sems.at[2])]
+            block_copies = [pltpu.make_async_copy(blocks_ref, held, sems.at[2])]
         for copy in row_copies + block_copies:
             copy.start()
 
@@ -245,19 +241,17 @@
     ]
     own_at = pos[1]
     if not aligned:
-        order = own_at ^ jnp.arange(n_own, dtype=jnp.int32)
-        stacked = jnp.take(jnp.stack(blocks), order, axis=0)
-        blocks = [stacked.transpose(1, 2, 0, 3, 4).reshape(half, 2, SITES, width)]
+        blocks = blocks.transpose(1, 2, 0, 3, 4).reshape(half, 2, SITES, width)
     anywhere = pl.BlockSpec(memory_space=pl.ANY)
     found = pl.pallas_call(
         body,
         out_shape=[pred_shape, pred_shape] + grad_shapes,
-        in_specs=[smem(), smem(), smem()] + [anywhere] * (2 + n_blocks),
+        in_specs=[smem(), smem(), smem()] + [anywhere] * 3,
         out_specs=[vmem()] * (2 + n_grads),
         scratch_shapes=scratch,
         compiler_params=params(),
         name="local_grads",
-    )(pos, touched, slot_map, mine, other, *blocks)
+    )(pos, touched, slot_map, mine, other, blocks)
     grads = []
     for chunk in range(len(sizes)):
         outs = found[2 + chunk * n_blocks : 2 + (chunk + 1) * n_blocks]
@@ -347,33 +341,61 @@
     )(pos, *arrived, weights, moment1, moment2, *before)
 
 
-def place_weights(chunk, start, half, before):
-    _, size, _, piece, full = chunk.shape
-
-    def body(chunk_ref, *refs):
-        out_ref, sems = refs[-2:]
-        copies = [
-            pltpu.make_async_copy(
-                chunk_ref.at[h], out_ref.at[pl.ds(h * half + start, size)], sems.at[h]
-            )
-            for h in range(2)
+def place_weights(pos, pieces, start, half, before):
+    n_dp = len(pieces)
+    _, size, _, piece, width = pieces[0].shape
+    per = math.gcd(math.gcd(size, start), half)
+    pieces = list(pieces)
+    far = isinstance(pieces[-1], tuple)
+    if far:
+        pieces[-1:] = pieces[-1]
+    n_in = len(pieces)
+
+    def body(pos_ref, *refs):
+        out_ref = refs[-1]
+        for k in range(n_dp):
+
+            @pl.when(pos_ref[0] == k)
+            def _(k=k):
+                for j in range(n_dp):
+                    first = (k ^ j) * width
+                    i = n_dp if far and j == n_dp - 1 and k in (0, n_dp - 1) else j
+                    out_ref[:, :, :, first : first + width] = refs[i][0]
+
+    def place(h, i, pos_ref):
+        return (h * (half // per) + start // per + i, 0, 0, 0)
+
+    grid_spec = pltpu.PrefetchScalarGridSpec(
+        num_scalar_prefetch=1,
+        grid=(2, size // per),
+        in_specs=[
+            pl.BlockSpec((1, per, 2, piece, width), lambda h, i, pos_ref: (h, i, 0, 0, 0))
         ]
-        for copy in copies:
-            copy.start()
-        for copy in copies:
-            copy.wait()
-
-    anywhere = pl.BlockSpec(memory_space=pl.ANY)
+        * n_in
+        + [pl.BlockSpec(memory_space=pl.ANY)] * len(before),
+        out_specs=pl.BlockSpec((per, 2, piece, n_dp * width), place),
+    )
     return pl.pallas_call(
         body,
-        out_shape=jax.ShapeDtypeStruct((2 * half, 2, piece, full), jnp.bfloat16),
-        in_specs=[anywhere] * (1 + len(before)),
-        out_specs=anywhere,
-        scratch_shapes=[pltpu.SemaphoreType.DMA((2,))],
-        input_output_aliases={1: 0} if before else {},
+        out_shape=jax.ShapeDtypeStruct((2 * half, 2, piece, n_dp * width), jnp.bfloat16),
+        grid_spec=grid_spec,
+        input_output_aliases={1 + n_in: 0} if before else {},
         compiler_params=params(),
         name="place_weights",
-    )(chunk, *before)
+    )(pos, *pieces, *before)
+
+
+def gather_planes(fresh, dp_at, n_dp):
+    if n_dp != 4:
+        whole = lax.all_gather(fresh, "dp", axis=0)
+        return [
+            lax.dynamic_index_in_dim(whole, dp_at ^ j, 0, keepdims=False) for j in range(n_dp)
+        ]
+    two = lax.ppermute(fresh, "dp", [(0, 2), (1, 3), (2, 0), (3, 1)])
+    one = lax.ppermute(fresh, "dp", [(0, 1), (1, 0), (2, 3), (3, 2)])
+    middle = lax.ppermute(fresh, "dp", [(1, 2), (2, 1)])
+    outer = lax.ppermute(two, "dp", [(2, 3), (1, 0)])
+    return [fresh, one, two, (middle, outer)]
 
 
 def finish_predicted(perm, parts):
@@ -418,13 +440,11 @@
     packed, perm = pack_rows(row_insertion.reshape(1, rows), signals, cotangent)
     mine = lax.all_gather(packed, "dp", axis=0)
 
-    def column(which):
-        return lax.dynamic_slice(
-            weights, (which * half, 0, 0, dp_at * width), (half, 2, piece, width)
-        )
-
-    outgoing = (column(core), column(1 - core))
-    blocks = [outgoing[0]] + [across(outgoing[j % 2], j) for j in range(1, n_own)]
+    column = lax.dynamic_slice_in_dim(weights, dp_at * width, width, 3)
+    outgoing = jnp.broadcast_to(
+        column.reshape(1, 2, half, 2, piece, width), (n_own // 2, 2, half, 2, piece, width)
+    ).reshape(n_own, half, 2, piece, width)
+    blocks = lax.all_to_all(outgoing, "own", split_axis=0, concat_axis=0, tiled=True)
     other = across(mine, 1)
 
     pred_mine, pred_other, grads = local_grads(
@@ -433,11 +453,16 @@
     moments = []
     new_weights = []
     start = 0
+    arrived = None
     for size, chunk in zip(sizes, grads):
+        if arrived:
+            for j in range(1, n_own):
+                before = arrived[j] if j < n_own // 2 else fresh
+                chunk[j], _ = lax.optimization_barrier((chunk[j], before))
         arrived = [chunk[0]] + [across(chunk[j], j) for j in range(1, n_own)]
         fresh, *moments = adam(pos, arrived, weights, moment1, moment2, start, moments)
-        whole = lax.all_gather(fresh, "dp", axis=4, tiled=True)
-        new_weights = [place_weights(whole, start, half, new_weights)]
+        pieces = gather_planes(fresh, dp_at, n_dp)
+        new_weights = [place_weights(pos, pieces, start, half, new_weights)]
         start += size
     new_weights = new_weights[0]
     new_moment1, new_moment2 = moments

time: 361 us -> 216 us (0.60)
  Pallas kernels: 135 us -> 45.4 us
  blocking collectives: 84.6 us -> 0 us
  starting transfers between devices: 40 us -> 66.7 us
    pallas_call x4, Pallas kernels: 99.8 us -> 11.1 us  [place_weights(): pl.pallas_call(body, out_shape=jax.ShapeDtypeStruct((2 * half, 2, piece,...]
    all_gather x4 -> x0, blocking collectives: 84.6 us -> none  [shards(): whole = lax.all_gather(fresh, 'dp', axis=4, tiled=True)]
    ppermute x0 -> x16, starting transfers between devices: none -> 28.8 us  [the longest x4 13.8 us: gather_planes(): two = lax.ppermute(fresh, 'dp', [(0, 2), (1, 3), (2, 0), (3, 1)])]
    ppermute x0 -> x16, waiting for transfers between devices: none -> 22.1 us  [the longest x4 13.5 us: gather_planes(): two = lax.ppermute(fresh, 'dp', [(0, 2), (1, 3), (2, 0), (3, 1)])]
    ppermute x37 -> x30, waiting for transfers between devices: 37.1 us -> 18.9 us  [across(): return lax.ppermute(value, 'own', [(o, o ^ j) for o in range(n_own)])]
    ppermute x37 -> x30, starting transfers between devices: 37.1 us -> 28.7 us  [across(): return lax.ppermute(value, 'own', [(o, o ^ j) for o in range(n_own)])]
    all_gather x1, waiting for transfers between devices: 39.7 us -> 32 us  [shards(): mine = lax.all_gather(packed, 'dp', axis=0)]
    all_to_all x0 -> x1, starting transfers between devices: none -> 4.4 us  [shards(): lax.all_to_all(outgoing, 'own', split_axis=0, concat_axis=0, tiled=True)]
  transfers between devices with their start and end apart: 41 -> 51, of which waited for: 11 -> 17; matrix products, arithmetic and copies ran while one was open for 1% -> 3% of each run, Pallas kernels for 32% -> 12%
where the time goes in v3:
time: 216 us; the launch traced here: 213 us
  waiting for transfers between devices  76.1 us (35%)
  starting transfers between devices  66.7 us (31%)
  Pallas kernels  45.4 us (21%)
  between operations  14.8 us (7%)
  local copies, waits for them, and re-layouts  9.3 us (4%)
    all_gather x1, waiting for transfers between devices, shards(): mine = lax.all_gather(packed, 'dp', axis=0)  32 us
    ppermute x30, starting transfers between devices, across(): return lax.ppermute(value, 'own', [(o, o ^ j) for o in range(n_own)])  28.7 us
    ppermute x30, waiting for transfers between devices, across(): return lax.ppermute(value, 'own', [(o, o ^ j) for o in range(n_own)])  18.9 us
    pallas_call x1, Pallas kernels, local_grads(): pl.pallas_call(body, out_shape=[pred_shape, pred_shape] + grad_shapes, in...  15 us
    pallas_call x4, Pallas kernels, adam(): pl.pallas_call(body, out_shape=[jax.ShapeDtypeStruct((2, size, 2, piece,...  14.7 us
    ppermute x4, starting transfers between devices, gather_planes(): two = lax.ppermute(fresh, 'dp', [(0, 2), (1, 3), (2, 0), (3, 1)])  13.8 us
    ppermute x4, waiting for transfers between devices, gather_planes(): two = lax.ppermute(fresh, 'dp', [(0, 2), (1, 3), (2, 0), (3, 1)])  13.5 us
    pallas_call x4, Pallas kernels, place_weights(): pl.pallas_call(body, out_shape=jax.ShapeDtypeStruct((2 * half, 2, piece,...  11.1 us
  transfers between devices with their start and end apart: 51, of which 17 were waited for; matrix products, arithmetic and copies ran while one was open for 3% of the time, Pallas kernels for 12%

profile of v3, /device:TPU:2, one launch (start us, length us, event | category | flops | bytes accessed | tf_op | source)
XLA Modules:
  0.0 213.1 jit_solution(2650571400087249769)
XLA Ops:
  7.2 2.4 %pack_rows.1 = (bf16[528,384]{1,0:T(8,128)(2,1)}, bf16[256,256]{1,0:T(8,128)(2,1)}) custom-call(s32[1,256]{1,0:T(1,128)} %bitcast.18, bf16[256,384]{1,0:T(8,128)(2,1)} %sig_ref.1, bf16[256,384]{1,0:T(8,128)(2,1)} %cot_ref.1), custom_call_target="tpu_custom_call" | custom-call | tf_op jit(solution)/shard_map/pack_rows/pallas_call | solution.py:79
  9.6 1.2 constant_dynamic-slice_fusion
  10.8 2.0 broadcast_in_dim.8
  12.9 4.4 %all-to-all-start = ((bf16[8,8,2,48,256]{4,3,2,1,0:T(8,128)(2,1)}), bf16[8,8,2,48,256]{4,3,2,1,0:T(8,128)(2,1)S(1)}, u32[]{:S(2)}, u32[]{:S(2)}) async-start(bf16[8,8,2,48,256]{4,3,2,1,0:T(8,128)(2,1)} %bitcast.14), calls=%async_computation | async-start | bytes 6291456 | tf_op jit(solution)/shard_map/all_to_all | solution.py:447
  17.3 32.0 %all-gather.3.cloned.1.call-done = bf16[2112,384]{1,0:T(8,128)(2,1)} async-done(((bf16[528,384]{1,0:T(8,128)(2,1)}), bf16[2112,384]{1,0:T(8,128)(2,1)}) %all-gather.3.cloned.1.call-update) | async-done | bytes 1622032 | tf_op jit(solution)/shard_map/all_gather | solution.py:441
  50.6 3.1 %all-to-all-done.rest_0_ = bf16[8,8,2,48,256]{4,3,2,1,0:T(8,128)(2,1)S(1)} async-done(((bf16[8,8,2,48,256]{4,3,2,1,0:T(8,128)(2,1)}), bf16[8,8,2,48,256]{4,3,2,1,0:T(8,128)(2,1)S(1)}, u32[]{:S(2)}, u32[]{:S(2)}) %all-to-all-start) | async-done | bytes 3145760 | tf_op jit(solution)/shard_map/all_to_all | solution.py:447
  53.7 1.7 copy-done
  55.3 15.0 %local_grads.1 = (bf16[4,256,384]{2,1,0:T(8,128)(2,1)}, bf16[4,256,384]{2,1,0:T(8,128)(2,1)}, bf16[2,2,48,256]{3,2,1,0:T(8,128)(2,1)}, bf16[2,2,48,256]{3,2,1,0:...) custom-call(s32[2]{0:T(128)} %pad_add_fusion.pos_ref, ...), custom_call_target="tpu_custom_call" | custom-call | tf_op jit(solution)/shard_map/local_grads/pallas_call | solution.py:246
  72.8 2.9 %collective-permute-start.17 = (bf16[2,2,48,256]{3,2,1,0:T(8,128)(2,1)}, bf16[2,2,48,256]{3,2,1,0:T(8,128)(2,1)S(1)}, u32[]{:S(2)}, u32[]{:S(2)}) collective-permute-start(bf16[2,2,48,256]{3,2,1,0:T(8,128)(2,1)} %get-tuple-element.105), channel_id=1, source_target_pairs={{0,4},{1,5},{2,6},{3,7},{4,0},{5,1},{6,2},{7,3},{8,12},{9,13},{10,... | collective-permute-start | bytes 294920 | tf_op jit(solution)/shard_map/ppermute | solution.py:438
  75.7 1.2 collective-permute-start.19
  79.4 1.8 collective-permute-start.10
  81.3 3.7 %collective-permute-done.18.refs_5_ = bf16[2,2,48,256]{3,2,1,0:T(8,128)(2,1)S(1)} collective-permute-done((bf16[2,2,48,256]{3,2,1,0:T(8,128)(2,1)}, bf16[2,2,48,256]{3,2,1,0:T(8,128)(2,1)S(1)}, u32[]{:S(2)}, u32[]{:S(2)}) %collective-permute-start.18) | collective-permute-done | bytes 98336 | tf_op jit(solution)/shard_map/ppermute | solution.py:438
  86.1 3.7 %adam_step.4 = (bf16[2,2,2,48,256]{4,3,2,1,0:T(8,128)(2,1)}, f32[16,2,48,256]{3,2,1,0:T(8,128)}, f32[16,2,48,256]{3,2,1,0:T(8,128)}) custom-call(s32[2]{0:T(128)} %pad_add_fusion.pos_ref, bf16[2,2,48,256]{3,2,1,0:T(8,128)(2,1)} %get-tuple-element.104.refs_0_, bf16[2,2,48,256]{3,2,1,0:T(8,128)(2,1)} %copy-done.35, bf16[2,2,48,256]{3,2,1,0:T(8,128)(2,1)} %copy-done.37, ...), custom_call_target="tpu_custom_call" | custom-call | tf_op jit(solution)/shard_map/adam_step/pallas_call | solution.py:330
  89.7 1.8 collective-permute-start.21
  91.6 2.6 %collective-permute-start.23 = (bf16[2,2,48,256]{3,2,1,0:T(8,128)(2,1)S(1)}, bf16[2,2,48,256]{3,2,1,0:T(8,128)(2,1)S(1)}, u32[]{:S(2)}, u32[]{:S(2)}) collective-permute-start(bf16[2,2,48,256]{3,2,1,0:T(8,128)(2,1)S(1)} %copy-done.67), channel_id=1, source_target_pairs={{0,6},{1,7},{2,4},{3,5},{4,2},{5,3},{6,0},{7,1},{8,14},{9,15},{10,... | collective-permute-start | bytes 294920 | tf_op jit(solution)/shard_map/ppermute | solution.py:438
  95.1 1.7 collective-permute-start.11
  96.8 3.8 %collective-permute-done.22.refs_5_ = bf16[2,2,48,256]{3,2,1,0:T(8,128)(2,1)S(1)} collective-permute-done((bf16[2,2,48,256]{3,2,1,0:T(8,128)(2,1)S(1)}, bf16[2,2,48,256]{3,2,1,0:T(8,128)(2,1)S(1)}, u32[]{:S(2)}, u32[]{:S(2)}) %collective-permute-start.22) | collective-permute-done | bytes 98336 | tf_op jit(solution)/shard_map/ppermute | solution.py:438
  100.7 1.6 collective-permute-start.15
  103.0 3.7 %adam_step.5 = (bf16[2,2,2,48,256]{4,3,2,1,0:T(8,128)(2,1)}, f32[16,2,48,256]{3,2,1,0:T(8,128)}, f32[16,2,48,256]{3,2,1,0:T(8,128)}) custom-call(s32[2]{0:T(128)} %pad_add_fusion.pos_ref, bf16[2,2,48,256]{3,2,1,0:T(8,128)(2,1)} %get-tuple-element.102.refs_0_, bf16[2,2,48,256]{3,2,1,0:T(8,128)(2,1)} %copy-done.28, ...), custom_call_target="tpu_custom_call", output_to_operand_aliasing={{1}: (12, {}), {2}: (13, {})} | custom-call | tf_op jit(solution)/shard_map/adam_step/pallas_call | solution.py:330
  106.7 1.8 collective-permute-start.25
  109.0 1.9 collective-permute-start.27
  112.3 3.6 %collective-permute-start.46 = (bf16[2,2,2,48,256]{4,3,2,1,0:T(8,128)(2,1)S(1)}, bf16[2,2,2,48,256]{4,3,2,1,0:T(8,128)(2,1)S(1)}, u32[]{:S(2)}, u32[]{:S(2)}) collective-permute-start(bf16[2,2,2,48,256]{4,3,2,1,0:T(8,128)(2,1)S(1)} %copy-done.2), channel_id=1, source_target_pairs={{0,16},{8,24},{16,0},{24,8},{1,17},{9,25},{17,1},{25,9},{2,18},{10... | collective-permute-start | bytes 589832 | tf_op jit(solution)/shard_map/ppermute | solution.py:394
  115.9 1.5 collective-permute-start.45
  118.1 5.3 %collective-permute-done.28.refs_7_ = bf16[2,2,48,256]{3,2,1,0:T(8,128)(2,1)S(1)} collective-permute-done((bf16[2,2,48,256]{3,2,1,0:T(8,128)(2,1)S(1)}, bf16[2,2,48,256]{3,2,1,0:T(8,128)(2,1)S(1)}, u32[]{:S(2)}, u32[]{:S(2)}) %collective-permute-start.28) | collective-permute-done | bytes 98336 | tf_op jit(solution)/shard_map/ppermute | solution.py:438
  123.6 5.1 %collective-permute-done.46.refs_2_ = bf16[2,2,2,48,256]{4,3,2,1,0:T(8,128)(2,1)S(1)} collective-permute-done((bf16[2,2,2,48,256]{4,3,2,1,0:T(8,128)(2,1)S(1)}, bf16[2,2,2,48,256]{4,3,2,1,0:T(8,128)(2,1)S(1)}, u32[]{:S(2)}, u32[]{:S(2)}) %collective-permute-start.46) | collective-permute-done | bytes 196640 | tf_op jit(solution)/shard_map/ppermute | solution.py:394
  128.9 3.7 %adam_step.6 = (bf16[2,2,2,48,256]{4,3,2,1,0:T(8,128)(2,1)}, f32[16,2,48,256]{3,2,1,0:T(8,128)}, f32[16,2,48,256]{3,2,1,0:T(8,128)}) custom-call(s32[2]{0:T(128)} %pad_add_fusion.pos_ref, bf16[2,2,48,256]{3,2,1,0:T(8,128)(2,1)} %get-tuple-element.100.refs_0_, bf16[2,2,48,256]{3,2,1,0:T(8,128)(2,1)} %copy-done.22, ...), custom_call_target="tpu_custom_call", output_to_operand_aliasing={{1}: (12, {}), {2}: (13, {})} | custom-call | tf_op jit(solution)/shard_map/adam_step/pallas_call | solution.py:330
  133.3 2.3 %collective-permute-start.30 = (bf16[2,2,48,256]{3,2,1,0:T(8,128)(2,1)S(1)}, bf16[2,2,48,256]{3,2,1,0:T(8,128)(2,1)S(1)}, u32[]{:S(2)}, u32[]{:S(2)}) collective-permute-start(bf16[2,2,48,256]{3,2,1,0:T(8,128)(2,1)S(1)} %copy-done.54), channel_id=1, source_target_pairs={{0,5},{1,4},{2,7},{3,6},{4,1},{5,0},{6,3},{7,2},{8,13},{9,12},{10,... | collective-permute-start | bytes 294920 | tf_op jit(solution)/shard_map/ppermute | solution.py:438
  136.3 2.4 %collective-permute-start.42 = (bf16[2,2,2,48,256]{4,3,2,1,0:T(8,128)(2,1)S(1)}, bf16[2,2,2,48,256]{4,3,2,1,0:T(8,128)(2,1)S(1)}, u32[]{:S(2)}, u32[]{:S(2)}) collective-permute-start(bf16[2,2,2,48,256]{4,3,2,1,0:T(8,128)(2,1)S(1)} %copy-done.10), channel_id=1, source_target_pairs={{0,16},{8,24},{16,0},{24,8},{1,17},{9,25},{17,1},{25,9},{2,18},{10... | collective-permute-start | bytes 589832 | tf_op jit(solution)/shard_map/ppermute | solution.py:394
  140.9 3.4 %collective-permute-done.31.refs_6_ = bf16[2,2,48,256]{3,2,1,0:T(8,128)(2,1)S(1)} collective-permute-done((bf16[2,2,48,256]{3,2,1,0:T(8,128)(2,1)S(1)}, bf16[2,2,48,256]{3,2,1,0:T(8,128)(2,1)S(1)}, u32[]{:S(2)}, u32[]{:S(2)}) %collective-permute-start.31) | collective-permute-done | bytes 98336 | tf_op jit(solution)/shard_map/ppermute | solution.py:438
  144.3 1.7 collective-permute-start.41
  147.1 2.7 %collective-permute-start.38 = (bf16[2,2,2,48,256]{4,3,2,1,0:T(8,128)(2,1)}, bf16[2,2,2,48,256]{4,3,2,1,0:T(8,128)(2,1)S(1)}, u32[]{:S(2)}, u32[]{:S(2)}) collective-permute-start(bf16[2,2,2,48,256]{4,3,2,1,0:T(8,128)(2,1)} %get-tuple-element.129.refs_0_), channel_id=1, source_target_pairs={{0,16},{8,24},{16,0},{24,8},{1,17},{9,25},{17,1},{25,9},{2,18},{10... | collective-permute-start | bytes 589832 | tf_op jit(solution)/shard_map/ppermute | solution.py:394
  149.8 1.4 collective-permute-done.42.refs_2_
  151.3 3.7 %adam_step.7 = (bf16[2,2,2,48,256]{4,3,2,1,0:T(8,128)(2,1)}, f32[16,2,48,256]{3,2,1,0:T(8,128)}, f32[16,2,48,256]{3,2,1,0:T(8,128)}) custom-call(s32[2]{0:T(128)} %pad_add_fusion.pos_ref, bf16[2,2,48,256]{3,2,1,0:T(8,128)(2,1)} %get-tuple-element.77.refs_0_, bf16[2,2,48,256]{3,2,1,0:T(8,128)(2,1)} %copy-done.24, ...), custom_call_target="tpu_custom_call", output_to_operand_aliasing={{1}: (12, {}), {2}: (13, {})} | custom-call | tf_op jit(solution)/shard_map/adam_step/pallas_call | solution.py:330
  155.0 1.3 collective-permute-start.48
  156.3 5.1 %collective-permute-start.34 = (bf16[2,2,2,48,256]{4,3,2,1,0:T(8,128)(2,1)}, bf16[2,2,2,48,256]{4,3,2,1,0:T(8,128)(2,1)S(1)}, u32[]{:S(2)}, u32[]{:S(2)}) collective-permute-start(bf16[2,2,2,48,256]{4,3,2,1,0:T(8,128)(2,1)} %get-tuple-element.139.refs_0_), channel_id=1, source_target_pairs={{0,16},{8,24},{16,0},{24,8},{1,17},{9,25},{17,1},{25,9},{2,18},{10... | collective-permute-start | bytes 589832 | tf_op jit(solution)/shard_map/ppermute | solution.py:394
  161.4 6.9 %collective-permute-done.38.refs_2_ = bf16[2,2,2,48,256]{4,3,2,1,0:T(8,128)(2,1)S(1)} collective-permute-done((bf16[2,2,2,48,256]{4,3,2,1,0:T(8,128)(2,1)}, bf16[2,2,2,48,256]{4,3,2,1,0:T(8,128)(2,1)S(1)}, u32[]{:S(2)}, u32[]{:S(2)}) %collective-permute-start.38) | collective-permute-done | bytes 196640 | tf_op jit(solution)/shard_map/ppermute | solution.py:394
  169.0 1.3 collective-permute-start.44
  170.3 1.3 collective-permute-start.40
  172.7 4.0 %collective-permute-start.33 = (bf16[2,2,2,48,256]{4,3,2,1,0:T(8,128)(2,1)S(1)}, bf16[2,2,2,48,256]{4,3,2,1,0:T(8,128)(2,1)S(1)}, u32[]{:S(2)}, u32[]{:S(2)}) collective-permute-start(bf16[2,2,2,48,256]{4,3,2,1,0:T(8,128)(2,1)S(1)} %copy-done.15), channel_id=1, source_target_pairs={{0,8},{8,0},{16,24},{24,16},{1,9},{9,1},{17,25},{25,17},{2,10},{10... | collective-permute-start | bytes 589832 | tf_op jit(solution)/shard_map/ppermute | solution.py:395
  176.7 1.3 collective-permute-start.36
  178.0 2.5 %collective-permute-start.4 = (bf16[256,384]{1,0:T(8,128)(2,1)S(1)}, bf16[256,384]{1,0:T(8,128)(2,1)S(1)}, u32[]{:S(2)}, u32[]{:S(2)}) collective-permute-start(bf16[256,384]{1,0:T(8,128)(2,1)S(1)} %get-tuple-element.142), channel_id=1, source_target_pairs={{0,24},{8,0},{16,8},{24,16},{1,25},{9,1},{17,9},{25,17},{2,26},{10... | collective-permute-start | bytes 589832 | tf_op jit(solution)/shard_map/ppermute | solution.py:474
  180.5 1.7 collective-permute-start.3
  183.7 2.8 %place_weights.4.refs_5_ = bf16[16,2,48,1024]{3,2,1,0:T(8,128)(2,1)} custom-call(s32[2]{0:T(128)} %pad_add_fusion.pos_ref, bf16[2,2,2,48,256]{4,3,2,1,0:T(8,128)(2,1)} %get-tuple-element.109.refs_0_, bf16[2,2,2,48,256]{4,3,2,1,0:T(8,128)(2,1)} %copy-done.5, bf16[2,2,2,48,256]{4,3,2,1,0:T(8,128)(2,1)} %copy-done.4, bf16[2,2,2,48,256]{4,3,2,1,0:T(8,128)(2,1)} %copy-done.3, ...), custom_call_target="tpu_custom_call" | custom-call | tf_op jit(solution)/shard_map/place_weights/pallas_call | solution.py:378
  186.5 2.8 %place_weights.5.refs_5_ = bf16[16,2,48,1024]{3,2,1,0:T(8,128)(2,1)} custom-call(s32[2]{0:T(128)} %pad_add_fusion.pos_ref, bf16[2,2,2,48,256]{4,3,2,1,0:T(8,128)(2,1)} %get-tuple-element.119.refs_0_, bf16[2,2,2,48,256]{4,3,2,1,0:T(8,128)(2,1)} %copy-done.13, bf16[2,2,2,48,256]{4,3,2,1,0:T(8,128)(2,1)} %copy-done.12, ...), custom_call_target="tpu_custom_call", output_to_operand_aliasing={{}: (6, {})} | custom-call | tf_op jit(solution)/shard_map/place_weights/pallas_call | solution.py:378
  189.3 2.8 %place_weights.6.refs_5_ = bf16[16,2,48,1024]{3,2,1,0:T(8,128)(2,1)} custom-call(s32[2]{0:T(128)} %pad_add_fusion.pos_ref, bf16[2,2,2,48,256]{4,3,2,1,0:T(8,128)(2,1)} %get-tuple-element.129.refs_0_, bf16[2,2,2,48,256]{4,3,2,1,0:T(8,128)(2,1)} %copy-done.17, bf16[2,2,2,48,256]{4,3,2,1,0:T(8,128)(2,1)} %copy-done.16, ...), custom_call_target="tpu_custom_call", output_to_operand_aliasing={{}: (6, {})} | custom-call | tf_op jit(solution)/shard_map/place_weights/pallas_call | solution.py:378
  192.0 7.8 %collective-permute-done.36.refs_4_ = bf16[2,2,2,48,256]{4,3,2,1,0:T(8,128)(2,1)S(1)} collective-permute-done((bf16[2,2,2,48,256]{4,3,2,1,0:T(8,128)(2,1)S(1)}, bf16[2,2,2,48,256]{4,3,2,1,0:T(8,128)(2,1)S(1)}, u32[]{:S(2)}, u32[]{:S(2)}) %collective-permute-start.36) | collective-permute-done | bytes 196640 | tf_op jit(solution)/shard_map/ppermute | solution.py:397
  200.5 2.8 %place_weights.7 = bf16[16,2,48,1024]{3,2,1,0:T(8,128)(2,1)} custom-call(s32[2]{0:T(128)} %pad_add_fusion.pos_ref, bf16[2,2,2,48,256]{4,3,2,1,0:T(8,128)(2,1)} %get-tuple-element.139.refs_0_, bf16[2,2,2,48,256]{4,3,2,1,0:T(8,128)(2,1)} %copy-done.20, bf16[2,2,2,48,256]{4,3,2,1,0:T(8,128)(2,1)} %copy-done.18, ...), custom_call_target="tpu_custom_call", output_to_operand_aliasing={{}: (6, {})} | custom-call | tf_op jit(solution)/shard_map/place_weights/pallas_call | solution.py:378
  204.1 2.2 %finish_predicted.1 = bf16[256,384]{1,0:T(8,128)(2,1)} custom-call(bf16[256,256]{1,0:T(8,128)(2,1)} %get-tuple-element.73.perm_ref, bf16[256,384]{1,0:T(8,128)(2,1)} %get-tuple-element.145.refs_0_, bf16[256,384]{1,0:T(8,128)(2,1)} %copy-done.9, bf16[256,384]{1,0:T(8,128)(2,1)} %copy-done.8, bf16[256,384]{1,0:T(8,128)(2,1)} %copy-done.7), custom_call_target="tpu_custom_call" | custom-call | tf_op jit(solution)/shard_map/finish_predicted/pallas_call | solution.py:413
  (212 shorter events, 21.2 us)
Async XLA Ops:
  7.2 42.1 %all-gather.3.cloned.1.call-start = ((), (), s32[]{:S(2)}) async-start(), calls=%async_computation.1 | async-start | bytes 2027520 | tf_op jit(solution)/shard_map/all_gather | solution.py:441
  12.9 40.8 %all-to-all-start = ((bf16[8,8,2,48,256]{4,3,2,1,0:T(8,128)(2,1)}), bf16[8,8,2,48,256]{4,3,2,1,0:T(8,128)(2,1)S(1)}, u32[]{:S(2)}, u32[]{:S(2)}) async-start(bf16[8,8,2,48,256]{4,3,2,1,0:T(8,128)(2,1)} %bitcast.14), calls=%async_computation | async-start | bytes 6291456 | tf_op jit(solution)/shard_map/all_to_all | solution.py:447
  71.4 5.9 %collective-permute-start.9 = (bf16[2,2,48,256]{3,2,1,0:T(8,128)(2,1)}, bf16[2,2,48,256]{3,2,1,0:T(8,128)(2,1)S(1)}, u32[]{:S(2)}, u32[]{:S(2)}) collective-permute-start(bf16[2,2,48,256]{3,2,1,0:T(8,128)(2,1)} %get-tuple-element.88), channel_id=1, source_target_pairs={{0,2},{1,3},{2,0},{3,1},{4,6},{5,7},{6,4},{7,5},{8,10},{9,11},{10,... | collective-permute-start | bytes 294920 | tf_op jit(solution)/shard_map/ppermute | solution.py:438
  72.0 6.4 %collective-permute-start.13 = (bf16[2,2,48,256]{3,2,1,0:T(8,128)(2,1)}, bf16[2,2,48,256]{3,2,1,0:T(8,128)(2,1)S(1)}, u32[]{:S(2)}, u32[]{:S(2)}) collective-permute-start(bf16[2,2,48,256]{3,2,1,0:T(8,128)(2,1)} %get-tuple-element.95), channel_id=1, source_target_pairs={{0,3},{1,2},{2,1},{3,0},{4,7},{5,6},{6,5},{7,4},{8,11},{9,10},{10,... | collective-permute-start | bytes 294920 | tf_op jit(solution)/shard_map/ppermute | solution.py:438
  72.8 6.6 %collective-permute-start.17 = (bf16[2,2,48,256]{3,2,1,0:T(8,128)(2,1)}, bf16[2,2,48,256]{3,2,1,0:T(8,128)(2,1)S(1)}, u32[]{:S(2)}, u32[]{:S(2)}) collective-permute-start(bf16[2,2,48,256]{3,2,1,0:T(8,128)(2,1)} %get-tuple-element.105), channel_id=1, source_target_pairs={{0,4},{1,5},{2,6},{3,7},{4,0},{5,1},{6,2},{7,3},{8,12},{9,13},{10,... | collective-permute-start | bytes 294920 | tf_op jit(solution)/shard_map/ppermute | solution.py:438
  75.7 9.3 %collective-permute-start.18 = (bf16[2,2,48,256]{3,2,1,0:T(8,128)(2,1)}, bf16[2,2,48,256]{3,2,1,0:T(8,128)(2,1)S(1)}, u32[]{:S(2)}, u32[]{:S(2)}) collective-permute-start(bf16[2,2,48,256]{3,2,1,0:T(8,128)(2,1)} %get-tuple-element.106), channel_id=1, source_target_pairs={{0,5},{1,4},{2,7},{3,6},{4,1},{5,0},{6,3},{7,2},{8,13},{9,12},{10,... | collective-permute-start | bytes 294920 | tf_op jit(solution)/shard_map/ppermute | solution.py:438
  75.7 9.6 %collective-permute-start.19 = (bf16[2,2,48,256]{3,2,1,0:T(8,128)(2,1)}, bf16[2,2,48,256]{3,2,1,0:T(8,128)(2,1)S(1)}, u32[]{:S(2)}, u32[]{:S(2)}) collective-permute-start(bf16[2,2,48,256]{3,2,1,0:T(8,128)(2,1)} %get-tuple-element.107), channel_id=1, source_target_pairs={{0,6},{1,7},{2,4},{3,5},{4,2},{5,3},{6,0},{7,1},{8,14},{9,15},{10,... | collective-permute-start | bytes 294920 | tf_op jit(solution)/shard_map/ppermute | solution.py:438
  77.2 8.1 %collective-permute-start.20 = (bf16[2,2,48,256]{3,2,1,0:T(8,128)(2,1)}, bf16[2,2,48,256]{3,2,1,0:T(8,128)(2,1)S(1)}, u32[]{:S(2)}, u32[]{:S(2)}) collective-permute-start(bf16[2,2,48,256]{3,2,1,0:T(8,128)(2,1)} %get-tuple-element.108), channel_id=1, source_target_pairs={{0,7},{1,6},{2,5},{3,4},{4,3},{5,2},{6,1},{7,0},{8,15},{9,14},{10,... | collective-permute-start | bytes 294920 | tf_op jit(solution)/shard_map/ppermute | solution.py:438
  78.4 13.2 %collective-permute-start.6 = (bf16[2,2,48,256]{3,2,1,0:T(8,128)(2,1)}, bf16[2,2,48,256]{3,2,1,0:T(8,128)(2,1)S(1)}, u32[]{:S(2)}, u32[]{:S(2)}) collective-permute-start(bf16[2,2,48,256]{3,2,1,0:T(8,128)(2,1)} %get-tuple-element.82), channel_id=1, source_target_pairs={{0,1},{1,0},{2,3},{3,2},{4,5},{5,4},{6,7},{7,6},{8,9},{9,8},{10,11... | collective-permute-start | bytes 294920 | tf_op jit(solution)/shard_map/ppermute | solution.py:438
  79.4 14.7 %collective-permute-start.10 = (bf16[2,2,48,256]{3,2,1,0:T(8,128)(2,1)}, bf16[2,2,48,256]{3,2,1,0:T(8,128)(2,1)S(1)}, u32[]{:S(2)}, u32[]{:S(2)}) collective-permute-start(bf16[2,2,48,256]{3,2,1,0:T(8,128)(2,1)} %get-tuple-element.89), channel_id=1, source_target_pairs={{0,2},{1,3},{2,0},{3,1},{4,6},{5,7},{6,4},{7,5},{8,10},{9,11},{10,... | collective-permute-start | bytes 294920 | tf_op jit(solution)/shard_map/ppermute | solution.py:438
  85.0 9.8 %collective-permute-start.14 = (bf16[2,2,48,256]{3,2,1,0:T(8,128)(2,1)}, bf16[2,2,48,256]{3,2,1,0:T(8,128)(2,1)S(1)}, u32[]{:S(2)}, u32[]{:S(2)}) collective-permute-start(bf16[2,2,48,256]{3,2,1,0:T(8,128)(2,1)} %get-tuple-element.96), channel_id=1, source_target_pairs={{0,3},{1,2},{2,1},{3,0},{4,7},{5,6},{6,5},{7,4},{8,11},{9,10},{10,... | collective-permute-start | bytes 294920 | tf_op jit(solution)/shard_map/ppermute | solution.py:438
  91.5 9.1 %collective-permute-start.22 = (bf16[2,2,48,256]{3,2,1,0:T(8,128)(2,1)S(1)}, bf16[2,2,48,256]{3,2,1,0:T(8,128)(2,1)S(1)}, u32[]{:S(2)}, u32[]{:S(2)}) collective-permute-start(bf16[2,2,48,256]{3,2,1,0:T(8,128)(2,1)S(1)} %copy-done.68), channel_id=1, source_target_pairs={{0,5},{1,4},{2,7},{3,6},{4,1},{5,0},{6,3},{7,2},{8,13},{9,12},{10,... | collective-permute-start | bytes 294920 | tf_op jit(solution)/shard_map/ppermute | solution.py:438
  91.6 10.7 %collective-permute-start.23 = (bf16[2,2,48,256]{3,2,1,0:T(8,128)(2,1)S(1)}, bf16[2,2,48,256]{3,2,1,0:T(8,128)(2,1)S(1)}, u32[]{:S(2)}, u32[]{:S(2)}) collective-permute-start(bf16[2,2,48,256]{3,2,1,0:T(8,128)(2,1)S(1)} %copy-done.67), channel_id=1, source_target_pairs={{0,6},{1,7},{2,4},{3,5},{4,2},{5,3},{6,0},{7,1},{8,14},{9,15},{10,... | collective-permute-start | bytes 294920 | tf_op jit(solution)/shard_map/ppermute | solution.py:438
  94.2 8.1 %collective-permute-start.24 = (bf16[2,2,48,256]{3,2,1,0:T(8,128)(2,1)S(1)}, bf16[2,2,48,256]{3,2,1,0:T(8,128)(2,1)S(1)}, u32[]{:S(2)}, u32[]{:S(2)}) collective-permute-start(bf16[2,2,48,256]{3,2,1,0:T(8,128)(2,1)S(1)} %copy-done.66), channel_id=1, source_target_pairs={{0,7},{1,6},{2,5},{3,4},{4,3},{5,2},{6,1},{7,0},{8,15},{9,14},{10,... | collective-permute-start | bytes 294920 | tf_op jit(solution)/shard_map/ppermute | solution.py:438
  94.8 13.7 %collective-permute-start.7 = (bf16[2,2,48,256]{3,2,1,0:T(8,128)(2,1)S(1)}, bf16[2,2,48,256]{3,2,1,0:T(8,128)(2,1)S(1)}, u32[]{:S(2)}, u32[]{:S(2)}) collective-permute-start(bf16[2,2,48,256]{3,2,1,0:T(8,128)(2,1)S(1)} %copy-done.65), channel_id=1, source_target_pairs={{0,1},{1,0},{2,3},{3,2},{4,5},{5,4},{6,7},{7,6},{8,9},{9,8},{10,11... | collective-permute-start | bytes 294920 | tf_op jit(solution)/shard_map/ppermute | solution.py:438
  95.1 13.8 %collective-permute-start.11 = (bf16[2,2,48,256]{3,2,1,0:T(8,128)(2,1)S(1)}, bf16[2,2,48,256]{3,2,1,0:T(8,128)(2,1)S(1)}, u32[]{:S(2)}, u32[]{:S(2)}) collective-permute-start(bf16[2,2,48,256]{3,2,1,0:T(8,128)(2,1)S(1)} %copy-done.64), channel_id=1, source_target_pairs={{0,2},{1,3},{2,0},{3,1},{4,6},{5,7},{6,4},{7,5},{8,10},{9,11},{10,... | collective-permute-start | bytes 294920 | tf_op jit(solution)/shard_map/ppermute | solution.py:438
  100.7 10.2 %collective-permute-start.15 = (bf16[2,2,48,256]{3,2,1,0:T(8,128)(2,1)S(1)}, bf16[2,2,48,256]{3,2,1,0:T(8,128)(2,1)S(1)}, u32[]{:S(2)}, u32[]{:S(2)}) collective-permute-start(bf16[2,2,48,256]{3,2,1,0:T(8,128)(2,1)S(1)} %copy-done.63), channel_id=1, source_target_pairs={{0,3},{1,2},{2,1},{3,0},{4,7},{5,6},{6,5},{7,4},{8,11},{9,10},{10,... | collective-permute-start | bytes 294920 | tf_op jit(solution)/shard_map/ppermute | solution.py:438
  106.7 5.6 %collective-permute-start.25 = (bf16[2,2,48,256]{3,2,1,0:T(8,128)(2,1)S(1)}, bf16[2,2,48,256]{3,2,1,0:T(8,128)(2,1)S(1)}, u32[]{:S(2)}, u32[]{:S(2)}) collective-permute-start(bf16[2,2,48,256]{3,2,1,0:T(8,128)(2,1)S(1)} %copy-done.62), channel_id=1, source_target_pairs={{0,4},{1,5},{2,6},{3,7},{4,0},{5,1},{6,2},{7,3},{8,12},{9,13},{10,... | collective-permute-start | bytes 294920 | tf_op jit(solution)/shard_map/ppermute | solution.py:438
  108.5 61.8 %collective-permute-start.1 = (bf16[4,256,384]{2,1,0:T(8,128)(2,1)S(1)}, bf16[4,256,384]{2,1,0:T(8,128)(2,1)S(1)}, u32[]{:S(2)}, u32[]{:S(2)}) collective-permute-start(bf16[4,256,384]{2,1,0:T(8,128)(2,1)S(1)} %copy-done.51), channel_id=1, source_target_pairs={{0,1},{1,0},{2,3},{3,2},{4,5},{5,4},{6,7},{7,6},{8,9},{9,8},{10,11... | collective-permute-start | bytes 2359304 | tf_op jit(solution)/shard_map/ppermute | solution.py:438
  108.6 7.3 %collective-permute-start.26 = (bf16[2,2,48,256]{3,2,1,0:T(8,128)(2,1)S(1)}, bf16[2,2,48,256]{3,2,1,0:T(8,128)(2,1)S(1)}, u32[]{:S(2)}, u32[]{:S(2)}) collective-permute-start(bf16[2,2,48,256]{3,2,1,0:T(8,128)(2,1)S(1)} %copy-done.61), channel_id=1, source_target_pairs={{0,5},{1,4},{2,7},{3,6},{4,1},{5,0},{6,3},{7,2},{8,13},{9,12},{10,... | collective-permute-start | bytes 294920 | tf_op jit(solution)/shard_map/ppermute | solution.py:438
  109.0 8.5 %collective-permute-start.27 = (bf16[2,2,48,256]{3,2,1,0:T(8,128)(2,1)S(1)}, bf16[2,2,48,256]{3,2,1,0:T(8,128)(2,1)S(1)}, u32[]{:S(2)}, u32[]{:S(2)}) collective-permute-start(bf16[2,2,48,256]{3,2,1,0:T(8,128)(2,1)S(1)} %copy-done.60), channel_id=1, source_target_pairs={{0,6},{1,7},{2,4},{3,5},{4,2},{5,3},{6,0},{7,1},{8,14},{9,15},{10,... | collective-permute-start | bytes 294920 | tf_op jit(solution)/shard_map/ppermute | solution.py:438
  110.9 12.7 %collective-permute-start.47 = (bf16[2,2,2,48,256]{4,3,2,1,0:T(8,128)(2,1)S(1)}, bf16[2,2,2,48,256]{4,3,2,1,0:T(8,128)(2,1)S(1)}, u32[]{:S(2)}, u32[]{:S(2)}) collective-permute-start(bf16[2,2,2,48,256]{4,3,2,1,0:T(8,128)(2,1)S(1)} %copy-done.2), channel_id=1, source_target_pairs={{8,16},{16,8},{9,17},{17,9},{10,18},{18,10},{11,19},{19,11},{12,20... | collective-permute-start | bytes 589832 | tf_op jit(solution)/shard_map/ppermute | solution.py:396
  112.3 16.4 %collective-permute-start.46 = (bf16[2,2,2,48,256]{4,3,2,1,0:T(8,128)(2,1)S(1)}, bf16[2,2,2,48,256]{4,3,2,1,0:T(8,128)(2,1)S(1)}, u32[]{:S(2)}, u32[]{:S(2)}) collective-permute-start(bf16[2,2,2,48,256]{4,3,2,1,0:T(8,128)(2,1)S(1)} %copy-done.2), channel_id=1, source_target_pairs={{0,16},{8,24},{16,0},{24,8},{1,17},{9,25},{17,1},{25,9},{2,18},{10... | collective-permute-start | bytes 589832 | tf_op jit(solution)/shard_map/ppermute | solution.py:394
  115.9 16.7 %collective-permute-start.45 = (bf16[2,2,2,48,256]{4,3,2,1,0:T(8,128)(2,1)S(1)}, bf16[2,2,2,48,256]{4,3,2,1,0:T(8,128)(2,1)S(1)}, u32[]{:S(2)}, u32[]{:S(2)}) collective-permute-start(bf16[2,2,2,48,256]{4,3,2,1,0:T(8,128)(2,1)S(1)} %copy-done.2), channel_id=1, source_target_pairs={{0,8},{8,0},{16,24},{24,16},{1,9},{9,1},{17,25},{25,17},{2,10},{10... | collective-permute-start | bytes 589832 | tf_op jit(solution)/shard_map/ppermute | solution.py:395
  117.4 6.0 %collective-permute-start.28 = (bf16[2,2,48,256]{3,2,1,0:T(8,128)(2,1)S(1)}, bf16[2,2,48,256]{3,2,1,0:T(8,128)(2,1)S(1)}, u32[]{:S(2)}, u32[]{:S(2)}) collective-permute-start(bf16[2,2,48,256]{3,2,1,0:T(8,128)(2,1)S(1)} %copy-done.59), channel_id=1, source_target_pairs={{0,7},{1,6},{2,5},{3,4},{4,3},{5,2},{6,1},{7,0},{8,15},{9,14},{10,... | collective-permute-start | bytes 294920 | tf_op jit(solution)/shard_map/ppermute | solution.py:438
  123.4 9.8 %collective-permute-start.8 = (bf16[2,2,48,256]{3,2,1,0:T(8,128)(2,1)S(1)}, bf16[2,2,48,256]{3,2,1,0:T(8,128)(2,1)S(1)}, u32[]{:S(2)}, u32[]{:S(2)}) collective-permute-start(bf16[2,2,48,256]{3,2,1,0:T(8,128)(2,1)S(1)} %copy-done.58), channel_id=1, source_target_pairs={{0,1},{1,0},{2,3},{3,2},{4,5},{5,4},{6,7},{7,6},{8,9},{9,8},{10,11... | collective-permute-start | bytes 294920 | tf_op jit(solution)/shard_map/ppermute | solution.py:438
  123.5 12.0 %collective-permute-start.12 = (bf16[2,2,48,256]{3,2,1,0:T(8,128)(2,1)S(1)}, bf16[2,2,48,256]{3,2,1,0:T(8,128)(2,1)S(1)}, u32[]{:S(2)}, u32[]{:S(2)}) collective-permute-start(bf16[2,2,48,256]{3,2,1,0:T(8,128)(2,1)S(1)} %copy-done.57), channel_id=1, source_target_pairs={{0,2},{1,3},{2,0},{3,1},{4,6},{5,7},{6,4},{7,5},{8,10},{9,11},{10,... | collective-permute-start | bytes 294920 | tf_op jit(solution)/shard_map/ppermute | solution.py:438
  128.7 7.5 %collective-permute-start.16 = (bf16[2,2,48,256]{3,2,1,0:T(8,128)(2,1)S(1)}, bf16[2,2,48,256]{3,2,1,0:T(8,128)(2,1)S(1)}, u32[]{:S(2)}, u32[]{:S(2)}) collective-permute-start(bf16[2,2,48,256]{3,2,1,0:T(8,128)(2,1)S(1)} %copy-done.56), channel_id=1, source_target_pairs={{0,3},{1,2},{2,1},{3,0},{4,7},{5,6},{6,5},{7,4},{8,11},{9,10},{10,... | collective-permute-start | bytes 294920 | tf_op jit(solution)/shard_map/ppermute | solution.py:438
  132.6 6.1 %collective-permute-start.29 = (bf16[2,2,48,256]{3,2,1,0:T(8,128)(2,1)S(1)}, bf16[2,2,48,256]{3,2,1,0:T(8,128)(2,1)S(1)}, u32[]{:S(2)}, u32[]{:S(2)}) collective-permute-start(bf16[2,2,48,256]{3,2,1,0:T(8,128)(2,1)S(1)} %copy-done.55), channel_id=1, source_target_pairs={{0,4},{1,5},{2,6},{3,7},{4,0},{5,1},{6,2},{7,3},{8,12},{9,13},{10,... | collective-permute-start | bytes 294920 | tf_op jit(solution)/shard_map/ppermute | solution.py:438
  133.3 7.2 %collective-permute-start.30 = (bf16[2,2,48,256]{3,2,1,0:T(8,128)(2,1)S(1)}, bf16[2,2,48,256]{3,2,1,0:T(8,128)(2,1)S(1)}, u32[]{:S(2)}, u32[]{:S(2)}) collective-permute-start(bf16[2,2,48,256]{3,2,1,0:T(8,128)(2,1)S(1)} %copy-done.54), channel_id=1, source_target_pairs={{0,5},{1,4},{2,7},{3,6},{4,1},{5,0},{6,3},{7,2},{8,13},{9,12},{10,... | collective-permute-start | bytes 294920 | tf_op jit(solution)/shard_map/ppermute | solution.py:438
  135.6 11.5 %collective-permute-start.43 = (bf16[2,2,2,48,256]{4,3,2,1,0:T(8,128)(2,1)S(1)}, bf16[2,2,2,48,256]{4,3,2,1,0:T(8,128)(2,1)S(1)}, u32[]{:S(2)}, u32[]{:S(2)}) collective-permute-start(bf16[2,2,2,48,256]{4,3,2,1,0:T(8,128)(2,1)S(1)} %copy-done.10), channel_id=1, source_target_pairs={{8,16},{16,8},{9,17},{17,9},{10,18},{18,10},{11,19},{19,11},{12,20... | collective-permute-start | bytes 589832 | tf_op jit(solution)/shard_map/ppermute | solution.py:396
  136.3 14.9 %collective-permute-start.42 = (bf16[2,2,2,48,256]{4,3,2,1,0:T(8,128)(2,1)S(1)}, bf16[2,2,2,48,256]{4,3,2,1,0:T(8,128)(2,1)S(1)}, u32[]{:S(2)}, u32[]{:S(2)}) collective-permute-start(bf16[2,2,2,48,256]{4,3,2,1,0:T(8,128)(2,1)S(1)} %copy-done.10), channel_id=1, source_target_pairs={{0,16},{8,24},{16,0},{24,8},{1,17},{9,25},{17,1},{25,9},{2,18},{10... | collective-permute-start | bytes 589832 | tf_op jit(solution)/shard_map/ppermute | solution.py:394
  138.7 5.6 %collective-permute-start.31 = (bf16[2,2,48,256]{3,2,1,0:T(8,128)(2,1)S(1)}, bf16[2,2,48,256]{3,2,1,0:T(8,128)(2,1)S(1)}, u32[]{:S(2)}, u32[]{:S(2)}) collective-permute-start(bf16[2,2,48,256]{3,2,1,0:T(8,128)(2,1)S(1)} %copy-done.53), channel_id=1, source_target_pairs={{0,6},{1,7},{2,4},{3,5},{4,2},{5,3},{6,0},{7,1},{8,14},{9,15},{10,... | collective-permute-start | bytes 294920 | tf_op jit(solution)/shard_map/ppermute | solution.py:438
  140.4 6.0 %collective-permute-start.32 = (bf16[2,2,48,256]{3,2,1,0:T(8,128)(2,1)S(1)}, bf16[2,2,48,256]{3,2,1,0:T(8,128)(2,1)S(1)}, u32[]{:S(2)}, u32[]{:S(2)}) collective-permute-start(bf16[2,2,48,256]{3,2,1,0:T(8,128)(2,1)S(1)} %copy-done.52), channel_id=1, source_target_pairs={{0,7},{1,6},{2,5},{3,4},{4,3},{5,2},{6,1},{7,0},{8,15},{9,14},{10,... | collective-permute-start | bytes 294920 | tf_op jit(solution)/shard_map/ppermute | solution.py:438
  144.3 10.7 %collective-permute-start.41 = (bf16[2,2,2,48,256]{4,3,2,1,0:T(8,128)(2,1)S(1)}, bf16[2,2,2,48,256]{4,3,2,1,0:T(8,128)(2,1)S(1)}, u32[]{:S(2)}, u32[]{:S(2)}) collective-permute-start(bf16[2,2,2,48,256]{4,3,2,1,0:T(8,128)(2,1)S(1)} %copy-done.10), channel_id=1, source_target_pairs={{0,8},{8,0},{16,24},{24,16},{1,9},{9,1},{17,25},{25,17},{2,10},{10... | collective-permute-start | bytes 589832 | tf_op jit(solution)/shard_map/ppermute | solution.py:395
  146.4 9.9 %collective-permute-start.39 = (bf16[2,2,2,48,256]{4,3,2,1,0:T(8,128)(2,1)}, bf16[2,2,2,48,256]{4,3,2,1,0:T(8,128)(2,1)S(1)}, u32[]{:S(2)}, u32[]{:S(2)}) collective-permute-start(bf16[2,2,2,48,256]{4,3,2,1,0:T(8,128)(2,1)} %get-tuple-element.129.refs_0_), channel_id=1, source_target_pairs={{8,16},{16,8},{9,17},{17,9},{10,18},{18,10},{11,19},{19,11},{12,20... | collective-permute-start | bytes 589832 | tf_op jit(solution)/shard_map/ppermute | solution.py:396
  147.1 21.2 %collective-permute-start.38 = (bf16[2,2,2,48,256]{4,3,2,1,0:T(8,128)(2,1)}, bf16[2,2,2,48,256]{4,3,2,1,0:T(8,128)(2,1)S(1)}, u32[]{:S(2)}, u32[]{:S(2)}) collective-permute-start(bf16[2,2,2,48,256]{4,3,2,1,0:T(8,128)(2,1)} %get-tuple-element.129.refs_0_), channel_id=1, source_target_pairs={{0,16},{8,24},{16,0},{24,8},{1,17},{9,25},{17,1},{25,9},{2,18},{10... | collective-permute-start | bytes 589832 | tf_op jit(solution)/shard_map/ppermute | solution.py:394
  151.2 17.8 %collective-permute-start.37 = (bf16[2,2,2,48,256]{4,3,2,1,0:T(8,128)(2,1)}, bf16[2,2,2,48,256]{4,3,2,1,0:T(8,128)(2,1)S(1)}, u32[]{:S(2)}, u32[]{:S(2)}) collective-permute-start(bf16[2,2,2,48,256]{4,3,2,1,0:T(8,128)(2,1)} %get-tuple-element.129.refs_0_), channel_id=1, source_target_pairs={{0,8},{8,0},{16,24},{24,16},{1,9},{9,1},{17,25},{25,17},{2,10},{10... | collective-permute-start | bytes 589832 | tf_op jit(solution)/shard_map/ppermute | solution.py:395
  155.0 17.7 %collective-permute-start.48 = (bf16[2,2,2,48,256]{4,3,2,1,0:T(8,128)(2,1)S(1)}, bf16[2,2,2,48,256]{4,3,2,1,0:T(8,128)(2,1)S(1)}, u32[]{:S(2)}, u32[]{:S(2)}) collective-permute-start(bf16[2,2,2,48,256]{4,3,2,1,0:T(8,128)(2,1)S(1)} %collective-permute-done.46.refs_2_), channel_id=1, source_target_pairs={{16,24},{8,0},{17,25},{9,1},{18,26},{10,2},{19,27},{11,3},{20,28},... | collective-permute-start | bytes 589832 | tf_op jit(solution)/shard_map/ppermute | solution.py:397
  156.3 20.4 %collective-permute-start.34 = (bf16[2,2,2,48,256]{4,3,2,1,0:T(8,128)(2,1)}, bf16[2,2,2,48,256]{4,3,2,1,0:T(8,128)(2,1)S(1)}, u32[]{:S(2)}, u32[]{:S(2)}) collective-permute-start(bf16[2,2,2,48,256]{4,3,2,1,0:T(8,128)(2,1)} %get-tuple-element.139.refs_0_), channel_id=1, source_target_pairs={{0,16},{8,24},{16,0},{24,8},{1,17},{9,25},{17,1},{25,9},{2,18},{10... | collective-permute-start | bytes 589832 | tf_op jit(solution)/shard_map/ppermute | solution.py:394
  168.3 9.7 %collective-permute-start.35 = (bf16[2,2,2,48,256]{4,3,2,1,0:T(8,128)(2,1)}, bf16[2,2,2,48,256]{4,3,2,1,0:T(8,128)(2,1)S(1)}, u32[]{:S(2)}, u32[]{:S(2)}) collective-permute-start(bf16[2,2,2,48,256]{4,3,2,1,0:T(8,128)(2,1)} %get-tuple-element.139.refs_0_), channel_id=1, source_target_pairs={{8,16},{16,8},{9,17},{17,9},{10,18},{18,10},{11,19},{19,11},{12,20... | collective-permute-start | bytes 589832 | tf_op jit(solution)/shard_map/ppermute | solution.py:396
  169.0 11.5 %collective-permute-start.44 = (bf16[2,2,2,48,256]{4,3,2,1,0:T(8,128)(2,1)S(1)}, bf16[2,2,2,48,256]{4,3,2,1,0:T(8,128)(2,1)}, u32[]{:S(2)}, u32[]{:S(2)}) collective-permute-start(bf16[2,2,2,48,256]{4,3,2,1,0:T(8,128)(2,1)S(1)} %collective-permute-done.42.refs_2_), channel_id=1, source_target_pairs={{16,24},{8,0},{17,25},{9,1},{18,26},{10,2},{19,27},{11,3},{20,28},... | collective-permute-start | bytes 589832 | tf_op jit(solution)/shard_map/ppermute | solution.py:397
  170.3 12.7 %collective-permute-start.40 = (bf16[2,2,2,48,256]{4,3,2,1,0:T(8,128)(2,1)S(1)}, bf16[2,2,2,48,256]{4,3,2,1,0:T(8,128)(2,1)}, u32[]{:S(2)}, u32[]{:S(2)}) collective-permute-start(bf16[2,2,2,48,256]{4,3,2,1,0:T(8,128)(2,1)S(1)} %collective-permute-done.38.refs_2_), channel_id=1, source_target_pairs={{16,24},{8,0},{17,25},{9,1},{18,26},{10,2},{19,27},{11,3},{20,28},... | collective-permute-start | bytes 589832 | tf_op jit(solution)/shard_map/ppermute | solution.py:397
  172.7 19.4 %collective-permute-start.33 = (bf16[2,2,2,48,256]{4,3,2,1,0:T(8,128)(2,1)S(1)}, bf16[2,2,2,48,256]{4,3,2,1,0:T(8,128)(2,1)S(1)}, u32[]{:S(2)}, u32[]{:S(2)}) collective-permute-start(bf16[2,2,2,48,256]{4,3,2,1,0:T(8,128)(2,1)S(1)} %copy-done.15), channel_id=1, source_target_pairs={{0,8},{8,0},{16,24},{24,16},{1,9},{9,1},{17,25},{25,17},{2,10},{10... | collective-permute-start | bytes 589832 | tf_op jit(solution)/shard_map/ppermute | solution.py:395
  176.7 23.1 %collective-permute-start.36 = (bf16[2,2,2,48,256]{4,3,2,1,0:T(8,128)(2,1)S(1)}, bf16[2,2,2,48,256]{4,3,2,1,0:T(8,128)(2,1)S(1)}, u32[]{:S(2)}, u32[]{:S(2)}) collective-permute-start(bf16[2,2,2,48,256]{4,3,2,1,0:T(8,128)(2,1)S(1)} %collective-permute-done.34.refs_2_), channel_id=1, source_target_pairs={{16,24},{8,0},{17,25},{9,1},{18,26},{10,2},{19,27},{11,3},{20,28},... | collective-permute-start | bytes 589832 | tf_op jit(solution)/shard_map/ppermute | solution.py:397
  178.0 25.3 %collective-permute-start.4 = (bf16[256,384]{1,0:T(8,128)(2,1)S(1)}, bf16[256,384]{1,0:T(8,128)(2,1)S(1)}, u32[]{:S(2)}, u32[]{:S(2)}) collective-permute-start(bf16[256,384]{1,0:T(8,128)(2,1)S(1)} %get-tuple-element.142), channel_id=1, source_target_pairs={{0,24},{8,0},{16,8},{24,16},{1,25},{9,1},{17,9},{25,17},{2,26},{10... | collective-permute-start | bytes 589832 | tf_op jit(solution)/shard_map/ppermute | solution.py:474
  180.5 22.8 %collective-permute-start.3 = (bf16[256,384]{1,0:T(8,128)(2,1)S(1)}, bf16[256,384]{1,0:T(8,128)(2,1)S(1)}, u32[]{:S(2)}, u32[]{:S(2)}) collective-permute-start(bf16[256,384]{1,0:T(8,128)(2,1)S(1)} %get-tuple-element.143), channel_id=1, source_target_pairs={{0,16},{8,24},{16,0},{24,8},{1,17},{9,25},{17,1},{25,9},{2,18},{10... | collective-permute-start | bytes 589832 | tf_op jit(solution)/shard_map/ppermute | solution.py:474
  183.0 20.2 %collective-permute-start.2 = (bf16[256,384]{1,0:T(8,128)(2,1)S(1)}, bf16[256,384]{1,0:T(8,128)(2,1)S(1)}, u32[]{:S(2)}, u32[]{:S(2)}) collective-permute-start(bf16[256,384]{1,0:T(8,128)(2,1)S(1)} %get-tuple-element.144), channel_id=1, source_target_pairs={{0,8},{8,16},{16,24},{24,0},{1,9},{9,17},{17,25},{25,1},{2,10},{10... | collective-permute-start | bytes 589832 | tf_op jit(solution)/shard_map/ppermute | solution.py:474
  (73 other events, 697.5 us)
Sparse Core Ops, SparseCore 0:
  10.1 39.1 all-gather.2

commit v4 on v3

--- a/solution.py
+++ b/solution.py
@@ -9,7 +9,7 @@
 
 SITES = 384
 CAP = 128
-CHUNK_PARTS = (2, 2, 2, 2)
+CHUNK_PARTS = (3, 5)
 ID_ROWS = 16
 VMEM_BYTES = 56 * 2**20
 
@@ -89,40 +89,47 @@
     )(ids, signals, cotangent)
 
 
-def local_grads(pos, touched, slot_map, mine, other, blocks, sizes, piece, width):
-    planes = mine.shape[0]
-    rows = (mine.shape[1] - ID_ROWS) // 2
+def local_grads(pos, touched, slot_map, rows_in, blocks, sizes, piece, width):
+    planes = rows_in[0].shape[0]
+    rows = (rows_in[0].shape[1] - ID_ROWS) // 2
     touch = touched.shape[1]
-    n_own = blocks.shape[0]
-    half = sum(sizes)
+    chips = len(blocks)
+    n_own = 2 * chips
+    half = blocks[0].shape[1]
     aligned = piece % 16 == 0
+    n_in = chips if aligned else 1
+    n_out = n_own if aligned else 1
     starts = [sum(sizes[:i]) for i in range(len(sizes))]
-    n_blocks = n_own if aligned else 1
-    n_grads = len(sizes) * n_blocks
-
-    def body(pos_ref, touched_ref, slot_ref, mine_ref, other_ref, *rest):
-        blocks_ref = rest[0]
-        pred_refs = rest[1:3]
-        grad_refs = rest[3 : 3 + n_grads]
-        acc, id_cols, held, sorted_rows, pred, full_of, tasks, sems = rest[3 + n_grads :]
-        own_at = pos_ref[1]
+
+    def body(pos_ref, touched_ref, slot_ref, *rest):
+        row_refs = rest[:2]
+        block_refs = rest[2 : 2 + n_in]
+        rest = rest[2 + n_in :]
+        pred_refs = rest[:2]
+        grad_refs = rest[2:-8]
+        acc, id_cols, held, sorted_rows, pred, full_of, tasks, sems = rest[-8:]
+        dp_at, own_at = pos_ref[0], pos_ref[1]
         core = lax.rem(own_at, 2)
-        partner = own_at + 1 - 2 * core
+
+        def sites(j):
+            return pl.ds(pl.multiple_of((own_at ^ j) * piece, 16), piece)
+
         row_copies = [
-            pltpu.make_async_copy(
-                ref, sorted_rows.at[pl.ds(which * planes, planes)], sems.at[which]
-            )
-            for which, ref in enumerate((mine_ref, other_ref))
+            pltpu.make_async_copy(ref, sorted_rows.at[pl.ds(i * planes, planes)], sems.at[i])
+            for i, ref in enumerate(row_refs)
         ]
         if aligned:
             block_copies = [
                 pltpu.make_async_copy(
-                    blocks_ref.at[s], held.at[:, :, pl.ds(s * piece, piece), :], sems.at[2 + s]
+                    ref.at[u],
+                    held.at[:, :, sites(2 * q + u), :],
+                    sems.at[2 + 2 * q + u],
                 )
-                for s in range(n_own)
+                for q, ref in enumerate(block_refs)
+                for u in range(2)
             ]
         else:
-            block_copies = [pltpu.make_async_copy(blocks_ref, held, sems.at[2])]
+            block_copies = [pltpu.make_async_copy(block_refs[0], held, sems.at[2])]
         for copy in row_copies + block_copies:
             copy.start()
 
@@ -143,15 +150,15 @@
             source = t // (touch + 1)
             j = t - source * (touch + 1)
             which = source // planes
-            device = (source - which * planes) * n_own + jnp.where(which == 0, own_at, partner)
+            device = (dp_at ^ (source - which * planes)) * n_own + (own_at ^ which)
             full = full_of[source]
             insertion = jnp.where(j == 0, full, touched_ref[device, jnp.maximum(j - 1, 0)])
-            stored = slot_ref[insertion]
-            here = (stored // half == core) & ((j == 0) | (insertion != full))
+            e = slot_ref[insertion] - core * half
+            here = (e >= 0) & (e < half) & ((j == 0) | (insertion != full))
             tasks[0, count] = source
             tasks[1, count] = jnp.where(j == 0, 0, CAP)
             tasks[2, count] = insertion
-            tasks[3, count] = stored - core * half
+            tasks[3, count] = e
             return count + here.astype(jnp.int32)
 
         count = lax.fori_loop(0, 2 * planes * (touch + 1), listing, 0)
@@ -204,17 +211,12 @@
         for which, ref in enumerate(pred_refs):
             ref[...] = pred[which * planes : (which + 1) * planes]
         for chunk, (start, size) in enumerate(zip(starts, sizes)):
-            for j in range(n_blocks):
-                ref = grad_refs[chunk * n_blocks + j]
+            for j in range(n_out):
+                ref = grad_refs[chunk * n_out + j]
 
                 def write(e, _, start=start, ref=ref, j=j):
                     if aligned:
-                        ref[e] = acc[
-                            start + e,
-                            :,
-                            pl.ds(pl.multiple_of((own_at ^ j) * piece, 16), piece),
-                            :,
-                        ].astype(jnp.bfloat16)
+                        ref[e] = acc[start + e, :, sites(j), :].astype(jnp.bfloat16)
                     else:
                         ref[e] = acc[start + e].astype(jnp.bfloat16)
                     return 0
@@ -222,45 +224,45 @@
                 lax.fori_loop(0, size, write, 0)
 
     pred_shape = jax.ShapeDtypeStruct((planes, rows, SITES), jnp.bfloat16)
-    grad_rows = piece if aligned else SITES
     grad_shapes = [
-        jax.ShapeDtypeStruct((size, 2, grad_rows, width), jnp.bfloat16)
+        jax.ShapeDtypeStruct((size, 2, piece if aligned else SITES, width), jnp.bfloat16)
         for size in sizes
-        for _ in range(n_blocks)
+        for _ in range(n_out)
     ]
     most = 2 * planes * (touch + 1)
     scratch = [
         pltpu.VMEM((half, 2, SITES, width), jnp.float32),
         pltpu.VMEM((2 * planes, rows, 128), jnp.float32),
         pltpu.VMEM((half, 2, SITES, width), jnp.bfloat16),
-        pltpu.VMEM((2 * planes,) + mine.shape[1:], jnp.bfloat16),
+        pltpu.VMEM((2 * planes,) + rows_in[0].shape[1:], jnp.bfloat16),
         pltpu.VMEM((2 * planes, rows, SITES), jnp.bfloat16),
         pltpu.SMEM((2 * planes,), jnp.int32),
         pltpu.SMEM((4, most + 1), jnp.int32),
-        pltpu.SemaphoreType.DMA((2 + n_blocks,)),
+        pltpu.SemaphoreType.DMA((2 + n_own,)),
     ]
     own_at = pos[1]
     if not aligned:
-        blocks = blocks.transpose(1, 2, 0, 3, 4).reshape(half, 2, SITES, width)
-    anywhere = pl.BlockSpec(memory_space=pl.ANY)
+        order = own_at ^ jnp.arange(n_own, dtype=jnp.int32)
+        stacked = jnp.take(jnp.concatenate(blocks), order, axis=0)
+        blocks = [stacked.transpose(1, 2, 0, 3, 4).reshape(half, 2, SITES, width)]
     found = pl.pallas_call(
         body,
         out_shape=[pred_shape, pred_shape] + grad_shapes,
-        in_specs=[smem(), smem(), smem()] + [anywhere] * 3,
-        out_specs=[vmem()] * (2 + n_grads),
+        in_specs=[smem(), smem(), smem()] + [pl.BlockSpec(memory_space=pl.ANY)] * (2 + n_in),
+        out_specs=[vmem()] * (2 + len(grad_shapes)),
         scratch_shapes=scratch,
         compiler_params=params(),
         name="local_grads",
-    )(pos, touched, slot_map, mine, other, blocks)
+    )(pos, touched, slot_map, *rows_in, *blocks)
     grads = []
     for chunk in range(len(sizes)):
-        outs = found[2 + chunk * n_blocks : 2 + (chunk + 1) * n_blocks]
+        outs = list(found[2 + chunk * n_out : 2 + (chunk + 1) * n_out])
         if not aligned:
             outs = [
                 lax.dynamic_slice_in_dim(outs[0], (own_at ^ j) * piece, piece, 2)
                 for j in range(n_own)
             ]
-        grads.append(list(outs))
+        grads.append(outs)
     return found[0], found[1], grads
 
 
@@ -285,8 +287,9 @@
             two = 0.999 * m2_ref[...] + 0.001 * gradient * gradient
             new_m1[...] = one
             new_m2[...] = two
-            updated = w_ref[...].astype(jnp.float32) - learn_rate * (one / correct_one) / (
-                jnp.sqrt(two / correct_two) + 1e-08
+            spread = two * (1.0 / correct_two)
+            updated = w_ref[...].astype(jnp.float32) - one * (learn_rate / correct_one) / (
+                spread * lax.rsqrt(spread) + 1e-08
             )
             new_w[0] = updated.astype(jnp.bfloat16)
 
@@ -385,6 +388,10 @@
     )(pos, *pieces, *before)
 
 
+def after(value, *others):
+    return lax.optimization_barrier((value,) + others)[0]
+
+
 def gather_planes(fresh, dp_at, n_dp):
     if n_dp != 4:
         whole = lax.all_gather(fresh, "dp", axis=0)
@@ -437,29 +444,39 @@
     def across(value, j):
         return lax.ppermute(value, "own", [(o, o ^ j) for o in range(n_own)])
 
+    def column(which):
+        return lax.dynamic_slice(
+            weights, (which * half, 0, 0, dp_at * width), (half, 2, piece, width)
+        )
+
     packed, perm = pack_rows(row_insertion.reshape(1, rows), signals, cotangent)
-    mine = lax.all_gather(packed, "dp", axis=0)
-
-    column = lax.dynamic_slice_in_dim(weights, dp_at * width, width, 3)
-    outgoing = jnp.broadcast_to(
-        column.reshape(1, 2, half, 2, piece, width), (n_own // 2, 2, half, 2, piece, width)
-    ).reshape(n_own, half, 2, piece, width)
-    blocks = lax.all_to_all(outgoing, "own", split_axis=0, concat_axis=0, tiled=True)
-    other = across(mine, 1)
+    def between(value, j):
+        return lax.ppermute(value, "dp", [(d, d ^ j) for d in range(n_dp)])
+
+    planes = jnp.stack([packed] + [between(packed, j) for j in range(1, n_dp)])
+
+    paired = jnp.stack([column(core), across(column(1 - core), 1)])
+    blocks = [paired] + [across(paired, 2 * q) for q in range(1, n_own // 2)]
+    rows_in = (planes, across(after(planes, *blocks[1:]), 1))
 
     pred_mine, pred_other, grads = local_grads(
-        pos, touched, slot_map, mine, other, blocks, sizes, piece, width
+        pos, touched, slot_map, rows_in, blocks, sizes, piece, width
     )
+    pred_part = pred_mine + across(pred_other, 1)
+    parts = [pred_part[0]] + [between(pred_part[j], j) for j in range(1, n_dp)]
+
     moments = []
     new_weights = []
+    pieces = None
     start = 0
-    arrived = None
     for size, chunk in zip(sizes, grads):
-        if arrived:
+        if pieces:
+            last = pieces[-1][-1] if isinstance(pieces[-1], tuple) else pieces[-1]
+            moving = parts[1:4] + [fresh, fresh, pieces[2], pieces[1]]
             for j in range(1, n_own):
-                before = arrived[j] if j < n_own // 2 else fresh
-                chunk[j], _ = lax.optimization_barrier((chunk[j], before))
+                chunk[j] = after(chunk[j], moving[min(j, len(moving)) - 1])
         arrived = [chunk[0]] + [across(chunk[j], j) for j in range(1, n_own)]
+        arrived[-1] = after(arrived[-1], last if pieces else pred_part)
         fresh, *moments = adam(pos, arrived, weights, moment1, moment2, start, moments)
         pieces = gather_planes(fresh, dp_at, n_dp)
         new_weights = [place_weights(pos, pieces, start, half, new_weights)]
@@ -467,11 +484,6 @@
     new_weights = new_weights[0]
     new_moment1, new_moment2 = moments
 
-    pred_part = pred_mine + across(pred_other, 1)
-    parts = [lax.dynamic_index_in_dim(pred_part, dp_at, 0, keepdims=False)]
-    for shift in range(1, n_dp):
-        block = lax.dynamic_index_in_dim(pred_part, lax.rem(dp_at + shift, n_dp), 0, keepdims=False)
-        parts.append(lax.ppermute(block, "dp", [(d, (d + shift) % n_dp) for d in range(n_dp)]))
     predicted = finish_predicted(perm, parts)
     return (predicted, new_weights, new_moment1, new_moment2)
 

time: 216 us -> 224 us (1.037)
  the two profiles are of different devices: /device:TPU:2 before, /device:TPU:10 now
where the time goes in v4:
time: 224 us; the launch traced here: 222 us
  waiting for transfers between devices  118 us (53%)
  Pallas kernels  47.6 us (21%)
  starting transfers between devices  43.3 us (19%)
  local copies, waits for them, and re-layouts  9.64 us (4%)
    ppermute x6, waiting for transfers between devices, between(): return lax.ppermute(value, 'dp', [(d, d ^ j) for d in range(n_dp)])  48.6 us
    ppermute x2, waiting for transfers between devices, gather_planes(): two = lax.ppermute(fresh, 'dp', [(0, 2), (1, 3), (2, 0), (3, 1)])  34.9 us
    ppermute x20, waiting for transfers between devices, across(): return lax.ppermute(value, 'own', [(o, o ^ j) for o in range(n_own)])  26.4 us
    ppermute x20, starting transfers between devices, across(): return lax.ppermute(value, 'own', [(o, o ^ j) for o in range(n_own)])  16.3 us
    pallas_call x1, Pallas kernels, local_grads(): pl.pallas_call(body, out_shape=[pred_shape, pred_shape] + grad_shapes, in...  15.8 us
    pallas_call x2, Pallas kernels, adam(): pl.pallas_call(body, out_shape=[jax.ShapeDtypeStruct((2, size, 2, piece,...  14.9 us
    pallas_call x2, Pallas kernels, place_weights(): pl.pallas_call(body, out_shape=jax.ShapeDtypeStruct((2 * half, 2, piece,...  12.2 us
    ppermute x2, starting transfers between devices, gather_planes(): outer = lax.ppermute(two, 'dp', [(2, 3), (1, 0)])  9.31 us
  transfers between devices with their start and end apart: 34, of which 16 were waited for; matrix products, arithmetic and copies ran while one was open for 2% of the time, Pallas kernels for 4%

profile of v4, /device:TPU:10, one launch (start us, length us, event | category | flops | bytes accessed | tf_op | source)
XLA Modules:
  0.0 222.3 jit_solution(8607260914551872854)
XLA Ops:
  0.6 1.2 dynamic-slice_bitcast_fusion
  1.9 2.4 %pack_rows.1 = (bf16[528,384]{1,0:T(8,128)(2,1)}, bf16[256,256]{1,0:T(8,128)(2,1)}) custom-call(s32[1,256]{1,0:T(1,128)} %bitcast.23, bf16[256,384]{1,0:T(8,128)(2,1)} %sig_ref.1, bf16[256,384]{1,0:T(8,128)(2,1)} %cot_ref.1), custom_call_target="tpu_custom_call" | custom-call | tf_op jit(solution)/shard_map/pack_rows/pallas_call | solution.py:79
  4.3 1.6 collective-permute-start.2
  6.0 1.6 collective-permute-start.6
  8.0 1.5 collective-permute-start.4
  9.5 1.2 collective-permute-start.1
  10.8 23.3 %collective-permute-done.2 = bf16[528,384]{1,0:T(8,128)(2,1)S(1)} collective-permute-done((bf16[528,384]{1,0:T(8,128)(2,1)}, bf16[528,384]{1,0:T(8,128)(2,1)S(1)}, u32[]{:S(2)}, u32[]{:S(2)}) %collective-permute-start.2) | collective-permute-done | bytes 405536 | tf_op jit(solution)/shard_map/ppermute | solution.py:454
  34.1 7.5 %collective-permute-done.1 = bf16[528,384]{1,0:T(8,128)(2,1)S(1)} collective-permute-done((bf16[528,384]{1,0:T(8,128)(2,1)}, bf16[528,384]{1,0:T(8,128)(2,1)S(1)}, u32[]{:S(2)}, u32[]{:S(2)}) %collective-permute-start.1) | collective-permute-done | bytes 405536 | tf_op jit(solution)/shard_map/ppermute | solution.py:454
  41.6 8.5 %collective-permute-done = bf16[528,384]{1,0:T(8,128)(2,1)S(1)} collective-permute-done((bf16[528,384]{1,0:T(8,128)(2,1)}, bf16[528,384]{1,0:T(8,128)(2,1)S(1)}, u32[]{:S(2)}, u32[]{:S(2)}) %collective-permute-start) | collective-permute-done | bytes 405536 | tf_op jit(solution)/shard_map/ppermute | solution.py:454
  50.5 0.9 copy-done.3
  51.6 0.9 copy-done.5
  53.8 2.2 collective-permute-done.7.rest_1_
  56.0 1.2 copy-done.2
  57.1 15.8 %local_grads.1 = (bf16[4,256,384]{2,1,0:T(8,128)(2,1)}, bf16[4,256,384]{2,1,0:T(8,128)(2,1)}, bf16[3,2,48,256]{3,2,1,0:T(8,128)(2,1)}, bf16[3,2,48,256]{3,2,1,0:...) custom-call(s32[2]{0:T(128)} %pad_add_fusion.pos_ref, ...), custom_call_target="tpu_custom_call" | custom-call | tf_op jit(solution)/shard_map/local_grads/pallas_call | solution.py:248
  73.6 1.2 collective-permute-start.21
  74.8 1.4 collective-permute-start.16
  76.3 1.3 collective-permute-start.18
  77.7 3.0 %collective-permute-done.21.refs_7_ = bf16[3,2,48,256]{3,2,1,0:T(8,128)(2,1)S(1)} collective-permute-done((bf16[3,2,48,256]{3,2,1,0:T(8,128)(2,1)}, bf16[3,2,48,256]{3,2,1,0:T(8,128)(2,1)S(1)}, u32[]{:S(2)}, u32[]{:S(2)}) %collective-permute-start.21) | collective-permute-done | bytes 147488 | tf_op jit(solution)/shard_map/ppermute | solution.py:445
  80.7 1.4 collective-permute-start.19
  82.0 1.4 collective-permute-start.20
  83.4 1.3 add.16
  84.8 2.2 collective-permute-done.17.refs_3_
  87.0 3.3 %collective-permute-done.20.refs_6_ = bf16[3,2,48,256]{3,2,1,0:T(8,128)(2,1)S(1)} collective-permute-done((bf16[3,2,48,256]{3,2,1,0:T(8,128)(2,1)}, bf16[3,2,48,256]{3,2,1,0:T(8,128)(2,1)S(1)}, u32[]{:S(2)}, u32[]{:S(2)}) %collective-permute-start.20) | collective-permute-done | bytes 147488 | tf_op jit(solution)/shard_map/ppermute | solution.py:445
  91.0 6.2 %adam_step.2 = (bf16[2,3,2,48,256]{4,3,2,1,0:T(8,128)(2,1)}, f32[16,2,48,256]{3,2,1,0:T(8,128)}, f32[16,2,48,256]{3,2,1,0:T(8,128)}) custom-call(s32[2]{0:T(128)} %pad_add_fusion.pos_ref, bf16[3,2,48,256]{3,2,1,0:T(8,128)(2,1)} %get-tuple-element.53.refs_0_, bf16[3,2,48,256]{3,2,1,0:T(8,128)(2,1)} %copy-done.26, bf16[3,2,48,256]{3,2,1,0:T(8,128)(2,1)} %copy-done.28, ...), custom_call_target="tpu_custom_call" | custom-call | tf_op jit(solution)/shard_map/adam_step/pallas_call | solution.py:333
  97.2 2.4 %collective-permute-start.26 = (bf16[2,3,2,48,256]{4,3,2,1,0:T(8,128)(2,1)}, bf16[2,3,2,48,256]{4,3,2,1,0:T(8,128)(2,1)S(1)}, u32[]{:S(2)}, u32[]{:S(2)}) collective-permute-start(bf16[2,3,2,48,256]{4,3,2,1,0:T(8,128)(2,1)} %get-tuple-element.62.refs_0_), channel_id=1, source_target_pairs={{0,8},{8,0},{16,24},{24,16},{1,9},{9,1},{17,25},{25,17},{2,10},{10... | collective-permute-start | bytes 884744 | tf_op jit(solution)/shard_map/ppermute | solution.py:402
  99.6 1.1 collective-permute-start.24
  101.9 17.0 %collective-permute-done.24.refs_2_ = bf16[2,3,2,48,256]{4,3,2,1,0:T(8,128)(2,1)S(1)} collective-permute-done((bf16[2,3,2,48,256]{4,3,2,1,0:T(8,128)(2,1)}, bf16[2,3,2,48,256]{4,3,2,1,0:T(8,128)(2,1)S(1)}, u32[]{:S(2)}, u32[]{:S(2)}) %collective-permute-start.24) | collective-permute-done | bytes 294944 | tf_op jit(solution)/shard_map/ppermute | solution.py:401
  118.9 4.3 %collective-permute-start.28 = (bf16[2,3,2,48,256]{4,3,2,1,0:T(8,128)(2,1)S(1)}, bf16[2,3,2,48,256]{4,3,2,1,0:T(8,128)(2,1)S(1)}, u32[]{:S(2)}, u32[]{:S(2)}) collective-permute-start(bf16[2,3,2,48,256]{4,3,2,1,0:T(8,128)(2,1)S(1)} %collective-permute-done.24.refs_2_), channel_id=1, source_target_pairs={{16,24},{8,0},{17,25},{9,1},{18,26},{10,2},{19,27},{11,3},{20,28},... | collective-permute-start | bytes 884744 | tf_op jit(solution)/shard_map/ppermute | solution.py:404
  123.2 1.6 collective-permute-start.22
  125.3 2.7 %collective-permute-start.9 = (bf16[256,384]{1,0:T(8,128)(2,1)S(1)}, bf16[256,384]{1,0:T(8,128)(2,1)S(1)}, u32[]{:S(2)}, u32[]{:S(2)}) collective-permute-start(bf16[256,384]{1,0:T(8,128)(2,1)S(1)} %get-tuple-element.80), channel_id=1, source_target_pairs={{0,8},{8,0},{16,24},{24,16},{1,9},{9,1},{17,25},{25,17},{2,10},{10... | collective-permute-start | bytes 589832 | tf_op jit(solution)/shard_map/ppermute | solution.py:454
  127.9 6.7 %collective-permute-done.10.refs_2_ = bf16[256,384]{1,0:T(8,128)(2,1)S(1)} collective-permute-done((bf16[256,384]{1,0:T(8,128)(2,1)S(1)}, bf16[256,384]{1,0:T(8,128)(2,1)S(1)}, u32[]{:S(2)}, u32[]{:S(2)}) %collective-permute-start.10) | collective-permute-done | bytes 196640 | tf_op jit(solution)/shard_map/ppermute | solution.py:454
  135.1 2.6 %collective-permute-done.9.refs_1_ = bf16[256,384]{1,0:T(8,128)(2,1)S(1)} collective-permute-done((bf16[256,384]{1,0:T(8,128)(2,1)S(1)}, bf16[256,384]{1,0:T(8,128)(2,1)S(1)}, u32[]{:S(2)}, u32[]{:S(2)}) %collective-permute-start.9) | collective-permute-done | bytes 196640 | tf_op jit(solution)/shard_map/ppermute | solution.py:454
  138.5 1.2 collective-permute-start.14
  139.7 1.1 collective-permute-start.25
  140.8 1.6 collective-permute-done.23.refs_5_
  142.4 4.5 %collective-permute-done.13.refs_2_ = bf16[5,2,48,256]{3,2,1,0:T(8,128)(2,1)S(1)} collective-permute-done((bf16[5,2,48,256]{3,2,1,0:T(8,128)(2,1)S(1)}, bf16[5,2,48,256]{3,2,1,0:T(8,128)(2,1)S(1)}, u32[]{:S(2)}, u32[]{:S(2)}) %collective-permute-start.13) | collective-permute-done | bytes 245792 | tf_op jit(solution)/shard_map/ppermute | solution.py:445
  146.9 3.7 %collective-permute-done.14.refs_3_ = bf16[5,2,48,256]{3,2,1,0:T(8,128)(2,1)S(1)} collective-permute-done((bf16[5,2,48,256]{3,2,1,0:T(8,128)(2,1)S(1)}, bf16[5,2,48,256]{3,2,1,0:T(8,128)(2,1)S(1)}, u32[]{:S(2)}, u32[]{:S(2)}) %collective-permute-start.14) | collective-permute-done | bytes 245792 | tf_op jit(solution)/shard_map/ppermute | solution.py:445
  150.6 6.0 %collective-permute-done.25.refs_6_ = bf16[5,2,48,256]{3,2,1,0:T(8,128)(2,1)S(1)} collective-permute-done((bf16[5,2,48,256]{3,2,1,0:T(8,128)(2,1)S(1)}, bf16[5,2,48,256]{3,2,1,0:T(8,128)(2,1)S(1)}, u32[]{:S(2)}, u32[]{:S(2)}) %collective-permute-start.25) | collective-permute-done | bytes 245792 | tf_op jit(solution)/shard_map/ppermute | solution.py:445
  157.2 8.8 %adam_step.3 = (bf16[2,5,2,48,256]{4,3,2,1,0:T(8,128)(2,1)}, f32[16,2,48,256]{3,2,1,0:T(8,128)}, f32[16,2,48,256]{3,2,1,0:T(8,128)}) custom-call(s32[2]{0:T(128)} %pad_add_fusion.pos_ref, bf16[5,2,48,256]{3,2,1,0:T(8,128)(2,1)} %get-tuple-element.45.refs_0_, bf16[5,2,48,256]{3,2,1,0:T(8,128)(2,1)} %copy-done.19, ...), custom_call_target="tpu_custom_call", output_to_operand_aliasing={{1}: (12, {}), {2}: (13, {})} | custom-call | tf_op jit(solution)/shard_map/adam_step/pallas_call | solution.py:333
  166.1 2.9 %collective-permute-start.30 = (bf16[2,5,2,48,256]{4,3,2,1,0:T(8,128)(2,1)}, bf16[2,5,2,48,256]{4,3,2,1,0:T(8,128)(2,1)S(1)}, u32[]{:S(2)}, u32[]{:S(2)}) collective-permute-start(bf16[2,5,2,48,256]{4,3,2,1,0:T(8,128)(2,1)} %get-tuple-element.73.refs_0_), channel_id=1, source_target_pairs={{0,16},{8,24},{16,0},{24,8},{1,17},{9,25},{17,1},{25,9},{2,18},{10... | collective-permute-start | bytes 1474568 | tf_op jit(solution)/shard_map/ppermute | solution.py:401
  168.9 2.3 %collective-permute-start.31 = (bf16[2,5,2,48,256]{4,3,2,1,0:T(8,128)(2,1)}, bf16[2,5,2,48,256]{4,3,2,1,0:T(8,128)(2,1)S(1)}, u32[]{:S(2)}, u32[]{:S(2)}) collective-permute-start(bf16[2,5,2,48,256]{4,3,2,1,0:T(8,128)(2,1)} %get-tuple-element.73.refs_0_), channel_id=1, source_target_pairs={{8,16},{16,8},{9,17},{17,9},{10,18},{18,10},{11,19},{19,11},{12,20... | collective-permute-start | bytes 1474568 | tf_op jit(solution)/shard_map/ppermute | solution.py:403
  171.3 17.9 %collective-permute-done.30.refs_2_ = bf16[2,5,2,48,256]{4,3,2,1,0:T(8,128)(2,1)S(1)} collective-permute-done((bf16[2,5,2,48,256]{4,3,2,1,0:T(8,128)(2,1)}, bf16[2,5,2,48,256]{4,3,2,1,0:T(8,128)(2,1)S(1)}, u32[]{:S(2)}, u32[]{:S(2)}) %collective-permute-start.30) | collective-permute-done | bytes 491552 | tf_op jit(solution)/shard_map/ppermute | solution.py:401
  189.2 5.0 %collective-permute-start.32 = (bf16[2,5,2,48,256]{4,3,2,1,0:T(8,128)(2,1)S(1)}, bf16[2,5,2,48,256]{4,3,2,1,0:T(8,128)(2,1)S(1)}, u32[]{:S(2)}, u32[]{:S(2)}) collective-permute-start(bf16[2,5,2,48,256]{4,3,2,1,0:T(8,128)(2,1)S(1)} %collective-permute-done.30.refs_2_), channel_id=1, source_target_pairs={{16,24},{8,0},{17,25},{9,1},{18,26},{10,2},{19,27},{11,3},{20,28},... | collective-permute-start | bytes 1474568 | tf_op jit(solution)/shard_map/ppermute | solution.py:404
  194.3 2.6 %collective-permute-start.33 = (bf16[2,3,2,48,256]{4,3,2,1,0:T(8,128)(2,1)S(1)}, bf16[2,3,2,48,256]{4,3,2,1,0:T(8,128)(2,1)S(1)}, u32[]{:S(2)}, u32[]{:S(2)}) collective-permute-start(bf16[2,3,2,48,256]{4,3,2,1,0:T(8,128)(2,1)S(1)} %copy-done.11), channel_id=1, source_target_pairs={{8,16},{16,8},{9,17},{17,9},{10,18},{18,10},{11,19},{19,11},{12,20... | collective-permute-start | bytes 884744 | tf_op jit(solution)/shard_map/ppermute | solution.py:403
  196.9 2.2 %finish_predicted.1 = bf16[256,384]{1,0:T(8,128)(2,1)} custom-call(bf16[256,256]{1,0:T(8,128)(2,1)} %get-tuple-element.40.perm_ref, bf16[256,384]{1,0:T(8,128)(2,1)} %get-tuple-element.81.refs_0_, bf16[256,384]{1,0:T(8,128)(2,1)} %copy-done.25, bf16[256,384]{1,0:T(8,128)(2,1)} %copy-done.24, bf16[256,384]{1,0:T(8,128)(2,1)} %copy-done.23), custom_call_target="tpu_custom_call" | custom-call | tf_op jit(solution)/shard_map/finish_predicted/pallas_call | solution.py:420
  199.2 8.5 %collective-permute-done.33.refs_3_ = bf16[2,3,2,48,256]{4,3,2,1,0:T(8,128)(2,1)S(1)} collective-permute-done((bf16[2,3,2,48,256]{4,3,2,1,0:T(8,128)(2,1)S(1)}, bf16[2,3,2,48,256]{4,3,2,1,0:T(8,128)(2,1)S(1)}, u32[]{:S(2)}, u32[]{:S(2)}) %collective-permute-start.33) | collective-permute-done | bytes 294944 | tf_op jit(solution)/shard_map/ppermute | solution.py:403
  208.3 5.0 %place_weights.2.refs_5_ = bf16[16,2,48,1024]{3,2,1,0:T(8,128)(2,1)} custom-call(s32[2]{0:T(128)} %pad_add_fusion.pos_ref, bf16[2,3,2,48,256]{4,3,2,1,0:T(8,128)(2,1)} %get-tuple-element.62.refs_0_, bf16[2,3,2,48,256]{4,3,2,1,0:T(8,128)(2,1)} %copy-done.12, bf16[2,3,2,48,256]{4,3,2,1,0:T(8,128)(2,1)} %copy-done.13, bf16[2,3,2,48,256]{4,3,2,1,0:T(8,128)(2,1)} %copy-done.15, ...), custom_call_target="tpu_custom_call" | custom-call | tf_op jit(solution)/shard_map/place_weights/pallas_call | solution.py:381
  215.1 7.2 %place_weights.3 = bf16[16,2,48,1024]{3,2,1,0:T(8,128)(2,1)} custom-call(s32[2]{0:T(128)} %pad_add_fusion.pos_ref, bf16[2,5,2,48,256]{4,3,2,1,0:T(8,128)(2,1)} %get-tuple-element.73.refs_0_, bf16[2,5,2,48,256]{4,3,2,1,0:T(8,128)(2,1)} %copy-done.8, bf16[2,5,2,48,256]{4,3,2,1,0:T(8,128)(2,1)} %copy-done.6, ...), custom_call_target="tpu_custom_call", output_to_operand_aliasing={{}: (6, {})} | custom-call | tf_op jit(solution)/shard_map/place_weights/pallas_call | solution.py:381
  (116 shorter events, 10.0 us)
Async XLA Ops:
  1.8 4.1 %collective-permute-start.3 = (bf16[8,2,48,256]{3,2,1,0:T(8,128)(2,1)S(1)}, bf16[8,2,48,256]{3,2,1,0:T(8,128)(2,1)S(1)}, u32[]{:S(2)}, u32[]{:S(2)}) collective-permute-start(bf16[8,2,48,256]{3,2,1,0:T(8,128)(2,1)S(1)} %get-tuple-element.77), channel_id=1, source_target_pairs={{0,1},{1,0},{2,3},{3,2},{4,5},{5,4},{6,7},{7,6},{8,9},{9,8},{10,11... | collective-permute-start | bytes 1179656 | tf_op jit(solution)/shard_map/ppermute | solution.py:445
  4.3 45.8 %copy-start.10 = (bf16[528,384]{1,0:T(8,128)(2,1)S(1)}, bf16[528,384]{1,0:T(8,128)(2,1)}, u32[]{:S(2)}) copy-start(bf16[528,384]{1,0:T(8,128)(2,1)} %get-tuple-element.41) | copy-start | bytes 1216516
  4.3 29.8 %collective-permute-start.2 = (bf16[528,384]{1,0:T(8,128)(2,1)}, bf16[528,384]{1,0:T(8,128)(2,1)S(1)}, u32[]{:S(2)}, u32[]{:S(2)}) collective-permute-start(bf16[528,384]{1,0:T(8,128)(2,1)} %get-tuple-element.41), channel_id=1, source_target_pairs={{0,24},{8,16},{16,8},{24,0},{1,25},{9,17},{17,9},{25,1},{2,26},{10... | collective-permute-start | bytes 1216520 | tf_op jit(solution)/shard_map/ppermute | solution.py:454
  6.0 44.4 %copy-start.1 = (bf16[2,8,2,48,256]{4,3,2,1,0:T(8,128)(2,1)}, bf16[2,8,2,48,256]{4,3,2,1,0:T(8,128)(2,1)S(1)}, u32[]{:S(2)}) copy-start(bf16[2,8,2,48,256]{4,3,2,1,0:T(8,128)(2,1)S(1)} %pad_maximum_fusion.1.rest_2_) | copy-start | bytes 2359300
  6.0 44.4 %collective-permute-start.6 = (bf16[2,8,2,48,256]{4,3,2,1,0:T(8,128)(2,1)S(1)}, bf16[2,8,2,48,256]{4,3,2,1,0:T(8,128)(2,1)S(1)}, u32[]{:S(2)}, u32[]{:S(2)}) collective-permute-start(bf16[2,8,2,48,256]{4,3,2,1,0:T(8,128)(2,1)S(1)} %pad_maximum_fusion.1.rest_2_), channel_id=1, source_target_pairs={{0,6},{1,7},{2,4},{3,5},{4,2},{5,3},{6,0},{7,1},{8,14},{9,15},{10,... | collective-permute-start | bytes 2359304 | tf_op jit(solution)/shard_map/ppermute | solution.py:445
  7.5 42.9 %collective-permute-start.5 = (bf16[2,8,2,48,256]{4,3,2,1,0:T(8,128)(2,1)S(1)}, bf16[2,8,2,48,256]{4,3,2,1,0:T(8,128)(2,1)S(1)}, u32[]{:S(2)}, u32[]{:S(2)}) collective-permute-start(bf16[2,8,2,48,256]{4,3,2,1,0:T(8,128)(2,1)S(1)} %pad_maximum_fusion.1.rest_2_), channel_id=1, source_target_pairs={{0,4},{1,5},{2,6},{3,7},{4,0},{5,1},{6,2},{7,3},{8,12},{9,13},{10,... | collective-permute-start | bytes 2359304 | tf_op jit(solution)/shard_map/ppermute | solution.py:445
  8.0 42.4 %collective-permute-start.4 = (bf16[2,8,2,48,256]{4,3,2,1,0:T(8,128)(2,1)S(1)}, bf16[2,8,2,48,256]{4,3,2,1,0:T(8,128)(2,1)S(1)}, u32[]{:S(2)}, u32[]{:S(2)}) collective-permute-start(bf16[2,8,2,48,256]{4,3,2,1,0:T(8,128)(2,1)S(1)} %pad_maximum_fusion.1.rest_2_), channel_id=1, source_target_pairs={{0,2},{1,3},{2,0},{3,1},{4,6},{5,7},{6,4},{7,5},{8,10},{9,11},{10,... | collective-permute-start | bytes 2359304 | tf_op jit(solution)/shard_map/ppermute | solution.py:445
  9.5 32.1 %collective-permute-start.1 = (bf16[528,384]{1,0:T(8,128)(2,1)}, bf16[528,384]{1,0:T(8,128)(2,1)S(1)}, u32[]{:S(2)}, u32[]{:S(2)}) collective-permute-start(bf16[528,384]{1,0:T(8,128)(2,1)} %get-tuple-element.41), channel_id=1, source_target_pairs={{0,16},{8,24},{16,0},{24,8},{1,17},{9,25},{17,1},{25,9},{2,18},{10... | collective-permute-start | bytes 1216520 | tf_op jit(solution)/shard_map/ppermute | solution.py:454
  34.1 16.1 %collective-permute-start = (bf16[528,384]{1,0:T(8,128)(2,1)}, bf16[528,384]{1,0:T(8,128)(2,1)S(1)}, u32[]{:S(2)}, u32[]{:S(2)}) collective-permute-start(bf16[528,384]{1,0:T(8,128)(2,1)} %get-tuple-element.41), channel_id=1, source_target_pairs={{0,8},{8,0},{16,24},{24,16},{1,9},{9,1},{17,25},{25,17},{2,10},{10... | collective-permute-start | bytes 1216520 | tf_op jit(solution)/shard_map/ppermute | solution.py:454
  52.5 3.5 %collective-permute-start.7 = (bf16[4,528,384]{2,1,0:T(8,128)(2,1)S(1)}, bf16[4,528,384]{2,1,0:T(8,128)(2,1)S(1)}, u32[]{:S(2)}, u32[]{:S(2)}) collective-permute-start(bf16[4,528,384]{2,1,0:T(8,128)(2,1)S(1)} %pad_maximum_fusion.rest_0_), channel_id=1, source_target_pairs={{0,1},{1,0},{2,3},{3,2},{4,5},{5,4},{6,7},{7,6},{8,9},{9,8},{10,11... | collective-permute-start | bytes 4866056 | tf_op jit(solution)/shard_map/ppermute | solution.py:445
  73.0 9.0 %collective-permute-start.8 = (bf16[4,256,384]{2,1,0:T(8,128)(2,1)}, bf16[4,256,384]{2,1,0:T(8,128)(2,1)S(1)}, u32[]{:S(2)}, u32[]{:S(2)}) collective-permute-start(bf16[4,256,384]{2,1,0:T(8,128)(2,1)} %get-tuple-element.44), channel_id=1, source_target_pairs={{0,1},{1,0},{2,3},{3,2},{4,5},{5,4},{6,7},{7,6},{8,9},{9,8},{10,11... | collective-permute-start | bytes 2359304 | tf_op jit(solution)/shard_map/ppermute | solution.py:445
  73.1 3.2 %collective-permute-start.15 = (bf16[3,2,48,256]{3,2,1,0:T(8,128)(2,1)}, bf16[3,2,48,256]{3,2,1,0:T(8,128)(2,1)S(1)}, u32[]{:S(2)}, u32[]{:S(2)}) collective-permute-start(bf16[3,2,48,256]{3,2,1,0:T(8,128)(2,1)} %get-tuple-element.54), channel_id=1, source_target_pairs={{0,1},{1,0},{2,3},{3,2},{4,5},{5,4},{6,7},{7,6},{8,9},{9,8},{10,11... | collective-permute-start | bytes 442376 | tf_op jit(solution)/shard_map/ppermute | solution.py:445
  73.6 7.1 %collective-permute-start.21 = (bf16[3,2,48,256]{3,2,1,0:T(8,128)(2,1)}, bf16[3,2,48,256]{3,2,1,0:T(8,128)(2,1)S(1)}, u32[]{:S(2)}, u32[]{:S(2)}) collective-permute-start(bf16[3,2,48,256]{3,2,1,0:T(8,128)(2,1)} %get-tuple-element.60), channel_id=1, source_target_pairs={{0,7},{1,6},{2,5},{3,4},{4,3},{5,2},{6,1},{7,0},{8,15},{9,14},{10,... | collective-permute-start | bytes 442376 | tf_op jit(solution)/shard_map/ppermute | solution.py:445
  74.8 10.0 %collective-permute-start.16 = (bf16[3,2,48,256]{3,2,1,0:T(8,128)(2,1)}, bf16[3,2,48,256]{3,2,1,0:T(8,128)(2,1)S(1)}, u32[]{:S(2)}, u32[]{:S(2)}) collective-permute-start(bf16[3,2,48,256]{3,2,1,0:T(8,128)(2,1)} %get-tuple-element.55), channel_id=1, source_target_pairs={{0,2},{1,3},{2,0},{3,1},{4,6},{5,7},{6,4},{7,5},{8,10},{9,11},{10,... | collective-permute-start | bytes 442376 | tf_op jit(solution)/shard_map/ppermute | solution.py:445
  76.2 10.7 %collective-permute-start.17 = (bf16[3,2,48,256]{3,2,1,0:T(8,128)(2,1)}, bf16[3,2,48,256]{3,2,1,0:T(8,128)(2,1)S(1)}, u32[]{:S(2)}, u32[]{:S(2)}) collective-permute-start(bf16[3,2,48,256]{3,2,1,0:T(8,128)(2,1)} %get-tuple-element.56), channel_id=1, source_target_pairs={{0,3},{1,2},{2,1},{3,0},{4,7},{5,6},{6,5},{7,4},{8,11},{9,10},{10,... | collective-permute-start | bytes 442376 | tf_op jit(solution)/shard_map/ppermute | solution.py:445
  76.3 10.6 %collective-permute-start.18 = (bf16[3,2,48,256]{3,2,1,0:T(8,128)(2,1)}, bf16[3,2,48,256]{3,2,1,0:T(8,128)(2,1)S(1)}, u32[]{:S(2)}, u32[]{:S(2)}) collective-permute-start(bf16[3,2,48,256]{3,2,1,0:T(8,128)(2,1)} %get-tuple-element.57), channel_id=1, source_target_pairs={{0,4},{1,5},{2,6},{3,7},{4,0},{5,1},{6,2},{7,3},{8,12},{9,13},{10,... | collective-permute-start | bytes 442376 | tf_op jit(solution)/shard_map/ppermute | solution.py:445
  80.7 6.3 %collective-permute-start.19 = (bf16[3,2,48,256]{3,2,1,0:T(8,128)(2,1)}, bf16[3,2,48,256]{3,2,1,0:T(8,128)(2,1)S(1)}, u32[]{:S(2)}, u32[]{:S(2)}) collective-permute-start(bf16[3,2,48,256]{3,2,1,0:T(8,128)(2,1)} %get-tuple-element.58), channel_id=1, source_target_pairs={{0,5},{1,4},{2,7},{3,6},{4,1},{5,0},{6,3},{7,2},{8,13},{9,12},{10,... | collective-permute-start | bytes 442376 | tf_op jit(solution)/shard_map/ppermute | solution.py:445
  82.0 8.3 %collective-permute-start.20 = (bf16[3,2,48,256]{3,2,1,0:T(8,128)(2,1)}, bf16[3,2,48,256]{3,2,1,0:T(8,128)(2,1)S(1)}, u32[]{:S(2)}, u32[]{:S(2)}) collective-permute-start(bf16[3,2,48,256]{3,2,1,0:T(8,128)(2,1)} %get-tuple-element.59), channel_id=1, source_target_pairs={{0,6},{1,7},{2,4},{3,5},{4,2},{5,3},{6,0},{7,1},{8,14},{9,15},{10,... | collective-permute-start | bytes 442376 | tf_op jit(solution)/shard_map/ppermute | solution.py:445
  91.0 32.3 %copy-start.40 = (bf16[5,2,48,256]{3,2,1,0:T(8,128)(2,1)S(1)}, bf16[5,2,48,256]{3,2,1,0:T(8,128)(2,1)}, u32[]{:S(2)}) copy-start(bf16[5,2,48,256]{3,2,1,0:T(8,128)(2,1)} %get-tuple-element.63) | copy-start | bytes 737284
  91.0 33.9 %copy-start.39 = (bf16[5,2,48,256]{3,2,1,0:T(8,128)(2,1)S(1)}, bf16[5,2,48,256]{3,2,1,0:T(8,128)(2,1)}, u32[]{:S(2)}) copy-start(bf16[5,2,48,256]{3,2,1,0:T(8,128)(2,1)} %get-tuple-element.69) | copy-start | bytes 737284
  91.0 43.6 %copy-start.38 = (bf16[5,2,48,256]{3,2,1,0:T(8,128)(2,1)S(1)}, bf16[5,2,48,256]{3,2,1,0:T(8,128)(2,1)}, u32[]{:S(2)}) copy-start(bf16[5,2,48,256]{3,2,1,0:T(8,128)(2,1)} %get-tuple-element.65) | copy-start | bytes 737284
  91.0 46.7 %copy-start.37 = (bf16[5,2,48,256]{3,2,1,0:T(8,128)(2,1)S(1)}, bf16[5,2,48,256]{3,2,1,0:T(8,128)(2,1)}, u32[]{:S(2)}) copy-start(bf16[5,2,48,256]{3,2,1,0:T(8,128)(2,1)} %get-tuple-element.47) | copy-start | bytes 737284
  91.0 47.1 %copy-start.36 = (bf16[5,2,48,256]{3,2,1,0:T(8,128)(2,1)S(1)}, bf16[5,2,48,256]{3,2,1,0:T(8,128)(2,1)}, u32[]{:S(2)}) copy-start(bf16[5,2,48,256]{3,2,1,0:T(8,128)(2,1)} %get-tuple-element.49) | copy-start | bytes 737284
  91.0 47.5 %copy-start.35 = (bf16[5,2,48,256]{3,2,1,0:T(8,128)(2,1)S(1)}, bf16[5,2,48,256]{3,2,1,0:T(8,128)(2,1)}, u32[]{:S(2)}) copy-start(bf16[5,2,48,256]{3,2,1,0:T(8,128)(2,1)} %get-tuple-element.51) | copy-start | bytes 737284
  91.0 48.7 %copy-start.34 = (bf16[5,2,48,256]{3,2,1,0:T(8,128)(2,1)S(1)}, bf16[5,2,48,256]{3,2,1,0:T(8,128)(2,1)}, u32[]{:S(2)}) copy-start(bf16[5,2,48,256]{3,2,1,0:T(8,128)(2,1)} %get-tuple-element.67) | copy-start | bytes 737284
  97.2 27.7 %collective-permute-start.26 = (bf16[2,3,2,48,256]{4,3,2,1,0:T(8,128)(2,1)}, bf16[2,3,2,48,256]{4,3,2,1,0:T(8,128)(2,1)S(1)}, u32[]{:S(2)}, u32[]{:S(2)}) collective-permute-start(bf16[2,3,2,48,256]{4,3,2,1,0:T(8,128)(2,1)} %get-tuple-element.62.refs_0_), channel_id=1, source_target_pairs={{0,8},{8,0},{16,24},{24,16},{1,9},{9,1},{17,25},{25,17},{2,10},{10... | collective-permute-start | bytes 884744 | tf_op jit(solution)/shard_map/ppermute | solution.py:402
  99.6 19.3 %collective-permute-start.24 = (bf16[2,3,2,48,256]{4,3,2,1,0:T(8,128)(2,1)}, bf16[2,3,2,48,256]{4,3,2,1,0:T(8,128)(2,1)S(1)}, u32[]{:S(2)}, u32[]{:S(2)}) collective-permute-start(bf16[2,3,2,48,256]{4,3,2,1,0:T(8,128)(2,1)} %get-tuple-element.62.refs_0_), channel_id=1, source_target_pairs={{0,16},{8,24},{16,0},{24,8},{1,17},{9,25},{17,1},{25,9},{2,18},{10... | collective-permute-start | bytes 884744 | tf_op jit(solution)/shard_map/ppermute | solution.py:401
  101.4 23.8 %collective-permute-start.11 = (bf16[256,384]{1,0:T(8,128)(2,1)S(1)}, bf16[256,384]{1,0:T(8,128)(2,1)S(1)}, u32[]{:S(2)}, u32[]{:S(2)}) collective-permute-start(bf16[256,384]{1,0:T(8,128)(2,1)S(1)} %get-tuple-element.78), channel_id=1, source_target_pairs={{0,24},{8,16},{16,8},{24,0},{1,25},{9,17},{17,9},{25,1},{2,26},{10... | collective-permute-start | bytes 589832 | tf_op jit(solution)/shard_map/ppermute | solution.py:454
  118.9 47.1 %copy-start.13 = (bf16[2,3,2,48,256]{4,3,2,1,0:T(8,128)(2,1)}, bf16[2,3,2,48,256]{4,3,2,1,0:T(8,128)(2,1)S(1)}, u32[]{:S(2)}) copy-start(bf16[2,3,2,48,256]{4,3,2,1,0:T(8,128)(2,1)S(1)} %collective-permute-done.24.refs_2_) | copy-start | bytes 884740
  118.9 20.7 %collective-permute-start.28 = (bf16[2,3,2,48,256]{4,3,2,1,0:T(8,128)(2,1)S(1)}, bf16[2,3,2,48,256]{4,3,2,1,0:T(8,128)(2,1)S(1)}, u32[]{:S(2)}, u32[]{:S(2)}) collective-permute-start(bf16[2,3,2,48,256]{4,3,2,1,0:T(8,128)(2,1)S(1)} %collective-permute-done.24.refs_2_), channel_id=1, source_target_pairs={{16,24},{8,0},{17,25},{9,1},{18,26},{10,2},{19,27},{11,3},{20,28},... | collective-permute-start | bytes 884744 | tf_op jit(solution)/shard_map/ppermute | solution.py:404
  123.2 14.8 %collective-permute-start.22 = (bf16[5,2,48,256]{3,2,1,0:T(8,128)(2,1)S(1)}, bf16[5,2,48,256]{3,2,1,0:T(8,128)(2,1)S(1)}, u32[]{:S(2)}, u32[]{:S(2)}) collective-permute-start(bf16[5,2,48,256]{3,2,1,0:T(8,128)(2,1)S(1)} %copy-done.40), channel_id=1, source_target_pairs={{0,4},{1,5},{2,6},{3,7},{4,0},{5,1},{6,2},{7,3},{8,12},{9,13},{10,... | collective-permute-start | bytes 737288 | tf_op jit(solution)/shard_map/ppermute | solution.py:445
  124.8 41.2 %copy-start.12 = (bf16[2,3,2,48,256]{4,3,2,1,0:T(8,128)(2,1)}, bf16[2,3,2,48,256]{4,3,2,1,0:T(8,128)(2,1)S(1)}, u32[]{:S(2)}) copy-start(bf16[2,3,2,48,256]{4,3,2,1,0:T(8,128)(2,1)S(1)} %collective-permute-done.26.refs_1_) | copy-start | bytes 884740
  124.9 13.6 %collective-permute-start.27 = (bf16[5,2,48,256]{3,2,1,0:T(8,128)(2,1)S(1)}, bf16[5,2,48,256]{3,2,1,0:T(8,128)(2,1)S(1)}, u32[]{:S(2)}, u32[]{:S(2)}) collective-permute-start(bf16[5,2,48,256]{3,2,1,0:T(8,128)(2,1)S(1)} %copy-done.39), channel_id=1, source_target_pairs={{0,7},{1,6},{2,5},{3,4},{4,3},{5,2},{6,1},{7,0},{8,15},{9,14},{10,... | collective-permute-start | bytes 737288 | tf_op jit(solution)/shard_map/ppermute | solution.py:445
  124.9 9.7 %collective-permute-start.10 = (bf16[256,384]{1,0:T(8,128)(2,1)S(1)}, bf16[256,384]{1,0:T(8,128)(2,1)S(1)}, u32[]{:S(2)}, u32[]{:S(2)}) collective-permute-start(bf16[256,384]{1,0:T(8,128)(2,1)S(1)} %get-tuple-element.79), channel_id=1, source_target_pairs={{0,16},{8,24},{16,0},{24,8},{1,17},{9,25},{17,1},{25,9},{2,18},{10... | collective-permute-start | bytes 589832 | tf_op jit(solution)/shard_map/ppermute | solution.py:454
  125.3 40.8 %copy-start.23 = (bf16[256,384]{1,0:T(8,128)(2,1)}, bf16[256,384]{1,0:T(8,128)(2,1)S(1)}, u32[]{:S(2)}) copy-start(bf16[256,384]{1,0:T(8,128)(2,1)S(1)} %collective-permute-done.11.refs_3_) | copy-start | bytes 589828
  125.3 12.4 %collective-permute-start.9 = (bf16[256,384]{1,0:T(8,128)(2,1)S(1)}, bf16[256,384]{1,0:T(8,128)(2,1)S(1)}, u32[]{:S(2)}, u32[]{:S(2)}) collective-permute-start(bf16[256,384]{1,0:T(8,128)(2,1)S(1)} %get-tuple-element.80), channel_id=1, source_target_pairs={{0,8},{8,0},{16,24},{24,16},{1,9},{9,1},{17,25},{25,17},{2,10},{10... | collective-permute-start | bytes 589832 | tf_op jit(solution)/shard_map/ppermute | solution.py:454
  134.6 31.4 %copy-start.24 = (bf16[256,384]{1,0:T(8,128)(2,1)}, bf16[256,384]{1,0:T(8,128)(2,1)S(1)}, u32[]{:S(2)}) copy-start(bf16[256,384]{1,0:T(8,128)(2,1)S(1)} %collective-permute-done.10.refs_2_) | copy-start | bytes 589828
  134.6 7.8 %collective-permute-start.23 = (bf16[5,2,48,256]{3,2,1,0:T(8,128)(2,1)S(1)}, bf16[5,2,48,256]{3,2,1,0:T(8,128)(2,1)S(1)}, u32[]{:S(2)}, u32[]{:S(2)}) collective-permute-start(bf16[5,2,48,256]{3,2,1,0:T(8,128)(2,1)S(1)} %copy-done.38), channel_id=1, source_target_pairs={{0,5},{1,4},{2,7},{3,6},{4,1},{5,0},{6,3},{7,2},{8,13},{9,12},{10,... | collective-permute-start | bytes 737288 | tf_op jit(solution)/shard_map/ppermute | solution.py:445
  137.7 4.7 %collective-permute-start.12 = (bf16[5,2,48,256]{3,2,1,0:T(8,128)(2,1)S(1)}, bf16[5,2,48,256]{3,2,1,0:T(8,128)(2,1)S(1)}, u32[]{:S(2)}, u32[]{:S(2)}) collective-permute-start(bf16[5,2,48,256]{3,2,1,0:T(8,128)(2,1)S(1)} %copy-done.37), channel_id=1, source_target_pairs={{0,1},{1,0},{2,3},{3,2},{4,5},{5,4},{6,7},{7,6},{8,9},{9,8},{10,11... | collective-permute-start | bytes 737288 | tf_op jit(solution)/shard_map/ppermute | solution.py:445
  138.1 8.9 %collective-permute-start.13 = (bf16[5,2,48,256]{3,2,1,0:T(8,128)(2,1)S(1)}, bf16[5,2,48,256]{3,2,1,0:T(8,128)(2,1)S(1)}, u32[]{:S(2)}, u32[]{:S(2)}) collective-permute-start(bf16[5,2,48,256]{3,2,1,0:T(8,128)(2,1)S(1)} %copy-done.36), channel_id=1, source_target_pairs={{0,2},{1,3},{2,0},{3,1},{4,6},{5,7},{6,4},{7,5},{8,10},{9,11},{10,... | collective-permute-start | bytes 737288 | tf_op jit(solution)/shard_map/ppermute | solution.py:445
  138.5 12.1 %collective-permute-start.14 = (bf16[5,2,48,256]{3,2,1,0:T(8,128)(2,1)S(1)}, bf16[5,2,48,256]{3,2,1,0:T(8,128)(2,1)S(1)}, u32[]{:S(2)}, u32[]{:S(2)}) collective-permute-start(bf16[5,2,48,256]{3,2,1,0:T(8,128)(2,1)S(1)} %copy-done.35), channel_id=1, source_target_pairs={{0,3},{1,2},{2,1},{3,0},{4,7},{5,6},{6,5},{7,4},{8,11},{9,10},{10,... | collective-permute-start | bytes 737288 | tf_op jit(solution)/shard_map/ppermute | solution.py:445
  139.7 16.9 %collective-permute-start.25 = (bf16[5,2,48,256]{3,2,1,0:T(8,128)(2,1)S(1)}, bf16[5,2,48,256]{3,2,1,0:T(8,128)(2,1)S(1)}, u32[]{:S(2)}, u32[]{:S(2)}) collective-permute-start(bf16[5,2,48,256]{3,2,1,0:T(8,128)(2,1)S(1)} %copy-done.34), channel_id=1, source_target_pairs={{0,6},{1,7},{2,4},{3,5},{4,2},{5,3},{6,0},{7,1},{8,14},{9,15},{10,... | collective-permute-start | bytes 737288 | tf_op jit(solution)/shard_map/ppermute | solution.py:445
  157.2 37.0 %copy-start.11 = (bf16[2,3,2,48,256]{4,3,2,1,0:T(8,128)(2,1)S(1)}, bf16[2,3,2,48,256]{4,3,2,1,0:T(8,128)(2,1)}, u32[]{:S(2)}) copy-start(bf16[2,3,2,48,256]{4,3,2,1,0:T(8,128)(2,1)} %get-tuple-element.62.refs_0_) | copy-start | bytes 884740
  166.1 23.2 %collective-permute-start.30 = (bf16[2,5,2,48,256]{4,3,2,1,0:T(8,128)(2,1)}, bf16[2,5,2,48,256]{4,3,2,1,0:T(8,128)(2,1)S(1)}, u32[]{:S(2)}, u32[]{:S(2)}) collective-permute-start(bf16[2,5,2,48,256]{4,3,2,1,0:T(8,128)(2,1)} %get-tuple-element.73.refs_0_), channel_id=1, source_target_pairs={{0,16},{8,24},{16,0},{24,8},{1,17},{9,25},{17,1},{25,9},{2,18},{10... | collective-permute-start | bytes 1474568 | tf_op jit(solution)/shard_map/ppermute | solution.py:401
  168.9 44.4 %collective-permute-start.31 = (bf16[2,5,2,48,256]{4,3,2,1,0:T(8,128)(2,1)}, bf16[2,5,2,48,256]{4,3,2,1,0:T(8,128)(2,1)S(1)}, u32[]{:S(2)}, u32[]{:S(2)}) collective-permute-start(bf16[2,5,2,48,256]{4,3,2,1,0:T(8,128)(2,1)} %get-tuple-element.73.refs_0_), channel_id=1, source_target_pairs={{8,16},{16,8},{9,17},{17,9},{10,18},{18,10},{11,19},{19,11},{12,20... | collective-permute-start | bytes 1474568 | tf_op jit(solution)/shard_map/ppermute | solution.py:403
  171.2 42.1 %collective-permute-start.29 = (bf16[2,5,2,48,256]{4,3,2,1,0:T(8,128)(2,1)}, bf16[2,5,2,48,256]{4,3,2,1,0:T(8,128)(2,1)S(1)}, u32[]{:S(2)}, u32[]{:S(2)}) collective-permute-start(bf16[2,5,2,48,256]{4,3,2,1,0:T(8,128)(2,1)} %get-tuple-element.73.refs_0_), channel_id=1, source_target_pairs={{0,8},{8,0},{16,24},{24,16},{1,9},{9,1},{17,25},{25,17},{2,10},{10... | collective-permute-start | bytes 1474568 | tf_op jit(solution)/shard_map/ppermute | solution.py:402
  189.2 24.2 %collective-permute-start.32 = (bf16[2,5,2,48,256]{4,3,2,1,0:T(8,128)(2,1)S(1)}, bf16[2,5,2,48,256]{4,3,2,1,0:T(8,128)(2,1)S(1)}, u32[]{:S(2)}, u32[]{:S(2)}) collective-permute-start(bf16[2,5,2,48,256]{4,3,2,1,0:T(8,128)(2,1)S(1)} %collective-permute-done.30.refs_2_), channel_id=1, source_target_pairs={{16,24},{8,0},{17,25},{9,1},{18,26},{10,2},{19,27},{11,3},{20,28},... | collective-permute-start | bytes 1474568 | tf_op jit(solution)/shard_map/ppermute | solution.py:404
  194.3 13.4 %collective-permute-start.33 = (bf16[2,3,2,48,256]{4,3,2,1,0:T(8,128)(2,1)S(1)}, bf16[2,3,2,48,256]{4,3,2,1,0:T(8,128)(2,1)S(1)}, u32[]{:S(2)}, u32[]{:S(2)}) collective-permute-start(bf16[2,3,2,48,256]{4,3,2,1,0:T(8,128)(2,1)S(1)} %copy-done.11), channel_id=1, source_target_pairs={{8,16},{16,8},{9,17},{17,9},{10,18},{18,10},{11,19},{19,11},{12,20... | collective-permute-start | bytes 884744 | tf_op jit(solution)/shard_map/ppermute | solution.py:403
  (27 other events, 215.4 us)

commit v5 on v4

--- a/solution.py
+++ b/solution.py
@@ -93,22 +93,20 @@
     planes = rows_in[0].shape[0]
     rows = (rows_in[0].shape[1] - ID_ROWS) // 2
     touch = touched.shape[1]
-    chips = len(blocks)
-    n_own = 2 * chips
-    half = blocks[0].shape[1]
+    n_own = blocks.shape[0]
+    half = sum(sizes)
     aligned = piece % 16 == 0
-    n_in = chips if aligned else 1
     n_out = n_own if aligned else 1
     starts = [sum(sizes[:i]) for i in range(len(sizes))]
 
     def body(pos_ref, touched_ref, slot_ref, *rest):
         row_refs = rest[:2]
-        block_refs = rest[2 : 2 + n_in]
-        rest = rest[2 + n_in :]
+        blocks_ref = rest[2]
+        rest = rest[3:]
         pred_refs = rest[:2]
         grad_refs = rest[2:-8]
         acc, id_cols, held, sorted_rows, pred, full_of, tasks, sems = rest[-8:]
-        dp_at, own_at = pos_ref[0], pos_ref[1]
+        own_at = pos_ref[1]
         core = lax.rem(own_at, 2)
 
         def sites(j):
@@ -121,15 +119,12 @@
         if aligned:
             block_copies = [
                 pltpu.make_async_copy(
-                    ref.at[u],
-                    held.at[:, :, sites(2 * q + u), :],
-                    sems.at[2 + 2 * q + u],
+                    blocks_ref.at[i], held.at[:, :, pl.ds(i * piece, piece), :], sems.at[2 + i]
                 )
-                for q, ref in enumerate(block_refs)
-                for u in range(2)
+                for i in range(n_own)
             ]
         else:
-            block_copies = [pltpu.make_async_copy(block_refs[0], held, sems.at[2])]
+            block_copies = [pltpu.make_async_copy(blocks_ref, held, sems.at[2])]
         for copy in row_copies + block_copies:
             copy.start()
 
@@ -150,7 +145,7 @@
             source = t // (touch + 1)
             j = t - source * (touch + 1)
             which = source // planes
-            device = (dp_at ^ (source - which * planes)) * n_own + (own_at ^ which)
+            device = (source - which * planes) * n_own + (own_at ^ which)
             full = full_of[source]
             insertion = jnp.where(j == 0, full, touched_ref[device, jnp.maximum(j - 1, 0)])
             e = slot_ref[insertion] - core * half
@@ -193,7 +188,7 @@
                 back_pre = (back_hidden * slopes).astype(jnp.bfloat16)
                 part = lax.dot_general(
                     hidden, read_out, (((1,), (1,)), ((), ())), preferred_element_type=jnp.float32
-                ).astype(jnp.bfloat16)
+                )
                 grad_in = lax.dot_general(
                     sig, back_pre, (((0,), (0,)), ((), ())), preferred_element_type=jnp.float32
                 )
@@ -223,7 +218,7 @@
 
                 lax.fori_loop(0, size, write, 0)
 
-    pred_shape = jax.ShapeDtypeStruct((planes, rows, SITES), jnp.bfloat16)
+    pred_shape = jax.ShapeDtypeStruct((planes, rows, SITES), jnp.float32)
     grad_shapes = [
         jax.ShapeDtypeStruct((size, 2, piece if aligned else SITES, width), jnp.bfloat16)
         for size in sizes
@@ -235,25 +230,23 @@
         pltpu.VMEM((2 * planes, rows, 128), jnp.float32),
         pltpu.VMEM((half, 2, SITES, width), jnp.bfloat16),
         pltpu.VMEM((2 * planes,) + rows_in[0].shape[1:], jnp.bfloat16),
-        pltpu.VMEM((2 * planes, rows, SITES), jnp.bfloat16),
+        pltpu.VMEM((2 * planes, rows, SITES), jnp.float32),
         pltpu.SMEM((2 * planes,), jnp.int32),
         pltpu.SMEM((4, most + 1), jnp.int32),
         pltpu.SemaphoreType.DMA((2 + n_own,)),
     ]
     own_at = pos[1]
     if not aligned:
-        order = own_at ^ jnp.arange(n_own, dtype=jnp.int32)
-        stacked = jnp.take(jnp.concatenate(blocks), order, axis=0)
-        blocks = [stacked.transpose(1, 2, 0, 3, 4).reshape(half, 2, SITES, width)]
+        blocks = blocks.transpose(1, 2, 0, 3, 4).reshape(half, 2, SITES, width)
     found = pl.pallas_call(
         body,
         out_shape=[pred_shape, pred_shape] + grad_shapes,
-        in_specs=[smem(), smem(), smem()] + [pl.BlockSpec(memory_space=pl.ANY)] * (2 + n_in),
+        in_specs=[smem(), smem(), smem()] + [pl.BlockSpec(memory_space=pl.ANY)] * 3,
         out_specs=[vmem()] * (2 + len(grad_shapes)),
         scratch_shapes=scratch,
         compiler_params=params(),
         name="local_grads",
-    )(pos, touched, slot_map, *rows_in, *blocks)
+    )(pos, touched, slot_map, *rows_in, blocks)
     grads = []
     for chunk in range(len(sizes)):
         outs = list(found[2 + chunk * n_out : 2 + (chunk + 1) * n_out])
@@ -277,67 +270,87 @@
     def body(pos_ref, *refs):
         grad_refs = refs[:n_own]
         w_ref, m1_ref, m2_ref = refs[n_own : n_own + 3]
-        new_w, new_m1, new_m2 = refs[-3:]
-
-        def step(chosen):
-            gradient = chosen[0][...].astype(jnp.float32)
-            for ref in chosen[1:]:
-                gradient = gradient + ref[...].astype(jnp.float32)
-            one = 0.9 * m1_ref[...] + 0.1 * gradient
-            two = 0.999 * m2_ref[...] + 0.001 * gradient * gradient
-            new_m1[...] = one
-            new_m2[...] = two
-            spread = two * (1.0 / correct_two)
-            updated = w_ref[...].astype(jnp.float32) - one * (learn_rate / correct_one) / (
-                spread * lax.rsqrt(spread) + 1e-08
+        new_w, new_m1, new_m2 = refs[n_own + 3 + len(before) : n_own + 6 + len(before)]
+        grads, w_in, m1_in, m2_in, w_out, m1_out, m2_out, sem_in, sem_grad, sem_out = refs[
+            n_own + 6 + len(before) :
+        ]
+        core = lax.rem(pos_ref[1], 2)
+        columns = pl.ds(pl.multiple_of(pos_ref[0] * width, 128), width)
+
+        def block_rows(g):
+            return pl.ds((core ^ g) * half + start, size)
+
+        copies = []
+        for g in range(2):
+            copies.append(
+                [
+                    pltpu.make_async_copy(
+                        w_ref.at[block_rows(g), :, :, columns], w_in.at[g], sem_in.at[g, 0]
+                    ),
+                    pltpu.make_async_copy(m1_ref.at[block_rows(g)], m1_in.at[g], sem_in.at[g, 1]),
+                    pltpu.make_async_copy(m2_ref.at[block_rows(g)], m2_in.at[g], sem_in.at[g, 2]),
+                ]
+                + [
+                    pltpu.make_async_copy(grad_refs[j], grads.at[j], sem_grad.at[j])
+                    for j in range(g, n_own, 2)
+                ]
             )
-            new_w[0] = updated.astype(jnp.bfloat16)
-
-        pl.when(pl.program_id(0) == 0)(lambda: step(grad_refs[0::2]))
-        pl.when(pl.program_id(0) == 1)(lambda: step(grad_refs[1::2]))
-
-    def which(g, pos_ref):
-        return lax.rem(pos_ref[1] + g, 2)
-
-    per = math.gcd(size, start) if start else size
-    per = math.gcd(per, half)
-
-    def place(g, i, pos_ref):
-        return (which(g, pos_ref) * (half // per) + start // per + i, 0, 0, 0)
-
-    small = pl.BlockSpec((per, 2, piece, width), place)
-    grad = pl.BlockSpec((per, 2, piece, width), lambda g, i, pos_ref: (i, 0, 0, 0))
+            for copy in copies[g]:
+                copy.start()
+        outs = []
+        for g in range(2):
+            for copy in copies[g]:
+                copy.wait()
+
+            def step(i, _, g=g):
+                gradient = grads[g, i].astype(jnp.float32)
+                for j in range(g + 2, n_own, 2):
+                    gradient = gradient + grads[j, i].astype(jnp.float32)
+                one = 0.9 * m1_in[g, i] + 0.1 * gradient
+                two = 0.999 * m2_in[g, i] + 0.001 * gradient * gradient
+                m1_out[g, i] = one
+                m2_out[g, i] = two
+                spread = two * (1.0 / correct_two)
+                updated = w_in[g, i].astype(jnp.float32) - one * (learn_rate / correct_one) / (
+                    spread * lax.rsqrt(spread) + 1e-08
+                )
+                w_out[g, i] = updated.astype(jnp.bfloat16)
+                return 0
+
+            lax.fori_loop(0, size, step, 0)
+            outs += [
+                pltpu.make_async_copy(w_out.at[g], new_w.at[core ^ g], sem_out.at[g, 0]),
+                pltpu.make_async_copy(m1_out.at[g], new_m1.at[block_rows(g)], sem_out.at[g, 1]),
+                pltpu.make_async_copy(m2_out.at[g], new_m2.at[block_rows(g)], sem_out.at[g, 2]),
+            ]
+            for copy in outs[-3:]:
+                copy.start()
+        for copy in outs:
+            copy.wait()
+
     anywhere = pl.BlockSpec(memory_space=pl.ANY)
-    grid_spec = pltpu.PrefetchScalarGridSpec(
-        num_scalar_prefetch=1,
-        grid=(2, size // per),
-        in_specs=[grad] * n_own
-        + [
-            pl.BlockSpec(
-                (per, 2, piece, width),
-                lambda g, i, pos_ref: place(g, i, pos_ref)[:3] + (pos_ref[0],),
-            ),
-            small,
-            small,
-        ]
-        + [anywhere] * len(before),
-        out_specs=[
-            pl.BlockSpec(
-                (1, per, 2, piece, width),
-                lambda g, i, pos_ref: (which(g, pos_ref), i, 0, 0, 0),
-            ),
-            small,
-            small,
-        ],
-    )
+    blocks = (2, size, 2, piece, width)
     return pl.pallas_call(
         body,
         out_shape=[
-            jax.ShapeDtypeStruct((2, size, 2, piece, width), jnp.bfloat16),
+            jax.ShapeDtypeStruct(blocks, jnp.bfloat16),
             jax.ShapeDtypeStruct(moment1.shape, jnp.float32),
             jax.ShapeDtypeStruct(moment1.shape, jnp.float32),
         ],
-        grid_spec=grid_spec,
+        in_specs=[smem()] + [anywhere] * (n_own + 3 + len(before)),
+        out_specs=[anywhere] * 3,
+        scratch_shapes=[
+            pltpu.VMEM((n_own,) + blocks[1:], jnp.bfloat16),
+            pltpu.VMEM(blocks, jnp.bfloat16),
+            pltpu.VMEM(blocks, jnp.float32),
+            pltpu.VMEM(blocks, jnp.float32),
+            pltpu.VMEM(blocks, jnp.bfloat16),
+            pltpu.VMEM(blocks, jnp.float32),
+            pltpu.VMEM(blocks, jnp.float32),
+            pltpu.SemaphoreType.DMA((2, 3)),
+            pltpu.SemaphoreType.DMA((n_own,)),
+            pltpu.SemaphoreType.DMA((2, 3)),
+        ],
         input_output_aliases={1 + n_own + 3 + i: 1 + i for i in range(len(before))},
         compiler_params=params(),
         name="adam_step",
@@ -347,7 +360,6 @@
 def place_weights(pos, pieces, start, half, before):
     n_dp = len(pieces)
     _, size, _, piece, width = pieces[0].shape
-    per = math.gcd(math.gcd(size, start), half)
     pieces = list(pieces)
     far = isinstance(pieces[-1], tuple)
     if far:
@@ -355,33 +367,49 @@
     n_in = len(pieces)
 
     def body(pos_ref, *refs):
-        out_ref = refs[-1]
-        for k in range(n_dp):
-
-            @pl.when(pos_ref[0] == k)
-            def _(k=k):
-                for j in range(n_dp):
-                    first = (k ^ j) * width
-                    i = n_dp if far and j == n_dp - 1 and k in (0, n_dp - 1) else j
-                    out_ref[:, :, :, first : first + width] = refs[i][0]
-
-    def place(h, i, pos_ref):
-        return (h * (half // per) + start // per + i, 0, 0, 0)
-
-    grid_spec = pltpu.PrefetchScalarGridSpec(
-        num_scalar_prefetch=1,
-        grid=(2, size // per),
-        in_specs=[
-            pl.BlockSpec((1, per, 2, piece, width), lambda h, i, pos_ref: (h, i, 0, 0, 0))
+        out_ref, held, sems, sem_out = refs[-4:]
+        dp_at = pos_ref[0]
+        inner = (dp_at > 0) & (dp_at < n_dp - 1)
+
+        def each(act):
+            for j in range(n_dp):
+                columns = pl.ds(pl.multiple_of((dp_at ^ j) * width, 128), width)
+
+                def copy(i, j=j, columns=columns):
+                    return pltpu.make_async_copy(
+                        refs[i], held.at[:, :, :, :, columns], sems.at[j]
+                    )
+
+                if far and j == n_dp - 1:
+                    pl.when(inner)(lambda: act(copy(j)))
+                    pl.when(~inner)(lambda: act(copy(j + 1)))
+                else:
+                    act(copy(j))
+
+        each(lambda copy: copy.start())
+        each(lambda copy: copy.wait())
+        outs = [
+            pltpu.make_async_copy(
+                held.at[h], out_ref.at[pl.ds(h * half + start, size)], sem_out.at[h]
+            )
+            for h in range(2)
         ]
-        * n_in
-        + [pl.BlockSpec(memory_space=pl.ANY)] * len(before),
-        out_specs=pl.BlockSpec((per, 2, piece, n_dp * width), place),
-    )
+        for copy in outs:
+            copy.start()
+        for copy in outs:
+            copy.wait()
+
+    anywhere = pl.BlockSpec(memory_space=pl.ANY)
     return pl.pallas_call(
         body,
         out_shape=jax.ShapeDtypeStruct((2 * half, 2, piece, n_dp * width), jnp.bfloat16),
-        grid_spec=grid_spec,
+        in_specs=[smem()] + [anywhere] * (n_in + len(before)),
+        out_specs=anywhere,
+        scratch_shapes=[
+            pltpu.VMEM((2, size, 2, piece, n_dp * width), jnp.bfloat16),
+            pltpu.SemaphoreType.DMA((n_dp,)),
+            pltpu.SemaphoreType.DMA((2,)),
+        ],
         input_output_aliases={1 + n_in: 0} if before else {},
         compiler_params=params(),
         name="place_weights",
@@ -405,26 +433,23 @@
     return [fresh, one, two, (middle, outer)]
 
 
-def finish_predicted(perm, parts):
-    def body(perm_ref, *refs):
-        total = refs[0][...].astype(jnp.float32)
-        for ref in refs[1:-1]:
-            total = total + ref[...].astype(jnp.float32)
-        refs[-1][...] = lax.dot_general(
+def finish_predicted(perm, total):
+    def body(perm_ref, total_ref, out_ref):
+        out_ref[...] = lax.dot_general(
             perm_ref[...],
-            total.astype(jnp.bfloat16),
+            total_ref[...].astype(jnp.bfloat16),
             (((0,), (0,)), ((), ())),
             preferred_element_type=jnp.float32,
         ).astype(jnp.bfloat16)
 
     return pl.pallas_call(
         body,
-        out_shape=jax.ShapeDtypeStruct(parts[0].shape, jnp.bfloat16),
-        in_specs=[vmem()] * (1 + len(parts)),
+        out_shape=jax.ShapeDtypeStruct(total.shape, jnp.bfloat16),
+        in_specs=[vmem(), vmem()],
         out_specs=vmem(),
         compiler_params=params(),
         name="finish_predicted",
-    )(perm, *parts)
+    )(perm, total)
 
 
 def shards(signals, cotangent, row_insertion, touched, slot_map, weights, moment1, moment2):
@@ -444,47 +469,44 @@
     def across(value, j):
         return lax.ppermute(value, "own", [(o, o ^ j) for o in range(n_own)])
 
-    def column(which):
-        return lax.dynamic_slice(
-            weights, (which * half, 0, 0, dp_at * width), (half, 2, piece, width)
-        )
-
     packed, perm = pack_rows(row_insertion.reshape(1, rows), signals, cotangent)
-    def between(value, j):
-        return lax.ppermute(value, "dp", [(d, d ^ j) for d in range(n_dp)])
-
-    planes = jnp.stack([packed] + [between(packed, j) for j in range(1, n_dp)])
-
-    paired = jnp.stack([column(core), across(column(1 - core), 1)])
-    blocks = [paired] + [across(paired, 2 * q) for q in range(1, n_own // 2)]
-    rows_in = (planes, across(after(planes, *blocks[1:]), 1))
-
+    planes = lax.all_gather(packed, "dp", axis=0)
+
+    column = lax.dynamic_slice_in_dim(weights, dp_at * width, width, 3)
+    outgoing = jnp.broadcast_to(
+        column.reshape(1, 2, half, 2, piece, width), (n_own // 2, 2, half, 2, piece, width)
+    ).reshape(n_own, half, 2, piece, width)
+    blocks = lax.all_to_all(outgoing, "own", split_axis=0, concat_axis=0, tiled=True)
+
+    rows_in = (planes, across(planes, 1))
     pred_mine, pred_other, grads = local_grads(
         pos, touched, slot_map, rows_in, blocks, sizes, piece, width
     )
     pred_part = pred_mine + across(pred_other, 1)
-    parts = [pred_part[0]] + [between(pred_part[j], j) for j in range(1, n_dp)]
+    total = lax.psum_scatter(pred_part, "dp", scatter_dimension=0)
+
+    arrived = []
+    for chunk in grads:
+        for j in range(1, n_own if arrived else 1):
+            chunk[j] = after(chunk[j], arrived[-1][j])
+        arrived.append([chunk[0]] + [across(chunk[j], j) for j in range(1, n_own)])
+    ready = [list(one) for one in arrived]
+    ready[0][-1] = after(ready[0][-1], pred_part, *arrived[-1][1 : n_own // 2])
 
     moments = []
     new_weights = []
-    pieces = None
     start = 0
-    for size, chunk in zip(sizes, grads):
-        if pieces:
-            last = pieces[-1][-1] if isinstance(pieces[-1], tuple) else pieces[-1]
-            moving = parts[1:4] + [fresh, fresh, pieces[2], pieces[1]]
-            for j in range(1, n_own):
-                chunk[j] = after(chunk[j], moving[min(j, len(moving)) - 1])
-        arrived = [chunk[0]] + [across(chunk[j], j) for j in range(1, n_own)]
-        arrived[-1] = after(arrived[-1], last if pieces else pred_part)
-        fresh, *moments = adam(pos, arrived, weights, moment1, moment2, start, moments)
+    for size, chunk in zip(sizes, ready):
+        if start:
+            chunk[-1] = after(chunk[-1], *jax.tree.leaves(pieces[1:]))
+        fresh, *moments = adam(pos, chunk, weights, moment1, moment2, start, moments)
         pieces = gather_planes(fresh, dp_at, n_dp)
         new_weights = [place_weights(pos, pieces, start, half, new_weights)]
         start += size
     new_weights = new_weights[0]
     new_moment1, new_moment2 = moments
 
-    predicted = finish_predicted(perm, parts)
+    predicted = finish_predicted(perm, total)
     return (predicted, new_weights, new_moment1, new_moment2)
 
 

time: 224 us -> 210 us (0.938)
  the two profiles are of different devices: /device:TPU:10 before, /device:TPU:2 now
where the time goes in v5:
time: 210 us; the launch traced here: 209 us
  waiting for transfers between devices  114 us (54%)
  Pallas kernels  35.7 us (17%)
  starting transfers between devices  33.6 us (16%)
  between operations  14.4 us (7%)
  local copies, waits for them, and re-layouts  7.8 us (4%)
  other arithmetic  3.47 us (2%)
    all_gather x1, waiting for transfers between devices, shards(): planes = lax.all_gather(packed, 'dp', axis=0)  32 us
    ppermute x16, waiting for transfers between devices, across(): return lax.ppermute(value, 'own', [(o, o ^ j) for o in range(n_own)])  31.2 us
    ppermute x2, waiting for transfers between devices, gather_planes(): two = lax.ppermute(fresh, 'dp', [(0, 2), (1, 3), (2, 0), (3, 1)])  30.2 us
    ppermute x2, waiting for transfers between devices, gather_planes(): outer = lax.ppermute(two, 'dp', [(2, 3), (1, 0)])  17.9 us
    pallas_call x1, Pallas kernels, local_grads(): pl.pallas_call(body, out_shape=[pred_shape, pred_shape] + grad_shapes, in...  16.4 us
    ppermute x16, starting transfers between devices, across(): return lax.ppermute(value, 'own', [(o, o ^ j) for o in range(n_own)])  13.3 us
    pallas_call x2, Pallas kernels, adam(): pl.pallas_call(body, out_shape=[jax.ShapeDtypeStruct(blocks, jnp.bfloat16...  8.49 us
    ppermute x2, starting transfers between devices, gather_planes(): two = lax.ppermute(fresh, 'dp', [(0, 2), (1, 3), (2, 0), (3, 1)])  7.3 us
  transfers between devices with their start and end apart: 27, of which 15 were waited for; matrix products, arithmetic and copies ran while one was open for 2% of the time, Pallas kernels for 7%

profile of v5, /device:TPU:2, one launch (start us, length us, event | category | flops | bytes accessed | tf_op | source)
XLA Modules:
  0.0 209.3 jit_solution(12106633897604166377)
XLA Ops:
  7.2 2.4 %pack_rows.1 = (bf16[528,384]{1,0:T(8,128)(2,1)}, bf16[256,256]{1,0:T(8,128)(2,1)}) custom-call(s32[1,256]{1,0:T(1,128)} %bitcast.12, bf16[256,384]{1,0:T(8,128)(2,1)} %sig_ref.1, bf16[256,384]{1,0:T(8,128)(2,1)} %cot_ref.1), custom_call_target="tpu_custom_call" | custom-call | tf_op jit(solution)/shard_map/pack_rows/pallas_call | solution.py:79
  9.6 1.2 constant_dynamic-slice_fusion
  10.8 2.0 broadcast_in_dim.8
  12.9 4.4 %all-to-all-start = ((bf16[8,8,2,48,256]{4,3,2,1,0:T(8,128)(2,1)}), bf16[8,8,2,48,256]{4,3,2,1,0:T(8,128)(2,1)S(1)}, u32[]{:S(2)}, u32[]{:S(2)}) async-start(bf16[8,8,2,48,256]{4,3,2,1,0:T(8,128)(2,1)} %bitcast.7), calls=%async_computation | async-start | bytes 6291456 | tf_op jit(solution)/shard_map/all_to_all | solution.py:479
  17.3 32.0 %all-gather.3.cloned.1.call-done = bf16[2112,384]{1,0:T(8,128)(2,1)} async-done(((bf16[528,384]{1,0:T(8,128)(2,1)}), bf16[2112,384]{1,0:T(8,128)(2,1)}) %all-gather.3.cloned.1.call-update) | async-done | bytes 1622032 | tf_op jit(solution)/shard_map/all_gather | solution.py:473
  49.3 0.7 copy.15.touched_ref
  50.0 0.6 pad_add_fusion.pos_ref
  50.6 3.0 %all-to-all-done.rest_2_ = bf16[8,8,2,48,256]{4,3,2,1,0:T(8,128)(2,1)S(1)} async-done(((bf16[8,8,2,48,256]{4,3,2,1,0:T(8,128)(2,1)}), bf16[8,8,2,48,256]{4,3,2,1,0:T(8,128)(2,1)S(1)}, u32[]{:S(2)}, u32[]{:S(2)}) %all-to-all-start) | async-done | bytes 3145760 | tf_op jit(solution)/shard_map/all_to_all | solution.py:479
  53.7 1.7 copy-done
  55.3 16.4 %local_grads.1 = (f32[4,256,384]{2,1,0:T(8,128)}, f32[4,256,384]{2,1,0:T(8,128)}, bf16[3,2,48,256]{3,2,1,0:T(8,128)(2,1)}, bf16[3,2,48,256]{3,2,1,0:T(8,128)(2,1...) custom-call(s32[2]{0:T(128)} %pad_add_fusion.pos_ref, ...), custom_call_target="tpu_custom_call" | custom-call | tf_op jit(solution)/shard_map/local_grads/pallas_call | solution.py:241
  71.8 3.6 %collective-permute-done.1 = f32[4,256,384]{2,1,0:T(8,128)S(1)} collective-permute-done((f32[4,256,384]{2,1,0:T(8,128)}, f32[4,256,384]{2,1,0:T(8,128)S(1)}, u32[]{:S(2)}, u32[]{:S(2)}) %collective-permute-start.1) | collective-permute-done | bytes 1572896 | tf_op jit(solution)/shard_map/ppermute | solution.py:470
  75.4 2.8 %add.9 = f32[4,256,384]{2,1,0:T(8,128)} add(f32[4,256,384]{2,1,0:T(8,128)} %get-tuple-element.41, f32[4,256,384]{2,1,0:T(8,128)S(1)} %collective-permute-done.1) | non-fusion elementwise | flops 393216 | bytes 4718592 | tf_op jit(solution)/shard_map/add | solution.py:485
  78.3 1.3 collective-permute-start.6
  80.0 0.6 collective-permute-start.4
  80.6 3.6 %collective-permute-done.6.refs_3_ = bf16[3,2,48,256]{3,2,1,0:T(8,128)(2,1)S(1)} collective-permute-done((bf16[3,2,48,256]{3,2,1,0:T(8,128)(2,1)S(1)}, bf16[3,2,48,256]{3,2,1,0:T(8,128)(2,1)S(1)}, u32[]{:S(2)}, u32[]{:S(2)}) %collective-permute-start.6) | collective-permute-done | bytes 147488 | tf_op jit(solution)/shard_map/ppermute | solution.py:470
  84.2 1.5 collective-permute-start.7
  85.8 2.1 collective-permute-start.14
  88.0 1.5 collective-permute-start.5
  89.5 1.1 collective-permute-start.8
  90.6 7.2 %collective-permute-done.14.refs_7_ = bf16[3,2,48,256]{3,2,1,0:T(8,128)(2,1)S(1)} collective-permute-done((bf16[3,2,48,256]{3,2,1,0:T(8,128)(2,1)S(1)}, bf16[3,2,48,256]{3,2,1,0:T(8,128)(2,1)S(1)}, u32[]{:S(2)}, u32[]{:S(2)}) %collective-permute-start.14) | collective-permute-done | bytes 147488 | tf_op jit(solution)/shard_map/ppermute | solution.py:470
  97.8 1.9 collective-permute-start.12
  99.7 1.7 collective-permute-done.5.refs_2_
  101.5 3.6 %collective-permute-done.10.refs_5_ = bf16[3,2,48,256]{3,2,1,0:T(8,128)(2,1)S(1)} collective-permute-done((bf16[3,2,48,256]{3,2,1,0:T(8,128)(2,1)S(1)}, bf16[3,2,48,256]{3,2,1,0:T(8,128)(2,1)S(1)}, u32[]{:S(2)}, u32[]{:S(2)}) %collective-permute-start.10) | collective-permute-done | bytes 147488 | tf_op jit(solution)/shard_map/ppermute | solution.py:470
  105.1 1.5 collective-permute-done.12.refs_6_
  106.6 0.6 copy-done.22
  107.3 3.9 %adam_step.2 = (bf16[2,3,2,48,256]{4,3,2,1,0:T(8,128)(2,1)}, f32[16,2,48,256]{3,2,1,0:T(8,128)}, f32[16,2,48,256]{3,2,1,0:T(8,128)}) custom-call(s32[2]{0:T(128)} %pad_add_fusion.pos_ref, bf16[3,2,48,256]{3,2,1,0:T(8,128)(2,1)} %get-tuple-element.65.refs_0_, bf16[3,2,48,256]{3,2,1,0:T(8,128)(2,1)} %copy-done.17, bf16[3,2,48,256]{3,2,1,0:T(8,128)(2,1)} %copy-done.18, ...), custom_call_target="tpu_custom_call" | custom-call | tf_op jit(solution)/shard_map/adam_step/pallas_call | solution.py:333
  111.2 2.7 %collective-permute-start.17 = (bf16[2,3,2,48,256]{4,3,2,1,0:T(8,128)(2,1)}, bf16[2,3,2,48,256]{4,3,2,1,0:T(8,128)(2,1)S(1)}, u32[]{:S(2)}, u32[]{:S(2)}) collective-permute-start(bf16[2,3,2,48,256]{4,3,2,1,0:T(8,128)(2,1)} %get-tuple-element.67.refs_0_), channel_id=1, source_target_pairs={{0,16},{8,24},{16,0},{24,8},{1,17},{9,25},{17,1},{25,9},{2,18},{10... | collective-permute-start | bytes 884744 | tf_op jit(solution)/shard_map/ppermute | solution.py:429
  113.8 0.7 collective-permute-start.18
  114.5 0.8 collective-permute-start.15
  115.3 2.8 %collective-permute-start.16 = (bf16[2,3,2,48,256]{4,3,2,1,0:T(8,128)(2,1)}, bf16[2,3,2,48,256]{4,3,2,1,0:T(8,128)(2,1)S(1)}, u32[]{:S(2)}, u32[]{:S(2)}) collective-permute-start(bf16[2,3,2,48,256]{4,3,2,1,0:T(8,128)(2,1)} %get-tuple-element.67.refs_0_), channel_id=1, source_target_pairs={{0,8},{8,0},{16,24},{24,16},{1,9},{9,1},{17,25},{25,17},{2,10},{10... | collective-permute-start | bytes 884744 | tf_op jit(solution)/shard_map/ppermute | solution.py:430
  118.1 10.5 %collective-permute-done.17.refs_2_ = bf16[2,3,2,48,256]{4,3,2,1,0:T(8,128)(2,1)S(1)} collective-permute-done((bf16[2,3,2,48,256]{4,3,2,1,0:T(8,128)(2,1)}, bf16[2,3,2,48,256]{4,3,2,1,0:T(8,128)(2,1)S(1)}, u32[]{:S(2)}, u32[]{:S(2)}) %collective-permute-start.17) | collective-permute-done | bytes 294944 | tf_op jit(solution)/shard_map/ppermute | solution.py:429
  128.6 1.3 collective-permute-start.19
  130.7 1.2 collective-permute-start.9
  131.9 7.2 %collective-permute-done.19.refs_4_ = bf16[2,3,2,48,256]{4,3,2,1,0:T(8,128)(2,1)S(1)} collective-permute-done((bf16[2,3,2,48,256]{4,3,2,1,0:T(8,128)(2,1)S(1)}, bf16[2,3,2,48,256]{4,3,2,1,0:T(8,128)(2,1)S(1)}, u32[]{:S(2)}, u32[]{:S(2)}) %collective-permute-start.19) | collective-permute-done | bytes 294944 | tf_op jit(solution)/shard_map/ppermute | solution.py:432
  139.2 4.6 %collective-permute-done.11.refs_5_ = bf16[5,2,48,256]{3,2,1,0:T(8,128)(2,1)S(1)} collective-permute-done((bf16[5,2,48,256]{3,2,1,0:T(8,128)(2,1)S(1)}, bf16[5,2,48,256]{3,2,1,0:T(8,128)(2,1)S(1)}, u32[]{:S(2)}, u32[]{:S(2)}) %collective-permute-start.11) | collective-permute-done | bytes 245792 | tf_op jit(solution)/shard_map/ppermute | solution.py:470
  143.8 5.2 %collective-permute-done.9.refs_4_ = bf16[5,2,48,256]{3,2,1,0:T(8,128)(2,1)S(1)} collective-permute-done((bf16[5,2,48,256]{3,2,1,0:T(8,128)(2,1)S(1)}, bf16[5,2,48,256]{3,2,1,0:T(8,128)(2,1)S(1)}, u32[]{:S(2)}, u32[]{:S(2)}) %collective-permute-start.9) | collective-permute-done | bytes 245792 | tf_op jit(solution)/shard_map/ppermute | solution.py:470
  149.0 0.7 copy-done.15
  149.7 4.6 %adam_step.3 = (bf16[2,5,2,48,256]{4,3,2,1,0:T(8,128)(2,1)}, f32[16,2,48,256]{3,2,1,0:T(8,128)}, f32[16,2,48,256]{3,2,1,0:T(8,128)}) custom-call(s32[2]{0:T(128)} %pad_add_fusion.pos_ref, bf16[5,2,48,256]{3,2,1,0:T(8,128)(2,1)} %get-tuple-element.43.refs_0_, bf16[5,2,48,256]{3,2,1,0:T(8,128)(2,1)} %copy-done.11, ...), custom_call_target="tpu_custom_call", output_to_operand_aliasing={{1}: (12, {}), {2}: (13, {})} | custom-call | tf_op jit(solution)/shard_map/adam_step/pallas_call | solution.py:333
  154.4 4.6 %collective-permute-start.21 = (bf16[2,5,2,48,256]{4,3,2,1,0:T(8,128)(2,1)}, bf16[2,5,2,48,256]{4,3,2,1,0:T(8,128)(2,1)S(1)}, u32[]{:S(2)}, u32[]{:S(2)}) collective-permute-start(bf16[2,5,2,48,256]{4,3,2,1,0:T(8,128)(2,1)} %get-tuple-element.71.refs_0_), channel_id=1, source_target_pairs={{0,16},{8,24},{16,0},{24,8},{1,17},{9,25},{17,1},{25,9},{2,18},{10... | collective-permute-start | bytes 1474568 | tf_op jit(solution)/shard_map/ppermute | solution.py:429
  159.0 0.7 collective-permute-start.22
  159.7 1.9 collective-permute-start.20
  161.5 19.7 %collective-permute-done.21.refs_2_ = bf16[2,5,2,48,256]{4,3,2,1,0:T(8,128)(2,1)S(1)} collective-permute-done((bf16[2,5,2,48,256]{4,3,2,1,0:T(8,128)(2,1)}, bf16[2,5,2,48,256]{4,3,2,1,0:T(8,128)(2,1)S(1)}, u32[]{:S(2)}, u32[]{:S(2)}) %collective-permute-start.21) | collective-permute-done | bytes 491552 | tf_op jit(solution)/shard_map/ppermute | solution.py:429
  181.2 1.3 collective-permute-start.23
  182.5 3.0 %place_weights.2.refs_5_ = bf16[16,2,48,1024]{3,2,1,0:T(8,128)(2,1)} custom-call(s32[2]{0:T(128)} %pad_add_fusion.pos_ref, bf16[2,3,2,48,256]{4,3,2,1,0:T(8,128)(2,1)} %get-tuple-element.67.refs_0_, bf16[2,3,2,48,256]{4,3,2,1,0:T(8,128)(2,1)} %copy-done.7, bf16[2,3,2,48,256]{4,3,2,1,0:T(8,128)(2,1)} %copy-done.5, bf16[2,3,2,48,256]{4,3,2,1,0:T(8,128)(2,1)} %copy-done.6, ...), custom_call_target="tpu_custom_call" | custom-call | tf_op jit(solution)/shard_map/place_weights/pallas_call | solution.py:403
  185.5 10.7 %collective-permute-done.23.refs_4_ = bf16[2,5,2,48,256]{4,3,2,1,0:T(8,128)(2,1)S(1)} collective-permute-done((bf16[2,5,2,48,256]{4,3,2,1,0:T(8,128)(2,1)S(1)}, bf16[2,5,2,48,256]{4,3,2,1,0:T(8,128)(2,1)S(1)}, u32[]{:S(2)}, u32[]{:S(2)}) %collective-permute-start.23) | collective-permute-done | bytes 491552 | tf_op jit(solution)/shard_map/ppermute | solution.py:432
  196.2 0.8 copy-done.4
  197.0 3.5 %place_weights.3 = bf16[16,2,48,1024]{3,2,1,0:T(8,128)(2,1)} custom-call(s32[2]{0:T(128)} %pad_add_fusion.pos_ref, bf16[2,5,2,48,256]{4,3,2,1,0:T(8,128)(2,1)} %get-tuple-element.71.refs_0_, bf16[2,5,2,48,256]{4,3,2,1,0:T(8,128)(2,1)} %copy-done.3, bf16[2,5,2,48,256]{4,3,2,1,0:T(8,128)(2,1)} %copy-done.1, ...), custom_call_target="tpu_custom_call", output_to_operand_aliasing={{}: (6, {})} | custom-call | tf_op jit(solution)/shard_map/place_weights/pallas_call | solution.py:403
  200.5 2.0 finish_predicted.1
  (96 shorter events, 1.6 us)
Async XLA Ops:
  7.2 42.1 %all-gather.3.cloned.1.call-start = ((), (), s32[]{:S(2)}) async-start(), calls=%async_computation.3 | async-start | bytes 2027520 | tf_op jit(solution)/shard_map/all_gather | solution.py:473
  12.9 36.4 %copy-start.23 = (s32[32,4]{0,1:T(4,128)S(1)}, s32[32,4]{0,1:T(4,128)}, u32[]{:S(2)}) copy-start(s32[32,4]{0,1:T(4,128)} %param.11) | copy-start | bytes 1540
  12.9 40.8 %all-to-all-start = ((bf16[8,8,2,48,256]{4,3,2,1,0:T(8,128)(2,1)}), bf16[8,8,2,48,256]{4,3,2,1,0:T(8,128)(2,1)S(1)}, u32[]{:S(2)}, u32[]{:S(2)}) async-start(bf16[8,8,2,48,256]{4,3,2,1,0:T(8,128)(2,1)} %bitcast.7), calls=%async_computation | async-start | bytes 6291456 | tf_op jit(solution)/shard_map/all_to_all | solution.py:479
  17.3 183.2 %reduce-scatter.2.cloned.1.call-start = ((), (), s32[]{:S(2)}) async-start(), calls=%async_computation.2 | async-start | bytes 1966080 | tf_op jit(solution)/shard_map/reduce_scatter | solution.py:486
  49.3 4.3 %collective-permute-start = (bf16[4,528,384]{2,1,0:T(8,128)(2,1)}, bf16[4,528,384]{2,1,0:T(8,128)(2,1)}, u32[]{:S(2)}, u32[]{:S(2)}) collective-permute-start(bf16[4,528,384]{2,1,0:T(8,128)(2,1)} %bitcast.9), channel_id=1, source_target_pairs={{0,1},{1,0},{2,3},{3,2},{4,5},{5,4},{6,7},{7,6},{8,9},{9,8},{10,11... | collective-permute-start | bytes 4866056 | tf_op jit(solution)/shard_map/ppermute | solution.py:470
  71.7 3.7 %collective-permute-start.1 = (f32[4,256,384]{2,1,0:T(8,128)}, f32[4,256,384]{2,1,0:T(8,128)S(1)}, u32[]{:S(2)}, u32[]{:S(2)}) collective-permute-start(f32[4,256,384]{2,1,0:T(8,128)} %get-tuple-element.42), channel_id=1, source_target_pairs={{0,1},{1,0},{2,3},{3,2},{4,5},{5,4},{6,7},{7,6},{8,9},{9,8},{10,11... | collective-permute-start | bytes 4718600 | tf_op jit(solution)/shard_map/ppermute | solution.py:470
  78.2 9.8 %copy-start.29 = (bf16[5,2,48,256]{3,2,1,0:T(8,128)(2,1)S(1)}, bf16[5,2,48,256]{3,2,1,0:T(8,128)(2,1)}, u32[]{:S(2)}) copy-start(bf16[5,2,48,256]{3,2,1,0:T(8,128)(2,1)} %get-tuple-element.49) | copy-start | bytes 737284
  78.2 11.3 %copy-start.28 = (bf16[5,2,48,256]{3,2,1,0:T(8,128)(2,1)S(1)}, bf16[5,2,48,256]{3,2,1,0:T(8,128)(2,1)}, u32[]{:S(2)}) copy-start(bf16[5,2,48,256]{3,2,1,0:T(8,128)(2,1)} %get-tuple-element.46) | copy-start | bytes 737284
  78.3 11.3 %copy-start.33 = (bf16[3,2,48,256]{3,2,1,0:T(8,128)(2,1)S(1)}, bf16[3,2,48,256]{3,2,1,0:T(8,128)(2,1)}, u32[]{:S(2)}) copy-start(bf16[3,2,48,256]{3,2,1,0:T(8,128)(2,1)} %get-tuple-element.54) | copy-start | bytes 442372
  78.3 19.5 %copy-start.32 = (bf16[3,2,48,256]{3,2,1,0:T(8,128)(2,1)S(1)}, bf16[3,2,48,256]{3,2,1,0:T(8,128)(2,1)}, u32[]{:S(2)}) copy-start(bf16[3,2,48,256]{3,2,1,0:T(8,128)(2,1)} %get-tuple-element.57) | copy-start | bytes 442372
  78.3 19.5 %copy-start.31 = (bf16[3,2,48,256]{3,2,1,0:T(8,128)(2,1)S(1)}, bf16[3,2,48,256]{3,2,1,0:T(8,128)(2,1)}, u32[]{:S(2)}) copy-start(bf16[3,2,48,256]{3,2,1,0:T(8,128)(2,1)} %get-tuple-element.60) | copy-start | bytes 442372
  78.3 5.9 %collective-permute-start.6 = (bf16[3,2,48,256]{3,2,1,0:T(8,128)(2,1)S(1)}, bf16[3,2,48,256]{3,2,1,0:T(8,128)(2,1)S(1)}, u32[]{:S(2)}, u32[]{:S(2)}) collective-permute-start(bf16[3,2,48,256]{3,2,1,0:T(8,128)(2,1)S(1)} %copy-done.37), channel_id=1, source_target_pairs={{0,3},{1,2},{2,1},{3,0},{4,7},{5,6},{6,5},{7,4},{8,11},{9,10},{10,... | collective-permute-start | bytes 442376 | tf_op jit(solution)/shard_map/ppermute | solution.py:470
  79.6 8.2 %collective-permute-start.2 = (bf16[3,2,48,256]{3,2,1,0:T(8,128)(2,1)S(1)}, bf16[3,2,48,256]{3,2,1,0:T(8,128)(2,1)S(1)}, u32[]{:S(2)}, u32[]{:S(2)}) collective-permute-start(bf16[3,2,48,256]{3,2,1,0:T(8,128)(2,1)S(1)} %copy-done.36), channel_id=1, source_target_pairs={{0,1},{1,0},{2,3},{3,2},{4,5},{5,4},{6,7},{7,6},{8,9},{9,8},{10,11... | collective-permute-start | bytes 442376 | tf_op jit(solution)/shard_map/ppermute | solution.py:470
  80.0 8.0 %collective-permute-start.4 = (bf16[3,2,48,256]{3,2,1,0:T(8,128)(2,1)S(1)}, bf16[3,2,48,256]{3,2,1,0:T(8,128)(2,1)S(1)}, u32[]{:S(2)}, u32[]{:S(2)}) collective-permute-start(bf16[3,2,48,256]{3,2,1,0:T(8,128)(2,1)S(1)} %copy-done.35), channel_id=1, source_target_pairs={{0,2},{1,3},{2,0},{3,1},{4,6},{5,7},{6,4},{7,5},{8,10},{9,11},{10,... | collective-permute-start | bytes 442376 | tf_op jit(solution)/shard_map/ppermute | solution.py:470
  84.2 22.4 %copy-start.16 = (bf16[3,2,48,256]{3,2,1,0:T(8,128)(2,1)}, bf16[3,2,48,256]{3,2,1,0:T(8,128)(2,1)S(1)}, u32[]{:S(2)}) copy-start(bf16[3,2,48,256]{3,2,1,0:T(8,128)(2,1)S(1)} %collective-permute-done.6.refs_3_) | copy-start | bytes 442372
  84.2 13.6 %collective-permute-start.7 = (bf16[5,2,48,256]{3,2,1,0:T(8,128)(2,1)S(1)}, bf16[5,2,48,256]{3,2,1,0:T(8,128)(2,1)S(1)}, u32[]{:S(2)}, u32[]{:S(2)}) collective-permute-start(bf16[5,2,48,256]{3,2,1,0:T(8,128)(2,1)S(1)} %copy-done.30), channel_id=1, source_target_pairs={{0,3},{1,2},{2,1},{3,0},{4,7},{5,6},{6,5},{7,4},{8,11},{9,10},{10,... | collective-permute-start | bytes 737288 | tf_op jit(solution)/shard_map/ppermute | solution.py:470
  85.8 12.0 %collective-permute-start.14 = (bf16[3,2,48,256]{3,2,1,0:T(8,128)(2,1)S(1)}, bf16[3,2,48,256]{3,2,1,0:T(8,128)(2,1)S(1)}, u32[]{:S(2)}, u32[]{:S(2)}) collective-permute-start(bf16[3,2,48,256]{3,2,1,0:T(8,128)(2,1)S(1)} %copy-done.34), channel_id=1, source_target_pairs={{0,7},{1,6},{2,5},{3,4},{4,3},{5,2},{6,1},{7,0},{8,15},{9,14},{10,... | collective-permute-start | bytes 442376 | tf_op jit(solution)/shard_map/ppermute | solution.py:470
  87.9 18.7 %copy-start.17 = (bf16[3,2,48,256]{3,2,1,0:T(8,128)(2,1)}, bf16[3,2,48,256]{3,2,1,0:T(8,128)(2,1)S(1)}, u32[]{:S(2)}) copy-start(bf16[3,2,48,256]{3,2,1,0:T(8,128)(2,1)S(1)} %collective-permute-done.2.refs_1_) | copy-start | bytes 442372
  88.0 18.6 %copy-start.18 = (bf16[3,2,48,256]{3,2,1,0:T(8,128)(2,1)}, bf16[3,2,48,256]{3,2,1,0:T(8,128)(2,1)S(1)}, u32[]{:S(2)}) copy-start(bf16[3,2,48,256]{3,2,1,0:T(8,128)(2,1)S(1)} %collective-permute-done.4.refs_2_) | copy-start | bytes 442372
  88.0 13.4 %collective-permute-start.5 = (bf16[5,2,48,256]{3,2,1,0:T(8,128)(2,1)S(1)}, bf16[5,2,48,256]{3,2,1,0:T(8,128)(2,1)S(1)}, u32[]{:S(2)}, u32[]{:S(2)}) collective-permute-start(bf16[5,2,48,256]{3,2,1,0:T(8,128)(2,1)S(1)} %copy-done.29), channel_id=1, source_target_pairs={{0,2},{1,3},{2,0},{3,1},{4,6},{5,7},{6,4},{7,5},{8,10},{9,11},{10,... | collective-permute-start | bytes 737288 | tf_op jit(solution)/shard_map/ppermute | solution.py:470
  89.5 11.9 %collective-permute-start.3 = (bf16[5,2,48,256]{3,2,1,0:T(8,128)(2,1)S(1)}, bf16[5,2,48,256]{3,2,1,0:T(8,128)(2,1)S(1)}, u32[]{:S(2)}, u32[]{:S(2)}) collective-permute-start(bf16[5,2,48,256]{3,2,1,0:T(8,128)(2,1)S(1)} %copy-done.28), channel_id=1, source_target_pairs={{0,1},{1,0},{2,3},{3,2},{4,5},{5,4},{6,7},{7,6},{8,9},{9,8},{10,11... | collective-permute-start | bytes 737288 | tf_op jit(solution)/shard_map/ppermute | solution.py:470
  89.5 11.9 %collective-permute-start.8 = (bf16[3,2,48,256]{3,2,1,0:T(8,128)(2,1)S(1)}, bf16[3,2,48,256]{3,2,1,0:T(8,128)(2,1)S(1)}, u32[]{:S(2)}, u32[]{:S(2)}) collective-permute-start(bf16[3,2,48,256]{3,2,1,0:T(8,128)(2,1)S(1)} %copy-done.33), channel_id=1, source_target_pairs={{0,4},{1,5},{2,6},{3,7},{4,0},{5,1},{6,2},{7,3},{8,12},{9,13},{10,... | collective-permute-start | bytes 442376 | tf_op jit(solution)/shard_map/ppermute | solution.py:470
  97.8 7.3 %collective-permute-start.10 = (bf16[3,2,48,256]{3,2,1,0:T(8,128)(2,1)S(1)}, bf16[3,2,48,256]{3,2,1,0:T(8,128)(2,1)S(1)}, u32[]{:S(2)}, u32[]{:S(2)}) collective-permute-start(bf16[3,2,48,256]{3,2,1,0:T(8,128)(2,1)S(1)} %copy-done.32), channel_id=1, source_target_pairs={{0,5},{1,4},{2,7},{3,6},{4,1},{5,0},{6,3},{7,2},{8,13},{9,12},{10,... | collective-permute-start | bytes 442376 | tf_op jit(solution)/shard_map/ppermute | solution.py:470
  97.8 13.3 %copy-start.9 = (bf16[5,2,48,256]{3,2,1,0:T(8,128)(2,1)}, bf16[5,2,48,256]{3,2,1,0:T(8,128)(2,1)S(1)}, u32[]{:S(2)}) copy-start(bf16[5,2,48,256]{3,2,1,0:T(8,128)(2,1)S(1)} %collective-permute-done.7.refs_3_) | copy-start | bytes 737284
  97.8 8.8 %collective-permute-start.12 = (bf16[3,2,48,256]{3,2,1,0:T(8,128)(2,1)S(1)}, bf16[3,2,48,256]{3,2,1,0:T(8,128)(2,1)S(1)}, u32[]{:S(2)}, u32[]{:S(2)}) collective-permute-start(bf16[3,2,48,256]{3,2,1,0:T(8,128)(2,1)S(1)} %copy-done.31), channel_id=1, source_target_pairs={{0,6},{1,7},{2,4},{3,5},{4,2},{5,3},{6,0},{7,1},{8,14},{9,15},{10,... | collective-permute-start | bytes 442376 | tf_op jit(solution)/shard_map/ppermute | solution.py:470
  107.2 22.6 %copy-start.26 = (bf16[5,2,48,256]{3,2,1,0:T(8,128)(2,1)S(1)}, bf16[5,2,48,256]{3,2,1,0:T(8,128)(2,1)}, u32[]{:S(2)}) copy-start(bf16[5,2,48,256]{3,2,1,0:T(8,128)(2,1)} %get-tuple-element.61) | copy-start | bytes 737284
  107.2 23.2 %copy-start.25 = (bf16[5,2,48,256]{3,2,1,0:T(8,128)(2,1)S(1)}, bf16[5,2,48,256]{3,2,1,0:T(8,128)(2,1)}, u32[]{:S(2)}) copy-start(bf16[5,2,48,256]{3,2,1,0:T(8,128)(2,1)} %get-tuple-element.58) | copy-start | bytes 737284
  107.2 23.4 %copy-start.24 = (bf16[5,2,48,256]{3,2,1,0:T(8,128)(2,1)S(1)}, bf16[5,2,48,256]{3,2,1,0:T(8,128)(2,1)}, u32[]{:S(2)}) copy-start(bf16[5,2,48,256]{3,2,1,0:T(8,128)(2,1)} %get-tuple-element.55) | copy-start | bytes 737284
  111.2 17.4 %collective-permute-start.17 = (bf16[2,3,2,48,256]{4,3,2,1,0:T(8,128)(2,1)}, bf16[2,3,2,48,256]{4,3,2,1,0:T(8,128)(2,1)S(1)}, u32[]{:S(2)}, u32[]{:S(2)}) collective-permute-start(bf16[2,3,2,48,256]{4,3,2,1,0:T(8,128)(2,1)} %get-tuple-element.67.refs_0_), channel_id=1, source_target_pairs={{0,16},{8,24},{16,0},{24,8},{1,17},{9,25},{17,1},{25,9},{2,18},{10... | collective-permute-start | bytes 884744 | tf_op jit(solution)/shard_map/ppermute | solution.py:429
  113.8 16.8 %collective-permute-start.18 = (bf16[2,3,2,48,256]{4,3,2,1,0:T(8,128)(2,1)}, bf16[2,3,2,48,256]{4,3,2,1,0:T(8,128)(2,1)S(1)}, u32[]{:S(2)}, u32[]{:S(2)}) collective-permute-start(bf16[2,3,2,48,256]{4,3,2,1,0:T(8,128)(2,1)} %get-tuple-element.67.refs_0_), channel_id=1, source_target_pairs={{8,16},{16,8},{9,17},{17,9},{10,18},{18,10},{11,19},{19,11},{12,20... | collective-permute-start | bytes 884744 | tf_op jit(solution)/shard_map/ppermute | solution.py:431
  114.5 15.9 %collective-permute-start.15 = (bf16[5,2,48,256]{3,2,1,0:T(8,128)(2,1)S(1)}, bf16[5,2,48,256]{3,2,1,0:T(8,128)(2,1)S(1)}, u32[]{:S(2)}, u32[]{:S(2)}) collective-permute-start(bf16[5,2,48,256]{3,2,1,0:T(8,128)(2,1)S(1)} %copy-done.27), channel_id=1, source_target_pairs={{0,7},{1,6},{2,5},{3,4},{4,3},{5,2},{6,1},{7,0},{8,15},{9,14},{10,... | collective-permute-start | bytes 737288 | tf_op jit(solution)/shard_map/ppermute | solution.py:470
  115.3 16.6 %collective-permute-start.16 = (bf16[2,3,2,48,256]{4,3,2,1,0:T(8,128)(2,1)}, bf16[2,3,2,48,256]{4,3,2,1,0:T(8,128)(2,1)S(1)}, u32[]{:S(2)}, u32[]{:S(2)}) collective-permute-start(bf16[2,3,2,48,256]{4,3,2,1,0:T(8,128)(2,1)} %get-tuple-element.67.refs_0_), channel_id=1, source_target_pairs={{0,8},{8,0},{16,24},{24,16},{1,9},{9,1},{17,25},{25,17},{2,10},{10... | collective-permute-start | bytes 884744 | tf_op jit(solution)/shard_map/ppermute | solution.py:430
  128.6 25.7 %copy-start.5 = (bf16[2,3,2,48,256]{4,3,2,1,0:T(8,128)(2,1)}, bf16[2,3,2,48,256]{4,3,2,1,0:T(8,128)(2,1)S(1)}, u32[]{:S(2)}) copy-start(bf16[2,3,2,48,256]{4,3,2,1,0:T(8,128)(2,1)S(1)} %collective-permute-done.17.refs_2_) | copy-start | bytes 884740
  128.6 10.6 %collective-permute-start.19 = (bf16[2,3,2,48,256]{4,3,2,1,0:T(8,128)(2,1)S(1)}, bf16[2,3,2,48,256]{4,3,2,1,0:T(8,128)(2,1)S(1)}, u32[]{:S(2)}, u32[]{:S(2)}) collective-permute-start(bf16[2,3,2,48,256]{4,3,2,1,0:T(8,128)(2,1)S(1)} %collective-permute-done.17.refs_2_), channel_id=1, source_target_pairs={{16,24},{8,0},{17,25},{9,1},{18,26},{10,2},{19,27},{11,3},{20,28},... | collective-permute-start | bytes 884744 | tf_op jit(solution)/shard_map/ppermute | solution.py:432
  129.9 9.3 %collective-permute-start.13 = (bf16[5,2,48,256]{3,2,1,0:T(8,128)(2,1)S(1)}, bf16[5,2,48,256]{3,2,1,0:T(8,128)(2,1)S(1)}, u32[]{:S(2)}, u32[]{:S(2)}) collective-permute-start(bf16[5,2,48,256]{3,2,1,0:T(8,128)(2,1)S(1)} %copy-done.26), channel_id=1, source_target_pairs={{0,6},{1,7},{2,4},{3,5},{4,2},{5,3},{6,0},{7,1},{8,14},{9,15},{10,... | collective-permute-start | bytes 737288 | tf_op jit(solution)/shard_map/ppermute | solution.py:470
  130.5 18.6 %copy-start.12 = (bf16[5,2,48,256]{3,2,1,0:T(8,128)(2,1)}, bf16[5,2,48,256]{3,2,1,0:T(8,128)(2,1)S(1)}, u32[]{:S(2)}) copy-start(bf16[5,2,48,256]{3,2,1,0:T(8,128)(2,1)S(1)} %collective-permute-done.15.refs_7_) | copy-start | bytes 737284
  130.5 13.3 %collective-permute-start.11 = (bf16[5,2,48,256]{3,2,1,0:T(8,128)(2,1)S(1)}, bf16[5,2,48,256]{3,2,1,0:T(8,128)(2,1)S(1)}, u32[]{:S(2)}, u32[]{:S(2)}) collective-permute-start(bf16[5,2,48,256]{3,2,1,0:T(8,128)(2,1)S(1)} %copy-done.25), channel_id=1, source_target_pairs={{0,5},{1,4},{2,7},{3,6},{4,1},{5,0},{6,3},{7,2},{8,13},{9,12},{10,... | collective-permute-start | bytes 737288 | tf_op jit(solution)/shard_map/ppermute | solution.py:470
  130.7 23.7 %copy-start.6 = (bf16[2,3,2,48,256]{4,3,2,1,0:T(8,128)(2,1)}, bf16[2,3,2,48,256]{4,3,2,1,0:T(8,128)(2,1)S(1)}, u32[]{:S(2)}) copy-start(bf16[2,3,2,48,256]{4,3,2,1,0:T(8,128)(2,1)S(1)} %collective-permute-done.18.refs_3_) | copy-start | bytes 884740
  130.7 18.3 %collective-permute-start.9 = (bf16[5,2,48,256]{3,2,1,0:T(8,128)(2,1)S(1)}, bf16[5,2,48,256]{3,2,1,0:T(8,128)(2,1)S(1)}, u32[]{:S(2)}, u32[]{:S(2)}) collective-permute-start(bf16[5,2,48,256]{3,2,1,0:T(8,128)(2,1)S(1)} %copy-done.24), channel_id=1, source_target_pairs={{0,4},{1,5},{2,6},{3,7},{4,0},{5,1},{6,2},{7,3},{8,12},{9,13},{10,... | collective-permute-start | bytes 737288 | tf_op jit(solution)/shard_map/ppermute | solution.py:470
  131.9 22.4 %copy-start.7 = (bf16[2,3,2,48,256]{4,3,2,1,0:T(8,128)(2,1)}, bf16[2,3,2,48,256]{4,3,2,1,0:T(8,128)(2,1)S(1)}, u32[]{:S(2)}) copy-start(bf16[2,3,2,48,256]{4,3,2,1,0:T(8,128)(2,1)S(1)} %collective-permute-done.16.refs_1_) | copy-start | bytes 884740
  139.2 15.2 %copy-start.8 = (bf16[2,3,2,48,256]{4,3,2,1,0:T(8,128)(2,1)}, bf16[2,3,2,48,256]{4,3,2,1,0:T(8,128)(2,1)S(1)}, u32[]{:S(2)}) copy-start(bf16[2,3,2,48,256]{4,3,2,1,0:T(8,128)(2,1)S(1)} %collective-permute-done.19.refs_4_) | copy-start | bytes 884740
  139.2 9.9 %copy-start.13 = (bf16[5,2,48,256]{3,2,1,0:T(8,128)(2,1)}, bf16[5,2,48,256]{3,2,1,0:T(8,128)(2,1)S(1)}, u32[]{:S(2)}) copy-start(bf16[5,2,48,256]{3,2,1,0:T(8,128)(2,1)S(1)} %collective-permute-done.13.refs_6_) | copy-start | bytes 737284
  154.4 26.8 %collective-permute-start.21 = (bf16[2,5,2,48,256]{4,3,2,1,0:T(8,128)(2,1)}, bf16[2,5,2,48,256]{4,3,2,1,0:T(8,128)(2,1)S(1)}, u32[]{:S(2)}, u32[]{:S(2)}) collective-permute-start(bf16[2,5,2,48,256]{4,3,2,1,0:T(8,128)(2,1)} %get-tuple-element.71.refs_0_), channel_id=1, source_target_pairs={{0,16},{8,24},{16,0},{24,8},{1,17},{9,25},{17,1},{25,9},{2,18},{10... | collective-permute-start | bytes 1474568 | tf_op jit(solution)/shard_map/ppermute | solution.py:429
  159.0 26.5 %collective-permute-start.22 = (bf16[2,5,2,48,256]{4,3,2,1,0:T(8,128)(2,1)}, bf16[2,5,2,48,256]{4,3,2,1,0:T(8,128)(2,1)S(1)}, u32[]{:S(2)}, u32[]{:S(2)}) collective-permute-start(bf16[2,5,2,48,256]{4,3,2,1,0:T(8,128)(2,1)} %get-tuple-element.71.refs_0_), channel_id=1, source_target_pairs={{8,16},{16,8},{9,17},{17,9},{10,18},{18,10},{11,19},{19,11},{12,20... | collective-permute-start | bytes 1474568 | tf_op jit(solution)/shard_map/ppermute | solution.py:431
  159.7 25.8 %collective-permute-start.20 = (bf16[2,5,2,48,256]{4,3,2,1,0:T(8,128)(2,1)}, bf16[2,5,2,48,256]{4,3,2,1,0:T(8,128)(2,1)S(1)}, u32[]{:S(2)}, u32[]{:S(2)}) collective-permute-start(bf16[2,5,2,48,256]{4,3,2,1,0:T(8,128)(2,1)} %get-tuple-element.71.refs_0_), channel_id=1, source_target_pairs={{0,8},{8,0},{16,24},{24,16},{1,9},{9,1},{17,25},{25,17},{2,10},{10... | collective-permute-start | bytes 1474568 | tf_op jit(solution)/shard_map/ppermute | solution.py:430
  181.2 15.0 %collective-permute-start.23 = (bf16[2,5,2,48,256]{4,3,2,1,0:T(8,128)(2,1)S(1)}, bf16[2,5,2,48,256]{4,3,2,1,0:T(8,128)(2,1)S(1)}, u32[]{:S(2)}, u32[]{:S(2)}) collective-permute-start(bf16[2,5,2,48,256]{4,3,2,1,0:T(8,128)(2,1)S(1)} %collective-permute-done.21.refs_2_), channel_id=1, source_target_pairs={{16,24},{8,0},{17,25},{9,1},{18,26},{10,2},{19,27},{11,3},{20,28},... | collective-permute-start | bytes 1474568 | tf_op jit(solution)/shard_map/ppermute | solution.py:432
  185.5 10.7 %copy-start.2 = (bf16[2,5,2,48,256]{4,3,2,1,0:T(8,128)(2,1)}, bf16[2,5,2,48,256]{4,3,2,1,0:T(8,128)(2,1)S(1)}, u32[]{:S(2)}) copy-start(bf16[2,5,2,48,256]{4,3,2,1,0:T(8,128)(2,1)S(1)} %collective-permute-done.22.refs_3_) | copy-start | bytes 1474564
  185.5 10.7 %copy-start.3 = (bf16[2,5,2,48,256]{4,3,2,1,0:T(8,128)(2,1)}, bf16[2,5,2,48,256]{4,3,2,1,0:T(8,128)(2,1)S(1)}, u32[]{:S(2)}) copy-start(bf16[2,5,2,48,256]{4,3,2,1,0:T(8,128)(2,1)S(1)} %collective-permute-done.20.refs_1_) | copy-start | bytes 1474564
  (17 other events, 78.0 us)
Sparse Core Ops, SparseCore 0:
  10.1 39.1 all-gather.2
  78.4 37.4 reduce-scatter.1

commit v6 on v5

--- a/solution.py
+++ b/solution.py
@@ -188,7 +188,7 @@
                 back_pre = (back_hidden * slopes).astype(jnp.bfloat16)
                 part = lax.dot_general(
                     hidden, read_out, (((1,), (1,)), ((), ())), preferred_element_type=jnp.float32
-                )
+                ).astype(jnp.bfloat16)
                 grad_in = lax.dot_general(
                     sig, back_pre, (((0,), (0,)), ((), ())), preferred_element_type=jnp.float32
                 )
@@ -218,7 +218,7 @@
 
                 lax.fori_loop(0, size, write, 0)
 
-    pred_shape = jax.ShapeDtypeStruct((planes, rows, SITES), jnp.float32)
+    pred_shape = jax.ShapeDtypeStruct((planes, rows, SITES), jnp.bfloat16)
     grad_shapes = [
         jax.ShapeDtypeStruct((size, 2, piece if aligned else SITES, width), jnp.bfloat16)
         for size in sizes
@@ -230,7 +230,7 @@
         pltpu.VMEM((2 * planes, rows, 128), jnp.float32),
         pltpu.VMEM((half, 2, SITES, width), jnp.bfloat16),
         pltpu.VMEM((2 * planes,) + rows_in[0].shape[1:], jnp.bfloat16),
-        pltpu.VMEM((2 * planes, rows, SITES), jnp.float32),
+        pltpu.VMEM((2 * planes, rows, SITES), jnp.bfloat16),
         pltpu.SMEM((2 * planes,), jnp.int32),
         pltpu.SMEM((4, most + 1), jnp.int32),
         pltpu.SemaphoreType.DMA((2 + n_own,)),
@@ -420,7 +420,7 @@
     return lax.optimization_barrier((value,) + others)[0]
 
 
-def gather_planes(fresh, dp_at, n_dp):
+def gather_planes(fresh, dp_at, n_dp, before):
     if n_dp != 4:
         whole = lax.all_gather(fresh, "dp", axis=0)
         return [
@@ -429,7 +429,7 @@
     two = lax.ppermute(fresh, "dp", [(0, 2), (1, 3), (2, 0), (3, 1)])
     one = lax.ppermute(fresh, "dp", [(0, 1), (1, 0), (2, 3), (3, 2)])
     middle = lax.ppermute(fresh, "dp", [(1, 2), (2, 1)])
-    outer = lax.ppermute(two, "dp", [(2, 3), (1, 0)])
+    outer = lax.ppermute(after(two, *before), "dp", [(2, 3), (1, 0)])
     return [fresh, one, two, (middle, outer)]
 
 
@@ -482,25 +482,24 @@
     pred_mine, pred_other, grads = local_grads(
         pos, touched, slot_map, rows_in, blocks, sizes, piece, width
     )
-    pred_part = pred_mine + across(pred_other, 1)
-    total = lax.psum_scatter(pred_part, "dp", scatter_dimension=0)
-
     arrived = []
     for chunk in grads:
         for j in range(1, n_own if arrived else 1):
             chunk[j] = after(chunk[j], arrived[-1][j])
         arrived.append([chunk[0]] + [across(chunk[j], j) for j in range(1, n_own)])
-    ready = [list(one) for one in arrived]
-    ready[0][-1] = after(ready[0][-1], pred_part, *arrived[-1][1 : n_own // 2])
+    pred_other = across(after(pred_other, arrived[0][1]), 1)
+    pred_part = pred_mine.astype(jnp.float32) + pred_other.astype(jnp.float32)
+    total = lax.psum_scatter(pred_part, "dp", scatter_dimension=0)
 
     moments = []
     new_weights = []
     start = 0
-    for size, chunk in zip(sizes, ready):
-        if start:
-            chunk[-1] = after(chunk[-1], *jax.tree.leaves(pieces[1:]))
-        fresh, *moments = adam(pos, chunk, weights, moment1, moment2, start, moments)
-        pieces = gather_planes(fresh, dp_at, n_dp)
+    for i, size in enumerate(sizes):
+        ready = list(arrived[i])
+        ready[-1] = after(ready[-1], *(jax.tree.leaves(pieces[1:])[:n_dp - 1] if i else [pred_part]))
+        fresh, *moments = adam(pos, ready, weights, moment1, moment2, start, moments)
+        later = arrived[i + 1][1 : n_own // 2 + 1] if i + 1 < len(sizes) else []
+        pieces = gather_planes(fresh, dp_at, n_dp, later)
         new_weights = [place_weights(pos, pieces, start, half, new_weights)]
         start += size
     new_weights = new_weights[0]

time: 210 us -> 211 us (level)
  starting transfers between devices: 33.6 us -> 28.3 us
  waiting for transfers between devices: 114 us -> 117 us
  local copies, waits for them, and re-layouts: 7.8 us -> 10.3 us
    ppermute x2, starting transfers between devices: 7.3 us -> 4.42 us  [gather_planes(): two = lax.ppermute(fresh, 'dp', [(0, 2), (1, 3), (2, 0), (3, 1)])]
    ppermute x16, starting transfers between devices: 13.3 us -> 10.6 us  [across(): return lax.ppermute(value, 'own', [(o, o ^ j) for o in range(n_own)])]
    unnamed x77 -> x75, local copies, waits for them, and re-layouts: 4.56 us -> 7.04 us
where the time goes in v6:
time: 211 us; the launch traced here: 209 us
  waiting for transfers between devices  117 us (55%)
  Pallas kernels  36 us (17%)
  starting transfers between devices  28.3 us (13%)
  between operations  14.4 us (7%)
  local copies, waits for them, and re-layouts  10.3 us (5%)
  other arithmetic  3.11 us (1%)
    ppermute x16, waiting for transfers between devices, across(): return lax.ppermute(value, 'own', [(o, o ^ j) for o in range(n_own)])  33 us
    all_gather x1, waiting for transfers between devices, shards(): planes = lax.all_gather(packed, 'dp', axis=0)  32 us
    ppermute x2, waiting for transfers between devices, gather_planes(): two = lax.ppermute(fresh, 'dp', [(0, 2), (1, 3), (2, 0), (3, 1)])  30 us
    ppermute x2, waiting for transfers between devices, gather_planes(): outer = lax.ppermute(after(two, *before), 'dp', [(2, 3), (1, 0)])  18.5 us
    pallas_call x1, Pallas kernels, local_grads(): pl.pallas_call(body, out_shape=[pred_shape, pred_shape] + grad_shapes, in...  16.7 us
    ppermute x16, starting transfers between devices, across(): return lax.ppermute(value, 'own', [(o, o ^ j) for o in range(n_own)])  10.6 us
    pallas_call x2, Pallas kernels, adam(): pl.pallas_call(body, out_shape=[jax.ShapeDtypeStruct(blocks, jnp.bfloat16...  8.49 us
    unnamed x75, local copies, waits for them, and re-layouts  7.04 us
  transfers between devices with their start and end apart: 27, of which 15 were waited for; matrix products, arithmetic and copies ran while one was open for 2% of the time, Pallas kernels for 7%

profile of v6, /device:TPU:2, one launch (start us, length us, event | category | flops | bytes accessed | tf_op | source)
XLA Modules:
  0.0 208.7 jit_solution(11057181835159200916)
XLA Ops:
  7.2 2.4 %pack_rows.1 = (bf16[528,384]{1,0:T(8,128)(2,1)}, bf16[256,256]{1,0:T(8,128)(2,1)}) custom-call(s32[1,256]{1,0:T(1,128)} %bitcast.12, bf16[256,384]{1,0:T(8,128)(2,1)} %sig_ref.1, bf16[256,384]{1,0:T(8,128)(2,1)} %cot_ref.1), custom_call_target="tpu_custom_call" | custom-call | tf_op jit(solution)/shard_map/pack_rows/pallas_call | solution.py:79
  9.6 1.2 constant_dynamic-slice_fusion
  10.8 2.0 broadcast_in_dim.8
  12.9 4.4 %all-to-all-start = ((bf16[8,8,2,48,256]{4,3,2,1,0:T(8,128)(2,1)}), bf16[8,8,2,48,256]{4,3,2,1,0:T(8,128)(2,1)S(1)}, u32[]{:S(2)}, u32[]{:S(2)}) async-start(bf16[8,8,2,48,256]{4,3,2,1,0:T(8,128)(2,1)} %bitcast.7), calls=%async_computation | async-start | bytes 6291456 | tf_op jit(solution)/shard_map/all_to_all | solution.py:479
  17.3 32.0 %all-gather.3.cloned.1.call-done = bf16[2112,384]{1,0:T(8,128)(2,1)} async-done(((bf16[528,384]{1,0:T(8,128)(2,1)}), bf16[2112,384]{1,0:T(8,128)(2,1)}) %all-gather.3.cloned.1.call-update) | async-done | bytes 1622032 | tf_op jit(solution)/shard_map/all_gather | solution.py:473
  49.3 0.7 copy.15.touched_ref
  50.0 0.7 pad_add_fusion.pos_ref
  50.7 3.0 %all-to-all-done.rest_2_ = bf16[8,8,2,48,256]{4,3,2,1,0:T(8,128)(2,1)S(1)} async-done(((bf16[8,8,2,48,256]{4,3,2,1,0:T(8,128)(2,1)}), bf16[8,8,2,48,256]{4,3,2,1,0:T(8,128)(2,1)S(1)}, u32[]{:S(2)}, u32[]{:S(2)}) %all-to-all-start) | async-done | bytes 3145760 | tf_op jit(solution)/shard_map/all_to_all | solution.py:479
  53.7 1.7 copy-done
  55.3 16.7 %local_grads.1 = (bf16[4,256,384]{2,1,0:T(8,128)(2,1)}, bf16[4,256,384]{2,1,0:T(8,128)(2,1)}, bf16[3,2,48,256]{3,2,1,0:T(8,128)(2,1)}, bf16[3,2,48,256]{3,2,1,0:...) custom-call(s32[2]{0:T(128)} %pad_add_fusion.pos_ref, ...), custom_call_target="tpu_custom_call" | custom-call | tf_op jit(solution)/shard_map/local_grads/pallas_call | solution.py:241
  72.1 1.6 collective-permute-done.1.refs_1_
  73.8 2.3 %collective-permute-done.2 = bf16[4,256,384]{2,1,0:T(8,128)(2,1)S(1)} collective-permute-done((bf16[4,256,384]{2,1,0:T(8,128)(2,1)}, bf16[4,256,384]{2,1,0:T(8,128)(2,1)S(1)}, u32[]{:S(2)}, u32[]{:S(2)}) %collective-permute-start.2) | collective-permute-done | bytes 786464 | tf_op jit(solution)/shard_map/ppermute | solution.py:470
  76.2 2.4 %convert_add_fusion = f32[4,256,384]{2,1,0:T(8,128)} fusion(bf16[4,256,384]{2,1,0:T(8,128)(2,1)S(1)} %collective-permute-done.2, bf16[4,256,384]{2,1,0:T(8,128)(2,1)} %get-tuple-element.43), kind=kLoop, calls=%fused_computation | loop fusion | flops 1179648 | bytes 3145728 | tf_op jit(solution)/shard_map/add | solution.py:491
  78.7 0.8 copy-done.36
  79.5 1.2 collective-permute-start.14
  80.8 1.7 collective-permute-start.6
  82.9 1.4 collective-permute-start.10
  84.3 2.0 collective-permute-done.14.refs_7_
  86.3 1.5 collective-permute-start.12
  87.9 0.5 collective-permute-done.4.refs_2_
  88.3 3.0 %collective-permute-done.6.refs_3_ = bf16[3,2,48,256]{3,2,1,0:T(8,128)(2,1)S(1)} collective-permute-done((bf16[3,2,48,256]{3,2,1,0:T(8,128)(2,1)S(1)}, bf16[3,2,48,256]{3,2,1,0:T(8,128)(2,1)S(1)}, u32[]{:S(2)}, u32[]{:S(2)}) %collective-permute-start.6) | collective-permute-done | bytes 147488 | tf_op jit(solution)/shard_map/ppermute | solution.py:470
  91.3 1.8 collective-permute-done.10.refs_5_
  93.1 2.9 %collective-permute-done.12.refs_6_ = bf16[3,2,48,256]{3,2,1,0:T(8,128)(2,1)S(1)} collective-permute-done((bf16[3,2,48,256]{3,2,1,0:T(8,128)(2,1)S(1)}, bf16[3,2,48,256]{3,2,1,0:T(8,128)(2,1)S(1)}, u32[]{:S(2)}, u32[]{:S(2)}) %collective-permute-start.12) | collective-permute-done | bytes 147488 | tf_op jit(solution)/shard_map/ppermute | solution.py:470
  96.1 0.6 copy-done.22
  96.8 3.9 %adam_step.2 = (bf16[2,3,2,48,256]{4,3,2,1,0:T(8,128)(2,1)}, f32[16,2,48,256]{3,2,1,0:T(8,128)}, f32[16,2,48,256]{3,2,1,0:T(8,128)}) custom-call(s32[2]{0:T(128)} %pad_add_fusion.pos_ref, bf16[3,2,48,256]{3,2,1,0:T(8,128)(2,1)} %get-tuple-element.68.refs_0_, bf16[3,2,48,256]{3,2,1,0:T(8,128)(2,1)} %copy-done.16, bf16[3,2,48,256]{3,2,1,0:T(8,128)(2,1)} %copy-done.18, ...), custom_call_target="tpu_custom_call" | custom-call | tf_op jit(solution)/shard_map/adam_step/pallas_call | solution.py:333
  100.6 0.7 collective-permute-start.18
  101.3 4.3 %collective-permute-start.17 = (bf16[2,3,2,48,256]{4,3,2,1,0:T(8,128)(2,1)}, bf16[2,3,2,48,256]{4,3,2,1,0:T(8,128)(2,1)S(1)}, u32[]{:S(2)}, u32[]{:S(2)}) collective-permute-start(bf16[2,3,2,48,256]{4,3,2,1,0:T(8,128)(2,1)} %get-tuple-element.70.refs_0_), channel_id=1, source_target_pairs={{0,16},{8,24},{16,0},{24,8},{1,17},{9,25},{17,1},{25,9},{2,18},{10... | collective-permute-start | bytes 884744 | tf_op jit(solution)/shard_map/ppermute | solution.py:429
  106.2 1.4 collective-permute-start.13
  107.6 7.3 %collective-permute-done.15.refs_7_ = bf16[5,2,48,256]{3,2,1,0:T(8,128)(2,1)S(1)} collective-permute-done((bf16[5,2,48,256]{3,2,1,0:T(8,128)(2,1)S(1)}, bf16[5,2,48,256]{3,2,1,0:T(8,128)(2,1)S(1)}, u32[]{:S(2)}, u32[]{:S(2)}) %collective-permute-start.15) | collective-permute-done | bytes 245792 | tf_op jit(solution)/shard_map/ppermute | solution.py:470
  115.0 4.3 %collective-permute-done.13.refs_6_ = bf16[5,2,48,256]{3,2,1,0:T(8,128)(2,1)S(1)} collective-permute-done((bf16[5,2,48,256]{3,2,1,0:T(8,128)(2,1)S(1)}, bf16[5,2,48,256]{3,2,1,0:T(8,128)(2,1)S(1)}, u32[]{:S(2)}, u32[]{:S(2)}) %collective-permute-start.13) | collective-permute-done | bytes 245792 | tf_op jit(solution)/shard_map/ppermute | solution.py:470
  119.3 1.8 collective-permute-start.7
  121.1 11.2 %collective-permute-done.17.refs_2_ = bf16[2,3,2,48,256]{4,3,2,1,0:T(8,128)(2,1)S(1)} collective-permute-done((bf16[2,3,2,48,256]{4,3,2,1,0:T(8,128)(2,1)}, bf16[2,3,2,48,256]{4,3,2,1,0:T(8,128)(2,1)S(1)}, u32[]{:S(2)}, u32[]{:S(2)}) %collective-permute-start.17) | collective-permute-done | bytes 294944 | tf_op jit(solution)/shard_map/ppermute | solution.py:429
  132.3 0.6 collective-permute-start.5
  133.0 7.2 %collective-permute-done.5.refs_2_ = bf16[5,2,48,256]{3,2,1,0:T(8,128)(2,1)S(1)} collective-permute-done((bf16[5,2,48,256]{3,2,1,0:T(8,128)(2,1)S(1)}, bf16[5,2,48,256]{3,2,1,0:T(8,128)(2,1)S(1)}, u32[]{:S(2)}, u32[]{:S(2)}) %collective-permute-start.5) | collective-permute-done | bytes 245792 | tf_op jit(solution)/shard_map/ppermute | solution.py:470
  140.2 0.6 copy-done.14
  141.0 4.6 %adam_step.3 = (bf16[2,5,2,48,256]{4,3,2,1,0:T(8,128)(2,1)}, f32[16,2,48,256]{3,2,1,0:T(8,128)}, f32[16,2,48,256]{3,2,1,0:T(8,128)}) custom-call(s32[2]{0:T(128)} %pad_add_fusion.pos_ref, bf16[5,2,48,256]{3,2,1,0:T(8,128)(2,1)} %get-tuple-element.47.refs_0_, bf16[5,2,48,256]{3,2,1,0:T(8,128)(2,1)} %copy-done.15, ...), custom_call_target="tpu_custom_call", output_to_operand_aliasing={{1}: (12, {}), {2}: (13, {})} | custom-call | tf_op jit(solution)/shard_map/adam_step/pallas_call | solution.py:333
  145.7 0.7 collective-permute-start.21
  146.4 4.7 %collective-permute-start.19 = (bf16[2,5,2,48,256]{4,3,2,1,0:T(8,128)(2,1)}, bf16[2,5,2,48,256]{4,3,2,1,0:T(8,128)(2,1)S(1)}, u32[]{:S(2)}, u32[]{:S(2)}) collective-permute-start(bf16[2,5,2,48,256]{4,3,2,1,0:T(8,128)(2,1)} %get-tuple-element.74.refs_0_), channel_id=1, source_target_pairs={{0,8},{8,0},{16,24},{24,16},{1,9},{9,1},{17,25},{25,17},{2,10},{10... | collective-permute-start | bytes 1474568 | tf_op jit(solution)/shard_map/ppermute | solution.py:430
  151.1 18.7 %collective-permute-done.20.refs_2_ = bf16[2,5,2,48,256]{4,3,2,1,0:T(8,128)(2,1)S(1)} collective-permute-done((bf16[2,5,2,48,256]{4,3,2,1,0:T(8,128)(2,1)}, bf16[2,5,2,48,256]{4,3,2,1,0:T(8,128)(2,1)S(1)}, u32[]{:S(2)}, u32[]{:S(2)}) %collective-permute-start.20) | collective-permute-done | bytes 491552 | tf_op jit(solution)/shard_map/ppermute | solution.py:429
  169.9 1.3 collective-permute-start.22
  171.2 1.3 collective-permute-start.23
  172.5 18.5 %collective-permute-done.23.refs_4_ = bf16[2,3,2,48,256]{4,3,2,1,0:T(8,128)(2,1)S(1)} collective-permute-done((bf16[2,3,2,48,256]{4,3,2,1,0:T(8,128)(2,1)S(1)}, bf16[2,3,2,48,256]{4,3,2,1,0:T(8,128)(2,1)S(1)}, u32[]{:S(2)}, u32[]{:S(2)}) %collective-permute-start.23) | collective-permute-done | bytes 294944 | tf_op jit(solution)/shard_map/ppermute | solution.py:432
  191.0 0.7 copy-done.8
  191.7 3.0 %place_weights.2.refs_5_ = bf16[16,2,48,1024]{3,2,1,0:T(8,128)(2,1)} custom-call(s32[2]{0:T(128)} %pad_add_fusion.pos_ref, bf16[2,3,2,48,256]{4,3,2,1,0:T(8,128)(2,1)} %get-tuple-element.70.refs_0_, bf16[2,3,2,48,256]{4,3,2,1,0:T(8,128)(2,1)} %copy-done.7, bf16[2,3,2,48,256]{4,3,2,1,0:T(8,128)(2,1)} %copy-done.6, bf16[2,3,2,48,256]{4,3,2,1,0:T(8,128)(2,1)} %copy-done.5, ...), custom_call_target="tpu_custom_call" | custom-call | tf_op jit(solution)/shard_map/place_weights/pallas_call | solution.py:403
  194.7 0.8 copy-done.2
  195.6 0.8 copy-done.4
  196.4 3.5 %place_weights.3 = bf16[16,2,48,1024]{3,2,1,0:T(8,128)(2,1)} custom-call(s32[2]{0:T(128)} %pad_add_fusion.pos_ref, bf16[2,5,2,48,256]{4,3,2,1,0:T(8,128)(2,1)} %get-tuple-element.74.refs_0_, bf16[2,5,2,48,256]{4,3,2,1,0:T(8,128)(2,1)} %copy-done.3, bf16[2,5,2,48,256]{4,3,2,1,0:T(8,128)(2,1)} %copy-done.1, ...), custom_call_target="tpu_custom_call", output_to_operand_aliasing={{}: (6, {})} | custom-call | tf_op jit(solution)/shard_map/place_weights/pallas_call | solution.py:403
  199.9 2.0 finish_predicted.1
  (94 shorter events, 1.7 us)
Async XLA Ops:
  7.2 42.1 %all-gather.3.cloned.1.call-start = ((), (), s32[]{:S(2)}) async-start(), calls=%async_computation.3 | async-start | bytes 2027520 | tf_op jit(solution)/shard_map/all_gather | solution.py:473
  12.9 36.4 %copy-start.23 = (s32[32,4]{0,1:T(4,128)S(1)}, s32[32,4]{0,1:T(4,128)}, u32[]{:S(2)}) copy-start(s32[32,4]{0,1:T(4,128)} %param.11) | copy-start | bytes 1540
  12.9 40.8 %all-to-all-start = ((bf16[8,8,2,48,256]{4,3,2,1,0:T(8,128)(2,1)}), bf16[8,8,2,48,256]{4,3,2,1,0:T(8,128)(2,1)S(1)}, u32[]{:S(2)}, u32[]{:S(2)}) async-start(bf16[8,8,2,48,256]{4,3,2,1,0:T(8,128)(2,1)} %bitcast.7), calls=%async_computation | async-start | bytes 6291456 | tf_op jit(solution)/shard_map/all_to_all | solution.py:479
  17.3 182.6 %reduce-scatter.2.cloned.1.call-start = ((), (), s32[]{:S(2)}) async-start(), calls=%async_computation.2 | async-start | bytes 1966080 | tf_op jit(solution)/shard_map/reduce_scatter | solution.py:492
  49.3 4.3 %collective-permute-start = (bf16[4,528,384]{2,1,0:T(8,128)(2,1)}, bf16[4,528,384]{2,1,0:T(8,128)(2,1)}, u32[]{:S(2)}, u32[]{:S(2)}) collective-permute-start(bf16[4,528,384]{2,1,0:T(8,128)(2,1)} %bitcast.9), channel_id=1, source_target_pairs={{0,1},{1,0},{2,3},{3,2},{4,5},{5,4},{6,7},{7,6},{8,9},{9,8},{10,11... | collective-permute-start | bytes 4866056 | tf_op jit(solution)/shard_map/ppermute | solution.py:470
  72.0 1.6 collective-permute-start.1
  73.7 4.9 %copy-start.16 = (bf16[3,2,48,256]{3,2,1,0:T(8,128)(2,1)}, bf16[3,2,48,256]{3,2,1,0:T(8,128)(2,1)S(1)}, u32[]{:S(2)}) copy-start(bf16[3,2,48,256]{3,2,1,0:T(8,128)(2,1)S(1)} %collective-permute-done.1.refs_1_) | copy-start | bytes 442372
  73.7 2.5 %collective-permute-start.2 = (bf16[4,256,384]{2,1,0:T(8,128)(2,1)}, bf16[4,256,384]{2,1,0:T(8,128)(2,1)S(1)}, u32[]{:S(2)}, u32[]{:S(2)}) collective-permute-start(bf16[4,256,384]{2,1,0:T(8,128)(2,1)} %get-tuple-element.46), channel_id=1, source_target_pairs={{0,1},{1,0},{2,3},{3,2},{4,5},{5,4},{6,7},{7,6},{8,9},{9,8},{10,11... | collective-permute-start | bytes 2359304 | tf_op jit(solution)/shard_map/ppermute | solution.py:470
  78.7 7.7 %copy-start.31 = (bf16[3,2,48,256]{3,2,1,0:T(8,128)(2,1)S(1)}, bf16[3,2,48,256]{3,2,1,0:T(8,128)(2,1)}, u32[]{:S(2)}) copy-start(bf16[3,2,48,256]{3,2,1,0:T(8,128)(2,1)} %get-tuple-element.63) | copy-start | bytes 442372
  79.5 6.8 %collective-permute-start.14 = (bf16[3,2,48,256]{3,2,1,0:T(8,128)(2,1)S(1)}, bf16[3,2,48,256]{3,2,1,0:T(8,128)(2,1)S(1)}, u32[]{:S(2)}, u32[]{:S(2)}) collective-permute-start(bf16[3,2,48,256]{3,2,1,0:T(8,128)(2,1)S(1)} %copy-done.36), channel_id=1, source_target_pairs={{0,7},{1,6},{2,5},{3,4},{4,3},{5,2},{6,1},{7,0},{8,15},{9,14},{10,... | collective-permute-start | bytes 442376 | tf_op jit(solution)/shard_map/ppermute | solution.py:470
  80.8 7.6 %collective-permute-start.4 = (bf16[3,2,48,256]{3,2,1,0:T(8,128)(2,1)S(1)}, bf16[3,2,48,256]{3,2,1,0:T(8,128)(2,1)S(1)}, u32[]{:S(2)}, u32[]{:S(2)}) collective-permute-start(bf16[3,2,48,256]{3,2,1,0:T(8,128)(2,1)S(1)} %copy-done.35), channel_id=1, source_target_pairs={{0,2},{1,3},{2,0},{3,1},{4,6},{5,7},{6,4},{7,5},{8,10},{9,11},{10,... | collective-permute-start | bytes 442376 | tf_op jit(solution)/shard_map/ppermute | solution.py:470
  80.8 10.5 %collective-permute-start.6 = (bf16[3,2,48,256]{3,2,1,0:T(8,128)(2,1)S(1)}, bf16[3,2,48,256]{3,2,1,0:T(8,128)(2,1)S(1)}, u32[]{:S(2)}, u32[]{:S(2)}) collective-permute-start(bf16[3,2,48,256]{3,2,1,0:T(8,128)(2,1)S(1)} %copy-done.34), channel_id=1, source_target_pairs={{0,3},{1,2},{2,1},{3,0},{4,7},{5,6},{6,5},{7,4},{8,11},{9,10},{10,... | collective-permute-start | bytes 442376 | tf_op jit(solution)/shard_map/ppermute | solution.py:470
  82.5 8.8 %collective-permute-start.8 = (bf16[3,2,48,256]{3,2,1,0:T(8,128)(2,1)S(1)}, bf16[3,2,48,256]{3,2,1,0:T(8,128)(2,1)S(1)}, u32[]{:S(2)}, u32[]{:S(2)}) collective-permute-start(bf16[3,2,48,256]{3,2,1,0:T(8,128)(2,1)S(1)} %copy-done.33), channel_id=1, source_target_pairs={{0,4},{1,5},{2,6},{3,7},{4,0},{5,1},{6,2},{7,3},{8,12},{9,13},{10,... | collective-permute-start | bytes 442376 | tf_op jit(solution)/shard_map/ppermute | solution.py:470
  82.9 10.3 %collective-permute-start.10 = (bf16[3,2,48,256]{3,2,1,0:T(8,128)(2,1)S(1)}, bf16[3,2,48,256]{3,2,1,0:T(8,128)(2,1)S(1)}, u32[]{:S(2)}, u32[]{:S(2)}) collective-permute-start(bf16[3,2,48,256]{3,2,1,0:T(8,128)(2,1)S(1)} %copy-done.32), channel_id=1, source_target_pairs={{0,5},{1,4},{2,7},{3,6},{4,1},{5,0},{6,3},{7,2},{8,13},{9,12},{10,... | collective-permute-start | bytes 442376 | tf_op jit(solution)/shard_map/ppermute | solution.py:470
  86.3 9.7 %copy-start.17 = (bf16[3,2,48,256]{3,2,1,0:T(8,128)(2,1)}, bf16[3,2,48,256]{3,2,1,0:T(8,128)(2,1)S(1)}, u32[]{:S(2)}) copy-start(bf16[3,2,48,256]{3,2,1,0:T(8,128)(2,1)S(1)} %collective-permute-done.14.refs_7_) | copy-start | bytes 442372
  86.3 9.7 %collective-permute-start.12 = (bf16[3,2,48,256]{3,2,1,0:T(8,128)(2,1)S(1)}, bf16[3,2,48,256]{3,2,1,0:T(8,128)(2,1)S(1)}, u32[]{:S(2)}, u32[]{:S(2)}) collective-permute-start(bf16[3,2,48,256]{3,2,1,0:T(8,128)(2,1)S(1)} %copy-done.31), channel_id=1, source_target_pairs={{0,6},{1,7},{2,4},{3,5},{4,2},{5,3},{6,0},{7,1},{8,14},{9,15},{10,... | collective-permute-start | bytes 442376 | tf_op jit(solution)/shard_map/ppermute | solution.py:470
  88.3 7.7 %copy-start.18 = (bf16[3,2,48,256]{3,2,1,0:T(8,128)(2,1)}, bf16[3,2,48,256]{3,2,1,0:T(8,128)(2,1)S(1)}, u32[]{:S(2)}) copy-start(bf16[3,2,48,256]{3,2,1,0:T(8,128)(2,1)S(1)} %collective-permute-done.4.refs_2_) | copy-start | bytes 442372
  96.7 9.2 %copy-start.30 = (bf16[5,2,48,256]{3,2,1,0:T(8,128)(2,1)S(1)}, bf16[5,2,48,256]{3,2,1,0:T(8,128)(2,1)}, u32[]{:S(2)}) copy-start(bf16[5,2,48,256]{3,2,1,0:T(8,128)(2,1)} %get-tuple-element.67) | copy-start | bytes 737284
  96.7 9.5 %copy-start.29 = (bf16[5,2,48,256]{3,2,1,0:T(8,128)(2,1)S(1)}, bf16[5,2,48,256]{3,2,1,0:T(8,128)(2,1)}, u32[]{:S(2)}) copy-start(bf16[5,2,48,256]{3,2,1,0:T(8,128)(2,1)} %get-tuple-element.64) | copy-start | bytes 737284
  96.7 18.2 %copy-start.28 = (bf16[5,2,48,256]{3,2,1,0:T(8,128)(2,1)S(1)}, bf16[5,2,48,256]{3,2,1,0:T(8,128)(2,1)}, u32[]{:S(2)}) copy-start(bf16[5,2,48,256]{3,2,1,0:T(8,128)(2,1)} %get-tuple-element.61) | copy-start | bytes 737284
  96.7 22.5 %copy-start.27 = (bf16[5,2,48,256]{3,2,1,0:T(8,128)(2,1)S(1)}, bf16[5,2,48,256]{3,2,1,0:T(8,128)(2,1)}, u32[]{:S(2)}) copy-start(bf16[5,2,48,256]{3,2,1,0:T(8,128)(2,1)} %get-tuple-element.58) | copy-start | bytes 737284
  96.7 22.6 %copy-start.26 = (bf16[5,2,48,256]{3,2,1,0:T(8,128)(2,1)S(1)}, bf16[5,2,48,256]{3,2,1,0:T(8,128)(2,1)}, u32[]{:S(2)}) copy-start(bf16[5,2,48,256]{3,2,1,0:T(8,128)(2,1)} %get-tuple-element.55) | copy-start | bytes 737284
  96.7 35.5 %copy-start.25 = (bf16[5,2,48,256]{3,2,1,0:T(8,128)(2,1)S(1)}, bf16[5,2,48,256]{3,2,1,0:T(8,128)(2,1)}, u32[]{:S(2)}) copy-start(bf16[5,2,48,256]{3,2,1,0:T(8,128)(2,1)} %get-tuple-element.52) | copy-start | bytes 737284
  96.7 36.1 %copy-start.24 = (bf16[5,2,48,256]{3,2,1,0:T(8,128)(2,1)S(1)}, bf16[5,2,48,256]{3,2,1,0:T(8,128)(2,1)}, u32[]{:S(2)}) copy-start(bf16[5,2,48,256]{3,2,1,0:T(8,128)(2,1)} %get-tuple-element.49) | copy-start | bytes 737284
  100.6 18.6 %collective-permute-start.18 = (bf16[2,3,2,48,256]{4,3,2,1,0:T(8,128)(2,1)}, bf16[2,3,2,48,256]{4,3,2,1,0:T(8,128)(2,1)S(1)}, u32[]{:S(2)}, u32[]{:S(2)}) collective-permute-start(bf16[2,3,2,48,256]{4,3,2,1,0:T(8,128)(2,1)} %get-tuple-element.70.refs_0_), channel_id=1, source_target_pairs={{8,16},{16,8},{9,17},{17,9},{10,18},{18,10},{11,19},{19,11},{12,20... | collective-permute-start | bytes 884744 | tf_op jit(solution)/shard_map/ppermute | solution.py:431
  101.3 31.0 %collective-permute-start.17 = (bf16[2,3,2,48,256]{4,3,2,1,0:T(8,128)(2,1)}, bf16[2,3,2,48,256]{4,3,2,1,0:T(8,128)(2,1)S(1)}, u32[]{:S(2)}, u32[]{:S(2)}) collective-permute-start(bf16[2,3,2,48,256]{4,3,2,1,0:T(8,128)(2,1)} %get-tuple-element.70.refs_0_), channel_id=1, source_target_pairs={{0,16},{8,24},{16,0},{24,8},{1,17},{9,25},{17,1},{25,9},{2,18},{10... | collective-permute-start | bytes 884744 | tf_op jit(solution)/shard_map/ppermute | solution.py:429
  105.7 27.2 %collective-permute-start.16 = (bf16[2,3,2,48,256]{4,3,2,1,0:T(8,128)(2,1)}, bf16[2,3,2,48,256]{4,3,2,1,0:T(8,128)(2,1)S(1)}, u32[]{:S(2)}, u32[]{:S(2)}) collective-permute-start(bf16[2,3,2,48,256]{4,3,2,1,0:T(8,128)(2,1)} %get-tuple-element.70.refs_0_), channel_id=1, source_target_pairs={{0,8},{8,0},{16,24},{24,16},{1,9},{9,1},{17,25},{25,17},{2,10},{10... | collective-permute-start | bytes 884744 | tf_op jit(solution)/shard_map/ppermute | solution.py:430
  105.9 9.1 %collective-permute-start.15 = (bf16[5,2,48,256]{3,2,1,0:T(8,128)(2,1)S(1)}, bf16[5,2,48,256]{3,2,1,0:T(8,128)(2,1)S(1)}, u32[]{:S(2)}, u32[]{:S(2)}) collective-permute-start(bf16[5,2,48,256]{3,2,1,0:T(8,128)(2,1)S(1)} %copy-done.30), channel_id=1, source_target_pairs={{0,7},{1,6},{2,5},{3,4},{4,3},{5,2},{6,1},{7,0},{8,15},{9,14},{10,... | collective-permute-start | bytes 737288 | tf_op jit(solution)/shard_map/ppermute | solution.py:470
  106.2 13.1 %collective-permute-start.13 = (bf16[5,2,48,256]{3,2,1,0:T(8,128)(2,1)S(1)}, bf16[5,2,48,256]{3,2,1,0:T(8,128)(2,1)S(1)}, u32[]{:S(2)}, u32[]{:S(2)}) collective-permute-start(bf16[5,2,48,256]{3,2,1,0:T(8,128)(2,1)S(1)} %copy-done.29), channel_id=1, source_target_pairs={{0,6},{1,7},{2,4},{3,5},{4,2},{5,3},{6,0},{7,1},{8,14},{9,15},{10,... | collective-permute-start | bytes 737288 | tf_op jit(solution)/shard_map/ppermute | solution.py:470
  115.0 25.2 %copy-start.9 = (bf16[5,2,48,256]{3,2,1,0:T(8,128)(2,1)}, bf16[5,2,48,256]{3,2,1,0:T(8,128)(2,1)S(1)}, u32[]{:S(2)}) copy-start(bf16[5,2,48,256]{3,2,1,0:T(8,128)(2,1)S(1)} %collective-permute-done.15.refs_7_) | copy-start | bytes 737284
  115.0 18.0 %collective-permute-start.11 = (bf16[5,2,48,256]{3,2,1,0:T(8,128)(2,1)S(1)}, bf16[5,2,48,256]{3,2,1,0:T(8,128)(2,1)S(1)}, u32[]{:S(2)}, u32[]{:S(2)}) collective-permute-start(bf16[5,2,48,256]{3,2,1,0:T(8,128)(2,1)S(1)} %copy-done.28), channel_id=1, source_target_pairs={{0,5},{1,4},{2,7},{3,6},{4,1},{5,0},{6,3},{7,2},{8,13},{9,12},{10,... | collective-permute-start | bytes 737288 | tf_op jit(solution)/shard_map/ppermute | solution.py:470
  119.3 20.9 %copy-start.10 = (bf16[5,2,48,256]{3,2,1,0:T(8,128)(2,1)}, bf16[5,2,48,256]{3,2,1,0:T(8,128)(2,1)S(1)}, u32[]{:S(2)}) copy-start(bf16[5,2,48,256]{3,2,1,0:T(8,128)(2,1)S(1)} %collective-permute-done.13.refs_6_) | copy-start | bytes 737284
  119.3 13.7 %collective-permute-start.9 = (bf16[5,2,48,256]{3,2,1,0:T(8,128)(2,1)S(1)}, bf16[5,2,48,256]{3,2,1,0:T(8,128)(2,1)S(1)}, u32[]{:S(2)}, u32[]{:S(2)}) collective-permute-start(bf16[5,2,48,256]{3,2,1,0:T(8,128)(2,1)S(1)} %copy-done.27), channel_id=1, source_target_pairs={{0,4},{1,5},{2,6},{3,7},{4,0},{5,1},{6,2},{7,3},{8,12},{9,13},{10,... | collective-permute-start | bytes 737288 | tf_op jit(solution)/shard_map/ppermute | solution.py:470
  119.3 26.3 %copy-start.5 = (bf16[2,3,2,48,256]{4,3,2,1,0:T(8,128)(2,1)}, bf16[2,3,2,48,256]{4,3,2,1,0:T(8,128)(2,1)S(1)}, u32[]{:S(2)}) copy-start(bf16[2,3,2,48,256]{4,3,2,1,0:T(8,128)(2,1)S(1)} %collective-permute-done.18.refs_3_) | copy-start | bytes 884740
  119.3 13.7 %collective-permute-start.7 = (bf16[5,2,48,256]{3,2,1,0:T(8,128)(2,1)S(1)}, bf16[5,2,48,256]{3,2,1,0:T(8,128)(2,1)S(1)}, u32[]{:S(2)}, u32[]{:S(2)}) collective-permute-start(bf16[5,2,48,256]{3,2,1,0:T(8,128)(2,1)S(1)} %copy-done.26), channel_id=1, source_target_pairs={{0,3},{1,2},{2,1},{3,0},{4,7},{5,6},{6,5},{7,4},{8,11},{9,10},{10,... | collective-permute-start | bytes 737288 | tf_op jit(solution)/shard_map/ppermute | solution.py:470
  132.3 38.9 %copy-start.6 = (bf16[2,3,2,48,256]{4,3,2,1,0:T(8,128)(2,1)}, bf16[2,3,2,48,256]{4,3,2,1,0:T(8,128)(2,1)S(1)}, u32[]{:S(2)}) copy-start(bf16[2,3,2,48,256]{4,3,2,1,0:T(8,128)(2,1)S(1)} %collective-permute-done.17.refs_2_) | copy-start | bytes 884740
  132.3 7.9 %collective-permute-start.5 = (bf16[5,2,48,256]{3,2,1,0:T(8,128)(2,1)S(1)}, bf16[5,2,48,256]{3,2,1,0:T(8,128)(2,1)S(1)}, u32[]{:S(2)}, u32[]{:S(2)}) collective-permute-start(bf16[5,2,48,256]{3,2,1,0:T(8,128)(2,1)S(1)} %copy-done.25), channel_id=1, source_target_pairs={{0,2},{1,3},{2,0},{3,1},{4,6},{5,7},{6,4},{7,5},{8,10},{9,11},{10,... | collective-permute-start | bytes 737288 | tf_op jit(solution)/shard_map/ppermute | solution.py:470
  132.8 12.8 %copy-start.7 = (bf16[2,3,2,48,256]{4,3,2,1,0:T(8,128)(2,1)}, bf16[2,3,2,48,256]{4,3,2,1,0:T(8,128)(2,1)S(1)}, u32[]{:S(2)}) copy-start(bf16[2,3,2,48,256]{4,3,2,1,0:T(8,128)(2,1)S(1)} %collective-permute-done.16.refs_1_) | copy-start | bytes 884740
  132.8 7.3 %collective-permute-start.3 = (bf16[5,2,48,256]{3,2,1,0:T(8,128)(2,1)S(1)}, bf16[5,2,48,256]{3,2,1,0:T(8,128)(2,1)S(1)}, u32[]{:S(2)}, u32[]{:S(2)}) collective-permute-start(bf16[5,2,48,256]{3,2,1,0:T(8,128)(2,1)S(1)} %copy-done.24), channel_id=1, source_target_pairs={{0,1},{1,0},{2,3},{3,2},{4,5},{5,4},{6,7},{7,6},{8,9},{9,8},{10,11... | collective-permute-start | bytes 737288 | tf_op jit(solution)/shard_map/ppermute | solution.py:470
  132.9 7.3 %copy-start.11 = (bf16[5,2,48,256]{3,2,1,0:T(8,128)(2,1)}, bf16[5,2,48,256]{3,2,1,0:T(8,128)(2,1)S(1)}, u32[]{:S(2)}) copy-start(bf16[5,2,48,256]{3,2,1,0:T(8,128)(2,1)S(1)} %collective-permute-done.11.refs_5_) | copy-start | bytes 737284
  133.0 7.3 %copy-start.12 = (bf16[5,2,48,256]{3,2,1,0:T(8,128)(2,1)}, bf16[5,2,48,256]{3,2,1,0:T(8,128)(2,1)S(1)}, u32[]{:S(2)}) copy-start(bf16[5,2,48,256]{3,2,1,0:T(8,128)(2,1)S(1)} %collective-permute-done.9.refs_4_) | copy-start | bytes 737284
  133.0 7.3 %copy-start.13 = (bf16[5,2,48,256]{3,2,1,0:T(8,128)(2,1)}, bf16[5,2,48,256]{3,2,1,0:T(8,128)(2,1)S(1)}, u32[]{:S(2)}) copy-start(bf16[5,2,48,256]{3,2,1,0:T(8,128)(2,1)S(1)} %collective-permute-done.7.refs_3_) | copy-start | bytes 737284
  145.6 24.3 %collective-permute-start.20 = (bf16[2,5,2,48,256]{4,3,2,1,0:T(8,128)(2,1)}, bf16[2,5,2,48,256]{4,3,2,1,0:T(8,128)(2,1)S(1)}, u32[]{:S(2)}, u32[]{:S(2)}) collective-permute-start(bf16[2,5,2,48,256]{4,3,2,1,0:T(8,128)(2,1)} %get-tuple-element.74.refs_0_), channel_id=1, source_target_pairs={{0,16},{8,24},{16,0},{24,8},{1,17},{9,25},{17,1},{25,9},{2,18},{10... | collective-permute-start | bytes 1474568 | tf_op jit(solution)/shard_map/ppermute | solution.py:429
  145.7 48.9 %collective-permute-start.21 = (bf16[2,5,2,48,256]{4,3,2,1,0:T(8,128)(2,1)}, bf16[2,5,2,48,256]{4,3,2,1,0:T(8,128)(2,1)S(1)}, u32[]{:S(2)}, u32[]{:S(2)}) collective-permute-start(bf16[2,5,2,48,256]{4,3,2,1,0:T(8,128)(2,1)} %get-tuple-element.74.refs_0_), channel_id=1, source_target_pairs={{8,16},{16,8},{9,17},{17,9},{10,18},{18,10},{11,19},{19,11},{12,20... | collective-permute-start | bytes 1474568 | tf_op jit(solution)/shard_map/ppermute | solution.py:431
  146.4 48.3 %collective-permute-start.19 = (bf16[2,5,2,48,256]{4,3,2,1,0:T(8,128)(2,1)}, bf16[2,5,2,48,256]{4,3,2,1,0:T(8,128)(2,1)S(1)}, u32[]{:S(2)}, u32[]{:S(2)}) collective-permute-start(bf16[2,5,2,48,256]{4,3,2,1,0:T(8,128)(2,1)} %get-tuple-element.74.refs_0_), channel_id=1, source_target_pairs={{0,8},{8,0},{16,24},{24,16},{1,9},{9,1},{17,25},{25,17},{2,10},{10... | collective-permute-start | bytes 1474568 | tf_op jit(solution)/shard_map/ppermute | solution.py:430
  169.9 24.7 %copy-start.1 = (bf16[2,5,2,48,256]{4,3,2,1,0:T(8,128)(2,1)}, bf16[2,5,2,48,256]{4,3,2,1,0:T(8,128)(2,1)S(1)}, u32[]{:S(2)}) copy-start(bf16[2,5,2,48,256]{4,3,2,1,0:T(8,128)(2,1)S(1)} %collective-permute-done.20.refs_2_) | copy-start | bytes 1474564
  169.9 24.8 %collective-permute-start.22 = (bf16[2,5,2,48,256]{4,3,2,1,0:T(8,128)(2,1)S(1)}, bf16[2,5,2,48,256]{4,3,2,1,0:T(8,128)(2,1)S(1)}, u32[]{:S(2)}, u32[]{:S(2)}) collective-permute-start(bf16[2,5,2,48,256]{4,3,2,1,0:T(8,128)(2,1)S(1)} %collective-permute-done.20.refs_2_), channel_id=1, source_target_pairs={{16,24},{8,0},{17,25},{9,1},{18,26},{10,2},{19,27},{11,3},{20,28},... | collective-permute-start | bytes 1474568 | tf_op jit(solution)/shard_map/ppermute | solution.py:432
  171.2 19.8 %collective-permute-start.23 = (bf16[2,3,2,48,256]{4,3,2,1,0:T(8,128)(2,1)S(1)}, bf16[2,3,2,48,256]{4,3,2,1,0:T(8,128)(2,1)S(1)}, u32[]{:S(2)}, u32[]{:S(2)}) collective-permute-start(bf16[2,3,2,48,256]{4,3,2,1,0:T(8,128)(2,1)S(1)} %collective-permute-done.17.refs_2_), channel_id=1, source_target_pairs={{16,24},{8,0},{17,25},{9,1},{18,26},{10,2},{19,27},{11,3},{20,28},... | collective-permute-start | bytes 884744 | tf_op jit(solution)/shard_map/ppermute | solution.py:432
  (16 other events, 32.7 us)
Sparse Core Ops, SparseCore 0:
  10.1 39.1 all-gather.2
  78.8 39.8 reduce-scatter.1

commit v7 on v6

--- a/solution.py
+++ b/solution.py
@@ -357,37 +357,21 @@
     )(pos, *arrived, weights, moment1, moment2, *before)
 
 
-def place_weights(pos, pieces, start, half, before):
-    n_dp = len(pieces)
-    _, size, _, piece, width = pieces[0].shape
-    pieces = list(pieces)
-    far = isinstance(pieces[-1], tuple)
-    if far:
-        pieces[-1:] = pieces[-1]
-    n_in = len(pieces)
-
-    def body(pos_ref, *refs):
+def place_weights(gathered, start, half, before):
+    n_dp, _, size, _, piece, width = gathered.shape
+
+    def body(gathered_ref, *refs):
         out_ref, held, sems, sem_out = refs[-4:]
-        dp_at = pos_ref[0]
-        inner = (dp_at > 0) & (dp_at < n_dp - 1)
-
-        def each(act):
-            for j in range(n_dp):
-                columns = pl.ds(pl.multiple_of((dp_at ^ j) * width, 128), width)
-
-                def copy(i, j=j, columns=columns):
-                    return pltpu.make_async_copy(
-                        refs[i], held.at[:, :, :, :, columns], sems.at[j]
-                    )
-
-                if far and j == n_dp - 1:
-                    pl.when(inner)(lambda: act(copy(j)))
-                    pl.when(~inner)(lambda: act(copy(j + 1)))
-                else:
-                    act(copy(j))
-
-        each(lambda copy: copy.start())
-        each(lambda copy: copy.wait())
+        copies = [
+            pltpu.make_async_copy(
+                gathered_ref.at[d], held.at[:, :, :, :, pl.ds(d * width, width)], sems.at[d]
+            )
+            for d in range(n_dp)
+        ]
+        for copy in copies:
+            copy.start()
+        for copy in copies:
+            copy.wait()
         outs = [
             pltpu.make_async_copy(
                 held.at[h], out_ref.at[pl.ds(h * half + start, size)], sem_out.at[h]
@@ -403,53 +387,43 @@
     return pl.pallas_call(
         body,
         out_shape=jax.ShapeDtypeStruct((2 * half, 2, piece, n_dp * width), jnp.bfloat16),
-        in_specs=[smem()] + [anywhere] * (n_in + len(before)),
+        in_specs=[anywhere] * (1 + len(before)),
         out_specs=anywhere,
         scratch_shapes=[
             pltpu.VMEM((2, size, 2, piece, n_dp * width), jnp.bfloat16),
             pltpu.SemaphoreType.DMA((n_dp,)),
             pltpu.SemaphoreType.DMA((2,)),
         ],
-        input_output_aliases={1 + n_in: 0} if before else {},
+        input_output_aliases={1: 0} if before else {},
         compiler_params=params(),
         name="place_weights",
-    )(pos, *pieces, *before)
+    )(gathered, *before)
 
 
 def after(value, *others):
     return lax.optimization_barrier((value,) + others)[0]
 
 
-def gather_planes(fresh, dp_at, n_dp, before):
-    if n_dp != 4:
-        whole = lax.all_gather(fresh, "dp", axis=0)
-        return [
-            lax.dynamic_index_in_dim(whole, dp_at ^ j, 0, keepdims=False) for j in range(n_dp)
-        ]
-    two = lax.ppermute(fresh, "dp", [(0, 2), (1, 3), (2, 0), (3, 1)])
-    one = lax.ppermute(fresh, "dp", [(0, 1), (1, 0), (2, 3), (3, 2)])
-    middle = lax.ppermute(fresh, "dp", [(1, 2), (2, 1)])
-    outer = lax.ppermute(after(two, *before), "dp", [(2, 3), (1, 0)])
-    return [fresh, one, two, (middle, outer)]
-
-
-def finish_predicted(perm, total):
-    def body(perm_ref, total_ref, out_ref):
-        out_ref[...] = lax.dot_general(
+def finish_predicted(perm, parts):
+    def body(perm_ref, *refs):
+        total = refs[0][...].astype(jnp.float32)
+        for ref in refs[1:-1]:
+            total = total + ref[...].astype(jnp.float32)
+        refs[-1][...] = lax.dot_general(
             perm_ref[...],
-            total_ref[...].astype(jnp.bfloat16),
+            total.astype(jnp.bfloat16),
             (((0,), (0,)), ((), ())),
             preferred_element_type=jnp.float32,
         ).astype(jnp.bfloat16)
 
     return pl.pallas_call(
         body,
-        out_shape=jax.ShapeDtypeStruct(total.shape, jnp.bfloat16),
-        in_specs=[vmem(), vmem()],
+        out_shape=jax.ShapeDtypeStruct(parts[0].shape, jnp.bfloat16),
+        in_specs=[vmem()] * (1 + len(parts)),
         out_specs=vmem(),
         compiler_params=params(),
         name="finish_predicted",
-    )(perm, total)
+    )(perm, *parts)
 
 
 def shards(signals, cotangent, row_insertion, touched, slot_map, weights, moment1, moment2):
@@ -487,25 +461,29 @@
         for j in range(1, n_own if arrived else 1):
             chunk[j] = after(chunk[j], arrived[-1][j])
         arrived.append([chunk[0]] + [across(chunk[j], j) for j in range(1, n_own)])
-    pred_other = across(after(pred_other, arrived[0][1]), 1)
-    pred_part = pred_mine.astype(jnp.float32) + pred_other.astype(jnp.float32)
-    total = lax.psum_scatter(pred_part, "dp", scatter_dimension=0)
+    pred_part = pred_mine + across(pred_other, 1)
+
+    def of_plane(j):
+        return lax.dynamic_index_in_dim(pred_part, dp_at ^ j, 0, keepdims=False)
+
+    parts = [of_plane(0)] + [
+        lax.ppermute(of_plane(j), "dp", [(d, d ^ j) for d in range(n_dp)]) for j in range(1, n_dp)
+    ]
+    arrived[-1][-1] = after(arrived[-1][-1], *parts[1:])
+    arrived[0][-1] = after(arrived[0][-1], pred_part)
 
     moments = []
     new_weights = []
     start = 0
-    for i, size in enumerate(sizes):
-        ready = list(arrived[i])
-        ready[-1] = after(ready[-1], *(jax.tree.leaves(pieces[1:])[:n_dp - 1] if i else [pred_part]))
+    for size, ready in zip(sizes, arrived):
         fresh, *moments = adam(pos, ready, weights, moment1, moment2, start, moments)
-        later = arrived[i + 1][1 : n_own // 2 + 1] if i + 1 < len(sizes) else []
-        pieces = gather_planes(fresh, dp_at, n_dp, later)
-        new_weights = [place_weights(pos, pieces, start, half, new_weights)]
+        gathered = lax.all_gather(fresh, "dp", axis=0)
+        new_weights = [place_weights(gathered, start, half, new_weights)]
         start += size
     new_weights = new_weights[0]
     new_moment1, new_moment2 = moments
 
-    predicted = finish_predicted(perm, total)
+    predicted = finish_predicted(perm, parts)
     return (predicted, new_weights, new_moment1, new_moment2)
 
 

time: 211 us -> 200 us (0.948)
  starting transfers between devices: 28.3 us -> 21.4 us
  local copies, waits for them, and re-layouts: 10.3 us -> 7.8 us
    all_gather x0 -> x2, waiting for transfers between devices: none -> 37.2 us  [shards(): gathered = lax.all_gather(fresh, 'dp', axis=0)]
    ppermute x8 -> x3, waiting for transfers between devices: 48.4 us -> 26 us  [shards(): lax.ppermute(of_plane(j), 'dp', [(d, d ^ j) for d in range(n_dp)])]
    ppermute x16, waiting for transfers between devices: 33 us -> 20.3 us  [across(): return lax.ppermute(value, 'own', [(o, o ^ j) for o in range(n_own)])]
    ppermute x8 -> x3, starting transfers between devices: 13.3 us -> 4.39 us  [shards(): lax.ppermute(of_plane(j), 'dp', [(d, d ^ j) for d in range(n_dp)])]
    unnamed x75 -> x53, local copies, waits for them, and re-layouts: 7.04 us -> 3.79 us
  transfers between devices with their start and end apart: 27 -> 23, of which waited for: 15 -> 12; matrix products, arithmetic and copies ran while one was open for 2% -> 3% of each run, Pallas kernels for 7% -> 5%
where the time goes in v7:
time: 200 us; the launch traced here: 198 us
  waiting for transfers between devices  119 us (60%)
  Pallas kernels  33.9 us (17%)
  starting transfers between devices  21.4 us (11%)
  between operations  14.1 us (7%)
  local copies, waits for them, and re-layouts  7.8 us (4%)
    all_gather x2, waiting for transfers between devices, shards(): gathered = lax.all_gather(fresh, 'dp', axis=0)  37.2 us
    all_gather x1, waiting for transfers between devices, shards(): planes = lax.all_gather(packed, 'dp', axis=0)  32 us
    ppermute x3, waiting for transfers between devices, shards(): lax.ppermute(of_plane(j), 'dp', [(d, d ^ j) for d in range(n_dp)])  26 us
    ppermute x16, waiting for transfers between devices, across(): return lax.ppermute(value, 'own', [(o, o ^ j) for o in range(n_own)])  20.3 us
    pallas_call x1, Pallas kernels, local_grads(): pl.pallas_call(body, out_shape=[pred_shape, pred_shape] + grad_shapes, in...  15.8 us
    ppermute x16, starting transfers between devices, across(): return lax.ppermute(value, 'own', [(o, o ^ j) for o in range(n_own)])  12.5 us
    pallas_call x2, Pallas kernels, adam(): pl.pallas_call(body, out_shape=[jax.ShapeDtypeStruct(blocks, jnp.bfloat16...  8.47 us
    pallas_call x2, Pallas kernels, place_weights(): pl.pallas_call(body, out_shape=jax.ShapeDtypeStruct((2 * half, 2, piece,...  5.08 us
  transfers between devices with their start and end apart: 23, of which 12 were waited for; matrix products, arithmetic and copies ran while one was open for 3% of the time, Pallas kernels for 5%

profile of v7, /device:TPU:2, one launch (start us, length us, event | category | flops | bytes accessed | tf_op | source)
XLA Modules:
  0.0 197.7 jit_solution(17264217560935838862)
XLA Ops:
  7.2 0.0 all-gather.7.cloned.1.call-start
  7.2 2.4 %pack_rows.1 = (bf16[528,384]{1,0:T(8,128)(2,1)}, bf16[256,256]{1,0:T(8,128)(2,1)}) custom-call(s32[1,256]{1,0:T(1,128)} %bitcast.22, bf16[256,384]{1,0:T(8,128)(2,1)} %sig_ref.1, bf16[256,384]{1,0:T(8,128)(2,1)} %cot_ref.1), custom_call_target="tpu_custom_call" | custom-call | tf_op jit(solution)/shard_map/pack_rows/pallas_call | solution.py:79
  9.6 0.0 all-gather.7.cloned.1.call-update
  9.6 1.2 constant_dynamic-slice_fusion
  10.8 2.0 %broadcast_in_dim.8 = bf16[4,2,8,2,48,256]{5,4,3,2,1,0:T(8,128)(2,1)} broadcast(bf16[2,8,2,48,256]{4,3,2,1,0:T(8,128)(2,1)S(1)} %bitcast.17), dimensions={1,2,3,4,5} | broadcast | bytes 3932160 | tf_op jit(solution)/shard_map/broadcast_in_dim | solution.py:450
  12.9 4.4 %all-to-all-start = ((bf16[8,8,2,48,256]{4,3,2,1,0:T(8,128)(2,1)}), bf16[8,8,2,48,256]{4,3,2,1,0:T(8,128)(2,1)S(1)}, u32[]{:S(2)}, u32[]{:S(2)}) async-start(bf16[8,8,2,48,256]{4,3,2,1,0:T(8,128)(2,1)} %bitcast.16), calls=%async_computation | async-start | bytes 6291456 | tf_op jit(solution)/shard_map/all_to_all | solution.py:453
  17.3 32.0 %all-gather.7.cloned.1.call-done = bf16[2112,384]{1,0:T(8,128)(2,1)} async-done(((bf16[528,384]{1,0:T(8,128)(2,1)}), bf16[2112,384]{1,0:T(8,128)(2,1)}) %all-gather.7.cloned.1.call-update) | async-done | bytes 1622032 | tf_op jit(solution)/shard_map/all_gather | solution.py:447
  49.3 0.7 copy.16.touched_ref
  50.0 0.6 pad_add_fusion.pos_ref
  50.6 3.0 %all-to-all-done.rest_2_ = bf16[8,8,2,48,256]{4,3,2,1,0:T(8,128)(2,1)S(1)} async-done(((bf16[8,8,2,48,256]{4,3,2,1,0:T(8,128)(2,1)}), bf16[8,8,2,48,256]{4,3,2,1,0:T(8,128)(2,1)S(1)}, u32[]{:S(2)}, u32[]{:S(2)}) %all-to-all-start) | async-done | bytes 3145760 | tf_op jit(solution)/shard_map/all_to_all | solution.py:453
  53.7 1.7 copy-done
  55.3 15.8 %local_grads.1 = (bf16[4,256,384]{2,1,0:T(8,128)(2,1)}, bf16[4,256,384]{2,1,0:T(8,128)(2,1)}, bf16[3,2,48,256]{3,2,1,0:T(8,128)(2,1)}, bf16[3,2,48,256]{3,2,1,0:...) custom-call(s32[2]{0:T(128)} %pad_add_fusion.pos_ref, ...), custom_call_target="tpu_custom_call" | custom-call | tf_op jit(solution)/shard_map/local_grads/pallas_call | solution.py:241
  71.1 0.1 collective-permute-start.1
  71.2 0.5 collective-permute-start.5
  71.7 0.3 collective-permute-start.17
  72.0 3.0 %collective-permute-start.7 = (bf16[3,2,48,256]{3,2,1,0:T(8,128)(2,1)}, bf16[3,2,48,256]{3,2,1,0:T(8,128)(2,1)S(1)}, u32[]{:S(2)}, u32[]{:S(2)}) collective-permute-start(bf16[3,2,48,256]{3,2,1,0:T(8,128)(2,1)} %get-tuple-element.48), channel_id=1, source_target_pairs={{0,2},{1,3},{2,0},{3,1},{4,6},{5,7},{6,4},{7,5},{8,10},{9,11},{10,... | collective-permute-start | bytes 442376 | tf_op jit(solution)/shard_map/ppermute | solution.py:444
  75.0 0.7 collective-permute-start.11
  75.7 3.0 %collective-permute-done.17.refs_7_ = bf16[3,2,48,256]{3,2,1,0:T(8,128)(2,1)S(1)} collective-permute-done((bf16[3,2,48,256]{3,2,1,0:T(8,128)(2,1)}, bf16[3,2,48,256]{3,2,1,0:T(8,128)(2,1)S(1)}, u32[]{:S(2)}, u32[]{:S(2)}) %collective-permute-start.17) | collective-permute-done | bytes 147488 | tf_op jit(solution)/shard_map/ppermute | solution.py:444
  78.7 2.0 %collective-permute-start.13 = (bf16[3,2,48,256]{3,2,1,0:T(8,128)(2,1)}, bf16[3,2,48,256]{3,2,1,0:T(8,128)(2,1)S(1)}, u32[]{:S(2)}, u32[]{:S(2)}) collective-permute-start(bf16[3,2,48,256]{3,2,1,0:T(8,128)(2,1)} %get-tuple-element.57), channel_id=1, source_target_pairs={{0,5},{1,4},{2,7},{3,6},{4,1},{5,0},{6,3},{7,2},{8,13},{9,12},{10,... | collective-permute-start | bytes 442376 | tf_op jit(solution)/shard_map/ppermute | solution.py:444
  80.7 1.3 add.20
  82.1 0.9 collective-permute-done.7.refs_2_
  83.0 2.0 %collective-permute-done.9.refs_3_ = bf16[3,2,48,256]{3,2,1,0:T(8,128)(2,1)S(1)} collective-permute-done((bf16[3,2,48,256]{3,2,1,0:T(8,128)(2,1)}, bf16[3,2,48,256]{3,2,1,0:T(8,128)(2,1)S(1)}, u32[]{:S(2)}, u32[]{:S(2)}) %collective-permute-start.9) | collective-permute-done | bytes 147488 | tf_op jit(solution)/shard_map/ppermute | solution.py:444
  85.0 0.3 collective-permute-done.13.refs_5_
  85.3 3.2 %collective-permute-done.15.refs_6_ = bf16[3,2,48,256]{3,2,1,0:T(8,128)(2,1)S(1)} collective-permute-done((bf16[3,2,48,256]{3,2,1,0:T(8,128)(2,1)}, bf16[3,2,48,256]{3,2,1,0:T(8,128)(2,1)S(1)}, u32[]{:S(2)}, u32[]{:S(2)}) %collective-permute-start.15) | collective-permute-done | bytes 147488 | tf_op jit(solution)/shard_map/ppermute | solution.py:444
  88.6 0.6 copy-done.17
  89.2 3.9 %adam_step.2 = (bf16[2,3,2,48,256]{4,3,2,1,0:T(8,128)(2,1)}, f32[16,2,48,256]{3,2,1,0:T(8,128)}, f32[16,2,48,256]{3,2,1,0:T(8,128)}) custom-call(s32[2]{0:T(128)} %pad_add_fusion.pos_ref, bf16[3,2,48,256]{3,2,1,0:T(8,128)(2,1)} %get-tuple-element.66.refs_0_, bf16[3,2,48,256]{3,2,1,0:T(8,128)(2,1)} %copy-done.11, bf16[3,2,48,256]{3,2,1,0:T(8,128)(2,1)} %copy-done.13, ...), custom_call_target="tpu_custom_call" | custom-call | tf_op jit(solution)/shard_map/adam_step/pallas_call | solution.py:333
  93.1 0.0 all-gather.9.cloned.1.call-start
  93.2 0.4 collective-permute-start.18
  93.6 2.4 %collective-permute-start.16 = (bf16[5,2,48,256]{3,2,1,0:T(8,128)(2,1)S(1)}, bf16[5,2,48,256]{3,2,1,0:T(8,128)(2,1)S(1)}, u32[]{:S(2)}, u32[]{:S(2)}) collective-permute-start(bf16[5,2,48,256]{3,2,1,0:T(8,128)(2,1)S(1)} %copy-done.24), channel_id=1, source_target_pairs={{0,6},{1,7},{2,4},{3,5},{4,2},{5,3},{6,0},{7,1},{8,14},{9,15},{10,... | collective-permute-start | bytes 737288 | tf_op jit(solution)/shard_map/ppermute | solution.py:444
  95.9 0.8 dynamic-slice_bitcast_fusion
  96.7 3.6 %collective-permute-start.4 = (bf16[256,384]{1,0:T(8,128)(2,1)S(1)}, bf16[256,384]{1,0:T(8,128)(2,1)S(1)}, u32[]{:S(2)}, u32[]{:S(2)}) collective-permute-start(bf16[256,384]{1,0:T(8,128)(2,1)S(1)} %get-tuple-element.74), channel_id=1, source_target_pairs={{0,24},{8,16},{16,8},{24,0},{1,25},{9,17},{17,9},{25,1},{2,26},{10... | collective-permute-start | bytes 589832 | tf_op jit(solution)/shard_map/ppermute | solution.py:470
  100.3 0.8 collective-permute-start.2
  101.1 1.0 collective-permute-done.18.refs_7_
  102.1 1.2 collective-permute-start.14
  103.3 4.5 %collective-permute-done.16.refs_6_ = bf16[5,2,48,256]{3,2,1,0:T(8,128)(2,1)S(1)} collective-permute-done((bf16[5,2,48,256]{3,2,1,0:T(8,128)(2,1)S(1)}, bf16[5,2,48,256]{3,2,1,0:T(8,128)(2,1)S(1)}, u32[]{:S(2)}, u32[]{:S(2)}) %collective-permute-start.16) | collective-permute-done | bytes 245792 | tf_op jit(solution)/shard_map/ppermute | solution.py:444
  107.8 1.1 collective-permute-start.12
  108.9 0.1 collective-permute-start.10
  109.0 26.0 %collective-permute-done.3.refs_2_ = bf16[256,384]{1,0:T(8,128)(2,1)S(1)} collective-permute-done((bf16[256,384]{1,0:T(8,128)(2,1)S(1)}, bf16[256,384]{1,0:T(8,128)(2,1)S(1)}, u32[]{:S(2)}, u32[]{:S(2)}) %collective-permute-start.3) | collective-permute-done | bytes 196640 | tf_op jit(solution)/shard_map/ppermute | solution.py:470
  135.0 0.7 collective-permute-start.8
  135.7 0.1 collective-permute-start.6
  135.9 5.4 %collective-permute-done.8.refs_2_ = bf16[5,2,48,256]{3,2,1,0:T(8,128)(2,1)S(1)} collective-permute-done((bf16[5,2,48,256]{3,2,1,0:T(8,128)(2,1)S(1)}, bf16[5,2,48,256]{3,2,1,0:T(8,128)(2,1)S(1)}, u32[]{:S(2)}, u32[]{:S(2)}) %collective-permute-start.8) | collective-permute-done | bytes 245792 | tf_op jit(solution)/shard_map/ppermute | solution.py:444
  141.3 0.6 copy-done.6
  141.9 0.1 copy-done.7
  142.0 4.6 %adam_step.3 = (bf16[2,5,2,48,256]{4,3,2,1,0:T(8,128)(2,1)}, f32[16,2,48,256]{3,2,1,0:T(8,128)}, f32[16,2,48,256]{3,2,1,0:T(8,128)}) custom-call(s32[2]{0:T(128)} %pad_add_fusion.pos_ref, bf16[5,2,48,256]{3,2,1,0:T(8,128)(2,1)} %get-tuple-element.43.refs_0_, bf16[5,2,48,256]{3,2,1,0:T(8,128)(2,1)} %copy-done.7, ...), custom_call_target="tpu_custom_call", output_to_operand_aliasing={{1}: (12, {}), {2}: (13, {})} | custom-call | tf_op jit(solution)/shard_map/adam_step/pallas_call | solution.py:333
  146.7 2.2 %finish_predicted.1 = bf16[256,384]{1,0:T(8,128)(2,1)} custom-call(bf16[256,256]{1,0:T(8,128)(2,1)} %get-tuple-element.39.perm_ref, bf16[256,384]{1,0:T(8,128)(2,1)} %get-tuple-element.77.refs_0_, bf16[256,384]{1,0:T(8,128)(2,1)} %copy-done.10, bf16[256,384]{1,0:T(8,128)(2,1)} %copy-done.9, bf16[256,384]{1,0:T(8,128)(2,1)} %copy-done.8), custom_call_target="tpu_custom_call" | custom-call | tf_op jit(solution)/shard_map/finish_predicted/pallas_call | solution.py:419
  148.9 2.3 %place_weights.2.refs_0_ = bf16[16,2,48,1024]{3,2,1,0:T(8,128)(2,1)} custom-call(bf16[4,2,3,2,48,256]{5,4,3,2,1,0:T(8,128)(2,1)} %bitcast.21), custom_call_target="tpu_custom_call" | custom-call | tf_op jit(solution)/shard_map/place_weights/pallas_call | solution.py:387
  151.2 37.2 %all-gather.9.cloned.1.call-done = bf16[8,5,2,48,256]{4,3,2,1,0:T(8,128)(2,1)} async-done(((bf16[2,5,2,48,256]{4,3,2,1,0:T(8,128)(2,1)}), bf16[8,5,2,48,256]{4,3,2,1,0:T(8,128)(2,1)}) %all-gather.9.cloned.1.call-update) | async-done | bytes 1966096 | tf_op jit(solution)/shard_map/all_gather | solution.py:480
  188.4 2.8 %place_weights.3 = bf16[16,2,48,1024]{3,2,1,0:T(8,128)(2,1)} custom-call(bf16[4,2,5,2,48,256]{5,4,3,2,1,0:T(8,128)(2,1)} %bitcast.18, bf16[16,2,48,1024]{3,2,1,0:T(8,128)(2,1)} %place_weights.2.refs_0_), custom_call_target="tpu_custom_call", output_to_operand_aliasing={{}: (1, {})} | custom-call | tf_op jit(solution)/shard_map/place_weights/pallas_call | solution.py:387
  (66 shorter events, 0.2 us)
Async XLA Ops:
  7.2 42.1 %all-gather.7.cloned.1.call-start = ((), (), s32[]{:S(2)}) async-start(), calls=%async_computation.1 | async-start | bytes 2027520 | tf_op jit(solution)/shard_map/all_gather | solution.py:447
  12.9 36.4 %copy-start.18 = (s32[32,4]{0,1:T(4,128)S(1)}, s32[32,4]{0,1:T(4,128)}, u32[]{:S(2)}) copy-start(s32[32,4]{0,1:T(4,128)} %param.11) | copy-start | bytes 1540
  12.9 40.8 %all-to-all-start = ((bf16[8,8,2,48,256]{4,3,2,1,0:T(8,128)(2,1)}), bf16[8,8,2,48,256]{4,3,2,1,0:T(8,128)(2,1)S(1)}, u32[]{:S(2)}, u32[]{:S(2)}) async-start(bf16[8,8,2,48,256]{4,3,2,1,0:T(8,128)(2,1)} %bitcast.16), calls=%async_computation | async-start | bytes 6291456 | tf_op jit(solution)/shard_map/all_to_all | solution.py:453
  17.3 131.6 %all-gather.11.cloned.1.call-start = ((), (), s32[]{:S(2)}) async-start(), calls=%async_computation.3 | async-start | bytes 1474560 | tf_op jit(solution)/shard_map/all_gather | solution.py:480
  49.3 4.3 %collective-permute-start = (bf16[4,528,384]{2,1,0:T(8,128)(2,1)}, bf16[4,528,384]{2,1,0:T(8,128)(2,1)}, u32[]{:S(2)}, u32[]{:S(2)}) collective-permute-start(bf16[4,528,384]{2,1,0:T(8,128)(2,1)} %bitcast.19), channel_id=1, source_target_pairs={{0,1},{1,0},{2,3},{3,2},{4,5},{5,4},{6,7},{7,6},{8,9},{9,8},{10,11... | collective-permute-start | bytes 4866056 | tf_op jit(solution)/shard_map/ppermute | solution.py:444
  53.6 1.7 copy-start
  71.1 9.6 %collective-permute-start.1 = (bf16[4,256,384]{2,1,0:T(8,128)(2,1)}, bf16[4,256,384]{2,1,0:T(8,128)(2,1)S(1)}, u32[]{:S(2)}, u32[]{:S(2)}) collective-permute-start(bf16[4,256,384]{2,1,0:T(8,128)(2,1)} %get-tuple-element.42), channel_id=1, source_target_pairs={{0,1},{1,0},{2,3},{3,2},{4,5},{5,4},{6,7},{7,6},{8,9},{9,8},{10,11... | collective-permute-start | bytes 2359304 | tf_op jit(solution)/shard_map/ppermute | solution.py:444
  71.2 3.8 %collective-permute-start.5 = (bf16[3,2,48,256]{3,2,1,0:T(8,128)(2,1)}, bf16[3,2,48,256]{3,2,1,0:T(8,128)(2,1)S(1)}, u32[]{:S(2)}, u32[]{:S(2)}) collective-permute-start(bf16[3,2,48,256]{3,2,1,0:T(8,128)(2,1)} %get-tuple-element.45), channel_id=1, source_target_pairs={{0,1},{1,0},{2,3},{3,2},{4,5},{5,4},{6,7},{7,6},{8,9},{9,8},{10,11... | collective-permute-start | bytes 442376 | tf_op jit(solution)/shard_map/ppermute | solution.py:444
  71.7 7.1 %collective-permute-start.17 = (bf16[3,2,48,256]{3,2,1,0:T(8,128)(2,1)}, bf16[3,2,48,256]{3,2,1,0:T(8,128)(2,1)S(1)}, u32[]{:S(2)}, u32[]{:S(2)}) collective-permute-start(bf16[3,2,48,256]{3,2,1,0:T(8,128)(2,1)} %get-tuple-element.63), channel_id=1, source_target_pairs={{0,7},{1,6},{2,5},{3,4},{4,3},{5,2},{6,1},{7,0},{8,15},{9,14},{10,... | collective-permute-start | bytes 442376 | tf_op jit(solution)/shard_map/ppermute | solution.py:444
  72.0 11.0 %collective-permute-start.7 = (bf16[3,2,48,256]{3,2,1,0:T(8,128)(2,1)}, bf16[3,2,48,256]{3,2,1,0:T(8,128)(2,1)S(1)}, u32[]{:S(2)}, u32[]{:S(2)}) collective-permute-start(bf16[3,2,48,256]{3,2,1,0:T(8,128)(2,1)} %get-tuple-element.48), channel_id=1, source_target_pairs={{0,2},{1,3},{2,0},{3,1},{4,6},{5,7},{6,4},{7,5},{8,10},{9,11},{10,... | collective-permute-start | bytes 442376 | tf_op jit(solution)/shard_map/ppermute | solution.py:444
  75.0 10.0 %collective-permute-start.9 = (bf16[3,2,48,256]{3,2,1,0:T(8,128)(2,1)}, bf16[3,2,48,256]{3,2,1,0:T(8,128)(2,1)S(1)}, u32[]{:S(2)}, u32[]{:S(2)}) collective-permute-start(bf16[3,2,48,256]{3,2,1,0:T(8,128)(2,1)} %get-tuple-element.51), channel_id=1, source_target_pairs={{0,3},{1,2},{2,1},{3,0},{4,7},{5,6},{6,5},{7,4},{8,11},{9,10},{10,... | collective-permute-start | bytes 442376 | tf_op jit(solution)/shard_map/ppermute | solution.py:444
  75.0 13.5 %copy-start.11 = (bf16[3,2,48,256]{3,2,1,0:T(8,128)(2,1)}, bf16[3,2,48,256]{3,2,1,0:T(8,128)(2,1)S(1)}, u32[]{:S(2)}) copy-start(bf16[3,2,48,256]{3,2,1,0:T(8,128)(2,1)S(1)} %collective-permute-done.5.refs_1_) | copy-start | bytes 442372
  75.0 10.0 %collective-permute-start.11 = (bf16[3,2,48,256]{3,2,1,0:T(8,128)(2,1)}, bf16[3,2,48,256]{3,2,1,0:T(8,128)(2,1)S(1)}, u32[]{:S(2)}, u32[]{:S(2)}) collective-permute-start(bf16[3,2,48,256]{3,2,1,0:T(8,128)(2,1)} %get-tuple-element.54), channel_id=1, source_target_pairs={{0,4},{1,5},{2,6},{3,7},{4,0},{5,1},{6,2},{7,3},{8,12},{9,13},{10,... | collective-permute-start | bytes 442376 | tf_op jit(solution)/shard_map/ppermute | solution.py:444
  78.7 9.8 %copy-start.12 = (bf16[3,2,48,256]{3,2,1,0:T(8,128)(2,1)}, bf16[3,2,48,256]{3,2,1,0:T(8,128)(2,1)S(1)}, u32[]{:S(2)}) copy-start(bf16[3,2,48,256]{3,2,1,0:T(8,128)(2,1)S(1)} %collective-permute-done.17.refs_7_) | copy-start | bytes 442372
  78.7 6.6 %collective-permute-start.13 = (bf16[3,2,48,256]{3,2,1,0:T(8,128)(2,1)}, bf16[3,2,48,256]{3,2,1,0:T(8,128)(2,1)S(1)}, u32[]{:S(2)}, u32[]{:S(2)}) collective-permute-start(bf16[3,2,48,256]{3,2,1,0:T(8,128)(2,1)} %get-tuple-element.57), channel_id=1, source_target_pairs={{0,5},{1,4},{2,7},{3,6},{4,1},{5,0},{6,3},{7,2},{8,13},{9,12},{10,... | collective-permute-start | bytes 442376 | tf_op jit(solution)/shard_map/ppermute | solution.py:444
  80.7 7.8 %collective-permute-start.15 = (bf16[3,2,48,256]{3,2,1,0:T(8,128)(2,1)}, bf16[3,2,48,256]{3,2,1,0:T(8,128)(2,1)S(1)}, u32[]{:S(2)}, u32[]{:S(2)}) collective-permute-start(bf16[3,2,48,256]{3,2,1,0:T(8,128)(2,1)} %get-tuple-element.60), channel_id=1, source_target_pairs={{0,6},{1,7},{2,4},{3,5},{4,2},{5,3},{6,0},{7,1},{8,14},{9,15},{10,... | collective-permute-start | bytes 442376 | tf_op jit(solution)/shard_map/ppermute | solution.py:444
  83.0 5.5 %copy-start.13 = (bf16[3,2,48,256]{3,2,1,0:T(8,128)(2,1)}, bf16[3,2,48,256]{3,2,1,0:T(8,128)(2,1)S(1)}, u32[]{:S(2)}) copy-start(bf16[3,2,48,256]{3,2,1,0:T(8,128)(2,1)S(1)} %collective-permute-done.7.refs_2_) | copy-start | bytes 442372
  85.0 3.5 %copy-start.14 = (bf16[3,2,48,256]{3,2,1,0:T(8,128)(2,1)}, bf16[3,2,48,256]{3,2,1,0:T(8,128)(2,1)S(1)}, u32[]{:S(2)}) copy-start(bf16[3,2,48,256]{3,2,1,0:T(8,128)(2,1)S(1)} %collective-permute-done.9.refs_3_) | copy-start | bytes 442372
  85.0 3.5 %copy-start.15 = (bf16[3,2,48,256]{3,2,1,0:T(8,128)(2,1)}, bf16[3,2,48,256]{3,2,1,0:T(8,128)(2,1)S(1)}, u32[]{:S(2)}) copy-start(bf16[3,2,48,256]{3,2,1,0:T(8,128)(2,1)S(1)} %collective-permute-done.11.refs_4_) | copy-start | bytes 442372
  85.3 3.2 %copy-start.16 = (bf16[3,2,48,256]{3,2,1,0:T(8,128)(2,1)}, bf16[3,2,48,256]{3,2,1,0:T(8,128)(2,1)S(1)}, u32[]{:S(2)}) copy-start(bf16[3,2,48,256]{3,2,1,0:T(8,128)(2,1)S(1)} %collective-permute-done.13.refs_5_) | copy-start | bytes 442372
  89.2 4.0 %copy-start.25 = (bf16[5,2,48,256]{3,2,1,0:T(8,128)(2,1)S(1)}, bf16[5,2,48,256]{3,2,1,0:T(8,128)(2,1)}, u32[]{:S(2)}) copy-start(bf16[5,2,48,256]{3,2,1,0:T(8,128)(2,1)} %get-tuple-element.64) | copy-start | bytes 737284
  89.2 4.4 %copy-start.24 = (bf16[5,2,48,256]{3,2,1,0:T(8,128)(2,1)S(1)}, bf16[5,2,48,256]{3,2,1,0:T(8,128)(2,1)}, u32[]{:S(2)}) copy-start(bf16[5,2,48,256]{3,2,1,0:T(8,128)(2,1)} %get-tuple-element.61) | copy-start | bytes 737284
  93.0 9.1 %copy-start.23 = (bf16[5,2,48,256]{3,2,1,0:T(8,128)(2,1)S(1)}, bf16[5,2,48,256]{3,2,1,0:T(8,128)(2,1)}, u32[]{:S(2)}) copy-start(bf16[5,2,48,256]{3,2,1,0:T(8,128)(2,1)} %get-tuple-element.58) | copy-start | bytes 737284
  93.0 14.7 %copy-start.22 = (bf16[5,2,48,256]{3,2,1,0:T(8,128)(2,1)S(1)}, bf16[5,2,48,256]{3,2,1,0:T(8,128)(2,1)}, u32[]{:S(2)}) copy-start(bf16[5,2,48,256]{3,2,1,0:T(8,128)(2,1)} %get-tuple-element.55) | copy-start | bytes 737284
  93.1 15.9 %copy-start.21 = (bf16[5,2,48,256]{3,2,1,0:T(8,128)(2,1)S(1)}, bf16[5,2,48,256]{3,2,1,0:T(8,128)(2,1)}, u32[]{:S(2)}) copy-start(bf16[5,2,48,256]{3,2,1,0:T(8,128)(2,1)} %get-tuple-element.52) | copy-start | bytes 737284
  93.1 41.9 %copy-start.20 = (bf16[5,2,48,256]{3,2,1,0:T(8,128)(2,1)S(1)}, bf16[5,2,48,256]{3,2,1,0:T(8,128)(2,1)}, u32[]{:S(2)}) copy-start(bf16[5,2,48,256]{3,2,1,0:T(8,128)(2,1)} %get-tuple-element.49) | copy-start | bytes 737284
  93.1 42.6 %copy-start.19 = (bf16[5,2,48,256]{3,2,1,0:T(8,128)(2,1)S(1)}, bf16[5,2,48,256]{3,2,1,0:T(8,128)(2,1)}, u32[]{:S(2)}) copy-start(bf16[5,2,48,256]{3,2,1,0:T(8,128)(2,1)} %get-tuple-element.46) | copy-start | bytes 737284
  93.1 95.3 %all-gather.9.cloned.1.call-start = ((), (), s32[]{:S(2)}) async-start(), calls=%async_computation.2 | async-start | bytes 2457600 | tf_op jit(solution)/shard_map/all_gather | solution.py:480
  93.2 8.9 %collective-permute-start.18 = (bf16[5,2,48,256]{3,2,1,0:T(8,128)(2,1)S(1)}, bf16[5,2,48,256]{3,2,1,0:T(8,128)(2,1)S(1)}, u32[]{:S(2)}, u32[]{:S(2)}) collective-permute-start(bf16[5,2,48,256]{3,2,1,0:T(8,128)(2,1)S(1)} %copy-done.25), channel_id=1, source_target_pairs={{0,7},{1,6},{2,5},{3,4},{4,3},{5,2},{6,1},{7,0},{8,15},{9,14},{10,... | collective-permute-start | bytes 737288 | tf_op jit(solution)/shard_map/ppermute | solution.py:444
  93.6 14.2 %collective-permute-start.16 = (bf16[5,2,48,256]{3,2,1,0:T(8,128)(2,1)S(1)}, bf16[5,2,48,256]{3,2,1,0:T(8,128)(2,1)S(1)}, u32[]{:S(2)}, u32[]{:S(2)}) collective-permute-start(bf16[5,2,48,256]{3,2,1,0:T(8,128)(2,1)S(1)} %copy-done.24), channel_id=1, source_target_pairs={{0,6},{1,7},{2,4},{3,5},{4,2},{5,3},{6,0},{7,1},{8,14},{9,15},{10,... | collective-permute-start | bytes 737288 | tf_op jit(solution)/shard_map/ppermute | solution.py:444
  96.7 12.2 %collective-permute-start.4 = (bf16[256,384]{1,0:T(8,128)(2,1)S(1)}, bf16[256,384]{1,0:T(8,128)(2,1)S(1)}, u32[]{:S(2)}, u32[]{:S(2)}) collective-permute-start(bf16[256,384]{1,0:T(8,128)(2,1)S(1)} %get-tuple-element.74), channel_id=1, source_target_pairs={{0,24},{8,16},{16,8},{24,0},{1,25},{9,17},{17,9},{25,1},{2,26},{10... | collective-permute-start | bytes 589832 | tf_op jit(solution)/shard_map/ppermute | solution.py:470
  100.3 34.7 %collective-permute-start.3 = (bf16[256,384]{1,0:T(8,128)(2,1)S(1)}, bf16[256,384]{1,0:T(8,128)(2,1)S(1)}, u32[]{:S(2)}, u32[]{:S(2)}) collective-permute-start(bf16[256,384]{1,0:T(8,128)(2,1)S(1)} %get-tuple-element.75), channel_id=1, source_target_pairs={{0,16},{8,24},{16,0},{24,8},{1,17},{9,25},{17,1},{25,9},{2,18},{10... | collective-permute-start | bytes 589832 | tf_op jit(solution)/shard_map/ppermute | solution.py:470
  100.3 35.4 %collective-permute-start.2 = (bf16[256,384]{1,0:T(8,128)(2,1)S(1)}, bf16[256,384]{1,0:T(8,128)(2,1)S(1)}, u32[]{:S(2)}, u32[]{:S(2)}) collective-permute-start(bf16[256,384]{1,0:T(8,128)(2,1)S(1)} %get-tuple-element.76), channel_id=1, source_target_pairs={{0,8},{8,0},{16,24},{24,16},{1,9},{9,1},{17,25},{25,17},{2,10},{10... | collective-permute-start | bytes 589832 | tf_op jit(solution)/shard_map/ppermute | solution.py:470
  102.1 39.1 %copy-start.1 = (bf16[5,2,48,256]{3,2,1,0:T(8,128)(2,1)}, bf16[5,2,48,256]{3,2,1,0:T(8,128)(2,1)S(1)}, u32[]{:S(2)}) copy-start(bf16[5,2,48,256]{3,2,1,0:T(8,128)(2,1)S(1)} %collective-permute-done.18.refs_7_) | copy-start | bytes 737284
  102.1 33.7 %collective-permute-start.14 = (bf16[5,2,48,256]{3,2,1,0:T(8,128)(2,1)S(1)}, bf16[5,2,48,256]{3,2,1,0:T(8,128)(2,1)S(1)}, u32[]{:S(2)}, u32[]{:S(2)}) collective-permute-start(bf16[5,2,48,256]{3,2,1,0:T(8,128)(2,1)S(1)} %copy-done.23), channel_id=1, source_target_pairs={{0,5},{1,4},{2,7},{3,6},{4,1},{5,0},{6,3},{7,2},{8,13},{9,12},{10,... | collective-permute-start | bytes 737288 | tf_op jit(solution)/shard_map/ppermute | solution.py:444
  107.8 33.4 %copy-start.2 = (bf16[5,2,48,256]{3,2,1,0:T(8,128)(2,1)}, bf16[5,2,48,256]{3,2,1,0:T(8,128)(2,1)S(1)}, u32[]{:S(2)}) copy-start(bf16[5,2,48,256]{3,2,1,0:T(8,128)(2,1)S(1)} %collective-permute-done.16.refs_6_) | copy-start | bytes 737284
  107.8 28.0 %collective-permute-start.12 = (bf16[5,2,48,256]{3,2,1,0:T(8,128)(2,1)S(1)}, bf16[5,2,48,256]{3,2,1,0:T(8,128)(2,1)S(1)}, u32[]{:S(2)}, u32[]{:S(2)}) collective-permute-start(bf16[5,2,48,256]{3,2,1,0:T(8,128)(2,1)S(1)} %copy-done.22), channel_id=1, source_target_pairs={{0,4},{1,5},{2,6},{3,7},{4,0},{5,1},{6,2},{7,3},{8,12},{9,13},{10,... | collective-permute-start | bytes 737288 | tf_op jit(solution)/shard_map/ppermute | solution.py:444
  108.9 37.7 %copy-start.8 = (bf16[256,384]{1,0:T(8,128)(2,1)}, bf16[256,384]{1,0:T(8,128)(2,1)S(1)}, u32[]{:S(2)}) copy-start(bf16[256,384]{1,0:T(8,128)(2,1)S(1)} %collective-permute-done.4.refs_3_) | copy-start | bytes 589828
  108.9 26.9 %collective-permute-start.10 = (bf16[5,2,48,256]{3,2,1,0:T(8,128)(2,1)S(1)}, bf16[5,2,48,256]{3,2,1,0:T(8,128)(2,1)S(1)}, u32[]{:S(2)}, u32[]{:S(2)}) collective-permute-start(bf16[5,2,48,256]{3,2,1,0:T(8,128)(2,1)S(1)} %copy-done.21), channel_id=1, source_target_pairs={{0,3},{1,2},{2,1},{3,0},{4,7},{5,6},{6,5},{7,4},{8,11},{9,10},{10,... | collective-permute-start | bytes 737288 | tf_op jit(solution)/shard_map/ppermute | solution.py:444
  135.0 11.6 %copy-start.9 = (bf16[256,384]{1,0:T(8,128)(2,1)}, bf16[256,384]{1,0:T(8,128)(2,1)S(1)}, u32[]{:S(2)}) copy-start(bf16[256,384]{1,0:T(8,128)(2,1)S(1)} %collective-permute-done.3.refs_2_) | copy-start | bytes 589828
  135.0 6.2 %collective-permute-start.8 = (bf16[5,2,48,256]{3,2,1,0:T(8,128)(2,1)S(1)}, bf16[5,2,48,256]{3,2,1,0:T(8,128)(2,1)S(1)}, u32[]{:S(2)}, u32[]{:S(2)}) collective-permute-start(bf16[5,2,48,256]{3,2,1,0:T(8,128)(2,1)S(1)} %copy-done.20), channel_id=1, source_target_pairs={{0,2},{1,3},{2,0},{3,1},{4,6},{5,7},{6,4},{7,5},{8,10},{9,11},{10,... | collective-permute-start | bytes 737288 | tf_op jit(solution)/shard_map/ppermute | solution.py:444
  135.7 10.9 %copy-start.10 = (bf16[256,384]{1,0:T(8,128)(2,1)}, bf16[256,384]{1,0:T(8,128)(2,1)S(1)}, u32[]{:S(2)}) copy-start(bf16[256,384]{1,0:T(8,128)(2,1)S(1)} %collective-permute-done.2.refs_1_) | copy-start | bytes 589828
  135.7 5.5 %collective-permute-start.6 = (bf16[5,2,48,256]{3,2,1,0:T(8,128)(2,1)S(1)}, bf16[5,2,48,256]{3,2,1,0:T(8,128)(2,1)S(1)}, u32[]{:S(2)}, u32[]{:S(2)}) collective-permute-start(bf16[5,2,48,256]{3,2,1,0:T(8,128)(2,1)S(1)} %copy-done.19), channel_id=1, source_target_pairs={{0,1},{1,0},{2,3},{3,2},{4,5},{5,4},{6,7},{7,6},{8,9},{9,8},{10,11... | collective-permute-start | bytes 737288 | tf_op jit(solution)/shard_map/ppermute | solution.py:444
  135.8 5.4 %copy-start.3 = (bf16[5,2,48,256]{3,2,1,0:T(8,128)(2,1)}, bf16[5,2,48,256]{3,2,1,0:T(8,128)(2,1)S(1)}, u32[]{:S(2)}) copy-start(bf16[5,2,48,256]{3,2,1,0:T(8,128)(2,1)S(1)} %collective-permute-done.14.refs_5_) | copy-start | bytes 737284
  135.8 5.4 %copy-start.4 = (bf16[5,2,48,256]{3,2,1,0:T(8,128)(2,1)}, bf16[5,2,48,256]{3,2,1,0:T(8,128)(2,1)S(1)}, u32[]{:S(2)}) copy-start(bf16[5,2,48,256]{3,2,1,0:T(8,128)(2,1)S(1)} %collective-permute-done.12.refs_4_) | copy-start | bytes 737284
  135.8 5.4 %copy-start.5 = (bf16[5,2,48,256]{3,2,1,0:T(8,128)(2,1)}, bf16[5,2,48,256]{3,2,1,0:T(8,128)(2,1)S(1)}, u32[]{:S(2)}) copy-start(bf16[5,2,48,256]{3,2,1,0:T(8,128)(2,1)S(1)} %collective-permute-done.10.refs_3_) | copy-start | bytes 737284
  141.2 0.7 copy-start.6
  141.2 0.8 copy-start.7
  (1 other events, 0.7 us)
Sparse Core Ops, SparseCore 0:
  10.1 39.1 all-gather.6
  93.2 43.3 all-gather.10
  146.8 41.5 all-gather.8

commit v8 on v6

--- a/solution.py
+++ b/solution.py
@@ -416,11 +416,7 @@
     )(pos, *pieces, *before)
 
 
-def after(value, *others):
-    return lax.optimization_barrier((value,) + others)[0]
-
-
-def gather_planes(fresh, dp_at, n_dp, before):
+def gather_planes(fresh, dp_at, n_dp):
     if n_dp != 4:
         whole = lax.all_gather(fresh, "dp", axis=0)
         return [
@@ -428,28 +424,35 @@
         ]
     two = lax.ppermute(fresh, "dp", [(0, 2), (1, 3), (2, 0), (3, 1)])
     one = lax.ppermute(fresh, "dp", [(0, 1), (1, 0), (2, 3), (3, 2)])
-    middle = lax.ppermute(fresh, "dp", [(1, 2), (2, 1)])
-    outer = lax.ppermute(after(two, *before), "dp", [(2, 3), (1, 0)])
+    outer = lax.ppermute(two, "dp", [(2, 3), (1, 0)])
+    middle = lax.ppermute(after(fresh, two), "dp", [(1, 2), (2, 1)])
     return [fresh, one, two, (middle, outer)]
 
 
-def finish_predicted(perm, total):
-    def body(perm_ref, total_ref, out_ref):
-        out_ref[...] = lax.dot_general(
+def after(value, *others):
+    return lax.optimization_barrier((value,) + others)[0]
+
+
+def finish_predicted(perm, parts):
+    def body(perm_ref, *refs):
+        total = refs[0][...].astype(jnp.float32)
+        for ref in refs[1:-1]:
+            total = total + ref[...].astype(jnp.float32)
+        refs[-1][...] = lax.dot_general(
             perm_ref[...],
-            total_ref[...].astype(jnp.bfloat16),
+            total.astype(jnp.bfloat16),
             (((0,), (0,)), ((), ())),
             preferred_element_type=jnp.float32,
         ).astype(jnp.bfloat16)
 
     return pl.pallas_call(
         body,
-        out_shape=jax.ShapeDtypeStruct(total.shape, jnp.bfloat16),
-        in_specs=[vmem(), vmem()],
+        out_shape=jax.ShapeDtypeStruct(parts[0].shape, jnp.bfloat16),
+        in_specs=[vmem()] * (1 + len(parts)),
         out_specs=vmem(),
         compiler_params=params(),
         name="finish_predicted",
-    )(perm, total)
+    )(perm, *parts)
 
 
 def shards(signals, cotangent, row_insertion, touched, slot_map, weights, moment1, moment2):
@@ -487,25 +490,32 @@
         for j in range(1, n_own if arrived else 1):
             chunk[j] = after(chunk[j], arrived[-1][j])
         arrived.append([chunk[0]] + [across(chunk[j], j) for j in range(1, n_own)])
-    pred_other = across(after(pred_other, arrived[0][1]), 1)
-    pred_part = pred_mine.astype(jnp.float32) + pred_other.astype(jnp.float32)
-    total = lax.psum_scatter(pred_part, "dp", scatter_dimension=0)
+    pred_part = pred_mine + across(pred_other, 1)
+
+    def of_plane(j):
+        return lax.dynamic_index_in_dim(pred_part, dp_at ^ j, 0, keepdims=False)
+
+    parts = [of_plane(0)] + [
+        lax.ppermute(of_plane(j), "dp", [(d, d ^ j) for d in range(n_dp)]) for j in range(1, n_dp)
+    ]
+    arrived[0][-1] = after(arrived[0][-1], *parts[1:])
 
     moments = []
     new_weights = []
     start = 0
-    for i, size in enumerate(sizes):
-        ready = list(arrived[i])
-        ready[-1] = after(ready[-1], *(jax.tree.leaves(pieces[1:])[:n_dp - 1] if i else [pred_part]))
+    pieces = []
+    for size, ready in zip(sizes, arrived):
+        ready[-1] = after(ready[-1], *pieces[1:3])
         fresh, *moments = adam(pos, ready, weights, moment1, moment2, start, moments)
-        later = arrived[i + 1][1 : n_own // 2 + 1] if i + 1 < len(sizes) else []
-        pieces = gather_planes(fresh, dp_at, n_dp, later)
+        if pieces:
+            fresh = after(fresh, *jax.tree.leaves(pieces[3:]))
+        pieces = gather_planes(fresh, dp_at, n_dp)
         new_weights = [place_weights(pos, pieces, start, half, new_weights)]
         start += size
     new_weights = new_weights[0]
     new_moment1, new_moment2 = moments
 
-    predicted = finish_predicted(perm, total)
+    predicted = finish_predicted(perm, parts)
     return (predicted, new_weights, new_moment1, new_moment2)
 
 

time: 211 us -> 205 us (0.972)
  waiting for transfers between devices: 117 us -> 110 us
  starting transfers between devices: 28.3 us -> 31.3 us
    ppermute x16, waiting for transfers between devices: 33 us -> 27.8 us  [across(): return lax.ppermute(value, 'own', [(o, o ^ j) for o in range(n_own)])]
    ppermute x4 -> x7, starting transfers between devices: 3.94 us -> 8.32 us  [the longest x3 4.39 us: shards(): lax.ppermute(of_plane(j), 'dp', [(d, d ^ j) for d in range(n_dp)])]
    ppermute x2, starting transfers between devices: 4.42 us -> 0.24 us  [gather_planes(): two = lax.ppermute(fresh, 'dp', [(0, 2), (1, 3), (2, 0), (3, 1)])]
    ppermute x4 -> x7, waiting for transfers between devices: 18.5 us -> 15.4 us  [the longest x2 8.49 us: gather_planes(): outer = lax.ppermute(two, 'dp', [(2, 3), (1, 0)])]
    ppermute x16, starting transfers between devices: 10.6 us -> 13.5 us  [across(): return lax.ppermute(value, 'own', [(o, o ^ j) for o in range(n_own)])]
    unnamed x75 -> x83, local copies, waits for them, and re-layouts: 7.04 us -> 4.65 us
  transfers between devices with their start and end apart: 27 -> 29, of which waited for: 15 -> 13; matrix products, arithmetic and copies ran while one was open for 2% -> 2% of each run, Pallas kernels for 7% -> 5%
where the time goes in v8:
time: 205 us; the launch traced here: 202 us
  waiting for transfers between devices  110 us (54%)
  Pallas kernels  35.3 us (17%)
  starting transfers between devices  31.3 us (15%)
  between operations  14.5 us (7%)
  local copies, waits for them, and re-layouts  8.64 us (4%)
    all_gather x1, waiting for transfers between devices, shards(): planes = lax.all_gather(packed, 'dp', axis=0)  32 us
    ppermute x2, waiting for transfers between devices, gather_planes(): two = lax.ppermute(fresh, 'dp', [(0, 2), (1, 3), (2, 0), (3, 1)])  31.7 us
    ppermute x16, waiting for transfers between devices, across(): return lax.ppermute(value, 'own', [(o, o ^ j) for o in range(n_own)])  27.8 us
    pallas_call x1, Pallas kernels, local_grads(): pl.pallas_call(body, out_shape=[pred_shape, pred_shape] + grad_shapes, in...  15.8 us
    ppermute x16, starting transfers between devices, across(): return lax.ppermute(value, 'own', [(o, o ^ j) for o in range(n_own)])  13.5 us
    ppermute x2, waiting for transfers between devices, gather_planes(): outer = lax.ppermute(two, 'dp', [(2, 3), (1, 0)])  8.49 us
    pallas_call x2, Pallas kernels, adam(): pl.pallas_call(body, out_shape=[jax.ShapeDtypeStruct(blocks, jnp.bfloat16...  8.48 us
    ppermute x3, waiting for transfers between devices, shards(): lax.ppermute(of_plane(j), 'dp', [(d, d ^ j) for d in range(n_dp)])  6.94 us
  transfers between devices with their start and end apart: 29, of which 13 were waited for; matrix products, arithmetic and copies ran while one was open for 2% of the time, Pallas kernels for 5%

profile of v8, /device:TPU:2, one launch (start us, length us, event | category | flops | bytes accessed | tf_op | source)
XLA Modules:
  0.0 201.9 jit_solution(3755035112601464741)
XLA Ops:
  7.2 2.4 %pack_rows.1 = (bf16[528,384]{1,0:T(8,128)(2,1)}, bf16[256,256]{1,0:T(8,128)(2,1)}) custom-call(s32[1,256]{1,0:T(1,128)} %bitcast.18, bf16[256,384]{1,0:T(8,128)(2,1)} %sig_ref.1, bf16[256,384]{1,0:T(8,128)(2,1)} %cot_ref.1), custom_call_target="tpu_custom_call" | custom-call | tf_op jit(solution)/shard_map/pack_rows/pallas_call | solution.py:79
  9.6 1.2 constant_dynamic-slice_fusion
  10.8 2.0 %broadcast_in_dim.8 = bf16[4,2,8,2,48,256]{5,4,3,2,1,0:T(8,128)(2,1)} broadcast(bf16[2,8,2,48,256]{4,3,2,1,0:T(8,128)(2,1)S(1)} %bitcast.15), dimensions={1,2,3,4,5} | broadcast | bytes 3932160 | tf_op jit(solution)/shard_map/broadcast_in_dim | solution.py:479
  12.9 4.4 %all-to-all-start = ((bf16[8,8,2,48,256]{4,3,2,1,0:T(8,128)(2,1)}), bf16[8,8,2,48,256]{4,3,2,1,0:T(8,128)(2,1)S(1)}, u32[]{:S(2)}, u32[]{:S(2)}) async-start(bf16[8,8,2,48,256]{4,3,2,1,0:T(8,128)(2,1)} %bitcast.14), calls=%async_computation | async-start | bytes 6291456 | tf_op jit(solution)/shard_map/all_to_all | solution.py:482
  17.3 32.0 %all-gather.3.cloned.1.call-done = bf16[2112,384]{1,0:T(8,128)(2,1)} async-done(((bf16[528,384]{1,0:T(8,128)(2,1)}), bf16[2112,384]{1,0:T(8,128)(2,1)}) %all-gather.3.cloned.1.call-update) | async-done | bytes 1622032 | tf_op jit(solution)/shard_map/all_gather | solution.py:476
  49.3 0.7 copy.15.touched_ref
  50.6 3.0 %all-to-all-done.rest_2_ = bf16[8,8,2,48,256]{4,3,2,1,0:T(8,128)(2,1)S(1)} async-done(((bf16[8,8,2,48,256]{4,3,2,1,0:T(8,128)(2,1)}), bf16[8,8,2,48,256]{4,3,2,1,0:T(8,128)(2,1)S(1)}, u32[]{:S(2)}, u32[]{:S(2)}) %all-to-all-start) | async-done | bytes 3145760 | tf_op jit(solution)/shard_map/all_to_all | solution.py:482
  53.7 1.7 copy-done
  55.3 15.8 %local_grads.1 = (bf16[4,256,384]{2,1,0:T(8,128)(2,1)}, bf16[4,256,384]{2,1,0:T(8,128)(2,1)}, bf16[3,2,48,256]{3,2,1,0:T(8,128)(2,1)}, bf16[3,2,48,256]{3,2,1,0:...) custom-call(s32[2]{0:T(128)} %pad_add_fusion.pos_ref, ...), custom_call_target="tpu_custom_call" | custom-call | tf_op jit(solution)/shard_map/local_grads/pallas_call | solution.py:241
  71.2 2.5 %collective-permute-done.1 = bf16[4,256,384]{2,1,0:T(8,128)(2,1)S(1)} collective-permute-done((bf16[4,256,384]{2,1,0:T(8,128)(2,1)}, bf16[4,256,384]{2,1,0:T(8,128)(2,1)S(1)}, u32[]{:S(2)}, u32[]{:S(2)}) %collective-permute-start.1) | collective-permute-done | bytes 786464 | tf_op jit(solution)/shard_map/ppermute | solution.py:473
  73.7 1.4 add.20
  75.1 0.8 dynamic-slice_bitcast_fusion
  75.9 3.6 %collective-permute-start.4 = (bf16[256,384]{1,0:T(8,128)(2,1)S(1)}, bf16[256,384]{1,0:T(8,128)(2,1)S(1)}, u32[]{:S(2)}, u32[]{:S(2)}) collective-permute-start(bf16[256,384]{1,0:T(8,128)(2,1)S(1)} %get-tuple-element.80), channel_id=1, source_target_pairs={{0,24},{8,16},{16,8},{24,0},{1,25},{9,17},{17,9},{25,1},{2,26},{10... | collective-permute-start | bytes 589832 | tf_op jit(solution)/shard_map/ppermute | solution.py:499
  79.5 0.8 collective-permute-start.2
  80.3 1.6 collective-permute-start.17
  81.9 1.3 collective-permute-start.7
  83.1 3.7 %collective-permute-done.17.refs_7_ = bf16[3,2,48,256]{3,2,1,0:T(8,128)(2,1)S(1)} collective-permute-done((bf16[3,2,48,256]{3,2,1,0:T(8,128)(2,1)S(1)}, bf16[3,2,48,256]{3,2,1,0:T(8,128)(2,1)S(1)}, u32[]{:S(2)}, u32[]{:S(2)}) %collective-permute-start.17) | collective-permute-done | bytes 147488 | tf_op jit(solution)/shard_map/ppermute | solution.py:473
  86.8 2.1 %collective-permute-start.9 = (bf16[3,2,48,256]{3,2,1,0:T(8,128)(2,1)S(1)}, bf16[3,2,48,256]{3,2,1,0:T(8,128)(2,1)S(1)}, u32[]{:S(2)}, u32[]{:S(2)}) collective-permute-start(bf16[3,2,48,256]{3,2,1,0:T(8,128)(2,1)S(1)} %copy-done.37), channel_id=1, source_target_pairs={{0,3},{1,2},{2,1},{3,0},{4,7},{5,6},{6,5},{7,4},{8,11},{9,10},{10,... | collective-permute-start | bytes 442376 | tf_op jit(solution)/shard_map/ppermute | solution.py:473
  88.9 0.6 collective-permute-start.11
  89.5 6.9 %collective-permute-done.3.refs_2_ = bf16[256,384]{1,0:T(8,128)(2,1)S(1)} collective-permute-done((bf16[256,384]{1,0:T(8,128)(2,1)S(1)}, bf16[256,384]{1,0:T(8,128)(2,1)S(1)}, u32[]{:S(2)}, u32[]{:S(2)}) %collective-permute-start.3) | collective-permute-done | bytes 196640 | tf_op jit(solution)/shard_map/ppermute | solution.py:499
  96.5 1.9 collective-permute-start.15
  98.4 6.8 %collective-permute-done.13.refs_5_ = bf16[3,2,48,256]{3,2,1,0:T(8,128)(2,1)S(1)} collective-permute-done((bf16[3,2,48,256]{3,2,1,0:T(8,128)(2,1)S(1)}, bf16[3,2,48,256]{3,2,1,0:T(8,128)(2,1)S(1)}, u32[]{:S(2)}, u32[]{:S(2)}) %collective-permute-start.13) | collective-permute-done | bytes 147488 | tf_op jit(solution)/shard_map/ppermute | solution.py:473
  106.0 3.9 %adam_step.2 = (bf16[2,3,2,48,256]{4,3,2,1,0:T(8,128)(2,1)}, f32[16,2,48,256]{3,2,1,0:T(8,128)}, f32[16,2,48,256]{3,2,1,0:T(8,128)}) custom-call(s32[2]{0:T(128)} %pad_add_fusion.pos_ref, bf16[3,2,48,256]{3,2,1,0:T(8,128)(2,1)} %get-tuple-element.68.refs_0_, bf16[3,2,48,256]{3,2,1,0:T(8,128)(2,1)} %copy-done.19, bf16[3,2,48,256]{3,2,1,0:T(8,128)(2,1)} %copy-done.21, ...), custom_call_target="tpu_custom_call" | custom-call | tf_op jit(solution)/shard_map/adam_step/pallas_call | solution.py:333
  110.0 3.0 %collective-permute-start.19 = (bf16[2,3,2,48,256]{4,3,2,1,0:T(8,128)(2,1)}, bf16[2,3,2,48,256]{4,3,2,1,0:T(8,128)(2,1)S(1)}, u32[]{:S(2)}, u32[]{:S(2)}) collective-permute-start(bf16[2,3,2,48,256]{4,3,2,1,0:T(8,128)(2,1)} %get-tuple-element.75.refs_0_), channel_id=1, source_target_pairs={{0,8},{8,0},{16,24},{24,16},{1,9},{9,1},{17,25},{25,17},{2,10},{10... | collective-permute-start | bytes 884744 | tf_op jit(solution)/shard_map/ppermute | solution.py:426
  113.0 1.2 collective-permute-start.18
  114.2 0.9 collective-permute-start.16
  115.1 0.8 collective-permute-start.14
  115.9 10.0 %collective-permute-done.20.refs_2_ = bf16[2,3,2,48,256]{4,3,2,1,0:T(8,128)(2,1)S(1)} collective-permute-done((bf16[2,3,2,48,256]{4,3,2,1,0:T(8,128)(2,1)}, bf16[2,3,2,48,256]{4,3,2,1,0:T(8,128)(2,1)S(1)}, u32[]{:S(2)}, u32[]{:S(2)}) %collective-permute-start.20) | collective-permute-done | bytes 294944 | tf_op jit(solution)/shard_map/ppermute | solution.py:425
  125.9 1.0 collective-permute-start.12
  126.9 0.7 collective-permute-start.21
  127.6 1.3 collective-permute-start.22
  128.9 3.4 %collective-permute-done.14.refs_5_ = bf16[5,2,48,256]{3,2,1,0:T(8,128)(2,1)S(1)} collective-permute-done((bf16[5,2,48,256]{3,2,1,0:T(8,128)(2,1)S(1)}, bf16[5,2,48,256]{3,2,1,0:T(8,128)(2,1)S(1)}, u32[]{:S(2)}, u32[]{:S(2)}) %collective-permute-start.14) | collective-permute-done | bytes 245792 | tf_op jit(solution)/shard_map/ppermute | solution.py:473
  132.3 0.8 collective-permute-start.10
  133.1 4.5 %collective-permute-done.12.refs_4_ = bf16[5,2,48,256]{3,2,1,0:T(8,128)(2,1)S(1)} collective-permute-done((bf16[5,2,48,256]{3,2,1,0:T(8,128)(2,1)S(1)}, bf16[5,2,48,256]{3,2,1,0:T(8,128)(2,1)S(1)}, u32[]{:S(2)}, u32[]{:S(2)}) %collective-permute-start.12) | collective-permute-done | bytes 245792 | tf_op jit(solution)/shard_map/ppermute | solution.py:473
  137.6 1.1 collective-permute-start.8
  138.8 1.4 collective-permute-done.10.refs_3_
  140.3 5.6 %collective-permute-done.8.refs_2_ = bf16[5,2,48,256]{3,2,1,0:T(8,128)(2,1)S(1)} collective-permute-done((bf16[5,2,48,256]{3,2,1,0:T(8,128)(2,1)S(1)}, bf16[5,2,48,256]{3,2,1,0:T(8,128)(2,1)S(1)}, u32[]{:S(2)}, u32[]{:S(2)}) %collective-permute-start.8) | collective-permute-done | bytes 245792 | tf_op jit(solution)/shard_map/ppermute | solution.py:473
  145.9 0.6 copy-done.14
  146.6 4.6 %adam_step.3 = (bf16[2,5,2,48,256]{4,3,2,1,0:T(8,128)(2,1)}, f32[16,2,48,256]{3,2,1,0:T(8,128)}, f32[16,2,48,256]{3,2,1,0:T(8,128)}) custom-call(s32[2]{0:T(128)} %pad_add_fusion.pos_ref, bf16[5,2,48,256]{3,2,1,0:T(8,128)(2,1)} %get-tuple-element.46.refs_0_, bf16[5,2,48,256]{3,2,1,0:T(8,128)(2,1)} %copy-done.15, ...), custom_call_target="tpu_custom_call", output_to_operand_aliasing={{1}: (12, {}), {2}: (13, {})} | custom-call | tf_op jit(solution)/shard_map/adam_step/pallas_call | solution.py:333
  151.4 1.8 collective-permute-start.23
  153.3 21.8 %collective-permute-done.24.refs_2_ = bf16[2,5,2,48,256]{4,3,2,1,0:T(8,128)(2,1)S(1)} collective-permute-done((bf16[2,5,2,48,256]{4,3,2,1,0:T(8,128)(2,1)}, bf16[2,5,2,48,256]{4,3,2,1,0:T(8,128)(2,1)S(1)}, u32[]{:S(2)}, u32[]{:S(2)}) %collective-permute-start.24) | collective-permute-done | bytes 491552 | tf_op jit(solution)/shard_map/ppermute | solution.py:425
  175.0 0.7 collective-permute-start.25
  175.7 1.3 collective-permute-start.26
  177.0 2.2 %finish_predicted.1 = bf16[256,384]{1,0:T(8,128)(2,1)} custom-call(bf16[256,256]{1,0:T(8,128)(2,1)} %get-tuple-element.42.perm_ref, bf16[256,384]{1,0:T(8,128)(2,1)} %get-tuple-element.83.refs_0_, bf16[256,384]{1,0:T(8,128)(2,1)} %copy-done.18, bf16[256,384]{1,0:T(8,128)(2,1)} %copy-done.17, bf16[256,384]{1,0:T(8,128)(2,1)} %copy-done.16), custom_call_target="tpu_custom_call" | custom-call | tf_op jit(solution)/shard_map/finish_predicted/pallas_call | solution.py:448
  179.2 3.0 %place_weights.2.refs_5_ = bf16[16,2,48,1024]{3,2,1,0:T(8,128)(2,1)} custom-call(s32[2]{0:T(128)} %pad_add_fusion.pos_ref, bf16[2,3,2,48,256]{4,3,2,1,0:T(8,128)(2,1)} %get-tuple-element.75.refs_0_, bf16[2,3,2,48,256]{4,3,2,1,0:T(8,128)(2,1)} %copy-done.6, bf16[2,3,2,48,256]{4,3,2,1,0:T(8,128)(2,1)} %copy-done.5, bf16[2,3,2,48,256]{4,3,2,1,0:T(8,128)(2,1)} %copy-done.7, ...), custom_call_target="tpu_custom_call" | custom-call | tf_op jit(solution)/shard_map/place_weights/pallas_call | solution.py:403
  182.3 8.5 %collective-permute-done.26.refs_4_ = bf16[2,5,2,48,256]{4,3,2,1,0:T(8,128)(2,1)S(1)} collective-permute-done((bf16[2,5,2,48,256]{4,3,2,1,0:T(8,128)(2,1)S(1)}, bf16[2,5,2,48,256]{4,3,2,1,0:T(8,128)(2,1)S(1)}, u32[]{:S(2)}, u32[]{:S(2)}) %collective-permute-start.26) | collective-permute-done | bytes 491552 | tf_op jit(solution)/shard_map/ppermute | solution.py:427
  190.8 0.8 copy-done.4
  191.5 3.5 %place_weights.3 = bf16[16,2,48,1024]{3,2,1,0:T(8,128)(2,1)} custom-call(s32[2]{0:T(128)} %pad_add_fusion.pos_ref, bf16[2,5,2,48,256]{4,3,2,1,0:T(8,128)(2,1)} %get-tuple-element.77.refs_0_, bf16[2,5,2,48,256]{4,3,2,1,0:T(8,128)(2,1)} %copy-done.2, bf16[2,5,2,48,256]{4,3,2,1,0:T(8,128)(2,1)} %copy-done.1, ...), custom_call_target="tpu_custom_call", output_to_operand_aliasing={{}: (6, {})} | custom-call | tf_op jit(solution)/shard_map/place_weights/pallas_call | solution.py:403
  (106 shorter events, 2.0 us)
Async XLA Ops:
  7.2 42.1 %all-gather.3.cloned.1.call-start = ((), (), s32[]{:S(2)}) async-start(), calls=%async_computation.1 | async-start | bytes 2027520 | tf_op jit(solution)/shard_map/all_gather | solution.py:476
  12.9 36.4 %copy-start.26 = (s32[32,4]{0,1:T(4,128)S(1)}, s32[32,4]{0,1:T(4,128)}, u32[]{:S(2)}) copy-start(s32[32,4]{0,1:T(4,128)} %param.11) | copy-start | bytes 1540
  12.9 40.8 %all-to-all-start = ((bf16[8,8,2,48,256]{4,3,2,1,0:T(8,128)(2,1)}), bf16[8,8,2,48,256]{4,3,2,1,0:T(8,128)(2,1)S(1)}, u32[]{:S(2)}, u32[]{:S(2)}) async-start(bf16[8,8,2,48,256]{4,3,2,1,0:T(8,128)(2,1)} %bitcast.14), calls=%async_computation | async-start | bytes 6291456 | tf_op jit(solution)/shard_map/all_to_all | solution.py:482
  49.3 4.3 %collective-permute-start = (bf16[4,528,384]{2,1,0:T(8,128)(2,1)}, bf16[4,528,384]{2,1,0:T(8,128)(2,1)}, u32[]{:S(2)}, u32[]{:S(2)}) collective-permute-start(bf16[4,528,384]{2,1,0:T(8,128)(2,1)} %bitcast.16), channel_id=1, source_target_pairs={{0,1},{1,0},{2,3},{3,2},{4,5},{5,4},{6,7},{7,6},{8,9},{9,8},{10,11... | collective-permute-start | bytes 4866056 | tf_op jit(solution)/shard_map/ppermute | solution.py:473
  71.1 2.6 %collective-permute-start.1 = (bf16[4,256,384]{2,1,0:T(8,128)(2,1)}, bf16[4,256,384]{2,1,0:T(8,128)(2,1)S(1)}, u32[]{:S(2)}, u32[]{:S(2)}) collective-permute-start(bf16[4,256,384]{2,1,0:T(8,128)(2,1)} %get-tuple-element.45), channel_id=1, source_target_pairs={{0,1},{1,0},{2,3},{3,2},{4,5},{5,4},{6,7},{7,6},{8,9},{9,8},{10,11... | collective-permute-start | bytes 2359304 | tf_op jit(solution)/shard_map/ppermute | solution.py:473
  73.7 15.2 %copy-start.36 = (bf16[3,2,48,256]{3,2,1,0:T(8,128)(2,1)S(1)}, bf16[3,2,48,256]{3,2,1,0:T(8,128)(2,1)}, u32[]{:S(2)}) copy-start(bf16[3,2,48,256]{3,2,1,0:T(8,128)(2,1)} %get-tuple-element.57) | copy-start | bytes 442372
  73.7 22.8 %copy-start.35 = (bf16[3,2,48,256]{3,2,1,0:T(8,128)(2,1)S(1)}, bf16[3,2,48,256]{3,2,1,0:T(8,128)(2,1)}, u32[]{:S(2)}) copy-start(bf16[3,2,48,256]{3,2,1,0:T(8,128)(2,1)} %get-tuple-element.60) | copy-start | bytes 442372
  73.7 22.8 %copy-start.34 = (bf16[3,2,48,256]{3,2,1,0:T(8,128)(2,1)S(1)}, bf16[3,2,48,256]{3,2,1,0:T(8,128)(2,1)}, u32[]{:S(2)}) copy-start(bf16[3,2,48,256]{3,2,1,0:T(8,128)(2,1)} %get-tuple-element.63) | copy-start | bytes 442372
  75.9 13.0 %collective-permute-start.4 = (bf16[256,384]{1,0:T(8,128)(2,1)S(1)}, bf16[256,384]{1,0:T(8,128)(2,1)S(1)}, u32[]{:S(2)}, u32[]{:S(2)}) collective-permute-start(bf16[256,384]{1,0:T(8,128)(2,1)S(1)} %get-tuple-element.80), channel_id=1, source_target_pairs={{0,24},{8,16},{16,8},{24,0},{1,25},{9,17},{17,9},{25,1},{2,26},{10... | collective-permute-start | bytes 589832 | tf_op jit(solution)/shard_map/ppermute | solution.py:499
  79.5 17.0 %collective-permute-start.3 = (bf16[256,384]{1,0:T(8,128)(2,1)S(1)}, bf16[256,384]{1,0:T(8,128)(2,1)S(1)}, u32[]{:S(2)}, u32[]{:S(2)}) collective-permute-start(bf16[256,384]{1,0:T(8,128)(2,1)S(1)} %get-tuple-element.81), channel_id=1, source_target_pairs={{0,16},{8,24},{16,0},{24,8},{1,17},{9,25},{17,1},{25,9},{2,18},{10... | collective-permute-start | bytes 589832 | tf_op jit(solution)/shard_map/ppermute | solution.py:499
  79.5 17.0 %collective-permute-start.2 = (bf16[256,384]{1,0:T(8,128)(2,1)S(1)}, bf16[256,384]{1,0:T(8,128)(2,1)S(1)}, u32[]{:S(2)}, u32[]{:S(2)}) collective-permute-start(bf16[256,384]{1,0:T(8,128)(2,1)S(1)} %get-tuple-element.82), channel_id=1, source_target_pairs={{0,8},{8,0},{16,24},{24,16},{1,9},{9,1},{17,25},{25,17},{2,10},{10... | collective-permute-start | bytes 589832 | tf_op jit(solution)/shard_map/ppermute | solution.py:499
  80.3 1.6 collective-permute-start.5
  80.3 6.5 %collective-permute-start.17 = (bf16[3,2,48,256]{3,2,1,0:T(8,128)(2,1)S(1)}, bf16[3,2,48,256]{3,2,1,0:T(8,128)(2,1)S(1)}, u32[]{:S(2)}, u32[]{:S(2)}) collective-permute-start(bf16[3,2,48,256]{3,2,1,0:T(8,128)(2,1)S(1)} %copy-done.39), channel_id=1, source_target_pairs={{0,7},{1,6},{2,5},{3,4},{4,3},{5,2},{6,1},{7,0},{8,15},{9,14},{10,... | collective-permute-start | bytes 442376 | tf_op jit(solution)/shard_map/ppermute | solution.py:473
  81.9 23.4 %copy-start.19 = (bf16[3,2,48,256]{3,2,1,0:T(8,128)(2,1)}, bf16[3,2,48,256]{3,2,1,0:T(8,128)(2,1)S(1)}, u32[]{:S(2)}) copy-start(bf16[3,2,48,256]{3,2,1,0:T(8,128)(2,1)S(1)} %collective-permute-done.5.refs_1_) | copy-start | bytes 442372
  81.9 16.5 %collective-permute-start.7 = (bf16[3,2,48,256]{3,2,1,0:T(8,128)(2,1)S(1)}, bf16[3,2,48,256]{3,2,1,0:T(8,128)(2,1)S(1)}, u32[]{:S(2)}, u32[]{:S(2)}) collective-permute-start(bf16[3,2,48,256]{3,2,1,0:T(8,128)(2,1)S(1)} %copy-done.38), channel_id=1, source_target_pairs={{0,2},{1,3},{2,0},{3,1},{4,6},{5,7},{6,4},{7,5},{8,10},{9,11},{10,... | collective-permute-start | bytes 442376 | tf_op jit(solution)/shard_map/ppermute | solution.py:473
  86.8 18.4 %copy-start.20 = (bf16[3,2,48,256]{3,2,1,0:T(8,128)(2,1)}, bf16[3,2,48,256]{3,2,1,0:T(8,128)(2,1)S(1)}, u32[]{:S(2)}) copy-start(bf16[3,2,48,256]{3,2,1,0:T(8,128)(2,1)S(1)} %collective-permute-done.17.refs_7_) | copy-start | bytes 442372
  86.8 11.6 %collective-permute-start.9 = (bf16[3,2,48,256]{3,2,1,0:T(8,128)(2,1)S(1)}, bf16[3,2,48,256]{3,2,1,0:T(8,128)(2,1)S(1)}, u32[]{:S(2)}, u32[]{:S(2)}) collective-permute-start(bf16[3,2,48,256]{3,2,1,0:T(8,128)(2,1)S(1)} %copy-done.37), channel_id=1, source_target_pairs={{0,3},{1,2},{2,1},{3,0},{4,7},{5,6},{6,5},{7,4},{8,11},{9,10},{10,... | collective-permute-start | bytes 442376 | tf_op jit(solution)/shard_map/ppermute | solution.py:473
  88.9 21.0 %copy-start.16 = (bf16[256,384]{1,0:T(8,128)(2,1)}, bf16[256,384]{1,0:T(8,128)(2,1)S(1)}, u32[]{:S(2)}) copy-start(bf16[256,384]{1,0:T(8,128)(2,1)S(1)} %collective-permute-done.4.refs_3_) | copy-start | bytes 589828
  88.9 9.5 %collective-permute-start.11 = (bf16[3,2,48,256]{3,2,1,0:T(8,128)(2,1)S(1)}, bf16[3,2,48,256]{3,2,1,0:T(8,128)(2,1)S(1)}, u32[]{:S(2)}, u32[]{:S(2)}) collective-permute-start(bf16[3,2,48,256]{3,2,1,0:T(8,128)(2,1)S(1)} %copy-done.36), channel_id=1, source_target_pairs={{0,4},{1,5},{2,6},{3,7},{4,0},{5,1},{6,2},{7,3},{8,12},{9,13},{10,... | collective-permute-start | bytes 442376 | tf_op jit(solution)/shard_map/ppermute | solution.py:473
  96.4 13.4 %copy-start.17 = (bf16[256,384]{1,0:T(8,128)(2,1)}, bf16[256,384]{1,0:T(8,128)(2,1)S(1)}, u32[]{:S(2)}) copy-start(bf16[256,384]{1,0:T(8,128)(2,1)S(1)} %collective-permute-done.3.refs_2_) | copy-start | bytes 589828
  96.5 8.8 %collective-permute-start.13 = (bf16[3,2,48,256]{3,2,1,0:T(8,128)(2,1)S(1)}, bf16[3,2,48,256]{3,2,1,0:T(8,128)(2,1)S(1)}, u32[]{:S(2)}, u32[]{:S(2)}) collective-permute-start(bf16[3,2,48,256]{3,2,1,0:T(8,128)(2,1)S(1)} %copy-done.35), channel_id=1, source_target_pairs={{0,5},{1,4},{2,7},{3,6},{4,1},{5,0},{6,3},{7,2},{8,13},{9,12},{10,... | collective-permute-start | bytes 442376 | tf_op jit(solution)/shard_map/ppermute | solution.py:473
  96.5 13.4 %copy-start.18 = (bf16[256,384]{1,0:T(8,128)(2,1)}, bf16[256,384]{1,0:T(8,128)(2,1)S(1)}, u32[]{:S(2)}) copy-start(bf16[256,384]{1,0:T(8,128)(2,1)S(1)} %collective-permute-done.2.refs_1_) | copy-start | bytes 589828
  96.5 8.8 %collective-permute-start.15 = (bf16[3,2,48,256]{3,2,1,0:T(8,128)(2,1)S(1)}, bf16[3,2,48,256]{3,2,1,0:T(8,128)(2,1)S(1)}, u32[]{:S(2)}, u32[]{:S(2)}) collective-permute-start(bf16[3,2,48,256]{3,2,1,0:T(8,128)(2,1)S(1)} %copy-done.34), channel_id=1, source_target_pairs={{0,6},{1,7},{2,4},{3,5},{4,2},{5,3},{6,0},{7,1},{8,14},{9,15},{10,... | collective-permute-start | bytes 442376 | tf_op jit(solution)/shard_map/ppermute | solution.py:473
  106.0 19.9 %copy-start.30 = (bf16[5,2,48,256]{3,2,1,0:T(8,128)(2,1)S(1)}, bf16[5,2,48,256]{3,2,1,0:T(8,128)(2,1)}, u32[]{:S(2)}) copy-start(bf16[5,2,48,256]{3,2,1,0:T(8,128)(2,1)} %get-tuple-element.58) | copy-start | bytes 737284
  106.0 26.3 %copy-start.29 = (bf16[5,2,48,256]{3,2,1,0:T(8,128)(2,1)S(1)}, bf16[5,2,48,256]{3,2,1,0:T(8,128)(2,1)}, u32[]{:S(2)}) copy-start(bf16[5,2,48,256]{3,2,1,0:T(8,128)(2,1)} %get-tuple-element.55) | copy-start | bytes 737284
  106.0 31.7 %copy-start.28 = (bf16[5,2,48,256]{3,2,1,0:T(8,128)(2,1)S(1)}, bf16[5,2,48,256]{3,2,1,0:T(8,128)(2,1)}, u32[]{:S(2)}) copy-start(bf16[5,2,48,256]{3,2,1,0:T(8,128)(2,1)} %get-tuple-element.52) | copy-start | bytes 737284
  106.0 32.8 %copy-start.27 = (bf16[5,2,48,256]{3,2,1,0:T(8,128)(2,1)S(1)}, bf16[5,2,48,256]{3,2,1,0:T(8,128)(2,1)}, u32[]{:S(2)}) copy-start(bf16[5,2,48,256]{3,2,1,0:T(8,128)(2,1)} %get-tuple-element.49) | copy-start | bytes 737284
  109.9 16.0 %collective-permute-start.20 = (bf16[2,3,2,48,256]{4,3,2,1,0:T(8,128)(2,1)}, bf16[2,3,2,48,256]{4,3,2,1,0:T(8,128)(2,1)S(1)}, u32[]{:S(2)}, u32[]{:S(2)}) collective-permute-start(bf16[2,3,2,48,256]{4,3,2,1,0:T(8,128)(2,1)} %get-tuple-element.75.refs_0_), channel_id=1, source_target_pairs={{0,16},{8,24},{16,0},{24,8},{1,17},{9,25},{17,1},{25,9},{2,18},{10... | collective-permute-start | bytes 884744 | tf_op jit(solution)/shard_map/ppermute | solution.py:425
  110.0 28.8 %collective-permute-start.19 = (bf16[2,3,2,48,256]{4,3,2,1,0:T(8,128)(2,1)}, bf16[2,3,2,48,256]{4,3,2,1,0:T(8,128)(2,1)S(1)}, u32[]{:S(2)}, u32[]{:S(2)}) collective-permute-start(bf16[2,3,2,48,256]{4,3,2,1,0:T(8,128)(2,1)} %get-tuple-element.75.refs_0_), channel_id=1, source_target_pairs={{0,8},{8,0},{16,24},{24,16},{1,9},{9,1},{17,25},{25,17},{2,10},{10... | collective-permute-start | bytes 884744 | tf_op jit(solution)/shard_map/ppermute | solution.py:426
  113.0 13.9 %collective-permute-start.18 = (bf16[5,2,48,256]{3,2,1,0:T(8,128)(2,1)S(1)}, bf16[5,2,48,256]{3,2,1,0:T(8,128)(2,1)S(1)}, u32[]{:S(2)}, u32[]{:S(2)}) collective-permute-start(bf16[5,2,48,256]{3,2,1,0:T(8,128)(2,1)S(1)} %copy-done.33), channel_id=1, source_target_pairs={{0,7},{1,6},{2,5},{3,4},{4,3},{5,2},{6,1},{7,0},{8,15},{9,14},{10,... | collective-permute-start | bytes 737288 | tf_op jit(solution)/shard_map/ppermute | solution.py:473
  114.2 13.4 %collective-permute-start.16 = (bf16[5,2,48,256]{3,2,1,0:T(8,128)(2,1)S(1)}, bf16[5,2,48,256]{3,2,1,0:T(8,128)(2,1)S(1)}, u32[]{:S(2)}, u32[]{:S(2)}) collective-permute-start(bf16[5,2,48,256]{3,2,1,0:T(8,128)(2,1)S(1)} %copy-done.32), channel_id=1, source_target_pairs={{0,6},{1,7},{2,4},{3,5},{4,2},{5,3},{6,0},{7,1},{8,14},{9,15},{10,... | collective-permute-start | bytes 737288 | tf_op jit(solution)/shard_map/ppermute | solution.py:473
  115.1 17.2 %collective-permute-start.14 = (bf16[5,2,48,256]{3,2,1,0:T(8,128)(2,1)S(1)}, bf16[5,2,48,256]{3,2,1,0:T(8,128)(2,1)S(1)}, u32[]{:S(2)}, u32[]{:S(2)}) collective-permute-start(bf16[5,2,48,256]{3,2,1,0:T(8,128)(2,1)S(1)} %copy-done.31), channel_id=1, source_target_pairs={{0,5},{1,4},{2,7},{3,6},{4,1},{5,0},{6,3},{7,2},{8,13},{9,12},{10,... | collective-permute-start | bytes 737288 | tf_op jit(solution)/shard_map/ppermute | solution.py:473
  125.9 25.3 %copy-start.5 = (bf16[2,3,2,48,256]{4,3,2,1,0:T(8,128)(2,1)}, bf16[2,3,2,48,256]{4,3,2,1,0:T(8,128)(2,1)S(1)}, u32[]{:S(2)}) copy-start(bf16[2,3,2,48,256]{4,3,2,1,0:T(8,128)(2,1)S(1)} %collective-permute-done.20.refs_2_) | copy-start | bytes 884740
  125.9 11.7 %collective-permute-start.12 = (bf16[5,2,48,256]{3,2,1,0:T(8,128)(2,1)S(1)}, bf16[5,2,48,256]{3,2,1,0:T(8,128)(2,1)S(1)}, u32[]{:S(2)}, u32[]{:S(2)}) collective-permute-start(bf16[5,2,48,256]{3,2,1,0:T(8,128)(2,1)S(1)} %copy-done.30), channel_id=1, source_target_pairs={{0,4},{1,5},{2,6},{3,7},{4,0},{5,1},{6,2},{7,3},{8,12},{9,13},{10,... | collective-permute-start | bytes 737288 | tf_op jit(solution)/shard_map/ppermute | solution.py:473
  126.9 18.9 %copy-start.9 = (bf16[5,2,48,256]{3,2,1,0:T(8,128)(2,1)}, bf16[5,2,48,256]{3,2,1,0:T(8,128)(2,1)S(1)}, u32[]{:S(2)}) copy-start(bf16[5,2,48,256]{3,2,1,0:T(8,128)(2,1)S(1)} %collective-permute-done.18.refs_7_) | copy-start | bytes 737284
  126.9 24.3 %collective-permute-start.21 = (bf16[2,3,2,48,256]{4,3,2,1,0:T(8,128)(2,1)}, bf16[2,3,2,48,256]{4,3,2,1,0:T(8,128)(2,1)S(1)}, u32[]{:S(2)}, u32[]{:S(2)}) collective-permute-start(bf16[2,3,2,48,256]{4,3,2,1,0:T(8,128)(2,1)} %get-tuple-element.75.refs_0_), channel_id=1, source_target_pairs={{8,16},{16,8},{9,17},{17,9},{10,18},{18,10},{11,19},{19,11},{12,20... | collective-permute-start | bytes 884744 | tf_op jit(solution)/shard_map/ppermute | solution.py:428
  127.6 18.2 %copy-start.10 = (bf16[5,2,48,256]{3,2,1,0:T(8,128)(2,1)}, bf16[5,2,48,256]{3,2,1,0:T(8,128)(2,1)S(1)}, u32[]{:S(2)}) copy-start(bf16[5,2,48,256]{3,2,1,0:T(8,128)(2,1)S(1)} %collective-permute-done.16.refs_6_) | copy-start | bytes 737284
  127.6 23.6 %collective-permute-start.22 = (bf16[2,3,2,48,256]{4,3,2,1,0:T(8,128)(2,1)S(1)}, bf16[2,3,2,48,256]{4,3,2,1,0:T(8,128)(2,1)S(1)}, u32[]{:S(2)}, u32[]{:S(2)}) collective-permute-start(bf16[2,3,2,48,256]{4,3,2,1,0:T(8,128)(2,1)S(1)} %collective-permute-done.20.refs_2_), channel_id=1, source_target_pairs={{16,24},{8,0},{17,25},{9,1},{18,26},{10,2},{19,27},{11,3},{20,28},... | collective-permute-start | bytes 884744 | tf_op jit(solution)/shard_map/ppermute | solution.py:427
  132.3 13.6 %copy-start.11 = (bf16[5,2,48,256]{3,2,1,0:T(8,128)(2,1)}, bf16[5,2,48,256]{3,2,1,0:T(8,128)(2,1)S(1)}, u32[]{:S(2)}) copy-start(bf16[5,2,48,256]{3,2,1,0:T(8,128)(2,1)S(1)} %collective-permute-done.14.refs_5_) | copy-start | bytes 737284
  132.3 8.0 %collective-permute-start.10 = (bf16[5,2,48,256]{3,2,1,0:T(8,128)(2,1)S(1)}, bf16[5,2,48,256]{3,2,1,0:T(8,128)(2,1)S(1)}, u32[]{:S(2)}, u32[]{:S(2)}) collective-permute-start(bf16[5,2,48,256]{3,2,1,0:T(8,128)(2,1)S(1)} %copy-done.29), channel_id=1, source_target_pairs={{0,3},{1,2},{2,1},{3,0},{4,7},{5,6},{6,5},{7,4},{8,11},{9,10},{10,... | collective-permute-start | bytes 737288 | tf_op jit(solution)/shard_map/ppermute | solution.py:473
  137.6 8.2 %collective-permute-start.8 = (bf16[5,2,48,256]{3,2,1,0:T(8,128)(2,1)S(1)}, bf16[5,2,48,256]{3,2,1,0:T(8,128)(2,1)S(1)}, u32[]{:S(2)}, u32[]{:S(2)}) collective-permute-start(bf16[5,2,48,256]{3,2,1,0:T(8,128)(2,1)S(1)} %copy-done.28), channel_id=1, source_target_pairs={{0,2},{1,3},{2,0},{3,1},{4,6},{5,7},{6,4},{7,5},{8,10},{9,11},{10,... | collective-permute-start | bytes 737288 | tf_op jit(solution)/shard_map/ppermute | solution.py:473
  138.8 7.1 %collective-permute-start.6 = (bf16[5,2,48,256]{3,2,1,0:T(8,128)(2,1)S(1)}, bf16[5,2,48,256]{3,2,1,0:T(8,128)(2,1)S(1)}, u32[]{:S(2)}, u32[]{:S(2)}) collective-permute-start(bf16[5,2,48,256]{3,2,1,0:T(8,128)(2,1)S(1)} %copy-done.27), channel_id=1, source_target_pairs={{0,1},{1,0},{2,3},{3,2},{4,5},{5,4},{6,7},{7,6},{8,9},{9,8},{10,11... | collective-permute-start | bytes 737288 | tf_op jit(solution)/shard_map/ppermute | solution.py:473
  151.2 28.0 %copy-start.7 = (bf16[2,3,2,48,256]{4,3,2,1,0:T(8,128)(2,1)}, bf16[2,3,2,48,256]{4,3,2,1,0:T(8,128)(2,1)S(1)}, u32[]{:S(2)}) copy-start(bf16[2,3,2,48,256]{4,3,2,1,0:T(8,128)(2,1)S(1)} %collective-permute-done.21.refs_3_) | copy-start | bytes 884740
  151.3 28.0 %copy-start.8 = (bf16[2,3,2,48,256]{4,3,2,1,0:T(8,128)(2,1)}, bf16[2,3,2,48,256]{4,3,2,1,0:T(8,128)(2,1)S(1)}, u32[]{:S(2)}) copy-start(bf16[2,3,2,48,256]{4,3,2,1,0:T(8,128)(2,1)S(1)} %collective-permute-done.22.refs_4_) | copy-start | bytes 884740
  151.3 23.7 %collective-permute-start.24 = (bf16[2,5,2,48,256]{4,3,2,1,0:T(8,128)(2,1)}, bf16[2,5,2,48,256]{4,3,2,1,0:T(8,128)(2,1)S(1)}, u32[]{:S(2)}, u32[]{:S(2)}) collective-permute-start(bf16[2,5,2,48,256]{4,3,2,1,0:T(8,128)(2,1)} %get-tuple-element.77.refs_0_), channel_id=1, source_target_pairs={{0,16},{8,24},{16,0},{24,8},{1,17},{9,25},{17,1},{25,9},{2,18},{10... | collective-permute-start | bytes 1474568 | tf_op jit(solution)/shard_map/ppermute | solution.py:425
  151.4 30.8 %collective-permute-start.23 = (bf16[2,5,2,48,256]{4,3,2,1,0:T(8,128)(2,1)}, bf16[2,5,2,48,256]{4,3,2,1,0:T(8,128)(2,1)S(1)}, u32[]{:S(2)}, u32[]{:S(2)}) collective-permute-start(bf16[2,5,2,48,256]{4,3,2,1,0:T(8,128)(2,1)} %get-tuple-element.77.refs_0_), channel_id=1, source_target_pairs={{0,8},{8,0},{16,24},{24,16},{1,9},{9,1},{17,25},{25,17},{2,10},{10... | collective-permute-start | bytes 1474568 | tf_op jit(solution)/shard_map/ppermute | solution.py:426
  175.0 7.2 %collective-permute-start.25 = (bf16[2,5,2,48,256]{4,3,2,1,0:T(8,128)(2,1)}, bf16[2,5,2,48,256]{4,3,2,1,0:T(8,128)(2,1)S(1)}, u32[]{:S(2)}, u32[]{:S(2)}) collective-permute-start(bf16[2,5,2,48,256]{4,3,2,1,0:T(8,128)(2,1)} %get-tuple-element.77.refs_0_), channel_id=1, source_target_pairs={{8,16},{16,8},{9,17},{17,9},{10,18},{18,10},{11,19},{19,11},{12,20... | collective-permute-start | bytes 1474568 | tf_op jit(solution)/shard_map/ppermute | solution.py:428
  175.7 15.0 %collective-permute-start.26 = (bf16[2,5,2,48,256]{4,3,2,1,0:T(8,128)(2,1)S(1)}, bf16[2,5,2,48,256]{4,3,2,1,0:T(8,128)(2,1)S(1)}, u32[]{:S(2)}, u32[]{:S(2)}) collective-permute-start(bf16[2,5,2,48,256]{4,3,2,1,0:T(8,128)(2,1)S(1)} %collective-permute-done.24.refs_2_), channel_id=1, source_target_pairs={{16,24},{8,0},{17,25},{9,1},{18,26},{10,2},{19,27},{11,3},{20,28},... | collective-permute-start | bytes 1474568 | tf_op jit(solution)/shard_map/ppermute | solution.py:427
  (22 other events, 135.4 us)
Sparse Core Ops, SparseCore 0:
  10.1 39.1 all-gather.2

commit v9 on v7

--- a/solution.py
+++ b/solution.py
@@ -9,8 +9,8 @@
 
 SITES = 384
 CAP = 128
-CHUNK_PARTS = (3, 5)
 ID_ROWS = 16
+PARTS = 4
 VMEM_BYTES = 56 * 2**20
 
 gelu_coef = math.sqrt(2.0 / math.pi)
@@ -89,28 +89,23 @@
     )(ids, signals, cotangent)
 
 
-def local_grads(pos, touched, slot_map, rows_in, blocks, sizes, piece, width):
+def local_grads(pos, touched, slot_map, rows_in, blocks, piece, width):
     planes = rows_in[0].shape[0]
     rows = (rows_in[0].shape[1] - ID_ROWS) // 2
     touch = touched.shape[1]
     n_own = blocks.shape[0]
-    half = sum(sizes)
+    half = blocks.shape[1]
     aligned = piece % 16 == 0
-    n_out = n_own if aligned else 1
-    starts = [sum(sizes[:i]) for i in range(len(sizes))]
 
     def body(pos_ref, touched_ref, slot_ref, *rest):
         row_refs = rest[:2]
         blocks_ref = rest[2]
         rest = rest[3:]
         pred_refs = rest[:2]
-        grad_refs = rest[2:-8]
+        grad_ref = rest[2]
         acc, id_cols, held, sorted_rows, pred, full_of, tasks, sems = rest[-8:]
         own_at = pos_ref[1]
         core = lax.rem(own_at, 2)
-
-        def sites(j):
-            return pl.ds(pl.multiple_of((own_at ^ j) * piece, 16), piece)
 
         row_copies = [
             pltpu.make_async_copy(ref, sorted_rows.at[pl.ds(i * planes, planes)], sems.at[i])
@@ -205,25 +200,19 @@
         lax.fori_loop(0, (count + 1) // 2, pair, 0)
         for which, ref in enumerate(pred_refs):
             ref[...] = pred[which * planes : (which + 1) * planes]
-        for chunk, (start, size) in enumerate(zip(starts, sizes)):
-            for j in range(n_out):
-                ref = grad_refs[chunk * n_out + j]
-
-                def write(e, _, start=start, ref=ref, j=j):
-                    if aligned:
-                        ref[e] = acc[start + e, :, sites(j), :].astype(jnp.bfloat16)
-                    else:
-                        ref[e] = acc[start + e].astype(jnp.bfloat16)
-                    return 0
-
-                lax.fori_loop(0, size, write, 0)
+
+        def write(e, _):
+            if aligned:
+                for i in range(n_own):
+                    grad_ref[i, e] = acc[e, :, i * piece : (i + 1) * piece, :].astype(jnp.bfloat16)
+            else:
+                grad_ref[e] = acc[e].astype(jnp.bfloat16)
+            return 0
+
+        lax.fori_loop(0, half, write, 0)
 
     pred_shape = jax.ShapeDtypeStruct((planes, rows, SITES), jnp.bfloat16)
-    grad_shapes = [
-        jax.ShapeDtypeStruct((size, 2, piece if aligned else SITES, width), jnp.bfloat16)
-        for size in sizes
-        for _ in range(n_out)
-    ]
+    grad_shape = (n_own, half, 2, piece, width) if aligned else (half, 2, SITES, width)
     most = 2 * planes * (touch + 1)
     scratch = [
         pltpu.VMEM((half, 2, SITES, width), jnp.float32),
@@ -235,169 +224,152 @@
         pltpu.SMEM((4, most + 1), jnp.int32),
         pltpu.SemaphoreType.DMA((2 + n_own,)),
     ]
-    own_at = pos[1]
     if not aligned:
         blocks = blocks.transpose(1, 2, 0, 3, 4).reshape(half, 2, SITES, width)
     found = pl.pallas_call(
         body,
-        out_shape=[pred_shape, pred_shape] + grad_shapes,
+        out_shape=[pred_shape, pred_shape, jax.ShapeDtypeStruct(grad_shape, jnp.bfloat16)],
         in_specs=[smem(), smem(), smem()] + [pl.BlockSpec(memory_space=pl.ANY)] * 3,
-        out_specs=[vmem()] * (2 + len(grad_shapes)),
+        out_specs=[vmem()] * 3,
         scratch_shapes=scratch,
         compiler_params=params(),
         name="local_grads",
     )(pos, touched, slot_map, *rows_in, blocks)
-    grads = []
-    for chunk in range(len(sizes)):
-        outs = list(found[2 + chunk * n_out : 2 + (chunk + 1) * n_out])
-        if not aligned:
-            outs = [
-                lax.dynamic_slice_in_dim(outs[0], (own_at ^ j) * piece, piece, 2)
-                for j in range(n_own)
-            ]
-        grads.append(outs)
+    grads = found[2]
+    if not aligned:
+        grads = grads.reshape(half, 2, n_own, piece, width).transpose(2, 0, 1, 3, 4)
     return found[0], found[1], grads
 
 
-def adam(pos, arrived, weights, moment1, moment2, start, before):
-    n_own = len(arrived)
-    size, _, piece, width = arrived[0].shape
-    number = weights.shape[0]
-    half = number // 2
+def adam(pos, arrived, weights, moment1, moment2):
+    n_own, half, _, piece, width = arrived.shape
     correct_one = 1.0 - 0.9**10
     correct_two = 1.0 - 0.999**10
 
-    def body(pos_ref, *refs):
-        grad_refs = refs[:n_own]
-        w_ref, m1_ref, m2_ref = refs[n_own : n_own + 3]
-        new_w, new_m1, new_m2 = refs[n_own + 3 + len(before) : n_own + 6 + len(before)]
-        grads, w_in, m1_in, m2_in, w_out, m1_out, m2_out, sem_in, sem_grad, sem_out = refs[
-            n_own + 6 + len(before) :
-        ]
-        core = lax.rem(pos_ref[1], 2)
+    def body(pos_ref, arrived_ref, w_ref, m1_ref, m2_ref, *refs):
+        new_w, new_m1, new_m2, grads, w_in, m1_in, m2_in, w_out, m1_out, m2_out = refs[:10]
+        sem_in, sem_out = refs[10:]
         columns = pl.ds(pl.multiple_of(pos_ref[0] * width, 128), width)
-
-        def block_rows(g):
-            return pl.ds((core ^ g) * half + start, size)
-
+        part = half // PARTS
+        steps = [(core, i * part) for core in range(2) for i in range(PARTS)]
         copies = []
-        for g in range(2):
+        for n, (core, first) in enumerate(steps):
+            rows = pl.ds(core * half + first, part)
             copies.append(
                 [
-                    pltpu.make_async_copy(
-                        w_ref.at[block_rows(g), :, :, columns], w_in.at[g], sem_in.at[g, 0]
-                    ),
-                    pltpu.make_async_copy(m1_ref.at[block_rows(g)], m1_in.at[g], sem_in.at[g, 1]),
-                    pltpu.make_async_copy(m2_ref.at[block_rows(g)], m2_in.at[g], sem_in.at[g, 2]),
+                    pltpu.make_async_copy(ref, into.at[rows], sem_in.at[n, i])
+                    for i, (ref, into) in enumerate(
+                        (
+                            (w_ref.at[rows, :, :, columns], w_in),
+                            (m1_ref.at[rows], m1_in),
+                            (m2_ref.at[rows], m2_in),
+                        )
+                    )
                 ]
                 + [
-                    pltpu.make_async_copy(grad_refs[j], grads.at[j], sem_grad.at[j])
-                    for j in range(g, n_own, 2)
+                    pltpu.make_async_copy(
+                        arrived_ref.at[i, pl.ds(first, part)],
+                        grads.at[i, pl.ds(first, part)],
+                        sem_in.at[n, 3 + i // 2],
+                    )
+                    for i in range(core, n_own, 2)
                 ]
             )
-            for copy in copies[g]:
+            for copy in copies[n]:
                 copy.start()
         outs = []
-        for g in range(2):
-            for copy in copies[g]:
+        for n, (core, first) in enumerate(steps):
+            for copy in copies[n]:
                 copy.wait()
 
-            def step(i, _, g=g):
-                gradient = grads[g, i].astype(jnp.float32)
-                for j in range(g + 2, n_own, 2):
-                    gradient = gradient + grads[j, i].astype(jnp.float32)
-                one = 0.9 * m1_in[g, i] + 0.1 * gradient
-                two = 0.999 * m2_in[g, i] + 0.001 * gradient * gradient
-                m1_out[g, i] = one
-                m2_out[g, i] = two
+            def step(i, _, core=core, first=first):
+                gradient = grads[core, first + i].astype(jnp.float32)
+                for j in range(core + 2, n_own, 2):
+                    gradient = gradient + grads[j, first + i].astype(jnp.float32)
+                at = core * half + first + i
+                one = 0.9 * m1_in[at] + 0.1 * gradient
+                two = 0.999 * m2_in[at] + 0.001 * gradient * gradient
+                m1_out[at] = one
+                m2_out[at] = two
                 spread = two * (1.0 / correct_two)
-                updated = w_in[g, i].astype(jnp.float32) - one * (learn_rate / correct_one) / (
+                updated = w_in[at].astype(jnp.float32) - one * (learn_rate / correct_one) / (
                     spread * lax.rsqrt(spread) + 1e-08
                 )
-                w_out[g, i] = updated.astype(jnp.bfloat16)
+                w_out[at] = updated.astype(jnp.bfloat16)
                 return 0
 
-            lax.fori_loop(0, size, step, 0)
-            outs += [
-                pltpu.make_async_copy(w_out.at[g], new_w.at[core ^ g], sem_out.at[g, 0]),
-                pltpu.make_async_copy(m1_out.at[g], new_m1.at[block_rows(g)], sem_out.at[g, 1]),
-                pltpu.make_async_copy(m2_out.at[g], new_m2.at[block_rows(g)], sem_out.at[g, 2]),
-            ]
-            for copy in outs[-3:]:
-                copy.start()
+            lax.fori_loop(0, part, step, 0)
+            rows = pl.ds(core * half + first, part)
+            for i, (held, ref) in enumerate(
+                ((w_out, new_w), (m1_out, new_m1), (m2_out, new_m2))
+            ):
+                outs.append(pltpu.make_async_copy(held.at[rows], ref.at[rows], sem_out.at[n, i]))
+                outs[-1].start()
         for copy in outs:
             copy.wait()
 
     anywhere = pl.BlockSpec(memory_space=pl.ANY)
-    blocks = (2, size, 2, piece, width)
     return pl.pallas_call(
         body,
         out_shape=[
-            jax.ShapeDtypeStruct(blocks, jnp.bfloat16),
+            jax.ShapeDtypeStruct(moment1.shape, jnp.bfloat16),
             jax.ShapeDtypeStruct(moment1.shape, jnp.float32),
             jax.ShapeDtypeStruct(moment1.shape, jnp.float32),
         ],
-        in_specs=[smem()] + [anywhere] * (n_own + 3 + len(before)),
+        in_specs=[smem()] + [anywhere] * 4,
         out_specs=[anywhere] * 3,
-        scratch_shapes=[
-            pltpu.VMEM((n_own,) + blocks[1:], jnp.bfloat16),
-            pltpu.VMEM(blocks, jnp.bfloat16),
-            pltpu.VMEM(blocks, jnp.float32),
-            pltpu.VMEM(blocks, jnp.float32),
-            pltpu.VMEM(blocks, jnp.bfloat16),
-            pltpu.VMEM(blocks, jnp.float32),
-            pltpu.VMEM(blocks, jnp.float32),
-            pltpu.SemaphoreType.DMA((2, 3)),
-            pltpu.SemaphoreType.DMA((n_own,)),
-            pltpu.SemaphoreType.DMA((2, 3)),
+        scratch_shapes=[pltpu.VMEM(arrived.shape, jnp.bfloat16)]
+        + [pltpu.VMEM(moment1.shape, kind) for kind in (jnp.bfloat16, jnp.float32, jnp.float32)] * 2
+        + [
+            pltpu.SemaphoreType.DMA((2 * PARTS, 3 + n_own // 2)),
+            pltpu.SemaphoreType.DMA((2 * PARTS, 3)),
         ],
-        input_output_aliases={1 + n_own + 3 + i: 1 + i for i in range(len(before))},
         compiler_params=params(),
         name="adam_step",
-    )(pos, *arrived, weights, moment1, moment2, *before)
-
-
-def place_weights(gathered, start, half, before):
-    n_dp, _, size, _, piece, width = gathered.shape
-
-    def body(gathered_ref, *refs):
-        out_ref, held, sems, sem_out = refs[-4:]
-        copies = [
-            pltpu.make_async_copy(
-                gathered_ref.at[d], held.at[:, :, :, :, pl.ds(d * width, width)], sems.at[d]
+    )(pos, arrived, weights, moment1, moment2)
+
+
+def place_weights(gathered):
+    n_dp, number, _, piece, width = gathered.shape
+    part = number // PARTS
+
+    def body(gathered_ref, out_ref, held, sems, sem_out):
+        def piece_in(i, d):
+            rows = pl.ds(i * part, part)
+            return pltpu.make_async_copy(
+                gathered_ref.at[d, rows],
+                held.at[rows, :, :, pl.ds(d * width, width)],
+                sems.at[i, d],
             )
-            for d in range(n_dp)
-        ]
-        for copy in copies:
-            copy.start()
-        for copy in copies:
-            copy.wait()
-        outs = [
-            pltpu.make_async_copy(
-                held.at[h], out_ref.at[pl.ds(h * half + start, size)], sem_out.at[h]
-            )
-            for h in range(2)
-        ]
-        for copy in outs:
-            copy.start()
+
+        for i in range(PARTS):
+            for d in range(n_dp):
+                piece_in(i, d).start()
+        outs = []
+        for i in range(PARTS):
+            for d in range(n_dp):
+                piece_in(i, d).wait()
+            rows = pl.ds(i * part, part)
+            outs.append(pltpu.make_async_copy(held.at[rows], out_ref.at[rows], sem_out.at[i]))
+            outs[-1].start()
         for copy in outs:
             copy.wait()
 
     anywhere = pl.BlockSpec(memory_space=pl.ANY)
+    shape = (number, 2, piece, n_dp * width)
     return pl.pallas_call(
         body,
-        out_shape=jax.ShapeDtypeStruct((2 * half, 2, piece, n_dp * width), jnp.bfloat16),
-        in_specs=[anywhere] * (1 + len(before)),
+        out_shape=jax.ShapeDtypeStruct(shape, jnp.bfloat16),
+        in_specs=[anywhere],
         out_specs=anywhere,
         scratch_shapes=[
-            pltpu.VMEM((2, size, 2, piece, n_dp * width), jnp.bfloat16),
-            pltpu.SemaphoreType.DMA((n_dp,)),
-            pltpu.SemaphoreType.DMA((2,)),
+            pltpu.VMEM(shape, jnp.bfloat16),
+            pltpu.SemaphoreType.DMA((PARTS, n_dp)),
+            pltpu.SemaphoreType.DMA((PARTS,)),
         ],
-        input_output_aliases={1: 0} if before else {},
         compiler_params=params(),
         name="place_weights",
-    )(gathered, *before)
+    )(gathered)
 
 
 def after(value, *others):
@@ -436,9 +408,6 @@
     half = number // 2
     rows = signals.shape[0]
     pos = jnp.stack([dp_at, own_at]).astype(jnp.int32)
-    core = lax.rem(own_at, 2)
-    parts_of_half = sum(CHUNK_PARTS)
-    sizes = [half * part // parts_of_half for part in CHUNK_PARTS]
 
     def across(value, j):
         return lax.ppermute(value, "own", [(o, o ^ j) for o in range(n_own)])
@@ -454,13 +423,10 @@
 
     rows_in = (planes, across(planes, 1))
     pred_mine, pred_other, grads = local_grads(
-        pos, touched, slot_map, rows_in, blocks, sizes, piece, width
+        pos, touched, slot_map, rows_in, blocks, piece, width
     )
-    arrived = []
-    for chunk in grads:
-        for j in range(1, n_own if arrived else 1):
-            chunk[j] = after(chunk[j], arrived[-1][j])
-        arrived.append([chunk[0]] + [across(chunk[j], j) for j in range(1, n_own)])
+    arrived = lax.all_to_all(grads, "own", split_axis=0, concat_axis=0, tiled=True)
+
     pred_part = pred_mine + across(pred_other, 1)
 
     def of_plane(j):
@@ -469,19 +435,10 @@
     parts = [of_plane(0)] + [
         lax.ppermute(of_plane(j), "dp", [(d, d ^ j) for d in range(n_dp)]) for j in range(1, n_dp)
     ]
-    arrived[-1][-1] = after(arrived[-1][-1], *parts[1:])
-    arrived[0][-1] = after(arrived[0][-1], pred_part)
-
-    moments = []
-    new_weights = []
-    start = 0
-    for size, ready in zip(sizes, arrived):
-        fresh, *moments = adam(pos, ready, weights, moment1, moment2, start, moments)
-        gathered = lax.all_gather(fresh, "dp", axis=0)
-        new_weights = [place_weights(gathered, start, half, new_weights)]
-        start += size
-    new_weights = new_weights[0]
-    new_moment1, new_moment2 = moments
+    arrived = after(arrived, *parts[1:])
+
+    fresh, new_moment1, new_moment2 = adam(pos, arrived, weights, moment1, moment2)
+    new_weights = place_weights(lax.all_gather(fresh, "dp", axis=0))
 
     predicted = finish_predicted(perm, parts)
     return (predicted, new_weights, new_moment1, new_moment2)

time: 200 us -> 196 us (0.980)
  starting transfers between devices: 21.4 us -> 12.6 us
  waiting for transfers between devices: 119 us -> 126 us
  Pallas kernels: 33.9 us -> 30.4 us
    all_gather x2 -> x1, waiting for transfers between devices: 37.2 us -> 61.8 us  [shards(): new_weights = place_weights(lax.all_gather(fresh, 'dp', axis=0))]
    ppermute x16 -> x2, waiting for transfers between devices: 20.3 us -> 2.65 us  [across(): return lax.ppermute(value, 'own', [(o, o ^ j) for o in range(n_own)])]
    ppermute x16 -> x2, starting transfers between devices: 12.5 us -> 0.08 us  [across(): return lax.ppermute(value, 'own', [(o, o ^ j) for o in range(n_own)])]
    all_to_all x0 -> x1, waiting for transfers between devices: none -> 12.2 us  [shards(): lax.all_to_all(grads, 'own', split_axis=0, concat_axis=0, tiled=True)]
    ppermute x3, waiting for transfers between devices: 26 us -> 14.3 us  [shards(): lax.ppermute(of_plane(j), 'dp', [(d, d ^ j) for d in range(n_dp)])]
    all_to_all x0 -> x1, starting transfers between devices: none -> 3.61 us  [shards(): lax.all_to_all(grads, 'own', split_axis=0, concat_axis=0, tiled=True)]
    pallas_call x5 -> x3, Pallas kernels: 29.3 us -> 25.7 us  [the longest x1 16.4 us: local_grads(): pl.pallas_call(body, out_shape=[pred_shape, pred_shape, jax.ShapeDtypeStr...]
    unnamed x53 -> x11, local copies, waits for them, and re-layouts: 3.79 us -> 4.03 us
  transfers between devices with their start and end apart: 23 -> 9, of which waited for: 12 -> 7; matrix products, arithmetic and copies ran while one was open for 3% -> 4% of each run, Pallas kernels for 5% -> 1%
where the time goes in v9:
time: 196 us; the launch traced here: 193 us
  waiting for transfers between devices  126 us (64%)
  Pallas kernels  30.4 us (16%)
  between operations  14.1 us (7%)
  starting transfers between devices  12.6 us (6%)
  local copies, waits for them, and re-layouts  8.03 us (4%)
  other arithmetic  2.21 us (1%)
    all_gather x1, waiting for transfers between devices, shards(): new_weights = place_weights(lax.all_gather(fresh, 'dp', axis=0))  61.8 us
    all_gather x1, waiting for transfers between devices, shards(): planes = lax.all_gather(packed, 'dp', axis=0)  32 us
    pallas_call x1, Pallas kernels, local_grads(): pl.pallas_call(body, out_shape=[pred_shape, pred_shape, jax.ShapeDtypeStr...  16.4 us
    ppermute x3, waiting for transfers between devices, shards(): lax.ppermute(of_plane(j), 'dp', [(d, d ^ j) for d in range(n_dp)])  14.3 us
    all_to_all x1, waiting for transfers between devices, shards(): lax.all_to_all(grads, 'own', split_axis=0, concat_axis=0, tiled=True)  12.2 us
    pallas_call x1, Pallas kernels, adam(): pl.pallas_call(body, out_shape=[jax.ShapeDtypeStruct(moment1.shape, jnp.b...  6.3 us
    ppermute x3, starting transfers between devices, shards(): lax.ppermute(of_plane(j), 'dp', [(d, d ^ j) for d in range(n_dp)])  4.4 us
    all_to_all x1, starting transfers between devices, shards(): lax.all_to_all(outgoing, 'own', split_axis=0, concat_axis=0, tiled=True)  4.4 us
  transfers between devices with their start and end apart: 9, of which 7 were waited for; matrix products, arithmetic and copies ran while one was open for 4% of the time, Pallas kernels for 1%

profile of v9, /device:TPU:2, one launch (start us, length us, event | category | flops | bytes accessed | tf_op | source)
XLA Modules:
  0.0 193.3 jit_solution(14230300355494001173)
XLA Ops:
  7.2 0.0 all-gather.5.cloned.1.call-start
  7.2 2.4 %pack_rows.1 = (bf16[528,384]{1,0:T(8,128)(2,1)}, bf16[256,256]{1,0:T(8,128)(2,1)}) custom-call(s32[1,256]{1,0:T(1,128)} %bitcast.20, bf16[256,384]{1,0:T(8,128)(2,1)} %sig_ref.1, bf16[256,384]{1,0:T(8,128)(2,1)} %cot_ref.1), custom_call_target="tpu_custom_call" | custom-call | tf_op jit(solution)/shard_map/pack_rows/pallas_call | solution.py:79
  9.6 0.0 all-gather.5.cloned.1.call-update
  9.6 1.2 constant_dynamic-slice_fusion
  10.8 2.0 %broadcast_in_dim.8 = bf16[4,2,8,2,48,256]{5,4,3,2,1,0:T(8,128)(2,1)} broadcast(bf16[2,8,2,48,256]{4,3,2,1,0:T(8,128)(2,1)S(1)} %bitcast.17), dimensions={1,2,3,4,5} | broadcast | bytes 3932160 | tf_op jit(solution)/shard_map/broadcast_in_dim | solution.py:419
  12.9 0.0 copy-start.4
  12.9 4.4 %all-to-all-start = ((bf16[8,8,2,48,256]{4,3,2,1,0:T(8,128)(2,1)}), bf16[8,8,2,48,256]{4,3,2,1,0:T(8,128)(2,1)S(1)}, u32[]{:S(2)}, u32[]{:S(2)}) async-start(bf16[8,8,2,48,256]{4,3,2,1,0:T(8,128)(2,1)} %bitcast.15), calls=%async_computation | async-start | bytes 6291456 | tf_op jit(solution)/shard_map/all_to_all | solution.py:422
  17.3 32.0 %all-gather.5.cloned.1.call-done = bf16[2112,384]{1,0:T(8,128)(2,1)} async-done(((bf16[528,384]{1,0:T(8,128)(2,1)}), bf16[2112,384]{1,0:T(8,128)(2,1)}) %all-gather.5.cloned.1.call-update) | async-done | bytes 1622032 | tf_op jit(solution)/shard_map/all_gather | solution.py:416
  49.3 0.0 collective-permute-start
  49.3 0.0 copy-done.4
  49.3 0.7 copy.13.touched_ref
  50.0 0.6 pad_add_fusion.pos_ref
  50.7 3.0 %all-to-all-done.rest_2_ = bf16[8,8,2,48,256]{4,3,2,1,0:T(8,128)(2,1)S(1)} async-done(((bf16[8,8,2,48,256]{4,3,2,1,0:T(8,128)(2,1)}), bf16[8,8,2,48,256]{4,3,2,1,0:T(8,128)(2,1)S(1)}, u32[]{:S(2)}, u32[]{:S(2)}) %all-to-all-start) | async-done | bytes 3145760 | tf_op jit(solution)/shard_map/all_to_all | solution.py:422
  53.6 0.0 copy-start.1
  53.6 0.0 collective-permute-done.rest_1_
  53.7 1.7 copy-done.1
  55.3 16.4 %local_grads.1 = (bf16[4,256,384]{2,1,0:T(8,128)(2,1)}, bf16[4,256,384]{2,1,0:T(8,128)(2,1)}, bf16[8,8,2,48,256]{4,3,2,1,0:T(8,128)(2,1)}) custom-call(s32[2]{0:T(128)} %pad_add_fusion.pos_ref, s32[32,4]{1,0:T(8,128)} %copy.13.touched_ref, s32[16]{0:T(128)} %slot_ref.1, bf16[4,528,384]{2,1,0:T(8,128)(2,1)} %bitcast.19, ...), custom_call_target="tpu_custom_call" | custom-call | tf_op jit(solution)/shard_map/local_grads/pallas_call | solution.py:229
  71.7 3.6 %all-to-all-start.1 = ((bf16[8,8,2,48,256]{4,3,2,1,0:T(8,128)(2,1)}), bf16[8,8,2,48,256]{4,3,2,1,0:T(8,128)(2,1)S(1)}, u32[]{:S(2)}, u32[]{:S(2)}) async-start(bf16[8,8,2,48,256]{4,3,2,1,0:T(8,128)(2,1)} %get-tuple-element.17), calls=%async_computation.1 | async-start | bytes 6291456 | tf_op jit(solution)/shard_map/all_to_all | solution.py:428
  75.3 0.0 all-gather.7.cloned.1.call-start
  75.4 0.1 collective-permute-start.1
  75.5 2.7 %collective-permute-done.1 = bf16[4,256,384]{2,1,0:T(8,128)(2,1)} collective-permute-done((bf16[4,256,384]{2,1,0:T(8,128)(2,1)}, bf16[4,256,384]{2,1,0:T(8,128)(2,1)}, u32[]{:S(2)}, u32[]{:S(2)}) %collective-permute-start.1) | collective-permute-done | bytes 786464 | tf_op jit(solution)/shard_map/ppermute | solution.py:413
  78.1 1.6 add.20
  79.7 0.8 dynamic-slice_bitcast_fusion
  80.5 1.6 collective-permute-start.2
  82.1 2.6 %collective-permute-start.3 = (bf16[256,384]{1,0:T(8,128)(2,1)S(1)}, bf16[256,384]{1,0:T(8,128)(2,1)S(1)}, u32[]{:S(2)}, u32[]{:S(2)}) collective-permute-start(bf16[256,384]{1,0:T(8,128)(2,1)S(1)} %get-tuple-element.23), channel_id=1, source_target_pairs={{0,16},{8,24},{16,0},{24,8},{1,17},{9,25},{17,1},{25,9},{2,18},{10... | collective-permute-start | bytes 589832 | tf_op jit(solution)/shard_map/ppermute | solution.py:436
  84.7 0.2 collective-permute-start.4
  84.9 6.5 %collective-permute-done.2.refs_1_ = bf16[256,384]{1,0:T(8,128)(2,1)S(1)} collective-permute-done((bf16[256,384]{1,0:T(8,128)(2,1)S(1)}, bf16[256,384]{1,0:T(8,128)(2,1)S(1)}, u32[]{:S(2)}, u32[]{:S(2)}) %collective-permute-start.2) | collective-permute-done | bytes 196640 | tf_op jit(solution)/shard_map/ppermute | solution.py:436
  91.4 0.0 copy-start.2
  91.4 7.8 %collective-permute-done.3.refs_2_ = bf16[256,384]{1,0:T(8,128)(2,1)S(1)} collective-permute-done((bf16[256,384]{1,0:T(8,128)(2,1)S(1)}, bf16[256,384]{1,0:T(8,128)(2,1)S(1)}, u32[]{:S(2)}, u32[]{:S(2)}) %collective-permute-start.3) | collective-permute-done | bytes 196640 | tf_op jit(solution)/shard_map/ppermute | solution.py:436
  99.2 0.0 copy-start.3
  99.2 0.0 collective-permute-done.4.refs_3_
  99.2 12.2 %all-to-all-done.1.arrived_ref = bf16[8,8,2,48,256]{4,3,2,1,0:T(8,128)(2,1)S(1)} async-done(((bf16[8,8,2,48,256]{4,3,2,1,0:T(8,128)(2,1)}), bf16[8,8,2,48,256]{4,3,2,1,0:T(8,128)(2,1)S(1)}, u32[]{:S(2)}, u32[]{:S(2)}) %all-to-all-start.1) | async-done | bytes 3145760 | tf_op jit(solution)/shard_map/all_to_all | solution.py:428
  111.4 0.0 copy-start
  111.4 1.7 copy-done
  113.1 6.3 %adam_step.1 = (bf16[16,2,48,256]{3,2,1,0:T(8,128)(2,1)}, f32[16,2,48,256]{3,2,1,0:T(8,128)}, f32[16,2,48,256]{3,2,1,0:T(8,128)}) custom-call(s32[2]{0:T(128)} %pad_add_fusion.pos_ref, bf16[8,8,2,48,256]{4,3,2,1,0:T(8,128)(2,1)} %copy-done, bf16[16,2,48,1024]{3,2,1,0:T(8,128)(2,1)} %w_ref.1, f32[16,2,48,256]{3,2,1,0:T(8,128)} %m1_ref.1, ...), custom_call_target="tpu_custom_call" | custom-call | tf_op jit(solution)/shard_map/adam_step/pallas_call | solution.py:312
  119.4 0.0 all-gather.7.cloned.1.call-update
  119.4 0.0 copy-done.2
  119.4 0.0 copy-done.3
  119.4 2.2 %finish_predicted.1 = bf16[256,384]{1,0:T(8,128)(2,1)} custom-call(bf16[256,256]{1,0:T(8,128)(2,1)} %get-tuple-element.13.perm_ref, bf16[256,384]{1,0:T(8,128)(2,1)} %get-tuple-element.25.refs_0_, bf16[256,384]{1,0:T(8,128)(2,1)} %copy-done.2, bf16[256,384]{1,0:T(8,128)(2,1)} %copy-done.3, bf16[256,384]{1,0:T(8,128)(2,1)} %collective-permute-done.4.refs_3_), custom_call_target="tpu_custom_call" | custom-call | tf_op jit(solution)/shard_map/finish_predicted/pallas_call | solution.py:391
  121.6 61.8 %all-gather.7.cloned.1.call-done = bf16[64,2,48,256]{3,2,1,0:T(8,128)(2,1)} async-done(((bf16[16,2,48,256]{3,2,1,0:T(8,128)(2,1)}), bf16[64,2,48,256]{3,2,1,0:T(8,128)(2,1)}) %all-gather.7.cloned.1.call-update) | async-done | bytes 3145744 | tf_op jit(solution)/shard_map/all_gather | solution.py:441
  183.4 3.0 %place_weights.1 = bf16[16,2,48,1024]{3,2,1,0:T(8,128)(2,1)} custom-call(bf16[4,16,2,48,256]{4,3,2,1,0:T(8,128)(2,1)} %bitcast.16), custom_call_target="tpu_custom_call" | custom-call | tf_op jit(solution)/shard_map/place_weights/pallas_call | solution.py:360
Async XLA Ops:
  7.2 42.1 %all-gather.5.cloned.1.call-start = ((), (), s32[]{:S(2)}) async-start(), calls=%async_computation.2 | async-start | bytes 2027520 | tf_op jit(solution)/shard_map/all_gather | solution.py:416
  12.9 36.4 %copy-start.4 = (s32[32,4]{0,1:T(4,128)S(1)}, s32[32,4]{0,1:T(4,128)}, u32[]{:S(2)}) copy-start(s32[32,4]{0,1:T(4,128)} %param.11) | copy-start | bytes 1540
  12.9 40.8 %all-to-all-start = ((bf16[8,8,2,48,256]{4,3,2,1,0:T(8,128)(2,1)}), bf16[8,8,2,48,256]{4,3,2,1,0:T(8,128)(2,1)S(1)}, u32[]{:S(2)}, u32[]{:S(2)}) async-start(bf16[8,8,2,48,256]{4,3,2,1,0:T(8,128)(2,1)} %bitcast.15), calls=%async_computation | async-start | bytes 6291456 | tf_op jit(solution)/shard_map/all_to_all | solution.py:422
  49.3 4.3 %collective-permute-start = (bf16[4,528,384]{2,1,0:T(8,128)(2,1)}, bf16[4,528,384]{2,1,0:T(8,128)(2,1)}, u32[]{:S(2)}, u32[]{:S(2)}) collective-permute-start(bf16[4,528,384]{2,1,0:T(8,128)(2,1)} %bitcast.18), channel_id=1, source_target_pairs={{0,1},{1,0},{2,3},{3,2},{4,5},{5,4},{6,7},{7,6},{8,9},{9,8},{10,11... | collective-permute-start | bytes 4866056 | tf_op jit(solution)/shard_map/ppermute | solution.py:413
  53.6 1.7 copy-start.1
  71.7 39.7 %all-to-all-start.1 = ((bf16[8,8,2,48,256]{4,3,2,1,0:T(8,128)(2,1)}), bf16[8,8,2,48,256]{4,3,2,1,0:T(8,128)(2,1)S(1)}, u32[]{:S(2)}, u32[]{:S(2)}) async-start(bf16[8,8,2,48,256]{4,3,2,1,0:T(8,128)(2,1)} %get-tuple-element.17), calls=%async_computation.1 | async-start | bytes 6291456 | tf_op jit(solution)/shard_map/all_to_all | solution.py:428
  75.3 108.1 %all-gather.7.cloned.1.call-start = ((), (), s32[]{:S(2)}) async-start(), calls=%async_computation.3 | async-start | bytes 3932160 | tf_op jit(solution)/shard_map/all_gather | solution.py:441
  75.4 2.8 %collective-permute-start.1 = (bf16[4,256,384]{2,1,0:T(8,128)(2,1)}, bf16[4,256,384]{2,1,0:T(8,128)(2,1)}, u32[]{:S(2)}, u32[]{:S(2)}) collective-permute-start(bf16[4,256,384]{2,1,0:T(8,128)(2,1)} %get-tuple-element.16), channel_id=1, source_target_pairs={{0,1},{1,0},{2,3},{3,2},{4,5},{5,4},{6,7},{7,6},{8,9},{9,8},{10,11... | collective-permute-start | bytes 2359304 | tf_op jit(solution)/shard_map/ppermute | solution.py:413
  80.5 10.9 %collective-permute-start.2 = (bf16[256,384]{1,0:T(8,128)(2,1)S(1)}, bf16[256,384]{1,0:T(8,128)(2,1)S(1)}, u32[]{:S(2)}, u32[]{:S(2)}) collective-permute-start(bf16[256,384]{1,0:T(8,128)(2,1)S(1)} %get-tuple-element.24), channel_id=1, source_target_pairs={{0,8},{8,0},{16,24},{24,16},{1,9},{9,1},{17,25},{25,17},{2,10},{10... | collective-permute-start | bytes 589832 | tf_op jit(solution)/shard_map/ppermute | solution.py:436
  82.1 17.1 %collective-permute-start.3 = (bf16[256,384]{1,0:T(8,128)(2,1)S(1)}, bf16[256,384]{1,0:T(8,128)(2,1)S(1)}, u32[]{:S(2)}, u32[]{:S(2)}) collective-permute-start(bf16[256,384]{1,0:T(8,128)(2,1)S(1)} %get-tuple-element.23), channel_id=1, source_target_pairs={{0,16},{8,24},{16,0},{24,8},{1,17},{9,25},{17,1},{25,9},{2,18},{10... | collective-permute-start | bytes 589832 | tf_op jit(solution)/shard_map/ppermute | solution.py:436
  84.7 14.5 %collective-permute-start.4 = (bf16[256,384]{1,0:T(8,128)(2,1)S(1)}, bf16[256,384]{1,0:T(8,128)(2,1)}, u32[]{:S(2)}, u32[]{:S(2)}) collective-permute-start(bf16[256,384]{1,0:T(8,128)(2,1)S(1)} %get-tuple-element.22), channel_id=1, source_target_pairs={{0,24},{8,16},{16,8},{24,0},{1,25},{9,17},{17,9},{25,1},{2,26},{10... | collective-permute-start | bytes 589832 | tf_op jit(solution)/shard_map/ppermute | solution.py:436
  91.4 28.0 %copy-start.2 = (bf16[256,384]{1,0:T(8,128)(2,1)}, bf16[256,384]{1,0:T(8,128)(2,1)S(1)}, u32[]{:S(2)}) copy-start(bf16[256,384]{1,0:T(8,128)(2,1)S(1)} %collective-permute-done.2.refs_1_) | copy-start | bytes 589828
  99.2 20.2 %copy-start.3 = (bf16[256,384]{1,0:T(8,128)(2,1)}, bf16[256,384]{1,0:T(8,128)(2,1)S(1)}, u32[]{:S(2)}) copy-start(bf16[256,384]{1,0:T(8,128)(2,1)S(1)} %collective-permute-done.3.refs_2_) | copy-start | bytes 589828
  111.4 1.7 copy-start
Sparse Core Ops, SparseCore 0:
  10.1 39.1 all-gather.4
  119.5 63.8 all-gather.6

commit v10 on v9

--- a/solution.py
+++ b/solution.py
@@ -11,7 +11,8 @@
 CAP = 128
 ID_ROWS = 16
 PARTS = 4
-VMEM_BYTES = 56 * 2**20
+VMEM_BYTES = 60 * 2**20
+SPARE_BYTES = 6 * 2**20
 
 gelu_coef = math.sqrt(2.0 / math.pi)
 cubic_coef = 0.044715
@@ -28,8 +29,12 @@
     return (gelu_val, slopes)
 
 
-def params():
-    return pltpu.CompilerParams(vmem_limit_bytes=VMEM_BYTES)
+def params(*held):
+    need = 0
+    for shape, item in held:
+        rows = -(-shape[-2] // 16) * 16
+        need += math.prod(shape[:-2]) * rows * max(shape[-1], 128) * item
+    return pltpu.CompilerParams(vmem_limit_bytes=min(need + SPARE_BYTES, VMEM_BYTES))
 
 
 def vmem():
@@ -214,12 +219,16 @@
     pred_shape = jax.ShapeDtypeStruct((planes, rows, SITES), jnp.bfloat16)
     grad_shape = (n_own, half, 2, piece, width) if aligned else (half, 2, SITES, width)
     most = 2 * planes * (touch + 1)
+    acc_shape = (half, 2, SITES, width)
+    id_shape = (2 * planes, rows, 128)
+    row_shape = (2 * planes,) + rows_in[0].shape[1:]
+    pred_all = (2 * planes, rows, SITES)
     scratch = [
-        pltpu.VMEM((half, 2, SITES, width), jnp.float32),
-        pltpu.VMEM((2 * planes, rows, 128), jnp.float32),
-        pltpu.VMEM((half, 2, SITES, width), jnp.bfloat16),
-        pltpu.VMEM((2 * planes,) + rows_in[0].shape[1:], jnp.bfloat16),
-        pltpu.VMEM((2 * planes, rows, SITES), jnp.bfloat16),
+        pltpu.VMEM(acc_shape, jnp.float32),
+        pltpu.VMEM(id_shape, jnp.float32),
+        pltpu.VMEM(acc_shape, jnp.bfloat16),
+        pltpu.VMEM(row_shape, jnp.bfloat16),
+        pltpu.VMEM(pred_all, jnp.bfloat16),
         pltpu.SMEM((2 * planes,), jnp.int32),
         pltpu.SMEM((4, most + 1), jnp.int32),
         pltpu.SemaphoreType.DMA((2 + n_own,)),
@@ -232,7 +241,10 @@
         in_specs=[smem(), smem(), smem()] + [pl.BlockSpec(memory_space=pl.ANY)] * 3,
         out_specs=[vmem()] * 3,
         scratch_shapes=scratch,
-        compiler_params=params(),
+        compiler_params=params(
+            (acc_shape, 4), (id_shape, 4), (acc_shape, 2), (row_shape, 2), (pred_all, 2), (pred_all, 2),
+            (grad_shape, 2), *([] if aligned else [(acc_shape, 2)])
+        ),
         name="local_grads",
     )(pos, touched, slot_map, *rows_in, blocks)
     grads = found[2]
@@ -324,52 +336,88 @@
             pltpu.SemaphoreType.DMA((2 * PARTS, 3 + n_own // 2)),
             pltpu.SemaphoreType.DMA((2 * PARTS, 3)),
         ],
-        compiler_params=params(),
+        compiler_params=params((arrived.shape, 2), *[(moment1.shape, 4)] * 5),
         name="adam_step",
     )(pos, arrived, weights, moment1, moment2)
 
 
-def place_weights(gathered):
-    n_dp, number, _, piece, width = gathered.shape
+def place_weights(pos, pieces, shape, before):
+    flat = [(plane, one if isinstance(one, tuple) else (one,)) for plane, one in pieces]
+    arrays = [one for _, group in flat for one in group]
+    number, _, _, width = arrays[0].shape
+    n_dp = shape[3] // width
     part = number // PARTS
 
-    def body(gathered_ref, out_ref, held, sems, sem_out):
-        def piece_in(i, d):
+    def body(pos_ref, *refs):
+        ins = refs[: len(arrays)]
+        out_ref, held, sems, sem_out = refs[-4:]
+        dp_at = pos_ref[0]
+        inner = (dp_at > 0) & (dp_at < n_dp - 1)
+
+        def into(act, i):
             rows = pl.ds(i * part, part)
-            return pltpu.make_async_copy(
-                gathered_ref.at[d, rows],
-                held.at[rows, :, :, pl.ds(d * width, width)],
-                sems.at[i, d],
-            )
+            at = 0
+            for n, (_, group) in enumerate(flat):
+                made = [
+                    pltpu.make_async_copy(ins[at + k].at[rows], held.at[n, rows], sems.at[i, n])
+                    for k in range(len(group))
+                ]
+                at += len(group)
+                if len(made) == 1:
+                    act(made[0])
+                else:
+                    pl.when(inner)(lambda made=made: act(made[0]))
+                    pl.when(~inner)(lambda made=made: act(made[1]))
 
         for i in range(PARTS):
-            for d in range(n_dp):
-                piece_in(i, d).start()
+            into(lambda copy: copy.start(), i)
         outs = []
         for i in range(PARTS):
-            for d in range(n_dp):
-                piece_in(i, d).wait()
+            into(lambda copy: copy.wait(), i)
             rows = pl.ds(i * part, part)
-            outs.append(pltpu.make_async_copy(held.at[rows], out_ref.at[rows], sem_out.at[i]))
-            outs[-1].start()
+            for n, (plane, _) in enumerate(flat):
+                columns = pl.ds(pl.multiple_of((dp_at ^ plane) * width, 128), width)
+                outs.append(
+                    pltpu.make_async_copy(
+                        held.at[n, rows], out_ref.at[rows, :, :, columns], sem_out.at[i, n]
+                    )
+                )
+                outs[-1].start()
         for copy in outs:
             copy.wait()
 
     anywhere = pl.BlockSpec(memory_space=pl.ANY)
-    shape = (number, 2, piece, n_dp * width)
+    held = (len(flat),) + arrays[0].shape
     return pl.pallas_call(
         body,
         out_shape=jax.ShapeDtypeStruct(shape, jnp.bfloat16),
-        in_specs=[anywhere],
+        in_specs=[smem()] + [anywhere] * (len(arrays) + len(before)),
         out_specs=anywhere,
         scratch_shapes=[
-            pltpu.VMEM(shape, jnp.bfloat16),
-            pltpu.SemaphoreType.DMA((PARTS, n_dp)),
-            pltpu.SemaphoreType.DMA((PARTS,)),
+            pltpu.VMEM(held, jnp.bfloat16),
+            pltpu.SemaphoreType.DMA((PARTS, len(flat))),
+            pltpu.SemaphoreType.DMA((PARTS, len(flat))),
         ],
-        compiler_params=params(),
+        input_output_aliases={1 + len(arrays): 0} if before else {},
+        compiler_params=params((held, 2)),
         name="place_weights",
-    )(gathered)
+    )(pos, *arrays, *before)
+
+
+def gather_weights(pos, fresh, dp_at, n_dp):
+    shape = fresh.shape[:3] + (n_dp * fresh.shape[3],)
+    if n_dp != 4:
+        whole = lax.all_gather(fresh, "dp", axis=0)
+        pieces = [
+            (j, lax.dynamic_index_in_dim(whole, dp_at ^ j, 0, keepdims=False)) for j in range(n_dp)
+        ]
+        return place_weights(pos, pieces, shape, [])
+    two = lax.ppermute(fresh, "dp", [(0, 2), (1, 3), (2, 0), (3, 1)])
+    one = lax.ppermute(fresh, "dp", [(0, 1), (1, 0), (2, 3), (3, 2)])
+    outer = lax.ppermute(two, "dp", [(2, 3), (1, 0)])
+    middle = lax.ppermute(after(fresh, two), "dp", [(1, 2), (2, 1)])
+    most = place_weights(pos, [(0, fresh), (1, one), (2, two)], shape, [])
+    return place_weights(pos, [(3, (middle, outer))], shape, [most])
 
 
 def after(value, *others):
@@ -438,7 +486,7 @@
     arrived = after(arrived, *parts[1:])
 
     fresh, new_moment1, new_moment2 = adam(pos, arrived, weights, moment1, moment2)
-    new_weights = place_weights(lax.all_gather(fresh, "dp", axis=0))
+    new_weights = gather_weights(pos, fresh, dp_at, n_dp)
 
     predicted = finish_predicted(perm, parts)
     return (predicted, new_weights, new_moment1, new_moment2)

time: 196 us -> 202 us (1.031)
  waiting for transfers between devices: 126 us -> 111 us
  local copies, waits for them, and re-layouts: 8.03 us -> 17.5 us
  starting transfers between devices: 12.6 us -> 21.3 us
  Pallas kernels: 30.4 us -> 34.6 us
    all_gather x1 -> x0, waiting for transfers between devices: 61.8 us -> none  [shards(): new_weights = place_weights(lax.all_gather(fresh, 'dp', axis=0))]
    ppermute x0 -> x4, waiting for transfers between devices: none -> 46.5 us  [the longest x1 33.2 us: gather_weights(): two = lax.ppermute(fresh, 'dp', [(0, 2), (1, 3), (2, 0), (3, 1)])]
    unnamed x11 -> x37, local copies, waits for them, and re-layouts: 4.03 us -> 14.2 us
    pallas_call x1, Pallas kernels: 6.3 us -> 12.6 us  [adam(): pl.pallas_call(body, out_shape=[jax.ShapeDtypeStruct(moment1.shape, jnp.b...]
    ppermute x0 -> x4, starting transfers between devices: none -> 6.23 us  [the longest x1 2.66 us: gather_weights(): two = lax.ppermute(fresh, 'dp', [(0, 2), (1, 3), (2, 0), (3, 1)])]
    pallas_call x1 -> x2, Pallas kernels: 3.05 us -> 7.68 us  [place_weights(): pl.pallas_call(body, out_shape=jax.ShapeDtypeStruct(shape, jnp.bfloat16),...]
    pallas_call x1, Pallas kernels: 16.4 us -> 12 us  [local_grads(): pl.pallas_call(body, out_shape=[pred_shape, pred_shape, jax.ShapeDtypeStr...]
    all_to_all x1, starting transfers between devices: 3.61 us -> 6.07 us  [shards(): lax.all_to_all(grads, 'own', split_axis=0, concat_axis=0, tiled=True)]
  transfers between devices with their start and end apart: 9 -> 12, of which waited for: 7 -> 8; matrix products, arithmetic and copies ran while one was open for 4% -> 3% of each run, Pallas kernels for 1% -> 3%
where the time goes in v10:
time: 202 us; the launch traced here: 201 us
  waiting for transfers between devices  111 us (55%)
  Pallas kernels  34.6 us (17%)
  starting transfers between devices  21.3 us (11%)
  local copies, waits for them, and re-layouts  17.5 us (9%)
  between operations  14.2 us (7%)
    ppermute x1, waiting for transfers between devices, gather_weights(): two = lax.ppermute(fresh, 'dp', [(0, 2), (1, 3), (2, 0), (3, 1)])  33.2 us
    all_gather x1, waiting for transfers between devices, shards(): planes = lax.all_gather(packed, 'dp', axis=0)  31.6 us
    ppermute x3, waiting for transfers between devices, shards(): lax.ppermute(of_plane(j), 'dp', [(d, d ^ j) for d in range(n_dp)])  14.3 us
    unnamed x37, local copies, waits for them, and re-layouts  14.2 us
    ppermute x1, waiting for transfers between devices, gather_weights(): outer = lax.ppermute(two, 'dp', [(2, 3), (1, 0)])  13.3 us
    pallas_call x1, Pallas kernels, adam(): pl.pallas_call(body, out_shape=[jax.ShapeDtypeStruct(moment1.shape, jnp.b...  12.6 us
    pallas_call x1, Pallas kernels, local_grads(): pl.pallas_call(body, out_shape=[pred_shape, pred_shape, jax.ShapeDtypeStr...  12 us
    all_to_all x1, waiting for transfers between devices, shards(): lax.all_to_all(grads, 'own', split_axis=0, concat_axis=0, tiled=True)  11.7 us
  transfers between devices with their start and end apart: 12, of which 8 were waited for; matrix products, arithmetic and copies ran while one was open for 3% of the time, Pallas kernels for 3%

profile of v10, /device:TPU:2, one launch (start us, length us, event | category | flops | bytes accessed | tf_op | source)
XLA Modules:
  0.0 200.7 jit_solution(8730143710856113076)
XLA Ops:
  7.2 0.0 all-gather.3.cloned.1.call-start
  7.2 0.9 copy-done.6
  8.1 0.9 copy-done.7
  9.1 0.7 copy-done.14
  9.7 1.4 pack_rows.1
  11.1 0.6 copy-done.12
  11.8 0.0 all-gather.3.cloned.1.call-update
  11.8 1.2 constant_dynamic-slice_fusion
  13.0 2.0 %broadcast_in_dim.8 = bf16[4,2,8,2,48,256]{5,4,3,2,1,0:T(8,128)(2,1)} broadcast(bf16[2,8,2,48,256]{4,3,2,1,0:T(8,128)(2,1)S(1)} %bitcast.18), dimensions={1,2,3,4,5} | broadcast | bytes 3932160 | tf_op jit(solution)/shard_map/broadcast_in_dim | solution.py:467
  15.0 4.4 %all-to-all-start = ((bf16[8,8,2,48,256]{4,3,2,1,0:T(8,128)(2,1)}), bf16[8,8,2,48,256]{4,3,2,1,0:T(8,128)(2,1)S(1)}, u32[]{:S(2)}, u32[]{:S(2)}) async-start(bf16[8,8,2,48,256]{4,3,2,1,0:T(8,128)(2,1)} %bitcast.17), calls=%async_computation | async-start | bytes 6291456 | tf_op jit(solution)/shard_map/all_to_all | solution.py:470
  19.4 31.6 %all-gather.3.cloned.1.call-done = bf16[2112,384]{1,0:T(8,128)(2,1)} async-done(((bf16[528,384]{1,0:T(8,128)(2,1)}), bf16[2112,384]{1,0:T(8,128)(2,1)}) %all-gather.3.cloned.1.call-update) | async-done | bytes 1622032 | tf_op jit(solution)/shard_map/all_gather | solution.py:464
  51.1 0.1 copy.13.touched_ref
  51.2 0.1 pad_add_fusion.pos_ref
  51.2 4.6 %all-to-all-done.rest_2_ = bf16[8,8,2,48,256]{4,3,2,1,0:T(8,128)(2,1)S(1)} async-done(((bf16[8,8,2,48,256]{4,3,2,1,0:T(8,128)(2,1)}), bf16[8,8,2,48,256]{4,3,2,1,0:T(8,128)(2,1)S(1)}, u32[]{:S(2)}, u32[]{:S(2)}) %all-to-all-start) | async-done | bytes 3145760 | tf_op jit(solution)/shard_map/all_to_all | solution.py:470
  55.8 1.4 copy-done.2
  57.2 12.0 %local_grads.1 = (bf16[4,256,384]{2,1,0:T(8,128)(2,1)S(1)}, bf16[4,256,384]{2,1,0:T(8,128)(2,1)S(1)}, bf16[8,8,2,48,256]{4,3,2,1,0:T(8,128)(2,1)S(1)}) custom-call(s32[2]{0:T(128)S(1)} %pad_add_fusion.pos_ref, s32[32,4]{1,0:T(8,128)S(1)} %copy.13.touched_ref, s32[16]{0:T(128)S(1)} %copy-done.15, bf16[4,528,384]{2,1,0:T(8,128)(2,1)S(1)} %bitcast.15, ...), custom_call_target="tpu_custom_call" | custom-call | tf_op jit(solution)/shard_map/local_grads/pallas_call | solution.py:238
  69.2 0.0 copy-start.1
  69.2 1.7 copy-done.1
  70.9 0.9 copy-done.5
  71.8 0.9 copy-done.16
  72.7 6.1 %all-to-all-start.1 = ((bf16[8,8,2,48,256]{4,3,2,1,0:T(8,128)(2,1)}), bf16[8,8,2,48,256]{4,3,2,1,0:T(8,128)(2,1)S(1)}, u32[]{:S(2)}, u32[]{:S(2)}) async-start(bf16[8,8,2,48,256]{4,3,2,1,0:T(8,128)(2,1)} %copy-done.1), calls=%async_computation.1 | async-start | bytes 6291456 | tf_op jit(solution)/shard_map/all_to_all | solution.py:476
  78.7 0.1 collective-permute-start.1
  78.9 2.7 %collective-permute-done.1 = bf16[4,256,384]{2,1,0:T(8,128)(2,1)} collective-permute-done((bf16[4,256,384]{2,1,0:T(8,128)(2,1)}, bf16[4,256,384]{2,1,0:T(8,128)(2,1)}, u32[]{:S(2)}, u32[]{:S(2)}) %collective-permute-start.1) | collective-permute-done | bytes 786464 | tf_op jit(solution)/shard_map/ppermute | solution.py:461
  81.5 1.6 add.20
  83.1 0.1 dynamic-slice_bitcast_fusion
  83.2 1.7 collective-permute-start.2
  84.9 2.6 %collective-permute-start.3 = (bf16[256,384]{1,0:T(8,128)(2,1)S(1)}, bf16[256,384]{1,0:T(8,128)(2,1)S(1)}, u32[]{:S(2)}, u32[]{:S(2)}) collective-permute-start(bf16[256,384]{1,0:T(8,128)(2,1)S(1)} %get-tuple-element.25), channel_id=1, source_target_pairs={{0,16},{8,24},{16,0},{24,8},{1,17},{9,25},{17,1},{25,9},{2,18},{10... | collective-permute-start | bytes 589832 | tf_op jit(solution)/shard_map/ppermute | solution.py:484
  87.5 0.2 collective-permute-start.4
  87.7 6.5 %collective-permute-done.2.refs_1_ = bf16[256,384]{1,0:T(8,128)(2,1)S(1)} collective-permute-done((bf16[256,384]{1,0:T(8,128)(2,1)S(1)}, bf16[256,384]{1,0:T(8,128)(2,1)S(1)}, u32[]{:S(2)}, u32[]{:S(2)}) %collective-permute-start.2) | collective-permute-done | bytes 196640 | tf_op jit(solution)/shard_map/ppermute | solution.py:484
  94.2 7.8 %collective-permute-done.3.refs_2_ = bf16[256,384]{1,0:T(8,128)(2,1)S(1)} collective-permute-done((bf16[256,384]{1,0:T(8,128)(2,1)S(1)}, bf16[256,384]{1,0:T(8,128)(2,1)S(1)}, u32[]{:S(2)}, u32[]{:S(2)}) %collective-permute-start.3) | collective-permute-done | bytes 196640 | tf_op jit(solution)/shard_map/ppermute | solution.py:484
  102.0 0.7 copy-done.8
  102.7 0.0 collective-permute-done.4.refs_3_
  102.7 0.7 copy-done.10
  103.3 11.7 %all-to-all-done.1.arrived_ref = bf16[8,8,2,48,256]{4,3,2,1,0:T(8,128)(2,1)S(1)} async-done(((bf16[8,8,2,48,256]{4,3,2,1,0:T(8,128)(2,1)}), bf16[8,8,2,48,256]{4,3,2,1,0:T(8,128)(2,1)S(1)}, u32[]{:S(2)}, u32[]{:S(2)}) %all-to-all-start.1) | async-done | bytes 3145760 | tf_op jit(solution)/shard_map/all_to_all | solution.py:476
  115.1 1.9 copy-done
  117.0 1.4 copy-done.3
  118.4 1.4 copy-done.4
  119.8 12.6 %adam_step.1 = (bf16[16,2,48,256]{3,2,1,0:T(8,128)(2,1)S(1)}, f32[16,2,48,256]{3,2,1,0:T(8,128)}, f32[16,2,48,256]{3,2,1,0:T(8,128)}) custom-call(s32[2]{0:T(128)S(1)} %pad_add_fusion.pos_ref, bf16[8,8,2,48,256]{4,3,2,1,0:T(8,128)(2,1)S(1)} %all-to-all-done.1.arrived_ref, bf16[16,2,48,1024]{3,2,1,0:T(8,128)(2,1)S(1)} %copy-done, ...), custom_call_target="tpu_custom_call" | custom-call | tf_op jit(solution)/shard_map/adam_step/pallas_call | solution.py:324
  132.4 2.7 %collective-permute-start.5 = (bf16[16,2,48,256]{3,2,1,0:T(8,128)(2,1)S(1)}, bf16[16,2,48,256]{3,2,1,0:T(8,128)(2,1)S(1)}, u32[]{:S(2)}, u32[]{:S(2)}) collective-permute-start(bf16[16,2,48,256]{3,2,1,0:T(8,128)(2,1)S(1)} %get-tuple-element.21.refs_0_), channel_id=1, source_target_pairs={{0,16},{8,24},{16,0},{24,8},{1,17},{9,25},{17,1},{25,9},{2,18},{10... | collective-permute-start | bytes 2359304 | tf_op jit(solution)/shard_map/ppermute | solution.py:415
  135.1 1.6 collective-permute-start.8
  136.7 33.2 %collective-permute-done.5.refs_2_ = bf16[16,2,48,256]{3,2,1,0:T(8,128)(2,1)S(1)} collective-permute-done((bf16[16,2,48,256]{3,2,1,0:T(8,128)(2,1)S(1)}, bf16[16,2,48,256]{3,2,1,0:T(8,128)(2,1)S(1)}, u32[]{:S(2)}, u32[]{:S(2)}) %collective-permute-start.5) | collective-permute-done | bytes 786464 | tf_op jit(solution)/shard_map/ppermute | solution.py:415
  169.9 0.7 collective-permute-start.6
  170.6 1.3 collective-permute-start.7
  171.9 1.0 finish_predicted.1
  172.9 5.2 %place_weights.2.refs_2_ = bf16[16,2,48,1024]{3,2,1,0:T(8,128)(2,1)} custom-call(s32[2]{0:T(128)S(1)} %pad_add_fusion.pos_ref, bf16[16,2,48,256]{3,2,1,0:T(8,128)(2,1)S(1)} %get-tuple-element.21.refs_0_, bf16[16,2,48,256]{3,2,1,0:T(8,128)(2,1)S(1)} %collective-permute-done.8.refs_1_, bf16[16,2,48,256]{3,2,1,0:T(8,128)(2,1)S(1)} %collective-permute-done.5.refs_2_), custom_call_target="tpu_custom_call" | custom-call | tf_op jit(solution)/shard_map/place_weights/pallas_call | solution.py:391
  178.1 0.0 collective-permute-done.6.refs_0_
  178.1 13.3 %collective-permute-done.7.refs_1_ = bf16[16,2,48,256]{3,2,1,0:T(8,128)(2,1)S(1)} collective-permute-done((bf16[16,2,48,256]{3,2,1,0:T(8,128)(2,1)S(1)}, bf16[16,2,48,256]{3,2,1,0:T(8,128)(2,1)S(1)}, u32[]{:S(2)}, u32[]{:S(2)}) %collective-permute-start.7) | collective-permute-done | bytes 786464 | tf_op jit(solution)/shard_map/ppermute | solution.py:417
  191.4 2.5 %place_weights.3 = bf16[16,2,48,1024]{3,2,1,0:T(8,128)(2,1)} custom-call(s32[2]{0:T(128)S(1)} %pad_add_fusion.pos_ref, bf16[16,2,48,256]{3,2,1,0:T(8,128)(2,1)S(1)} %collective-permute-done.6.refs_0_, bf16[16,2,48,256]{3,2,1,0:T(8,128)(2,1)S(1)} %collective-permute-done.7.refs_1_, ...), custom_call_target="tpu_custom_call", output_to_operand_aliasing={{}: (3, {})} | custom-call | tf_op jit(solution)/shard_map/place_weights/pallas_call | solution.py:391
  (25 shorter events, 0.0 us)
Async XLA Ops:
  7.2 43.9 %all-gather.3.cloned.1.call-start = ((), (), s32[]{:S(2)}) async-start(), calls=%async_computation.2 | async-start | bytes 2027520 | tf_op jit(solution)/shard_map/all_gather | solution.py:464
  7.2 0.9 copy-start.6
  8.1 0.9 copy-start.7
  9.1 0.7 copy-start.14
  11.1 0.7 copy-start.12
  15.0 36.0 %copy-start.17 = (s32[32,4]{0,1:T(4,128)S(1)}, s32[32,4]{0,1:T(4,128)}, u32[]{:S(2)}) copy-start(s32[32,4]{0,1:T(4,128)} %param.11) | copy-start | bytes 1540
  15.0 40.8 %copy-start.15 = (s32[16]{0:T(128)S(1)}, s32[16]{0:T(128)}, u32[]{:S(2)}) copy-start(s32[16]{0:T(128)} %slot_ref.1) | copy-start | bytes 196
  15.0 40.8 %all-to-all-start = ((bf16[8,8,2,48,256]{4,3,2,1,0:T(8,128)(2,1)}), bf16[8,8,2,48,256]{4,3,2,1,0:T(8,128)(2,1)S(1)}, u32[]{:S(2)}, u32[]{:S(2)}) async-start(bf16[8,8,2,48,256]{4,3,2,1,0:T(8,128)(2,1)} %bitcast.17), calls=%async_computation | async-start | bytes 6291456 | tf_op jit(solution)/shard_map/all_to_all | solution.py:470
  51.1 4.7 %collective-permute-start = (bf16[4,528,384]{2,1,0:T(8,128)(2,1)}, bf16[4,528,384]{2,1,0:T(8,128)(2,1)}, u32[]{:S(2)}, u32[]{:S(2)}) collective-permute-start(bf16[4,528,384]{2,1,0:T(8,128)(2,1)} %bitcast.14), channel_id=1, source_target_pairs={{0,1},{1,0},{2,3},{3,2},{4,5},{5,4},{6,7},{7,6},{8,9},{9,8},{10,11... | collective-permute-start | bytes 4866056 | tf_op jit(solution)/shard_map/ppermute | solution.py:461
  55.8 1.4 copy-start.2
  69.2 1.7 copy-start.1
  70.9 0.9 copy-start.5
  71.8 0.9 copy-start.16
  72.7 42.4 %all-to-all-start.1 = ((bf16[8,8,2,48,256]{4,3,2,1,0:T(8,128)(2,1)}), bf16[8,8,2,48,256]{4,3,2,1,0:T(8,128)(2,1)S(1)}, u32[]{:S(2)}, u32[]{:S(2)}) async-start(bf16[8,8,2,48,256]{4,3,2,1,0:T(8,128)(2,1)} %copy-done.1), calls=%async_computation.1 | async-start | bytes 6291456 | tf_op jit(solution)/shard_map/all_to_all | solution.py:476
  78.7 2.8 %collective-permute-start.1 = (bf16[4,256,384]{2,1,0:T(8,128)(2,1)}, bf16[4,256,384]{2,1,0:T(8,128)(2,1)}, u32[]{:S(2)}, u32[]{:S(2)}) collective-permute-start(bf16[4,256,384]{2,1,0:T(8,128)(2,1)} %copy-done.16), channel_id=1, source_target_pairs={{0,1},{1,0},{2,3},{3,2},{4,5},{5,4},{6,7},{7,6},{8,9},{9,8},{10,11... | collective-permute-start | bytes 2359304 | tf_op jit(solution)/shard_map/ppermute | solution.py:461
  83.2 10.9 %collective-permute-start.2 = (bf16[256,384]{1,0:T(8,128)(2,1)S(1)}, bf16[256,384]{1,0:T(8,128)(2,1)S(1)}, u32[]{:S(2)}, u32[]{:S(2)}) collective-permute-start(bf16[256,384]{1,0:T(8,128)(2,1)S(1)} %get-tuple-element.26), channel_id=1, source_target_pairs={{0,8},{8,0},{16,24},{24,16},{1,9},{9,1},{17,25},{25,17},{2,10},{10... | collective-permute-start | bytes 589832 | tf_op jit(solution)/shard_map/ppermute | solution.py:484
  84.9 17.1 %collective-permute-start.3 = (bf16[256,384]{1,0:T(8,128)(2,1)S(1)}, bf16[256,384]{1,0:T(8,128)(2,1)S(1)}, u32[]{:S(2)}, u32[]{:S(2)}) collective-permute-start(bf16[256,384]{1,0:T(8,128)(2,1)S(1)} %get-tuple-element.25), channel_id=1, source_target_pairs={{0,16},{8,24},{16,0},{24,8},{1,17},{9,25},{17,1},{25,9},{2,18},{10... | collective-permute-start | bytes 589832 | tf_op jit(solution)/shard_map/ppermute | solution.py:484
  87.5 15.2 %collective-permute-start.4 = (bf16[256,384]{1,0:T(8,128)(2,1)S(1)}, bf16[256,384]{1,0:T(8,128)(2,1)S(1)}, u32[]{:S(2)}, u32[]{:S(2)}) collective-permute-start(bf16[256,384]{1,0:T(8,128)(2,1)S(1)} %get-tuple-element.24), channel_id=1, source_target_pairs={{0,24},{8,16},{16,8},{24,0},{1,25},{9,17},{17,9},{25,1},{2,26},{10... | collective-permute-start | bytes 589832 | tf_op jit(solution)/shard_map/ppermute | solution.py:484
  102.0 0.7 copy-start.8
  102.7 0.7 copy-start.10
  115.1 1.9 copy-start
  117.0 1.4 copy-start.3
  118.4 1.4 copy-start.4
  119.8 52.1 %copy-start.9 = (bf16[256,384]{1,0:T(8,128)(2,1)S(1)}, bf16[256,384]{1,0:T(8,128)(2,1)}, u32[]{:S(2)}) copy-start(bf16[256,384]{1,0:T(8,128)(2,1)} %copy-done.8) | copy-start | bytes 589828
  119.8 52.1 %copy-start.11 = (bf16[256,384]{1,0:T(8,128)(2,1)S(1)}, bf16[256,384]{1,0:T(8,128)(2,1)}, u32[]{:S(2)}) copy-start(bf16[256,384]{1,0:T(8,128)(2,1)} %copy-done.10) | copy-start | bytes 589828
  119.8 52.1 %copy-start.13 = (bf16[256,256]{1,0:T(8,128)(2,1)S(1)}, bf16[256,256]{1,0:T(8,128)(2,1)}, u32[]{:S(2)}) copy-start(bf16[256,256]{1,0:T(8,128)(2,1)} %copy-done.12) | copy-start | bytes 393220
  132.4 37.4 %collective-permute-start.5 = (bf16[16,2,48,256]{3,2,1,0:T(8,128)(2,1)S(1)}, bf16[16,2,48,256]{3,2,1,0:T(8,128)(2,1)S(1)}, u32[]{:S(2)}, u32[]{:S(2)}) collective-permute-start(bf16[16,2,48,256]{3,2,1,0:T(8,128)(2,1)S(1)} %get-tuple-element.21.refs_0_), channel_id=1, source_target_pairs={{0,16},{8,24},{16,0},{24,8},{1,17},{9,25},{17,1},{25,9},{2,18},{10... | collective-permute-start | bytes 2359304 | tf_op jit(solution)/shard_map/ppermute | solution.py:415
  135.1 37.8 %collective-permute-start.8 = (bf16[16,2,48,256]{3,2,1,0:T(8,128)(2,1)S(1)}, bf16[16,2,48,256]{3,2,1,0:T(8,128)(2,1)S(1)}, u32[]{:S(2)}, u32[]{:S(2)}) collective-permute-start(bf16[16,2,48,256]{3,2,1,0:T(8,128)(2,1)S(1)} %get-tuple-element.21.refs_0_), channel_id=1, source_target_pairs={{0,8},{8,0},{16,24},{24,16},{1,9},{9,1},{17,25},{25,17},{2,10},{10... | collective-permute-start | bytes 2359304 | tf_op jit(solution)/shard_map/ppermute | solution.py:416
  169.9 8.2 %collective-permute-start.6 = (bf16[16,2,48,256]{3,2,1,0:T(8,128)(2,1)S(1)}, bf16[16,2,48,256]{3,2,1,0:T(8,128)(2,1)S(1)}, u32[]{:S(2)}, u32[]{:S(2)}) collective-permute-start(bf16[16,2,48,256]{3,2,1,0:T(8,128)(2,1)S(1)} %get-tuple-element.21.refs_0_), channel_id=1, source_target_pairs={{8,16},{16,8},{9,17},{17,9},{10,18},{18,10},{11,19},{19,11},{12,20... | collective-permute-start | bytes 2359304 | tf_op jit(solution)/shard_map/ppermute | solution.py:418
  170.6 20.8 %collective-permute-start.7 = (bf16[16,2,48,256]{3,2,1,0:T(8,128)(2,1)S(1)}, bf16[16,2,48,256]{3,2,1,0:T(8,128)(2,1)S(1)}, u32[]{:S(2)}, u32[]{:S(2)}) collective-permute-start(bf16[16,2,48,256]{3,2,1,0:T(8,128)(2,1)S(1)} %collective-permute-done.5.refs_2_), channel_id=1, source_target_pairs={{16,24},{8,0},{17,25},{9,1},{18,26},{10,2},{19,27},{11,3},{20,28},... | collective-permute-start | bytes 2359304 | tf_op jit(solution)/shard_map/ppermute | solution.py:417
Sparse Core Ops, SparseCore 0:
  11.9 39.1 all-gather.2

commit v11 on v10

--- a/solution.py
+++ b/solution.py
@@ -11,8 +11,7 @@
 CAP = 128
 ID_ROWS = 16
 PARTS = 4
-VMEM_BYTES = 60 * 2**20
-SPARE_BYTES = 6 * 2**20
+VMEM_BYTES = 56 * 2**20
 
 gelu_coef = math.sqrt(2.0 / math.pi)
 cubic_coef = 0.044715
@@ -29,12 +28,8 @@
     return (gelu_val, slopes)
 
 
-def params(*held):
-    need = 0
-    for shape, item in held:
-        rows = -(-shape[-2] // 16) * 16
-        need += math.prod(shape[:-2]) * rows * max(shape[-1], 128) * item
-    return pltpu.CompilerParams(vmem_limit_bytes=min(need + SPARE_BYTES, VMEM_BYTES))
+def params():
+    return pltpu.CompilerParams(vmem_limit_bytes=VMEM_BYTES)
 
 
 def vmem():
@@ -98,14 +93,18 @@
     planes = rows_in[0].shape[0]
     rows = (rows_in[0].shape[1] - ID_ROWS) // 2
     touch = touched.shape[1]
-    n_own = blocks.shape[0]
-    half = blocks.shape[1]
-    aligned = piece % 16 == 0
+    n_own = SITES // piece
+    aligned = isinstance(blocks, list)
+    arrays = []
+    for array, _ in blocks if aligned else [(blocks, None)]:
+        if not any(array is one for one in arrays):
+            arrays.append(array)
+    half = arrays[0].shape[-4]
 
     def body(pos_ref, touched_ref, slot_ref, *rest):
         row_refs = rest[:2]
-        blocks_ref = rest[2]
-        rest = rest[3:]
+        block_refs = rest[2 : 2 + len(arrays)]
+        rest = rest[2 + len(arrays) :]
         pred_refs = rest[:2]
         grad_ref = rest[2]
         acc, id_cols, held, sorted_rows, pred, full_of, tasks, sems = rest[-8:]
@@ -117,14 +116,17 @@
             for i, ref in enumerate(row_refs)
         ]
         if aligned:
-            block_copies = [
-                pltpu.make_async_copy(
-                    blocks_ref.at[i], held.at[:, :, pl.ds(i * piece, piece), :], sems.at[2 + i]
+            block_copies = []
+            for j, (array, at) in enumerate(blocks):
+                ref = [one for one, other in zip(block_refs, arrays) if other is array][0]
+                sites = pl.ds(pl.multiple_of((own_at ^ j) * piece, 16), piece)
+                block_copies.append(
+                    pltpu.make_async_copy(
+                        ref if at is None else ref.at[at], held.at[:, :, sites, :], sems.at[2 + j]
+                    )
                 )
-                for i in range(n_own)
-            ]
         else:
-            block_copies = [pltpu.make_async_copy(blocks_ref, held, sems.at[2])]
+            block_copies = [pltpu.make_async_copy(block_refs[0], held, sems.at[2])]
         for copy in row_copies + block_copies:
             copy.start()
 
@@ -145,7 +147,7 @@
             source = t // (touch + 1)
             j = t - source * (touch + 1)
             which = source // planes
-            device = (source - which * planes) * n_own + (own_at ^ which)
+            device = (pos_ref[0] ^ (source - which * planes)) * n_own + (own_at ^ which)
             full = full_of[source]
             insertion = jnp.where(j == 0, full, touched_ref[device, jnp.maximum(j - 1, 0)])
             e = slot_ref[insertion] - core * half
@@ -233,20 +235,15 @@
         pltpu.SMEM((4, most + 1), jnp.int32),
         pltpu.SemaphoreType.DMA((2 + n_own,)),
     ]
-    if not aligned:
-        blocks = blocks.transpose(1, 2, 0, 3, 4).reshape(half, 2, SITES, width)
     found = pl.pallas_call(
         body,
         out_shape=[pred_shape, pred_shape, jax.ShapeDtypeStruct(grad_shape, jnp.bfloat16)],
-        in_specs=[smem(), smem(), smem()] + [pl.BlockSpec(memory_space=pl.ANY)] * 3,
+        in_specs=[smem(), smem(), smem()] + [pl.BlockSpec(memory_space=pl.ANY)] * (2 + len(arrays)),
         out_specs=[vmem()] * 3,
         scratch_shapes=scratch,
-        compiler_params=params(
-            (acc_shape, 4), (id_shape, 4), (acc_shape, 2), (row_shape, 2), (pred_all, 2), (pred_all, 2),
-            (grad_shape, 2), *([] if aligned else [(acc_shape, 2)])
-        ),
+        compiler_params=params(),
         name="local_grads",
-    )(pos, touched, slot_map, *rows_in, blocks)
+    )(pos, touched, slot_map, *rows_in, *arrays)
     grads = found[2]
     if not aligned:
         grads = grads.reshape(half, 2, n_own, piece, width).transpose(2, 0, 1, 3, 4)
@@ -336,7 +333,7 @@
             pltpu.SemaphoreType.DMA((2 * PARTS, 3 + n_own // 2)),
             pltpu.SemaphoreType.DMA((2 * PARTS, 3)),
         ],
-        compiler_params=params((arrived.shape, 2), *[(moment1.shape, 4)] * 5),
+        compiler_params=params(),
         name="adam_step",
     )(pos, arrived, weights, moment1, moment2)
 
@@ -399,25 +396,29 @@
             pltpu.SemaphoreType.DMA((PARTS, len(flat))),
         ],
         input_output_aliases={1 + len(arrays): 0} if before else {},
-        compiler_params=params((held, 2)),
+        compiler_params=params(),
         name="place_weights",
     )(pos, *arrays, *before)
 
 
+def between_planes(value, dp_at, n_dp, first=(), second=()):
+    if n_dp != 4:
+        whole = lax.all_gather(value, "dp", axis=0)
+        return [
+            lax.dynamic_index_in_dim(whole, dp_at ^ j, 0, keepdims=False) for j in range(n_dp)
+        ]
+    two = lax.ppermute(value, "dp", [(0, 2), (1, 3), (2, 0), (3, 1)])
+    one = lax.ppermute(after(value, *first), "dp", [(0, 1), (1, 0), (2, 3), (3, 2)])
+    outer = lax.ppermute(after(two, one, *second), "dp", [(2, 3), (1, 0)])
+    middle = lax.ppermute(after(value, two, one, *second), "dp", [(1, 2), (2, 1)])
+    return [value, one, two, (middle, outer)]
+
+
 def gather_weights(pos, fresh, dp_at, n_dp):
     shape = fresh.shape[:3] + (n_dp * fresh.shape[3],)
-    if n_dp != 4:
-        whole = lax.all_gather(fresh, "dp", axis=0)
-        pieces = [
-            (j, lax.dynamic_index_in_dim(whole, dp_at ^ j, 0, keepdims=False)) for j in range(n_dp)
-        ]
-        return place_weights(pos, pieces, shape, [])
-    two = lax.ppermute(fresh, "dp", [(0, 2), (1, 3), (2, 0), (3, 1)])
-    one = lax.ppermute(fresh, "dp", [(0, 1), (1, 0), (2, 3), (3, 2)])
-    outer = lax.ppermute(two, "dp", [(2, 3), (1, 0)])
-    middle = lax.ppermute(after(fresh, two), "dp", [(1, 2), (2, 1)])
-    most = place_weights(pos, [(0, fresh), (1, one), (2, two)], shape, [])
-    return place_weights(pos, [(3, (middle, outer))], shape, [most])
+    pieces = list(enumerate(between_planes(fresh, dp_at, n_dp)))
+    most = place_weights(pos, pieces[:-1], shape, [])
+    return place_weights(pos, pieces[-1:], shape, [most])
 
 
 def after(value, *others):
@@ -461,15 +462,34 @@
         return lax.ppermute(value, "own", [(o, o ^ j) for o in range(n_own)])
 
     packed, perm = pack_rows(row_insertion.reshape(1, rows), signals, cotangent)
-    planes = lax.all_gather(packed, "dp", axis=0)
-
-    column = lax.dynamic_slice_in_dim(weights, dp_at * width, width, 3)
-    outgoing = jnp.broadcast_to(
-        column.reshape(1, 2, half, 2, piece, width), (n_own // 2, 2, half, 2, piece, width)
-    ).reshape(n_own, half, 2, piece, width)
-    blocks = lax.all_to_all(outgoing, "own", split_axis=0, concat_axis=0, tiled=True)
-
-    rows_in = (planes, across(planes, 1))
+    if n_own == 8 and piece % 16 == 0:
+        core = lax.rem(own_at, 2)
+        columns = [
+            lax.dynamic_slice(
+                weights, (which * half, 0, 0, dp_at * width), (half, 2, piece, width)
+            )
+            for which in (core, 1 - core)
+        ]
+        chip = jnp.stack([columns[0], across(columns[1], 1)])
+        beside = [across(chip, 2), across(chip, 4)]
+        diagonal = [across(beside[0][0], 4), across(beside[1][1], 2)]
+        blocks = [(one, u) for one in [chip] + beside for u in range(2)]
+        blocks += [(one, None) for one in diagonal]
+        first, second, last = [chip], beside, diagonal
+    else:
+        column = lax.dynamic_slice_in_dim(weights, dp_at * width, width, 3)
+        outgoing = jnp.broadcast_to(
+            column.reshape(1, 2, half, 2, piece, width), (n_own // 2, 2, half, 2, piece, width)
+        ).reshape(n_own, half, 2, piece, width)
+        blocks = lax.all_to_all(outgoing, "own", split_axis=0, concat_axis=0, tiled=True)
+        blocks = blocks.transpose(1, 2, 0, 3, 4).reshape(half, 2, SITES, width)
+        first, second, last = [], [], []
+    *near, far = between_planes(packed, dp_at, n_dp, first, second)
+    if isinstance(far, tuple):
+        far = far[0] + far[1]
+    planes = jnp.stack(near + [far])
+    rows_in = (planes, across(after(planes, *last), 1))
+
     pred_mine, pred_other, grads = local_grads(
         pos, touched, slot_map, rows_in, blocks, piece, width
     )
@@ -477,11 +497,8 @@
 
     pred_part = pred_mine + across(pred_other, 1)
 
-    def of_plane(j):
-        return lax.dynamic_index_in_dim(pred_part, dp_at ^ j, 0, keepdims=False)
-
-    parts = [of_plane(0)] + [
-        lax.ppermute(of_plane(j), "dp", [(d, d ^ j) for d in range(n_dp)]) for j in range(1, n_dp)
+    parts = [pred_part[0]] + [
+        lax.ppermute(pred_part[j], "dp", [(d, d ^ j) for d in range(n_dp)]) for j in range(1, n_dp)
     ]
     arrived = after(arrived, *parts[1:])
 

time: 202 us -> 179 us (0.89)
  between operations: 14.2 us -> 0.89 us
  local copies, waits for them, and re-layouts: 17.5 us -> 8.02 us
  starting transfers between devices: 21.3 us -> 26.9 us
  Pallas kernels: 34.6 us -> 31.6 us
  waiting for transfers between devices: 111 us -> 108 us
    all_gather x1 -> x0, waiting for transfers between devices: 31.6 us -> none  [shards(): planes = lax.all_gather(packed, 'dp', axis=0)]
    ppermute x7 -> x11, waiting for transfers between devices: 60.8 us -> 91.8 us  [the longest x2 32.4 us: between_planes(): lax.ppermute(after(value, *first), 'dp', [(0, 1), (1, 0), (2, 3), (3, 2)])]
    unnamed x37 -> x33, local copies, waits for them, and re-layouts: 14.2 us -> 6.01 us
    ppermute x7 -> x11, starting transfers between devices: 10.7 us -> 17.3 us  [the longest x2 5.23 us: between_planes(): two = lax.ppermute(value, 'dp', [(0, 2), (1, 3), (2, 0), (3, 1)])]
    pallas_call x1, Pallas kernels: 12.6 us -> 6.3 us  [adam(): pl.pallas_call(body, out_shape=[jax.ShapeDtypeStruct(moment1.shape, jnp.b...]
    all_to_all x1 -> x0, waiting for transfers between devices: 4.56 us -> none  [shards(): lax.all_to_all(outgoing, 'own', split_axis=0, concat_axis=0, tiled=True)]
    all_to_all x1 -> x0, starting transfers between devices: 4.39 us -> none  [shards(): lax.all_to_all(outgoing, 'own', split_axis=0, concat_axis=0, tiled=True)]
    ppermute x2 -> x7, starting transfers between devices: 0.15 us -> 4.48 us  [across(): return lax.ppermute(value, 'own', [(o, o ^ j) for o in range(n_own)])]
  transfers between devices with their start and end apart: 12 -> 19, of which waited for: 8 -> 11; matrix products, arithmetic and copies ran while one was open for 3% -> 2% of each run, Pallas kernels for 3% -> 5%
where the time goes in v11:
time: 179 us; the launch traced here: 178 us
  waiting for transfers between devices  108 us (60%)
  Pallas kernels  31.6 us (18%)
  starting transfers between devices  26.9 us (15%)
  local copies, waits for them, and re-layouts  8.02 us (4%)
  other arithmetic  2.35 us (1%)
    ppermute x2, waiting for transfers between devices, between_planes(): lax.ppermute(after(value, *first), 'dp', [(0, 1), (1, 0), (2, 3), (3, 2)])  32.4 us
    ppermute x2, waiting for transfers between devices, between_planes(): outer = lax.ppermute(after(two, one, *second), 'dp', [(2, 3), (1, 0)])  25.6 us
    ppermute x3, waiting for transfers between devices, shards(): lax.ppermute(pred_part[j], 'dp', [(d, d ^ j) for d in range(n_dp)])  17.2 us
    ppermute x2, waiting for transfers between devices, between_planes(): two = lax.ppermute(value, 'dp', [(0, 2), (1, 3), (2, 0), (3, 1)])  16.6 us
    pallas_call x1, Pallas kernels, local_grads(): pl.pallas_call(body, out_shape=[pred_shape, pred_shape, jax.ShapeDtypeStr...  14.6 us
    all_to_all x1, waiting for transfers between devices, shards(): lax.all_to_all(grads, 'own', split_axis=0, concat_axis=0, tiled=True)  9.67 us
    ppermute x7, waiting for transfers between devices, across(): return lax.ppermute(value, 'own', [(o, o ^ j) for o in range(n_own)])  6.4 us
    pallas_call x1, Pallas kernels, adam(): pl.pallas_call(body, out_shape=[jax.ShapeDtypeStruct(moment1.shape, jnp.b...  6.3 us
  transfers between devices with their start and end apart: 19, of which 11 were waited for; matrix products, arithmetic and copies ran while one was open for 2% of the time, Pallas kernels for 5%

profile of v11, /device:TPU:2, one launch (start us, length us, event | category | flops | bytes accessed | tf_op | source)
XLA Modules:
  0.0 177.5 jit_solution(14439749020714330068)
XLA Ops:
  0.6 1.2 dynamic-slice_bitcast_fusion
  1.8 0.1 collective-permute-start
  1.9 1.7 collective-permute-done
  3.6 0.1 pad_maximum_fusion.1.rest_2_
  3.7 0.0 copy-start.2
  3.7 1.6 collective-permute-start.4
  5.3 0.5 collective-permute-start.3
  5.8 2.4 %pack_rows.1 = (bf16[528,384]{1,0:T(8,128)(2,1)}, bf16[256,256]{1,0:T(8,128)(2,1)}) custom-call(s32[1,256]{1,0:T(1,128)} %bitcast.27, bf16[256,384]{1,0:T(8,128)(2,1)} %sig_ref.1, bf16[256,384]{1,0:T(8,128)(2,1)} %cot_ref.1), custom_call_target="tpu_custom_call" | custom-call | tf_op jit(solution)/shard_map/pack_rows/pallas_call | solution.py:79
  8.2 2.6 %collective-permute-start.2 = (bf16[528,384]{1,0:T(8,128)(2,1)}, bf16[528,384]{1,0:T(8,128)(2,1)S(1)}, u32[]{:S(2)}, u32[]{:S(2)}) collective-permute-start(bf16[528,384]{1,0:T(8,128)(2,1)} %get-tuple-element.22), channel_id=1, source_target_pairs={{0,16},{8,24},{16,0},{24,8},{1,17},{9,25},{17,1},{25,9},{2,18},{10... | collective-permute-start | bytes 1216520 | tf_op jit(solution)/shard_map/ppermute | solution.py:410
  10.8 1.6 collective-permute-start.1
  12.4 16.6 %collective-permute-done.2 = bf16[528,384]{1,0:T(8,128)(2,1)S(1)} collective-permute-done((bf16[528,384]{1,0:T(8,128)(2,1)}, bf16[528,384]{1,0:T(8,128)(2,1)S(1)}, u32[]{:S(2)}, u32[]{:S(2)}) %collective-permute-start.2) | collective-permute-done | bytes 405536 | tf_op jit(solution)/shard_map/ppermute | solution.py:410
  29.0 0.2 collective-permute-done.1
  29.2 0.7 collective-permute-start.5
  29.9 1.3 collective-permute-start.6
  31.2 1.6 collective-permute-start.8
  32.8 0.6 collective-permute-start.7
  33.4 9.1 %collective-permute-done.6 = bf16[528,384]{1,0:T(8,128)(2,1)S(1)} collective-permute-done((bf16[528,384]{1,0:T(8,128)(2,1)S(1)}, bf16[528,384]{1,0:T(8,128)(2,1)S(1)}, u32[]{:S(2)}, u32[]{:S(2)}) %collective-permute-start.6) | collective-permute-done | bytes 405536 | tf_op jit(solution)/shard_map/ppermute | solution.py:412
  42.5 0.3 pad_maximum_fusion.rest_0_
  42.9 0.8 copy-done.11
  43.6 0.8 copy-done.12
  44.4 0.7 copy.13.touched_ref
  45.1 0.7 pad_add_fusion.pos_ref
  45.7 2.1 %collective-permute-done.9.rest_1_ = bf16[4,528,384]{2,1,0:T(8,128)(2,1)S(1)} collective-permute-done((bf16[4,528,384]{2,1,0:T(8,128)(2,1)S(1)}, bf16[4,528,384]{2,1,0:T(8,128)(2,1)S(1)}, u32[]{:S(2)}, u32[]{:S(2)}) %collective-permute-start.9) | collective-permute-done | bytes 1622048 | tf_op jit(solution)/shard_map/ppermute | solution.py:462
  47.9 1.2 copy-done.5
  49.0 14.6 %local_grads.1 = (bf16[4,256,384]{2,1,0:T(8,128)(2,1)}, bf16[4,256,384]{2,1,0:T(8,128)(2,1)}, bf16[8,8,2,48,256]{4,3,2,1,0:T(8,128)(2,1)}) custom-call(s32[2]{0:T(128)} %pad_add_fusion.pos_ref, s32[32,4]{1,0:T(8,128)} %copy.13.touched_ref, s32[16]{0:T(128)} %slot_ref.1, bf16[4,528,384]{2,1,0:T(8,128)(2,1)} %copy-done.1, bf16[4,528,384]{2,1,0:T(8,128)(2,1)} %copy-done.5, ...), custom_call_target="tpu_custom_call" | custom-call | tf_op jit(solution)/shard_map/local_grads/pallas_call | solution.py:238
  63.7 5.1 %all-to-all-start = ((bf16[8,8,2,48,256]{4,3,2,1,0:T(8,128)(2,1)}), bf16[8,8,2,48,256]{4,3,2,1,0:T(8,128)(2,1)S(1)}, u32[]{:S(2)}, u32[]{:S(2)}) async-start(bf16[8,8,2,48,256]{4,3,2,1,0:T(8,128)(2,1)} %get-tuple-element.27), calls=%async_computation | async-start | bytes 6291456 | tf_op jit(solution)/shard_map/all_to_all | solution.py:496
  68.7 0.1 collective-permute-start.10
  68.9 2.5 %collective-permute-done.10 = bf16[4,256,384]{2,1,0:T(8,128)(2,1)S(1)} collective-permute-done((bf16[4,256,384]{2,1,0:T(8,128)(2,1)}, bf16[4,256,384]{2,1,0:T(8,128)(2,1)S(1)}, u32[]{:S(2)}, u32[]{:S(2)}) %collective-permute-start.10) | collective-permute-done | bytes 786464 | tf_op jit(solution)/shard_map/ppermute | solution.py:462
  71.4 1.3 add.20
  72.8 0.8 slice_bitcast_fusion.2
  73.5 3.9 %collective-permute-start.13 = (bf16[256,384]{1,0:T(8,128)(2,1)S(1)}, bf16[256,384]{1,0:T(8,128)(2,1)S(1)}, u32[]{:S(2)}, u32[]{:S(2)}) collective-permute-start(bf16[256,384]{1,0:T(8,128)(2,1)S(1)} %get-tuple-element.36), channel_id=1, source_target_pairs={{0,24},{8,16},{16,8},{24,0},{1,25},{9,17},{17,9},{25,1},{2,26},{10... | collective-permute-start | bytes 589832 | tf_op jit(solution)/shard_map/ppermute | solution.py:501
  77.4 0.3 collective-permute-start.12
  77.7 0.6 collective-permute-start.11
  78.3 5.0 %collective-permute-done.13.refs_3_ = bf16[256,384]{1,0:T(8,128)(2,1)S(1)} collective-permute-done((bf16[256,384]{1,0:T(8,128)(2,1)S(1)}, bf16[256,384]{1,0:T(8,128)(2,1)S(1)}, u32[]{:S(2)}, u32[]{:S(2)}) %collective-permute-start.13) | collective-permute-done | bytes 196640 | tf_op jit(solution)/shard_map/ppermute | solution.py:501
  83.3 12.2 %collective-permute-done.12.refs_2_ = bf16[256,384]{1,0:T(8,128)(2,1)S(1)} collective-permute-done((bf16[256,384]{1,0:T(8,128)(2,1)S(1)}, bf16[256,384]{1,0:T(8,128)(2,1)S(1)}, u32[]{:S(2)}, u32[]{:S(2)}) %collective-permute-start.12) | collective-permute-done | bytes 196640 | tf_op jit(solution)/shard_map/ppermute | solution.py:501
  95.5 9.7 %all-to-all-done.arrived_ref = bf16[8,8,2,48,256]{4,3,2,1,0:T(8,128)(2,1)S(1)} async-done(((bf16[8,8,2,48,256]{4,3,2,1,0:T(8,128)(2,1)}), bf16[8,8,2,48,256]{4,3,2,1,0:T(8,128)(2,1)S(1)}, u32[]{:S(2)}, u32[]{:S(2)}) %all-to-all-start) | async-done | bytes 3145760 | tf_op jit(solution)/shard_map/all_to_all | solution.py:496
  105.1 1.7 copy-done
  106.8 6.3 %adam_step.1 = (bf16[16,2,48,256]{3,2,1,0:T(8,128)(2,1)}, f32[16,2,48,256]{3,2,1,0:T(8,128)}, f32[16,2,48,256]{3,2,1,0:T(8,128)}) custom-call(s32[2]{0:T(128)} %pad_add_fusion.pos_ref, bf16[8,8,2,48,256]{4,3,2,1,0:T(8,128)(2,1)} %copy-done, bf16[16,2,48,1024]{3,2,1,0:T(8,128)(2,1)} %w_ref.1, f32[16,2,48,256]{3,2,1,0:T(8,128)} %m1_ref.1, ...), custom_call_target="tpu_custom_call" | custom-call | tf_op jit(solution)/shard_map/adam_step/pallas_call | solution.py:321
  113.1 1.8 %collective-permute-start.15 = (bf16[16,2,48,256]{3,2,1,0:T(8,128)(2,1)}, bf16[16,2,48,256]{3,2,1,0:T(8,128)(2,1)S(1)}, u32[]{:S(2)}, u32[]{:S(2)}) collective-permute-start(bf16[16,2,48,256]{3,2,1,0:T(8,128)(2,1)} %get-tuple-element.30.refs_0_), channel_id=1, source_target_pairs={{0,8},{8,0},{16,24},{24,16},{1,9},{9,1},{17,25},{25,17},{2,10},{10... | collective-permute-start | bytes 2359304 | tf_op jit(solution)/shard_map/ppermute | solution.py:411
  114.9 2.6 %collective-permute-start.14 = (bf16[16,2,48,256]{3,2,1,0:T(8,128)(2,1)}, bf16[16,2,48,256]{3,2,1,0:T(8,128)(2,1)S(1)}, u32[]{:S(2)}, u32[]{:S(2)}) collective-permute-start(bf16[16,2,48,256]{3,2,1,0:T(8,128)(2,1)} %get-tuple-element.30.refs_0_), channel_id=1, source_target_pairs={{0,16},{8,24},{16,0},{24,8},{1,17},{9,25},{17,1},{25,9},{2,18},{10... | collective-permute-start | bytes 2359304 | tf_op jit(solution)/shard_map/ppermute | solution.py:410
  117.6 32.2 %collective-permute-done.15.refs_1_ = bf16[16,2,48,256]{3,2,1,0:T(8,128)(2,1)S(1)} collective-permute-done((bf16[16,2,48,256]{3,2,1,0:T(8,128)(2,1)}, bf16[16,2,48,256]{3,2,1,0:T(8,128)(2,1)S(1)}, u32[]{:S(2)}, u32[]{:S(2)}) %collective-permute-start.15) | collective-permute-done | bytes 786464 | tf_op jit(solution)/shard_map/ppermute | solution.py:411
  149.8 0.7 collective-permute-start.16
  150.5 1.3 collective-permute-start.17
  151.8 2.2 %finish_predicted.1 = bf16[256,384]{1,0:T(8,128)(2,1)} custom-call(bf16[256,256]{1,0:T(8,128)(2,1)} %get-tuple-element.19.perm_ref, bf16[256,384]{1,0:T(8,128)(2,1)} %get-tuple-element.39.refs_0_, bf16[256,384]{1,0:T(8,128)(2,1)} %collective-permute-done.11.refs_1_, bf16[256,384]{1,0:T(8,128)(2,1)} %copy-done.14, bf16[256,384]{1,0:T(8,128)(2,1)} %copy-done.13), custom_call_target="tpu_custom_call" | custom-call | tf_op jit(solution)/shard_map/finish_predicted/pallas_call | solution.py:440
  154.0 3.4 %place_weights.2.refs_2_ = bf16[16,2,48,1024]{3,2,1,0:T(8,128)(2,1)} custom-call(s32[2]{0:T(128)} %pad_add_fusion.pos_ref, bf16[16,2,48,256]{3,2,1,0:T(8,128)(2,1)} %get-tuple-element.30.refs_0_, bf16[16,2,48,256]{3,2,1,0:T(8,128)(2,1)} %copy-done.7, bf16[16,2,48,256]{3,2,1,0:T(8,128)(2,1)} %copy-done.6), custom_call_target="tpu_custom_call" | custom-call | tf_op jit(solution)/shard_map/place_weights/pallas_call | solution.py:388
  157.5 16.5 %collective-permute-done.17.refs_1_ = bf16[16,2,48,256]{3,2,1,0:T(8,128)(2,1)S(1)} collective-permute-done((bf16[16,2,48,256]{3,2,1,0:T(8,128)(2,1)S(1)}, bf16[16,2,48,256]{3,2,1,0:T(8,128)(2,1)S(1)}, u32[]{:S(2)}, u32[]{:S(2)}) %collective-permute-start.17) | collective-permute-done | bytes 786464 | tf_op jit(solution)/shard_map/ppermute | solution.py:412
  174.0 0.9 copy-done.9
  174.9 2.6 %place_weights.3 = bf16[16,2,48,1024]{3,2,1,0:T(8,128)(2,1)} custom-call(s32[2]{0:T(128)} %pad_add_fusion.pos_ref, bf16[16,2,48,256]{3,2,1,0:T(8,128)(2,1)} %copy-done.8, bf16[16,2,48,256]{3,2,1,0:T(8,128)(2,1)} %copy-done.9, bf16[16,2,48,1024]{3,2,1,0:T(8,128)(2,1)} %place_weights.2.refs_2_), custom_call_target="tpu_custom_call", output_to_operand_aliasing={{}: (3, {})} | custom-call | tf_op jit(solution)/shard_map/place_weights/pallas_call | solution.py:388
  (38 shorter events, 0.2 us)
Async XLA Ops:
  1.8 1.8 %collective-permute-start = (bf16[8,2,48,256]{3,2,1,0:T(8,128)(2,1)S(1)}, bf16[8,2,48,256]{3,2,1,0:T(8,128)(2,1)S(1)}, u32[]{:S(2)}, u32[]{:S(2)}) collective-permute-start(bf16[8,2,48,256]{3,2,1,0:T(8,128)(2,1)S(1)} %get-tuple-element.35), channel_id=1, source_target_pairs={{0,1},{1,0},{2,3},{3,2},{4,5},{5,4},{6,7},{7,6},{8,9},{9,8},{10,11... | collective-permute-start | bytes 1179656 | tf_op jit(solution)/shard_map/ppermute | solution.py:462
  3.7 39.1 %copy-start.2 = (bf16[2,8,2,48,256]{4,3,2,1,0:T(8,128)(2,1)}, bf16[2,8,2,48,256]{4,3,2,1,0:T(8,128)(2,1)S(1)}, u32[]{:S(2)}) copy-start(bf16[2,8,2,48,256]{4,3,2,1,0:T(8,128)(2,1)S(1)} %pad_maximum_fusion.1.rest_2_) | copy-start | bytes 2359300
  3.7 25.5 %collective-permute-start.4 = (bf16[2,8,2,48,256]{4,3,2,1,0:T(8,128)(2,1)S(1)}, bf16[2,8,2,48,256]{4,3,2,1,0:T(8,128)(2,1)S(1)}, u32[]{:S(2)}, u32[]{:S(2)}) collective-permute-start(bf16[2,8,2,48,256]{4,3,2,1,0:T(8,128)(2,1)S(1)} %pad_maximum_fusion.1.rest_2_), channel_id=1, source_target_pairs={{0,4},{1,5},{2,6},{3,7},{4,0},{5,1},{6,2},{7,3},{8,12},{9,13},{10,... | collective-permute-start | bytes 2359304 | tf_op jit(solution)/shard_map/ppermute | solution.py:462
  5.3 23.9 %collective-permute-start.3 = (bf16[2,8,2,48,256]{4,3,2,1,0:T(8,128)(2,1)S(1)}, bf16[2,8,2,48,256]{4,3,2,1,0:T(8,128)(2,1)S(1)}, u32[]{:S(2)}, u32[]{:S(2)}) collective-permute-start(bf16[2,8,2,48,256]{4,3,2,1,0:T(8,128)(2,1)S(1)} %pad_maximum_fusion.1.rest_2_), channel_id=1, source_target_pairs={{0,2},{1,3},{2,0},{3,1},{4,6},{5,7},{6,4},{7,5},{8,10},{9,11},{10,... | collective-permute-start | bytes 2359304 | tf_op jit(solution)/shard_map/ppermute | solution.py:462
  8.2 34.3 %copy-start.10 = (bf16[528,384]{1,0:T(8,128)(2,1)S(1)}, bf16[528,384]{1,0:T(8,128)(2,1)}, u32[]{:S(2)}) copy-start(bf16[528,384]{1,0:T(8,128)(2,1)} %get-tuple-element.22) | copy-start | bytes 1216516
  8.2 20.8 %collective-permute-start.2 = (bf16[528,384]{1,0:T(8,128)(2,1)}, bf16[528,384]{1,0:T(8,128)(2,1)S(1)}, u32[]{:S(2)}, u32[]{:S(2)}) collective-permute-start(bf16[528,384]{1,0:T(8,128)(2,1)} %get-tuple-element.22), channel_id=1, source_target_pairs={{0,16},{8,24},{16,0},{24,8},{1,17},{9,25},{17,1},{25,9},{2,18},{10... | collective-permute-start | bytes 1216520 | tf_op jit(solution)/shard_map/ppermute | solution.py:410
  10.8 18.4 %collective-permute-start.1 = (bf16[528,384]{1,0:T(8,128)(2,1)}, bf16[528,384]{1,0:T(8,128)(2,1)S(1)}, u32[]{:S(2)}, u32[]{:S(2)}) collective-permute-start(bf16[528,384]{1,0:T(8,128)(2,1)} %get-tuple-element.22), channel_id=1, source_target_pairs={{0,8},{8,0},{16,24},{24,16},{1,9},{9,1},{17,25},{25,17},{2,10},{10... | collective-permute-start | bytes 1216520 | tf_op jit(solution)/shard_map/ppermute | solution.py:411
  29.2 13.6 %copy-start.3 = (bf16[2,8,2,48,256]{4,3,2,1,0:T(8,128)(2,1)}, bf16[2,8,2,48,256]{4,3,2,1,0:T(8,128)(2,1)S(1)}, u32[]{:S(2)}) copy-start(bf16[2,8,2,48,256]{4,3,2,1,0:T(8,128)(2,1)S(1)} %collective-permute-done.4.rest_4_) | copy-start | bytes 2359300
  29.2 13.6 %copy-start.4 = (bf16[2,8,2,48,256]{4,3,2,1,0:T(8,128)(2,1)}, bf16[2,8,2,48,256]{4,3,2,1,0:T(8,128)(2,1)S(1)}, u32[]{:S(2)}) copy-start(bf16[2,8,2,48,256]{4,3,2,1,0:T(8,128)(2,1)S(1)} %collective-permute-done.3.rest_3_) | copy-start | bytes 2359300
  29.2 4.2 %collective-permute-start.5 = (bf16[528,384]{1,0:T(8,128)(2,1)}, bf16[528,384]{1,0:T(8,128)(2,1)S(1)}, u32[]{:S(2)}, u32[]{:S(2)}) collective-permute-start(bf16[528,384]{1,0:T(8,128)(2,1)} %get-tuple-element.22), channel_id=1, source_target_pairs={{8,16},{16,8},{9,17},{17,9},{10,18},{18,10},{11,19},{19,11},{12,20... | collective-permute-start | bytes 1216520 | tf_op jit(solution)/shard_map/ppermute | solution.py:413
  29.9 12.6 %collective-permute-start.6 = (bf16[528,384]{1,0:T(8,128)(2,1)S(1)}, bf16[528,384]{1,0:T(8,128)(2,1)S(1)}, u32[]{:S(2)}, u32[]{:S(2)}) collective-permute-start(bf16[528,384]{1,0:T(8,128)(2,1)S(1)} %collective-permute-done.2), channel_id=1, source_target_pairs={{16,24},{8,0},{17,25},{9,1},{18,26},{10,2},{19,27},{11,3},{20,28},... | collective-permute-start | bytes 1216520 | tf_op jit(solution)/shard_map/ppermute | solution.py:412
  31.2 11.6 %collective-permute-start.8 = (bf16[8,2,48,256]{3,2,1,0:T(8,128)(2,1)S(1)}, bf16[8,2,48,256]{3,2,1,0:T(8,128)(2,1)S(1)}, u32[]{:S(2)}, u32[]{:S(2)}) collective-permute-start(bf16[8,2,48,256]{3,2,1,0:T(8,128)(2,1)S(1)} %slice_bitcast_fusion), channel_id=1, source_target_pairs={{0,2},{1,3},{2,0},{3,1},{4,6},{5,7},{6,4},{7,5},{8,10},{9,11},{10,... | collective-permute-start | bytes 1179656 | tf_op jit(solution)/shard_map/ppermute | solution.py:462
  32.8 10.0 %collective-permute-start.7 = (bf16[8,2,48,256]{3,2,1,0:T(8,128)(2,1)S(1)}, bf16[8,2,48,256]{3,2,1,0:T(8,128)(2,1)S(1)}, u32[]{:S(2)}, u32[]{:S(2)}) collective-permute-start(bf16[8,2,48,256]{3,2,1,0:T(8,128)(2,1)S(1)} %slice_bitcast_fusion.1), channel_id=1, source_target_pairs={{0,4},{1,5},{2,6},{3,7},{4,0},{5,1},{6,2},{7,3},{8,12},{9,13},{10,... | collective-permute-start | bytes 1179656 | tf_op jit(solution)/shard_map/ppermute | solution.py:462
  42.5 1.9 %copy-start.15 = (s32[32,4]{0,1:T(4,128)S(1)}, s32[32,4]{0,1:T(4,128)}, u32[]{:S(2)}) copy-start(s32[32,4]{0,1:T(4,128)} %param.11) | copy-start | bytes 1540
  42.8 5.0 %copy-start.1 = (bf16[4,528,384]{2,1,0:T(8,128)(2,1)}, bf16[4,528,384]{2,1,0:T(8,128)(2,1)S(1)}, u32[]{:S(2)}) copy-start(bf16[4,528,384]{2,1,0:T(8,128)(2,1)S(1)} %pad_maximum_fusion.rest_0_) | copy-start | bytes 4866052
  42.8 0.8 copy-start.11
  43.6 0.8 copy-start.12
  44.4 3.5 %collective-permute-start.9 = (bf16[4,528,384]{2,1,0:T(8,128)(2,1)S(1)}, bf16[4,528,384]{2,1,0:T(8,128)(2,1)S(1)}, u32[]{:S(2)}, u32[]{:S(2)}) collective-permute-start(bf16[4,528,384]{2,1,0:T(8,128)(2,1)S(1)} %pad_maximum_fusion.rest_0_), channel_id=1, source_target_pairs={{0,1},{1,0},{2,3},{3,2},{4,5},{5,4},{6,7},{7,6},{8,9},{9,8},{10,11... | collective-permute-start | bytes 4866056 | tf_op jit(solution)/shard_map/ppermute | solution.py:462
  47.9 1.2 copy-start.5
  63.7 41.5 %all-to-all-start = ((bf16[8,8,2,48,256]{4,3,2,1,0:T(8,128)(2,1)}), bf16[8,8,2,48,256]{4,3,2,1,0:T(8,128)(2,1)S(1)}, u32[]{:S(2)}, u32[]{:S(2)}) async-start(bf16[8,8,2,48,256]{4,3,2,1,0:T(8,128)(2,1)} %get-tuple-element.27), calls=%async_computation | async-start | bytes 6291456 | tf_op jit(solution)/shard_map/all_to_all | solution.py:496
  68.7 2.7 %collective-permute-start.10 = (bf16[4,256,384]{2,1,0:T(8,128)(2,1)}, bf16[4,256,384]{2,1,0:T(8,128)(2,1)S(1)}, u32[]{:S(2)}, u32[]{:S(2)}) collective-permute-start(bf16[4,256,384]{2,1,0:T(8,128)(2,1)} %get-tuple-element.26), channel_id=1, source_target_pairs={{0,1},{1,0},{2,3},{3,2},{4,5},{5,4},{6,7},{7,6},{8,9},{9,8},{10,11... | collective-permute-start | bytes 2359304 | tf_op jit(solution)/shard_map/ppermute | solution.py:462
  73.5 9.7 %collective-permute-start.13 = (bf16[256,384]{1,0:T(8,128)(2,1)S(1)}, bf16[256,384]{1,0:T(8,128)(2,1)S(1)}, u32[]{:S(2)}, u32[]{:S(2)}) collective-permute-start(bf16[256,384]{1,0:T(8,128)(2,1)S(1)} %get-tuple-element.36), channel_id=1, source_target_pairs={{0,24},{8,16},{16,8},{24,0},{1,25},{9,17},{17,9},{25,1},{2,26},{10... | collective-permute-start | bytes 589832 | tf_op jit(solution)/shard_map/ppermute | solution.py:501
  77.4 18.1 %collective-permute-start.12 = (bf16[256,384]{1,0:T(8,128)(2,1)S(1)}, bf16[256,384]{1,0:T(8,128)(2,1)S(1)}, u32[]{:S(2)}, u32[]{:S(2)}) collective-permute-start(bf16[256,384]{1,0:T(8,128)(2,1)S(1)} %get-tuple-element.37), channel_id=1, source_target_pairs={{0,16},{8,24},{16,0},{24,8},{1,17},{9,25},{17,1},{25,9},{2,18},{10... | collective-permute-start | bytes 589832 | tf_op jit(solution)/shard_map/ppermute | solution.py:501
  77.7 17.8 %collective-permute-start.11 = (bf16[256,384]{1,0:T(8,128)(2,1)S(1)}, bf16[256,384]{1,0:T(8,128)(2,1)}, u32[]{:S(2)}, u32[]{:S(2)}) collective-permute-start(bf16[256,384]{1,0:T(8,128)(2,1)S(1)} %get-tuple-element.38), channel_id=1, source_target_pairs={{0,8},{8,0},{16,24},{24,16},{1,9},{9,1},{17,25},{25,17},{2,10},{10... | collective-permute-start | bytes 589832 | tf_op jit(solution)/shard_map/ppermute | solution.py:501
  83.3 68.5 %copy-start.13 = (bf16[256,384]{1,0:T(8,128)(2,1)}, bf16[256,384]{1,0:T(8,128)(2,1)S(1)}, u32[]{:S(2)}) copy-start(bf16[256,384]{1,0:T(8,128)(2,1)S(1)} %collective-permute-done.13.refs_3_) | copy-start | bytes 589828
  95.5 56.3 %copy-start.14 = (bf16[256,384]{1,0:T(8,128)(2,1)}, bf16[256,384]{1,0:T(8,128)(2,1)S(1)}, u32[]{:S(2)}) copy-start(bf16[256,384]{1,0:T(8,128)(2,1)S(1)} %collective-permute-done.12.refs_2_) | copy-start | bytes 589828
  105.1 1.7 copy-start
  113.1 36.7 %collective-permute-start.15 = (bf16[16,2,48,256]{3,2,1,0:T(8,128)(2,1)}, bf16[16,2,48,256]{3,2,1,0:T(8,128)(2,1)S(1)}, u32[]{:S(2)}, u32[]{:S(2)}) collective-permute-start(bf16[16,2,48,256]{3,2,1,0:T(8,128)(2,1)} %get-tuple-element.30.refs_0_), channel_id=1, source_target_pairs={{0,8},{8,0},{16,24},{24,16},{1,9},{9,1},{17,25},{25,17},{2,10},{10... | collective-permute-start | bytes 2359304 | tf_op jit(solution)/shard_map/ppermute | solution.py:411
  114.9 34.8 %collective-permute-start.14 = (bf16[16,2,48,256]{3,2,1,0:T(8,128)(2,1)}, bf16[16,2,48,256]{3,2,1,0:T(8,128)(2,1)S(1)}, u32[]{:S(2)}, u32[]{:S(2)}) collective-permute-start(bf16[16,2,48,256]{3,2,1,0:T(8,128)(2,1)} %get-tuple-element.30.refs_0_), channel_id=1, source_target_pairs={{0,16},{8,24},{16,0},{24,8},{1,17},{9,25},{17,1},{25,9},{2,18},{10... | collective-permute-start | bytes 2359304 | tf_op jit(solution)/shard_map/ppermute | solution.py:410
  149.8 4.3 %copy-start.7 = (bf16[16,2,48,256]{3,2,1,0:T(8,128)(2,1)}, bf16[16,2,48,256]{3,2,1,0:T(8,128)(2,1)S(1)}, u32[]{:S(2)}) copy-start(bf16[16,2,48,256]{3,2,1,0:T(8,128)(2,1)S(1)} %collective-permute-done.15.refs_1_) | copy-start | bytes 2359300
  149.8 4.3 %copy-start.6 = (bf16[16,2,48,256]{3,2,1,0:T(8,128)(2,1)}, bf16[16,2,48,256]{3,2,1,0:T(8,128)(2,1)S(1)}, u32[]{:S(2)}) copy-start(bf16[16,2,48,256]{3,2,1,0:T(8,128)(2,1)S(1)} %collective-permute-done.14.refs_2_) | copy-start | bytes 2359300
  149.8 7.7 %collective-permute-start.16 = (bf16[16,2,48,256]{3,2,1,0:T(8,128)(2,1)}, bf16[16,2,48,256]{3,2,1,0:T(8,128)(2,1)S(1)}, u32[]{:S(2)}, u32[]{:S(2)}) collective-permute-start(bf16[16,2,48,256]{3,2,1,0:T(8,128)(2,1)} %get-tuple-element.30.refs_0_), channel_id=1, source_target_pairs={{8,16},{16,8},{9,17},{17,9},{10,18},{18,10},{11,19},{19,11},{12,20... | collective-permute-start | bytes 2359304 | tf_op jit(solution)/shard_map/ppermute | solution.py:413
  150.5 23.5 %collective-permute-start.17 = (bf16[16,2,48,256]{3,2,1,0:T(8,128)(2,1)S(1)}, bf16[16,2,48,256]{3,2,1,0:T(8,128)(2,1)S(1)}, u32[]{:S(2)}, u32[]{:S(2)}) collective-permute-start(bf16[16,2,48,256]{3,2,1,0:T(8,128)(2,1)S(1)} %collective-permute-done.14.refs_2_), channel_id=1, source_target_pairs={{16,24},{8,0},{17,25},{9,1},{18,26},{10,2},{19,27},{11,3},{20,28},... | collective-permute-start | bytes 2359304 | tf_op jit(solution)/shard_map/ppermute | solution.py:412
  157.5 16.6 %copy-start.8 = (bf16[16,2,48,256]{3,2,1,0:T(8,128)(2,1)}, bf16[16,2,48,256]{3,2,1,0:T(8,128)(2,1)S(1)}, u32[]{:S(2)}) copy-start(bf16[16,2,48,256]{3,2,1,0:T(8,128)(2,1)S(1)} %collective-permute-done.16.refs_0_) | copy-start | bytes 2359300
  174.0 0.9 copy-start.9

commit v12 on v11

--- a/solution.py
+++ b/solution.py
@@ -89,7 +89,7 @@
     )(ids, signals, cotangent)
 
 
-def local_grads(pos, touched, slot_map, rows_in, blocks, piece, width):
+def local_grads(pos, touched, slot_map, rows_in, blocks, sends, piece, width):
     planes = rows_in[0].shape[0]
     rows = (rows_in[0].shape[1] - ID_ROWS) // 2
     touch = touched.shape[1]
@@ -106,7 +106,7 @@
         block_refs = rest[2 : 2 + len(arrays)]
         rest = rest[2 + len(arrays) :]
         pred_refs = rest[:2]
-        grad_ref = rest[2]
+        grad_refs = rest[2:-8]
         acc, id_cols, held, sorted_rows, pred, full_of, tasks, sems = rest[-8:]
         own_at = pos_ref[1]
         core = lax.rem(own_at, 2)
@@ -206,20 +206,30 @@
 
         lax.fori_loop(0, (count + 1) // 2, pair, 0)
         for which, ref in enumerate(pred_refs):
-            ref[...] = pred[which * planes : (which + 1) * planes]
+            for i in range(planes):
+                ref[pos_ref[0] ^ i] = pred[which * planes + i]
 
         def write(e, _):
             if aligned:
-                for i in range(n_own):
-                    grad_ref[i, e] = acc[e, :, i * piece : (i + 1) * piece, :].astype(jnp.bfloat16)
+                for ref, group in zip(grad_refs, sends):
+                    for i, j in enumerate(group):
+                        first = pl.multiple_of((own_at ^ j) * piece, 16)
+                        ref[i, e] = acc[e, :, pl.ds(first, piece), :].astype(jnp.bfloat16)
             else:
-                grad_ref[e] = acc[e].astype(jnp.bfloat16)
+                grad_refs[0][e] = acc[e].astype(jnp.bfloat16)
             return 0
 
         lax.fori_loop(0, half, write, 0)
 
     pred_shape = jax.ShapeDtypeStruct((planes, rows, SITES), jnp.bfloat16)
-    grad_shape = (n_own, half, 2, piece, width) if aligned else (half, 2, SITES, width)
+    grad_shapes = [
+        jax.ShapeDtypeStruct(shape, jnp.bfloat16)
+        for shape in (
+            [(len(group), half, 2, piece, width) for group in sends]
+            if aligned
+            else [(half, 2, SITES, width)]
+        )
+    ]
     most = 2 * planes * (touch + 1)
     acc_shape = (half, 2, SITES, width)
     id_shape = (2 * planes, rows, 128)
@@ -237,33 +247,43 @@
     ]
     found = pl.pallas_call(
         body,
-        out_shape=[pred_shape, pred_shape, jax.ShapeDtypeStruct(grad_shape, jnp.bfloat16)],
+        out_shape=[pred_shape, pred_shape] + grad_shapes,
         in_specs=[smem(), smem(), smem()] + [pl.BlockSpec(memory_space=pl.ANY)] * (2 + len(arrays)),
-        out_specs=[vmem()] * 3,
+        out_specs=[vmem()] * (2 + len(grad_shapes)),
         scratch_shapes=scratch,
         compiler_params=params(),
         name="local_grads",
     )(pos, touched, slot_map, *rows_in, *arrays)
-    grads = found[2]
+    grads = list(found[2:])
     if not aligned:
-        grads = grads.reshape(half, 2, n_own, piece, width).transpose(2, 0, 1, 3, 4)
+        grads = grads[0].reshape(half, 2, n_own, piece, width).transpose(2, 0, 1, 3, 4)
     return found[0], found[1], grads
 
 
-def adam(pos, arrived, weights, moment1, moment2):
-    n_own, half, _, piece, width = arrived.shape
+def adam(pos, terms, weights, moment1, moment2):
+    number, _, piece, width = moment1.shape
+    half = number // 2
+    flat = [one if isinstance(one, tuple) else (one, None) for group in terms for one in group]
+    arrays = [array for array, _ in flat]
+    per = len(terms[0])
     correct_one = 1.0 - 0.9**10
     correct_two = 1.0 - 0.999**10
 
-    def body(pos_ref, arrived_ref, w_ref, m1_ref, m2_ref, *refs):
+    def body(pos_ref, *refs):
+        term_refs = [
+            ref if at is None else ref.at[at] for ref, (_, at) in zip(refs, flat)
+        ]
+        w_ref, m1_ref, m2_ref = refs[len(flat) : len(flat) + 3]
+        refs = refs[len(flat) + 3 :]
         new_w, new_m1, new_m2, grads, w_in, m1_in, m2_in, w_out, m1_out, m2_out = refs[:10]
         sem_in, sem_out = refs[10:]
         columns = pl.ds(pl.multiple_of(pos_ref[0] * width, 128), width)
         part = half // PARTS
-        steps = [(core, i * part) for core in range(2) for i in range(PARTS)]
+        steps = [(g, i * part) for g in range(2) for i in range(PARTS)]
+        own_core = lax.rem(pos_ref[1], 2)
         copies = []
-        for n, (core, first) in enumerate(steps):
-            rows = pl.ds(core * half + first, part)
+        for n, (g, first) in enumerate(steps):
+            rows = pl.ds((own_core ^ g) * half + first, part)
             copies.append(
                 [
                     pltpu.make_async_copy(ref, into.at[rows], sem_in.at[n, i])
@@ -277,25 +297,25 @@
                 ]
                 + [
                     pltpu.make_async_copy(
-                        arrived_ref.at[i, pl.ds(first, part)],
-                        grads.at[i, pl.ds(first, part)],
-                        sem_in.at[n, 3 + i // 2],
+                        term_refs[g * per + i].at[pl.ds(first, part)],
+                        grads.at[g * per + i, pl.ds(first, part)],
+                        sem_in.at[n, 3 + i],
                     )
-                    for i in range(core, n_own, 2)
+                    for i in range(per)
                 ]
             )
             for copy in copies[n]:
                 copy.start()
         outs = []
-        for n, (core, first) in enumerate(steps):
+        for n, (g, first) in enumerate(steps):
             for copy in copies[n]:
                 copy.wait()
 
-            def step(i, _, core=core, first=first):
-                gradient = grads[core, first + i].astype(jnp.float32)
-                for j in range(core + 2, n_own, 2):
-                    gradient = gradient + grads[j, first + i].astype(jnp.float32)
-                at = core * half + first + i
+            def step(i, _, g=g, first=first):
+                gradient = grads[g * per, first + i].astype(jnp.float32)
+                for j in range(1, per):
+                    gradient = gradient + grads[g * per + j, first + i].astype(jnp.float32)
+                at = (own_core ^ g) * half + first + i
                 one = 0.9 * m1_in[at] + 0.1 * gradient
                 two = 0.999 * m2_in[at] + 0.001 * gradient * gradient
                 m1_out[at] = one
@@ -308,7 +328,7 @@
                 return 0
 
             lax.fori_loop(0, part, step, 0)
-            rows = pl.ds(core * half + first, part)
+            rows = pl.ds((own_core ^ g) * half + first, part)
             for i, (held, ref) in enumerate(
                 ((w_out, new_w), (m1_out, new_m1), (m2_out, new_m2))
             ):
@@ -325,17 +345,17 @@
             jax.ShapeDtypeStruct(moment1.shape, jnp.float32),
             jax.ShapeDtypeStruct(moment1.shape, jnp.float32),
         ],
-        in_specs=[smem()] + [anywhere] * 4,
+        in_specs=[smem()] + [anywhere] * (len(flat) + 3),
         out_specs=[anywhere] * 3,
-        scratch_shapes=[pltpu.VMEM(arrived.shape, jnp.bfloat16)]
+        scratch_shapes=[pltpu.VMEM((len(flat), half, 2, piece, width), jnp.bfloat16)]
         + [pltpu.VMEM(moment1.shape, kind) for kind in (jnp.bfloat16, jnp.float32, jnp.float32)] * 2
         + [
-            pltpu.SemaphoreType.DMA((2 * PARTS, 3 + n_own // 2)),
+            pltpu.SemaphoreType.DMA((2 * PARTS, 3 + per)),
             pltpu.SemaphoreType.DMA((2 * PARTS, 3)),
         ],
         compiler_params=params(),
         name="adam_step",
-    )(pos, arrived, weights, moment1, moment2)
+    )(pos, *arrays, weights, moment1, moment2)
 
 
 def place_weights(pos, pieces, shape, before):
@@ -426,11 +446,9 @@
 
 
 def finish_predicted(perm, parts):
-    def body(perm_ref, *refs):
-        total = refs[0][...].astype(jnp.float32)
-        for ref in refs[1:-1]:
-            total = total + ref[...].astype(jnp.float32)
-        refs[-1][...] = lax.dot_general(
+    def body(perm_ref, parts_ref, out_ref):
+        total = jnp.sum(parts_ref[...].astype(jnp.float32), axis=0)
+        out_ref[...] = lax.dot_general(
             perm_ref[...],
             total.astype(jnp.bfloat16),
             (((0,), (0,)), ((), ())),
@@ -439,12 +457,12 @@
 
     return pl.pallas_call(
         body,
-        out_shape=jax.ShapeDtypeStruct(parts[0].shape, jnp.bfloat16),
-        in_specs=[vmem()] * (1 + len(parts)),
+        out_shape=jax.ShapeDtypeStruct(parts.shape[1:], jnp.bfloat16),
+        in_specs=[vmem(), vmem()],
         out_specs=vmem(),
         compiler_params=params(),
         name="finish_predicted",
-    )(perm, *parts)
+    )(perm, parts)
 
 
 def shards(signals, cotangent, row_insertion, touched, slot_map, weights, moment1, moment2):
@@ -470,12 +488,13 @@
             )
             for which in (core, 1 - core)
         ]
-        chip = jnp.stack([columns[0], across(columns[1], 1)])
+        chip = jnp.stack([columns[0], after(across(columns[1], 1), packed)])
         beside = [across(chip, 2), across(chip, 4)]
         diagonal = [across(beside[0][0], 4), across(beside[1][1], 2)]
         blocks = [(one, u) for one in [chip] + beside for u in range(2)]
         blocks += [(one, None) for one in diagonal]
         first, second, last = [chip], beside, diagonal
+        sends = [(0,), (1,), (2, 6), (7,), (5,), (3,), (4,)]
     else:
         column = lax.dynamic_slice_in_dim(weights, dp_at * width, width, 3)
         outgoing = jnp.broadcast_to(
@@ -484,6 +503,7 @@
         blocks = lax.all_to_all(outgoing, "own", split_axis=0, concat_axis=0, tiled=True)
         blocks = blocks.transpose(1, 2, 0, 3, 4).reshape(half, 2, SITES, width)
         first, second, last = [], [], []
+        sends = None
     *near, far = between_planes(packed, dp_at, n_dp, first, second)
     if isinstance(far, tuple):
         far = far[0] + far[1]
@@ -491,21 +511,32 @@
     rows_in = (planes, across(after(planes, *last), 1))
 
     pred_mine, pred_other, grads = local_grads(
-        pos, touched, slot_map, rows_in, blocks, piece, width
+        pos, touched, slot_map, rows_in, blocks, sends, piece, width
     )
-    arrived = lax.all_to_all(grads, "own", split_axis=0, concat_axis=0, tiled=True)
+    if sends:
+        own, partner, x_same, y_diagonal, y_cross, x_cross, y_same = grads
+        x_same = across(x_same, 2)
+        y_diagonal = across(y_diagonal, 4)
+        y_cross = across(y_cross, 5)
+        partner = across(partner, 1)
+        x_cross = across(x_cross[0] + y_diagonal[0], 3)
+        y_same = across(y_same[0] + x_same[1], 4)
+        terms = [[(own, 0), (x_same, 0), y_same], [(partner, 0), (y_cross, 0), x_cross]]
+    else:
+        arrived = lax.all_to_all(grads, "own", split_axis=0, concat_axis=0, tiled=True)
+        arrived = [
+            lax.dynamic_index_in_dim(arrived, own_at ^ j, 0, keepdims=False) for j in range(n_own)
+        ]
+        terms = [arrived[0::2], arrived[1::2]]
 
     pred_part = pred_mine + across(pred_other, 1)
-
-    parts = [pred_part[0]] + [
-        lax.ppermute(pred_part[j], "dp", [(d, d ^ j) for d in range(n_dp)]) for j in range(1, n_dp)
-    ]
-    arrived = after(arrived, *parts[1:])
-
-    fresh, new_moment1, new_moment2 = adam(pos, arrived, weights, moment1, moment2)
+    parts = lax.all_to_all(pred_part, "dp", split_axis=0, concat_axis=0, tiled=True)
+    predicted = finish_predicted(perm, parts)
+    terms[0][-1] = after(terms[0][-1], parts)
+
+    fresh, new_moment1, new_moment2 = adam(pos, terms, weights, moment1, moment2)
     new_weights = gather_weights(pos, fresh, dp_at, n_dp)
 
-    predicted = finish_predicted(perm, parts)
     return (predicted, new_weights, new_moment1, new_moment2)
 
 

time: 179 us -> 172 us (0.961)
  waiting for transfers between devices: 108 us -> 98.3 us
    ppermute x7 -> x13, waiting for transfers between devices: 6.4 us -> 26.9 us  [across(): return lax.ppermute(value, 'own', [(o, o ^ j) for o in range(n_own)])]
    ppermute x3 -> x0, waiting for transfers between devices: 17.2 us -> none  [shards(): lax.ppermute(pred_part[j], 'dp', [(d, d ^ j) for d in range(n_dp)])]
    all_to_all x1, waiting for transfers between devices: 9.67 us -> 0.01 us  [shards(): lax.all_to_all(pred_part, 'dp', split_axis=0, concat_axis=0, tiled=True)]
    ppermute x7 -> x13, starting transfers between devices: 4.48 us -> 9.73 us  [across(): return lax.ppermute(value, 'own', [(o, o ^ j) for o in range(n_own)])]
    ppermute x2, waiting for transfers between devices: 25.6 us -> 20.8 us  [between_planes(): outer = lax.ppermute(after(two, one, *second), 'dp', [(2, 3), (1, 0)])]
    ppermute x3 -> x0, starting transfers between devices: 4.73 us -> none  [shards(): lax.ppermute(pred_part[j], 'dp', [(d, d ^ j) for d in range(n_dp)])]
    ppermute x2, waiting for transfers between devices: 16.6 us -> 19.3 us  [between_planes(): two = lax.ppermute(value, 'dp', [(0, 2), (1, 3), (2, 0), (3, 1)])]
    unnamed x33 -> x45, local copies, waits for them, and re-layouts: 6.01 us -> 5.46 us
  transfers between devices with their start and end apart: 19 -> 22, of which waited for: 11 -> 11; matrix products, arithmetic and copies ran while one was open for 2% -> 2% of each run, Pallas kernels for 5% -> 5%
where the time goes in v12:
time: 172 us; the launch traced here: 169 us
  waiting for transfers between devices  98.3 us (57%)
  Pallas kernels  32.1 us (19%)
  starting transfers between devices  27.4 us (16%)
  local copies, waits for them, and re-layouts  6.69 us (4%)
  other arithmetic  3.4 us (2%)
    ppermute x2, waiting for transfers between devices, between_planes(): lax.ppermute(after(value, *first), 'dp', [(0, 1), (1, 0), (2, 3), (3, 2)])  31.4 us
    ppermute x13, waiting for transfers between devices, across(): return lax.ppermute(value, 'own', [(o, o ^ j) for o in range(n_own)])  26.9 us
    ppermute x2, waiting for transfers between devices, between_planes(): outer = lax.ppermute(after(two, one, *second), 'dp', [(2, 3), (1, 0)])  20.8 us
    ppermute x2, waiting for transfers between devices, between_planes(): two = lax.ppermute(value, 'dp', [(0, 2), (1, 3), (2, 0), (3, 1)])  19.3 us
    pallas_call x1, Pallas kernels, local_grads(): pl.pallas_call(body, out_shape=[pred_shape, pred_shape] + grad_shapes, in...  15.5 us
    ppermute x13, starting transfers between devices, across(): return lax.ppermute(value, 'own', [(o, o ^ j) for o in range(n_own)])  9.73 us
    pallas_call x2, Pallas kernels, place_weights(): pl.pallas_call(body, out_shape=jax.ShapeDtypeStruct(shape, jnp.bfloat16),...  6.03 us
    pallas_call x1, Pallas kernels, adam(): pl.pallas_call(body, out_shape=[jax.ShapeDtypeStruct(moment1.shape, jnp.b...  6 us
  transfers between devices with their start and end apart: 22, of which 11 were waited for; matrix products, arithmetic and copies ran while one was open for 2% of the time, Pallas kernels for 5%

profile of v12, /device:TPU:2, one launch (start us, length us, event | category | flops | bytes accessed | tf_op | source)
XLA Modules:
  0.0 168.9 jit_solution(17048617276435072890)
XLA Ops:
  0.6 1.2 dynamic-slice_bitcast_fusion
  1.8 0.1 collective-permute-start
  1.9 2.4 %pack_rows.1 = (bf16[528,384]{1,0:T(8,128)(2,1)}, bf16[256,256]{1,0:T(8,128)(2,1)}) custom-call(s32[1,256]{1,0:T(1,128)} %bitcast.23, bf16[256,384]{1,0:T(8,128)(2,1)} %sig_ref.1, bf16[256,384]{1,0:T(8,128)(2,1)} %cot_ref.1), custom_call_target="tpu_custom_call" | custom-call | tf_op jit(solution)/shard_map/pack_rows/pallas_call | solution.py:79
  4.3 0.1 pad_maximum_fusion.1.rest_2_
  4.4 1.6 collective-permute-start.4
  6.0 0.5 collective-permute-start.3
  6.5 2.6 %collective-permute-start.2 = (bf16[528,384]{1,0:T(8,128)(2,1)}, bf16[528,384]{1,0:T(8,128)(2,1)S(1)}, u32[]{:S(2)}, u32[]{:S(2)}) collective-permute-start(bf16[528,384]{1,0:T(8,128)(2,1)} %get-tuple-element.30), channel_id=1, source_target_pairs={{0,16},{8,24},{16,0},{24,8},{1,17},{9,25},{17,1},{25,9},{2,18},{10... | collective-permute-start | bytes 1216520 | tf_op jit(solution)/shard_map/ppermute | solution.py:430
  9.1 1.6 collective-permute-start.1
  10.7 17.0 %collective-permute-done.2 = bf16[528,384]{1,0:T(8,128)(2,1)S(1)} collective-permute-done((bf16[528,384]{1,0:T(8,128)(2,1)}, bf16[528,384]{1,0:T(8,128)(2,1)S(1)}, u32[]{:S(2)}, u32[]{:S(2)}) %collective-permute-start.2) | collective-permute-done | bytes 405536 | tf_op jit(solution)/shard_map/ppermute | solution.py:430
  27.7 0.2 collective-permute-done.1
  27.9 0.7 collective-permute-start.5
  28.6 1.3 collective-permute-start.6
  29.9 1.6 collective-permute-start.8
  31.5 0.6 collective-permute-start.7
  32.1 9.3 %collective-permute-done.6 = bf16[528,384]{1,0:T(8,128)(2,1)S(1)} collective-permute-done((bf16[528,384]{1,0:T(8,128)(2,1)S(1)}, bf16[528,384]{1,0:T(8,128)(2,1)S(1)}, u32[]{:S(2)}, u32[]{:S(2)}) %collective-permute-start.6) | collective-permute-done | bytes 405536 | tf_op jit(solution)/shard_map/ppermute | solution.py:432
  41.4 0.3 pad_maximum_fusion.rest_0_
  41.7 0.8 copy-done.18
  42.5 0.7 copy-done.19
  43.2 0.7 copy.13.touched_ref
  43.9 0.7 pad_add_fusion.pos_ref
  44.6 2.1 %collective-permute-done.9.rest_1_ = bf16[4,528,384]{2,1,0:T(8,128)(2,1)S(1)} collective-permute-done((bf16[4,528,384]{2,1,0:T(8,128)(2,1)S(1)}, bf16[4,528,384]{2,1,0:T(8,128)(2,1)S(1)}, u32[]{:S(2)}, u32[]{:S(2)}) %collective-permute-start.9) | collective-permute-done | bytes 1622048 | tf_op jit(solution)/shard_map/ppermute | solution.py:480
  46.7 1.2 copy-done.6
  47.9 15.5 %local_grads.1 = (bf16[4,256,384]{2,1,0:T(8,128)(2,1)}, bf16[4,256,384]{2,1,0:T(8,128)(2,1)}, bf16[1,8,2,48,256]{4,3,2,1,0:T(8,128)(2,1)}, bf16[1,8,2,48,256]{4,...) custom-call(s32[2]{0:T(128)} %pad_add_fusion.pos_ref, ...), custom_call_target="tpu_custom_call" | custom-call | tf_op jit(solution)/shard_map/local_grads/pallas_call | solution.py:248
  63.4 0.1 collective-permute-start.10
  63.5 1.6 collective-permute-start.11
  65.1 0.9 collective-permute-done.10
  66.0 2.3 %add.32 = bf16[4,256,384]{2,1,0:T(8,128)(2,1)} add(bf16[4,256,384]{2,1,0:T(8,128)(2,1)} %get-tuple-element.33, bf16[4,256,384]{2,1,0:T(8,128)(2,1)S(1)} %collective-permute-done.10) | non-fusion elementwise | flops 393216 | bytes 2359296 | tf_op jit(solution)/shard_map/add | solution.py:532
  68.3 5.4 %all-to-all-start = ((bf16[4,256,384]{2,1,0:T(8,128)(2,1)}), bf16[4,256,384]{2,1,0:T(8,128)(2,1)S(1)}, u32[]{:S(2)}, u32[]{:S(2)}) async-start(bf16[4,256,384]{2,1,0:T(8,128)(2,1)} %add.32), calls=%async_computation | async-start | bytes 1572864 | tf_op jit(solution)/shard_map/all_to_all | solution.py:533
  73.6 1.4 collective-permute-start.15
  75.1 0.7 collective-permute-start.14
  75.8 7.9 %collective-permute-done.11.refs_1_ = bf16[2,8,2,48,256]{4,3,2,1,0:T(8,128)(2,1)S(1)} collective-permute-done((bf16[2,8,2,48,256]{4,3,2,1,0:T(8,128)(2,1)}, bf16[2,8,2,48,256]{4,3,2,1,0:T(8,128)(2,1)S(1)}, u32[]{:S(2)}, u32[]{:S(2)}) %collective-permute-start.11) | collective-permute-done | bytes 786464 | tf_op jit(solution)/shard_map/ppermute | solution.py:480
  83.7 1.5 collective-permute-start.12
  85.2 0.4 collective-permute-done.15
  85.7 0.1 collective-permute-start.16
  85.8 15.6 %collective-permute-done.12.refs_2_ = bf16[8,2,48,256]{3,2,1,0:T(8,128)(2,1)S(1)} collective-permute-done((bf16[8,2,48,256]{3,2,1,0:T(8,128)(2,1)S(1)}, bf16[8,2,48,256]{3,2,1,0:T(8,128)(2,1)S(1)}, u32[]{:S(2)}, u32[]{:S(2)}) %collective-permute-start.12) | collective-permute-done | bytes 393248 | tf_op jit(solution)/shard_map/ppermute | solution.py:480
  101.4 1.1 copy-done.14
  102.5 6.0 %adam_step.1 = (bf16[16,2,48,256]{3,2,1,0:T(8,128)(2,1)}, f32[16,2,48,256]{3,2,1,0:T(8,128)}, f32[16,2,48,256]{3,2,1,0:T(8,128)}) custom-call(s32[2]{0:T(128)} %pad_add_fusion.pos_ref, bf16[1,8,2,48,256]{4,3,2,1,0:T(8,128)(2,1)} %get-tuple-element.35.refs_0_, bf16[2,8,2,48,256]{4,3,2,1,0:T(8,128)(2,1)} %copy-done.3, bf16[8,2,48,256]{3,2,1,0:T(8,128)(2,1)} %copy-done.14, ...), custom_call_target="tpu_custom_call" | custom-call | tf_op jit(solution)/shard_map/adam_step/pallas_call | solution.py:341
  108.6 1.8 %collective-permute-start.18 = (bf16[16,2,48,256]{3,2,1,0:T(8,128)(2,1)}, bf16[16,2,48,256]{3,2,1,0:T(8,128)(2,1)S(1)}, u32[]{:S(2)}, u32[]{:S(2)}) collective-permute-start(bf16[16,2,48,256]{3,2,1,0:T(8,128)(2,1)} %get-tuple-element.44.refs_0_), channel_id=1, source_target_pairs={{0,8},{8,0},{16,24},{24,16},{1,9},{9,1},{17,25},{25,17},{2,10},{10... | collective-permute-start | bytes 2359304 | tf_op jit(solution)/shard_map/ppermute | solution.py:431
  110.4 2.4 %collective-permute-start.17 = (bf16[16,2,48,256]{3,2,1,0:T(8,128)(2,1)}, bf16[16,2,48,256]{3,2,1,0:T(8,128)(2,1)S(1)}, u32[]{:S(2)}, u32[]{:S(2)}) collective-permute-start(bf16[16,2,48,256]{3,2,1,0:T(8,128)(2,1)} %get-tuple-element.44.refs_0_), channel_id=1, source_target_pairs={{0,16},{8,24},{16,0},{24,8},{1,17},{9,25},{17,1},{25,9},{2,18},{10... | collective-permute-start | bytes 2359304 | tf_op jit(solution)/shard_map/ppermute | solution.py:430
  112.7 31.2 %collective-permute-done.18.refs_1_ = bf16[16,2,48,256]{3,2,1,0:T(8,128)(2,1)S(1)} collective-permute-done((bf16[16,2,48,256]{3,2,1,0:T(8,128)(2,1)}, bf16[16,2,48,256]{3,2,1,0:T(8,128)(2,1)S(1)}, u32[]{:S(2)}, u32[]{:S(2)}) %collective-permute-start.18) | collective-permute-done | bytes 786464 | tf_op jit(solution)/shard_map/ppermute | solution.py:431
  143.9 2.3 %collective-permute-done.17.refs_2_ = bf16[16,2,48,256]{3,2,1,0:T(8,128)(2,1)S(1)} collective-permute-done((bf16[16,2,48,256]{3,2,1,0:T(8,128)(2,1)}, bf16[16,2,48,256]{3,2,1,0:T(8,128)(2,1)S(1)}, u32[]{:S(2)}, u32[]{:S(2)}) %collective-permute-start.17) | collective-permute-done | bytes 786464 | tf_op jit(solution)/shard_map/ppermute | solution.py:430
  146.2 0.7 collective-permute-start.19
  146.9 1.3 collective-permute-start.20
  148.2 2.2 %finish_predicted.1 = bf16[256,384]{1,0:T(8,128)(2,1)} custom-call(bf16[256,256]{1,0:T(8,128)(2,1)} %get-tuple-element.26.perm_ref, bf16[4,256,384]{2,1,0:T(8,128)(2,1)} %copy-done.1), custom_call_target="tpu_custom_call" | custom-call | tf_op jit(solution)/shard_map/finish_predicted/pallas_call | solution.py:458
  150.4 3.4 %place_weights.2.refs_2_ = bf16[16,2,48,1024]{3,2,1,0:T(8,128)(2,1)} custom-call(s32[2]{0:T(128)} %pad_add_fusion.pos_ref, bf16[16,2,48,256]{3,2,1,0:T(8,128)(2,1)} %get-tuple-element.44.refs_0_, bf16[16,2,48,256]{3,2,1,0:T(8,128)(2,1)} %copy-done.8, bf16[16,2,48,256]{3,2,1,0:T(8,128)(2,1)} %copy-done.7), custom_call_target="tpu_custom_call" | custom-call | tf_op jit(solution)/shard_map/place_weights/pallas_call | solution.py:408
  153.8 11.6 %collective-permute-done.20.refs_1_ = bf16[16,2,48,256]{3,2,1,0:T(8,128)(2,1)S(1)} collective-permute-done((bf16[16,2,48,256]{3,2,1,0:T(8,128)(2,1)S(1)}, bf16[16,2,48,256]{3,2,1,0:T(8,128)(2,1)S(1)}, u32[]{:S(2)}, u32[]{:S(2)}) %collective-permute-start.20) | collective-permute-done | bytes 786464 | tf_op jit(solution)/shard_map/ppermute | solution.py:432
  165.4 0.9 copy-done.10
  166.3 2.6 %place_weights.3 = bf16[16,2,48,1024]{3,2,1,0:T(8,128)(2,1)} custom-call(s32[2]{0:T(128)} %pad_add_fusion.pos_ref, bf16[16,2,48,256]{3,2,1,0:T(8,128)(2,1)} %copy-done.9, bf16[16,2,48,256]{3,2,1,0:T(8,128)(2,1)} %copy-done.10, bf16[16,2,48,1024]{3,2,1,0:T(8,128)(2,1)} %place_weights.2.refs_2_), custom_call_target="tpu_custom_call", output_to_operand_aliasing={{}: (3, {})} | custom-call | tf_op jit(solution)/shard_map/place_weights/pallas_call | solution.py:408
  (57 shorter events, 0.3 us)
Async XLA Ops:
  1.8 2.5 %collective-permute-start = (bf16[8,2,48,256]{3,2,1,0:T(8,128)(2,1)S(1)}, bf16[8,2,48,256]{3,2,1,0:T(8,128)(2,1)S(1)}, u32[]{:S(2)}, u32[]{:S(2)}) collective-permute-start(bf16[8,2,48,256]{3,2,1,0:T(8,128)(2,1)S(1)} %get-tuple-element.49), channel_id=1, source_target_pairs={{0,1},{1,0},{2,3},{3,2},{4,5},{5,4},{6,7},{7,6},{8,9},{9,8},{10,11... | collective-permute-start | bytes 1179656 | tf_op jit(solution)/shard_map/ppermute | solution.py:480
  4.4 37.3 %copy-start.2 = (bf16[2,8,2,48,256]{4,3,2,1,0:T(8,128)(2,1)}, bf16[2,8,2,48,256]{4,3,2,1,0:T(8,128)(2,1)S(1)}, u32[]{:S(2)}) copy-start(bf16[2,8,2,48,256]{4,3,2,1,0:T(8,128)(2,1)S(1)} %pad_maximum_fusion.1.rest_2_) | copy-start | bytes 2359300
  4.4 37.0 %copy-start.11 = (bf16[528,384]{1,0:T(8,128)(2,1)S(1)}, bf16[528,384]{1,0:T(8,128)(2,1)}, u32[]{:S(2)}) copy-start(bf16[528,384]{1,0:T(8,128)(2,1)} %get-tuple-element.30) | copy-start | bytes 1216516
  4.4 23.4 %collective-permute-start.4 = (bf16[2,8,2,48,256]{4,3,2,1,0:T(8,128)(2,1)S(1)}, bf16[2,8,2,48,256]{4,3,2,1,0:T(8,128)(2,1)S(1)}, u32[]{:S(2)}, u32[]{:S(2)}) collective-permute-start(bf16[2,8,2,48,256]{4,3,2,1,0:T(8,128)(2,1)S(1)} %pad_maximum_fusion.1.rest_2_), channel_id=1, source_target_pairs={{0,4},{1,5},{2,6},{3,7},{4,0},{5,1},{6,2},{7,3},{8,12},{9,13},{10,... | collective-permute-start | bytes 2359304 | tf_op jit(solution)/shard_map/ppermute | solution.py:480
  6.0 21.9 %collective-permute-start.3 = (bf16[2,8,2,48,256]{4,3,2,1,0:T(8,128)(2,1)S(1)}, bf16[2,8,2,48,256]{4,3,2,1,0:T(8,128)(2,1)S(1)}, u32[]{:S(2)}, u32[]{:S(2)}) collective-permute-start(bf16[2,8,2,48,256]{4,3,2,1,0:T(8,128)(2,1)S(1)} %pad_maximum_fusion.1.rest_2_), channel_id=1, source_target_pairs={{0,2},{1,3},{2,0},{3,1},{4,6},{5,7},{6,4},{7,5},{8,10},{9,11},{10,... | collective-permute-start | bytes 2359304 | tf_op jit(solution)/shard_map/ppermute | solution.py:480
  6.5 21.1 %collective-permute-start.2 = (bf16[528,384]{1,0:T(8,128)(2,1)}, bf16[528,384]{1,0:T(8,128)(2,1)S(1)}, u32[]{:S(2)}, u32[]{:S(2)}) collective-permute-start(bf16[528,384]{1,0:T(8,128)(2,1)} %get-tuple-element.30), channel_id=1, source_target_pairs={{0,16},{8,24},{16,0},{24,8},{1,17},{9,25},{17,1},{25,9},{2,18},{10... | collective-permute-start | bytes 1216520 | tf_op jit(solution)/shard_map/ppermute | solution.py:430
  9.1 18.7 %collective-permute-start.1 = (bf16[528,384]{1,0:T(8,128)(2,1)}, bf16[528,384]{1,0:T(8,128)(2,1)S(1)}, u32[]{:S(2)}, u32[]{:S(2)}) collective-permute-start(bf16[528,384]{1,0:T(8,128)(2,1)} %get-tuple-element.30), channel_id=1, source_target_pairs={{0,8},{8,0},{16,24},{24,16},{1,9},{9,1},{17,25},{25,17},{2,10},{10... | collective-permute-start | bytes 1216520 | tf_op jit(solution)/shard_map/ppermute | solution.py:431
  27.9 13.8 %copy-start.4 = (bf16[2,8,2,48,256]{4,3,2,1,0:T(8,128)(2,1)}, bf16[2,8,2,48,256]{4,3,2,1,0:T(8,128)(2,1)S(1)}, u32[]{:S(2)}) copy-start(bf16[2,8,2,48,256]{4,3,2,1,0:T(8,128)(2,1)S(1)} %collective-permute-done.4.rest_4_) | copy-start | bytes 2359300
  27.9 3.6 %copy-start.5 = (bf16[2,8,2,48,256]{4,3,2,1,0:T(8,128)(2,1)}, bf16[2,8,2,48,256]{4,3,2,1,0:T(8,128)(2,1)S(1)}, u32[]{:S(2)}) copy-start(bf16[2,8,2,48,256]{4,3,2,1,0:T(8,128)(2,1)S(1)} %collective-permute-done.3.rest_3_) | copy-start | bytes 2359300
  27.9 4.2 %collective-permute-start.5 = (bf16[528,384]{1,0:T(8,128)(2,1)}, bf16[528,384]{1,0:T(8,128)(2,1)S(1)}, u32[]{:S(2)}, u32[]{:S(2)}) collective-permute-start(bf16[528,384]{1,0:T(8,128)(2,1)} %get-tuple-element.30), channel_id=1, source_target_pairs={{8,16},{16,8},{9,17},{17,9},{10,18},{18,10},{11,19},{19,11},{12,20... | collective-permute-start | bytes 1216520 | tf_op jit(solution)/shard_map/ppermute | solution.py:433
  28.6 12.8 %collective-permute-start.6 = (bf16[528,384]{1,0:T(8,128)(2,1)S(1)}, bf16[528,384]{1,0:T(8,128)(2,1)S(1)}, u32[]{:S(2)}, u32[]{:S(2)}) collective-permute-start(bf16[528,384]{1,0:T(8,128)(2,1)S(1)} %collective-permute-done.2), channel_id=1, source_target_pairs={{16,24},{8,0},{17,25},{9,1},{18,26},{10,2},{19,27},{11,3},{20,28},... | collective-permute-start | bytes 1216520 | tf_op jit(solution)/shard_map/ppermute | solution.py:432
  29.9 11.8 %collective-permute-start.8 = (bf16[8,2,48,256]{3,2,1,0:T(8,128)(2,1)S(1)}, bf16[8,2,48,256]{3,2,1,0:T(8,128)(2,1)S(1)}, u32[]{:S(2)}, u32[]{:S(2)}) collective-permute-start(bf16[8,2,48,256]{3,2,1,0:T(8,128)(2,1)S(1)} %slice_bitcast_fusion), channel_id=1, source_target_pairs={{0,2},{1,3},{2,0},{3,1},{4,6},{5,7},{6,4},{7,5},{8,10},{9,11},{10,... | collective-permute-start | bytes 1179656 | tf_op jit(solution)/shard_map/ppermute | solution.py:480
  31.5 10.2 %collective-permute-start.7 = (bf16[8,2,48,256]{3,2,1,0:T(8,128)(2,1)S(1)}, bf16[8,2,48,256]{3,2,1,0:T(8,128)(2,1)S(1)}, u32[]{:S(2)}, u32[]{:S(2)}) collective-permute-start(bf16[8,2,48,256]{3,2,1,0:T(8,128)(2,1)S(1)} %slice_bitcast_fusion.1), channel_id=1, source_target_pairs={{0,4},{1,5},{2,6},{3,7},{4,0},{5,1},{6,2},{7,3},{8,12},{9,13},{10,... | collective-permute-start | bytes 1179656 | tf_op jit(solution)/shard_map/ppermute | solution.py:480
  41.4 1.8 %copy-start.20 = (s32[32,4]{0,1:T(4,128)S(1)}, s32[32,4]{0,1:T(4,128)}, u32[]{:S(2)}) copy-start(s32[32,4]{0,1:T(4,128)} %param.11) | copy-start | bytes 1540
  41.7 5.0 %copy-start = (bf16[4,528,384]{2,1,0:T(8,128)(2,1)}, bf16[4,528,384]{2,1,0:T(8,128)(2,1)S(1)}, u32[]{:S(2)}) copy-start(bf16[4,528,384]{2,1,0:T(8,128)(2,1)S(1)} %pad_maximum_fusion.rest_0_) | copy-start | bytes 4866052
  41.7 0.8 copy-start.18
  42.5 0.7 copy-start.19
  43.2 3.5 %collective-permute-start.9 = (bf16[4,528,384]{2,1,0:T(8,128)(2,1)S(1)}, bf16[4,528,384]{2,1,0:T(8,128)(2,1)S(1)}, u32[]{:S(2)}, u32[]{:S(2)}) collective-permute-start(bf16[4,528,384]{2,1,0:T(8,128)(2,1)S(1)} %pad_maximum_fusion.rest_0_), channel_id=1, source_target_pairs={{0,1},{1,0},{2,3},{3,2},{4,5},{5,4},{6,7},{7,6},{8,9},{9,8},{10,11... | collective-permute-start | bytes 4866056 | tf_op jit(solution)/shard_map/ppermute | solution.py:480
  46.7 1.2 copy-start.6
  63.4 2.6 %collective-permute-start.10 = (bf16[4,256,384]{2,1,0:T(8,128)(2,1)}, bf16[4,256,384]{2,1,0:T(8,128)(2,1)S(1)}, u32[]{:S(2)}, u32[]{:S(2)}) collective-permute-start(bf16[4,256,384]{2,1,0:T(8,128)(2,1)} %get-tuple-element.34), channel_id=1, source_target_pairs={{0,1},{1,0},{2,3},{3,2},{4,5},{5,4},{6,7},{7,6},{8,9},{9,8},{10,11... | collective-permute-start | bytes 2359304 | tf_op jit(solution)/shard_map/ppermute | solution.py:480
  63.5 20.2 %collective-permute-start.11 = (bf16[2,8,2,48,256]{4,3,2,1,0:T(8,128)(2,1)}, bf16[2,8,2,48,256]{4,3,2,1,0:T(8,128)(2,1)S(1)}, u32[]{:S(2)}, u32[]{:S(2)}) collective-permute-start(bf16[2,8,2,48,256]{4,3,2,1,0:T(8,128)(2,1)} %get-tuple-element.36), channel_id=1, source_target_pairs={{0,2},{1,3},{2,0},{3,1},{4,6},{5,7},{6,4},{7,5},{8,10},{9,11},{10,... | collective-permute-start | bytes 2359304 | tf_op jit(solution)/shard_map/ppermute | solution.py:480
  66.0 7.6 %copy-start.21 = (bf16[1,8,2,48,256]{4,3,2,1,0:T(8,128)(2,1)S(1)}, bf16[1,8,2,48,256]{4,3,2,1,0:T(8,128)(2,1)}, u32[]{:S(2)}) copy-start(bf16[1,8,2,48,256]{4,3,2,1,0:T(8,128)(2,1)} %get-tuple-element.42) | copy-start | bytes 1179652
  66.0 17.7 %copy-start.17 = (bf16[1,8,2,48,256]{4,3,2,1,0:T(8,128)(2,1)S(1)}, bf16[1,8,2,48,256]{4,3,2,1,0:T(8,128)(2,1)}, u32[]{:S(2)}) copy-start(bf16[1,8,2,48,256]{4,3,2,1,0:T(8,128)(2,1)} %get-tuple-element.37) | copy-start | bytes 1179652
  68.3 17.4 %copy-start.16 = (bf16[1,8,2,48,256]{4,3,2,1,0:T(8,128)(2,1)S(1)}, bf16[1,8,2,48,256]{4,3,2,1,0:T(8,128)(2,1)}, u32[]{:S(2)}) copy-start(bf16[1,8,2,48,256]{4,3,2,1,0:T(8,128)(2,1)} %get-tuple-element.41) | copy-start | bytes 1179652
  68.3 33.1 %all-to-all-start = ((bf16[4,256,384]{2,1,0:T(8,128)(2,1)}), bf16[4,256,384]{2,1,0:T(8,128)(2,1)S(1)}, u32[]{:S(2)}, u32[]{:S(2)}) async-start(bf16[4,256,384]{2,1,0:T(8,128)(2,1)} %add.32), calls=%async_computation | async-start | bytes 1572864 | tf_op jit(solution)/shard_map/all_to_all | solution.py:533
  73.6 12.0 %collective-permute-start.15 = (bf16[1,8,2,48,256]{4,3,2,1,0:T(8,128)(2,1)S(1)}, bf16[1,8,2,48,256]{4,3,2,1,0:T(8,128)(2,1)S(1)}, u32[]{:S(2)}, u32[]{:S(2)}) collective-permute-start(bf16[1,8,2,48,256]{4,3,2,1,0:T(8,128)(2,1)S(1)} %copy-done.21), channel_id=1, source_target_pairs={{0,4},{1,5},{2,6},{3,7},{4,0},{5,1},{6,2},{7,3},{8,12},{9,13},{10,... | collective-permute-start | bytes 1179656 | tf_op jit(solution)/shard_map/ppermute | solution.py:480
  75.1 26.3 %collective-permute-start.13 = (bf16[1,8,2,48,256]{4,3,2,1,0:T(8,128)(2,1)}, bf16[1,8,2,48,256]{4,3,2,1,0:T(8,128)(2,1)S(1)}, u32[]{:S(2)}, u32[]{:S(2)}) collective-permute-start(bf16[1,8,2,48,256]{4,3,2,1,0:T(8,128)(2,1)} %get-tuple-element.39), channel_id=1, source_target_pairs={{0,1},{1,0},{2,3},{3,2},{4,5},{5,4},{6,7},{7,6},{8,9},{9,8},{10,11... | collective-permute-start | bytes 1179656 | tf_op jit(solution)/shard_map/ppermute | solution.py:480
  75.1 26.3 %collective-permute-start.14 = (bf16[1,8,2,48,256]{4,3,2,1,0:T(8,128)(2,1)}, bf16[1,8,2,48,256]{4,3,2,1,0:T(8,128)(2,1)S(1)}, u32[]{:S(2)}, u32[]{:S(2)}) collective-permute-start(bf16[1,8,2,48,256]{4,3,2,1,0:T(8,128)(2,1)} %get-tuple-element.40), channel_id=1, source_target_pairs={{0,5},{1,4},{2,7},{3,6},{4,1},{5,0},{6,3},{7,2},{8,13},{9,12},{10,... | collective-permute-start | bytes 1179656 | tf_op jit(solution)/shard_map/ppermute | solution.py:480
  83.7 17.8 %copy-start.3 = (bf16[2,8,2,48,256]{4,3,2,1,0:T(8,128)(2,1)}, bf16[2,8,2,48,256]{4,3,2,1,0:T(8,128)(2,1)S(1)}, u32[]{:S(2)}) copy-start(bf16[2,8,2,48,256]{4,3,2,1,0:T(8,128)(2,1)S(1)} %collective-permute-done.11.refs_1_) | copy-start | bytes 2359300
  83.7 17.6 %collective-permute-start.12 = (bf16[8,2,48,256]{3,2,1,0:T(8,128)(2,1)S(1)}, bf16[8,2,48,256]{3,2,1,0:T(8,128)(2,1)S(1)}, u32[]{:S(2)}, u32[]{:S(2)}) collective-permute-start(bf16[8,2,48,256]{3,2,1,0:T(8,128)(2,1)S(1)} %fusion), channel_id=1, source_target_pairs={{0,4},{1,5},{2,6},{3,7},{4,0},{5,1},{6,2},{7,3},{8,12},{9,13},{10,... | collective-permute-start | bytes 1179656 | tf_op jit(solution)/shard_map/ppermute | solution.py:480
  85.7 15.7 %collective-permute-start.16 = (bf16[8,2,48,256]{3,2,1,0:T(8,128)(2,1)S(1)}, bf16[8,2,48,256]{3,2,1,0:T(8,128)(2,1)S(1)}, u32[]{:S(2)}, u32[]{:S(2)}) collective-permute-start(bf16[8,2,48,256]{3,2,1,0:T(8,128)(2,1)S(1)} %add_bitcast_fusion.1), channel_id=1, source_target_pairs={{0,3},{1,2},{2,1},{3,0},{4,7},{5,6},{6,5},{7,4},{8,11},{9,10},{10,... | collective-permute-start | bytes 1179656 | tf_op jit(solution)/shard_map/ppermute | solution.py:480
  101.4 1.2 copy-start.14
  101.4 7.2 %copy-start.1 = (bf16[4,256,384]{2,1,0:T(8,128)(2,1)}, bf16[4,256,384]{2,1,0:T(8,128)(2,1)S(1)}, u32[]{:S(2)}) copy-start(bf16[4,256,384]{2,1,0:T(8,128)(2,1)S(1)} %all-to-all-done.parts_ref) | copy-start | bytes 2359300
  101.4 1.2 copy-start.12
  101.4 1.1 copy-start.13
  101.4 1.1 copy-start.15
  108.6 35.3 %collective-permute-start.18 = (bf16[16,2,48,256]{3,2,1,0:T(8,128)(2,1)}, bf16[16,2,48,256]{3,2,1,0:T(8,128)(2,1)S(1)}, u32[]{:S(2)}, u32[]{:S(2)}) collective-permute-start(bf16[16,2,48,256]{3,2,1,0:T(8,128)(2,1)} %get-tuple-element.44.refs_0_), channel_id=1, source_target_pairs={{0,8},{8,0},{16,24},{24,16},{1,9},{9,1},{17,25},{25,17},{2,10},{10... | collective-permute-start | bytes 2359304 | tf_op jit(solution)/shard_map/ppermute | solution.py:431
  110.4 35.8 %collective-permute-start.17 = (bf16[16,2,48,256]{3,2,1,0:T(8,128)(2,1)}, bf16[16,2,48,256]{3,2,1,0:T(8,128)(2,1)S(1)}, u32[]{:S(2)}, u32[]{:S(2)}) collective-permute-start(bf16[16,2,48,256]{3,2,1,0:T(8,128)(2,1)} %get-tuple-element.44.refs_0_), channel_id=1, source_target_pairs={{0,16},{8,24},{16,0},{24,8},{1,17},{9,25},{17,1},{25,9},{2,18},{10... | collective-permute-start | bytes 2359304 | tf_op jit(solution)/shard_map/ppermute | solution.py:430
  143.9 6.5 %copy-start.8 = (bf16[16,2,48,256]{3,2,1,0:T(8,128)(2,1)}, bf16[16,2,48,256]{3,2,1,0:T(8,128)(2,1)S(1)}, u32[]{:S(2)}) copy-start(bf16[16,2,48,256]{3,2,1,0:T(8,128)(2,1)S(1)} %collective-permute-done.18.refs_1_) | copy-start | bytes 2359300
  146.2 4.2 %copy-start.7 = (bf16[16,2,48,256]{3,2,1,0:T(8,128)(2,1)}, bf16[16,2,48,256]{3,2,1,0:T(8,128)(2,1)S(1)}, u32[]{:S(2)}) copy-start(bf16[16,2,48,256]{3,2,1,0:T(8,128)(2,1)S(1)} %collective-permute-done.17.refs_2_) | copy-start | bytes 2359300
  146.2 7.6 %collective-permute-start.19 = (bf16[16,2,48,256]{3,2,1,0:T(8,128)(2,1)}, bf16[16,2,48,256]{3,2,1,0:T(8,128)(2,1)S(1)}, u32[]{:S(2)}, u32[]{:S(2)}) collective-permute-start(bf16[16,2,48,256]{3,2,1,0:T(8,128)(2,1)} %get-tuple-element.44.refs_0_), channel_id=1, source_target_pairs={{8,16},{16,8},{9,17},{17,9},{10,18},{18,10},{11,19},{19,11},{12,20... | collective-permute-start | bytes 2359304 | tf_op jit(solution)/shard_map/ppermute | solution.py:433
  146.9 18.5 %collective-permute-start.20 = (bf16[16,2,48,256]{3,2,1,0:T(8,128)(2,1)S(1)}, bf16[16,2,48,256]{3,2,1,0:T(8,128)(2,1)S(1)}, u32[]{:S(2)}, u32[]{:S(2)}) collective-permute-start(bf16[16,2,48,256]{3,2,1,0:T(8,128)(2,1)S(1)} %collective-permute-done.17.refs_2_), channel_id=1, source_target_pairs={{16,24},{8,0},{17,25},{9,1},{18,26},{10,2},{19,27},{11,3},{20,28},... | collective-permute-start | bytes 2359304 | tf_op jit(solution)/shard_map/ppermute | solution.py:432
  153.8 11.6 %copy-start.9 = (bf16[16,2,48,256]{3,2,1,0:T(8,128)(2,1)}, bf16[16,2,48,256]{3,2,1,0:T(8,128)(2,1)S(1)}, u32[]{:S(2)}) copy-start(bf16[16,2,48,256]{3,2,1,0:T(8,128)(2,1)S(1)} %collective-permute-done.19.refs_0_) | copy-start | bytes 2359300
  165.4 0.9 copy-start.10

commit v13 on v12

--- a/solution.py
+++ b/solution.py
@@ -90,7 +90,8 @@
 
 
 def local_grads(pos, touched, slot_map, rows_in, blocks, sends, piece, width):
-    planes = rows_in[0].shape[0]
+    near = rows_in[0].shape[0]
+    planes = near + 1
     rows = (rows_in[0].shape[1] - ID_ROWS) // 2
     touch = touched.shape[1]
     n_own = SITES // piece
@@ -102,18 +103,22 @@
     half = arrays[0].shape[-4]
 
     def body(pos_ref, touched_ref, slot_ref, *rest):
-        row_refs = rest[:2]
-        block_refs = rest[2 : 2 + len(arrays)]
-        rest = rest[2 + len(arrays) :]
+        row_refs = rest[:4]
+        block_refs = rest[4 : 4 + len(arrays)]
+        rest = rest[4 + len(arrays) :]
         pred_refs = rest[:2]
-        grad_refs = rest[2:-8]
-        acc, id_cols, held, sorted_rows, pred, full_of, tasks, sems = rest[-8:]
+        n_out = len(grad_shapes)
+        grad_refs = rest[2 : 2 + n_out]
+        staged = rest[2 + n_out : 2 + 2 * n_out]
+        acc, id_cols, held, sorted_rows, pred, full_of, tasks, sems, sem_out = rest[-9:]
         own_at = pos_ref[1]
         core = lax.rem(own_at, 2)
 
         row_copies = [
-            pltpu.make_async_copy(ref, sorted_rows.at[pl.ds(i * planes, planes)], sems.at[i])
-            for i, ref in enumerate(row_refs)
+            pltpu.make_async_copy(
+                ref, sorted_rows.at[pl.ds(at, near) if i % 2 == 0 else at], sems.at[i]
+            )
+            for i, (ref, at) in enumerate(zip(row_refs, (0, near, planes, planes + near)))
         ]
         if aligned:
             block_copies = []
@@ -122,11 +127,11 @@
                 sites = pl.ds(pl.multiple_of((own_at ^ j) * piece, 16), piece)
                 block_copies.append(
                     pltpu.make_async_copy(
-                        ref if at is None else ref.at[at], held.at[:, :, sites, :], sems.at[2 + j]
+                        ref if at is None else ref.at[at], held.at[:, :, sites, :], sems.at[4 + j]
                     )
                 )
         else:
-            block_copies = [pltpu.make_async_copy(block_refs[0], held, sems.at[2])]
+            block_copies = [pltpu.make_async_copy(block_refs[0], held, sems.at[4])]
         for copy in row_copies + block_copies:
             copy.start()
 
@@ -205,21 +210,30 @@
             return 0
 
         lax.fori_loop(0, (count + 1) // 2, pair, 0)
-        for which, ref in enumerate(pred_refs):
-            for i in range(planes):
-                ref[pos_ref[0] ^ i] = pred[which * planes + i]
-
-        def write(e, _):
-            if aligned:
-                for ref, group in zip(grad_refs, sends):
-                    for i, j in enumerate(group):
+        outs = [
+            pltpu.make_async_copy(
+                pred.at[pl.ds(which * planes, planes)], pred_refs[which], sem_out.at[which]
+            )
+            for which in (1, 0)
+        ]
+        for copy in outs:
+            copy.start()
+        for n, (ref, into) in enumerate(zip(grad_refs, staged)):
+
+            def write(e, _, into=into, n=n):
+                if aligned:
+                    for i, j in enumerate(sends[n]):
                         first = pl.multiple_of((own_at ^ j) * piece, 16)
-                        ref[i, e] = acc[e, :, pl.ds(first, piece), :].astype(jnp.bfloat16)
-            else:
-                grad_refs[0][e] = acc[e].astype(jnp.bfloat16)
-            return 0
-
-        lax.fori_loop(0, half, write, 0)
+                        into[i, e] = acc[e, :, pl.ds(first, piece), :].astype(jnp.bfloat16)
+                else:
+                    into[e] = acc[e].astype(jnp.bfloat16)
+                return 0
+
+            lax.fori_loop(0, half, write, 0)
+            outs.append(pltpu.make_async_copy(into, ref, sem_out.at[2 + n]))
+            outs[-1].start()
+        for copy in outs:
+            copy.wait()
 
     pred_shape = jax.ShapeDtypeStruct((planes, rows, SITES), jnp.bfloat16)
     grad_shapes = [
@@ -235,7 +249,7 @@
     id_shape = (2 * planes, rows, 128)
     row_shape = (2 * planes,) + rows_in[0].shape[1:]
     pred_all = (2 * planes, rows, SITES)
-    scratch = [
+    scratch = [pltpu.VMEM(one.shape, jnp.bfloat16) for one in grad_shapes] + [
         pltpu.VMEM(acc_shape, jnp.float32),
         pltpu.VMEM(id_shape, jnp.float32),
         pltpu.VMEM(acc_shape, jnp.bfloat16),
@@ -243,13 +257,14 @@
         pltpu.VMEM(pred_all, jnp.bfloat16),
         pltpu.SMEM((2 * planes,), jnp.int32),
         pltpu.SMEM((4, most + 1), jnp.int32),
-        pltpu.SemaphoreType.DMA((2 + n_own,)),
+        pltpu.SemaphoreType.DMA((4 + n_own,)),
+        pltpu.SemaphoreType.DMA((2 + len(grad_shapes),)),
     ]
     found = pl.pallas_call(
         body,
         out_shape=[pred_shape, pred_shape] + grad_shapes,
-        in_specs=[smem(), smem(), smem()] + [pl.BlockSpec(memory_space=pl.ANY)] * (2 + len(arrays)),
-        out_specs=[vmem()] * (2 + len(grad_shapes)),
+        in_specs=[smem(), smem(), smem()] + [pl.BlockSpec(memory_space=pl.ANY)] * (4 + len(arrays)),
+        out_specs=[pl.BlockSpec(memory_space=pl.ANY)] * (2 + len(grad_shapes)),
         scratch_shapes=scratch,
         compiler_params=params(),
         name="local_grads",
@@ -446,9 +461,11 @@
 
 
 def finish_predicted(perm, parts):
-    def body(perm_ref, parts_ref, out_ref):
-        total = jnp.sum(parts_ref[...].astype(jnp.float32), axis=0)
-        out_ref[...] = lax.dot_general(
+    def body(perm_ref, *refs):
+        total = refs[0][...].astype(jnp.float32)
+        for ref in refs[1:-1]:
+            total = total + ref[...].astype(jnp.float32)
+        refs[-1][...] = lax.dot_general(
             perm_ref[...],
             total.astype(jnp.bfloat16),
             (((0,), (0,)), ((), ())),
@@ -457,12 +474,12 @@
 
     return pl.pallas_call(
         body,
-        out_shape=jax.ShapeDtypeStruct(parts.shape[1:], jnp.bfloat16),
-        in_specs=[vmem(), vmem()],
+        out_shape=jax.ShapeDtypeStruct(parts[0].shape, jnp.bfloat16),
+        in_specs=[vmem()] * (1 + len(parts)),
         out_specs=vmem(),
         compiler_params=params(),
         name="finish_predicted",
-    )(perm, parts)
+    )(perm, *parts)
 
 
 def shards(signals, cotangent, row_insertion, touched, slot_map, weights, moment1, moment2):
@@ -494,7 +511,7 @@
         blocks = [(one, u) for one in [chip] + beside for u in range(2)]
         blocks += [(one, None) for one in diagonal]
         first, second, last = [chip], beside, diagonal
-        sends = [(0,), (1,), (2, 6), (7,), (5,), (3,), (4,)]
+        sends = [(2, 6), (7,), (5,), (1,), (3,), (4,), (0,)]
     else:
         column = lax.dynamic_slice_in_dim(weights, dp_at * width, width, 3)
         outgoing = jnp.broadcast_to(
@@ -507,20 +524,21 @@
     *near, far = between_planes(packed, dp_at, n_dp, first, second)
     if isinstance(far, tuple):
         far = far[0] + far[1]
-    planes = jnp.stack(near + [far])
-    rows_in = (planes, across(after(planes, *last), 1))
+    near = jnp.stack(near)
+    rows_in = (near, far, across(near, 1), across(after(far, *last), 1))
 
     pred_mine, pred_other, grads = local_grads(
         pos, touched, slot_map, rows_in, blocks, sends, piece, width
     )
     if sends:
-        own, partner, x_same, y_diagonal, y_cross, x_cross, y_same = grads
+        x_same, y_diagonal, y_cross, partner, x_cross, y_same, own = grads
         x_same = across(x_same, 2)
         y_diagonal = across(y_diagonal, 4)
         y_cross = across(y_cross, 5)
         partner = across(partner, 1)
-        x_cross = across(x_cross[0] + y_diagonal[0], 3)
-        y_same = across(y_same[0] + x_same[1], 4)
+        first = (x_same, y_diagonal, y_cross, partner)
+        x_cross = across(after(x_cross[0] + y_diagonal[0], *first), 3)
+        y_same = across(after(y_same[0] + x_same[1], *first), 4)
         terms = [[(own, 0), (x_same, 0), y_same], [(partner, 0), (y_cross, 0), x_cross]]
     else:
         arrived = lax.all_to_all(grads, "own", split_axis=0, concat_axis=0, tiled=True)
@@ -530,9 +548,11 @@
         terms = [arrived[0::2], arrived[1::2]]
 
     pred_part = pred_mine + across(pred_other, 1)
-    parts = lax.all_to_all(pred_part, "dp", split_axis=0, concat_axis=0, tiled=True)
+    parts = [pred_part[0]] + [
+        lax.ppermute(pred_part[j], "dp", [(d, d ^ j) for d in range(n_dp)]) for j in range(1, n_dp)
+    ]
     predicted = finish_predicted(perm, parts)
-    terms[0][-1] = after(terms[0][-1], parts)
+    terms[0][-1] = after(terms[0][-1], *parts[1:])
 
     fresh, new_moment1, new_moment2 = adam(pos, terms, weights, moment1, moment2)
     new_weights = gather_weights(pos, fresh, dp_at, n_dp)

time: 172 us -> 176 us (1.023)
  waiting for transfers between devices: 98.3 us -> 105 us
    ppermute x0 -> x3, waiting for transfers between devices: none -> 15.8 us  [shards(): lax.ppermute(pred_part[j], 'dp', [(d, d ^ j) for d in range(n_dp)])]
    ppermute x13 -> x14, waiting for transfers between devices: 26.9 us -> 15.3 us  [across(): return lax.ppermute(value, 'own', [(o, o ^ j) for o in range(n_own)])]
    all_to_all x1 -> x0, starting transfers between devices: 5.36 us -> none  [shards(): lax.all_to_all(pred_part, 'dp', split_axis=0, concat_axis=0, tiled=True)]
    ppermute x0 -> x3, starting transfers between devices: none -> 4.39 us  [shards(): lax.ppermute(pred_part[j], 'dp', [(d, d ^ j) for d in range(n_dp)])]
    add x2 -> x3, other arithmetic: 0.1 us -> 2.46 us  [the longest x1 1.3 us: shards(): y_same = across(after(y_same[0] + x_same[1], *first), 4)]
    ppermute x2, waiting for transfers between devices: 20.8 us -> 23 us  [between_planes(): outer = lax.ppermute(after(two, one, *second), 'dp', [(2, 3), (1, 0)])]
    add x1, other arithmetic: 2.28 us -> 0.19 us  [shards(): pred_part = pred_mine + across(pred_other, 1)]
    ppermute x13 -> x14, starting transfers between devices: 9.73 us -> 11.1 us  [across(): return lax.ppermute(value, 'own', [(o, o ^ j) for o in range(n_own)])]
  transfers between devices with their start and end apart: 22 -> 25, of which waited for: 11 -> 12; matrix products, arithmetic and copies ran while one was open for 2% -> 3% of each run, Pallas kernels for 5% -> 5%
where the time goes in v13:
time: 176 us; the launch traced here: 174 us
  waiting for transfers between devices  105 us (60%)
  Pallas kernels  30.9 us (18%)
  starting transfers between devices  26.9 us (15%)
  local copies, waits for them, and re-layouts  6.83 us (4%)
  other arithmetic  3.48 us (2%)
    ppermute x2, waiting for transfers between devices, between_planes(): lax.ppermute(after(value, *first), 'dp', [(0, 1), (1, 0), (2, 3), (3, 2)])  33 us
    ppermute x2, waiting for transfers between devices, between_planes(): outer = lax.ppermute(after(two, one, *second), 'dp', [(2, 3), (1, 0)])  23 us
    ppermute x2, waiting for transfers between devices, between_planes(): two = lax.ppermute(value, 'dp', [(0, 2), (1, 3), (2, 0), (3, 1)])  18 us
    ppermute x3, waiting for transfers between devices, shards(): lax.ppermute(pred_part[j], 'dp', [(d, d ^ j) for d in range(n_dp)])  15.8 us
    ppermute x14, waiting for transfers between devices, across(): return lax.ppermute(value, 'own', [(o, o ^ j) for o in range(n_own)])  15.3 us
    pallas_call x1, Pallas kernels, local_grads(): pl.pallas_call(body, out_shape=[pred_shape, pred_shape] + grad_shapes, in...  14.2 us
    ppermute x14, starting transfers between devices, across(): return lax.ppermute(value, 'own', [(o, o ^ j) for o in range(n_own)])  11.1 us
    pallas_call x2, Pallas kernels, place_weights(): pl.pallas_call(body, out_shape=jax.ShapeDtypeStruct(shape, jnp.bfloat16),...  6.03 us
  transfers between devices with their start and end apart: 25, of which 12 were waited for; matrix products, arithmetic and copies ran while one was open for 3% of the time, Pallas kernels for 5%

profile of v13, /device:TPU:2, one launch (start us, length us, event | category | flops | bytes accessed | tf_op | source)
XLA Modules:
  0.0 174.3 jit_solution(10340348269579768028)
XLA Ops:
  0.6 1.2 dynamic-slice_bitcast_fusion
  1.9 2.4 %pack_rows.1 = (bf16[528,384]{1,0:T(8,128)(2,1)}, bf16[256,256]{1,0:T(8,128)(2,1)}) custom-call(s32[1,256]{1,0:T(1,128)} %bitcast.29, bf16[256,384]{1,0:T(8,128)(2,1)} %sig_ref.1, bf16[256,384]{1,0:T(8,128)(2,1)} %cot_ref.1), custom_call_target="tpu_custom_call" | custom-call | tf_op jit(solution)/shard_map/pack_rows/pallas_call | solution.py:79
  4.4 1.6 collective-permute-start.4
  6.0 2.6 %collective-permute-start.2 = (bf16[528,384]{1,0:T(8,128)(2,1)S(1)}, bf16[528,384]{1,0:T(8,128)(2,1)S(1)}, u32[]{:S(2)}, u32[]{:S(2)}) collective-permute-start(bf16[528,384]{1,0:T(8,128)(2,1)S(1)} %copy-done.11), channel_id=1, source_target_pairs={{0,16},{8,24},{16,0},{24,8},{1,17},{9,25},{17,1},{25,9},{2,18},{10... | collective-permute-start | bytes 1216520 | tf_op jit(solution)/shard_map/ppermute | solution.py:445
  8.6 1.6 collective-permute-start.1
  10.2 0.5 collective-permute-start.3
  10.7 16.5 %collective-permute-done.2 = bf16[528,384]{1,0:T(8,128)(2,1)S(1)} collective-permute-done((bf16[528,384]{1,0:T(8,128)(2,1)S(1)}, bf16[528,384]{1,0:T(8,128)(2,1)S(1)}, u32[]{:S(2)}, u32[]{:S(2)}) %collective-permute-start.2) | collective-permute-done | bytes 405536 | tf_op jit(solution)/shard_map/ppermute | solution.py:445
  27.7 0.6 collective-permute-start.9
  28.3 0.9 collective-permute-done.3.rest_5_
  29.3 0.7 collective-permute-start.5
  29.9 1.3 collective-permute-start.6
  31.3 1.2 collective-permute-start.8
  32.5 10.3 %collective-permute-done.6 = bf16[528,384]{1,0:T(8,128)(2,1)S(1)} collective-permute-done((bf16[528,384]{1,0:T(8,128)(2,1)S(1)}, bf16[528,384]{1,0:T(8,128)(2,1)S(1)}, u32[]{:S(2)}, u32[]{:S(2)}) %collective-permute-start.6) | collective-permute-done | bytes 405536 | tf_op jit(solution)/shard_map/ppermute | solution.py:447
  43.0 0.8 copy-done.17
  43.8 0.7 copy-done.18
  44.5 0.7 copy.13.touched_ref
  45.2 0.6 pad_add_fusion.pos_ref
  45.8 0.5 collective-permute-done.10.rest_3_
  46.3 0.7 copy-done.12
  47.0 14.2 %local_grads.1 = (bf16[4,256,384]{2,1,0:T(8,128)(2,1)}, bf16[4,256,384]{2,1,0:T(8,128)(2,1)}, bf16[2,8,2,48,256]{4,3,2,1,0:T(8,128)(2,1)}, bf16[1,8,2,48,256]{4,...) custom-call(s32[2]{0:T(128)} %pad_add_fusion.pos_ref, ...), custom_call_target="tpu_custom_call" | custom-call | tf_op jit(solution)/shard_map/local_grads/pallas_call | solution.py:263
  61.3 0.6 collective-permute-start.15
  61.9 0.7 collective-permute-start.16
  62.6 2.8 %collective-permute-start.11 = (bf16[4,256,384]{2,1,0:T(8,128)(2,1)}, bf16[4,256,384]{2,1,0:T(8,128)(2,1)S(1)}, u32[]{:S(2)}, u32[]{:S(2)}) collective-permute-start(bf16[4,256,384]{2,1,0:T(8,128)(2,1)} %get-tuple-element.36), channel_id=1, source_target_pairs={{0,1},{1,0},{2,3},{3,2},{4,5},{5,4},{6,7},{7,6},{8,9},{9,8},{10,11... | collective-permute-start | bytes 2359304 | tf_op jit(solution)/shard_map/ppermute | solution.py:497
  65.4 0.5 collective-permute-start.17
  65.9 0.5 collective-permute-start.18
  66.4 6.0 %collective-permute-done.16 = bf16[1,8,2,48,256]{4,3,2,1,0:T(8,128)(2,1)S(1)} collective-permute-done((bf16[1,8,2,48,256]{4,3,2,1,0:T(8,128)(2,1)}, bf16[1,8,2,48,256]{4,3,2,1,0:T(8,128)(2,1)S(1)}, u32[]{:S(2)}, u32[]{:S(2)}) %collective-permute-start.16) | collective-permute-done | bytes 393248 | tf_op jit(solution)/shard_map/ppermute | solution.py:497
  72.4 1.1 add_bitcast_fusion
  73.5 7.8 %collective-permute-done.15.refs_1_ = bf16[2,8,2,48,256]{4,3,2,1,0:T(8,128)(2,1)S(1)} collective-permute-done((bf16[2,8,2,48,256]{4,3,2,1,0:T(8,128)(2,1)}, bf16[2,8,2,48,256]{4,3,2,1,0:T(8,128)(2,1)S(1)}, u32[]{:S(2)}, u32[]{:S(2)}) %collective-permute-start.15) | collective-permute-done | bytes 786464 | tf_op jit(solution)/shard_map/ppermute | solution.py:497
  81.3 1.3 fusion
  82.6 1.0 collective-permute-start.20
  83.7 0.8 collective-permute-start.19
  84.7 0.8 slice_bitcast_fusion.2
  85.5 2.7 %collective-permute-start.14 = (bf16[256,384]{1,0:T(8,128)(2,1)S(1)}, bf16[256,384]{1,0:T(8,128)(2,1)S(1)}, u32[]{:S(2)}, u32[]{:S(2)}) collective-permute-start(bf16[256,384]{1,0:T(8,128)(2,1)S(1)} %get-tuple-element.54), channel_id=1, source_target_pairs={{0,24},{8,16},{16,8},{24,0},{1,25},{9,17},{17,9},{25,1},{2,26},{10... | collective-permute-start | bytes 589832 | tf_op jit(solution)/shard_map/ppermute | solution.py:552
  88.2 1.7 collective-permute-start.12
  89.9 5.2 %collective-permute-done.14.refs_3_ = bf16[256,384]{1,0:T(8,128)(2,1)S(1)} collective-permute-done((bf16[256,384]{1,0:T(8,128)(2,1)S(1)}, bf16[256,384]{1,0:T(8,128)(2,1)S(1)}, u32[]{:S(2)}, u32[]{:S(2)}) %collective-permute-start.14) | collective-permute-done | bytes 196640 | tf_op jit(solution)/shard_map/ppermute | solution.py:552
  95.1 10.6 %collective-permute-done.13.refs_2_ = bf16[256,384]{1,0:T(8,128)(2,1)S(1)} collective-permute-done((bf16[256,384]{1,0:T(8,128)(2,1)S(1)}, bf16[256,384]{1,0:T(8,128)(2,1)S(1)}, u32[]{:S(2)}, u32[]{:S(2)}) %collective-permute-start.13) | collective-permute-done | bytes 196640 | tf_op jit(solution)/shard_map/ppermute | solution.py:552
  105.7 0.8 copy-done.16
  106.6 6.0 %adam_step.1 = (bf16[16,2,48,256]{3,2,1,0:T(8,128)(2,1)}, f32[16,2,48,256]{3,2,1,0:T(8,128)}, f32[16,2,48,256]{3,2,1,0:T(8,128)}) custom-call(s32[2]{0:T(128)} %pad_add_fusion.pos_ref, bf16[1,8,2,48,256]{4,3,2,1,0:T(8,128)(2,1)} %get-tuple-element.37.refs_0_, bf16[2,8,2,48,256]{4,3,2,1,0:T(8,128)(2,1)} %copy-done.2, bf16[8,2,48,256]{3,2,1,0:T(8,128)(2,1)} %copy-done.16, ...), custom_call_target="tpu_custom_call" | custom-call | tf_op jit(solution)/shard_map/adam_step/pallas_call | solution.py:356
  112.7 3.2 %collective-permute-start.21 = (bf16[16,2,48,256]{3,2,1,0:T(8,128)(2,1)}, bf16[16,2,48,256]{3,2,1,0:T(8,128)(2,1)S(1)}, u32[]{:S(2)}, u32[]{:S(2)}) collective-permute-start(bf16[16,2,48,256]{3,2,1,0:T(8,128)(2,1)} %get-tuple-element.48.refs_0_), channel_id=1, source_target_pairs={{0,16},{8,24},{16,0},{24,8},{1,17},{9,25},{17,1},{25,9},{2,18},{10... | collective-permute-start | bytes 2359304 | tf_op jit(solution)/shard_map/ppermute | solution.py:445
  115.9 32.8 %collective-permute-done.22.refs_1_ = bf16[16,2,48,256]{3,2,1,0:T(8,128)(2,1)S(1)} collective-permute-done((bf16[16,2,48,256]{3,2,1,0:T(8,128)(2,1)}, bf16[16,2,48,256]{3,2,1,0:T(8,128)(2,1)S(1)}, u32[]{:S(2)}, u32[]{:S(2)}) %collective-permute-start.22) | collective-permute-done | bytes 786464 | tf_op jit(solution)/shard_map/ppermute | solution.py:446
  148.8 1.6 collective-permute-done.21.refs_2_
  150.3 0.7 collective-permute-start.23
  151.0 1.3 collective-permute-start.24
  152.4 2.2 %finish_predicted.1 = bf16[256,384]{1,0:T(8,128)(2,1)} custom-call(bf16[256,256]{1,0:T(8,128)(2,1)} %get-tuple-element.28.perm_ref, bf16[256,384]{1,0:T(8,128)(2,1)} %get-tuple-element.57.refs_0_, bf16[256,384]{1,0:T(8,128)(2,1)} %copy-done.21, bf16[256,384]{1,0:T(8,128)(2,1)} %copy-done.20, bf16[256,384]{1,0:T(8,128)(2,1)} %copy-done.19), custom_call_target="tpu_custom_call" | custom-call | tf_op jit(solution)/shard_map/finish_predicted/pallas_call | solution.py:475
  154.6 3.4 %place_weights.2.refs_2_ = bf16[16,2,48,1024]{3,2,1,0:T(8,128)(2,1)} custom-call(s32[2]{0:T(128)} %pad_add_fusion.pos_ref, bf16[16,2,48,256]{3,2,1,0:T(8,128)(2,1)} %get-tuple-element.48.refs_0_, bf16[16,2,48,256]{3,2,1,0:T(8,128)(2,1)} %copy-done.8, bf16[16,2,48,256]{3,2,1,0:T(8,128)(2,1)} %copy-done.7), custom_call_target="tpu_custom_call" | custom-call | tf_op jit(solution)/shard_map/place_weights/pallas_call | solution.py:423
  158.0 12.7 %collective-permute-done.24.refs_1_ = bf16[16,2,48,256]{3,2,1,0:T(8,128)(2,1)S(1)} collective-permute-done((bf16[16,2,48,256]{3,2,1,0:T(8,128)(2,1)S(1)}, bf16[16,2,48,256]{3,2,1,0:T(8,128)(2,1)S(1)}, u32[]{:S(2)}, u32[]{:S(2)}) %collective-permute-start.24) | collective-permute-done | bytes 786464 | tf_op jit(solution)/shard_map/ppermute | solution.py:447
  170.7 0.9 copy-done.10
  171.6 2.6 %place_weights.3 = bf16[16,2,48,1024]{3,2,1,0:T(8,128)(2,1)} custom-call(s32[2]{0:T(128)} %pad_add_fusion.pos_ref, bf16[16,2,48,256]{3,2,1,0:T(8,128)(2,1)} %copy-done.9, bf16[16,2,48,256]{3,2,1,0:T(8,128)(2,1)} %copy-done.10, bf16[16,2,48,1024]{3,2,1,0:T(8,128)(2,1)} %place_weights.2.refs_2_), custom_call_target="tpu_custom_call", output_to_operand_aliasing={{}: (3, {})} | custom-call | tf_op jit(solution)/shard_map/place_weights/pallas_call | solution.py:423
  (66 shorter events, 1.2 us)
Async XLA Ops:
  1.8 2.5 %collective-permute-start = (bf16[8,2,48,256]{3,2,1,0:T(8,128)(2,1)S(1)}, bf16[8,2,48,256]{3,2,1,0:T(8,128)(2,1)S(1)}, u32[]{:S(2)}, u32[]{:S(2)}) collective-permute-start(bf16[8,2,48,256]{3,2,1,0:T(8,128)(2,1)S(1)} %get-tuple-element.53), channel_id=1, source_target_pairs={{0,1},{1,0},{2,3},{3,2},{4,5},{5,4},{6,7},{7,6},{8,9},{9,8},{10,11... | collective-permute-start | bytes 1179656 | tf_op jit(solution)/shard_map/ppermute | solution.py:497
  4.3 1.7 copy-start.11
  4.4 23.3 %copy-start.1 = (bf16[2,8,2,48,256]{4,3,2,1,0:T(8,128)(2,1)}, bf16[2,8,2,48,256]{4,3,2,1,0:T(8,128)(2,1)S(1)}, u32[]{:S(2)}) copy-start(bf16[2,8,2,48,256]{4,3,2,1,0:T(8,128)(2,1)S(1)} %pad_maximum_fusion.1.rest_4_) | copy-start | bytes 2359300
  4.4 23.2 %collective-permute-start.4 = (bf16[2,8,2,48,256]{4,3,2,1,0:T(8,128)(2,1)S(1)}, bf16[2,8,2,48,256]{4,3,2,1,0:T(8,128)(2,1)S(1)}, u32[]{:S(2)}, u32[]{:S(2)}) collective-permute-start(bf16[2,8,2,48,256]{4,3,2,1,0:T(8,128)(2,1)S(1)} %pad_maximum_fusion.1.rest_4_), channel_id=1, source_target_pairs={{0,4},{1,5},{2,6},{3,7},{4,0},{5,1},{6,2},{7,3},{8,12},{9,13},{10,... | collective-permute-start | bytes 2359304 | tf_op jit(solution)/shard_map/ppermute | solution.py:497
  6.0 21.2 %collective-permute-start.2 = (bf16[528,384]{1,0:T(8,128)(2,1)S(1)}, bf16[528,384]{1,0:T(8,128)(2,1)S(1)}, u32[]{:S(2)}, u32[]{:S(2)}) collective-permute-start(bf16[528,384]{1,0:T(8,128)(2,1)S(1)} %copy-done.11), channel_id=1, source_target_pairs={{0,16},{8,24},{16,0},{24,8},{1,17},{9,25},{17,1},{25,9},{2,18},{10... | collective-permute-start | bytes 1216520 | tf_op jit(solution)/shard_map/ppermute | solution.py:445
  8.6 18.8 %collective-permute-start.1 = (bf16[528,384]{1,0:T(8,128)(2,1)S(1)}, bf16[528,384]{1,0:T(8,128)(2,1)S(1)}, u32[]{:S(2)}, u32[]{:S(2)}) collective-permute-start(bf16[528,384]{1,0:T(8,128)(2,1)S(1)} %copy-done.11), channel_id=1, source_target_pairs={{0,8},{8,0},{16,24},{24,16},{1,9},{9,1},{17,25},{25,17},{2,10},{10... | collective-permute-start | bytes 1216520 | tf_op jit(solution)/shard_map/ppermute | solution.py:446
  10.2 19.1 %collective-permute-start.3 = (bf16[2,8,2,48,256]{4,3,2,1,0:T(8,128)(2,1)S(1)}, bf16[2,8,2,48,256]{4,3,2,1,0:T(8,128)(2,1)S(1)}, u32[]{:S(2)}, u32[]{:S(2)}) collective-permute-start(bf16[2,8,2,48,256]{4,3,2,1,0:T(8,128)(2,1)S(1)} %pad_maximum_fusion.1.rest_4_), channel_id=1, source_target_pairs={{0,2},{1,3},{2,0},{3,1},{4,6},{5,7},{6,4},{7,5},{8,10},{9,11},{10,... | collective-permute-start | bytes 2359304 | tf_op jit(solution)/shard_map/ppermute | solution.py:497
  27.5 18.7 %copy-start = (bf16[3,528,384]{2,1,0:T(8,128)(2,1)}, bf16[3,528,384]{2,1,0:T(8,128)(2,1)S(1)}, u32[]{:S(2)}) copy-start(bf16[3,528,384]{2,1,0:T(8,128)(2,1)S(1)} %pad_maximum_fusion.rest_0_) | copy-start | bytes 3649540
  27.6 17.0 %copy-start.22 = (s32[32,4]{0,1:T(4,128)S(1)}, s32[32,4]{0,1:T(4,128)}, u32[]{:S(2)}) copy-start(s32[32,4]{0,1:T(4,128)} %param.11) | copy-start | bytes 1540
  27.6 18.7 %collective-permute-start.7 = (bf16[3,528,384]{2,1,0:T(8,128)(2,1)S(1)}, bf16[3,528,384]{2,1,0:T(8,128)(2,1)}, u32[]{:S(2)}, u32[]{:S(2)}) collective-permute-start(bf16[3,528,384]{2,1,0:T(8,128)(2,1)S(1)} %pad_maximum_fusion.rest_0_), channel_id=1, source_target_pairs={{0,1},{1,0},{2,3},{3,2},{4,5},{5,4},{6,7},{7,6},{8,9},{9,8},{10,11... | collective-permute-start | bytes 3649544 | tf_op jit(solution)/shard_map/ppermute | solution.py:497
  27.7 18.6 %copy-start.3 = (bf16[2,8,2,48,256]{4,3,2,1,0:T(8,128)(2,1)}, bf16[2,8,2,48,256]{4,3,2,1,0:T(8,128)(2,1)S(1)}, u32[]{:S(2)}) copy-start(bf16[2,8,2,48,256]{4,3,2,1,0:T(8,128)(2,1)S(1)} %collective-permute-done.4.rest_6_) | copy-start | bytes 2359300
  27.7 15.3 %collective-permute-start.9 = (bf16[8,2,48,256]{3,2,1,0:T(8,128)(2,1)S(1)}, bf16[8,2,48,256]{3,2,1,0:T(8,128)(2,1)S(1)}, u32[]{:S(2)}, u32[]{:S(2)}) collective-permute-start(bf16[8,2,48,256]{3,2,1,0:T(8,128)(2,1)S(1)} %slice_bitcast_fusion), channel_id=1, source_target_pairs={{0,2},{1,3},{2,0},{3,1},{4,6},{5,7},{6,4},{7,5},{8,10},{9,11},{10,... | collective-permute-start | bytes 1179656 | tf_op jit(solution)/shard_map/ppermute | solution.py:497
  29.3 2.0 %copy-start.4 = (bf16[2,8,2,48,256]{4,3,2,1,0:T(8,128)(2,1)}, bf16[2,8,2,48,256]{4,3,2,1,0:T(8,128)(2,1)S(1)}, u32[]{:S(2)}) copy-start(bf16[2,8,2,48,256]{4,3,2,1,0:T(8,128)(2,1)S(1)} %collective-permute-done.3.rest_5_) | copy-start | bytes 2359300
  29.3 3.3 %collective-permute-start.5 = (bf16[528,384]{1,0:T(8,128)(2,1)S(1)}, bf16[528,384]{1,0:T(8,128)(2,1)S(1)}, u32[]{:S(2)}, u32[]{:S(2)}) collective-permute-start(bf16[528,384]{1,0:T(8,128)(2,1)S(1)} %copy-done.11), channel_id=1, source_target_pairs={{8,16},{16,8},{9,17},{17,9},{10,18},{18,10},{11,19},{19,11},{12,20... | collective-permute-start | bytes 1216520 | tf_op jit(solution)/shard_map/ppermute | solution.py:448
  29.9 12.9 %collective-permute-start.6 = (bf16[528,384]{1,0:T(8,128)(2,1)S(1)}, bf16[528,384]{1,0:T(8,128)(2,1)S(1)}, u32[]{:S(2)}, u32[]{:S(2)}) collective-permute-start(bf16[528,384]{1,0:T(8,128)(2,1)S(1)} %collective-permute-done.2), channel_id=1, source_target_pairs={{16,24},{8,0},{17,25},{9,1},{18,26},{10,2},{19,27},{11,3},{20,28},... | collective-permute-start | bytes 1216520 | tf_op jit(solution)/shard_map/ppermute | solution.py:447
  31.3 11.7 %collective-permute-start.8 = (bf16[8,2,48,256]{3,2,1,0:T(8,128)(2,1)S(1)}, bf16[8,2,48,256]{3,2,1,0:T(8,128)(2,1)S(1)}, u32[]{:S(2)}, u32[]{:S(2)}) collective-permute-start(bf16[8,2,48,256]{3,2,1,0:T(8,128)(2,1)S(1)} %slice_bitcast_fusion.1), channel_id=1, source_target_pairs={{0,4},{1,5},{2,6},{3,7},{4,0},{5,1},{6,2},{7,3},{8,12},{9,13},{10,... | collective-permute-start | bytes 1179656 | tf_op jit(solution)/shard_map/ppermute | solution.py:497
  43.0 3.3 %copy-start.5 = (bf16[528,384]{1,0:T(8,128)(2,1)}, bf16[528,384]{1,0:T(8,128)(2,1)S(1)}, u32[]{:S(2)}) copy-start(bf16[528,384]{1,0:T(8,128)(2,1)S(1)} %add.31.rest_1_) | copy-start | bytes 1216516
  43.0 0.8 copy-start.17
  43.8 0.7 copy-start.18
  44.5 1.7 collective-permute-start.10
  46.3 0.8 copy-start.12
  61.3 23.3 %copy-start.6 = (bf16[4,256,384]{2,1,0:T(8,128)(2,1)S(1)}, bf16[4,256,384]{2,1,0:T(8,128)(2,1)}, u32[]{:S(2)}) copy-start(bf16[4,256,384]{2,1,0:T(8,128)(2,1)} %get-tuple-element.35) | copy-start | bytes 2359300
  61.3 20.0 %collective-permute-start.15 = (bf16[2,8,2,48,256]{4,3,2,1,0:T(8,128)(2,1)}, bf16[2,8,2,48,256]{4,3,2,1,0:T(8,128)(2,1)S(1)}, u32[]{:S(2)}, u32[]{:S(2)}) collective-permute-start(bf16[2,8,2,48,256]{4,3,2,1,0:T(8,128)(2,1)} %get-tuple-element.38), channel_id=1, source_target_pairs={{0,2},{1,3},{2,0},{3,1},{4,6},{5,7},{6,4},{7,5},{8,10},{9,11},{10,... | collective-permute-start | bytes 2359304 | tf_op jit(solution)/shard_map/ppermute | solution.py:497
  61.9 10.5 %collective-permute-start.16 = (bf16[1,8,2,48,256]{4,3,2,1,0:T(8,128)(2,1)}, bf16[1,8,2,48,256]{4,3,2,1,0:T(8,128)(2,1)S(1)}, u32[]{:S(2)}, u32[]{:S(2)}) collective-permute-start(bf16[1,8,2,48,256]{4,3,2,1,0:T(8,128)(2,1)} %get-tuple-element.40), channel_id=1, source_target_pairs={{0,4},{1,5},{2,6},{3,7},{4,0},{5,1},{6,2},{7,3},{8,12},{9,13},{10,... | collective-permute-start | bytes 1179656 | tf_op jit(solution)/shard_map/ppermute | solution.py:497
  62.6 21.9 %collective-permute-start.11 = (bf16[4,256,384]{2,1,0:T(8,128)(2,1)}, bf16[4,256,384]{2,1,0:T(8,128)(2,1)S(1)}, u32[]{:S(2)}, u32[]{:S(2)}) collective-permute-start(bf16[4,256,384]{2,1,0:T(8,128)(2,1)} %get-tuple-element.36), channel_id=1, source_target_pairs={{0,1},{1,0},{2,3},{3,2},{4,5},{5,4},{6,7},{7,6},{8,9},{9,8},{10,11... | collective-permute-start | bytes 2359304 | tf_op jit(solution)/shard_map/ppermute | solution.py:497
  65.4 17.2 %collective-permute-start.17 = (bf16[1,8,2,48,256]{4,3,2,1,0:T(8,128)(2,1)}, bf16[1,8,2,48,256]{4,3,2,1,0:T(8,128)(2,1)S(1)}, u32[]{:S(2)}, u32[]{:S(2)}) collective-permute-start(bf16[1,8,2,48,256]{4,3,2,1,0:T(8,128)(2,1)} %get-tuple-element.41), channel_id=1, source_target_pairs={{0,5},{1,4},{2,7},{3,6},{4,1},{5,0},{6,3},{7,2},{8,13},{9,12},{10,... | collective-permute-start | bytes 1179656 | tf_op jit(solution)/shard_map/ppermute | solution.py:497
  65.9 16.7 %collective-permute-start.18 = (bf16[1,8,2,48,256]{4,3,2,1,0:T(8,128)(2,1)}, bf16[1,8,2,48,256]{4,3,2,1,0:T(8,128)(2,1)S(1)}, u32[]{:S(2)}, u32[]{:S(2)}) collective-permute-start(bf16[1,8,2,48,256]{4,3,2,1,0:T(8,128)(2,1)} %get-tuple-element.42), channel_id=1, source_target_pairs={{0,1},{1,0},{2,3},{3,2},{4,5},{5,4},{6,7},{7,6},{8,9},{9,8},{10,11... | collective-permute-start | bytes 1179656 | tf_op jit(solution)/shard_map/ppermute | solution.py:497
  81.3 3.4 %copy-start.2 = (bf16[2,8,2,48,256]{4,3,2,1,0:T(8,128)(2,1)}, bf16[2,8,2,48,256]{4,3,2,1,0:T(8,128)(2,1)S(1)}, u32[]{:S(2)}) copy-start(bf16[2,8,2,48,256]{4,3,2,1,0:T(8,128)(2,1)S(1)} %collective-permute-done.15.refs_1_) | copy-start | bytes 2359300
  82.6 2.9 %copy-start.13 = (bf16[1,8,2,48,256]{4,3,2,1,0:T(8,128)(2,1)}, bf16[1,8,2,48,256]{4,3,2,1,0:T(8,128)(2,1)S(1)}, u32[]{:S(2)}) copy-start(bf16[1,8,2,48,256]{4,3,2,1,0:T(8,128)(2,1)S(1)} %collective-permute-done.17.refs_4_) | copy-start | bytes 1179652
  82.6 2.9 %copy-start.14 = (bf16[1,8,2,48,256]{4,3,2,1,0:T(8,128)(2,1)}, bf16[1,8,2,48,256]{4,3,2,1,0:T(8,128)(2,1)S(1)}, u32[]{:S(2)}) copy-start(bf16[1,8,2,48,256]{4,3,2,1,0:T(8,128)(2,1)S(1)} %collective-permute-done.18.refs_3_) | copy-start | bytes 1179652
  82.6 23.1 %collective-permute-start.20 = (bf16[8,2,48,256]{3,2,1,0:T(8,128)(2,1)S(1)}, bf16[8,2,48,256]{3,2,1,0:T(8,128)(2,1)S(1)}, u32[]{:S(2)}, u32[]{:S(2)}) collective-permute-start(bf16[8,2,48,256]{3,2,1,0:T(8,128)(2,1)S(1)} %add_bitcast_fusion), channel_id=1, source_target_pairs={{0,3},{1,2},{2,1},{3,0},{4,7},{5,6},{6,5},{7,4},{8,11},{9,10},{10,... | collective-permute-start | bytes 1179656 | tf_op jit(solution)/shard_map/ppermute | solution.py:497
  83.7 22.0 %collective-permute-start.19 = (bf16[8,2,48,256]{3,2,1,0:T(8,128)(2,1)S(1)}, bf16[8,2,48,256]{3,2,1,0:T(8,128)(2,1)S(1)}, u32[]{:S(2)}, u32[]{:S(2)}) collective-permute-start(bf16[8,2,48,256]{3,2,1,0:T(8,128)(2,1)S(1)} %fusion), channel_id=1, source_target_pairs={{0,4},{1,5},{2,6},{3,7},{4,0},{5,1},{6,2},{7,3},{8,12},{9,13},{10,... | collective-permute-start | bytes 1179656 | tf_op jit(solution)/shard_map/ppermute | solution.py:497
  85.5 9.6 %collective-permute-start.14 = (bf16[256,384]{1,0:T(8,128)(2,1)S(1)}, bf16[256,384]{1,0:T(8,128)(2,1)S(1)}, u32[]{:S(2)}, u32[]{:S(2)}) collective-permute-start(bf16[256,384]{1,0:T(8,128)(2,1)S(1)} %get-tuple-element.54), channel_id=1, source_target_pairs={{0,24},{8,16},{16,8},{24,0},{1,25},{9,17},{17,9},{25,1},{2,26},{10... | collective-permute-start | bytes 589832 | tf_op jit(solution)/shard_map/ppermute | solution.py:552
  88.2 17.5 %collective-permute-start.13 = (bf16[256,384]{1,0:T(8,128)(2,1)S(1)}, bf16[256,384]{1,0:T(8,128)(2,1)S(1)}, u32[]{:S(2)}, u32[]{:S(2)}) collective-permute-start(bf16[256,384]{1,0:T(8,128)(2,1)S(1)} %get-tuple-element.55), channel_id=1, source_target_pairs={{0,16},{8,24},{16,0},{24,8},{1,17},{9,25},{17,1},{25,9},{2,18},{10... | collective-permute-start | bytes 589832 | tf_op jit(solution)/shard_map/ppermute | solution.py:552
  88.2 17.5 %collective-permute-start.12 = (bf16[256,384]{1,0:T(8,128)(2,1)S(1)}, bf16[256,384]{1,0:T(8,128)(2,1)S(1)}, u32[]{:S(2)}, u32[]{:S(2)}) collective-permute-start(bf16[256,384]{1,0:T(8,128)(2,1)S(1)} %get-tuple-element.56), channel_id=1, source_target_pairs={{0,8},{8,0},{16,24},{24,16},{1,9},{9,1},{17,25},{25,17},{2,10},{10... | collective-permute-start | bytes 589832 | tf_op jit(solution)/shard_map/ppermute | solution.py:552
  95.1 57.2 %copy-start.19 = (bf16[256,384]{1,0:T(8,128)(2,1)}, bf16[256,384]{1,0:T(8,128)(2,1)S(1)}, u32[]{:S(2)}) copy-start(bf16[256,384]{1,0:T(8,128)(2,1)S(1)} %collective-permute-done.14.refs_3_) | copy-start | bytes 589828
  105.7 46.6 %copy-start.20 = (bf16[256,384]{1,0:T(8,128)(2,1)}, bf16[256,384]{1,0:T(8,128)(2,1)S(1)}, u32[]{:S(2)}) copy-start(bf16[256,384]{1,0:T(8,128)(2,1)S(1)} %collective-permute-done.13.refs_2_) | copy-start | bytes 589828
  105.7 46.7 %copy-start.21 = (bf16[256,384]{1,0:T(8,128)(2,1)}, bf16[256,384]{1,0:T(8,128)(2,1)S(1)}, u32[]{:S(2)}) copy-start(bf16[256,384]{1,0:T(8,128)(2,1)S(1)} %collective-permute-done.12.refs_1_) | copy-start | bytes 589828
  105.7 0.8 copy-start.16
  105.7 0.9 copy-start.15
  112.7 36.1 %collective-permute-start.22 = (bf16[16,2,48,256]{3,2,1,0:T(8,128)(2,1)}, bf16[16,2,48,256]{3,2,1,0:T(8,128)(2,1)S(1)}, u32[]{:S(2)}, u32[]{:S(2)}) collective-permute-start(bf16[16,2,48,256]{3,2,1,0:T(8,128)(2,1)} %get-tuple-element.48.refs_0_), channel_id=1, source_target_pairs={{0,8},{8,0},{16,24},{24,16},{1,9},{9,1},{17,25},{25,17},{2,10},{10... | collective-permute-start | bytes 2359304 | tf_op jit(solution)/shard_map/ppermute | solution.py:446
  112.7 37.6 %collective-permute-start.21 = (bf16[16,2,48,256]{3,2,1,0:T(8,128)(2,1)}, bf16[16,2,48,256]{3,2,1,0:T(8,128)(2,1)S(1)}, u32[]{:S(2)}, u32[]{:S(2)}) collective-permute-start(bf16[16,2,48,256]{3,2,1,0:T(8,128)(2,1)} %get-tuple-element.48.refs_0_), channel_id=1, source_target_pairs={{0,16},{8,24},{16,0},{24,8},{1,17},{9,25},{17,1},{25,9},{2,18},{10... | collective-permute-start | bytes 2359304 | tf_op jit(solution)/shard_map/ppermute | solution.py:445
  148.8 5.8 %copy-start.8 = (bf16[16,2,48,256]{3,2,1,0:T(8,128)(2,1)}, bf16[16,2,48,256]{3,2,1,0:T(8,128)(2,1)S(1)}, u32[]{:S(2)}) copy-start(bf16[16,2,48,256]{3,2,1,0:T(8,128)(2,1)S(1)} %collective-permute-done.22.refs_1_) | copy-start | bytes 2359300
  150.3 4.3 %copy-start.7 = (bf16[16,2,48,256]{3,2,1,0:T(8,128)(2,1)}, bf16[16,2,48,256]{3,2,1,0:T(8,128)(2,1)S(1)}, u32[]{:S(2)}) copy-start(bf16[16,2,48,256]{3,2,1,0:T(8,128)(2,1)S(1)} %collective-permute-done.21.refs_2_) | copy-start | bytes 2359300
  150.3 7.7 %collective-permute-start.23 = (bf16[16,2,48,256]{3,2,1,0:T(8,128)(2,1)}, bf16[16,2,48,256]{3,2,1,0:T(8,128)(2,1)S(1)}, u32[]{:S(2)}, u32[]{:S(2)}) collective-permute-start(bf16[16,2,48,256]{3,2,1,0:T(8,128)(2,1)} %get-tuple-element.48.refs_0_), channel_id=1, source_target_pairs={{8,16},{16,8},{9,17},{17,9},{10,18},{18,10},{11,19},{19,11},{12,20... | collective-permute-start | bytes 2359304 | tf_op jit(solution)/shard_map/ppermute | solution.py:448
  151.0 19.7 %collective-permute-start.24 = (bf16[16,2,48,256]{3,2,1,0:T(8,128)(2,1)S(1)}, bf16[16,2,48,256]{3,2,1,0:T(8,128)(2,1)S(1)}, u32[]{:S(2)}, u32[]{:S(2)}) collective-permute-start(bf16[16,2,48,256]{3,2,1,0:T(8,128)(2,1)S(1)} %collective-permute-done.21.refs_2_), channel_id=1, source_target_pairs={{16,24},{8,0},{17,25},{9,1},{18,26},{10,2},{19,27},{11,3},{20,28},... | collective-permute-start | bytes 2359304 | tf_op jit(solution)/shard_map/ppermute | solution.py:447
  158.0 12.7 %copy-start.9 = (bf16[16,2,48,256]{3,2,1,0:T(8,128)(2,1)}, bf16[16,2,48,256]{3,2,1,0:T(8,128)(2,1)S(1)}, u32[]{:S(2)}) copy-start(bf16[16,2,48,256]{3,2,1,0:T(8,128)(2,1)S(1)} %collective-permute-done.23.refs_0_) | copy-start | bytes 2359300
  170.7 0.9 copy-start.10

commit v14 on v13

--- a/solution.py
+++ b/solution.py
@@ -12,6 +12,7 @@
 ID_ROWS = 16
 PARTS = 4
 VMEM_BYTES = 56 * 2**20
+LAST_VMEM_BYTES = 8 * 2**20
 
 gelu_coef = math.sqrt(2.0 / math.pi)
 cubic_coef = 0.044715
@@ -28,8 +29,8 @@
     return (gelu_val, slopes)
 
 
-def params():
-    return pltpu.CompilerParams(vmem_limit_bytes=VMEM_BYTES)
+def params(limit=VMEM_BYTES):
+    return pltpu.CompilerParams(vmem_limit_bytes=limit)
 
 
 def vmem():
@@ -212,9 +213,10 @@
         lax.fori_loop(0, (count + 1) // 2, pair, 0)
         outs = [
             pltpu.make_async_copy(
-                pred.at[pl.ds(which * planes, planes)], pred_refs[which], sem_out.at[which]
+                pred.at[which * planes + i], pred_refs[which].at[pos_ref[0] ^ i], sem_out.at[which, i]
             )
             for which in (1, 0)
+            for i in range(planes)
         ]
         for copy in outs:
             copy.start()
@@ -230,7 +232,7 @@
                 return 0
 
             lax.fori_loop(0, half, write, 0)
-            outs.append(pltpu.make_async_copy(into, ref, sem_out.at[2 + n]))
+            outs.append(pltpu.make_async_copy(into, ref, sem_out.at[2 + n, 0]))
             outs[-1].start()
         for copy in outs:
             copy.wait()
@@ -258,7 +260,7 @@
         pltpu.SMEM((2 * planes,), jnp.int32),
         pltpu.SMEM((4, most + 1), jnp.int32),
         pltpu.SemaphoreType.DMA((4 + n_own,)),
-        pltpu.SemaphoreType.DMA((2 + len(grad_shapes),)),
+        pltpu.SemaphoreType.DMA((2 + len(grad_shapes), planes)),
     ]
     found = pl.pallas_call(
         body,
@@ -431,7 +433,7 @@
             pltpu.SemaphoreType.DMA((PARTS, len(flat))),
         ],
         input_output_aliases={1 + len(arrays): 0} if before else {},
-        compiler_params=params(),
+        compiler_params=params(LAST_VMEM_BYTES if before else VMEM_BYTES),
         name="place_weights",
     )(pos, *arrays, *before)
 
@@ -461,11 +463,9 @@
 
 
 def finish_predicted(perm, parts):
-    def body(perm_ref, *refs):
-        total = refs[0][...].astype(jnp.float32)
-        for ref in refs[1:-1]:
-            total = total + ref[...].astype(jnp.float32)
-        refs[-1][...] = lax.dot_general(
+    def body(perm_ref, parts_ref, out_ref):
+        total = jnp.sum(parts_ref[...].astype(jnp.float32), axis=0)
+        out_ref[...] = lax.dot_general(
             perm_ref[...],
             total.astype(jnp.bfloat16),
             (((0,), (0,)), ((), ())),
@@ -474,12 +474,12 @@
 
     return pl.pallas_call(
         body,
-        out_shape=jax.ShapeDtypeStruct(parts[0].shape, jnp.bfloat16),
-        in_specs=[vmem()] * (1 + len(parts)),
+        out_shape=jax.ShapeDtypeStruct(parts.shape[1:], jnp.bfloat16),
+        in_specs=[vmem(), vmem()],
         out_specs=vmem(),
         compiler_params=params(),
         name="finish_predicted",
-    )(perm, *parts)
+    )(perm, parts)
 
 
 def shards(signals, cotangent, row_insertion, touched, slot_map, weights, moment1, moment2):
@@ -530,12 +530,14 @@
     pred_mine, pred_other, grads = local_grads(
         pos, touched, slot_map, rows_in, blocks, sends, piece, width
     )
+    pred_part = pred_mine + across(pred_other, 1)
+    parts = lax.all_to_all(pred_part, "dp", split_axis=0, concat_axis=0, tiled=True)
     if sends:
         x_same, y_diagonal, y_cross, partner, x_cross, y_same, own = grads
         x_same = across(x_same, 2)
         y_diagonal = across(y_diagonal, 4)
-        y_cross = across(y_cross, 5)
-        partner = across(partner, 1)
+        y_cross = across(after(y_cross, pred_part), 5)
+        partner = across(after(partner, pred_part), 1)
         first = (x_same, y_diagonal, y_cross, partner)
         x_cross = across(after(x_cross[0] + y_diagonal[0], *first), 3)
         y_same = across(after(y_same[0] + x_same[1], *first), 4)
@@ -547,12 +549,8 @@
         ]
         terms = [arrived[0::2], arrived[1::2]]
 
-    pred_part = pred_mine + across(pred_other, 1)
-    parts = [pred_part[0]] + [
-        lax.ppermute(pred_part[j], "dp", [(d, d ^ j) for d in range(n_dp)]) for j in range(1, n_dp)
-    ]
     predicted = finish_predicted(perm, parts)
-    terms[0][-1] = after(terms[0][-1], *parts[1:])
+    terms[0][-1] = after(terms[0][-1], parts)
 
     fresh, new_moment1, new_moment2 = adam(pos, terms, weights, moment1, moment2)
     new_weights = gather_weights(pos, fresh, dp_at, n_dp)

time: 176 us -> 168 us (0.955)
  waiting for transfers between devices: 105 us -> 95.4 us
  local copies, waits for them, and re-layouts: 6.83 us -> 4.36 us
    ppermute x3 -> x0, waiting for transfers between devices: 15.8 us -> none  [shards(): lax.ppermute(pred_part[j], 'dp', [(d, d ^ j) for d in range(n_dp)])]
    ppermute x14, waiting for transfers between devices: 15.3 us -> 20.1 us  [across(): return lax.ppermute(value, 'own', [(o, o ^ j) for o in range(n_own)])]
    ppermute x3 -> x0, starting transfers between devices: 4.39 us -> none  [shards(): lax.ppermute(pred_part[j], 'dp', [(d, d ^ j) for d in range(n_dp)])]
    all_to_all x0 -> x1, starting transfers between devices: none -> 4.15 us  [shards(): lax.all_to_all(pred_part, 'dp', split_axis=0, concat_axis=0, tiled=True)]
    ppermute x2, starting transfers between devices: 1.65 us -> 3.79 us  [between_planes(): lax.ppermute(after(value, *first), 'dp', [(0, 1), (1, 0), (2, 3), (3, 2)])]
    add x1, other arithmetic: 0.19 us -> 2.25 us  [shards(): pred_part = pred_mine + across(pred_other, 1)]
    unnamed x47 -> x43, local copies, waits for them, and re-layouts: 4.84 us -> 3.13 us
  transfers between devices with their start and end apart: 25 -> 23, of which waited for: 12 -> 13; matrix products, arithmetic and copies ran while one was open for 3% -> 3% of each run, Pallas kernels for 5% -> 5%
where the time goes in v14:
time: 168 us; the launch traced here: 165 us
  waiting for transfers between devices  95.4 us (57%)
  Pallas kernels  31.9 us (19%)
  starting transfers between devices  28.4 us (17%)
  local copies, waits for them, and re-layouts  4.36 us (3%)
  other arithmetic  4.34 us (3%)
    ppermute x2, waiting for transfers between devices, between_planes(): lax.ppermute(after(value, *first), 'dp', [(0, 1), (1, 0), (2, 3), (3, 2)])  32.6 us
    ppermute x2, waiting for transfers between devices, between_planes(): outer = lax.ppermute(after(two, one, *second), 'dp', [(2, 3), (1, 0)])  23.5 us
    ppermute x14, waiting for transfers between devices, across(): return lax.ppermute(value, 'own', [(o, o ^ j) for o in range(n_own)])  20.1 us
    ppermute x2, waiting for transfers between devices, between_planes(): two = lax.ppermute(value, 'dp', [(0, 2), (1, 3), (2, 0), (3, 1)])  19.1 us
    pallas_call x1, Pallas kernels, local_grads(): pl.pallas_call(body, out_shape=[pred_shape, pred_shape] + grad_shapes, in...  15.3 us
    ppermute x14, starting transfers between devices, across(): return lax.ppermute(value, 'own', [(o, o ^ j) for o in range(n_own)])  11.6 us
    pallas_call x1, Pallas kernels, adam(): pl.pallas_call(body, out_shape=[jax.ShapeDtypeStruct(moment1.shape, jnp.b...  6 us
    pallas_call x2, Pallas kernels, place_weights(): pl.pallas_call(body, out_shape=jax.ShapeDtypeStruct(shape, jnp.bfloat16),...  5.98 us
  transfers between devices with their start and end apart: 23, of which 13 were waited for; matrix products, arithmetic and copies ran while one was open for 3% of the time, Pallas kernels for 5%

profile of v14, /device:TPU:2, one launch (start us, length us, event | category | flops | bytes accessed | tf_op | source)
XLA Modules:
  0.0 165.4 jit_solution(12308645048530160441)
XLA Ops:
  0.6 1.2 dynamic-slice_bitcast_fusion
  1.9 2.4 %pack_rows.1 = (bf16[528,384]{1,0:T(8,128)(2,1)}, bf16[256,256]{1,0:T(8,128)(2,1)}) custom-call(s32[1,256]{1,0:T(1,128)} %bitcast.21, bf16[256,384]{1,0:T(8,128)(2,1)} %sig_ref.1, bf16[256,384]{1,0:T(8,128)(2,1)} %cot_ref.1), custom_call_target="tpu_custom_call" | custom-call | tf_op jit(solution)/shard_map/pack_rows/pallas_call | solution.py:80
  4.4 1.6 collective-permute-start.4
  6.0 2.6 %collective-permute-start.2 = (bf16[528,384]{1,0:T(8,128)(2,1)S(1)}, bf16[528,384]{1,0:T(8,128)(2,1)S(1)}, u32[]{:S(2)}, u32[]{:S(2)}) collective-permute-start(bf16[528,384]{1,0:T(8,128)(2,1)S(1)} %copy-done.10), channel_id=1, source_target_pairs={{0,16},{8,24},{16,0},{24,8},{1,17},{9,25},{17,1},{25,9},{2,18},{10... | collective-permute-start | bytes 1216520 | tf_op jit(solution)/shard_map/ppermute | solution.py:447
  8.6 1.6 collective-permute-start.1
  10.2 0.5 collective-permute-start.3
  10.7 16.5 %collective-permute-done.2 = bf16[528,384]{1,0:T(8,128)(2,1)S(1)} collective-permute-done((bf16[528,384]{1,0:T(8,128)(2,1)S(1)}, bf16[528,384]{1,0:T(8,128)(2,1)S(1)}, u32[]{:S(2)}, u32[]{:S(2)}) %collective-permute-start.2) | collective-permute-done | bytes 405536 | tf_op jit(solution)/shard_map/ppermute | solution.py:447
  27.2 0.2 collective-permute-done.1
  27.4 0.2 pad_maximum_fusion.rest_0_
  27.7 0.6 collective-permute-start.9
  28.3 0.9 collective-permute-done.3.rest_5_
  29.3 0.7 collective-permute-start.5
  29.9 1.3 collective-permute-start.6
  31.3 1.2 collective-permute-start.8
  32.5 10.3 %collective-permute-done.6 = bf16[528,384]{1,0:T(8,128)(2,1)S(1)} collective-permute-done((bf16[528,384]{1,0:T(8,128)(2,1)S(1)}, bf16[528,384]{1,0:T(8,128)(2,1)S(1)}, u32[]{:S(2)}, u32[]{:S(2)}) %collective-permute-start.6) | collective-permute-done | bytes 405536 | tf_op jit(solution)/shard_map/ppermute | solution.py:449
  42.8 0.1 add.31.rest_1_
  43.1 0.7 copy.13.touched_ref
  43.8 0.7 pad_add_fusion.pos_ref
  44.5 0.3 collective-permute-done.10.rest_3_
  44.8 0.7 copy-done.11
  45.6 15.3 %local_grads.1 = (bf16[4,256,384]{2,1,0:T(8,128)(2,1)}, bf16[4,256,384]{2,1,0:T(8,128)(2,1)}, bf16[2,8,2,48,256]{4,3,2,1,0:T(8,128)(2,1)}, bf16[1,8,2,48,256]{4,...) custom-call(s32[2]{0:T(128)} %pad_add_fusion.pos_ref, ...), custom_call_target="tpu_custom_call" | custom-call | tf_op jit(solution)/shard_map/local_grads/pallas_call | solution.py:265
  61.0 1.5 collective-permute-start.12
  62.6 4.0 %collective-permute-start.13 = (bf16[1,8,2,48,256]{4,3,2,1,0:T(8,128)(2,1)}, bf16[1,8,2,48,256]{4,3,2,1,0:T(8,128)(2,1)S(1)}, u32[]{:S(2)}, u32[]{:S(2)}) collective-permute-start(bf16[1,8,2,48,256]{4,3,2,1,0:T(8,128)(2,1)} %get-tuple-element.42), channel_id=1, source_target_pairs={{0,4},{1,5},{2,6},{3,7},{4,0},{5,1},{6,2},{7,3},{8,12},{9,13},{10,... | collective-permute-start | bytes 1179656 | tf_op jit(solution)/shard_map/ppermute | solution.py:497
  66.5 2.3 %add.32 = bf16[4,256,384]{2,1,0:T(8,128)(2,1)} add(bf16[4,256,384]{2,1,0:T(8,128)(2,1)} %get-tuple-element.37, bf16[4,256,384]{2,1,0:T(8,128)(2,1)S(1)} %collective-permute-done.11) | non-fusion elementwise | flops 393216 | bytes 2359296 | tf_op jit(solution)/shard_map/add | solution.py:533
  68.8 4.2 %all-to-all-start = ((bf16[4,256,384]{2,1,0:T(8,128)(2,1)}), bf16[4,256,384]{2,1,0:T(8,128)(2,1)S(1)}, u32[]{:S(2)}, u32[]{:S(2)}) async-start(bf16[4,256,384]{2,1,0:T(8,128)(2,1)} %add.32), calls=%async_computation | async-start | bytes 1572864 | tf_op jit(solution)/shard_map/all_to_all | solution.py:534
  72.9 0.1 collective-permute-start.15
  73.1 3.3 %collective-permute-done.13 = bf16[1,8,2,48,256]{4,3,2,1,0:T(8,128)(2,1)S(1)} collective-permute-done((bf16[1,8,2,48,256]{4,3,2,1,0:T(8,128)(2,1)}, bf16[1,8,2,48,256]{4,3,2,1,0:T(8,128)(2,1)S(1)}, u32[]{:S(2)}, u32[]{:S(2)}) %collective-permute-start.13) | collective-permute-done | bytes 393248 | tf_op jit(solution)/shard_map/ppermute | solution.py:497
  76.4 0.7 copy-done.18
  77.1 1.0 add_bitcast_fusion
  78.2 3.0 %collective-permute-done.12.refs_1_ = bf16[2,8,2,48,256]{4,3,2,1,0:T(8,128)(2,1)S(1)} collective-permute-done((bf16[2,8,2,48,256]{4,3,2,1,0:T(8,128)(2,1)}, bf16[2,8,2,48,256]{4,3,2,1,0:T(8,128)(2,1)S(1)}, u32[]{:S(2)}, u32[]{:S(2)}) %collective-permute-start.12) | collective-permute-done | bytes 786464 | tf_op jit(solution)/shard_map/ppermute | solution.py:497
  81.2 3.0 %collective-permute-done.14.refs_4_ = bf16[1,8,2,48,256]{4,3,2,1,0:T(8,128)(2,1)S(1)} collective-permute-done((bf16[1,8,2,48,256]{4,3,2,1,0:T(8,128)(2,1)}, bf16[1,8,2,48,256]{4,3,2,1,0:T(8,128)(2,1)S(1)}, u32[]{:S(2)}, u32[]{:S(2)}) %collective-permute-start.14) | collective-permute-done | bytes 393248 | tf_op jit(solution)/shard_map/ppermute | solution.py:497
  84.2 0.6 collective-permute-start.16
  84.9 1.1 collective-permute-start.17
  85.9 9.2 %collective-permute-done.16.refs_2_ = bf16[8,2,48,256]{3,2,1,0:T(8,128)(2,1)S(1)} collective-permute-done((bf16[8,2,48,256]{3,2,1,0:T(8,128)(2,1)S(1)}, bf16[8,2,48,256]{3,2,1,0:T(8,128)(2,1)S(1)}, u32[]{:S(2)}, u32[]{:S(2)}) %collective-permute-start.16) | collective-permute-done | bytes 393248 | tf_op jit(solution)/shard_map/ppermute | solution.py:497
  95.2 0.3 collective-permute-done.17.refs_5_
  95.5 0.4 copy-done.14
  95.9 0.4 copy-done.15
  96.3 6.0 %adam_step.1 = (bf16[16,2,48,256]{3,2,1,0:T(8,128)(2,1)}, f32[16,2,48,256]{3,2,1,0:T(8,128)}, f32[16,2,48,256]{3,2,1,0:T(8,128)}) custom-call(s32[2]{0:T(128)} %pad_add_fusion.pos_ref, bf16[1,8,2,48,256]{4,3,2,1,0:T(8,128)(2,1)} %get-tuple-element.39.refs_0_, bf16[2,8,2,48,256]{4,3,2,1,0:T(8,128)(2,1)} %copy-done.4, bf16[8,2,48,256]{3,2,1,0:T(8,128)(2,1)} %copy-done.14, ...), custom_call_target="tpu_custom_call" | custom-call | tf_op jit(solution)/shard_map/adam_step/pallas_call | solution.py:358
  102.3 2.2 %collective-permute-start.19 = (bf16[16,2,48,256]{3,2,1,0:T(8,128)(2,1)}, bf16[16,2,48,256]{3,2,1,0:T(8,128)(2,1)S(1)}, u32[]{:S(2)}, u32[]{:S(2)}) collective-permute-start(bf16[16,2,48,256]{3,2,1,0:T(8,128)(2,1)} %get-tuple-element.52.refs_0_), channel_id=1, source_target_pairs={{0,8},{8,0},{16,24},{24,16},{1,9},{9,1},{17,25},{25,17},{2,10},{10... | collective-permute-start | bytes 2359304 | tf_op jit(solution)/shard_map/ppermute | solution.py:448
  104.5 2.4 %collective-permute-start.18 = (bf16[16,2,48,256]{3,2,1,0:T(8,128)(2,1)}, bf16[16,2,48,256]{3,2,1,0:T(8,128)(2,1)S(1)}, u32[]{:S(2)}, u32[]{:S(2)}) collective-permute-start(bf16[16,2,48,256]{3,2,1,0:T(8,128)(2,1)} %get-tuple-element.52.refs_0_), channel_id=1, source_target_pairs={{0,16},{8,24},{16,0},{24,8},{1,17},{9,25},{17,1},{25,9},{2,18},{10... | collective-permute-start | bytes 2359304 | tf_op jit(solution)/shard_map/ppermute | solution.py:447
  106.9 32.4 %collective-permute-done.19.refs_1_ = bf16[16,2,48,256]{3,2,1,0:T(8,128)(2,1)S(1)} collective-permute-done((bf16[16,2,48,256]{3,2,1,0:T(8,128)(2,1)}, bf16[16,2,48,256]{3,2,1,0:T(8,128)(2,1)S(1)}, u32[]{:S(2)}, u32[]{:S(2)}) %collective-permute-start.19) | collective-permute-done | bytes 786464 | tf_op jit(solution)/shard_map/ppermute | solution.py:448
  139.3 2.7 %collective-permute-done.18.refs_2_ = bf16[16,2,48,256]{3,2,1,0:T(8,128)(2,1)S(1)} collective-permute-done((bf16[16,2,48,256]{3,2,1,0:T(8,128)(2,1)}, bf16[16,2,48,256]{3,2,1,0:T(8,128)(2,1)S(1)}, u32[]{:S(2)}, u32[]{:S(2)}) %collective-permute-start.18) | collective-permute-done | bytes 786464 | tf_op jit(solution)/shard_map/ppermute | solution.py:447
  142.0 0.7 collective-permute-start.20
  142.7 1.3 collective-permute-start.21
  144.0 2.2 %finish_predicted.1 = bf16[256,384]{1,0:T(8,128)(2,1)} custom-call(bf16[256,256]{1,0:T(8,128)(2,1)} %get-tuple-element.30.perm_ref, bf16[4,256,384]{2,1,0:T(8,128)(2,1)} %copy-done.2), custom_call_target="tpu_custom_call" | custom-call | tf_op jit(solution)/shard_map/finish_predicted/pallas_call | solution.py:475
  146.2 3.5 %place_weights.2.refs_2_ = bf16[16,2,48,1024]{3,2,1,0:T(8,128)(2,1)} custom-call(s32[2]{0:T(128)} %pad_add_fusion.pos_ref, bf16[16,2,48,256]{3,2,1,0:T(8,128)(2,1)} %get-tuple-element.52.refs_0_, bf16[16,2,48,256]{3,2,1,0:T(8,128)(2,1)} %copy-done.9, bf16[16,2,48,256]{3,2,1,0:T(8,128)(2,1)} %copy-done.8), custom_call_target="tpu_custom_call" | custom-call | tf_op jit(solution)/shard_map/place_weights/pallas_call | solution.py:425
  149.7 13.2 %collective-permute-done.21.refs_1_ = bf16[16,2,48,256]{3,2,1,0:T(8,128)(2,1)S(1)} collective-permute-done((bf16[16,2,48,256]{3,2,1,0:T(8,128)(2,1)S(1)}, bf16[16,2,48,256]{3,2,1,0:T(8,128)(2,1)S(1)}, u32[]{:S(2)}, u32[]{:S(2)}) %collective-permute-start.21) | collective-permute-done | bytes 786464 | tf_op jit(solution)/shard_map/ppermute | solution.py:449
  162.9 2.5 %place_weights.3 = bf16[16,2,48,1024]{3,2,1,0:T(8,128)(2,1)} custom-call(s32[2]{0:T(128)S(1)} %copy-done, bf16[16,2,48,256]{3,2,1,0:T(8,128)(2,1)S(1)} %collective-permute-done.20.refs_0_, bf16[16,2,48,256]{3,2,1,0:T(8,128)(2,1)S(1)} %collective-permute-done.21.refs_1_, bf16[16,2,48,1024]{3,2,1,0:T(8,128)(2,1)} %place_weights.2.refs_2_), custom_call_target="tpu_custom_call", output_to_operand_aliasing={{}: (3, {})} | custom-call | tf_op jit(solution)/shard_map/place_weights/pallas_call | solution.py:425
  (57 shorter events, 0.6 us)
Async XLA Ops:
  1.8 2.5 %collective-permute-start = (bf16[8,2,48,256]{3,2,1,0:T(8,128)(2,1)S(1)}, bf16[8,2,48,256]{3,2,1,0:T(8,128)(2,1)S(1)}, u32[]{:S(2)}, u32[]{:S(2)}) collective-permute-start(bf16[8,2,48,256]{3,2,1,0:T(8,128)(2,1)S(1)} %get-tuple-element.57), channel_id=1, source_target_pairs={{0,1},{1,0},{2,3},{3,2},{4,5},{5,4},{6,7},{7,6},{8,9},{9,8},{10,11... | collective-permute-start | bytes 1179656 | tf_op jit(solution)/shard_map/ppermute | solution.py:497
  4.3 1.7 %copy-start.10 = (bf16[528,384]{1,0:T(8,128)(2,1)S(1)}, bf16[528,384]{1,0:T(8,128)(2,1)}, u32[]{:S(2)}) copy-start(bf16[528,384]{1,0:T(8,128)(2,1)} %get-tuple-element.34) | copy-start | bytes 1216516
  4.4 23.3 %copy-start.3 = (bf16[2,8,2,48,256]{4,3,2,1,0:T(8,128)(2,1)}, bf16[2,8,2,48,256]{4,3,2,1,0:T(8,128)(2,1)S(1)}, u32[]{:S(2)}) copy-start(bf16[2,8,2,48,256]{4,3,2,1,0:T(8,128)(2,1)S(1)} %pad_maximum_fusion.1.rest_4_) | copy-start | bytes 2359300
  4.4 23.2 %collective-permute-start.4 = (bf16[2,8,2,48,256]{4,3,2,1,0:T(8,128)(2,1)S(1)}, bf16[2,8,2,48,256]{4,3,2,1,0:T(8,128)(2,1)S(1)}, u32[]{:S(2)}, u32[]{:S(2)}) collective-permute-start(bf16[2,8,2,48,256]{4,3,2,1,0:T(8,128)(2,1)S(1)} %pad_maximum_fusion.1.rest_4_), channel_id=1, source_target_pairs={{0,4},{1,5},{2,6},{3,7},{4,0},{5,1},{6,2},{7,3},{8,12},{9,13},{10,... | collective-permute-start | bytes 2359304 | tf_op jit(solution)/shard_map/ppermute | solution.py:497
  6.0 21.2 %collective-permute-start.2 = (bf16[528,384]{1,0:T(8,128)(2,1)S(1)}, bf16[528,384]{1,0:T(8,128)(2,1)S(1)}, u32[]{:S(2)}, u32[]{:S(2)}) collective-permute-start(bf16[528,384]{1,0:T(8,128)(2,1)S(1)} %copy-done.10), channel_id=1, source_target_pairs={{0,16},{8,24},{16,0},{24,8},{1,17},{9,25},{17,1},{25,9},{2,18},{10... | collective-permute-start | bytes 1216520 | tf_op jit(solution)/shard_map/ppermute | solution.py:447
  8.6 18.8 %collective-permute-start.1 = (bf16[528,384]{1,0:T(8,128)(2,1)S(1)}, bf16[528,384]{1,0:T(8,128)(2,1)S(1)}, u32[]{:S(2)}, u32[]{:S(2)}) collective-permute-start(bf16[528,384]{1,0:T(8,128)(2,1)S(1)} %copy-done.10), channel_id=1, source_target_pairs={{0,8},{8,0},{16,24},{24,16},{1,9},{9,1},{17,25},{25,17},{2,10},{10... | collective-permute-start | bytes 1216520 | tf_op jit(solution)/shard_map/ppermute | solution.py:448
  10.2 19.1 %collective-permute-start.3 = (bf16[2,8,2,48,256]{4,3,2,1,0:T(8,128)(2,1)S(1)}, bf16[2,8,2,48,256]{4,3,2,1,0:T(8,128)(2,1)S(1)}, u32[]{:S(2)}, u32[]{:S(2)}) collective-permute-start(bf16[2,8,2,48,256]{4,3,2,1,0:T(8,128)(2,1)S(1)} %pad_maximum_fusion.1.rest_4_), channel_id=1, source_target_pairs={{0,2},{1,3},{2,0},{3,1},{4,6},{5,7},{6,4},{7,5},{8,10},{9,11},{10,... | collective-permute-start | bytes 2359304 | tf_op jit(solution)/shard_map/ppermute | solution.py:497
  27.5 17.3 %copy-start.1 = (bf16[3,528,384]{2,1,0:T(8,128)(2,1)}, bf16[3,528,384]{2,1,0:T(8,128)(2,1)S(1)}, u32[]{:S(2)}) copy-start(bf16[3,528,384]{2,1,0:T(8,128)(2,1)S(1)} %pad_maximum_fusion.rest_0_) | copy-start | bytes 3649540
  27.6 15.5 %copy-start.20 = (s32[32,4]{0,1:T(4,128)S(1)}, s32[32,4]{0,1:T(4,128)}, u32[]{:S(2)}) copy-start(s32[32,4]{0,1:T(4,128)} %param.11) | copy-start | bytes 1540
  27.6 17.2 %collective-permute-start.7 = (bf16[3,528,384]{2,1,0:T(8,128)(2,1)S(1)}, bf16[3,528,384]{2,1,0:T(8,128)(2,1)}, u32[]{:S(2)}, u32[]{:S(2)}) collective-permute-start(bf16[3,528,384]{2,1,0:T(8,128)(2,1)S(1)} %pad_maximum_fusion.rest_0_), channel_id=1, source_target_pairs={{0,1},{1,0},{2,3},{3,2},{4,5},{5,4},{6,7},{7,6},{8,9},{9,8},{10,11... | collective-permute-start | bytes 3649544 | tf_op jit(solution)/shard_map/ppermute | solution.py:497
  27.7 17.2 %copy-start.5 = (bf16[2,8,2,48,256]{4,3,2,1,0:T(8,128)(2,1)}, bf16[2,8,2,48,256]{4,3,2,1,0:T(8,128)(2,1)S(1)}, u32[]{:S(2)}) copy-start(bf16[2,8,2,48,256]{4,3,2,1,0:T(8,128)(2,1)S(1)} %collective-permute-done.4.rest_6_) | copy-start | bytes 2359300
  27.7 15.3 %collective-permute-start.9 = (bf16[8,2,48,256]{3,2,1,0:T(8,128)(2,1)S(1)}, bf16[8,2,48,256]{3,2,1,0:T(8,128)(2,1)S(1)}, u32[]{:S(2)}, u32[]{:S(2)}) collective-permute-start(bf16[8,2,48,256]{3,2,1,0:T(8,128)(2,1)S(1)} %slice_bitcast_fusion), channel_id=1, source_target_pairs={{0,2},{1,3},{2,0},{3,1},{4,6},{5,7},{6,4},{7,5},{8,10},{9,11},{10,... | collective-permute-start | bytes 1179656 | tf_op jit(solution)/shard_map/ppermute | solution.py:497
  29.3 2.0 %copy-start.6 = (bf16[2,8,2,48,256]{4,3,2,1,0:T(8,128)(2,1)}, bf16[2,8,2,48,256]{4,3,2,1,0:T(8,128)(2,1)S(1)}, u32[]{:S(2)}) copy-start(bf16[2,8,2,48,256]{4,3,2,1,0:T(8,128)(2,1)S(1)} %collective-permute-done.3.rest_5_) | copy-start | bytes 2359300
  29.3 3.3 %collective-permute-start.5 = (bf16[528,384]{1,0:T(8,128)(2,1)S(1)}, bf16[528,384]{1,0:T(8,128)(2,1)S(1)}, u32[]{:S(2)}, u32[]{:S(2)}) collective-permute-start(bf16[528,384]{1,0:T(8,128)(2,1)S(1)} %copy-done.10), channel_id=1, source_target_pairs={{8,16},{16,8},{9,17},{17,9},{10,18},{18,10},{11,19},{19,11},{12,20... | collective-permute-start | bytes 1216520 | tf_op jit(solution)/shard_map/ppermute | solution.py:450
  29.9 12.9 %collective-permute-start.6 = (bf16[528,384]{1,0:T(8,128)(2,1)S(1)}, bf16[528,384]{1,0:T(8,128)(2,1)S(1)}, u32[]{:S(2)}, u32[]{:S(2)}) collective-permute-start(bf16[528,384]{1,0:T(8,128)(2,1)S(1)} %collective-permute-done.2), channel_id=1, source_target_pairs={{16,24},{8,0},{17,25},{9,1},{18,26},{10,2},{19,27},{11,3},{20,28},... | collective-permute-start | bytes 1216520 | tf_op jit(solution)/shard_map/ppermute | solution.py:449
  31.3 11.7 %collective-permute-start.8 = (bf16[8,2,48,256]{3,2,1,0:T(8,128)(2,1)S(1)}, bf16[8,2,48,256]{3,2,1,0:T(8,128)(2,1)}, u32[]{:S(2)}, u32[]{:S(2)}) collective-permute-start(bf16[8,2,48,256]{3,2,1,0:T(8,128)(2,1)S(1)} %slice_bitcast_fusion.1), channel_id=1, source_target_pairs={{0,4},{1,5},{2,6},{3,7},{4,0},{5,1},{6,2},{7,3},{8,12},{9,13},{10,... | collective-permute-start | bytes 1179656 | tf_op jit(solution)/shard_map/ppermute | solution.py:497
  43.0 1.9 %copy-start.7 = (bf16[528,384]{1,0:T(8,128)(2,1)}, bf16[528,384]{1,0:T(8,128)(2,1)S(1)}, u32[]{:S(2)}) copy-start(bf16[528,384]{1,0:T(8,128)(2,1)S(1)} %add.31.rest_1_) | copy-start | bytes 1216516
  43.0 1.9 %copy-start.19 = (bf16[8,2,48,256]{3,2,1,0:T(8,128)(2,1)}, bf16[8,2,48,256]{3,2,1,0:T(8,128)(2,1)S(1)}, u32[]{:S(2)}) copy-start(bf16[8,2,48,256]{3,2,1,0:T(8,128)(2,1)S(1)} %collective-permute-done.9.rest_8_) | copy-start | bytes 1179652
  43.0 1.8 %collective-permute-start.10 = (bf16[528,384]{1,0:T(8,128)(2,1)S(1)}, bf16[528,384]{1,0:T(8,128)(2,1)S(1)}, u32[]{:S(2)}, u32[]{:S(2)}) collective-permute-start(bf16[528,384]{1,0:T(8,128)(2,1)S(1)} %add.31.rest_1_), channel_id=1, source_target_pairs={{0,1},{1,0},{2,3},{3,2},{4,5},{5,4},{6,7},{7,6},{8,9},{9,8},{10,11... | collective-permute-start | bytes 1216520 | tf_op jit(solution)/shard_map/ppermute | solution.py:497
  44.8 0.8 copy-start.11
  60.9 5.6 %collective-permute-start.11 = (bf16[4,256,384]{2,1,0:T(8,128)(2,1)}, bf16[4,256,384]{2,1,0:T(8,128)(2,1)S(1)}, u32[]{:S(2)}, u32[]{:S(2)}) collective-permute-start(bf16[4,256,384]{2,1,0:T(8,128)(2,1)} %get-tuple-element.38), channel_id=1, source_target_pairs={{0,1},{1,0},{2,3},{3,2},{4,5},{5,4},{6,7},{7,6},{8,9},{9,8},{10,11... | collective-permute-start | bytes 2359304 | tf_op jit(solution)/shard_map/ppermute | solution.py:497
  61.0 20.2 %collective-permute-start.12 = (bf16[2,8,2,48,256]{4,3,2,1,0:T(8,128)(2,1)}, bf16[2,8,2,48,256]{4,3,2,1,0:T(8,128)(2,1)S(1)}, u32[]{:S(2)}, u32[]{:S(2)}) collective-permute-start(bf16[2,8,2,48,256]{4,3,2,1,0:T(8,128)(2,1)} %get-tuple-element.40), channel_id=1, source_target_pairs={{0,2},{1,3},{2,0},{3,1},{4,6},{5,7},{6,4},{7,5},{8,10},{9,11},{10,... | collective-permute-start | bytes 2359304 | tf_op jit(solution)/shard_map/ppermute | solution.py:497
  62.6 13.8 %collective-permute-start.13 = (bf16[1,8,2,48,256]{4,3,2,1,0:T(8,128)(2,1)}, bf16[1,8,2,48,256]{4,3,2,1,0:T(8,128)(2,1)S(1)}, u32[]{:S(2)}, u32[]{:S(2)}) collective-permute-start(bf16[1,8,2,48,256]{4,3,2,1,0:T(8,128)(2,1)} %get-tuple-element.42), channel_id=1, source_target_pairs={{0,4},{1,5},{2,6},{3,7},{4,0},{5,1},{6,2},{7,3},{8,12},{9,13},{10,... | collective-permute-start | bytes 1179656 | tf_op jit(solution)/shard_map/ppermute | solution.py:497
  66.5 10.6 %copy-start.17 = (bf16[1,8,2,48,256]{4,3,2,1,0:T(8,128)(2,1)S(1)}, bf16[1,8,2,48,256]{4,3,2,1,0:T(8,128)(2,1)}, u32[]{:S(2)}) copy-start(bf16[1,8,2,48,256]{4,3,2,1,0:T(8,128)(2,1)} %get-tuple-element.49) | copy-start | bytes 1179652
  68.8 12.4 %copy-start.16 = (bf16[1,8,2,48,256]{4,3,2,1,0:T(8,128)(2,1)S(1)}, bf16[1,8,2,48,256]{4,3,2,1,0:T(8,128)(2,1)}, u32[]{:S(2)}) copy-start(bf16[1,8,2,48,256]{4,3,2,1,0:T(8,128)(2,1)} %get-tuple-element.41) | copy-start | bytes 1179652
  68.8 26.4 %all-to-all-start = ((bf16[4,256,384]{2,1,0:T(8,128)(2,1)}), bf16[4,256,384]{2,1,0:T(8,128)(2,1)S(1)}, u32[]{:S(2)}, u32[]{:S(2)}) async-start(bf16[4,256,384]{2,1,0:T(8,128)(2,1)} %add.32), calls=%async_computation | async-start | bytes 1572864 | tf_op jit(solution)/shard_map/all_to_all | solution.py:534
  72.9 11.3 %collective-permute-start.14 = (bf16[1,8,2,48,256]{4,3,2,1,0:T(8,128)(2,1)}, bf16[1,8,2,48,256]{4,3,2,1,0:T(8,128)(2,1)S(1)}, u32[]{:S(2)}, u32[]{:S(2)}) collective-permute-start(bf16[1,8,2,48,256]{4,3,2,1,0:T(8,128)(2,1)} %get-tuple-element.44), channel_id=1, source_target_pairs={{0,5},{1,4},{2,7},{3,6},{4,1},{5,0},{6,3},{7,2},{8,13},{9,12},{10,... | collective-permute-start | bytes 1179656 | tf_op jit(solution)/shard_map/ppermute | solution.py:497
  72.9 11.3 %collective-permute-start.15 = (bf16[1,8,2,48,256]{4,3,2,1,0:T(8,128)(2,1)}, bf16[1,8,2,48,256]{4,3,2,1,0:T(8,128)(2,1)S(1)}, u32[]{:S(2)}, u32[]{:S(2)}) collective-permute-start(bf16[1,8,2,48,256]{4,3,2,1,0:T(8,128)(2,1)} %get-tuple-element.46), channel_id=1, source_target_pairs={{0,1},{1,0},{2,3},{3,2},{4,5},{5,4},{6,7},{7,6},{8,9},{9,8},{10,11... | collective-permute-start | bytes 1179656 | tf_op jit(solution)/shard_map/ppermute | solution.py:497
  76.4 0.7 copy-start.18
  81.2 14.3 %copy-start.4 = (bf16[2,8,2,48,256]{4,3,2,1,0:T(8,128)(2,1)}, bf16[2,8,2,48,256]{4,3,2,1,0:T(8,128)(2,1)S(1)}, u32[]{:S(2)}) copy-start(bf16[2,8,2,48,256]{4,3,2,1,0:T(8,128)(2,1)S(1)} %collective-permute-done.12.refs_1_) | copy-start | bytes 2359300
  84.2 11.2 %copy-start.12 = (bf16[1,8,2,48,256]{4,3,2,1,0:T(8,128)(2,1)}, bf16[1,8,2,48,256]{4,3,2,1,0:T(8,128)(2,1)S(1)}, u32[]{:S(2)}) copy-start(bf16[1,8,2,48,256]{4,3,2,1,0:T(8,128)(2,1)S(1)} %collective-permute-done.14.refs_4_) | copy-start | bytes 1179652
  84.2 11.2 %copy-start.13 = (bf16[1,8,2,48,256]{4,3,2,1,0:T(8,128)(2,1)}, bf16[1,8,2,48,256]{4,3,2,1,0:T(8,128)(2,1)S(1)}, u32[]{:S(2)}) copy-start(bf16[1,8,2,48,256]{4,3,2,1,0:T(8,128)(2,1)S(1)} %collective-permute-done.15.refs_3_) | copy-start | bytes 1179652
  84.2 10.9 %collective-permute-start.16 = (bf16[8,2,48,256]{3,2,1,0:T(8,128)(2,1)S(1)}, bf16[8,2,48,256]{3,2,1,0:T(8,128)(2,1)S(1)}, u32[]{:S(2)}, u32[]{:S(2)}) collective-permute-start(bf16[8,2,48,256]{3,2,1,0:T(8,128)(2,1)S(1)} %fusion), channel_id=1, source_target_pairs={{0,4},{1,5},{2,6},{3,7},{4,0},{5,1},{6,2},{7,3},{8,12},{9,13},{10,... | collective-permute-start | bytes 1179656 | tf_op jit(solution)/shard_map/ppermute | solution.py:497
  84.9 10.6 %collective-permute-start.17 = (bf16[8,2,48,256]{3,2,1,0:T(8,128)(2,1)S(1)}, bf16[8,2,48,256]{3,2,1,0:T(8,128)(2,1)S(1)}, u32[]{:S(2)}, u32[]{:S(2)}) collective-permute-start(bf16[8,2,48,256]{3,2,1,0:T(8,128)(2,1)S(1)} %add_bitcast_fusion), channel_id=1, source_target_pairs={{0,3},{1,2},{2,1},{3,0},{4,7},{5,6},{6,5},{7,4},{8,11},{9,10},{10,... | collective-permute-start | bytes 1179656 | tf_op jit(solution)/shard_map/ppermute | solution.py:497
  95.1 0.7 copy-start.14
  95.2 7.1 %copy-start.2 = (bf16[4,256,384]{2,1,0:T(8,128)(2,1)}, bf16[4,256,384]{2,1,0:T(8,128)(2,1)S(1)}, u32[]{:S(2)}) copy-start(bf16[4,256,384]{2,1,0:T(8,128)(2,1)S(1)} %all-to-all-done.parts_ref) | copy-start | bytes 2359300
  95.4 0.8 copy-start.15
  102.3 37.0 %collective-permute-start.19 = (bf16[16,2,48,256]{3,2,1,0:T(8,128)(2,1)}, bf16[16,2,48,256]{3,2,1,0:T(8,128)(2,1)S(1)}, u32[]{:S(2)}, u32[]{:S(2)}) collective-permute-start(bf16[16,2,48,256]{3,2,1,0:T(8,128)(2,1)} %get-tuple-element.52.refs_0_), channel_id=1, source_target_pairs={{0,8},{8,0},{16,24},{24,16},{1,9},{9,1},{17,25},{25,17},{2,10},{10... | collective-permute-start | bytes 2359304 | tf_op jit(solution)/shard_map/ppermute | solution.py:448
  104.5 37.5 %collective-permute-start.18 = (bf16[16,2,48,256]{3,2,1,0:T(8,128)(2,1)}, bf16[16,2,48,256]{3,2,1,0:T(8,128)(2,1)S(1)}, u32[]{:S(2)}, u32[]{:S(2)}) collective-permute-start(bf16[16,2,48,256]{3,2,1,0:T(8,128)(2,1)} %get-tuple-element.52.refs_0_), channel_id=1, source_target_pairs={{0,16},{8,24},{16,0},{24,8},{1,17},{9,25},{17,1},{25,9},{2,18},{10... | collective-permute-start | bytes 2359304 | tf_op jit(solution)/shard_map/ppermute | solution.py:447
  139.3 6.9 %copy-start.9 = (bf16[16,2,48,256]{3,2,1,0:T(8,128)(2,1)}, bf16[16,2,48,256]{3,2,1,0:T(8,128)(2,1)S(1)}, u32[]{:S(2)}) copy-start(bf16[16,2,48,256]{3,2,1,0:T(8,128)(2,1)S(1)} %collective-permute-done.19.refs_1_) | copy-start | bytes 2359300
  142.0 4.2 %copy-start.8 = (bf16[16,2,48,256]{3,2,1,0:T(8,128)(2,1)}, bf16[16,2,48,256]{3,2,1,0:T(8,128)(2,1)S(1)}, u32[]{:S(2)}) copy-start(bf16[16,2,48,256]{3,2,1,0:T(8,128)(2,1)S(1)} %collective-permute-done.18.refs_2_) | copy-start | bytes 2359300
  142.0 7.7 %collective-permute-start.20 = (bf16[16,2,48,256]{3,2,1,0:T(8,128)(2,1)}, bf16[16,2,48,256]{3,2,1,0:T(8,128)(2,1)S(1)}, u32[]{:S(2)}, u32[]{:S(2)}) collective-permute-start(bf16[16,2,48,256]{3,2,1,0:T(8,128)(2,1)} %get-tuple-element.52.refs_0_), channel_id=1, source_target_pairs={{8,16},{16,8},{9,17},{17,9},{10,18},{18,10},{11,19},{19,11},{12,20... | collective-permute-start | bytes 2359304 | tf_op jit(solution)/shard_map/ppermute | solution.py:450
  142.7 20.2 %collective-permute-start.21 = (bf16[16,2,48,256]{3,2,1,0:T(8,128)(2,1)S(1)}, bf16[16,2,48,256]{3,2,1,0:T(8,128)(2,1)S(1)}, u32[]{:S(2)}, u32[]{:S(2)}) collective-permute-start(bf16[16,2,48,256]{3,2,1,0:T(8,128)(2,1)S(1)} %collective-permute-done.18.refs_2_), channel_id=1, source_target_pairs={{16,24},{8,0},{17,25},{9,1},{18,26},{10,2},{19,27},{11,3},{20,28},... | collective-permute-start | bytes 2359304 | tf_op jit(solution)/shard_map/ppermute | solution.py:449
  146.2 16.7 %copy-start = (s32[2]{0:T(128)S(1)}, s32[2]{0:T(128)}, u32[]{:S(2)}) copy-start(s32[2]{0:T(128)} %pad_add_fusion.pos_ref) | copy-start | bytes 28

commit v15 on v14

--- a/solution.py
+++ b/solution.py
@@ -10,7 +10,8 @@
 SITES = 384
 CAP = 128
 ID_ROWS = 16
-PARTS = 4
+CHUNKS = 2
+PARTS = 2
 VMEM_BYTES = 56 * 2**20
 LAST_VMEM_BYTES = 8 * 2**20
 
@@ -277,12 +278,14 @@
     return found[0], found[1], grads
 
 
-def adam(pos, terms, weights, moment1, moment2):
+def adam(pos, terms, weights, moment1, moment2, chunk, before):
     number, _, piece, width = moment1.shape
     half = number // 2
     flat = [one if isinstance(one, tuple) else (one, None) for group in terms for one in group]
     arrays = [array for array, _ in flat]
     per = len(terms[0])
+    size = half // CHUNKS
+    held = (2, size, 2, piece, width)
     correct_one = 1.0 - 0.9**10
     correct_two = 1.0 - 0.999**10
 
@@ -291,19 +294,20 @@
             ref if at is None else ref.at[at] for ref, (_, at) in zip(refs, flat)
         ]
         w_ref, m1_ref, m2_ref = refs[len(flat) : len(flat) + 3]
-        refs = refs[len(flat) + 3 :]
+        refs = refs[len(flat) + 3 + len(before) :]
         new_w, new_m1, new_m2, grads, w_in, m1_in, m2_in, w_out, m1_out, m2_out = refs[:10]
         sem_in, sem_out = refs[10:]
         columns = pl.ds(pl.multiple_of(pos_ref[0] * width, 128), width)
-        part = half // PARTS
+        part = size // PARTS
         steps = [(g, i * part) for g in range(2) for i in range(PARTS)]
         own_core = lax.rem(pos_ref[1], 2)
         copies = []
         for n, (g, first) in enumerate(steps):
-            rows = pl.ds((own_core ^ g) * half + first, part)
+            rows = pl.ds((own_core ^ g) * half + chunk * size + first, part)
+            local = pl.ds(first, part)
             copies.append(
                 [
-                    pltpu.make_async_copy(ref, into.at[rows], sem_in.at[n, i])
+                    pltpu.make_async_copy(ref, into.at[g, local], sem_in.at[n, i])
                     for i, (ref, into) in enumerate(
                         (
                             (w_ref.at[rows, :, :, columns], w_in),
@@ -314,8 +318,8 @@
                 ]
                 + [
                     pltpu.make_async_copy(
-                        term_refs[g * per + i].at[pl.ds(first, part)],
-                        grads.at[g * per + i, pl.ds(first, part)],
+                        term_refs[g * per + i].at[pl.ds(chunk * size + first, part)],
+                        grads.at[g * per + i, local],
                         sem_in.at[n, 3 + i],
                     )
                     for i in range(per)
@@ -329,27 +333,33 @@
                 copy.wait()
 
             def step(i, _, g=g, first=first):
-                gradient = grads[g * per, first + i].astype(jnp.float32)
+                at = first + i
+                gradient = grads[g * per, at].astype(jnp.float32)
                 for j in range(1, per):
-                    gradient = gradient + grads[g * per + j, first + i].astype(jnp.float32)
-                at = (own_core ^ g) * half + first + i
-                one = 0.9 * m1_in[at] + 0.1 * gradient
-                two = 0.999 * m2_in[at] + 0.001 * gradient * gradient
-                m1_out[at] = one
-                m2_out[at] = two
+                    gradient = gradient + grads[g * per + j, at].astype(jnp.float32)
+                one = 0.9 * m1_in[g, at] + 0.1 * gradient
+                two = 0.999 * m2_in[g, at] + 0.001 * gradient * gradient
+                m1_out[g, at] = one
+                m2_out[g, at] = two
                 spread = two * (1.0 / correct_two)
-                updated = w_in[at].astype(jnp.float32) - one * (learn_rate / correct_one) / (
+                updated = w_in[g, at].astype(jnp.float32) - one * (learn_rate / correct_one) / (
                     spread * lax.rsqrt(spread) + 1e-08
                 )
-                w_out[at] = updated.astype(jnp.bfloat16)
+                w_out[g, at] = updated.astype(jnp.bfloat16)
                 return 0
 
             lax.fori_loop(0, part, step, 0)
-            rows = pl.ds((own_core ^ g) * half + first, part)
-            for i, (held, ref) in enumerate(
-                ((w_out, new_w), (m1_out, new_m1), (m2_out, new_m2))
+            half_at = own_core ^ g
+            local = pl.ds(first, part)
+            rows = pl.ds(half_at * half + chunk * size + first, part)
+            for i, (source, ref) in enumerate(
+                (
+                    (w_out, new_w.at[pl.ds(half_at * size + first, part)]),
+                    (m1_out, new_m1.at[rows]),
+                    (m2_out, new_m2.at[rows]),
+                )
             ):
-                outs.append(pltpu.make_async_copy(held.at[rows], ref.at[rows], sem_out.at[n, i]))
+                outs.append(pltpu.make_async_copy(source.at[g, local], ref, sem_out.at[n, i]))
                 outs[-1].start()
         for copy in outs:
             copy.wait()
@@ -358,29 +368,30 @@
     return pl.pallas_call(
         body,
         out_shape=[
-            jax.ShapeDtypeStruct(moment1.shape, jnp.bfloat16),
+            jax.ShapeDtypeStruct((2 * size, 2, piece, width), jnp.bfloat16),
             jax.ShapeDtypeStruct(moment1.shape, jnp.float32),
             jax.ShapeDtypeStruct(moment1.shape, jnp.float32),
         ],
-        in_specs=[smem()] + [anywhere] * (len(flat) + 3),
+        in_specs=[smem()] + [anywhere] * (len(flat) + 3 + len(before)),
         out_specs=[anywhere] * 3,
-        scratch_shapes=[pltpu.VMEM((len(flat), half, 2, piece, width), jnp.bfloat16)]
-        + [pltpu.VMEM(moment1.shape, kind) for kind in (jnp.bfloat16, jnp.float32, jnp.float32)] * 2
+        scratch_shapes=[pltpu.VMEM((len(flat), size, 2, piece, width), jnp.bfloat16)]
+        + [pltpu.VMEM(held, kind) for kind in (jnp.bfloat16, jnp.float32, jnp.float32)] * 2
         + [
             pltpu.SemaphoreType.DMA((2 * PARTS, 3 + per)),
             pltpu.SemaphoreType.DMA((2 * PARTS, 3)),
         ],
+        input_output_aliases={1 + len(flat) + 3 + i: 1 + i for i in range(len(before))},
         compiler_params=params(),
         name="adam_step",
-    )(pos, *arrays, weights, moment1, moment2)
-
-
-def place_weights(pos, pieces, shape, before):
+    )(pos, *arrays, weights, moment1, moment2, *before)
+
+
+def place_weights(pos, pieces, shape, chunk, before):
     flat = [(plane, one if isinstance(one, tuple) else (one,)) for plane, one in pieces]
     arrays = [one for _, group in flat for one in group]
     number, _, _, width = arrays[0].shape
     n_dp = shape[3] // width
-    part = number // PARTS
+    part = number // 2
 
     def body(pos_ref, *refs):
         ins = refs[: len(arrays)]
@@ -403,17 +414,18 @@
                     pl.when(inner)(lambda made=made: act(made[0]))
                     pl.when(~inner)(lambda made=made: act(made[1]))
 
-        for i in range(PARTS):
+        for i in range(2):
             into(lambda copy: copy.start(), i)
         outs = []
-        for i in range(PARTS):
+        for i in range(2):
             into(lambda copy: copy.wait(), i)
             rows = pl.ds(i * part, part)
+            to = pl.ds((i * CHUNKS + chunk) * part, part)
             for n, (plane, _) in enumerate(flat):
                 columns = pl.ds(pl.multiple_of((dp_at ^ plane) * width, 128), width)
                 outs.append(
                     pltpu.make_async_copy(
-                        held.at[n, rows], out_ref.at[rows, :, :, columns], sem_out.at[i, n]
+                        held.at[n, rows], out_ref.at[to, :, :, columns], sem_out.at[i, n]
                     )
                 )
                 outs[-1].start()
@@ -429,11 +441,11 @@
         out_specs=anywhere,
         scratch_shapes=[
             pltpu.VMEM(held, jnp.bfloat16),
-            pltpu.SemaphoreType.DMA((PARTS, len(flat))),
-            pltpu.SemaphoreType.DMA((PARTS, len(flat))),
+            pltpu.SemaphoreType.DMA((2, len(flat))),
+            pltpu.SemaphoreType.DMA((2, len(flat))),
         ],
         input_output_aliases={1 + len(arrays): 0} if before else {},
-        compiler_params=params(LAST_VMEM_BYTES if before else VMEM_BYTES),
+        compiler_params=params(LAST_VMEM_BYTES if len(flat) == 1 else VMEM_BYTES),
         name="place_weights",
     )(pos, *arrays, *before)
 
@@ -451,11 +463,12 @@
     return [value, one, two, (middle, outer)]
 
 
-def gather_weights(pos, fresh, dp_at, n_dp):
-    shape = fresh.shape[:3] + (n_dp * fresh.shape[3],)
-    pieces = list(enumerate(between_planes(fresh, dp_at, n_dp)))
-    most = place_weights(pos, pieces[:-1], shape, [])
-    return place_weights(pos, pieces[-1:], shape, [most])
+def gather_weights(pos, fresh, dp_at, n_dp, chunk, before, moving):
+    number, _, piece, width = fresh.shape
+    shape = (CHUNKS * number, 2, piece, n_dp * width)
+    pieces = between_planes(fresh, dp_at, n_dp, (), jax.tree.leaves(moving[3:]))
+    most = place_weights(pos, list(enumerate(pieces))[:-1], shape, chunk, before)
+    return [place_weights(pos, [(n_dp - 1, pieces[-1])], shape, chunk, [most])], pieces
 
 
 def after(value, *others):
@@ -552,8 +565,17 @@
     predicted = finish_predicted(perm, parts)
     terms[0][-1] = after(terms[0][-1], parts)
 
-    fresh, new_moment1, new_moment2 = adam(pos, terms, weights, moment1, moment2)
-    new_weights = gather_weights(pos, fresh, dp_at, n_dp)
+    moments = []
+    new_weights = []
+    pieces = []
+    for chunk in range(CHUNKS):
+        terms[0][-1] = after(terms[0][-1], *pieces[1:2])
+        fresh, *moments = adam(pos, terms, weights, moment1, moment2, chunk, moments)
+        new_weights, pieces = gather_weights(
+            pos, fresh, dp_at, n_dp, chunk, new_weights, pieces
+        )
+    new_weights = new_weights[0]
+    new_moment1, new_moment2 = moments
 
     return (predicted, new_weights, new_moment1, new_moment2)
 

time: 168 us -> 178 us (1.060)
  starting transfers between devices: 28.4 us -> 34.7 us
  Pallas kernels: 31.9 us -> 34.8 us
    ppermute x14, waiting for transfers between devices: 20.1 us -> 28.4 us  [across(): return lax.ppermute(value, 'own', [(o, o ^ j) for o in range(n_own)])]
    ppermute x2 -> x3, waiting for transfers between devices: 23.5 us -> 18.4 us  [between_planes(): outer = lax.ppermute(after(two, one, *second), 'dp', [(2, 3), (1, 0)])]
    pallas_call x2 -> x4, Pallas kernels: 5.98 us -> 9.69 us  [place_weights(): pl.pallas_call(body, out_shape=jax.ShapeDtypeStruct(shape, jnp.bfloat16),...]
    pallas_call x1, Pallas kernels: 15.3 us -> 12.6 us  [local_grads(): pl.pallas_call(body, out_shape=[pred_shape, pred_shape] + grad_shapes, in...]
    ppermute x2 -> x3, waiting for transfers between devices: 19.1 us -> 16.5 us  [between_planes(): two = lax.ppermute(value, 'dp', [(0, 2), (1, 3), (2, 0), (3, 1)])]
    ppermute x14, starting transfers between devices: 11.6 us -> 13.8 us  [across(): return lax.ppermute(value, 'own', [(o, o ^ j) for o in range(n_own)])]
    pallas_call x1 -> x2, Pallas kernels: 6 us -> 7.82 us  [adam(): pl.pallas_call(body, out_shape=[jax.ShapeDtypeStruct((2 * size, 2, piece,...]
    ppermute x2 -> x3, starting transfers between devices: 3.79 us -> 5.4 us  [between_planes(): lax.ppermute(after(value, *first), 'dp', [(0, 1), (1, 0), (2, 3), (3, 2)])]
  transfers between devices with their start and end apart: 23 -> 27, of which waited for: 13 -> 14; matrix products, arithmetic and copies ran while one was open for 3% -> 2% of each run, Pallas kernels for 5% -> 9%
where the time goes in v15:
time: 178 us; the launch traced here: 175 us
  waiting for transfers between devices  95.9 us (54%)
  Pallas kernels  34.8 us (20%)
  starting transfers between devices  34.7 us (19%)
  local copies, waits for them, and re-layouts  5.12 us (3%)
  other arithmetic  3.36 us (2%)
    ppermute x3, waiting for transfers between devices, between_planes(): lax.ppermute(after(value, *first), 'dp', [(0, 1), (1, 0), (2, 3), (3, 2)])  32.6 us
    ppermute x14, waiting for transfers between devices, across(): return lax.ppermute(value, 'own', [(o, o ^ j) for o in range(n_own)])  28.4 us
    ppermute x3, waiting for transfers between devices, between_planes(): outer = lax.ppermute(after(two, one, *second), 'dp', [(2, 3), (1, 0)])  18.4 us
    ppermute x3, waiting for transfers between devices, between_planes(): two = lax.ppermute(value, 'dp', [(0, 2), (1, 3), (2, 0), (3, 1)])  16.5 us
    ppermute x14, starting transfers between devices, across(): return lax.ppermute(value, 'own', [(o, o ^ j) for o in range(n_own)])  13.8 us
    pallas_call x1, Pallas kernels, local_grads(): pl.pallas_call(body, out_shape=[pred_shape, pred_shape] + grad_shapes, in...  12.6 us
    pallas_call x4, Pallas kernels, place_weights(): pl.pallas_call(body, out_shape=jax.ShapeDtypeStruct(shape, jnp.bfloat16),...  9.69 us
    pallas_call x2, Pallas kernels, adam(): pl.pallas_call(body, out_shape=[jax.ShapeDtypeStruct((2 * size, 2, piece,...  7.82 us
  transfers between devices with their start and end apart: 27, of which 14 were waited for; matrix products, arithmetic and copies ran while one was open for 2% of the time, Pallas kernels for 9%

profile of v15, /device:TPU:2, one launch (start us, length us, event | category | flops | bytes accessed | tf_op | source)
XLA Modules:
  0.0 174.9 jit_solution(18076794256477397324)
XLA Ops:
  0.6 1.2 dynamic-slice_bitcast_fusion
  1.9 2.4 %pack_rows.1 = (bf16[528,384]{1,0:T(8,128)(2,1)}, bf16[256,256]{1,0:T(8,128)(2,1)}) custom-call(s32[1,256]{1,0:T(1,128)} %bitcast.21, bf16[256,384]{1,0:T(8,128)(2,1)} %sig_ref.1, bf16[256,384]{1,0:T(8,128)(2,1)} %cot_ref.1), custom_call_target="tpu_custom_call" | custom-call | tf_op jit(solution)/shard_map/pack_rows/pallas_call | solution.py:81
  4.4 1.6 collective-permute-start.4
  6.0 2.6 %collective-permute-start.2 = (bf16[528,384]{1,0:T(8,128)(2,1)S(1)}, bf16[528,384]{1,0:T(8,128)(2,1)S(1)}, u32[]{:S(2)}, u32[]{:S(2)}) collective-permute-start(bf16[528,384]{1,0:T(8,128)(2,1)S(1)} %copy-done.13), channel_id=1, source_target_pairs={{0,16},{8,24},{16,0},{24,8},{1,17},{9,25},{17,1},{25,9},{2,18},{10... | collective-permute-start | bytes 1216520 | tf_op jit(solution)/shard_map/ppermute | solution.py:459
  8.6 1.6 collective-permute-start.1
  10.7 16.5 %collective-permute-done.2 = bf16[528,384]{1,0:T(8,128)(2,1)S(1)} collective-permute-done((bf16[528,384]{1,0:T(8,128)(2,1)S(1)}, bf16[528,384]{1,0:T(8,128)(2,1)S(1)}, u32[]{:S(2)}, u32[]{:S(2)}) %collective-permute-start.2) | collective-permute-done | bytes 405536 | tf_op jit(solution)/shard_map/ppermute | solution.py:459
  28.3 0.9 collective-permute-done.3.rest_5_
  29.3 0.7 collective-permute-start.5
  29.9 1.3 collective-permute-start.6
  31.3 1.2 collective-permute-start.8
  32.5 10.3 %collective-permute-done.6 = bf16[528,384]{1,0:T(8,128)(2,1)S(1)} collective-permute-done((bf16[528,384]{1,0:T(8,128)(2,1)S(1)}, bf16[528,384]{1,0:T(8,128)(2,1)S(1)}, u32[]{:S(2)}, u32[]{:S(2)}) %collective-permute-start.6) | collective-permute-done | bytes 405536 | tf_op jit(solution)/shard_map/ppermute | solution.py:461
  43.0 0.8 copy-done.20
  43.8 0.8 copy-done.22
  44.5 0.7 copy.17.touched_ref
  45.2 0.6 pad_add_fusion.pos_ref
  46.3 0.7 copy-done.14
  47.0 12.6 %local_grads.1 = (bf16[4,256,384]{2,1,0:T(8,128)(2,1)}, bf16[4,256,384]{2,1,0:T(8,128)(2,1)}, bf16[2,8,2,48,256]{4,3,2,1,0:T(8,128)(2,1)}, bf16[1,8,2,48,256]{4,...) custom-call(s32[2]{0:T(128)} %pad_add_fusion.pos_ref, ...), custom_call_target="tpu_custom_call" | custom-call | tf_op jit(solution)/shard_map/local_grads/pallas_call | solution.py:266
  59.7 3.9 %collective-permute-start.11 = (bf16[4,256,384]{2,1,0:T(8,128)(2,1)}, bf16[4,256,384]{2,1,0:T(8,128)(2,1)S(1)}, u32[]{:S(2)}, u32[]{:S(2)}) collective-permute-start(bf16[4,256,384]{2,1,0:T(8,128)(2,1)} %get-tuple-element.44), channel_id=1, source_target_pairs={{0,1},{1,0},{2,3},{3,2},{4,5},{5,4},{6,7},{7,6},{8,9},{9,8},{10,11... | collective-permute-start | bytes 2359304 | tf_op jit(solution)/shard_map/ppermute | solution.py:510
  63.5 1.4 collective-permute-start.12
  65.0 0.7 collective-permute-done.11
  65.7 2.3 %add.32 = bf16[4,256,384]{2,1,0:T(8,128)(2,1)} add(bf16[4,256,384]{2,1,0:T(8,128)(2,1)} %get-tuple-element.43, bf16[4,256,384]{2,1,0:T(8,128)(2,1)S(1)} %collective-permute-done.11) | non-fusion elementwise | flops 393216 | bytes 2359296 | tf_op jit(solution)/shard_map/add | solution.py:546
  67.9 4.1 %all-to-all-start = ((bf16[4,256,384]{2,1,0:T(8,128)(2,1)}), bf16[4,256,384]{2,1,0:T(8,128)(2,1)S(1)}, u32[]{:S(2)}, u32[]{:S(2)}) async-start(bf16[4,256,384]{2,1,0:T(8,128)(2,1)} %add.32), calls=%async_computation | async-start | bytes 1572864 | tf_op jit(solution)/shard_map/all_to_all | solution.py:547
  72.5 0.9 collective-permute-start.14
  73.5 0.7 collective-permute-start.15
  74.2 9.1 %collective-permute-done.12.refs_1_ = bf16[2,8,2,48,256]{4,3,2,1,0:T(8,128)(2,1)S(1)} collective-permute-done((bf16[2,8,2,48,256]{4,3,2,1,0:T(8,128)(2,1)}, bf16[2,8,2,48,256]{4,3,2,1,0:T(8,128)(2,1)S(1)}, u32[]{:S(2)}, u32[]{:S(2)}) %collective-permute-start.12) | collective-permute-done | bytes 786464 | tf_op jit(solution)/shard_map/ppermute | solution.py:510
  83.4 0.9 collective-permute-done.13
  84.2 6.7 %collective-permute-done.14.refs_4_ = bf16[1,8,2,48,256]{4,3,2,1,0:T(8,128)(2,1)S(1)} collective-permute-done((bf16[1,8,2,48,256]{4,3,2,1,0:T(8,128)(2,1)}, bf16[1,8,2,48,256]{4,3,2,1,0:T(8,128)(2,1)S(1)}, u32[]{:S(2)}, u32[]{:S(2)}) %collective-permute-start.14) | collective-permute-done | bytes 393248 | tf_op jit(solution)/shard_map/ppermute | solution.py:510
  91.5 1.7 collective-permute-start.17
  93.2 9.7 %collective-permute-done.16.refs_2_ = bf16[8,2,48,256]{3,2,1,0:T(8,128)(2,1)S(1)} collective-permute-done((bf16[8,2,48,256]{3,2,1,0:T(8,128)(2,1)S(1)}, bf16[8,2,48,256]{3,2,1,0:T(8,128)(2,1)S(1)}, u32[]{:S(2)}, u32[]{:S(2)}) %collective-permute-start.16) | collective-permute-done | bytes 393248 | tf_op jit(solution)/shard_map/ppermute | solution.py:510
  103.0 0.8 copy-done.11
  103.8 3.8 %adam_step.2 = (bf16[8,2,48,256]{3,2,1,0:T(8,128)(2,1)}, f32[16,2,48,256]{3,2,1,0:T(8,128)}, f32[16,2,48,256]{3,2,1,0:T(8,128)}) custom-call(s32[2]{0:T(128)} %pad_add_fusion.pos_ref, bf16[1,8,2,48,256]{4,3,2,1,0:T(8,128)(2,1)} %get-tuple-element.45.refs_0_, bf16[2,8,2,48,256]{4,3,2,1,0:T(8,128)(2,1)} %copy-done.2, bf16[8,2,48,256]{3,2,1,0:T(8,128)(2,1)} %copy-done.11, ...), custom_call_target="tpu_custom_call" | custom-call | tf_op jit(solution)/shard_map/adam_step/pallas_call | solution.py:368
  107.7 1.4 collective-permute-start.18
  109.1 2.4 %collective-permute-start.21 = (bf16[8,2,48,256]{3,2,1,0:T(8,128)(2,1)}, bf16[8,2,48,256]{3,2,1,0:T(8,128)(2,1)S(1)}, u32[]{:S(2)}, u32[]{:S(2)}) collective-permute-start(bf16[8,2,48,256]{3,2,1,0:T(8,128)(2,1)} %get-tuple-element.62.refs_0_), channel_id=1, source_target_pairs={{0,16},{8,24},{16,0},{24,8},{1,17},{9,25},{17,1},{25,9},{2,18},{10... | collective-permute-start | bytes 1179656 | tf_op jit(solution)/shard_map/ppermute | solution.py:459
  111.5 15.8 %collective-permute-done.18.refs_1_ = bf16[8,2,48,256]{3,2,1,0:T(8,128)(2,1)S(1)} collective-permute-done((bf16[8,2,48,256]{3,2,1,0:T(8,128)(2,1)}, bf16[8,2,48,256]{3,2,1,0:T(8,128)(2,1)S(1)}, u32[]{:S(2)}, u32[]{:S(2)}) %collective-permute-start.18) | collective-permute-done | bytes 393248 | tf_op jit(solution)/shard_map/ppermute | solution.py:460
  127.3 4.0 %adam_step.3 = (bf16[8,2,48,256]{3,2,1,0:T(8,128)(2,1)}, f32[16,2,48,256]{3,2,1,0:T(8,128)}, f32[16,2,48,256]{3,2,1,0:T(8,128)}) custom-call(s32[2]{0:T(128)} %pad_add_fusion.pos_ref, bf16[1,8,2,48,256]{4,3,2,1,0:T(8,128)(2,1)} %get-tuple-element.45.refs_0_, bf16[2,8,2,48,256]{4,3,2,1,0:T(8,128)(2,1)} %copy-done.2, ...), custom_call_target="tpu_custom_call", output_to_operand_aliasing={{1}: (10, {}), {2}: (11, {})} | custom-call | tf_op jit(solution)/shard_map/adam_step/pallas_call | solution.py:368
  131.9 2.4 %collective-permute-start.20 = (bf16[8,2,48,256]{3,2,1,0:T(8,128)(2,1)}, bf16[8,2,48,256]{3,2,1,0:T(8,128)(2,1)S(1)}, u32[]{:S(2)}, u32[]{:S(2)}) collective-permute-start(bf16[8,2,48,256]{3,2,1,0:T(8,128)(2,1)} %get-tuple-element.64.refs_0_), channel_id=1, source_target_pairs={{0,8},{8,0},{16,24},{24,16},{1,9},{9,1},{17,25},{25,17},{2,10},{10... | collective-permute-start | bytes 1179656 | tf_op jit(solution)/shard_map/ppermute | solution.py:460
  134.3 0.7 collective-permute-start.22
  135.0 1.3 collective-permute-start.23
  136.3 16.6 %collective-permute-done.20.refs_1_ = bf16[8,2,48,256]{3,2,1,0:T(8,128)(2,1)S(1)} collective-permute-done((bf16[8,2,48,256]{3,2,1,0:T(8,128)(2,1)}, bf16[8,2,48,256]{3,2,1,0:T(8,128)(2,1)S(1)}, u32[]{:S(2)}, u32[]{:S(2)}) %collective-permute-start.20) | collective-permute-done | bytes 393248 | tf_op jit(solution)/shard_map/ppermute | solution.py:460
  152.9 6.8 %collective-permute-done.23.refs_1_ = bf16[8,2,48,256]{3,2,1,0:T(8,128)(2,1)S(1)} collective-permute-done((bf16[8,2,48,256]{3,2,1,0:T(8,128)(2,1)S(1)}, bf16[8,2,48,256]{3,2,1,0:T(8,128)(2,1)S(1)}, u32[]{:S(2)}, u32[]{:S(2)}) %collective-permute-start.23) | collective-permute-done | bytes 393248 | tf_op jit(solution)/shard_map/ppermute | solution.py:461
  159.7 0.7 collective-permute-start.24
  160.4 1.3 collective-permute-start.25
  161.7 2.2 %finish_predicted.1 = bf16[256,384]{1,0:T(8,128)(2,1)} custom-call(bf16[256,256]{1,0:T(8,128)(2,1)} %get-tuple-element.36.perm_ref, bf16[4,256,384]{2,1,0:T(8,128)(2,1)} %copy-done.4), custom_call_target="tpu_custom_call" | custom-call | tf_op jit(solution)/shard_map/finish_predicted/pallas_call | solution.py:488
  163.9 3.0 %place_weights.4.refs_2_ = bf16[16,2,48,1024]{3,2,1,0:T(8,128)(2,1)} custom-call(s32[2]{0:T(128)} %pad_add_fusion.pos_ref, bf16[8,2,48,256]{3,2,1,0:T(8,128)(2,1)} %get-tuple-element.62.refs_0_, bf16[8,2,48,256]{3,2,1,0:T(8,128)(2,1)} %copy-done.16, bf16[8,2,48,256]{3,2,1,0:T(8,128)(2,1)} %copy-done.17), custom_call_target="tpu_custom_call" | custom-call | tf_op jit(solution)/shard_map/place_weights/pallas_call | solution.py:437
  166.9 1.8 %place_weights.5.refs_3_ = bf16[16,2,48,1024]{3,2,1,0:T(8,128)(2,1)} custom-call(s32[2]{0:T(128)S(1)} %copy-done, bf16[8,2,48,256]{3,2,1,0:T(8,128)(2,1)S(1)} %collective-permute-done.22.refs_0_, bf16[8,2,48,256]{3,2,1,0:T(8,128)(2,1)S(1)} %collective-permute-done.23.refs_1_, ...), custom_call_target="tpu_custom_call", output_to_operand_aliasing={{}: (3, {})} | custom-call | tf_op jit(solution)/shard_map/place_weights/pallas_call | solution.py:437
  168.8 3.0 %place_weights.6.refs_2_ = bf16[16,2,48,1024]{3,2,1,0:T(8,128)(2,1)} custom-call(s32[2]{0:T(128)} %pad_add_fusion.pos_ref, bf16[8,2,48,256]{3,2,1,0:T(8,128)(2,1)} %get-tuple-element.64.refs_0_, bf16[8,2,48,256]{3,2,1,0:T(8,128)(2,1)} %copy-done.23, bf16[8,2,48,256]{3,2,1,0:T(8,128)(2,1)} %copy-done.21, ...), custom_call_target="tpu_custom_call", output_to_operand_aliasing={{}: (4, {})} | custom-call | tf_op jit(solution)/shard_map/place_weights/pallas_call | solution.py:437
  171.8 1.2 collective-permute-done.25.refs_1_
  173.0 1.8 %place_weights.7 = bf16[16,2,48,1024]{3,2,1,0:T(8,128)(2,1)} custom-call(s32[2]{0:T(128)S(1)} %copy-done.1, bf16[8,2,48,256]{3,2,1,0:T(8,128)(2,1)S(1)} %collective-permute-done.24.refs_0_, bf16[8,2,48,256]{3,2,1,0:T(8,128)(2,1)S(1)} %collective-permute-done.25.refs_1_, bf16[16,2,48,1024]{3,2,1,0:T(8,128)(2,1)} %place_weights.6.refs_2_), custom_call_target="tpu_custom_call", output_to_operand_aliasing={{}: (3, {})} | custom-call | tf_op jit(solution)/shard_map/place_weights/pallas_call | solution.py:437
  (78 shorter events, 4.1 us)
Async XLA Ops:
  1.8 2.5 %collective-permute-start = (bf16[8,2,48,256]{3,2,1,0:T(8,128)(2,1)S(1)}, bf16[8,2,48,256]{3,2,1,0:T(8,128)(2,1)S(1)}, u32[]{:S(2)}, u32[]{:S(2)}) collective-permute-start(bf16[8,2,48,256]{3,2,1,0:T(8,128)(2,1)S(1)} %get-tuple-element.69), channel_id=1, source_target_pairs={{0,1},{1,0},{2,3},{3,2},{4,5},{5,4},{6,7},{7,6},{8,9},{9,8},{10,11... | collective-permute-start | bytes 1179656 | tf_op jit(solution)/shard_map/ppermute | solution.py:510
  4.3 1.7 copy-start.13
  4.4 23.3 %copy-start.5 = (bf16[2,8,2,48,256]{4,3,2,1,0:T(8,128)(2,1)}, bf16[2,8,2,48,256]{4,3,2,1,0:T(8,128)(2,1)S(1)}, u32[]{:S(2)}) copy-start(bf16[2,8,2,48,256]{4,3,2,1,0:T(8,128)(2,1)S(1)} %pad_maximum_fusion.1.rest_4_) | copy-start | bytes 2359300
  4.4 23.2 %collective-permute-start.4 = (bf16[2,8,2,48,256]{4,3,2,1,0:T(8,128)(2,1)S(1)}, bf16[2,8,2,48,256]{4,3,2,1,0:T(8,128)(2,1)S(1)}, u32[]{:S(2)}, u32[]{:S(2)}) collective-permute-start(bf16[2,8,2,48,256]{4,3,2,1,0:T(8,128)(2,1)S(1)} %pad_maximum_fusion.1.rest_4_), channel_id=1, source_target_pairs={{0,4},{1,5},{2,6},{3,7},{4,0},{5,1},{6,2},{7,3},{8,12},{9,13},{10,... | collective-permute-start | bytes 2359304 | tf_op jit(solution)/shard_map/ppermute | solution.py:510
  6.0 21.2 %collective-permute-start.2 = (bf16[528,384]{1,0:T(8,128)(2,1)S(1)}, bf16[528,384]{1,0:T(8,128)(2,1)S(1)}, u32[]{:S(2)}, u32[]{:S(2)}) collective-permute-start(bf16[528,384]{1,0:T(8,128)(2,1)S(1)} %copy-done.13), channel_id=1, source_target_pairs={{0,16},{8,24},{16,0},{24,8},{1,17},{9,25},{17,1},{25,9},{2,18},{10... | collective-permute-start | bytes 1216520 | tf_op jit(solution)/shard_map/ppermute | solution.py:459
  8.6 18.8 %collective-permute-start.1 = (bf16[528,384]{1,0:T(8,128)(2,1)S(1)}, bf16[528,384]{1,0:T(8,128)(2,1)S(1)}, u32[]{:S(2)}, u32[]{:S(2)}) collective-permute-start(bf16[528,384]{1,0:T(8,128)(2,1)S(1)} %copy-done.13), channel_id=1, source_target_pairs={{0,8},{8,0},{16,24},{24,16},{1,9},{9,1},{17,25},{25,17},{2,10},{10... | collective-permute-start | bytes 1216520 | tf_op jit(solution)/shard_map/ppermute | solution.py:460
  10.2 19.1 %collective-permute-start.3 = (bf16[2,8,2,48,256]{4,3,2,1,0:T(8,128)(2,1)S(1)}, bf16[2,8,2,48,256]{4,3,2,1,0:T(8,128)(2,1)S(1)}, u32[]{:S(2)}, u32[]{:S(2)}) collective-permute-start(bf16[2,8,2,48,256]{4,3,2,1,0:T(8,128)(2,1)S(1)} %pad_maximum_fusion.1.rest_4_), channel_id=1, source_target_pairs={{0,2},{1,3},{2,0},{3,1},{4,6},{5,7},{6,4},{7,5},{8,10},{9,11},{10,... | collective-permute-start | bytes 2359304 | tf_op jit(solution)/shard_map/ppermute | solution.py:510
  27.5 18.7 %copy-start.3 = (bf16[3,528,384]{2,1,0:T(8,128)(2,1)}, bf16[3,528,384]{2,1,0:T(8,128)(2,1)S(1)}, u32[]{:S(2)}) copy-start(bf16[3,528,384]{2,1,0:T(8,128)(2,1)S(1)} %pad_maximum_fusion.rest_0_) | copy-start | bytes 3649540
  27.6 17.0 %copy-start.24 = (s32[32,4]{0,1:T(4,128)S(1)}, s32[32,4]{0,1:T(4,128)}, u32[]{:S(2)}) copy-start(s32[32,4]{0,1:T(4,128)} %param.11) | copy-start | bytes 1540
  27.6 18.7 %collective-permute-start.7 = (bf16[3,528,384]{2,1,0:T(8,128)(2,1)S(1)}, bf16[3,528,384]{2,1,0:T(8,128)(2,1)}, u32[]{:S(2)}, u32[]{:S(2)}) collective-permute-start(bf16[3,528,384]{2,1,0:T(8,128)(2,1)S(1)} %pad_maximum_fusion.rest_0_), channel_id=1, source_target_pairs={{0,1},{1,0},{2,3},{3,2},{4,5},{5,4},{6,7},{7,6},{8,9},{9,8},{10,11... | collective-permute-start | bytes 3649544 | tf_op jit(solution)/shard_map/ppermute | solution.py:510
  27.7 18.6 %copy-start.6 = (bf16[2,8,2,48,256]{4,3,2,1,0:T(8,128)(2,1)}, bf16[2,8,2,48,256]{4,3,2,1,0:T(8,128)(2,1)S(1)}, u32[]{:S(2)}) copy-start(bf16[2,8,2,48,256]{4,3,2,1,0:T(8,128)(2,1)S(1)} %collective-permute-done.4.rest_6_) | copy-start | bytes 2359300
  27.7 15.3 %collective-permute-start.9 = (bf16[8,2,48,256]{3,2,1,0:T(8,128)(2,1)S(1)}, bf16[8,2,48,256]{3,2,1,0:T(8,128)(2,1)S(1)}, u32[]{:S(2)}, u32[]{:S(2)}) collective-permute-start(bf16[8,2,48,256]{3,2,1,0:T(8,128)(2,1)S(1)} %slice_bitcast_fusion), channel_id=1, source_target_pairs={{0,2},{1,3},{2,0},{3,1},{4,6},{5,7},{6,4},{7,5},{8,10},{9,11},{10,... | collective-permute-start | bytes 1179656 | tf_op jit(solution)/shard_map/ppermute | solution.py:510
  29.3 2.0 %copy-start.7 = (bf16[2,8,2,48,256]{4,3,2,1,0:T(8,128)(2,1)}, bf16[2,8,2,48,256]{4,3,2,1,0:T(8,128)(2,1)S(1)}, u32[]{:S(2)}) copy-start(bf16[2,8,2,48,256]{4,3,2,1,0:T(8,128)(2,1)S(1)} %collective-permute-done.3.rest_5_) | copy-start | bytes 2359300
  29.3 3.3 %collective-permute-start.5 = (bf16[528,384]{1,0:T(8,128)(2,1)S(1)}, bf16[528,384]{1,0:T(8,128)(2,1)S(1)}, u32[]{:S(2)}, u32[]{:S(2)}) collective-permute-start(bf16[528,384]{1,0:T(8,128)(2,1)S(1)} %copy-done.13), channel_id=1, source_target_pairs={{8,16},{16,8},{9,17},{17,9},{10,18},{18,10},{11,19},{19,11},{12,20... | collective-permute-start | bytes 1216520 | tf_op jit(solution)/shard_map/ppermute | solution.py:462
  29.9 12.9 %collective-permute-start.6 = (bf16[528,384]{1,0:T(8,128)(2,1)S(1)}, bf16[528,384]{1,0:T(8,128)(2,1)S(1)}, u32[]{:S(2)}, u32[]{:S(2)}) collective-permute-start(bf16[528,384]{1,0:T(8,128)(2,1)S(1)} %collective-permute-done.2), channel_id=1, source_target_pairs={{16,24},{8,0},{17,25},{9,1},{18,26},{10,2},{19,27},{11,3},{20,28},... | collective-permute-start | bytes 1216520 | tf_op jit(solution)/shard_map/ppermute | solution.py:461
  31.3 11.7 %collective-permute-start.8 = (bf16[8,2,48,256]{3,2,1,0:T(8,128)(2,1)S(1)}, bf16[8,2,48,256]{3,2,1,0:T(8,128)(2,1)S(1)}, u32[]{:S(2)}, u32[]{:S(2)}) collective-permute-start(bf16[8,2,48,256]{3,2,1,0:T(8,128)(2,1)S(1)} %slice_bitcast_fusion.1), channel_id=1, source_target_pairs={{0,4},{1,5},{2,6},{3,7},{4,0},{5,1},{6,2},{7,3},{8,12},{9,13},{10,... | collective-permute-start | bytes 1179656 | tf_op jit(solution)/shard_map/ppermute | solution.py:510
  43.0 3.3 %copy-start.8 = (bf16[528,384]{1,0:T(8,128)(2,1)}, bf16[528,384]{1,0:T(8,128)(2,1)S(1)}, u32[]{:S(2)}) copy-start(bf16[528,384]{1,0:T(8,128)(2,1)S(1)} %add.31.rest_1_) | copy-start | bytes 1216516
  44.5 1.7 collective-permute-start.10
  59.7 6.0 %collective-permute-start.11 = (bf16[4,256,384]{2,1,0:T(8,128)(2,1)}, bf16[4,256,384]{2,1,0:T(8,128)(2,1)S(1)}, u32[]{:S(2)}, u32[]{:S(2)}) collective-permute-start(bf16[4,256,384]{2,1,0:T(8,128)(2,1)} %get-tuple-element.44), channel_id=1, source_target_pairs={{0,1},{1,0},{2,3},{3,2},{4,5},{5,4},{6,7},{7,6},{8,9},{9,8},{10,11... | collective-permute-start | bytes 2359304 | tf_op jit(solution)/shard_map/ppermute | solution.py:510
  63.5 19.8 %collective-permute-start.12 = (bf16[2,8,2,48,256]{4,3,2,1,0:T(8,128)(2,1)}, bf16[2,8,2,48,256]{4,3,2,1,0:T(8,128)(2,1)S(1)}, u32[]{:S(2)}, u32[]{:S(2)}) collective-permute-start(bf16[2,8,2,48,256]{4,3,2,1,0:T(8,128)(2,1)} %get-tuple-element.46), channel_id=1, source_target_pairs={{0,2},{1,3},{2,0},{3,1},{4,6},{5,7},{6,4},{7,5},{8,10},{9,11},{10,... | collective-permute-start | bytes 2359304 | tf_op jit(solution)/shard_map/ppermute | solution.py:510
  65.7 7.8 %copy-start.25 = (bf16[1,8,2,48,256]{4,3,2,1,0:T(8,128)(2,1)S(1)}, bf16[1,8,2,48,256]{4,3,2,1,0:T(8,128)(2,1)}, u32[]{:S(2)}) copy-start(bf16[1,8,2,48,256]{4,3,2,1,0:T(8,128)(2,1)} %get-tuple-element.52) | copy-start | bytes 1179652
  65.7 17.7 %copy-start.19 = (bf16[1,8,2,48,256]{4,3,2,1,0:T(8,128)(2,1)S(1)}, bf16[1,8,2,48,256]{4,3,2,1,0:T(8,128)(2,1)}, u32[]{:S(2)}) copy-start(bf16[1,8,2,48,256]{4,3,2,1,0:T(8,128)(2,1)} %get-tuple-element.47) | copy-start | bytes 1179652
  67.9 23.5 %copy-start.18 = (bf16[1,8,2,48,256]{4,3,2,1,0:T(8,128)(2,1)S(1)}, bf16[1,8,2,48,256]{4,3,2,1,0:T(8,128)(2,1)}, u32[]{:S(2)}) copy-start(bf16[1,8,2,48,256]{4,3,2,1,0:T(8,128)(2,1)} %get-tuple-element.55) | copy-start | bytes 1179652
  67.9 35.0 %all-to-all-start = ((bf16[4,256,384]{2,1,0:T(8,128)(2,1)}), bf16[4,256,384]{2,1,0:T(8,128)(2,1)S(1)}, u32[]{:S(2)}, u32[]{:S(2)}) async-start(bf16[4,256,384]{2,1,0:T(8,128)(2,1)} %add.32), calls=%async_computation | async-start | bytes 1572864 | tf_op jit(solution)/shard_map/all_to_all | solution.py:547
  72.0 12.2 %collective-permute-start.13 = (bf16[1,8,2,48,256]{4,3,2,1,0:T(8,128)(2,1)}, bf16[1,8,2,48,256]{4,3,2,1,0:T(8,128)(2,1)S(1)}, u32[]{:S(2)}, u32[]{:S(2)}) collective-permute-start(bf16[1,8,2,48,256]{4,3,2,1,0:T(8,128)(2,1)} %get-tuple-element.48), channel_id=1, source_target_pairs={{0,4},{1,5},{2,6},{3,7},{4,0},{5,1},{6,2},{7,3},{8,12},{9,13},{10,... | collective-permute-start | bytes 1179656 | tf_op jit(solution)/shard_map/ppermute | solution.py:510
  72.5 18.4 %collective-permute-start.14 = (bf16[1,8,2,48,256]{4,3,2,1,0:T(8,128)(2,1)}, bf16[1,8,2,48,256]{4,3,2,1,0:T(8,128)(2,1)S(1)}, u32[]{:S(2)}, u32[]{:S(2)}) collective-permute-start(bf16[1,8,2,48,256]{4,3,2,1,0:T(8,128)(2,1)} %get-tuple-element.50), channel_id=1, source_target_pairs={{0,5},{1,4},{2,7},{3,6},{4,1},{5,0},{6,3},{7,2},{8,13},{9,12},{10,... | collective-permute-start | bytes 1179656 | tf_op jit(solution)/shard_map/ppermute | solution.py:510
  73.5 17.4 %collective-permute-start.15 = (bf16[1,8,2,48,256]{4,3,2,1,0:T(8,128)(2,1)S(1)}, bf16[1,8,2,48,256]{4,3,2,1,0:T(8,128)(2,1)S(1)}, u32[]{:S(2)}, u32[]{:S(2)}) collective-permute-start(bf16[1,8,2,48,256]{4,3,2,1,0:T(8,128)(2,1)S(1)} %copy-done.25), channel_id=1, source_target_pairs={{0,1},{1,0},{2,3},{3,2},{4,5},{5,4},{6,7},{7,6},{8,9},{9,8},{10,11... | collective-permute-start | bytes 1179656 | tf_op jit(solution)/shard_map/ppermute | solution.py:510
  83.3 19.6 %copy-start.2 = (bf16[2,8,2,48,256]{4,3,2,1,0:T(8,128)(2,1)}, bf16[2,8,2,48,256]{4,3,2,1,0:T(8,128)(2,1)S(1)}, u32[]{:S(2)}) copy-start(bf16[2,8,2,48,256]{4,3,2,1,0:T(8,128)(2,1)S(1)} %collective-permute-done.12.refs_1_) | copy-start | bytes 2359300
  90.9 12.1 %copy-start.9 = (bf16[1,8,2,48,256]{4,3,2,1,0:T(8,128)(2,1)}, bf16[1,8,2,48,256]{4,3,2,1,0:T(8,128)(2,1)S(1)}, u32[]{:S(2)}) copy-start(bf16[1,8,2,48,256]{4,3,2,1,0:T(8,128)(2,1)S(1)} %collective-permute-done.14.refs_4_) | copy-start | bytes 1179652
  90.9 12.1 %copy-start.10 = (bf16[1,8,2,48,256]{4,3,2,1,0:T(8,128)(2,1)}, bf16[1,8,2,48,256]{4,3,2,1,0:T(8,128)(2,1)S(1)}, u32[]{:S(2)}) copy-start(bf16[1,8,2,48,256]{4,3,2,1,0:T(8,128)(2,1)S(1)} %collective-permute-done.15.refs_3_) | copy-start | bytes 1179652
  90.9 12.0 %collective-permute-start.16 = (bf16[8,2,48,256]{3,2,1,0:T(8,128)(2,1)S(1)}, bf16[8,2,48,256]{3,2,1,0:T(8,128)(2,1)S(1)}, u32[]{:S(2)}, u32[]{:S(2)}) collective-permute-start(bf16[8,2,48,256]{3,2,1,0:T(8,128)(2,1)S(1)} %fusion), channel_id=1, source_target_pairs={{0,4},{1,5},{2,6},{3,7},{4,0},{5,1},{6,2},{7,3},{8,12},{9,13},{10,... | collective-permute-start | bytes 1179656 | tf_op jit(solution)/shard_map/ppermute | solution.py:510
  91.5 11.4 %collective-permute-start.17 = (bf16[8,2,48,256]{3,2,1,0:T(8,128)(2,1)S(1)}, bf16[8,2,48,256]{3,2,1,0:T(8,128)(2,1)S(1)}, u32[]{:S(2)}, u32[]{:S(2)}) collective-permute-start(bf16[8,2,48,256]{3,2,1,0:T(8,128)(2,1)S(1)} %add_bitcast_fusion), channel_id=1, source_target_pairs={{0,3},{1,2},{2,1},{3,0},{4,7},{5,6},{6,5},{7,4},{8,11},{9,10},{10,... | collective-permute-start | bytes 1179656 | tf_op jit(solution)/shard_map/ppermute | solution.py:510
  102.9 4.8 %copy-start.4 = (bf16[4,256,384]{2,1,0:T(8,128)(2,1)}, bf16[4,256,384]{2,1,0:T(8,128)(2,1)S(1)}, u32[]{:S(2)}) copy-start(bf16[4,256,384]{2,1,0:T(8,128)(2,1)S(1)} %all-to-all-done.parts_ref) | copy-start | bytes 2359300
  107.7 19.6 %collective-permute-start.18 = (bf16[8,2,48,256]{3,2,1,0:T(8,128)(2,1)}, bf16[8,2,48,256]{3,2,1,0:T(8,128)(2,1)S(1)}, u32[]{:S(2)}, u32[]{:S(2)}) collective-permute-start(bf16[8,2,48,256]{3,2,1,0:T(8,128)(2,1)} %get-tuple-element.62.refs_0_), channel_id=1, source_target_pairs={{0,8},{8,0},{16,24},{24,16},{1,9},{9,1},{17,25},{25,17},{2,10},{10... | collective-permute-start | bytes 1179656 | tf_op jit(solution)/shard_map/ppermute | solution.py:460
  109.1 25.1 %collective-permute-start.21 = (bf16[8,2,48,256]{3,2,1,0:T(8,128)(2,1)}, bf16[8,2,48,256]{3,2,1,0:T(8,128)(2,1)S(1)}, u32[]{:S(2)}, u32[]{:S(2)}) collective-permute-start(bf16[8,2,48,256]{3,2,1,0:T(8,128)(2,1)} %get-tuple-element.62.refs_0_), channel_id=1, source_target_pairs={{0,16},{8,24},{16,0},{24,8},{1,17},{9,25},{17,1},{25,9},{2,18},{10... | collective-permute-start | bytes 1179656 | tf_op jit(solution)/shard_map/ppermute | solution.py:459
  127.3 4.0 %copy-start.16 = (bf16[8,2,48,256]{3,2,1,0:T(8,128)(2,1)}, bf16[8,2,48,256]{3,2,1,0:T(8,128)(2,1)S(1)}, u32[]{:S(2)}) copy-start(bf16[8,2,48,256]{3,2,1,0:T(8,128)(2,1)S(1)} %collective-permute-done.18.refs_1_) | copy-start | bytes 1179652
  127.3 7.0 %copy-start.15 = (bf16[8,2,48,256]{3,2,1,0:T(8,128)(2,1)S(1)}, bf16[8,2,48,256]{3,2,1,0:T(8,128)(2,1)}, u32[]{:S(2)}) copy-start(bf16[8,2,48,256]{3,2,1,0:T(8,128)(2,1)} %get-tuple-element.62.refs_0_) | copy-start | bytes 1179652
  131.3 21.6 %collective-permute-start.19 = (bf16[8,2,48,256]{3,2,1,0:T(8,128)(2,1)}, bf16[8,2,48,256]{3,2,1,0:T(8,128)(2,1)S(1)}, u32[]{:S(2)}, u32[]{:S(2)}) collective-permute-start(bf16[8,2,48,256]{3,2,1,0:T(8,128)(2,1)} %get-tuple-element.64.refs_0_), channel_id=1, source_target_pairs={{0,16},{8,24},{16,0},{24,8},{1,17},{9,25},{17,1},{25,9},{2,18},{10... | collective-permute-start | bytes 1179656 | tf_op jit(solution)/shard_map/ppermute | solution.py:459
  131.9 21.0 %collective-permute-start.20 = (bf16[8,2,48,256]{3,2,1,0:T(8,128)(2,1)}, bf16[8,2,48,256]{3,2,1,0:T(8,128)(2,1)S(1)}, u32[]{:S(2)}, u32[]{:S(2)}) collective-permute-start(bf16[8,2,48,256]{3,2,1,0:T(8,128)(2,1)} %get-tuple-element.64.refs_0_), channel_id=1, source_target_pairs={{0,8},{8,0},{16,24},{24,16},{1,9},{9,1},{17,25},{25,17},{2,10},{10... | collective-permute-start | bytes 1179656 | tf_op jit(solution)/shard_map/ppermute | solution.py:460
  134.3 29.6 %copy-start.17 = (bf16[8,2,48,256]{3,2,1,0:T(8,128)(2,1)}, bf16[8,2,48,256]{3,2,1,0:T(8,128)(2,1)S(1)}, u32[]{:S(2)}) copy-start(bf16[8,2,48,256]{3,2,1,0:T(8,128)(2,1)S(1)} %collective-permute-done.21.refs_2_) | copy-start | bytes 1179652
  134.3 18.6 %collective-permute-start.22 = (bf16[8,2,48,256]{3,2,1,0:T(8,128)(2,1)S(1)}, bf16[8,2,48,256]{3,2,1,0:T(8,128)(2,1)S(1)}, u32[]{:S(2)}, u32[]{:S(2)}) collective-permute-start(bf16[8,2,48,256]{3,2,1,0:T(8,128)(2,1)S(1)} %copy-done.15), channel_id=1, source_target_pairs={{8,16},{16,8},{9,17},{17,9},{10,18},{18,10},{11,19},{19,11},{12,20... | collective-permute-start | bytes 1179656 | tf_op jit(solution)/shard_map/ppermute | solution.py:462
  135.0 24.7 %collective-permute-start.23 = (bf16[8,2,48,256]{3,2,1,0:T(8,128)(2,1)S(1)}, bf16[8,2,48,256]{3,2,1,0:T(8,128)(2,1)S(1)}, u32[]{:S(2)}, u32[]{:S(2)}) collective-permute-start(bf16[8,2,48,256]{3,2,1,0:T(8,128)(2,1)S(1)} %collective-permute-done.21.refs_2_), channel_id=1, source_target_pairs={{16,24},{8,0},{17,25},{9,1},{18,26},{10,2},{19,27},{11,3},{20,28},... | collective-permute-start | bytes 1179656 | tf_op jit(solution)/shard_map/ppermute | solution.py:461
  152.9 14.1 %copy-start.23 = (bf16[8,2,48,256]{3,2,1,0:T(8,128)(2,1)}, bf16[8,2,48,256]{3,2,1,0:T(8,128)(2,1)S(1)}, u32[]{:S(2)}) copy-start(bf16[8,2,48,256]{3,2,1,0:T(8,128)(2,1)S(1)} %collective-permute-done.20.refs_1_) | copy-start | bytes 1179652
  152.9 14.1 %copy-start.21 = (bf16[8,2,48,256]{3,2,1,0:T(8,128)(2,1)}, bf16[8,2,48,256]{3,2,1,0:T(8,128)(2,1)S(1)}, u32[]{:S(2)}) copy-start(bf16[8,2,48,256]{3,2,1,0:T(8,128)(2,1)S(1)} %collective-permute-done.19.refs_2_) | copy-start | bytes 1179652
  159.7 12.1 %collective-permute-start.24 = (bf16[8,2,48,256]{3,2,1,0:T(8,128)(2,1)}, bf16[8,2,48,256]{3,2,1,0:T(8,128)(2,1)S(1)}, u32[]{:S(2)}, u32[]{:S(2)}) collective-permute-start(bf16[8,2,48,256]{3,2,1,0:T(8,128)(2,1)} %get-tuple-element.64.refs_0_), channel_id=1, source_target_pairs={{8,16},{16,8},{9,17},{17,9},{10,18},{18,10},{11,19},{19,11},{12,20... | collective-permute-start | bytes 1179656 | tf_op jit(solution)/shard_map/ppermute | solution.py:462
  160.4 12.6 %collective-permute-start.25 = (bf16[8,2,48,256]{3,2,1,0:T(8,128)(2,1)S(1)}, bf16[8,2,48,256]{3,2,1,0:T(8,128)(2,1)S(1)}, u32[]{:S(2)}, u32[]{:S(2)}) collective-permute-start(bf16[8,2,48,256]{3,2,1,0:T(8,128)(2,1)S(1)} %collective-permute-done.19.refs_2_), channel_id=1, source_target_pairs={{16,24},{8,0},{17,25},{9,1},{18,26},{10,2},{19,27},{11,3},{20,28},... | collective-permute-start | bytes 1179656 | tf_op jit(solution)/shard_map/ppermute | solution.py:461
  163.9 3.1 %copy-start = (s32[2]{0:T(128)S(1)}, s32[2]{0:T(128)}, u32[]{:S(2)}) copy-start(s32[2]{0:T(128)} %pad_add_fusion.pos_ref) | copy-start | bytes 28
  168.8 4.2 %copy-start.1 = (s32[2]{0:T(128)S(1)}, s32[2]{0:T(128)}, u32[]{:S(2)}) copy-start(s32[2]{0:T(128)} %pad_add_fusion.pos_ref) | copy-start | bytes 28
  (5 other events, 4.1 us)

commit v16 on v14

--- a/solution.py
+++ b/solution.py
@@ -11,6 +11,7 @@
 CAP = 128
 ID_ROWS = 16
 PARTS = 4
+TOGETHER = 4
 VMEM_BYTES = 56 * 2**20
 LAST_VMEM_BYTES = 8 * 2**20
 
@@ -146,42 +147,42 @@
             copy.wait()
         for source in range(2 * planes):
             ids_row = sorted_rows[source, 2 * rows :, :rows][:1].astype(jnp.float32)
-            id_cols[source] = jnp.broadcast_to(ids_row, (128, rows)).T
-            full_of[source] = jnp.max(ids_row[:, :128]).astype(jnp.int32)
-
-        def listing(t, count):
-            source = t // (touch + 1)
-            j = t - source * (touch + 1)
-            which = source // planes
-            device = (pos_ref[0] ^ (source - which * planes)) * n_own + (own_at ^ which)
+            id_cols[source] = jnp.broadcast_to(ids_row[:, CAP:], (128, rows - CAP)).T
+            full_of[source] = jnp.max(ids_row[:, :CAP]).astype(jnp.int32)
+
+        count = jnp.int32(0)
+        for source in range(2 * planes):
+            which, plane = divmod(source, planes)
+            device = (pos_ref[0] ^ plane) * n_own + (own_at ^ which)
             full = full_of[source]
-            insertion = jnp.where(j == 0, full, touched_ref[device, jnp.maximum(j - 1, 0)])
-            e = slot_ref[insertion] - core * half
-            here = (e >= 0) & (e < half) & ((j == 0) | (insertion != full))
-            tasks[0, count] = source
-            tasks[1, count] = jnp.where(j == 0, 0, CAP)
-            tasks[2, count] = insertion
-            tasks[3, count] = e
-            return count + here.astype(jnp.int32)
-
-        count = lax.fori_loop(0, 2 * planes * (touch + 1), listing, 0)
-        tasks[0, count] = 0
-        tasks[1, count] = 0
-        tasks[2, count] = -1
-        tasks[3, count] = 0
+            for j in range(touch + 1):
+                insertion = full if j == 0 else touched_ref[device, j - 1]
+                e = slot_ref[insertion] - core * half
+                here = (e >= 0) & (e < half)
+                if j:
+                    here = here & (insertion != full)
+                tasks[0, count] = jnp.int32(source)
+                tasks[1, count] = jnp.int32(0 if j == 0 else CAP)
+                tasks[2, count] = insertion
+                tasks[3, count] = e
+                count = count + here.astype(jnp.int32)
+        for u in range(TOGETHER - 1):
+            tasks[0, count + u] = jnp.int32(0)
+            tasks[1, count + u] = jnp.int32(CAP)
+            tasks[2, count + u] = jnp.int32(-1)
+            tasks[3, count + u] = jnp.int32(0)
         for copy in block_copies:
             copy.wait()
 
-        def pair(i, _):
+        def together(i, _):
             loaded = []
-            for u in range(2):
-                source, insertion, e = tasks[0, 2 * i + u], tasks[2, 2 * i + u], tasks[3, 2 * i + u]
-                first = pl.multiple_of(tasks[1, 2 * i + u], CAP)
-                keep = (
-                    (id_cols[source, pl.ds(first, CAP), :] == insertion.astype(jnp.float32))
-                    .astype(jnp.float32)
-                    .astype(jnp.bfloat16)
-                )
+            for u in range(TOGETHER):
+                source, offset, insertion, e = [tasks[k, TOGETHER * i + u] for k in range(4)]
+                first = pl.multiple_of(offset, CAP)
+                wanted = jnp.where(offset == 0, -1, insertion).astype(jnp.float32)
+                every = (offset == 0).astype(jnp.float32)
+                keep = (id_cols[source] == wanted).astype(jnp.float32)
+                keep = jnp.maximum(keep, every).astype(jnp.bfloat16)
                 keep = jnp.concatenate([keep] * (SITES // 128), axis=1)
                 sig = sorted_rows[source, pl.ds(first, CAP), :] * keep
                 cot = sorted_rows[source, pl.ds(rows + first, CAP), :] * keep
@@ -210,7 +211,7 @@
                 acc[e, 1] += grad_out
             return 0
 
-        lax.fori_loop(0, (count + 1) // 2, pair, 0)
+        lax.fori_loop(0, (count + TOGETHER - 1) // TOGETHER, together, 0)
         outs = [
             pltpu.make_async_copy(
                 pred.at[which * planes + i], pred_refs[which].at[pos_ref[0] ^ i], sem_out.at[which, i]
@@ -248,7 +249,7 @@
     ]
     most = 2 * planes * (touch + 1)
     acc_shape = (half, 2, SITES, width)
-    id_shape = (2 * planes, rows, 128)
+    id_shape = (2 * planes, rows - CAP, 128)
     row_shape = (2 * planes,) + rows_in[0].shape[1:]
     pred_all = (2 * planes, rows, SITES)
     scratch = [pltpu.VMEM(one.shape, jnp.bfloat16) for one in grad_shapes] + [
@@ -258,7 +259,7 @@
         pltpu.VMEM(row_shape, jnp.bfloat16),
         pltpu.VMEM(pred_all, jnp.bfloat16),
         pltpu.SMEM((2 * planes,), jnp.int32),
-        pltpu.SMEM((4, most + 1), jnp.int32),
+        pltpu.SMEM((4, most + TOGETHER), jnp.int32),
         pltpu.SemaphoreType.DMA((4 + n_own,)),
         pltpu.SemaphoreType.DMA((2 + len(grad_shapes), planes)),
     ]

time: 168 us -> 165 us (0.982)
  starting transfers between devices: 28.4 us -> 26.7 us
    ppermute x14, starting transfers between devices: 11.6 us -> 9.85 us  [across(): return lax.ppermute(value, 'own', [(o, o ^ j) for o in range(n_own)])]
where the time goes in v16:
time: 165 us; the launch traced here: 163 us
  waiting for transfers between devices  95.2 us (58%)
  Pallas kernels  31.2 us (19%)
  starting transfers between devices  26.7 us (16%)
  other arithmetic  4.34 us (3%)
  local copies, waits for them, and re-layouts  4.27 us (3%)
    ppermute x2, waiting for transfers between devices, between_planes(): lax.ppermute(after(value, *first), 'dp', [(0, 1), (1, 0), (2, 3), (3, 2)])  32.5 us
    ppermute x2, waiting for transfers between devices, between_planes(): outer = lax.ppermute(after(two, one, *second), 'dp', [(2, 3), (1, 0)])  23.3 us
    ppermute x14, waiting for transfers between devices, across(): return lax.ppermute(value, 'own', [(o, o ^ j) for o in range(n_own)])  20.2 us
    ppermute x2, waiting for transfers between devices, between_planes(): two = lax.ppermute(value, 'dp', [(0, 2), (1, 3), (2, 0), (3, 1)])  19.2 us
    pallas_call x1, Pallas kernels, local_grads(): pl.pallas_call(body, out_shape=[pred_shape, pred_shape] + grad_shapes, in...  14.6 us
    ppermute x14, starting transfers between devices, across(): return lax.ppermute(value, 'own', [(o, o ^ j) for o in range(n_own)])  9.85 us
    pallas_call x1, Pallas kernels, adam(): pl.pallas_call(body, out_shape=[jax.ShapeDtypeStruct(moment1.shape, jnp.b...  6 us
    pallas_call x2, Pallas kernels, place_weights(): pl.pallas_call(body, out_shape=jax.ShapeDtypeStruct(shape, jnp.bfloat16),...  5.98 us
  transfers between devices with their start and end apart: 23, of which 13 were waited for; matrix products, arithmetic and copies ran while one was open for 3% of the time, Pallas kernels for 5%

profile of v16, /device:TPU:2, one launch (start us, length us, event | category | flops | bytes accessed | tf_op | source)
XLA Modules:
  0.0 162.7 jit_solution(3011220395317834337)
XLA Ops:
  0.6 1.2 dynamic-slice_bitcast_fusion
  1.9 2.4 %pack_rows.1 = (bf16[528,384]{1,0:T(8,128)(2,1)}, bf16[256,256]{1,0:T(8,128)(2,1)}) custom-call(s32[1,256]{1,0:T(1,128)} %bitcast.21, bf16[256,384]{1,0:T(8,128)(2,1)} %sig_ref.1, bf16[256,384]{1,0:T(8,128)(2,1)} %cot_ref.1), custom_call_target="tpu_custom_call" | custom-call | tf_op jit(solution)/shard_map/pack_rows/pallas_call | solution.py:81
  4.3 0.1 pad_maximum_fusion.1.rest_4_
  4.4 1.6 collective-permute-start.4
  6.0 2.6 %collective-permute-start.2 = (bf16[528,384]{1,0:T(8,128)(2,1)S(1)}, bf16[528,384]{1,0:T(8,128)(2,1)S(1)}, u32[]{:S(2)}, u32[]{:S(2)}) collective-permute-start(bf16[528,384]{1,0:T(8,128)(2,1)S(1)} %copy-done.10), channel_id=1, source_target_pairs={{0,16},{8,24},{16,0},{24,8},{1,17},{9,25},{17,1},{25,9},{2,18},{10... | collective-permute-start | bytes 1216520 | tf_op jit(solution)/shard_map/ppermute | solution.py:448
  8.6 1.6 collective-permute-start.1
  10.2 0.5 collective-permute-start.3
  10.7 16.5 %collective-permute-done.2 = bf16[528,384]{1,0:T(8,128)(2,1)S(1)} collective-permute-done((bf16[528,384]{1,0:T(8,128)(2,1)S(1)}, bf16[528,384]{1,0:T(8,128)(2,1)S(1)}, u32[]{:S(2)}, u32[]{:S(2)}) %collective-permute-start.2) | collective-permute-done | bytes 405536 | tf_op jit(solution)/shard_map/ppermute | solution.py:448
  27.2 0.2 collective-permute-done.1
  27.4 0.2 pad_maximum_fusion.rest_0_
  27.7 0.6 collective-permute-start.9
  28.3 0.9 collective-permute-done.3.rest_5_
  29.3 0.7 collective-permute-start.5
  29.9 1.3 collective-permute-start.6
  31.3 1.2 collective-permute-start.8
  32.5 10.3 %collective-permute-done.6 = bf16[528,384]{1,0:T(8,128)(2,1)S(1)} collective-permute-done((bf16[528,384]{1,0:T(8,128)(2,1)S(1)}, bf16[528,384]{1,0:T(8,128)(2,1)S(1)}, u32[]{:S(2)}, u32[]{:S(2)}) %collective-permute-start.6) | collective-permute-done | bytes 405536 | tf_op jit(solution)/shard_map/ppermute | solution.py:450
  42.8 0.1 add.31.rest_1_
  43.1 0.7 copy.13.touched_ref
  43.8 0.7 pad_add_fusion.pos_ref
  44.5 0.3 collective-permute-done.10.rest_3_
  44.8 0.7 copy-done.11
  45.6 14.6 %local_grads.1 = (bf16[4,256,384]{2,1,0:T(8,128)(2,1)}, bf16[4,256,384]{2,1,0:T(8,128)(2,1)}, bf16[2,8,2,48,256]{4,3,2,1,0:T(8,128)(2,1)}, bf16[1,8,2,48,256]{4,...) custom-call(s32[2]{0:T(128)} %pad_add_fusion.pos_ref, ...), custom_call_target="tpu_custom_call" | custom-call | tf_op jit(solution)/shard_map/local_grads/pallas_call | solution.py:266
  60.3 2.6 %collective-permute-start.13 = (bf16[1,8,2,48,256]{4,3,2,1,0:T(8,128)(2,1)}, bf16[1,8,2,48,256]{4,3,2,1,0:T(8,128)(2,1)S(1)}, u32[]{:S(2)}, u32[]{:S(2)}) collective-permute-start(bf16[1,8,2,48,256]{4,3,2,1,0:T(8,128)(2,1)} %get-tuple-element.42), channel_id=1, source_target_pairs={{0,4},{1,5},{2,6},{3,7},{4,0},{5,1},{6,2},{7,3},{8,12},{9,13},{10,... | collective-permute-start | bytes 1179656 | tf_op jit(solution)/shard_map/ppermute | solution.py:498
  63.0 2.3 %add.32 = bf16[4,256,384]{2,1,0:T(8,128)(2,1)} add(bf16[4,256,384]{2,1,0:T(8,128)(2,1)} %get-tuple-element.37, bf16[4,256,384]{2,1,0:T(8,128)(2,1)S(1)} %collective-permute-done.11) | non-fusion elementwise | flops 393216 | bytes 2359296 | tf_op jit(solution)/shard_map/add | solution.py:534
  65.2 4.2 %all-to-all-start = ((bf16[4,256,384]{2,1,0:T(8,128)(2,1)}), bf16[4,256,384]{2,1,0:T(8,128)(2,1)S(1)}, u32[]{:S(2)}, u32[]{:S(2)}) async-start(bf16[4,256,384]{2,1,0:T(8,128)(2,1)} %add.32), calls=%async_computation | async-start | bytes 1572864 | tf_op jit(solution)/shard_map/all_to_all | solution.py:535
  69.4 0.4 collective-permute-start.14
  69.8 0.7 collective-permute-start.15
  70.5 2.3 %collective-permute-done.13 = bf16[1,8,2,48,256]{4,3,2,1,0:T(8,128)(2,1)S(1)} collective-permute-done((bf16[1,8,2,48,256]{4,3,2,1,0:T(8,128)(2,1)}, bf16[1,8,2,48,256]{4,3,2,1,0:T(8,128)(2,1)S(1)}, u32[]{:S(2)}, u32[]{:S(2)}) %collective-permute-start.13) | collective-permute-done | bytes 393248 | tf_op jit(solution)/shard_map/ppermute | solution.py:498
  72.8 0.7 copy-done.18
  73.5 1.0 add_bitcast_fusion
  74.5 5.9 %collective-permute-done.12.refs_1_ = bf16[2,8,2,48,256]{4,3,2,1,0:T(8,128)(2,1)S(1)} collective-permute-done((bf16[2,8,2,48,256]{4,3,2,1,0:T(8,128)(2,1)}, bf16[2,8,2,48,256]{4,3,2,1,0:T(8,128)(2,1)S(1)}, u32[]{:S(2)}, u32[]{:S(2)}) %collective-permute-start.12) | collective-permute-done | bytes 786464 | tf_op jit(solution)/shard_map/ppermute | solution.py:498
  80.5 0.6 collective-permute-done.14.refs_4_
  81.0 1.0 collective-permute-start.16
  82.1 0.8 collective-permute-start.17
  82.9 9.3 %collective-permute-done.16.refs_2_ = bf16[8,2,48,256]{3,2,1,0:T(8,128)(2,1)S(1)} collective-permute-done((bf16[8,2,48,256]{3,2,1,0:T(8,128)(2,1)S(1)}, bf16[8,2,48,256]{3,2,1,0:T(8,128)(2,1)S(1)}, u32[]{:S(2)}, u32[]{:S(2)}) %collective-permute-start.16) | collective-permute-done | bytes 393248 | tf_op jit(solution)/shard_map/ppermute | solution.py:498
  92.2 0.9 collective-permute-done.17.refs_5_
  93.1 0.7 copy-done.15
  93.8 6.0 %adam_step.1 = (bf16[16,2,48,256]{3,2,1,0:T(8,128)(2,1)}, f32[16,2,48,256]{3,2,1,0:T(8,128)}, f32[16,2,48,256]{3,2,1,0:T(8,128)}) custom-call(s32[2]{0:T(128)} %pad_add_fusion.pos_ref, bf16[1,8,2,48,256]{4,3,2,1,0:T(8,128)(2,1)} %get-tuple-element.39.refs_0_, bf16[2,8,2,48,256]{4,3,2,1,0:T(8,128)(2,1)} %copy-done.4, bf16[8,2,48,256]{3,2,1,0:T(8,128)(2,1)} %copy-done.14, ...), custom_call_target="tpu_custom_call" | custom-call | tf_op jit(solution)/shard_map/adam_step/pallas_call | solution.py:359
  99.8 2.3 %collective-permute-start.19 = (bf16[16,2,48,256]{3,2,1,0:T(8,128)(2,1)}, bf16[16,2,48,256]{3,2,1,0:T(8,128)(2,1)S(1)}, u32[]{:S(2)}, u32[]{:S(2)}) collective-permute-start(bf16[16,2,48,256]{3,2,1,0:T(8,128)(2,1)} %get-tuple-element.52.refs_0_), channel_id=1, source_target_pairs={{0,8},{8,0},{16,24},{24,16},{1,9},{9,1},{17,25},{25,17},{2,10},{10... | collective-permute-start | bytes 2359304 | tf_op jit(solution)/shard_map/ppermute | solution.py:449
  102.1 2.3 %collective-permute-start.18 = (bf16[16,2,48,256]{3,2,1,0:T(8,128)(2,1)}, bf16[16,2,48,256]{3,2,1,0:T(8,128)(2,1)S(1)}, u32[]{:S(2)}, u32[]{:S(2)}) collective-permute-start(bf16[16,2,48,256]{3,2,1,0:T(8,128)(2,1)} %get-tuple-element.52.refs_0_), channel_id=1, source_target_pairs={{0,16},{8,24},{16,0},{24,8},{1,17},{9,25},{17,1},{25,9},{2,18},{10... | collective-permute-start | bytes 2359304 | tf_op jit(solution)/shard_map/ppermute | solution.py:448
  104.4 32.3 %collective-permute-done.19.refs_1_ = bf16[16,2,48,256]{3,2,1,0:T(8,128)(2,1)S(1)} collective-permute-done((bf16[16,2,48,256]{3,2,1,0:T(8,128)(2,1)}, bf16[16,2,48,256]{3,2,1,0:T(8,128)(2,1)S(1)}, u32[]{:S(2)}, u32[]{:S(2)}) %collective-permute-start.19) | collective-permute-done | bytes 786464 | tf_op jit(solution)/shard_map/ppermute | solution.py:449
  136.7 2.7 %collective-permute-done.18.refs_2_ = bf16[16,2,48,256]{3,2,1,0:T(8,128)(2,1)S(1)} collective-permute-done((bf16[16,2,48,256]{3,2,1,0:T(8,128)(2,1)}, bf16[16,2,48,256]{3,2,1,0:T(8,128)(2,1)S(1)}, u32[]{:S(2)}, u32[]{:S(2)}) %collective-permute-start.18) | collective-permute-done | bytes 786464 | tf_op jit(solution)/shard_map/ppermute | solution.py:448
  139.4 0.7 collective-permute-start.20
  140.1 1.3 collective-permute-start.21
  141.4 2.2 %finish_predicted.1 = bf16[256,384]{1,0:T(8,128)(2,1)} custom-call(bf16[256,256]{1,0:T(8,128)(2,1)} %get-tuple-element.30.perm_ref, bf16[4,256,384]{2,1,0:T(8,128)(2,1)} %copy-done.2), custom_call_target="tpu_custom_call" | custom-call | tf_op jit(solution)/shard_map/finish_predicted/pallas_call | solution.py:476
  143.6 3.5 %place_weights.2.refs_2_ = bf16[16,2,48,1024]{3,2,1,0:T(8,128)(2,1)} custom-call(s32[2]{0:T(128)} %pad_add_fusion.pos_ref, bf16[16,2,48,256]{3,2,1,0:T(8,128)(2,1)} %get-tuple-element.52.refs_0_, bf16[16,2,48,256]{3,2,1,0:T(8,128)(2,1)} %copy-done.9, bf16[16,2,48,256]{3,2,1,0:T(8,128)(2,1)} %copy-done.8), custom_call_target="tpu_custom_call" | custom-call | tf_op jit(solution)/shard_map/place_weights/pallas_call | solution.py:426
  147.1 13.0 %collective-permute-done.21.refs_1_ = bf16[16,2,48,256]{3,2,1,0:T(8,128)(2,1)S(1)} collective-permute-done((bf16[16,2,48,256]{3,2,1,0:T(8,128)(2,1)S(1)}, bf16[16,2,48,256]{3,2,1,0:T(8,128)(2,1)S(1)}, u32[]{:S(2)}, u32[]{:S(2)}) %collective-permute-start.21) | collective-permute-done | bytes 786464 | tf_op jit(solution)/shard_map/ppermute | solution.py:450
  160.2 2.5 %place_weights.3 = bf16[16,2,48,1024]{3,2,1,0:T(8,128)(2,1)} custom-call(s32[2]{0:T(128)S(1)} %copy-done, bf16[16,2,48,256]{3,2,1,0:T(8,128)(2,1)S(1)} %collective-permute-done.20.refs_0_, bf16[16,2,48,256]{3,2,1,0:T(8,128)(2,1)S(1)} %collective-permute-done.21.refs_1_, bf16[16,2,48,1024]{3,2,1,0:T(8,128)(2,1)} %place_weights.2.refs_2_), custom_call_target="tpu_custom_call", output_to_operand_aliasing={{}: (3, {})} | custom-call | tf_op jit(solution)/shard_map/place_weights/pallas_call | solution.py:426
  (57 shorter events, 0.6 us)
Async XLA Ops:
  1.8 2.5 %collective-permute-start = (bf16[8,2,48,256]{3,2,1,0:T(8,128)(2,1)S(1)}, bf16[8,2,48,256]{3,2,1,0:T(8,128)(2,1)S(1)}, u32[]{:S(2)}, u32[]{:S(2)}) collective-permute-start(bf16[8,2,48,256]{3,2,1,0:T(8,128)(2,1)S(1)} %get-tuple-element.57), channel_id=1, source_target_pairs={{0,1},{1,0},{2,3},{3,2},{4,5},{5,4},{6,7},{7,6},{8,9},{9,8},{10,11... | collective-permute-start | bytes 1179656 | tf_op jit(solution)/shard_map/ppermute | solution.py:498
  4.3 1.7 %copy-start.10 = (bf16[528,384]{1,0:T(8,128)(2,1)S(1)}, bf16[528,384]{1,0:T(8,128)(2,1)}, u32[]{:S(2)}) copy-start(bf16[528,384]{1,0:T(8,128)(2,1)} %get-tuple-element.34) | copy-start | bytes 1216516
  4.4 23.3 %copy-start.3 = (bf16[2,8,2,48,256]{4,3,2,1,0:T(8,128)(2,1)}, bf16[2,8,2,48,256]{4,3,2,1,0:T(8,128)(2,1)S(1)}, u32[]{:S(2)}) copy-start(bf16[2,8,2,48,256]{4,3,2,1,0:T(8,128)(2,1)S(1)} %pad_maximum_fusion.1.rest_4_) | copy-start | bytes 2359300
  4.4 23.2 %collective-permute-start.4 = (bf16[2,8,2,48,256]{4,3,2,1,0:T(8,128)(2,1)S(1)}, bf16[2,8,2,48,256]{4,3,2,1,0:T(8,128)(2,1)S(1)}, u32[]{:S(2)}, u32[]{:S(2)}) collective-permute-start(bf16[2,8,2,48,256]{4,3,2,1,0:T(8,128)(2,1)S(1)} %pad_maximum_fusion.1.rest_4_), channel_id=1, source_target_pairs={{0,4},{1,5},{2,6},{3,7},{4,0},{5,1},{6,2},{7,3},{8,12},{9,13},{10,... | collective-permute-start | bytes 2359304 | tf_op jit(solution)/shard_map/ppermute | solution.py:498
  6.0 21.2 %collective-permute-start.2 = (bf16[528,384]{1,0:T(8,128)(2,1)S(1)}, bf16[528,384]{1,0:T(8,128)(2,1)S(1)}, u32[]{:S(2)}, u32[]{:S(2)}) collective-permute-start(bf16[528,384]{1,0:T(8,128)(2,1)S(1)} %copy-done.10), channel_id=1, source_target_pairs={{0,16},{8,24},{16,0},{24,8},{1,17},{9,25},{17,1},{25,9},{2,18},{10... | collective-permute-start | bytes 1216520 | tf_op jit(solution)/shard_map/ppermute | solution.py:448
  8.6 18.8 %collective-permute-start.1 = (bf16[528,384]{1,0:T(8,128)(2,1)S(1)}, bf16[528,384]{1,0:T(8,128)(2,1)S(1)}, u32[]{:S(2)}, u32[]{:S(2)}) collective-permute-start(bf16[528,384]{1,0:T(8,128)(2,1)S(1)} %copy-done.10), channel_id=1, source_target_pairs={{0,8},{8,0},{16,24},{24,16},{1,9},{9,1},{17,25},{25,17},{2,10},{10... | collective-permute-start | bytes 1216520 | tf_op jit(solution)/shard_map/ppermute | solution.py:449
  10.2 19.1 %collective-permute-start.3 = (bf16[2,8,2,48,256]{4,3,2,1,0:T(8,128)(2,1)S(1)}, bf16[2,8,2,48,256]{4,3,2,1,0:T(8,128)(2,1)S(1)}, u32[]{:S(2)}, u32[]{:S(2)}) collective-permute-start(bf16[2,8,2,48,256]{4,3,2,1,0:T(8,128)(2,1)S(1)} %pad_maximum_fusion.1.rest_4_), channel_id=1, source_target_pairs={{0,2},{1,3},{2,0},{3,1},{4,6},{5,7},{6,4},{7,5},{8,10},{9,11},{10,... | collective-permute-start | bytes 2359304 | tf_op jit(solution)/shard_map/ppermute | solution.py:498
  27.5 17.3 %copy-start.1 = (bf16[3,528,384]{2,1,0:T(8,128)(2,1)}, bf16[3,528,384]{2,1,0:T(8,128)(2,1)S(1)}, u32[]{:S(2)}) copy-start(bf16[3,528,384]{2,1,0:T(8,128)(2,1)S(1)} %pad_maximum_fusion.rest_0_) | copy-start | bytes 3649540
  27.6 15.5 %copy-start.20 = (s32[32,4]{0,1:T(4,128)S(1)}, s32[32,4]{0,1:T(4,128)}, u32[]{:S(2)}) copy-start(s32[32,4]{0,1:T(4,128)} %param.11) | copy-start | bytes 1540
  27.6 17.2 %collective-permute-start.7 = (bf16[3,528,384]{2,1,0:T(8,128)(2,1)S(1)}, bf16[3,528,384]{2,1,0:T(8,128)(2,1)}, u32[]{:S(2)}, u32[]{:S(2)}) collective-permute-start(bf16[3,528,384]{2,1,0:T(8,128)(2,1)S(1)} %pad_maximum_fusion.rest_0_), channel_id=1, source_target_pairs={{0,1},{1,0},{2,3},{3,2},{4,5},{5,4},{6,7},{7,6},{8,9},{9,8},{10,11... | collective-permute-start | bytes 3649544 | tf_op jit(solution)/shard_map/ppermute | solution.py:498
  27.7 17.2 %copy-start.5 = (bf16[2,8,2,48,256]{4,3,2,1,0:T(8,128)(2,1)}, bf16[2,8,2,48,256]{4,3,2,1,0:T(8,128)(2,1)S(1)}, u32[]{:S(2)}) copy-start(bf16[2,8,2,48,256]{4,3,2,1,0:T(8,128)(2,1)S(1)} %collective-permute-done.4.rest_6_) | copy-start | bytes 2359300
  27.7 15.3 %collective-permute-start.9 = (bf16[8,2,48,256]{3,2,1,0:T(8,128)(2,1)S(1)}, bf16[8,2,48,256]{3,2,1,0:T(8,128)(2,1)S(1)}, u32[]{:S(2)}, u32[]{:S(2)}) collective-permute-start(bf16[8,2,48,256]{3,2,1,0:T(8,128)(2,1)S(1)} %slice_bitcast_fusion), channel_id=1, source_target_pairs={{0,2},{1,3},{2,0},{3,1},{4,6},{5,7},{6,4},{7,5},{8,10},{9,11},{10,... | collective-permute-start | bytes 1179656 | tf_op jit(solution)/shard_map/ppermute | solution.py:498
  29.3 2.0 %copy-start.6 = (bf16[2,8,2,48,256]{4,3,2,1,0:T(8,128)(2,1)}, bf16[2,8,2,48,256]{4,3,2,1,0:T(8,128)(2,1)S(1)}, u32[]{:S(2)}) copy-start(bf16[2,8,2,48,256]{4,3,2,1,0:T(8,128)(2,1)S(1)} %collective-permute-done.3.rest_5_) | copy-start | bytes 2359300
  29.3 3.3 %collective-permute-start.5 = (bf16[528,384]{1,0:T(8,128)(2,1)S(1)}, bf16[528,384]{1,0:T(8,128)(2,1)S(1)}, u32[]{:S(2)}, u32[]{:S(2)}) collective-permute-start(bf16[528,384]{1,0:T(8,128)(2,1)S(1)} %copy-done.10), channel_id=1, source_target_pairs={{8,16},{16,8},{9,17},{17,9},{10,18},{18,10},{11,19},{19,11},{12,20... | collective-permute-start | bytes 1216520 | tf_op jit(solution)/shard_map/ppermute | solution.py:451
  29.9 12.9 %collective-permute-start.6 = (bf16[528,384]{1,0:T(8,128)(2,1)S(1)}, bf16[528,384]{1,0:T(8,128)(2,1)S(1)}, u32[]{:S(2)}, u32[]{:S(2)}) collective-permute-start(bf16[528,384]{1,0:T(8,128)(2,1)S(1)} %collective-permute-done.2), channel_id=1, source_target_pairs={{16,24},{8,0},{17,25},{9,1},{18,26},{10,2},{19,27},{11,3},{20,28},... | collective-permute-start | bytes 1216520 | tf_op jit(solution)/shard_map/ppermute | solution.py:450
  31.3 11.7 %collective-permute-start.8 = (bf16[8,2,48,256]{3,2,1,0:T(8,128)(2,1)S(1)}, bf16[8,2,48,256]{3,2,1,0:T(8,128)(2,1)}, u32[]{:S(2)}, u32[]{:S(2)}) collective-permute-start(bf16[8,2,48,256]{3,2,1,0:T(8,128)(2,1)S(1)} %slice_bitcast_fusion.1), channel_id=1, source_target_pairs={{0,4},{1,5},{2,6},{3,7},{4,0},{5,1},{6,2},{7,3},{8,12},{9,13},{10,... | collective-permute-start | bytes 1179656 | tf_op jit(solution)/shard_map/ppermute | solution.py:498
  43.0 1.9 %copy-start.7 = (bf16[528,384]{1,0:T(8,128)(2,1)}, bf16[528,384]{1,0:T(8,128)(2,1)S(1)}, u32[]{:S(2)}) copy-start(bf16[528,384]{1,0:T(8,128)(2,1)S(1)} %add.31.rest_1_) | copy-start | bytes 1216516
  43.0 1.9 %copy-start.19 = (bf16[8,2,48,256]{3,2,1,0:T(8,128)(2,1)}, bf16[8,2,48,256]{3,2,1,0:T(8,128)(2,1)S(1)}, u32[]{:S(2)}) copy-start(bf16[8,2,48,256]{3,2,1,0:T(8,128)(2,1)S(1)} %collective-permute-done.9.rest_8_) | copy-start | bytes 1179652
  43.0 1.8 %collective-permute-start.10 = (bf16[528,384]{1,0:T(8,128)(2,1)S(1)}, bf16[528,384]{1,0:T(8,128)(2,1)S(1)}, u32[]{:S(2)}, u32[]{:S(2)}) collective-permute-start(bf16[528,384]{1,0:T(8,128)(2,1)S(1)} %add.31.rest_1_), channel_id=1, source_target_pairs={{0,1},{1,0},{2,3},{3,2},{4,5},{5,4},{6,7},{7,6},{8,9},{9,8},{10,11... | collective-permute-start | bytes 1216520 | tf_op jit(solution)/shard_map/ppermute | solution.py:498
  44.8 0.8 copy-start.11
  60.2 2.8 %collective-permute-start.11 = (bf16[4,256,384]{2,1,0:T(8,128)(2,1)}, bf16[4,256,384]{2,1,0:T(8,128)(2,1)S(1)}, u32[]{:S(2)}, u32[]{:S(2)}) collective-permute-start(bf16[4,256,384]{2,1,0:T(8,128)(2,1)} %get-tuple-element.38), channel_id=1, source_target_pairs={{0,1},{1,0},{2,3},{3,2},{4,5},{5,4},{6,7},{7,6},{8,9},{9,8},{10,11... | collective-permute-start | bytes 2359304 | tf_op jit(solution)/shard_map/ppermute | solution.py:498
  60.3 20.2 %collective-permute-start.12 = (bf16[2,8,2,48,256]{4,3,2,1,0:T(8,128)(2,1)}, bf16[2,8,2,48,256]{4,3,2,1,0:T(8,128)(2,1)S(1)}, u32[]{:S(2)}, u32[]{:S(2)}) collective-permute-start(bf16[2,8,2,48,256]{4,3,2,1,0:T(8,128)(2,1)} %get-tuple-element.40), channel_id=1, source_target_pairs={{0,2},{1,3},{2,0},{3,1},{4,6},{5,7},{6,4},{7,5},{8,10},{9,11},{10,... | collective-permute-start | bytes 2359304 | tf_op jit(solution)/shard_map/ppermute | solution.py:498
  60.3 12.4 %collective-permute-start.13 = (bf16[1,8,2,48,256]{4,3,2,1,0:T(8,128)(2,1)}, bf16[1,8,2,48,256]{4,3,2,1,0:T(8,128)(2,1)S(1)}, u32[]{:S(2)}, u32[]{:S(2)}) collective-permute-start(bf16[1,8,2,48,256]{4,3,2,1,0:T(8,128)(2,1)} %get-tuple-element.42), channel_id=1, source_target_pairs={{0,4},{1,5},{2,6},{3,7},{4,0},{5,1},{6,2},{7,3},{8,12},{9,13},{10,... | collective-permute-start | bytes 1179656 | tf_op jit(solution)/shard_map/ppermute | solution.py:498
  63.0 10.5 %copy-start.17 = (bf16[1,8,2,48,256]{4,3,2,1,0:T(8,128)(2,1)S(1)}, bf16[1,8,2,48,256]{4,3,2,1,0:T(8,128)(2,1)}, u32[]{:S(2)}) copy-start(bf16[1,8,2,48,256]{4,3,2,1,0:T(8,128)(2,1)} %get-tuple-element.49) | copy-start | bytes 1179652
  65.2 15.2 %copy-start.16 = (bf16[1,8,2,48,256]{4,3,2,1,0:T(8,128)(2,1)S(1)}, bf16[1,8,2,48,256]{4,3,2,1,0:T(8,128)(2,1)}, u32[]{:S(2)}) copy-start(bf16[1,8,2,48,256]{4,3,2,1,0:T(8,128)(2,1)} %get-tuple-element.41) | copy-start | bytes 1179652
  65.2 27.0 %all-to-all-start = ((bf16[4,256,384]{2,1,0:T(8,128)(2,1)}), bf16[4,256,384]{2,1,0:T(8,128)(2,1)S(1)}, u32[]{:S(2)}, u32[]{:S(2)}) async-start(bf16[4,256,384]{2,1,0:T(8,128)(2,1)} %add.32), calls=%async_computation | async-start | bytes 1572864 | tf_op jit(solution)/shard_map/all_to_all | solution.py:535
  69.4 11.6 %collective-permute-start.14 = (bf16[1,8,2,48,256]{4,3,2,1,0:T(8,128)(2,1)}, bf16[1,8,2,48,256]{4,3,2,1,0:T(8,128)(2,1)S(1)}, u32[]{:S(2)}, u32[]{:S(2)}) collective-permute-start(bf16[1,8,2,48,256]{4,3,2,1,0:T(8,128)(2,1)} %get-tuple-element.44), channel_id=1, source_target_pairs={{0,5},{1,4},{2,7},{3,6},{4,1},{5,0},{6,3},{7,2},{8,13},{9,12},{10,... | collective-permute-start | bytes 1179656 | tf_op jit(solution)/shard_map/ppermute | solution.py:498
  69.8 11.2 %collective-permute-start.15 = (bf16[1,8,2,48,256]{4,3,2,1,0:T(8,128)(2,1)}, bf16[1,8,2,48,256]{4,3,2,1,0:T(8,128)(2,1)S(1)}, u32[]{:S(2)}, u32[]{:S(2)}) collective-permute-start(bf16[1,8,2,48,256]{4,3,2,1,0:T(8,128)(2,1)} %get-tuple-element.46), channel_id=1, source_target_pairs={{0,1},{1,0},{2,3},{3,2},{4,5},{5,4},{6,7},{7,6},{8,9},{9,8},{10,11... | collective-permute-start | bytes 1179656 | tf_op jit(solution)/shard_map/ppermute | solution.py:498
  72.8 0.7 copy-start.18
  80.4 12.6 %copy-start.4 = (bf16[2,8,2,48,256]{4,3,2,1,0:T(8,128)(2,1)}, bf16[2,8,2,48,256]{4,3,2,1,0:T(8,128)(2,1)S(1)}, u32[]{:S(2)}) copy-start(bf16[2,8,2,48,256]{4,3,2,1,0:T(8,128)(2,1)S(1)} %collective-permute-done.12.refs_1_) | copy-start | bytes 2359300
  81.0 12.0 %copy-start.12 = (bf16[1,8,2,48,256]{4,3,2,1,0:T(8,128)(2,1)}, bf16[1,8,2,48,256]{4,3,2,1,0:T(8,128)(2,1)S(1)}, u32[]{:S(2)}) copy-start(bf16[1,8,2,48,256]{4,3,2,1,0:T(8,128)(2,1)S(1)} %collective-permute-done.14.refs_4_) | copy-start | bytes 1179652
  81.0 12.0 %copy-start.13 = (bf16[1,8,2,48,256]{4,3,2,1,0:T(8,128)(2,1)}, bf16[1,8,2,48,256]{4,3,2,1,0:T(8,128)(2,1)S(1)}, u32[]{:S(2)}) copy-start(bf16[1,8,2,48,256]{4,3,2,1,0:T(8,128)(2,1)S(1)} %collective-permute-done.15.refs_3_) | copy-start | bytes 1179652
  81.0 11.1 %collective-permute-start.16 = (bf16[8,2,48,256]{3,2,1,0:T(8,128)(2,1)S(1)}, bf16[8,2,48,256]{3,2,1,0:T(8,128)(2,1)S(1)}, u32[]{:S(2)}, u32[]{:S(2)}) collective-permute-start(bf16[8,2,48,256]{3,2,1,0:T(8,128)(2,1)S(1)} %fusion), channel_id=1, source_target_pairs={{0,4},{1,5},{2,6},{3,7},{4,0},{5,1},{6,2},{7,3},{8,12},{9,13},{10,... | collective-permute-start | bytes 1179656 | tf_op jit(solution)/shard_map/ppermute | solution.py:498
  82.1 11.0 %collective-permute-start.17 = (bf16[8,2,48,256]{3,2,1,0:T(8,128)(2,1)S(1)}, bf16[8,2,48,256]{3,2,1,0:T(8,128)(2,1)S(1)}, u32[]{:S(2)}, u32[]{:S(2)}) collective-permute-start(bf16[8,2,48,256]{3,2,1,0:T(8,128)(2,1)S(1)} %add_bitcast_fusion), channel_id=1, source_target_pairs={{0,3},{1,2},{2,1},{3,0},{4,7},{5,6},{6,5},{7,4},{8,11},{9,10},{10,... | collective-permute-start | bytes 1179656 | tf_op jit(solution)/shard_map/ppermute | solution.py:498
  92.2 0.9 copy-start.14
  92.2 7.6 %copy-start.2 = (bf16[4,256,384]{2,1,0:T(8,128)(2,1)}, bf16[4,256,384]{2,1,0:T(8,128)(2,1)S(1)}, u32[]{:S(2)}) copy-start(bf16[4,256,384]{2,1,0:T(8,128)(2,1)S(1)} %all-to-all-done.parts_ref) | copy-start | bytes 2359300
  93.1 0.8 copy-start.15
  99.8 36.9 %collective-permute-start.19 = (bf16[16,2,48,256]{3,2,1,0:T(8,128)(2,1)}, bf16[16,2,48,256]{3,2,1,0:T(8,128)(2,1)S(1)}, u32[]{:S(2)}, u32[]{:S(2)}) collective-permute-start(bf16[16,2,48,256]{3,2,1,0:T(8,128)(2,1)} %get-tuple-element.52.refs_0_), channel_id=1, source_target_pairs={{0,8},{8,0},{16,24},{24,16},{1,9},{9,1},{17,25},{25,17},{2,10},{10... | collective-permute-start | bytes 2359304 | tf_op jit(solution)/shard_map/ppermute | solution.py:449
  102.1 37.3 %collective-permute-start.18 = (bf16[16,2,48,256]{3,2,1,0:T(8,128)(2,1)}, bf16[16,2,48,256]{3,2,1,0:T(8,128)(2,1)S(1)}, u32[]{:S(2)}, u32[]{:S(2)}) collective-permute-start(bf16[16,2,48,256]{3,2,1,0:T(8,128)(2,1)} %get-tuple-element.52.refs_0_), channel_id=1, source_target_pairs={{0,16},{8,24},{16,0},{24,8},{1,17},{9,25},{17,1},{25,9},{2,18},{10... | collective-permute-start | bytes 2359304 | tf_op jit(solution)/shard_map/ppermute | solution.py:448
  136.7 6.9 %copy-start.9 = (bf16[16,2,48,256]{3,2,1,0:T(8,128)(2,1)}, bf16[16,2,48,256]{3,2,1,0:T(8,128)(2,1)S(1)}, u32[]{:S(2)}) copy-start(bf16[16,2,48,256]{3,2,1,0:T(8,128)(2,1)S(1)} %collective-permute-done.19.refs_1_) | copy-start | bytes 2359300
  139.4 4.2 %copy-start.8 = (bf16[16,2,48,256]{3,2,1,0:T(8,128)(2,1)}, bf16[16,2,48,256]{3,2,1,0:T(8,128)(2,1)S(1)}, u32[]{:S(2)}) copy-start(bf16[16,2,48,256]{3,2,1,0:T(8,128)(2,1)S(1)} %collective-permute-done.18.refs_2_) | copy-start | bytes 2359300
  139.4 7.7 %collective-permute-start.20 = (bf16[16,2,48,256]{3,2,1,0:T(8,128)(2,1)}, bf16[16,2,48,256]{3,2,1,0:T(8,128)(2,1)S(1)}, u32[]{:S(2)}, u32[]{:S(2)}) collective-permute-start(bf16[16,2,48,256]{3,2,1,0:T(8,128)(2,1)} %get-tuple-element.52.refs_0_), channel_id=1, source_target_pairs={{8,16},{16,8},{9,17},{17,9},{10,18},{18,10},{11,19},{19,11},{12,20... | collective-permute-start | bytes 2359304 | tf_op jit(solution)/shard_map/ppermute | solution.py:451
  140.1 20.0 %collective-permute-start.21 = (bf16[16,2,48,256]{3,2,1,0:T(8,128)(2,1)S(1)}, bf16[16,2,48,256]{3,2,1,0:T(8,128)(2,1)S(1)}, u32[]{:S(2)}, u32[]{:S(2)}) collective-permute-start(bf16[16,2,48,256]{3,2,1,0:T(8,128)(2,1)S(1)} %collective-permute-done.18.refs_2_), channel_id=1, source_target_pairs={{16,24},{8,0},{17,25},{9,1},{18,26},{10,2},{19,27},{11,3},{20,28},... | collective-permute-start | bytes 2359304 | tf_op jit(solution)/shard_map/ppermute | solution.py:450
  143.6 16.5 %copy-start = (s32[2]{0:T(128)S(1)}, s32[2]{0:T(128)}, u32[]{:S(2)}) copy-start(s32[2]{0:T(128)} %pad_add_fusion.pos_ref) | copy-start | bytes 28

commit v17 on v16

--- a/solution.py
+++ b/solution.py
@@ -13,7 +13,7 @@
 PARTS = 4
 TOGETHER = 4
 VMEM_BYTES = 56 * 2**20
-LAST_VMEM_BYTES = 8 * 2**20
+LAST_VMEM_BYTES = 4 * 2**20
 
 gelu_coef = math.sqrt(2.0 / math.pi)
 cubic_coef = 0.044715
@@ -382,6 +382,7 @@
     number, _, _, width = arrays[0].shape
     n_dp = shape[3] // width
     part = number // PARTS
+    last = bool(before)
 
     def body(pos_ref, *refs):
         ins = refs[: len(arrays)]
@@ -404,25 +405,35 @@
                     pl.when(inner)(lambda made=made: act(made[0]))
                     pl.when(~inner)(lambda made=made: act(made[1]))
 
+        def onto(n, source, rows, sem):
+            columns = pl.ds(pl.multiple_of((dp_at ^ flat[n][0]) * width, 128), width)
+            return pltpu.make_async_copy(source, out_ref.at[rows, :, :, columns], sem)
+
+        if last:
+            every = pl.ds(0, number)
+            copies = [onto(0, ref, every, sem_out.at[0, 0]) for ref in ins]
+            for act in (lambda copy: copy.start(), lambda copy: copy.wait()):
+                if len(copies) == 1:
+                    act(copies[0])
+                else:
+                    pl.when(inner)(lambda act=act: act(copies[0]))
+                    pl.when(~inner)(lambda act=act: act(copies[1]))
+            return
+
         for i in range(PARTS):
             into(lambda copy: copy.start(), i)
         outs = []
         for i in range(PARTS):
             into(lambda copy: copy.wait(), i)
             rows = pl.ds(i * part, part)
-            for n, (plane, _) in enumerate(flat):
-                columns = pl.ds(pl.multiple_of((dp_at ^ plane) * width, 128), width)
-                outs.append(
-                    pltpu.make_async_copy(
-                        held.at[n, rows], out_ref.at[rows, :, :, columns], sem_out.at[i, n]
-                    )
-                )
+            for n in range(len(flat)):
+                outs.append(onto(n, held.at[n, rows], rows, sem_out.at[i, n]))
                 outs[-1].start()
         for copy in outs:
             copy.wait()
 
     anywhere = pl.BlockSpec(memory_space=pl.ANY)
-    held = (len(flat),) + arrays[0].shape
+    held = (1, 16, 128) if last else (len(flat),) + arrays[0].shape
     return pl.pallas_call(
         body,
         out_shape=jax.ShapeDtypeStruct(shape, jnp.bfloat16),
@@ -452,15 +463,15 @@
     return [value, one, two, (middle, outer)]
 
 
-def gather_weights(pos, fresh, dp_at, n_dp):
+def gather_weights(pos, fresh, dp_at, n_dp, first):
     shape = fresh.shape[:3] + (n_dp * fresh.shape[3],)
-    pieces = list(enumerate(between_planes(fresh, dp_at, n_dp)))
+    pieces = list(enumerate(between_planes(fresh, dp_at, n_dp, first)))
     most = place_weights(pos, pieces[:-1], shape, [])
     return place_weights(pos, pieces[-1:], shape, [most])
 
 
 def after(value, *others):
-    return lax.optimization_barrier((value,) + others)[0]
+    return lax.optimization_barrier((value,) + others)[0] if others else value
 
 
 def finish_predicted(perm, parts):
@@ -550,11 +561,11 @@
         ]
         terms = [arrived[0::2], arrived[1::2]]
 
-    predicted = finish_predicted(perm, parts)
     terms[0][-1] = after(terms[0][-1], parts)
 
     fresh, new_moment1, new_moment2 = adam(pos, terms, weights, moment1, moment2)
-    new_weights = gather_weights(pos, fresh, dp_at, n_dp)
+    predicted = finish_predicted(perm, after(parts, fresh))
+    new_weights = gather_weights(pos, fresh, dp_at, n_dp, [predicted])
 
     return (predicted, new_weights, new_moment1, new_moment2)
 

time: 165 us -> 166 us (level)
  waiting for transfers between devices: 95.2 us -> 97.7 us
    ppermute x2, waiting for transfers between devices: 23.3 us -> 25.7 us  [between_planes(): outer = lax.ppermute(after(two, one, *second), 'dp', [(2, 3), (1, 0)])]
  transfers between devices with their start and end apart: 23 -> 23, of which waited for: 13 -> 13; matrix products, arithmetic and copies ran while one was open for 3% -> 3% of each run, Pallas kernels for 5% -> 4%
where the time goes in v17:
time: 166 us; the launch traced here: 164 us
  waiting for transfers between devices  97.7 us (59%)
  Pallas kernels  30.1 us (18%)
  starting transfers between devices  26.5 us (16%)
  other arithmetic  4.34 us (3%)
  local copies, waits for them, and re-layouts  4.27 us (3%)
    ppermute x2, waiting for transfers between devices, between_planes(): lax.ppermute(after(value, *first), 'dp', [(0, 1), (1, 0), (2, 3), (3, 2)])  32.6 us
    ppermute x2, waiting for transfers between devices, between_planes(): outer = lax.ppermute(after(two, one, *second), 'dp', [(2, 3), (1, 0)])  25.7 us
    ppermute x14, waiting for transfers between devices, across(): return lax.ppermute(value, 'own', [(o, o ^ j) for o in range(n_own)])  20.3 us
    ppermute x2, waiting for transfers between devices, between_planes(): two = lax.ppermute(value, 'dp', [(0, 2), (1, 3), (2, 0), (3, 1)])  19.2 us
    pallas_call x1, Pallas kernels, local_grads(): pl.pallas_call(body, out_shape=[pred_shape, pred_shape] + grad_shapes, in...  14.6 us
    ppermute x14, starting transfers between devices, across(): return lax.ppermute(value, 'own', [(o, o ^ j) for o in range(n_own)])  9.81 us
    pallas_call x1, Pallas kernels, adam(): pl.pallas_call(body, out_shape=[jax.ShapeDtypeStruct(moment1.shape, jnp.b...  6 us
    pallas_call x2, Pallas kernels, place_weights(): pl.pallas_call(body, out_shape=jax.ShapeDtypeStruct(shape, jnp.bfloat16),...  4.9 us
  transfers between devices with their start and end apart: 23, of which 13 were waited for; matrix products, arithmetic and copies ran while one was open for 3% of the time, Pallas kernels for 4%

profile of v17, /device:TPU:2, one launch (start us, length us, event | category | flops | bytes accessed | tf_op | source)
XLA Modules:
  0.0 163.8 jit_solution(2003472376657157501)
XLA Ops:
  0.6 1.2 dynamic-slice_bitcast_fusion
  1.9 2.4 %pack_rows.1 = (bf16[528,384]{1,0:T(8,128)(2,1)}, bf16[256,256]{1,0:T(8,128)(2,1)}) custom-call(s32[1,256]{1,0:T(1,128)} %bitcast.21, bf16[256,384]{1,0:T(8,128)(2,1)} %sig_ref.1, bf16[256,384]{1,0:T(8,128)(2,1)} %cot_ref.1), custom_call_target="tpu_custom_call" | custom-call | tf_op jit(solution)/shard_map/pack_rows/pallas_call | solution.py:81
  4.3 0.1 pad_maximum_fusion.1.rest_4_
  4.4 1.6 collective-permute-start.4
  6.0 2.6 %collective-permute-start.2 = (bf16[528,384]{1,0:T(8,128)(2,1)S(1)}, bf16[528,384]{1,0:T(8,128)(2,1)S(1)}, u32[]{:S(2)}, u32[]{:S(2)}) collective-permute-start(bf16[528,384]{1,0:T(8,128)(2,1)S(1)} %copy-done.10), channel_id=1, source_target_pairs={{0,16},{8,24},{16,0},{24,8},{1,17},{9,25},{17,1},{25,9},{2,18},{10... | collective-permute-start | bytes 1216520 | tf_op jit(solution)/shard_map/ppermute | solution.py:459
  8.6 1.6 collective-permute-start.1
  10.2 0.5 collective-permute-start.3
  10.7 16.5 %collective-permute-done.2 = bf16[528,384]{1,0:T(8,128)(2,1)S(1)} collective-permute-done((bf16[528,384]{1,0:T(8,128)(2,1)S(1)}, bf16[528,384]{1,0:T(8,128)(2,1)S(1)}, u32[]{:S(2)}, u32[]{:S(2)}) %collective-permute-start.2) | collective-permute-done | bytes 405536 | tf_op jit(solution)/shard_map/ppermute | solution.py:459
  27.2 0.2 collective-permute-done.1
  27.4 0.2 pad_maximum_fusion.rest_0_
  27.7 0.6 collective-permute-start.9
  28.3 0.9 collective-permute-done.3.rest_5_
  29.3 0.7 collective-permute-start.5
  29.9 1.3 collective-permute-start.6
  31.3 1.2 collective-permute-start.8
  32.5 10.3 %collective-permute-done.6 = bf16[528,384]{1,0:T(8,128)(2,1)S(1)} collective-permute-done((bf16[528,384]{1,0:T(8,128)(2,1)S(1)}, bf16[528,384]{1,0:T(8,128)(2,1)S(1)}, u32[]{:S(2)}, u32[]{:S(2)}) %collective-permute-start.6) | collective-permute-done | bytes 405536 | tf_op jit(solution)/shard_map/ppermute | solution.py:461
  42.8 0.1 add.31.rest_1_
  43.1 0.7 copy.13.touched_ref
  43.8 0.7 pad_add_fusion.pos_ref
  44.5 0.3 collective-permute-done.10.rest_3_
  44.8 0.7 copy-done.11
  45.6 14.6 %local_grads.1 = (bf16[4,256,384]{2,1,0:T(8,128)(2,1)}, bf16[4,256,384]{2,1,0:T(8,128)(2,1)}, bf16[2,8,2,48,256]{4,3,2,1,0:T(8,128)(2,1)}, bf16[1,8,2,48,256]{4,...) custom-call(s32[2]{0:T(128)} %pad_add_fusion.pos_ref, ...), custom_call_target="tpu_custom_call" | custom-call | tf_op jit(solution)/shard_map/local_grads/pallas_call | solution.py:266
  60.3 1.6 collective-permute-start.12
  61.9 1.1 collective-permute-start.13
  63.0 2.3 %add.32 = bf16[4,256,384]{2,1,0:T(8,128)(2,1)} add(bf16[4,256,384]{2,1,0:T(8,128)(2,1)} %get-tuple-element.39, bf16[4,256,384]{2,1,0:T(8,128)(2,1)S(1)} %collective-permute-done.11) | non-fusion elementwise | flops 393216 | bytes 2359296 | tf_op jit(solution)/shard_map/add | solution.py:545
  65.3 4.2 %all-to-all-start = ((bf16[4,256,384]{2,1,0:T(8,128)(2,1)}), bf16[4,256,384]{2,1,0:T(8,128)(2,1)S(1)}, u32[]{:S(2)}, u32[]{:S(2)}) async-start(bf16[4,256,384]{2,1,0:T(8,128)(2,1)} %add.32), calls=%async_computation | async-start | bytes 1572864 | tf_op jit(solution)/shard_map/all_to_all | solution.py:546
  69.4 1.0 collective-permute-start.15
  70.4 2.7 %collective-permute-done.13 = bf16[1,8,2,48,256]{4,3,2,1,0:T(8,128)(2,1)S(1)} collective-permute-done((bf16[1,8,2,48,256]{4,3,2,1,0:T(8,128)(2,1)}, bf16[1,8,2,48,256]{4,3,2,1,0:T(8,128)(2,1)S(1)}, u32[]{:S(2)}, u32[]{:S(2)}) %collective-permute-start.13) | collective-permute-done | bytes 393248 | tf_op jit(solution)/shard_map/ppermute | solution.py:509
  73.2 0.7 copy-done.18
  73.9 1.0 add_bitcast_fusion
  74.9 5.5 %collective-permute-done.12.refs_1_ = bf16[2,8,2,48,256]{4,3,2,1,0:T(8,128)(2,1)S(1)} collective-permute-done((bf16[2,8,2,48,256]{4,3,2,1,0:T(8,128)(2,1)}, bf16[2,8,2,48,256]{4,3,2,1,0:T(8,128)(2,1)S(1)}, u32[]{:S(2)}, u32[]{:S(2)}) %collective-permute-start.12) | collective-permute-done | bytes 786464 | tf_op jit(solution)/shard_map/ppermute | solution.py:509
  80.5 0.6 collective-permute-done.14.refs_4_
  81.1 1.0 collective-permute-start.16
  82.1 0.8 collective-permute-start.17
  82.9 9.4 %collective-permute-done.16.refs_2_ = bf16[8,2,48,256]{3,2,1,0:T(8,128)(2,1)S(1)} collective-permute-done((bf16[8,2,48,256]{3,2,1,0:T(8,128)(2,1)S(1)}, bf16[8,2,48,256]{3,2,1,0:T(8,128)(2,1)S(1)}, u32[]{:S(2)}, u32[]{:S(2)}) %collective-permute-start.16) | collective-permute-done | bytes 393248 | tf_op jit(solution)/shard_map/ppermute | solution.py:509
  92.3 0.8 collective-permute-done.17.refs_5_
  93.1 0.7 copy-done.15
  93.9 6.0 %adam_step.1 = (bf16[16,2,48,256]{3,2,1,0:T(8,128)(2,1)}, f32[16,2,48,256]{3,2,1,0:T(8,128)}, f32[16,2,48,256]{3,2,1,0:T(8,128)}) custom-call(s32[2]{0:T(128)} %pad_add_fusion.pos_ref, bf16[1,8,2,48,256]{4,3,2,1,0:T(8,128)(2,1)} %get-tuple-element.41.refs_0_, bf16[2,8,2,48,256]{4,3,2,1,0:T(8,128)(2,1)} %copy-done.4, bf16[8,2,48,256]{3,2,1,0:T(8,128)(2,1)} %copy-done.14, ...), custom_call_target="tpu_custom_call" | custom-call | tf_op jit(solution)/shard_map/adam_step/pallas_call | solution.py:359
  99.9 2.2 %finish_predicted.1 = bf16[256,384]{1,0:T(8,128)(2,1)} custom-call(bf16[256,256]{1,0:T(8,128)(2,1)} %get-tuple-element.32.perm_ref, bf16[4,256,384]{2,1,0:T(8,128)(2,1)} %copy-done.2), custom_call_target="tpu_custom_call" | custom-call | tf_op jit(solution)/shard_map/finish_predicted/pallas_call | solution.py:487
  102.1 2.2 %collective-permute-start.19 = (bf16[16,2,48,256]{3,2,1,0:T(8,128)(2,1)}, bf16[16,2,48,256]{3,2,1,0:T(8,128)(2,1)S(1)}, u32[]{:S(2)}, u32[]{:S(2)}) collective-permute-start(bf16[16,2,48,256]{3,2,1,0:T(8,128)(2,1)} %get-tuple-element.56.refs_0_), channel_id=1, source_target_pairs={{0,8},{8,0},{16,24},{24,16},{1,9},{9,1},{17,25},{25,17},{2,10},{10... | collective-permute-start | bytes 2359304 | tf_op jit(solution)/shard_map/ppermute | solution.py:460
  104.3 2.2 %collective-permute-start.18 = (bf16[16,2,48,256]{3,2,1,0:T(8,128)(2,1)}, bf16[16,2,48,256]{3,2,1,0:T(8,128)(2,1)S(1)}, u32[]{:S(2)}, u32[]{:S(2)}) collective-permute-start(bf16[16,2,48,256]{3,2,1,0:T(8,128)(2,1)} %get-tuple-element.56.refs_0_), channel_id=1, source_target_pairs={{0,16},{8,24},{16,0},{24,8},{1,17},{9,25},{17,1},{25,9},{2,18},{10... | collective-permute-start | bytes 2359304 | tf_op jit(solution)/shard_map/ppermute | solution.py:459
  106.5 32.4 %collective-permute-done.19.refs_1_ = bf16[16,2,48,256]{3,2,1,0:T(8,128)(2,1)S(1)} collective-permute-done((bf16[16,2,48,256]{3,2,1,0:T(8,128)(2,1)}, bf16[16,2,48,256]{3,2,1,0:T(8,128)(2,1)S(1)}, u32[]{:S(2)}, u32[]{:S(2)}) %collective-permute-start.19) | collective-permute-done | bytes 786464 | tf_op jit(solution)/shard_map/ppermute | solution.py:460
  138.9 2.7 %collective-permute-done.18.refs_2_ = bf16[16,2,48,256]{3,2,1,0:T(8,128)(2,1)S(1)} collective-permute-done((bf16[16,2,48,256]{3,2,1,0:T(8,128)(2,1)}, bf16[16,2,48,256]{3,2,1,0:T(8,128)(2,1)S(1)}, u32[]{:S(2)}, u32[]{:S(2)}) %collective-permute-start.18) | collective-permute-done | bytes 786464 | tf_op jit(solution)/shard_map/ppermute | solution.py:459
  141.5 0.7 collective-permute-start.20
  142.2 1.3 collective-permute-start.21
  143.6 3.4 %place_weights.2.refs_2_ = bf16[16,2,48,1024]{3,2,1,0:T(8,128)(2,1)} custom-call(s32[2]{0:T(128)} %pad_add_fusion.pos_ref, bf16[16,2,48,256]{3,2,1,0:T(8,128)(2,1)} %get-tuple-element.56.refs_0_, bf16[16,2,48,256]{3,2,1,0:T(8,128)(2,1)} %copy-done.9, bf16[16,2,48,256]{3,2,1,0:T(8,128)(2,1)} %copy-done.8), custom_call_target="tpu_custom_call" | custom-call | tf_op jit(solution)/shard_map/place_weights/pallas_call | solution.py:437
  147.0 15.3 %collective-permute-done.21.refs_1_ = bf16[16,2,48,256]{3,2,1,0:T(8,128)(2,1)S(1)} collective-permute-done((bf16[16,2,48,256]{3,2,1,0:T(8,128)(2,1)S(1)}, bf16[16,2,48,256]{3,2,1,0:T(8,128)(2,1)S(1)}, u32[]{:S(2)}, u32[]{:S(2)}) %collective-permute-start.21) | collective-permute-done | bytes 786464 | tf_op jit(solution)/shard_map/ppermute | solution.py:461
  162.3 1.5 place_weights.3
  (57 shorter events, 0.5 us)
Async XLA Ops:
  1.8 2.5 %collective-permute-start = (bf16[8,2,48,256]{3,2,1,0:T(8,128)(2,1)S(1)}, bf16[8,2,48,256]{3,2,1,0:T(8,128)(2,1)S(1)}, u32[]{:S(2)}, u32[]{:S(2)}) collective-permute-start(bf16[8,2,48,256]{3,2,1,0:T(8,128)(2,1)S(1)} %get-tuple-element.61), channel_id=1, source_target_pairs={{0,1},{1,0},{2,3},{3,2},{4,5},{5,4},{6,7},{7,6},{8,9},{9,8},{10,11... | collective-permute-start | bytes 1179656 | tf_op jit(solution)/shard_map/ppermute | solution.py:509
  4.3 1.7 %copy-start.10 = (bf16[528,384]{1,0:T(8,128)(2,1)S(1)}, bf16[528,384]{1,0:T(8,128)(2,1)}, u32[]{:S(2)}) copy-start(bf16[528,384]{1,0:T(8,128)(2,1)} %get-tuple-element.36) | copy-start | bytes 1216516
  4.4 23.3 %copy-start.3 = (bf16[2,8,2,48,256]{4,3,2,1,0:T(8,128)(2,1)}, bf16[2,8,2,48,256]{4,3,2,1,0:T(8,128)(2,1)S(1)}, u32[]{:S(2)}) copy-start(bf16[2,8,2,48,256]{4,3,2,1,0:T(8,128)(2,1)S(1)} %pad_maximum_fusion.1.rest_4_) | copy-start | bytes 2359300
  4.4 23.2 %collective-permute-start.4 = (bf16[2,8,2,48,256]{4,3,2,1,0:T(8,128)(2,1)S(1)}, bf16[2,8,2,48,256]{4,3,2,1,0:T(8,128)(2,1)S(1)}, u32[]{:S(2)}, u32[]{:S(2)}) collective-permute-start(bf16[2,8,2,48,256]{4,3,2,1,0:T(8,128)(2,1)S(1)} %pad_maximum_fusion.1.rest_4_), channel_id=1, source_target_pairs={{0,4},{1,5},{2,6},{3,7},{4,0},{5,1},{6,2},{7,3},{8,12},{9,13},{10,... | collective-permute-start | bytes 2359304 | tf_op jit(solution)/shard_map/ppermute | solution.py:509
  6.0 21.2 %collective-permute-start.2 = (bf16[528,384]{1,0:T(8,128)(2,1)S(1)}, bf16[528,384]{1,0:T(8,128)(2,1)S(1)}, u32[]{:S(2)}, u32[]{:S(2)}) collective-permute-start(bf16[528,384]{1,0:T(8,128)(2,1)S(1)} %copy-done.10), channel_id=1, source_target_pairs={{0,16},{8,24},{16,0},{24,8},{1,17},{9,25},{17,1},{25,9},{2,18},{10... | collective-permute-start | bytes 1216520 | tf_op jit(solution)/shard_map/ppermute | solution.py:459
  8.6 18.8 %collective-permute-start.1 = (bf16[528,384]{1,0:T(8,128)(2,1)S(1)}, bf16[528,384]{1,0:T(8,128)(2,1)S(1)}, u32[]{:S(2)}, u32[]{:S(2)}) collective-permute-start(bf16[528,384]{1,0:T(8,128)(2,1)S(1)} %copy-done.10), channel_id=1, source_target_pairs={{0,8},{8,0},{16,24},{24,16},{1,9},{9,1},{17,25},{25,17},{2,10},{10... | collective-permute-start | bytes 1216520 | tf_op jit(solution)/shard_map/ppermute | solution.py:460
  10.2 19.1 %collective-permute-start.3 = (bf16[2,8,2,48,256]{4,3,2,1,0:T(8,128)(2,1)S(1)}, bf16[2,8,2,48,256]{4,3,2,1,0:T(8,128)(2,1)S(1)}, u32[]{:S(2)}, u32[]{:S(2)}) collective-permute-start(bf16[2,8,2,48,256]{4,3,2,1,0:T(8,128)(2,1)S(1)} %pad_maximum_fusion.1.rest_4_), channel_id=1, source_target_pairs={{0,2},{1,3},{2,0},{3,1},{4,6},{5,7},{6,4},{7,5},{8,10},{9,11},{10,... | collective-permute-start | bytes 2359304 | tf_op jit(solution)/shard_map/ppermute | solution.py:509
  27.5 17.3 %copy-start.1 = (bf16[3,528,384]{2,1,0:T(8,128)(2,1)}, bf16[3,528,384]{2,1,0:T(8,128)(2,1)S(1)}, u32[]{:S(2)}) copy-start(bf16[3,528,384]{2,1,0:T(8,128)(2,1)S(1)} %pad_maximum_fusion.rest_0_) | copy-start | bytes 3649540
  27.6 15.5 %copy-start.20 = (s32[32,4]{0,1:T(4,128)S(1)}, s32[32,4]{0,1:T(4,128)}, u32[]{:S(2)}) copy-start(s32[32,4]{0,1:T(4,128)} %param.11) | copy-start | bytes 1540
  27.6 17.2 %collective-permute-start.7 = (bf16[3,528,384]{2,1,0:T(8,128)(2,1)S(1)}, bf16[3,528,384]{2,1,0:T(8,128)(2,1)}, u32[]{:S(2)}, u32[]{:S(2)}) collective-permute-start(bf16[3,528,384]{2,1,0:T(8,128)(2,1)S(1)} %pad_maximum_fusion.rest_0_), channel_id=1, source_target_pairs={{0,1},{1,0},{2,3},{3,2},{4,5},{5,4},{6,7},{7,6},{8,9},{9,8},{10,11... | collective-permute-start | bytes 3649544 | tf_op jit(solution)/shard_map/ppermute | solution.py:509
  27.7 17.2 %copy-start.5 = (bf16[2,8,2,48,256]{4,3,2,1,0:T(8,128)(2,1)}, bf16[2,8,2,48,256]{4,3,2,1,0:T(8,128)(2,1)S(1)}, u32[]{:S(2)}) copy-start(bf16[2,8,2,48,256]{4,3,2,1,0:T(8,128)(2,1)S(1)} %collective-permute-done.4.rest_6_) | copy-start | bytes 2359300
  27.7 15.3 %collective-permute-start.9 = (bf16[8,2,48,256]{3,2,1,0:T(8,128)(2,1)S(1)}, bf16[8,2,48,256]{3,2,1,0:T(8,128)(2,1)S(1)}, u32[]{:S(2)}, u32[]{:S(2)}) collective-permute-start(bf16[8,2,48,256]{3,2,1,0:T(8,128)(2,1)S(1)} %slice_bitcast_fusion), channel_id=1, source_target_pairs={{0,2},{1,3},{2,0},{3,1},{4,6},{5,7},{6,4},{7,5},{8,10},{9,11},{10,... | collective-permute-start | bytes 1179656 | tf_op jit(solution)/shard_map/ppermute | solution.py:509
  29.3 2.0 %copy-start.6 = (bf16[2,8,2,48,256]{4,3,2,1,0:T(8,128)(2,1)}, bf16[2,8,2,48,256]{4,3,2,1,0:T(8,128)(2,1)S(1)}, u32[]{:S(2)}) copy-start(bf16[2,8,2,48,256]{4,3,2,1,0:T(8,128)(2,1)S(1)} %collective-permute-done.3.rest_5_) | copy-start | bytes 2359300
  29.3 3.3 %collective-permute-start.5 = (bf16[528,384]{1,0:T(8,128)(2,1)S(1)}, bf16[528,384]{1,0:T(8,128)(2,1)S(1)}, u32[]{:S(2)}, u32[]{:S(2)}) collective-permute-start(bf16[528,384]{1,0:T(8,128)(2,1)S(1)} %copy-done.10), channel_id=1, source_target_pairs={{8,16},{16,8},{9,17},{17,9},{10,18},{18,10},{11,19},{19,11},{12,20... | collective-permute-start | bytes 1216520 | tf_op jit(solution)/shard_map/ppermute | solution.py:462
  29.9 12.9 %collective-permute-start.6 = (bf16[528,384]{1,0:T(8,128)(2,1)S(1)}, bf16[528,384]{1,0:T(8,128)(2,1)S(1)}, u32[]{:S(2)}, u32[]{:S(2)}) collective-permute-start(bf16[528,384]{1,0:T(8,128)(2,1)S(1)} %collective-permute-done.2), channel_id=1, source_target_pairs={{16,24},{8,0},{17,25},{9,1},{18,26},{10,2},{19,27},{11,3},{20,28},... | collective-permute-start | bytes 1216520 | tf_op jit(solution)/shard_map/ppermute | solution.py:461
  31.3 11.7 %collective-permute-start.8 = (bf16[8,2,48,256]{3,2,1,0:T(8,128)(2,1)S(1)}, bf16[8,2,48,256]{3,2,1,0:T(8,128)(2,1)}, u32[]{:S(2)}, u32[]{:S(2)}) collective-permute-start(bf16[8,2,48,256]{3,2,1,0:T(8,128)(2,1)S(1)} %slice_bitcast_fusion.1), channel_id=1, source_target_pairs={{0,4},{1,5},{2,6},{3,7},{4,0},{5,1},{6,2},{7,3},{8,12},{9,13},{10,... | collective-permute-start | bytes 1179656 | tf_op jit(solution)/shard_map/ppermute | solution.py:509
  43.0 1.9 %copy-start.7 = (bf16[528,384]{1,0:T(8,128)(2,1)}, bf16[528,384]{1,0:T(8,128)(2,1)S(1)}, u32[]{:S(2)}) copy-start(bf16[528,384]{1,0:T(8,128)(2,1)S(1)} %add.31.rest_1_) | copy-start | bytes 1216516
  43.0 1.9 %copy-start.19 = (bf16[8,2,48,256]{3,2,1,0:T(8,128)(2,1)}, bf16[8,2,48,256]{3,2,1,0:T(8,128)(2,1)S(1)}, u32[]{:S(2)}) copy-start(bf16[8,2,48,256]{3,2,1,0:T(8,128)(2,1)S(1)} %collective-permute-done.9.rest_8_) | copy-start | bytes 1179652
  43.0 1.8 %collective-permute-start.10 = (bf16[528,384]{1,0:T(8,128)(2,1)S(1)}, bf16[528,384]{1,0:T(8,128)(2,1)S(1)}, u32[]{:S(2)}, u32[]{:S(2)}) collective-permute-start(bf16[528,384]{1,0:T(8,128)(2,1)S(1)} %add.31.rest_1_), channel_id=1, source_target_pairs={{0,1},{1,0},{2,3},{3,2},{4,5},{5,4},{6,7},{7,6},{8,9},{9,8},{10,11... | collective-permute-start | bytes 1216520 | tf_op jit(solution)/shard_map/ppermute | solution.py:509
  44.8 0.8 copy-start.11
  60.2 2.8 %collective-permute-start.11 = (bf16[4,256,384]{2,1,0:T(8,128)(2,1)}, bf16[4,256,384]{2,1,0:T(8,128)(2,1)S(1)}, u32[]{:S(2)}, u32[]{:S(2)}) collective-permute-start(bf16[4,256,384]{2,1,0:T(8,128)(2,1)} %get-tuple-element.40), channel_id=1, source_target_pairs={{0,1},{1,0},{2,3},{3,2},{4,5},{5,4},{6,7},{7,6},{8,9},{9,8},{10,11... | collective-permute-start | bytes 2359304 | tf_op jit(solution)/shard_map/ppermute | solution.py:509
  60.3 20.2 %collective-permute-start.12 = (bf16[2,8,2,48,256]{4,3,2,1,0:T(8,128)(2,1)}, bf16[2,8,2,48,256]{4,3,2,1,0:T(8,128)(2,1)S(1)}, u32[]{:S(2)}, u32[]{:S(2)}) collective-permute-start(bf16[2,8,2,48,256]{4,3,2,1,0:T(8,128)(2,1)} %get-tuple-element.42), channel_id=1, source_target_pairs={{0,2},{1,3},{2,0},{3,1},{4,6},{5,7},{6,4},{7,5},{8,10},{9,11},{10,... | collective-permute-start | bytes 2359304 | tf_op jit(solution)/shard_map/ppermute | solution.py:509
  61.9 11.3 %collective-permute-start.13 = (bf16[1,8,2,48,256]{4,3,2,1,0:T(8,128)(2,1)}, bf16[1,8,2,48,256]{4,3,2,1,0:T(8,128)(2,1)S(1)}, u32[]{:S(2)}, u32[]{:S(2)}) collective-permute-start(bf16[1,8,2,48,256]{4,3,2,1,0:T(8,128)(2,1)} %get-tuple-element.44), channel_id=1, source_target_pairs={{0,4},{1,5},{2,6},{3,7},{4,0},{5,1},{6,2},{7,3},{8,12},{9,13},{10,... | collective-permute-start | bytes 1179656 | tf_op jit(solution)/shard_map/ppermute | solution.py:509
  63.0 10.9 %copy-start.17 = (bf16[1,8,2,48,256]{4,3,2,1,0:T(8,128)(2,1)S(1)}, bf16[1,8,2,48,256]{4,3,2,1,0:T(8,128)(2,1)}, u32[]{:S(2)}) copy-start(bf16[1,8,2,48,256]{4,3,2,1,0:T(8,128)(2,1)} %get-tuple-element.51) | copy-start | bytes 1179652
  65.3 15.2 %copy-start.16 = (bf16[1,8,2,48,256]{4,3,2,1,0:T(8,128)(2,1)S(1)}, bf16[1,8,2,48,256]{4,3,2,1,0:T(8,128)(2,1)}, u32[]{:S(2)}) copy-start(bf16[1,8,2,48,256]{4,3,2,1,0:T(8,128)(2,1)} %get-tuple-element.43) | copy-start | bytes 1179652
  65.3 27.0 %all-to-all-start = ((bf16[4,256,384]{2,1,0:T(8,128)(2,1)}), bf16[4,256,384]{2,1,0:T(8,128)(2,1)S(1)}, u32[]{:S(2)}, u32[]{:S(2)}) async-start(bf16[4,256,384]{2,1,0:T(8,128)(2,1)} %add.32), calls=%async_computation | async-start | bytes 1572864 | tf_op jit(solution)/shard_map/all_to_all | solution.py:546
  69.4 11.7 %collective-permute-start.14 = (bf16[1,8,2,48,256]{4,3,2,1,0:T(8,128)(2,1)}, bf16[1,8,2,48,256]{4,3,2,1,0:T(8,128)(2,1)S(1)}, u32[]{:S(2)}, u32[]{:S(2)}) collective-permute-start(bf16[1,8,2,48,256]{4,3,2,1,0:T(8,128)(2,1)} %get-tuple-element.46), channel_id=1, source_target_pairs={{0,5},{1,4},{2,7},{3,6},{4,1},{5,0},{6,3},{7,2},{8,13},{9,12},{10,... | collective-permute-start | bytes 1179656 | tf_op jit(solution)/shard_map/ppermute | solution.py:509
  69.4 11.7 %collective-permute-start.15 = (bf16[1,8,2,48,256]{4,3,2,1,0:T(8,128)(2,1)}, bf16[1,8,2,48,256]{4,3,2,1,0:T(8,128)(2,1)S(1)}, u32[]{:S(2)}, u32[]{:S(2)}) collective-permute-start(bf16[1,8,2,48,256]{4,3,2,1,0:T(8,128)(2,1)} %get-tuple-element.48), channel_id=1, source_target_pairs={{0,1},{1,0},{2,3},{3,2},{4,5},{5,4},{6,7},{7,6},{8,9},{9,8},{10,11... | collective-permute-start | bytes 1179656 | tf_op jit(solution)/shard_map/ppermute | solution.py:509
  73.2 0.7 copy-start.18
  80.4 12.7 %copy-start.4 = (bf16[2,8,2,48,256]{4,3,2,1,0:T(8,128)(2,1)}, bf16[2,8,2,48,256]{4,3,2,1,0:T(8,128)(2,1)S(1)}, u32[]{:S(2)}) copy-start(bf16[2,8,2,48,256]{4,3,2,1,0:T(8,128)(2,1)S(1)} %collective-permute-done.12.refs_1_) | copy-start | bytes 2359300
  81.1 12.0 %copy-start.12 = (bf16[1,8,2,48,256]{4,3,2,1,0:T(8,128)(2,1)}, bf16[1,8,2,48,256]{4,3,2,1,0:T(8,128)(2,1)S(1)}, u32[]{:S(2)}) copy-start(bf16[1,8,2,48,256]{4,3,2,1,0:T(8,128)(2,1)S(1)} %collective-permute-done.14.refs_4_) | copy-start | bytes 1179652
  81.1 12.0 %copy-start.13 = (bf16[1,8,2,48,256]{4,3,2,1,0:T(8,128)(2,1)}, bf16[1,8,2,48,256]{4,3,2,1,0:T(8,128)(2,1)S(1)}, u32[]{:S(2)}) copy-start(bf16[1,8,2,48,256]{4,3,2,1,0:T(8,128)(2,1)S(1)} %collective-permute-done.15.refs_3_) | copy-start | bytes 1179652
  81.1 11.2 %collective-permute-start.16 = (bf16[8,2,48,256]{3,2,1,0:T(8,128)(2,1)S(1)}, bf16[8,2,48,256]{3,2,1,0:T(8,128)(2,1)S(1)}, u32[]{:S(2)}, u32[]{:S(2)}) collective-permute-start(bf16[8,2,48,256]{3,2,1,0:T(8,128)(2,1)S(1)} %fusion), channel_id=1, source_target_pairs={{0,4},{1,5},{2,6},{3,7},{4,0},{5,1},{6,2},{7,3},{8,12},{9,13},{10,... | collective-permute-start | bytes 1179656 | tf_op jit(solution)/shard_map/ppermute | solution.py:509
  82.1 11.0 %collective-permute-start.17 = (bf16[8,2,48,256]{3,2,1,0:T(8,128)(2,1)S(1)}, bf16[8,2,48,256]{3,2,1,0:T(8,128)(2,1)S(1)}, u32[]{:S(2)}, u32[]{:S(2)}) collective-permute-start(bf16[8,2,48,256]{3,2,1,0:T(8,128)(2,1)S(1)} %add_bitcast_fusion), channel_id=1, source_target_pairs={{0,3},{1,2},{2,1},{3,0},{4,7},{5,6},{6,5},{7,4},{8,11},{9,10},{10,... | collective-permute-start | bytes 1179656 | tf_op jit(solution)/shard_map/ppermute | solution.py:509
  92.3 0.8 copy-start.14
  92.3 7.6 %copy-start.2 = (bf16[4,256,384]{2,1,0:T(8,128)(2,1)}, bf16[4,256,384]{2,1,0:T(8,128)(2,1)S(1)}, u32[]{:S(2)}) copy-start(bf16[4,256,384]{2,1,0:T(8,128)(2,1)S(1)} %all-to-all-done.parts_ref) | copy-start | bytes 2359300
  93.1 0.8 copy-start.15
  102.1 60.3 %copy-start = (s32[2]{0:T(128)S(1)}, s32[2]{0:T(128)}, u32[]{:S(2)}) copy-start(s32[2]{0:T(128)} %pad_add_fusion.pos_ref) | copy-start | bytes 28
  102.1 36.8 %collective-permute-start.19 = (bf16[16,2,48,256]{3,2,1,0:T(8,128)(2,1)}, bf16[16,2,48,256]{3,2,1,0:T(8,128)(2,1)S(1)}, u32[]{:S(2)}, u32[]{:S(2)}) collective-permute-start(bf16[16,2,48,256]{3,2,1,0:T(8,128)(2,1)} %get-tuple-element.56.refs_0_), channel_id=1, source_target_pairs={{0,8},{8,0},{16,24},{24,16},{1,9},{9,1},{17,25},{25,17},{2,10},{10... | collective-permute-start | bytes 2359304 | tf_op jit(solution)/shard_map/ppermute | solution.py:460
  104.3 37.3 %collective-permute-start.18 = (bf16[16,2,48,256]{3,2,1,0:T(8,128)(2,1)}, bf16[16,2,48,256]{3,2,1,0:T(8,128)(2,1)S(1)}, u32[]{:S(2)}, u32[]{:S(2)}) collective-permute-start(bf16[16,2,48,256]{3,2,1,0:T(8,128)(2,1)} %get-tuple-element.56.refs_0_), channel_id=1, source_target_pairs={{0,16},{8,24},{16,0},{24,8},{1,17},{9,25},{17,1},{25,9},{2,18},{10... | collective-permute-start | bytes 2359304 | tf_op jit(solution)/shard_map/ppermute | solution.py:459
  138.9 4.7 %copy-start.9 = (bf16[16,2,48,256]{3,2,1,0:T(8,128)(2,1)}, bf16[16,2,48,256]{3,2,1,0:T(8,128)(2,1)S(1)}, u32[]{:S(2)}) copy-start(bf16[16,2,48,256]{3,2,1,0:T(8,128)(2,1)S(1)} %collective-permute-done.19.refs_1_) | copy-start | bytes 2359300
  141.5 2.0 %copy-start.8 = (bf16[16,2,48,256]{3,2,1,0:T(8,128)(2,1)}, bf16[16,2,48,256]{3,2,1,0:T(8,128)(2,1)S(1)}, u32[]{:S(2)}) copy-start(bf16[16,2,48,256]{3,2,1,0:T(8,128)(2,1)S(1)} %collective-permute-done.18.refs_2_) | copy-start | bytes 2359300
  141.5 5.4 %collective-permute-start.20 = (bf16[16,2,48,256]{3,2,1,0:T(8,128)(2,1)}, bf16[16,2,48,256]{3,2,1,0:T(8,128)(2,1)S(1)}, u32[]{:S(2)}, u32[]{:S(2)}) collective-permute-start(bf16[16,2,48,256]{3,2,1,0:T(8,128)(2,1)} %get-tuple-element.56.refs_0_), channel_id=1, source_target_pairs={{8,16},{16,8},{9,17},{17,9},{10,18},{18,10},{11,19},{19,11},{12,20... | collective-permute-start | bytes 2359304 | tf_op jit(solution)/shard_map/ppermute | solution.py:462
  142.2 20.1 %collective-permute-start.21 = (bf16[16,2,48,256]{3,2,1,0:T(8,128)(2,1)S(1)}, bf16[16,2,48,256]{3,2,1,0:T(8,128)(2,1)S(1)}, u32[]{:S(2)}, u32[]{:S(2)}) collective-permute-start(bf16[16,2,48,256]{3,2,1,0:T(8,128)(2,1)S(1)} %collective-permute-done.18.refs_2_), channel_id=1, source_target_pairs={{16,24},{8,0},{17,25},{9,1},{18,26},{10,2},{19,27},{11,3},{20,28},... | collective-permute-start | bytes 2359304 | tf_op jit(solution)/shard_map/ppermute | solution.py:461

commit v18 on v17

--- a/solution.py
+++ b/solution.py
@@ -10,7 +10,7 @@
 SITES = 384
 CAP = 128
 ID_ROWS = 16
-PARTS = 4
+PARTS = 2
 TOGETHER = 4
 VMEM_BYTES = 56 * 2**20
 LAST_VMEM_BYTES = 4 * 2**20
@@ -463,9 +463,9 @@
     return [value, one, two, (middle, outer)]
 
 
-def gather_weights(pos, fresh, dp_at, n_dp, first):
+def gather_weights(pos, fresh, dp_at, n_dp):
     shape = fresh.shape[:3] + (n_dp * fresh.shape[3],)
-    pieces = list(enumerate(between_planes(fresh, dp_at, n_dp, first)))
+    pieces = list(enumerate(between_planes(fresh, dp_at, n_dp)))
     most = place_weights(pos, pieces[:-1], shape, [])
     return place_weights(pos, pieces[-1:], shape, [most])
 
@@ -561,11 +561,11 @@
         ]
         terms = [arrived[0::2], arrived[1::2]]
 
+    predicted = finish_predicted(perm, parts)
     terms[0][-1] = after(terms[0][-1], parts)
 
     fresh, new_moment1, new_moment2 = adam(pos, terms, weights, moment1, moment2)
-    predicted = finish_predicted(perm, after(parts, fresh))
-    new_weights = gather_weights(pos, fresh, dp_at, n_dp, [predicted])
+    new_weights = gather_weights(pos, fresh, dp_at, n_dp)
 
     return (predicted, new_weights, new_moment1, new_moment2)
 

time: 166 us -> 163 us (0.982)
  Pallas kernels: 30.1 us -> 28 us
    ppermute x2, waiting for transfers between devices: 19.2 us -> 16.5 us  [between_planes(): two = lax.ppermute(value, 'dp', [(0, 2), (1, 3), (2, 0), (3, 1)])]
    pallas_call x1, Pallas kernels: 14.6 us -> 12.9 us  [local_grads(): pl.pallas_call(body, out_shape=[pred_shape, pred_shape] + grad_shapes, in...]
  transfers between devices with their start and end apart: 23 -> 23, of which waited for: 13 -> 13; matrix products, arithmetic and copies ran while one was open for 3% -> 3% of each run, Pallas kernels for 4% -> 5%
where the time goes in v18:
time: 163 us; the launch traced here: 161 us
  waiting for transfers between devices  96.2 us (59%)
  Pallas kernels  28 us (17%)
  starting transfers between devices  27 us (17%)
  other arithmetic  4.34 us (3%)
  local copies, waits for them, and re-layouts  4.27 us (3%)
    ppermute x2, waiting for transfers between devices, between_planes(): lax.ppermute(after(value, *first), 'dp', [(0, 1), (1, 0), (2, 3), (3, 2)])  32.9 us
    ppermute x2, waiting for transfers between devices, between_planes(): outer = lax.ppermute(after(two, one, *second), 'dp', [(2, 3), (1, 0)])  25.5 us
    ppermute x14, waiting for transfers between devices, across(): return lax.ppermute(value, 'own', [(o, o ^ j) for o in range(n_own)])  21.4 us
    ppermute x2, waiting for transfers between devices, between_planes(): two = lax.ppermute(value, 'dp', [(0, 2), (1, 3), (2, 0), (3, 1)])  16.5 us
    pallas_call x1, Pallas kernels, local_grads(): pl.pallas_call(body, out_shape=[pred_shape, pred_shape] + grad_shapes, in...  12.9 us
    ppermute x14, starting transfers between devices, across(): return lax.ppermute(value, 'own', [(o, o ^ j) for o in range(n_own)])  10.6 us
    pallas_call x1, Pallas kernels, adam(): pl.pallas_call(body, out_shape=[jax.ShapeDtypeStruct(moment1.shape, jnp.b...  5.59 us
    ppermute x2, starting transfers between devices, between_planes(): two = lax.ppermute(value, 'dp', [(0, 2), (1, 3), (2, 0), (3, 1)])  4.94 us
  transfers between devices with their start and end apart: 23, of which 13 were waited for; matrix products, arithmetic and copies ran while one was open for 3% of the time, Pallas kernels for 5%

profile of v18, /device:TPU:2, one launch (start us, length us, event | category | flops | bytes accessed | tf_op | source)
XLA Modules:
  0.0 160.8 jit_solution(11076598146808055431)
XLA Ops:
  0.6 1.2 dynamic-slice_bitcast_fusion
  1.9 2.4 %pack_rows.1 = (bf16[528,384]{1,0:T(8,128)(2,1)}, bf16[256,256]{1,0:T(8,128)(2,1)}) custom-call(s32[1,256]{1,0:T(1,128)} %bitcast.21, bf16[256,384]{1,0:T(8,128)(2,1)} %sig_ref.1, bf16[256,384]{1,0:T(8,128)(2,1)} %cot_ref.1), custom_call_target="tpu_custom_call" | custom-call | tf_op jit(solution)/shard_map/pack_rows/pallas_call | solution.py:81
  4.4 1.6 collective-permute-start.4
  6.0 2.6 %collective-permute-start.2 = (bf16[528,384]{1,0:T(8,128)(2,1)S(1)}, bf16[528,384]{1,0:T(8,128)(2,1)S(1)}, u32[]{:S(2)}, u32[]{:S(2)}) collective-permute-start(bf16[528,384]{1,0:T(8,128)(2,1)S(1)} %copy-done.10), channel_id=1, source_target_pairs={{0,16},{8,24},{16,0},{24,8},{1,17},{9,25},{17,1},{25,9},{2,18},{10... | collective-permute-start | bytes 1216520 | tf_op jit(solution)/shard_map/ppermute | solution.py:459
  8.6 1.6 collective-permute-start.1
  10.2 0.5 collective-permute-start.3
  10.7 16.5 %collective-permute-done.2 = bf16[528,384]{1,0:T(8,128)(2,1)S(1)} collective-permute-done((bf16[528,384]{1,0:T(8,128)(2,1)S(1)}, bf16[528,384]{1,0:T(8,128)(2,1)S(1)}, u32[]{:S(2)}, u32[]{:S(2)}) %collective-permute-start.2) | collective-permute-done | bytes 405536 | tf_op jit(solution)/shard_map/ppermute | solution.py:459
  27.2 0.2 collective-permute-done.1
  27.4 0.2 pad_maximum_fusion.rest_0_
  27.7 0.6 collective-permute-start.9
  28.3 0.9 collective-permute-done.3.rest_5_
  29.3 0.7 collective-permute-start.5
  29.9 1.3 collective-permute-start.6
  31.3 1.2 collective-permute-start.8
  32.5 10.3 %collective-permute-done.6 = bf16[528,384]{1,0:T(8,128)(2,1)S(1)} collective-permute-done((bf16[528,384]{1,0:T(8,128)(2,1)S(1)}, bf16[528,384]{1,0:T(8,128)(2,1)S(1)}, u32[]{:S(2)}, u32[]{:S(2)}) %collective-permute-start.6) | collective-permute-done | bytes 405536 | tf_op jit(solution)/shard_map/ppermute | solution.py:461
  42.8 0.1 add.31.rest_1_
  43.1 0.7 copy.13.touched_ref
  43.8 0.7 pad_add_fusion.pos_ref
  44.5 0.3 collective-permute-done.10.rest_3_
  44.8 0.7 copy-done.11
  45.6 12.9 %local_grads.1 = (bf16[4,256,384]{2,1,0:T(8,128)(2,1)}, bf16[4,256,384]{2,1,0:T(8,128)(2,1)}, bf16[2,8,2,48,256]{4,3,2,1,0:T(8,128)(2,1)}, bf16[1,8,2,48,256]{4,...) custom-call(s32[2]{0:T(128)} %pad_add_fusion.pos_ref, ...), custom_call_target="tpu_custom_call" | custom-call | tf_op jit(solution)/shard_map/local_grads/pallas_call | solution.py:266
  58.5 1.8 %collective-permute-start.11 = (bf16[4,256,384]{2,1,0:T(8,128)(2,1)}, bf16[4,256,384]{2,1,0:T(8,128)(2,1)S(1)}, u32[]{:S(2)}, u32[]{:S(2)}) collective-permute-start(bf16[4,256,384]{2,1,0:T(8,128)(2,1)} %get-tuple-element.38), channel_id=1, source_target_pairs={{0,1},{1,0},{2,3},{3,2},{4,5},{5,4},{6,7},{7,6},{8,9},{9,8},{10,11... | collective-permute-start | bytes 2359304 | tf_op jit(solution)/shard_map/ppermute | solution.py:509
  60.4 1.4 collective-permute-start.12
  61.8 0.7 collective-permute-done.11
  62.5 2.3 %add.32 = bf16[4,256,384]{2,1,0:T(8,128)(2,1)} add(bf16[4,256,384]{2,1,0:T(8,128)(2,1)} %get-tuple-element.37, bf16[4,256,384]{2,1,0:T(8,128)(2,1)S(1)} %collective-permute-done.11) | non-fusion elementwise | flops 393216 | bytes 2359296 | tf_op jit(solution)/shard_map/add | solution.py:545
  64.7 4.2 %all-to-all-start = ((bf16[4,256,384]{2,1,0:T(8,128)(2,1)}), bf16[4,256,384]{2,1,0:T(8,128)(2,1)S(1)}, u32[]{:S(2)}, u32[]{:S(2)}) async-start(bf16[4,256,384]{2,1,0:T(8,128)(2,1)} %add.32), calls=%async_computation | async-start | bytes 1572864 | tf_op jit(solution)/shard_map/all_to_all | solution.py:546
  69.0 0.8 collective-permute-start.14
  69.8 0.7 collective-permute-start.15
  70.5 3.5 %collective-permute-done.13 = bf16[1,8,2,48,256]{4,3,2,1,0:T(8,128)(2,1)S(1)} collective-permute-done((bf16[1,8,2,48,256]{4,3,2,1,0:T(8,128)(2,1)}, bf16[1,8,2,48,256]{4,3,2,1,0:T(8,128)(2,1)S(1)}, u32[]{:S(2)}, u32[]{:S(2)}) %collective-permute-start.13) | collective-permute-done | bytes 393248 | tf_op jit(solution)/shard_map/ppermute | solution.py:509
  74.0 0.7 copy-done.18
  74.7 1.0 add_bitcast_fusion
  75.8 4.4 %collective-permute-done.12.refs_1_ = bf16[2,8,2,48,256]{4,3,2,1,0:T(8,128)(2,1)S(1)} collective-permute-done((bf16[2,8,2,48,256]{4,3,2,1,0:T(8,128)(2,1)}, bf16[2,8,2,48,256]{4,3,2,1,0:T(8,128)(2,1)S(1)}, u32[]{:S(2)}, u32[]{:S(2)}) %collective-permute-start.12) | collective-permute-done | bytes 786464 | tf_op jit(solution)/shard_map/ppermute | solution.py:509
  80.2 0.6 collective-permute-done.14.refs_4_
  80.9 1.1 collective-permute-start.16
  82.0 0.5 collective-permute-start.17
  82.5 10.0 %collective-permute-done.16.refs_2_ = bf16[8,2,48,256]{3,2,1,0:T(8,128)(2,1)S(1)} collective-permute-done((bf16[8,2,48,256]{3,2,1,0:T(8,128)(2,1)S(1)}, bf16[8,2,48,256]{3,2,1,0:T(8,128)(2,1)S(1)}, u32[]{:S(2)}, u32[]{:S(2)}) %collective-permute-start.16) | collective-permute-done | bytes 393248 | tf_op jit(solution)/shard_map/ppermute | solution.py:509
  92.5 0.9 collective-permute-done.17.refs_5_
  93.4 0.7 copy-done.15
  94.2 5.6 %adam_step.1 = (bf16[16,2,48,256]{3,2,1,0:T(8,128)(2,1)}, f32[16,2,48,256]{3,2,1,0:T(8,128)}, f32[16,2,48,256]{3,2,1,0:T(8,128)}) custom-call(s32[2]{0:T(128)} %pad_add_fusion.pos_ref, bf16[1,8,2,48,256]{4,3,2,1,0:T(8,128)(2,1)} %get-tuple-element.39.refs_0_, bf16[2,8,2,48,256]{4,3,2,1,0:T(8,128)(2,1)} %copy-done.4, bf16[8,2,48,256]{3,2,1,0:T(8,128)(2,1)} %copy-done.14, ...), custom_call_target="tpu_custom_call" | custom-call | tf_op jit(solution)/shard_map/adam_step/pallas_call | solution.py:359
  99.8 1.7 %collective-permute-start.19 = (bf16[16,2,48,256]{3,2,1,0:T(8,128)(2,1)}, bf16[16,2,48,256]{3,2,1,0:T(8,128)(2,1)S(1)}, u32[]{:S(2)}, u32[]{:S(2)}) collective-permute-start(bf16[16,2,48,256]{3,2,1,0:T(8,128)(2,1)} %get-tuple-element.52.refs_0_), channel_id=1, source_target_pairs={{0,8},{8,0},{16,24},{24,16},{1,9},{9,1},{17,25},{25,17},{2,10},{10... | collective-permute-start | bytes 2359304 | tf_op jit(solution)/shard_map/ppermute | solution.py:460
  101.4 2.4 %collective-permute-start.18 = (bf16[16,2,48,256]{3,2,1,0:T(8,128)(2,1)}, bf16[16,2,48,256]{3,2,1,0:T(8,128)(2,1)S(1)}, u32[]{:S(2)}, u32[]{:S(2)}) collective-permute-start(bf16[16,2,48,256]{3,2,1,0:T(8,128)(2,1)} %get-tuple-element.52.refs_0_), channel_id=1, source_target_pairs={{0,16},{8,24},{16,0},{24,8},{1,17},{9,25},{17,1},{25,9},{2,18},{10... | collective-permute-start | bytes 2359304 | tf_op jit(solution)/shard_map/ppermute | solution.py:459
  103.8 32.7 %collective-permute-done.19.refs_1_ = bf16[16,2,48,256]{3,2,1,0:T(8,128)(2,1)S(1)} collective-permute-done((bf16[16,2,48,256]{3,2,1,0:T(8,128)(2,1)}, bf16[16,2,48,256]{3,2,1,0:T(8,128)(2,1)S(1)}, u32[]{:S(2)}, u32[]{:S(2)}) %collective-permute-start.19) | collective-permute-done | bytes 786464 | tf_op jit(solution)/shard_map/ppermute | solution.py:460
  136.5 0.7 collective-permute-start.20
  137.2 1.3 collective-permute-start.21
  138.5 2.2 %finish_predicted.1 = bf16[256,384]{1,0:T(8,128)(2,1)} custom-call(bf16[256,256]{1,0:T(8,128)(2,1)} %get-tuple-element.30.perm_ref, bf16[4,256,384]{2,1,0:T(8,128)(2,1)} %copy-done.2), custom_call_target="tpu_custom_call" | custom-call | tf_op jit(solution)/shard_map/finish_predicted/pallas_call | solution.py:487
  140.7 3.5 %place_weights.2.refs_2_ = bf16[16,2,48,1024]{3,2,1,0:T(8,128)(2,1)} custom-call(s32[2]{0:T(128)} %pad_add_fusion.pos_ref, bf16[16,2,48,256]{3,2,1,0:T(8,128)(2,1)} %get-tuple-element.52.refs_0_, bf16[16,2,48,256]{3,2,1,0:T(8,128)(2,1)} %copy-done.9, bf16[16,2,48,256]{3,2,1,0:T(8,128)(2,1)} %copy-done.8), custom_call_target="tpu_custom_call" | custom-call | tf_op jit(solution)/shard_map/place_weights/pallas_call | solution.py:437
  144.1 15.2 %collective-permute-done.21.refs_1_ = bf16[16,2,48,256]{3,2,1,0:T(8,128)(2,1)S(1)} collective-permute-done((bf16[16,2,48,256]{3,2,1,0:T(8,128)(2,1)S(1)}, bf16[16,2,48,256]{3,2,1,0:T(8,128)(2,1)S(1)}, u32[]{:S(2)}, u32[]{:S(2)}) %collective-permute-start.21) | collective-permute-done | bytes 786464 | tf_op jit(solution)/shard_map/ppermute | solution.py:461
  159.3 1.5 place_weights.3
  (57 shorter events, 0.5 us)
Async XLA Ops:
  1.8 2.5 %collective-permute-start = (bf16[8,2,48,256]{3,2,1,0:T(8,128)(2,1)S(1)}, bf16[8,2,48,256]{3,2,1,0:T(8,128)(2,1)S(1)}, u32[]{:S(2)}, u32[]{:S(2)}) collective-permute-start(bf16[8,2,48,256]{3,2,1,0:T(8,128)(2,1)S(1)} %get-tuple-element.57), channel_id=1, source_target_pairs={{0,1},{1,0},{2,3},{3,2},{4,5},{5,4},{6,7},{7,6},{8,9},{9,8},{10,11... | collective-permute-start | bytes 1179656 | tf_op jit(solution)/shard_map/ppermute | solution.py:509
  4.3 1.7 %copy-start.10 = (bf16[528,384]{1,0:T(8,128)(2,1)S(1)}, bf16[528,384]{1,0:T(8,128)(2,1)}, u32[]{:S(2)}) copy-start(bf16[528,384]{1,0:T(8,128)(2,1)} %get-tuple-element.34) | copy-start | bytes 1216516
  4.4 23.3 %copy-start.3 = (bf16[2,8,2,48,256]{4,3,2,1,0:T(8,128)(2,1)}, bf16[2,8,2,48,256]{4,3,2,1,0:T(8,128)(2,1)S(1)}, u32[]{:S(2)}) copy-start(bf16[2,8,2,48,256]{4,3,2,1,0:T(8,128)(2,1)S(1)} %pad_maximum_fusion.1.rest_4_) | copy-start | bytes 2359300
  4.4 23.2 %collective-permute-start.4 = (bf16[2,8,2,48,256]{4,3,2,1,0:T(8,128)(2,1)S(1)}, bf16[2,8,2,48,256]{4,3,2,1,0:T(8,128)(2,1)S(1)}, u32[]{:S(2)}, u32[]{:S(2)}) collective-permute-start(bf16[2,8,2,48,256]{4,3,2,1,0:T(8,128)(2,1)S(1)} %pad_maximum_fusion.1.rest_4_), channel_id=1, source_target_pairs={{0,4},{1,5},{2,6},{3,7},{4,0},{5,1},{6,2},{7,3},{8,12},{9,13},{10,... | collective-permute-start | bytes 2359304 | tf_op jit(solution)/shard_map/ppermute | solution.py:509
  6.0 21.2 %collective-permute-start.2 = (bf16[528,384]{1,0:T(8,128)(2,1)S(1)}, bf16[528,384]{1,0:T(8,128)(2,1)S(1)}, u32[]{:S(2)}, u32[]{:S(2)}) collective-permute-start(bf16[528,384]{1,0:T(8,128)(2,1)S(1)} %copy-done.10), channel_id=1, source_target_pairs={{0,16},{8,24},{16,0},{24,8},{1,17},{9,25},{17,1},{25,9},{2,18},{10... | collective-permute-start | bytes 1216520 | tf_op jit(solution)/shard_map/ppermute | solution.py:459
  8.6 18.8 %collective-permute-start.1 = (bf16[528,384]{1,0:T(8,128)(2,1)S(1)}, bf16[528,384]{1,0:T(8,128)(2,1)S(1)}, u32[]{:S(2)}, u32[]{:S(2)}) collective-permute-start(bf16[528,384]{1,0:T(8,128)(2,1)S(1)} %copy-done.10), channel_id=1, source_target_pairs={{0,8},{8,0},{16,24},{24,16},{1,9},{9,1},{17,25},{25,17},{2,10},{10... | collective-permute-start | bytes 1216520 | tf_op jit(solution)/shard_map/ppermute | solution.py:460
  10.2 19.1 %collective-permute-start.3 = (bf16[2,8,2,48,256]{4,3,2,1,0:T(8,128)(2,1)S(1)}, bf16[2,8,2,48,256]{4,3,2,1,0:T(8,128)(2,1)S(1)}, u32[]{:S(2)}, u32[]{:S(2)}) collective-permute-start(bf16[2,8,2,48,256]{4,3,2,1,0:T(8,128)(2,1)S(1)} %pad_maximum_fusion.1.rest_4_), channel_id=1, source_target_pairs={{0,2},{1,3},{2,0},{3,1},{4,6},{5,7},{6,4},{7,5},{8,10},{9,11},{10,... | collective-permute-start | bytes 2359304 | tf_op jit(solution)/shard_map/ppermute | solution.py:509
  27.5 17.3 %copy-start.1 = (bf16[3,528,384]{2,1,0:T(8,128)(2,1)}, bf16[3,528,384]{2,1,0:T(8,128)(2,1)S(1)}, u32[]{:S(2)}) copy-start(bf16[3,528,384]{2,1,0:T(8,128)(2,1)S(1)} %pad_maximum_fusion.rest_0_) | copy-start | bytes 3649540
  27.6 15.5 %copy-start.20 = (s32[32,4]{0,1:T(4,128)S(1)}, s32[32,4]{0,1:T(4,128)}, u32[]{:S(2)}) copy-start(s32[32,4]{0,1:T(4,128)} %param.11) | copy-start | bytes 1540
  27.6 17.2 %collective-permute-start.7 = (bf16[3,528,384]{2,1,0:T(8,128)(2,1)S(1)}, bf16[3,528,384]{2,1,0:T(8,128)(2,1)}, u32[]{:S(2)}, u32[]{:S(2)}) collective-permute-start(bf16[3,528,384]{2,1,0:T(8,128)(2,1)S(1)} %pad_maximum_fusion.rest_0_), channel_id=1, source_target_pairs={{0,1},{1,0},{2,3},{3,2},{4,5},{5,4},{6,7},{7,6},{8,9},{9,8},{10,11... | collective-permute-start | bytes 3649544 | tf_op jit(solution)/shard_map/ppermute | solution.py:509
  27.7 17.2 %copy-start.5 = (bf16[2,8,2,48,256]{4,3,2,1,0:T(8,128)(2,1)}, bf16[2,8,2,48,256]{4,3,2,1,0:T(8,128)(2,1)S(1)}, u32[]{:S(2)}) copy-start(bf16[2,8,2,48,256]{4,3,2,1,0:T(8,128)(2,1)S(1)} %collective-permute-done.4.rest_6_) | copy-start | bytes 2359300
  27.7 15.3 %collective-permute-start.9 = (bf16[8,2,48,256]{3,2,1,0:T(8,128)(2,1)S(1)}, bf16[8,2,48,256]{3,2,1,0:T(8,128)(2,1)S(1)}, u32[]{:S(2)}, u32[]{:S(2)}) collective-permute-start(bf16[8,2,48,256]{3,2,1,0:T(8,128)(2,1)S(1)} %slice_bitcast_fusion), channel_id=1, source_target_pairs={{0,2},{1,3},{2,0},{3,1},{4,6},{5,7},{6,4},{7,5},{8,10},{9,11},{10,... | collective-permute-start | bytes 1179656 | tf_op jit(solution)/shard_map/ppermute | solution.py:509
  29.3 2.0 %copy-start.6 = (bf16[2,8,2,48,256]{4,3,2,1,0:T(8,128)(2,1)}, bf16[2,8,2,48,256]{4,3,2,1,0:T(8,128)(2,1)S(1)}, u32[]{:S(2)}) copy-start(bf16[2,8,2,48,256]{4,3,2,1,0:T(8,128)(2,1)S(1)} %collective-permute-done.3.rest_5_) | copy-start | bytes 2359300
  29.3 3.3 %collective-permute-start.5 = (bf16[528,384]{1,0:T(8,128)(2,1)S(1)}, bf16[528,384]{1,0:T(8,128)(2,1)S(1)}, u32[]{:S(2)}, u32[]{:S(2)}) collective-permute-start(bf16[528,384]{1,0:T(8,128)(2,1)S(1)} %copy-done.10), channel_id=1, source_target_pairs={{8,16},{16,8},{9,17},{17,9},{10,18},{18,10},{11,19},{19,11},{12,20... | collective-permute-start | bytes 1216520 | tf_op jit(solution)/shard_map/ppermute | solution.py:462
  29.9 12.9 %collective-permute-start.6 = (bf16[528,384]{1,0:T(8,128)(2,1)S(1)}, bf16[528,384]{1,0:T(8,128)(2,1)S(1)}, u32[]{:S(2)}, u32[]{:S(2)}) collective-permute-start(bf16[528,384]{1,0:T(8,128)(2,1)S(1)} %collective-permute-done.2), channel_id=1, source_target_pairs={{16,24},{8,0},{17,25},{9,1},{18,26},{10,2},{19,27},{11,3},{20,28},... | collective-permute-start | bytes 1216520 | tf_op jit(solution)/shard_map/ppermute | solution.py:461
  31.3 11.7 %collective-permute-start.8 = (bf16[8,2,48,256]{3,2,1,0:T(8,128)(2,1)S(1)}, bf16[8,2,48,256]{3,2,1,0:T(8,128)(2,1)}, u32[]{:S(2)}, u32[]{:S(2)}) collective-permute-start(bf16[8,2,48,256]{3,2,1,0:T(8,128)(2,1)S(1)} %slice_bitcast_fusion.1), channel_id=1, source_target_pairs={{0,4},{1,5},{2,6},{3,7},{4,0},{5,1},{6,2},{7,3},{8,12},{9,13},{10,... | collective-permute-start | bytes 1179656 | tf_op jit(solution)/shard_map/ppermute | solution.py:509
  43.0 1.9 %copy-start.7 = (bf16[528,384]{1,0:T(8,128)(2,1)}, bf16[528,384]{1,0:T(8,128)(2,1)S(1)}, u32[]{:S(2)}) copy-start(bf16[528,384]{1,0:T(8,128)(2,1)S(1)} %add.31.rest_1_) | copy-start | bytes 1216516
  43.0 1.9 %copy-start.19 = (bf16[8,2,48,256]{3,2,1,0:T(8,128)(2,1)}, bf16[8,2,48,256]{3,2,1,0:T(8,128)(2,1)S(1)}, u32[]{:S(2)}) copy-start(bf16[8,2,48,256]{3,2,1,0:T(8,128)(2,1)S(1)} %collective-permute-done.9.rest_8_) | copy-start | bytes 1179652
  43.0 1.8 %collective-permute-start.10 = (bf16[528,384]{1,0:T(8,128)(2,1)S(1)}, bf16[528,384]{1,0:T(8,128)(2,1)S(1)}, u32[]{:S(2)}, u32[]{:S(2)}) collective-permute-start(bf16[528,384]{1,0:T(8,128)(2,1)S(1)} %add.31.rest_1_), channel_id=1, source_target_pairs={{0,1},{1,0},{2,3},{3,2},{4,5},{5,4},{6,7},{7,6},{8,9},{9,8},{10,11... | collective-permute-start | bytes 1216520 | tf_op jit(solution)/shard_map/ppermute | solution.py:509
  44.8 0.8 copy-start.11
  58.5 4.0 %collective-permute-start.11 = (bf16[4,256,384]{2,1,0:T(8,128)(2,1)}, bf16[4,256,384]{2,1,0:T(8,128)(2,1)S(1)}, u32[]{:S(2)}, u32[]{:S(2)}) collective-permute-start(bf16[4,256,384]{2,1,0:T(8,128)(2,1)} %get-tuple-element.38), channel_id=1, source_target_pairs={{0,1},{1,0},{2,3},{3,2},{4,5},{5,4},{6,7},{7,6},{8,9},{9,8},{10,11... | collective-permute-start | bytes 2359304 | tf_op jit(solution)/shard_map/ppermute | solution.py:509
  60.4 19.8 %collective-permute-start.12 = (bf16[2,8,2,48,256]{4,3,2,1,0:T(8,128)(2,1)}, bf16[2,8,2,48,256]{4,3,2,1,0:T(8,128)(2,1)S(1)}, u32[]{:S(2)}, u32[]{:S(2)}) collective-permute-start(bf16[2,8,2,48,256]{4,3,2,1,0:T(8,128)(2,1)} %get-tuple-element.40), channel_id=1, source_target_pairs={{0,2},{1,3},{2,0},{3,1},{4,6},{5,7},{6,4},{7,5},{8,10},{9,11},{10,... | collective-permute-start | bytes 2359304 | tf_op jit(solution)/shard_map/ppermute | solution.py:509
  61.8 12.2 %collective-permute-start.13 = (bf16[1,8,2,48,256]{4,3,2,1,0:T(8,128)(2,1)}, bf16[1,8,2,48,256]{4,3,2,1,0:T(8,128)(2,1)S(1)}, u32[]{:S(2)}, u32[]{:S(2)}) collective-permute-start(bf16[1,8,2,48,256]{4,3,2,1,0:T(8,128)(2,1)} %get-tuple-element.42), channel_id=1, source_target_pairs={{0,4},{1,5},{2,6},{3,7},{4,0},{5,1},{6,2},{7,3},{8,12},{9,13},{10,... | collective-permute-start | bytes 1179656 | tf_op jit(solution)/shard_map/ppermute | solution.py:509
  62.5 12.2 %copy-start.17 = (bf16[1,8,2,48,256]{4,3,2,1,0:T(8,128)(2,1)S(1)}, bf16[1,8,2,48,256]{4,3,2,1,0:T(8,128)(2,1)}, u32[]{:S(2)}) copy-start(bf16[1,8,2,48,256]{4,3,2,1,0:T(8,128)(2,1)} %get-tuple-element.49) | copy-start | bytes 1179652
  64.7 15.4 %copy-start.16 = (bf16[1,8,2,48,256]{4,3,2,1,0:T(8,128)(2,1)S(1)}, bf16[1,8,2,48,256]{4,3,2,1,0:T(8,128)(2,1)}, u32[]{:S(2)}) copy-start(bf16[1,8,2,48,256]{4,3,2,1,0:T(8,128)(2,1)} %get-tuple-element.41) | copy-start | bytes 1179652
  64.7 27.8 %all-to-all-start = ((bf16[4,256,384]{2,1,0:T(8,128)(2,1)}), bf16[4,256,384]{2,1,0:T(8,128)(2,1)S(1)}, u32[]{:S(2)}, u32[]{:S(2)}) async-start(bf16[4,256,384]{2,1,0:T(8,128)(2,1)} %add.32), calls=%async_computation | async-start | bytes 1572864 | tf_op jit(solution)/shard_map/all_to_all | solution.py:546
  69.0 11.9 %collective-permute-start.14 = (bf16[1,8,2,48,256]{4,3,2,1,0:T(8,128)(2,1)}, bf16[1,8,2,48,256]{4,3,2,1,0:T(8,128)(2,1)S(1)}, u32[]{:S(2)}, u32[]{:S(2)}) collective-permute-start(bf16[1,8,2,48,256]{4,3,2,1,0:T(8,128)(2,1)} %get-tuple-element.44), channel_id=1, source_target_pairs={{0,5},{1,4},{2,7},{3,6},{4,1},{5,0},{6,3},{7,2},{8,13},{9,12},{10,... | collective-permute-start | bytes 1179656 | tf_op jit(solution)/shard_map/ppermute | solution.py:509
  69.8 11.1 %collective-permute-start.15 = (bf16[1,8,2,48,256]{4,3,2,1,0:T(8,128)(2,1)}, bf16[1,8,2,48,256]{4,3,2,1,0:T(8,128)(2,1)S(1)}, u32[]{:S(2)}, u32[]{:S(2)}) collective-permute-start(bf16[1,8,2,48,256]{4,3,2,1,0:T(8,128)(2,1)} %get-tuple-element.46), channel_id=1, source_target_pairs={{0,1},{1,0},{2,3},{3,2},{4,5},{5,4},{6,7},{7,6},{8,9},{9,8},{10,11... | collective-permute-start | bytes 1179656 | tf_op jit(solution)/shard_map/ppermute | solution.py:509
  74.0 0.7 copy-start.18
  80.2 13.2 %copy-start.4 = (bf16[2,8,2,48,256]{4,3,2,1,0:T(8,128)(2,1)}, bf16[2,8,2,48,256]{4,3,2,1,0:T(8,128)(2,1)S(1)}, u32[]{:S(2)}) copy-start(bf16[2,8,2,48,256]{4,3,2,1,0:T(8,128)(2,1)S(1)} %collective-permute-done.12.refs_1_) | copy-start | bytes 2359300
  80.9 12.6 %copy-start.12 = (bf16[1,8,2,48,256]{4,3,2,1,0:T(8,128)(2,1)}, bf16[1,8,2,48,256]{4,3,2,1,0:T(8,128)(2,1)S(1)}, u32[]{:S(2)}) copy-start(bf16[1,8,2,48,256]{4,3,2,1,0:T(8,128)(2,1)S(1)} %collective-permute-done.14.refs_4_) | copy-start | bytes 1179652
  80.9 12.6 %copy-start.13 = (bf16[1,8,2,48,256]{4,3,2,1,0:T(8,128)(2,1)}, bf16[1,8,2,48,256]{4,3,2,1,0:T(8,128)(2,1)S(1)}, u32[]{:S(2)}) copy-start(bf16[1,8,2,48,256]{4,3,2,1,0:T(8,128)(2,1)S(1)} %collective-permute-done.15.refs_3_) | copy-start | bytes 1179652
  80.9 11.7 %collective-permute-start.16 = (bf16[8,2,48,256]{3,2,1,0:T(8,128)(2,1)S(1)}, bf16[8,2,48,256]{3,2,1,0:T(8,128)(2,1)S(1)}, u32[]{:S(2)}, u32[]{:S(2)}) collective-permute-start(bf16[8,2,48,256]{3,2,1,0:T(8,128)(2,1)S(1)} %fusion), channel_id=1, source_target_pairs={{0,4},{1,5},{2,6},{3,7},{4,0},{5,1},{6,2},{7,3},{8,12},{9,13},{10,... | collective-permute-start | bytes 1179656 | tf_op jit(solution)/shard_map/ppermute | solution.py:509
  82.0 11.4 %collective-permute-start.17 = (bf16[8,2,48,256]{3,2,1,0:T(8,128)(2,1)S(1)}, bf16[8,2,48,256]{3,2,1,0:T(8,128)(2,1)S(1)}, u32[]{:S(2)}, u32[]{:S(2)}) collective-permute-start(bf16[8,2,48,256]{3,2,1,0:T(8,128)(2,1)S(1)} %add_bitcast_fusion), channel_id=1, source_target_pairs={{0,3},{1,2},{2,1},{3,0},{4,7},{5,6},{6,5},{7,4},{8,11},{9,10},{10,... | collective-permute-start | bytes 1179656 | tf_op jit(solution)/shard_map/ppermute | solution.py:509
  92.5 0.9 copy-start.14
  92.5 7.2 %copy-start.2 = (bf16[4,256,384]{2,1,0:T(8,128)(2,1)}, bf16[4,256,384]{2,1,0:T(8,128)(2,1)S(1)}, u32[]{:S(2)}) copy-start(bf16[4,256,384]{2,1,0:T(8,128)(2,1)S(1)} %all-to-all-done.parts_ref) | copy-start | bytes 2359300
  93.4 0.8 copy-start.15
  99.8 36.7 %collective-permute-start.19 = (bf16[16,2,48,256]{3,2,1,0:T(8,128)(2,1)}, bf16[16,2,48,256]{3,2,1,0:T(8,128)(2,1)S(1)}, u32[]{:S(2)}, u32[]{:S(2)}) collective-permute-start(bf16[16,2,48,256]{3,2,1,0:T(8,128)(2,1)} %get-tuple-element.52.refs_0_), channel_id=1, source_target_pairs={{0,8},{8,0},{16,24},{24,16},{1,9},{9,1},{17,25},{25,17},{2,10},{10... | collective-permute-start | bytes 2359304 | tf_op jit(solution)/shard_map/ppermute | solution.py:460
  101.4 35.0 %collective-permute-start.18 = (bf16[16,2,48,256]{3,2,1,0:T(8,128)(2,1)}, bf16[16,2,48,256]{3,2,1,0:T(8,128)(2,1)S(1)}, u32[]{:S(2)}, u32[]{:S(2)}) collective-permute-start(bf16[16,2,48,256]{3,2,1,0:T(8,128)(2,1)} %get-tuple-element.52.refs_0_), channel_id=1, source_target_pairs={{0,16},{8,24},{16,0},{24,8},{1,17},{9,25},{17,1},{25,9},{2,18},{10... | collective-permute-start | bytes 2359304 | tf_op jit(solution)/shard_map/ppermute | solution.py:459
  136.4 4.2 %copy-start.9 = (bf16[16,2,48,256]{3,2,1,0:T(8,128)(2,1)}, bf16[16,2,48,256]{3,2,1,0:T(8,128)(2,1)S(1)}, u32[]{:S(2)}) copy-start(bf16[16,2,48,256]{3,2,1,0:T(8,128)(2,1)S(1)} %collective-permute-done.19.refs_1_) | copy-start | bytes 2359300
  136.5 4.2 %copy-start.8 = (bf16[16,2,48,256]{3,2,1,0:T(8,128)(2,1)}, bf16[16,2,48,256]{3,2,1,0:T(8,128)(2,1)S(1)}, u32[]{:S(2)}) copy-start(bf16[16,2,48,256]{3,2,1,0:T(8,128)(2,1)S(1)} %collective-permute-done.18.refs_2_) | copy-start | bytes 2359300
  136.5 7.7 %collective-permute-start.20 = (bf16[16,2,48,256]{3,2,1,0:T(8,128)(2,1)}, bf16[16,2,48,256]{3,2,1,0:T(8,128)(2,1)S(1)}, u32[]{:S(2)}, u32[]{:S(2)}) collective-permute-start(bf16[16,2,48,256]{3,2,1,0:T(8,128)(2,1)} %get-tuple-element.52.refs_0_), channel_id=1, source_target_pairs={{8,16},{16,8},{9,17},{17,9},{10,18},{18,10},{11,19},{19,11},{12,20... | collective-permute-start | bytes 2359304 | tf_op jit(solution)/shard_map/ppermute | solution.py:462
  137.2 22.2 %collective-permute-start.21 = (bf16[16,2,48,256]{3,2,1,0:T(8,128)(2,1)S(1)}, bf16[16,2,48,256]{3,2,1,0:T(8,128)(2,1)S(1)}, u32[]{:S(2)}, u32[]{:S(2)}) collective-permute-start(bf16[16,2,48,256]{3,2,1,0:T(8,128)(2,1)S(1)} %collective-permute-done.18.refs_2_), channel_id=1, source_target_pairs={{16,24},{8,0},{17,25},{9,1},{18,26},{10,2},{19,27},{11,3},{20,28},... | collective-permute-start | bytes 2359304 | tf_op jit(solution)/shard_map/ppermute | solution.py:461
  140.7 18.7 %copy-start = (s32[2]{0:T(128)S(1)}, s32[2]{0:T(128)}, u32[]{:S(2)}) copy-start(s32[2]{0:T(128)} %pad_add_fusion.pos_ref) | copy-start | bytes 28

commit v19 on v18

--- a/solution.py
+++ b/solution.py
@@ -542,13 +542,14 @@
     pred_mine, pred_other, grads = local_grads(
         pos, touched, slot_map, rows_in, blocks, sends, piece, width
     )
-    pred_part = pred_mine + across(pred_other, 1)
+    pred_swapped = across(pred_other, 1)
+    pred_part = pred_mine + pred_swapped
     parts = lax.all_to_all(pred_part, "dp", split_axis=0, concat_axis=0, tiled=True)
     if sends:
         x_same, y_diagonal, y_cross, partner, x_cross, y_same, own = grads
         x_same = across(x_same, 2)
         y_diagonal = across(y_diagonal, 4)
-        y_cross = across(after(y_cross, pred_part), 5)
+        y_cross = across(after(y_cross, pred_swapped), 5)
         partner = across(after(partner, pred_part), 1)
         first = (x_same, y_diagonal, y_cross, partner)
         x_cross = across(after(x_cross[0] + y_diagonal[0], *first), 3)

time: 163 us -> 163 us (level)
    ppermute x2, waiting for transfers between devices: 16.5 us -> 19.2 us  [between_planes(): two = lax.ppermute(value, 'dp', [(0, 2), (1, 3), (2, 0), (3, 1)])]
    ppermute x2, waiting for transfers between devices: 25.5 us -> 23.4 us  [between_planes(): outer = lax.ppermute(after(two, one, *second), 'dp', [(2, 3), (1, 0)])]
where the time goes in v19:
time: 163 us; the launch traced here: 161 us
  waiting for transfers between devices  95.4 us (59%)
  starting transfers between devices  28.3 us (17%)
  Pallas kernels  28 us (17%)
  other arithmetic  4.34 us (3%)
  local copies, waits for them, and re-layouts  4.27 us (3%)
    ppermute x2, waiting for transfers between devices, between_planes(): lax.ppermute(after(value, *first), 'dp', [(0, 1), (1, 0), (2, 3), (3, 2)])  32.6 us
    ppermute x2, waiting for transfers between devices, between_planes(): outer = lax.ppermute(after(two, one, *second), 'dp', [(2, 3), (1, 0)])  23.4 us
    ppermute x14, waiting for transfers between devices, across(): return lax.ppermute(value, 'own', [(o, o ^ j) for o in range(n_own)])  20.3 us
    ppermute x2, waiting for transfers between devices, between_planes(): two = lax.ppermute(value, 'dp', [(0, 2), (1, 3), (2, 0), (3, 1)])  19.2 us
    pallas_call x1, Pallas kernels, local_grads(): pl.pallas_call(body, out_shape=[pred_shape, pred_shape] + grad_shapes, in...  12.9 us
    ppermute x14, starting transfers between devices, across(): return lax.ppermute(value, 'own', [(o, o ^ j) for o in range(n_own)])  11.5 us
    pallas_call x1, Pallas kernels, adam(): pl.pallas_call(body, out_shape=[jax.ShapeDtypeStruct(moment1.shape, jnp.b...  5.59 us
    pallas_call x2, Pallas kernels, place_weights(): pl.pallas_call(body, out_shape=jax.ShapeDtypeStruct(shape, jnp.bfloat16),...  4.92 us
  transfers between devices with their start and end apart: 23, of which 13 were waited for; matrix products, arithmetic and copies ran while one was open for 3% of the time, Pallas kernels for 5%

profile of v19, /device:TPU:2, one launch (start us, length us, event | category | flops | bytes accessed | tf_op | source)
XLA Modules:
  0.0 161.3 jit_solution(11076598146808055431)
XLA Ops:
  0.6 1.2 dynamic-slice_bitcast_fusion
  1.9 2.4 %pack_rows.1 = (bf16[528,384]{1,0:T(8,128)(2,1)}, bf16[256,256]{1,0:T(8,128)(2,1)}) custom-call(s32[1,256]{1,0:T(1,128)} %bitcast.21, bf16[256,384]{1,0:T(8,128)(2,1)} %sig_ref.1, bf16[256,384]{1,0:T(8,128)(2,1)} %cot_ref.1), custom_call_target="tpu_custom_call" | custom-call | tf_op jit(solution)/shard_map/pack_rows/pallas_call | solution.py:81
  4.4 1.6 collective-permute-start.4
  6.0 2.6 %collective-permute-start.2 = (bf16[528,384]{1,0:T(8,128)(2,1)S(1)}, bf16[528,384]{1,0:T(8,128)(2,1)S(1)}, u32[]{:S(2)}, u32[]{:S(2)}) collective-permute-start(bf16[528,384]{1,0:T(8,128)(2,1)S(1)} %copy-done.10), channel_id=1, source_target_pairs={{0,16},{8,24},{16,0},{24,8},{1,17},{9,25},{17,1},{25,9},{2,18},{10... | collective-permute-start | bytes 1216520 | tf_op jit(solution)/shard_map/ppermute | solution.py:459
  8.6 1.6 collective-permute-start.1
  10.2 0.5 collective-permute-start.3
  10.7 16.5 %collective-permute-done.2 = bf16[528,384]{1,0:T(8,128)(2,1)S(1)} collective-permute-done((bf16[528,384]{1,0:T(8,128)(2,1)S(1)}, bf16[528,384]{1,0:T(8,128)(2,1)S(1)}, u32[]{:S(2)}, u32[]{:S(2)}) %collective-permute-start.2) | collective-permute-done | bytes 405536 | tf_op jit(solution)/shard_map/ppermute | solution.py:459
  27.2 0.2 collective-permute-done.1
  27.4 0.2 pad_maximum_fusion.rest_0_
  27.7 0.6 collective-permute-start.9
  28.3 0.9 collective-permute-done.3.rest_5_
  29.3 0.7 collective-permute-start.5
  29.9 1.3 collective-permute-start.6
  31.3 1.2 collective-permute-start.8
  32.5 10.3 %collective-permute-done.6 = bf16[528,384]{1,0:T(8,128)(2,1)S(1)} collective-permute-done((bf16[528,384]{1,0:T(8,128)(2,1)S(1)}, bf16[528,384]{1,0:T(8,128)(2,1)S(1)}, u32[]{:S(2)}, u32[]{:S(2)}) %collective-permute-start.6) | collective-permute-done | bytes 405536 | tf_op jit(solution)/shard_map/ppermute | solution.py:461
  43.1 0.7 copy.13.touched_ref
  43.8 0.7 pad_add_fusion.pos_ref
  44.5 0.3 collective-permute-done.10.rest_3_
  44.8 0.7 copy-done.11
  45.6 12.9 %local_grads.1 = (bf16[4,256,384]{2,1,0:T(8,128)(2,1)}, bf16[4,256,384]{2,1,0:T(8,128)(2,1)}, bf16[2,8,2,48,256]{4,3,2,1,0:T(8,128)(2,1)}, bf16[1,8,2,48,256]{4,...) custom-call(s32[2]{0:T(128)} %pad_add_fusion.pos_ref, ...), custom_call_target="tpu_custom_call" | custom-call | tf_op jit(solution)/shard_map/local_grads/pallas_call | solution.py:266
  58.5 1.9 %collective-permute-start.11 = (bf16[4,256,384]{2,1,0:T(8,128)(2,1)}, bf16[4,256,384]{2,1,0:T(8,128)(2,1)S(1)}, u32[]{:S(2)}, u32[]{:S(2)}) collective-permute-start(bf16[4,256,384]{2,1,0:T(8,128)(2,1)} %get-tuple-element.38), channel_id=1, source_target_pairs={{0,1},{1,0},{2,3},{3,2},{4,5},{5,4},{6,7},{7,6},{8,9},{9,8},{10,11... | collective-permute-start | bytes 2359304 | tf_op jit(solution)/shard_map/ppermute | solution.py:509
  60.4 1.5 collective-permute-start.12
  61.9 1.1 collective-permute-start.13
  63.0 2.3 %add.32 = bf16[4,256,384]{2,1,0:T(8,128)(2,1)} add(bf16[4,256,384]{2,1,0:T(8,128)(2,1)} %get-tuple-element.37, bf16[4,256,384]{2,1,0:T(8,128)(2,1)S(1)} %collective-permute-done.11) | non-fusion elementwise | flops 393216 | bytes 2359296 | tf_op jit(solution)/shard_map/add | solution.py:546
  65.3 4.1 %all-to-all-start = ((bf16[4,256,384]{2,1,0:T(8,128)(2,1)}), bf16[4,256,384]{2,1,0:T(8,128)(2,1)S(1)}, u32[]{:S(2)}, u32[]{:S(2)}) async-start(bf16[4,256,384]{2,1,0:T(8,128)(2,1)} %add.32), calls=%async_computation | async-start | bytes 1572864 | tf_op jit(solution)/shard_map/all_to_all | solution.py:547
  69.4 0.4 collective-permute-start.14
  69.8 0.7 collective-permute-start.15
  70.5 2.7 %collective-permute-done.13 = bf16[1,8,2,48,256]{4,3,2,1,0:T(8,128)(2,1)S(1)} collective-permute-done((bf16[1,8,2,48,256]{4,3,2,1,0:T(8,128)(2,1)}, bf16[1,8,2,48,256]{4,3,2,1,0:T(8,128)(2,1)S(1)}, u32[]{:S(2)}, u32[]{:S(2)}) %collective-permute-start.13) | collective-permute-done | bytes 393248 | tf_op jit(solution)/shard_map/ppermute | solution.py:509
  73.1 0.7 copy-done.18
  73.9 1.0 add_bitcast_fusion
  74.9 5.2 %collective-permute-done.12.refs_1_ = bf16[2,8,2,48,256]{4,3,2,1,0:T(8,128)(2,1)S(1)} collective-permute-done((bf16[2,8,2,48,256]{4,3,2,1,0:T(8,128)(2,1)}, bf16[2,8,2,48,256]{4,3,2,1,0:T(8,128)(2,1)S(1)}, u32[]{:S(2)}, u32[]{:S(2)}) %collective-permute-start.12) | collective-permute-done | bytes 786464 | tf_op jit(solution)/shard_map/ppermute | solution.py:509
  80.2 0.9 collective-permute-done.14.refs_4_
  81.1 1.0 collective-permute-start.16
  82.1 0.8 collective-permute-start.17
  82.9 9.4 %collective-permute-done.16.refs_2_ = bf16[8,2,48,256]{3,2,1,0:T(8,128)(2,1)S(1)} collective-permute-done((bf16[8,2,48,256]{3,2,1,0:T(8,128)(2,1)S(1)}, bf16[8,2,48,256]{3,2,1,0:T(8,128)(2,1)S(1)}, u32[]{:S(2)}, u32[]{:S(2)}) %collective-permute-start.16) | collective-permute-done | bytes 393248 | tf_op jit(solution)/shard_map/ppermute | solution.py:509
  92.3 0.8 collective-permute-done.17.refs_5_
  93.1 0.7 copy-done.15
  93.9 5.6 %adam_step.1 = (bf16[16,2,48,256]{3,2,1,0:T(8,128)(2,1)}, f32[16,2,48,256]{3,2,1,0:T(8,128)}, f32[16,2,48,256]{3,2,1,0:T(8,128)}) custom-call(s32[2]{0:T(128)} %pad_add_fusion.pos_ref, bf16[1,8,2,48,256]{4,3,2,1,0:T(8,128)(2,1)} %get-tuple-element.39.refs_0_, bf16[2,8,2,48,256]{4,3,2,1,0:T(8,128)(2,1)} %copy-done.4, bf16[8,2,48,256]{3,2,1,0:T(8,128)(2,1)} %copy-done.14, ...), custom_call_target="tpu_custom_call" | custom-call | tf_op jit(solution)/shard_map/adam_step/pallas_call | solution.py:359
  99.5 2.3 %collective-permute-start.19 = (bf16[16,2,48,256]{3,2,1,0:T(8,128)(2,1)}, bf16[16,2,48,256]{3,2,1,0:T(8,128)(2,1)S(1)}, u32[]{:S(2)}, u32[]{:S(2)}) collective-permute-start(bf16[16,2,48,256]{3,2,1,0:T(8,128)(2,1)} %get-tuple-element.52.refs_0_), channel_id=1, source_target_pairs={{0,8},{8,0},{16,24},{24,16},{1,9},{9,1},{17,25},{25,17},{2,10},{10... | collective-permute-start | bytes 2359304 | tf_op jit(solution)/shard_map/ppermute | solution.py:460
  101.7 2.3 %collective-permute-start.18 = (bf16[16,2,48,256]{3,2,1,0:T(8,128)(2,1)}, bf16[16,2,48,256]{3,2,1,0:T(8,128)(2,1)S(1)}, u32[]{:S(2)}, u32[]{:S(2)}) collective-permute-start(bf16[16,2,48,256]{3,2,1,0:T(8,128)(2,1)} %get-tuple-element.52.refs_0_), channel_id=1, source_target_pairs={{0,16},{8,24},{16,0},{24,8},{1,17},{9,25},{17,1},{25,9},{2,18},{10... | collective-permute-start | bytes 2359304 | tf_op jit(solution)/shard_map/ppermute | solution.py:459
  104.0 32.4 %collective-permute-done.19.refs_1_ = bf16[16,2,48,256]{3,2,1,0:T(8,128)(2,1)S(1)} collective-permute-done((bf16[16,2,48,256]{3,2,1,0:T(8,128)(2,1)}, bf16[16,2,48,256]{3,2,1,0:T(8,128)(2,1)S(1)}, u32[]{:S(2)}, u32[]{:S(2)}) %collective-permute-start.19) | collective-permute-done | bytes 786464 | tf_op jit(solution)/shard_map/ppermute | solution.py:460
  136.4 2.7 %collective-permute-done.18.refs_2_ = bf16[16,2,48,256]{3,2,1,0:T(8,128)(2,1)S(1)} collective-permute-done((bf16[16,2,48,256]{3,2,1,0:T(8,128)(2,1)}, bf16[16,2,48,256]{3,2,1,0:T(8,128)(2,1)S(1)}, u32[]{:S(2)}, u32[]{:S(2)}) %collective-permute-start.18) | collective-permute-done | bytes 786464 | tf_op jit(solution)/shard_map/ppermute | solution.py:459
  139.0 0.7 collective-permute-start.20
  139.7 1.3 collective-permute-start.21
  141.0 2.2 %finish_predicted.1 = bf16[256,384]{1,0:T(8,128)(2,1)} custom-call(bf16[256,256]{1,0:T(8,128)(2,1)} %get-tuple-element.30.perm_ref, bf16[4,256,384]{2,1,0:T(8,128)(2,1)} %copy-done.2), custom_call_target="tpu_custom_call" | custom-call | tf_op jit(solution)/shard_map/finish_predicted/pallas_call | solution.py:487
  143.2 3.5 %place_weights.2.refs_2_ = bf16[16,2,48,1024]{3,2,1,0:T(8,128)(2,1)} custom-call(s32[2]{0:T(128)} %pad_add_fusion.pos_ref, bf16[16,2,48,256]{3,2,1,0:T(8,128)(2,1)} %get-tuple-element.52.refs_0_, bf16[16,2,48,256]{3,2,1,0:T(8,128)(2,1)} %copy-done.9, bf16[16,2,48,256]{3,2,1,0:T(8,128)(2,1)} %copy-done.8), custom_call_target="tpu_custom_call" | custom-call | tf_op jit(solution)/shard_map/place_weights/pallas_call | solution.py:437
  146.7 13.1 %collective-permute-done.21.refs_1_ = bf16[16,2,48,256]{3,2,1,0:T(8,128)(2,1)S(1)} collective-permute-done((bf16[16,2,48,256]{3,2,1,0:T(8,128)(2,1)S(1)}, bf16[16,2,48,256]{3,2,1,0:T(8,128)(2,1)S(1)}, u32[]{:S(2)}, u32[]{:S(2)}) %collective-permute-start.21) | collective-permute-done | bytes 786464 | tf_op jit(solution)/shard_map/ppermute | solution.py:461
  159.8 1.5 place_weights.3
  (57 shorter events, 0.6 us)
Async XLA Ops:
  1.8 2.5 %collective-permute-start = (bf16[8,2,48,256]{3,2,1,0:T(8,128)(2,1)S(1)}, bf16[8,2,48,256]{3,2,1,0:T(8,128)(2,1)S(1)}, u32[]{:S(2)}, u32[]{:S(2)}) collective-permute-start(bf16[8,2,48,256]{3,2,1,0:T(8,128)(2,1)S(1)} %get-tuple-element.57), channel_id=1, source_target_pairs={{0,1},{1,0},{2,3},{3,2},{4,5},{5,4},{6,7},{7,6},{8,9},{9,8},{10,11... | collective-permute-start | bytes 1179656 | tf_op jit(solution)/shard_map/ppermute | solution.py:509
  4.3 1.7 %copy-start.10 = (bf16[528,384]{1,0:T(8,128)(2,1)S(1)}, bf16[528,384]{1,0:T(8,128)(2,1)}, u32[]{:S(2)}) copy-start(bf16[528,384]{1,0:T(8,128)(2,1)} %get-tuple-element.34) | copy-start | bytes 1216516
  4.4 23.3 %copy-start.3 = (bf16[2,8,2,48,256]{4,3,2,1,0:T(8,128)(2,1)}, bf16[2,8,2,48,256]{4,3,2,1,0:T(8,128)(2,1)S(1)}, u32[]{:S(2)}) copy-start(bf16[2,8,2,48,256]{4,3,2,1,0:T(8,128)(2,1)S(1)} %pad_maximum_fusion.1.rest_4_) | copy-start | bytes 2359300
  4.4 23.2 %collective-permute-start.4 = (bf16[2,8,2,48,256]{4,3,2,1,0:T(8,128)(2,1)S(1)}, bf16[2,8,2,48,256]{4,3,2,1,0:T(8,128)(2,1)S(1)}, u32[]{:S(2)}, u32[]{:S(2)}) collective-permute-start(bf16[2,8,2,48,256]{4,3,2,1,0:T(8,128)(2,1)S(1)} %pad_maximum_fusion.1.rest_4_), channel_id=1, source_target_pairs={{0,4},{1,5},{2,6},{3,7},{4,0},{5,1},{6,2},{7,3},{8,12},{9,13},{10,... | collective-permute-start | bytes 2359304 | tf_op jit(solution)/shard_map/ppermute | solution.py:509
  6.0 21.2 %collective-permute-start.2 = (bf16[528,384]{1,0:T(8,128)(2,1)S(1)}, bf16[528,384]{1,0:T(8,128)(2,1)S(1)}, u32[]{:S(2)}, u32[]{:S(2)}) collective-permute-start(bf16[528,384]{1,0:T(8,128)(2,1)S(1)} %copy-done.10), channel_id=1, source_target_pairs={{0,16},{8,24},{16,0},{24,8},{1,17},{9,25},{17,1},{25,9},{2,18},{10... | collective-permute-start | bytes 1216520 | tf_op jit(solution)/shard_map/ppermute | solution.py:459
  8.6 18.8 %collective-permute-start.1 = (bf16[528,384]{1,0:T(8,128)(2,1)S(1)}, bf16[528,384]{1,0:T(8,128)(2,1)S(1)}, u32[]{:S(2)}, u32[]{:S(2)}) collective-permute-start(bf16[528,384]{1,0:T(8,128)(2,1)S(1)} %copy-done.10), channel_id=1, source_target_pairs={{0,8},{8,0},{16,24},{24,16},{1,9},{9,1},{17,25},{25,17},{2,10},{10... | collective-permute-start | bytes 1216520 | tf_op jit(solution)/shard_map/ppermute | solution.py:460
  10.2 19.1 %collective-permute-start.3 = (bf16[2,8,2,48,256]{4,3,2,1,0:T(8,128)(2,1)S(1)}, bf16[2,8,2,48,256]{4,3,2,1,0:T(8,128)(2,1)S(1)}, u32[]{:S(2)}, u32[]{:S(2)}) collective-permute-start(bf16[2,8,2,48,256]{4,3,2,1,0:T(8,128)(2,1)S(1)} %pad_maximum_fusion.1.rest_4_), channel_id=1, source_target_pairs={{0,2},{1,3},{2,0},{3,1},{4,6},{5,7},{6,4},{7,5},{8,10},{9,11},{10,... | collective-permute-start | bytes 2359304 | tf_op jit(solution)/shard_map/ppermute | solution.py:509
  27.5 17.3 %copy-start.1 = (bf16[3,528,384]{2,1,0:T(8,128)(2,1)}, bf16[3,528,384]{2,1,0:T(8,128)(2,1)S(1)}, u32[]{:S(2)}) copy-start(bf16[3,528,384]{2,1,0:T(8,128)(2,1)S(1)} %pad_maximum_fusion.rest_0_) | copy-start | bytes 3649540
  27.6 15.5 %copy-start.20 = (s32[32,4]{0,1:T(4,128)S(1)}, s32[32,4]{0,1:T(4,128)}, u32[]{:S(2)}) copy-start(s32[32,4]{0,1:T(4,128)} %param.11) | copy-start | bytes 1540
  27.6 17.2 %collective-permute-start.7 = (bf16[3,528,384]{2,1,0:T(8,128)(2,1)S(1)}, bf16[3,528,384]{2,1,0:T(8,128)(2,1)}, u32[]{:S(2)}, u32[]{:S(2)}) collective-permute-start(bf16[3,528,384]{2,1,0:T(8,128)(2,1)S(1)} %pad_maximum_fusion.rest_0_), channel_id=1, source_target_pairs={{0,1},{1,0},{2,3},{3,2},{4,5},{5,4},{6,7},{7,6},{8,9},{9,8},{10,11... | collective-permute-start | bytes 3649544 | tf_op jit(solution)/shard_map/ppermute | solution.py:509
  27.7 17.2 %copy-start.5 = (bf16[2,8,2,48,256]{4,3,2,1,0:T(8,128)(2,1)}, bf16[2,8,2,48,256]{4,3,2,1,0:T(8,128)(2,1)S(1)}, u32[]{:S(2)}) copy-start(bf16[2,8,2,48,256]{4,3,2,1,0:T(8,128)(2,1)S(1)} %collective-permute-done.4.rest_6_) | copy-start | bytes 2359300
  27.7 15.3 %collective-permute-start.9 = (bf16[8,2,48,256]{3,2,1,0:T(8,128)(2,1)S(1)}, bf16[8,2,48,256]{3,2,1,0:T(8,128)(2,1)S(1)}, u32[]{:S(2)}, u32[]{:S(2)}) collective-permute-start(bf16[8,2,48,256]{3,2,1,0:T(8,128)(2,1)S(1)} %slice_bitcast_fusion), channel_id=1, source_target_pairs={{0,2},{1,3},{2,0},{3,1},{4,6},{5,7},{6,4},{7,5},{8,10},{9,11},{10,... | collective-permute-start | bytes 1179656 | tf_op jit(solution)/shard_map/ppermute | solution.py:509
  29.3 2.0 %copy-start.6 = (bf16[2,8,2,48,256]{4,3,2,1,0:T(8,128)(2,1)}, bf16[2,8,2,48,256]{4,3,2,1,0:T(8,128)(2,1)S(1)}, u32[]{:S(2)}) copy-start(bf16[2,8,2,48,256]{4,3,2,1,0:T(8,128)(2,1)S(1)} %collective-permute-done.3.rest_5_) | copy-start | bytes 2359300
  29.3 3.3 %collective-permute-start.5 = (bf16[528,384]{1,0:T(8,128)(2,1)S(1)}, bf16[528,384]{1,0:T(8,128)(2,1)S(1)}, u32[]{:S(2)}, u32[]{:S(2)}) collective-permute-start(bf16[528,384]{1,0:T(8,128)(2,1)S(1)} %copy-done.10), channel_id=1, source_target_pairs={{8,16},{16,8},{9,17},{17,9},{10,18},{18,10},{11,19},{19,11},{12,20... | collective-permute-start | bytes 1216520 | tf_op jit(solution)/shard_map/ppermute | solution.py:462
  29.9 12.9 %collective-permute-start.6 = (bf16[528,384]{1,0:T(8,128)(2,1)S(1)}, bf16[528,384]{1,0:T(8,128)(2,1)S(1)}, u32[]{:S(2)}, u32[]{:S(2)}) collective-permute-start(bf16[528,384]{1,0:T(8,128)(2,1)S(1)} %collective-permute-done.2), channel_id=1, source_target_pairs={{16,24},{8,0},{17,25},{9,1},{18,26},{10,2},{19,27},{11,3},{20,28},... | collective-permute-start | bytes 1216520 | tf_op jit(solution)/shard_map/ppermute | solution.py:461
  31.3 11.7 %collective-permute-start.8 = (bf16[8,2,48,256]{3,2,1,0:T(8,128)(2,1)S(1)}, bf16[8,2,48,256]{3,2,1,0:T(8,128)(2,1)}, u32[]{:S(2)}, u32[]{:S(2)}) collective-permute-start(bf16[8,2,48,256]{3,2,1,0:T(8,128)(2,1)S(1)} %slice_bitcast_fusion.1), channel_id=1, source_target_pairs={{0,4},{1,5},{2,6},{3,7},{4,0},{5,1},{6,2},{7,3},{8,12},{9,13},{10,... | collective-permute-start | bytes 1179656 | tf_op jit(solution)/shard_map/ppermute | solution.py:509
  43.0 1.9 %copy-start.7 = (bf16[528,384]{1,0:T(8,128)(2,1)}, bf16[528,384]{1,0:T(8,128)(2,1)S(1)}, u32[]{:S(2)}) copy-start(bf16[528,384]{1,0:T(8,128)(2,1)S(1)} %add.31.rest_1_) | copy-start | bytes 1216516
  43.0 1.9 %copy-start.19 = (bf16[8,2,48,256]{3,2,1,0:T(8,128)(2,1)}, bf16[8,2,48,256]{3,2,1,0:T(8,128)(2,1)S(1)}, u32[]{:S(2)}) copy-start(bf16[8,2,48,256]{3,2,1,0:T(8,128)(2,1)S(1)} %collective-permute-done.9.rest_8_) | copy-start | bytes 1179652
  43.0 1.8 %collective-permute-start.10 = (bf16[528,384]{1,0:T(8,128)(2,1)S(1)}, bf16[528,384]{1,0:T(8,128)(2,1)S(1)}, u32[]{:S(2)}, u32[]{:S(2)}) collective-permute-start(bf16[528,384]{1,0:T(8,128)(2,1)S(1)} %add.31.rest_1_), channel_id=1, source_target_pairs={{0,1},{1,0},{2,3},{3,2},{4,5},{5,4},{6,7},{7,6},{8,9},{9,8},{10,11... | collective-permute-start | bytes 1216520 | tf_op jit(solution)/shard_map/ppermute | solution.py:509
  44.8 0.8 copy-start.11
  58.5 4.5 %collective-permute-start.11 = (bf16[4,256,384]{2,1,0:T(8,128)(2,1)}, bf16[4,256,384]{2,1,0:T(8,128)(2,1)S(1)}, u32[]{:S(2)}, u32[]{:S(2)}) collective-permute-start(bf16[4,256,384]{2,1,0:T(8,128)(2,1)} %get-tuple-element.38), channel_id=1, source_target_pairs={{0,1},{1,0},{2,3},{3,2},{4,5},{5,4},{6,7},{7,6},{8,9},{9,8},{10,11... | collective-permute-start | bytes 2359304 | tf_op jit(solution)/shard_map/ppermute | solution.py:509
  60.4 19.7 %collective-permute-start.12 = (bf16[2,8,2,48,256]{4,3,2,1,0:T(8,128)(2,1)}, bf16[2,8,2,48,256]{4,3,2,1,0:T(8,128)(2,1)S(1)}, u32[]{:S(2)}, u32[]{:S(2)}) collective-permute-start(bf16[2,8,2,48,256]{4,3,2,1,0:T(8,128)(2,1)} %get-tuple-element.40), channel_id=1, source_target_pairs={{0,2},{1,3},{2,0},{3,1},{4,6},{5,7},{6,4},{7,5},{8,10},{9,11},{10,... | collective-permute-start | bytes 2359304 | tf_op jit(solution)/shard_map/ppermute | solution.py:509
  61.9 11.2 %collective-permute-start.13 = (bf16[1,8,2,48,256]{4,3,2,1,0:T(8,128)(2,1)}, bf16[1,8,2,48,256]{4,3,2,1,0:T(8,128)(2,1)S(1)}, u32[]{:S(2)}, u32[]{:S(2)}) collective-permute-start(bf16[1,8,2,48,256]{4,3,2,1,0:T(8,128)(2,1)} %get-tuple-element.42), channel_id=1, source_target_pairs={{0,4},{1,5},{2,6},{3,7},{4,0},{5,1},{6,2},{7,3},{8,12},{9,13},{10,... | collective-permute-start | bytes 1179656 | tf_op jit(solution)/shard_map/ppermute | solution.py:509
  63.0 10.8 %copy-start.17 = (bf16[1,8,2,48,256]{4,3,2,1,0:T(8,128)(2,1)S(1)}, bf16[1,8,2,48,256]{4,3,2,1,0:T(8,128)(2,1)}, u32[]{:S(2)}) copy-start(bf16[1,8,2,48,256]{4,3,2,1,0:T(8,128)(2,1)} %get-tuple-element.49) | copy-start | bytes 1179652
  65.3 14.9 %copy-start.16 = (bf16[1,8,2,48,256]{4,3,2,1,0:T(8,128)(2,1)S(1)}, bf16[1,8,2,48,256]{4,3,2,1,0:T(8,128)(2,1)}, u32[]{:S(2)}) copy-start(bf16[1,8,2,48,256]{4,3,2,1,0:T(8,128)(2,1)} %get-tuple-element.41) | copy-start | bytes 1179652
  65.3 27.0 %all-to-all-start = ((bf16[4,256,384]{2,1,0:T(8,128)(2,1)}), bf16[4,256,384]{2,1,0:T(8,128)(2,1)S(1)}, u32[]{:S(2)}, u32[]{:S(2)}) async-start(bf16[4,256,384]{2,1,0:T(8,128)(2,1)} %add.32), calls=%async_computation | async-start | bytes 1572864 | tf_op jit(solution)/shard_map/all_to_all | solution.py:547
  69.4 11.7 %collective-permute-start.14 = (bf16[1,8,2,48,256]{4,3,2,1,0:T(8,128)(2,1)}, bf16[1,8,2,48,256]{4,3,2,1,0:T(8,128)(2,1)S(1)}, u32[]{:S(2)}, u32[]{:S(2)}) collective-permute-start(bf16[1,8,2,48,256]{4,3,2,1,0:T(8,128)(2,1)} %get-tuple-element.44), channel_id=1, source_target_pairs={{0,5},{1,4},{2,7},{3,6},{4,1},{5,0},{6,3},{7,2},{8,13},{9,12},{10,... | collective-permute-start | bytes 1179656 | tf_op jit(solution)/shard_map/ppermute | solution.py:509
  69.8 11.3 %collective-permute-start.15 = (bf16[1,8,2,48,256]{4,3,2,1,0:T(8,128)(2,1)}, bf16[1,8,2,48,256]{4,3,2,1,0:T(8,128)(2,1)S(1)}, u32[]{:S(2)}, u32[]{:S(2)}) collective-permute-start(bf16[1,8,2,48,256]{4,3,2,1,0:T(8,128)(2,1)} %get-tuple-element.46), channel_id=1, source_target_pairs={{0,1},{1,0},{2,3},{3,2},{4,5},{5,4},{6,7},{7,6},{8,9},{9,8},{10,11... | collective-permute-start | bytes 1179656 | tf_op jit(solution)/shard_map/ppermute | solution.py:509
  73.1 0.7 copy-start.18
  80.1 13.0 %copy-start.4 = (bf16[2,8,2,48,256]{4,3,2,1,0:T(8,128)(2,1)}, bf16[2,8,2,48,256]{4,3,2,1,0:T(8,128)(2,1)S(1)}, u32[]{:S(2)}) copy-start(bf16[2,8,2,48,256]{4,3,2,1,0:T(8,128)(2,1)S(1)} %collective-permute-done.12.refs_1_) | copy-start | bytes 2359300
  81.1 12.0 %copy-start.12 = (bf16[1,8,2,48,256]{4,3,2,1,0:T(8,128)(2,1)}, bf16[1,8,2,48,256]{4,3,2,1,0:T(8,128)(2,1)S(1)}, u32[]{:S(2)}) copy-start(bf16[1,8,2,48,256]{4,3,2,1,0:T(8,128)(2,1)S(1)} %collective-permute-done.14.refs_4_) | copy-start | bytes 1179652
  81.1 12.0 %copy-start.13 = (bf16[1,8,2,48,256]{4,3,2,1,0:T(8,128)(2,1)}, bf16[1,8,2,48,256]{4,3,2,1,0:T(8,128)(2,1)S(1)}, u32[]{:S(2)}) copy-start(bf16[1,8,2,48,256]{4,3,2,1,0:T(8,128)(2,1)S(1)} %collective-permute-done.15.refs_3_) | copy-start | bytes 1179652
  81.1 11.2 %collective-permute-start.16 = (bf16[8,2,48,256]{3,2,1,0:T(8,128)(2,1)S(1)}, bf16[8,2,48,256]{3,2,1,0:T(8,128)(2,1)S(1)}, u32[]{:S(2)}, u32[]{:S(2)}) collective-permute-start(bf16[8,2,48,256]{3,2,1,0:T(8,128)(2,1)S(1)} %fusion), channel_id=1, source_target_pairs={{0,4},{1,5},{2,6},{3,7},{4,0},{5,1},{6,2},{7,3},{8,12},{9,13},{10,... | collective-permute-start | bytes 1179656 | tf_op jit(solution)/shard_map/ppermute | solution.py:509
  82.1 11.0 %collective-permute-start.17 = (bf16[8,2,48,256]{3,2,1,0:T(8,128)(2,1)S(1)}, bf16[8,2,48,256]{3,2,1,0:T(8,128)(2,1)S(1)}, u32[]{:S(2)}, u32[]{:S(2)}) collective-permute-start(bf16[8,2,48,256]{3,2,1,0:T(8,128)(2,1)S(1)} %add_bitcast_fusion), channel_id=1, source_target_pairs={{0,3},{1,2},{2,1},{3,0},{4,7},{5,6},{6,5},{7,4},{8,11},{9,10},{10,... | collective-permute-start | bytes 1179656 | tf_op jit(solution)/shard_map/ppermute | solution.py:509
  92.3 0.8 copy-start.14
  92.3 7.1 %copy-start.2 = (bf16[4,256,384]{2,1,0:T(8,128)(2,1)}, bf16[4,256,384]{2,1,0:T(8,128)(2,1)S(1)}, u32[]{:S(2)}) copy-start(bf16[4,256,384]{2,1,0:T(8,128)(2,1)S(1)} %all-to-all-done.parts_ref) | copy-start | bytes 2359300
  93.1 0.8 copy-start.15
  99.5 36.9 %collective-permute-start.19 = (bf16[16,2,48,256]{3,2,1,0:T(8,128)(2,1)}, bf16[16,2,48,256]{3,2,1,0:T(8,128)(2,1)S(1)}, u32[]{:S(2)}, u32[]{:S(2)}) collective-permute-start(bf16[16,2,48,256]{3,2,1,0:T(8,128)(2,1)} %get-tuple-element.52.refs_0_), channel_id=1, source_target_pairs={{0,8},{8,0},{16,24},{24,16},{1,9},{9,1},{17,25},{25,17},{2,10},{10... | collective-permute-start | bytes 2359304 | tf_op jit(solution)/shard_map/ppermute | solution.py:460
  101.7 37.3 %collective-permute-start.18 = (bf16[16,2,48,256]{3,2,1,0:T(8,128)(2,1)}, bf16[16,2,48,256]{3,2,1,0:T(8,128)(2,1)S(1)}, u32[]{:S(2)}, u32[]{:S(2)}) collective-permute-start(bf16[16,2,48,256]{3,2,1,0:T(8,128)(2,1)} %get-tuple-element.52.refs_0_), channel_id=1, source_target_pairs={{0,16},{8,24},{16,0},{24,8},{1,17},{9,25},{17,1},{25,9},{2,18},{10... | collective-permute-start | bytes 2359304 | tf_op jit(solution)/shard_map/ppermute | solution.py:459
  136.4 6.9 %copy-start.9 = (bf16[16,2,48,256]{3,2,1,0:T(8,128)(2,1)}, bf16[16,2,48,256]{3,2,1,0:T(8,128)(2,1)S(1)}, u32[]{:S(2)}) copy-start(bf16[16,2,48,256]{3,2,1,0:T(8,128)(2,1)S(1)} %collective-permute-done.19.refs_1_) | copy-start | bytes 2359300
  139.0 4.2 %copy-start.8 = (bf16[16,2,48,256]{3,2,1,0:T(8,128)(2,1)}, bf16[16,2,48,256]{3,2,1,0:T(8,128)(2,1)S(1)}, u32[]{:S(2)}) copy-start(bf16[16,2,48,256]{3,2,1,0:T(8,128)(2,1)S(1)} %collective-permute-done.18.refs_2_) | copy-start | bytes 2359300
  139.0 7.7 %collective-permute-start.20 = (bf16[16,2,48,256]{3,2,1,0:T(8,128)(2,1)}, bf16[16,2,48,256]{3,2,1,0:T(8,128)(2,1)S(1)}, u32[]{:S(2)}, u32[]{:S(2)}) collective-permute-start(bf16[16,2,48,256]{3,2,1,0:T(8,128)(2,1)} %get-tuple-element.52.refs_0_), channel_id=1, source_target_pairs={{8,16},{16,8},{9,17},{17,9},{10,18},{18,10},{11,19},{19,11},{12,20... | collective-permute-start | bytes 2359304 | tf_op jit(solution)/shard_map/ppermute | solution.py:462
  139.7 20.1 %collective-permute-start.21 = (bf16[16,2,48,256]{3,2,1,0:T(8,128)(2,1)S(1)}, bf16[16,2,48,256]{3,2,1,0:T(8,128)(2,1)S(1)}, u32[]{:S(2)}, u32[]{:S(2)}) collective-permute-start(bf16[16,2,48,256]{3,2,1,0:T(8,128)(2,1)S(1)} %collective-permute-done.18.refs_2_), channel_id=1, source_target_pairs={{16,24},{8,0},{17,25},{9,1},{18,26},{10,2},{19,27},{11,3},{20,28},... | collective-permute-start | bytes 2359304 | tf_op jit(solution)/shard_map/ppermute | solution.py:461
  143.2 16.6 %copy-start = (s32[2]{0:T(128)S(1)}, s32[2]{0:T(128)}, u32[]{:S(2)}) copy-start(s32[2]{0:T(128)} %pad_add_fusion.pos_ref) | copy-start | bytes 28
